TPU v7x, 32 devices: a whole 2x2x4 slice. The times are simulated.
32 devices in a mesh: pipe: 2 (over core), dp: 4 (over y, x), tensor: 4 (over z).
Axes of the slice: x: 2, y: 2, z: 4, core: 2. Of those that a mesh axis runs over, the one named last changes fastest.
Arguments:
- acts: bfloat16 [2, 2048, 4096], P('pipe', 'dp', 'tensor'), may hold values from -6 to 6
- out_grad: bfloat16 [2, 2048, 1024], P('pipe', 'dp', 'tensor'), may hold values from -6 to 6
- old_factor: float32 [2, 4, 1024, 1024], P('pipe', 'tensor', 'dp'), may hold values from -2 to 4, as said below
- old_root: bfloat16 [2, 4, 1024, 1024], P('pipe', 'tensor', 'dp'), may hold values from -2 to 2, as said below
- iter_count: int32 [2, 4], P('pipe', 'tensor'), may hold values from 1 to 2
Outputs:
- new_factor: float32 [2, 4, 1024, 1024], P('pipe', 'tensor', 'dp')
- new_root: bfloat16 [2, 4, 1024, 1024], P('pipe', 'tensor', 'dp')
- step: bfloat16 [2, 4, 256, 1024], P('pipe', 'tensor', None, 'dp')
Inputs may be any that keep to these rules, and one draw needn't show every extreme that they name: Every block of old_factor is symmetric, with diagonal entries of 0.5 or more. Every block of old_root is symmetric.
All inputs are finite; a program needn't handle non-finite values.
Results may differ from a plain program's by a relative error of at most 0.0056.
Values may be sent and summed in bfloat16 or wider, within the bound.
No kernel may reach another device: no remote copies, remote signals or barrier semaphores. Data moves between devices by JAX's collectives and lax.ppermute only.
A program may use at most 64 MiB of HBM per device.

v0:
```python
import math

import jax
import jax.numpy as jnp
from jax import lax
from jax.sharding import PartitionSpec as P

DECAY = 0.75
DAMPING = 0.1
EPSILON = 1e-06


def passed_along(block, axis, distance):
    devices = range(lax.axis_size(axis))
    route = [((i - distance) % len(devices), i) for i in devices]
    return lax.ppermute(block, axis, route)


def local(acts, out_grad, old_factor, old_root, iter_count):
    inputs = acts[0]
    replicas = lax.axis_size("dp")
    tokens_all = inputs.shape[0] * replicas
    order = inputs.shape[1]
    share = order // replicas
    offset = lax.axis_index("dp") * share
    received = passed_along(out_grad, "pipe", -1)[0]
    partial_grad = jnp.dot(received.T, inputs, preferred_element_type=jnp.float32) / math.sqrt(
        tokens_all
    )
    columns = inputs
    batch = lax.psum_scatter(
        jnp.dot(columns.T, inputs, preferred_element_type=jnp.float32) / tokens_all,
        "dp",
        scatter_dimension=0,
        tiled=True,
    )
    row_ids = lax.broadcasted_iota(jnp.int32, (share, order), 0) + offset
    col_ids = lax.broadcasted_iota(jnp.int32, (share, order), 1)
    eye_rows = (row_ids == col_ids).astype(jnp.float32)
    factor = DECAY * old_factor[0, 0] + (1.0 - DECAY) * batch + DAMPING * eye_rows
    squares = jnp.sum(factor * factor)
    grad_total = lax.psum(partial_grad, "dp")
    square_total = lax.psum(squares, "dp")
    scale = jnp.sqrt(square_total / order + EPSILON)
    grad16 = grad_total.astype(jnp.bfloat16)
    step_cols = lax.dot_general(
        grad16, old_root[0, 0], (((1,), (1,)), ((), ())), preferred_element_type=jnp.float32
    )
    step_out = step_cols.astype(jnp.bfloat16)[None, None]
    first_rows = (factor / scale).astype(jnp.bfloat16)
    first_full = lax.all_gather(first_rows, "dp", axis=0, tiled=True)
    full_rows = lax.broadcasted_iota(jnp.int32, (order, order), 0)
    full_cols = lax.broadcasted_iota(jnp.int32, (order, order), 1)
    eye_full = (full_rows == full_cols).astype(jnp.float32)
    turn_one = (1.5 * eye_full - 0.5 * first_full.astype(jnp.float32)).astype(jnp.bfloat16)
    second_rows = jnp.dot(first_rows, turn_one, preferred_element_type=jnp.float32).astype(
        jnp.bfloat16
    )
    turn_rows = lax.dynamic_slice_in_dim(turn_one, offset, share, 0)
    columns = turn_rows
    product = jnp.dot(
        columns,
        lax.all_gather(second_rows, "dp", axis=0, tiled=True),
        preferred_element_type=jnp.float32,
    )
    turn_two = (1.5 * eye_rows - 0.5 * product).astype(jnp.bfloat16)
    inverse_rows = jnp.dot(turn_two, turn_one, preferred_element_type=jnp.float32)
    chosen = jnp.where(iter_count[0, 0] == 1, turn_rows.astype(jnp.float32), inverse_rows)
    root = (chosen / jnp.sqrt(scale)).astype(jnp.bfloat16)
    return (factor[None, None], root[None, None], step_out)


def solution(mesh):
    return jax.shard_map(
        local,
        mesh=mesh,
        in_specs=(
            P("pipe", "dp", "tensor"),
            P("pipe", "dp", "tensor"),
            P("pipe", "tensor", "dp", None),
            P("pipe", "tensor", "dp", None),
            P("pipe", "tensor"),
        ),
        out_specs=(
            P("pipe", "tensor", "dp", None),
            P("pipe", "tensor", "dp", None),
            P("pipe", "tensor", None, "dp"),
        ),
        check_vma=False,
    )
```

profile of v0, /device:TPU:0, one launch (start us, length us, event | category | flops | bytes accessed | tf_op | source)
XLA Modules:
  0.0 198.5 jit_solution(17458141217148074890)
XLA Ops:
  7.2 0.0 copy-start
  7.2 0.0 copy-start.4
  7.2 0.0 reduce-scatter.2.cloned.1.call-start
  7.2 1.2 copy-done
  8.4 3.2 %convolution_multiply_fusion = f32[1024,1024]{1,0:T(8,128)} fusion(bf16[1,512,1024]{2,1,0:T(8,128)(2,1)S(1)} %copy-done), kind=kOutput, calls=%fused_computation.2 | convolution fusion | flops 1074790400 | bytes 5242880 | tf_op jit(solution)/shard_map/dot_general | solution.py:32
  11.6 0.0 reduce-scatter.2.cloned.1.call-update
  11.6 0.0 all-gather.3.cloned.1.call-start
  11.7 0.0 copy-done.4
  11.7 0.5 collective-permute-start
  12.2 1.2 collective-permute-done
  13.4 0.5 convolution_multiply_fusion.1
  13.8 53.4 %reduce-scatter.2.cloned.1.call-done = f32[256,1024]{1,0:T(8,128)} async-done(((f32[1024,1024]{1,0:T(8,128)}), f32[256,1024]{1,0:T(8,128)}) %reduce-scatter.2.cloned.1.call-update) | async-done | bytes 1048592 | tf_op jit(solution)/shard_map/reduce_scatter | solution.py:31
  67.2 2.6 %multiply_reduce_fusion = (f32[]{:T(128)}, f32[256,1024]{1,0:T(8,128)S(1)}) fusion(s32[256]{0:T(256)S(1)} %iota_add_fusion, f32[256,1024]{1,0:T(8,128)} %reduce-scatter.2.cloned.1.call-done, f32[1,1,256,1024]{3,2,1,0:T(8,128)} %param.7), kind=kLoop, calls=%fused_computation.19 | loop fusion | flops 2097151 | bytes 3146756 | tf_op jit(solution)/shard_map/reduce_sum | solution.py:41
  69.8 0.0 copy-start.1
  69.8 42.7 %all-reduce.2 = (f32[]{:T(128)}, bf16[256,1024]{1,0:T(8,128)(2,1)}) all-reduce(f32[]{:T(128)} %get-tuple-element.5, f32[256,1024]{1,0:T(8,128)S(1)} %convolution_multiply_fusion.1), channel_id=1, replica_groups=mesh['pipe'=2,'dp'=4,'tensor'=4] {'dp'}, use_global_device_ids=true, to_apply=%region_2.0 | all-reduce | flops 262145 | bytes 1572872 | tf_op jit(solution)/shard_map/psum | solution.py:43
  113.3 0.9 divide_convert_fusion
  114.2 0.0 all-gather.3.cloned.1.call-update
  114.2 0.0 copy-start.2
  114.2 0.0 copy-start.3
  114.2 0.0 all-gather.5.cloned.1.call-start
  114.3 35.1 %all-gather.3.cloned.1.call-done = bf16[1024,1024]{1,0:T(8,128)(2,1)} async-done(((bf16[256,1024]{1,0:T(8,128)(2,1)}), bf16[1024,1024]{1,0:T(8,128)(2,1)}) %all-gather.3.cloned.1.call-update) | async-done | bytes 2097168 | tf_op jit(solution)/shard_map/all_gather | solution.py:51
  149.4 3.3 %convolution_convert_fusion = bf16[256,1024]{1,0:T(8,128)(2,1)} fusion(bf16[256,1024]{1,0:T(8,128)(2,1)} %divide_convert_fusion, bf16[1024,1024]{1,0:T(8,128)(2,1)} %all-gather.3.cloned.1.call-done), kind=kOutput, calls=%fused_computation.8 | convolution fusion | flops 543424512 | bytes 3145728 | tf_op jit(solution)/shard_map/dot_general | solution.py:56
  152.7 0.0 copy-done.1
  152.7 0.0 all-gather.5.cloned.1.call-update
  153.5 0.0 copy-done.2
  153.5 0.0 copy-done.3
  153.5 1.0 fusion.5
  154.5 2.1 %subtract_convert_fusion = bf16[1024,1024]{1,0:T(8,128)(2,1)S(1)} fusion(bf16[1024,1024]{1,0:T(8,128)(2,1)} %all-gather.3.cloned.1.call-done), kind=kLoop, calls=%fused_computation | loop fusion | flops 6291456 | bytes 4194304 | tf_op jit(solution)/shard_map/convert_element_type | solution.py:55
  156.6 31.6 %all-gather.5.cloned.1.call-done = bf16[1024,1024]{1,0:T(8,128)(2,1)} async-done(((bf16[256,1024]{1,0:T(8,128)(2,1)}), bf16[1024,1024]{1,0:T(8,128)(2,1)}) %all-gather.5.cloned.1.call-update) | async-done | bytes 2097168 | tf_op jit(solution)/shard_map/all_gather | solution.py:63
  188.2 3.8 %fusion.4 = bf16[1,1,256,1024]{3,2,1,0:T(8,128)(2,1)} fusion(bf16[1024,1024]{1,0:T(8,128)(2,1)S(1)} %subtract_convert_fusion, bf16[1024,1024]{1,0:T(8,128)(2,1)} %all-gather.5.cloned.1.call-done, f32[]{:T(128)S(6)} %sqrt.7, s32[]{:T(128)S(6)} %select_n.12, s32[256]{0:T(256)S(1)} %iota_add_fusion, pred[]{:T(512)} %bitcast.3), kind=kOutput, calls=%fused_computation.11 | convolution fusion | flops 1076101120 | bytes 5769729 | tf_op jit(solution)/shard_map/dot_general | solution.py:67
  (1 shorter events, 0.0 us)
Async XLA Ops:
  7.2 1.2 copy-start
  7.2 4.5 %copy-start.4 = (bf16[1,512,256]{2,1,0:T(8,128)(2,1)S(1)}, bf16[1,512,256]{2,1,0:T(8,128)(2,1)}, u32[]{:S(2)}) copy-start(bf16[1,512,256]{2,1,0:T(8,128)(2,1)} %param.6) | copy-start | bytes 786436
  7.2 60.0 %reduce-scatter.2.cloned.1.call-start = ((), (), s32[]{:S(2)}) async-start(), calls=%async_computation.1 | async-start | bytes 5242880 | tf_op jit(solution)/shard_map/reduce_scatter | solution.py:31
  11.6 137.7 %all-gather.3.cloned.1.call-start = ((), (), s32[]{:S(2)}) async-start(), calls=%async_computation.2 | async-start | bytes 2621440 | tf_op jit(solution)/shard_map/all_gather | solution.py:51
  11.7 1.7 collective-permute-start
  69.8 82.9 %copy-start.1 = (f32[256,1024]{1,0:T(8,128)}, f32[256,1024]{1,0:T(8,128)S(1)}, u32[]{:S(2)}) copy-start(f32[256,1024]{1,0:T(8,128)S(1)} %get-tuple-element.6) | copy-start | bytes 3145732
  114.2 39.2 %copy-start.2 = (bf16[1,1,256,1024]{3,2,1,0:T(8,128)(2,1)S(1)}, bf16[1,1,256,1024]{3,2,1,0:T(8,128)(2,1)}, u32[]{:S(2)}) copy-start(bf16[1,1,256,1024]{3,2,1,0:T(8,128)(2,1)} %param.8) | copy-start | bytes 1572868
  114.2 39.2 %copy-start.3 = (bf16[256,1024]{1,0:T(8,128)(2,1)S(1)}, bf16[256,1024]{1,0:T(8,128)(2,1)}, u32[]{:S(2)}) copy-start(bf16[256,1024]{1,0:T(8,128)(2,1)} %get-tuple-element.4) | copy-start | bytes 1572868
  114.2 74.0 %all-gather.5.cloned.1.call-start = ((), (), s32[]{:S(2)}) async-start(), calls=%async_computation.3 | async-start | bytes 2621440 | tf_op jit(solution)/shard_map/all_gather | solution.py:63
Sparse Core Ops, SparseCore 0:
  11.8 55.3 reduce-scatter.1
  114.3 34.9 all-gather.2
  152.9 35.2 all-gather.4
where the time goes:
time: 199 us
  waiting for transfers between devices  121 us (61%)
  blocking collectives  42.7 us (21%)
  between operations  15.2 us (8%)
  matrix products  11.8 us (6%)
  other arithmetic  5.71 us (3%)
    reduce_scatter x1, waiting for transfers between devices, local(): lax.psum_scatter(jnp.dot(columns.T, inputs, preferred_element_type=jnp.fl...  53.4 us
    psum x1, blocking collectives, local(): square_total = lax.psum(squares, 'dp')  42.7 us
    all_gather x1, waiting for transfers between devices, local(): first_full = lax.all_gather(first_rows, 'dp', axis=0, tiled=True)  35.1 us
    all_gather x1, waiting for transfers between devices, local(): lax.all_gather(second_rows, 'dp', axis=0, tiled=True)  31.6 us
  transfers between devices with their start and end apart: 4, of which 4 were waited for; matrix products, arithmetic and copies ran while one was open for 2% of the time, Pallas kernels for 0%

commit v1 on v0

v1 whole, which is shorter than its diff:
```python
import functools
import math

import jax
import jax.numpy as jnp
from jax import lax
from jax.experimental import pallas as pl
from jax.experimental.pallas import tpu as pltpu
from jax.sharding import PartitionSpec as P

DECAY = 0.75
DAMPING = 0.1
EPSILON = 1e-06
BF16 = jnp.bfloat16
F32 = jnp.float32
VMEM_LIMIT = 28 * 1024 * 1024


def passed_along(block, axis, distance):
    devices = range(lax.axis_size(axis))
    route = [((i - distance) % len(devices), i) for i in devices]
    return lax.ppermute(block, axis, route)


def swapped(block, offset):
    return lax.ppermute(block, "dp", [(i, i ^ offset) for i in range(lax.axis_size("dp"))])


def eye_of(rows, cols, shift=0):
    row_ids = lax.broadcasted_iota(jnp.int32, (rows, cols), 0) + shift
    col_ids = lax.broadcasted_iota(jnp.int32, (rows, cols), 1)
    return (row_ids == col_ids).astype(F32)


def whole(count):
    return [pl.BlockSpec(memory_space=pltpu.VMEM)] * count


def products_kernel(replicas, tokens_all, acts, grads, own, *rest):
    sends, grad_sum = rest[:-1], rest[-1]
    order = acts.shape[1]
    share = order // replicas
    strip = grads.shape[1] // replicas
    mine = lax.axis_index("dp")
    everything = acts[...]
    grad_sum[...] = lax.dot_general(
        grads[...], everything, (((0,), (0,)), ((), ())), preferred_element_type=F32
    ) * (1.0 / math.sqrt(tokens_all))
    for offset in reversed(range(replicas)):
        other = mine ^ offset
        columns = acts[:, pl.ds(pl.multiple_of(other * share, share), share)]
        batch = lax.dot_general(
            columns, everything, (((0,), (0,)), ((), ())), preferred_element_type=F32
        ) * (1.0 / tokens_all)
        part = grad_sum[pl.ds(pl.multiple_of(other * strip, strip), strip), :]
        target = own if offset == 0 else sends[offset - 1]
        target[0:share, :] = batch.astype(target.dtype)
        target[share:, :] = part.astype(target.dtype)


def factor_kernel(replicas, own, *rest):
    got, old, factor_out = rest[: replicas - 1], rest[replicas - 1], rest[replicas]
    rows_out, sends = rest[replicas + 1], rest[replicas + 2 :]
    share, order = old.shape
    strip = own.shape[0] - share
    half = share // 2
    mine = lax.axis_index("dp")
    total = own[...]
    for message in got:
        total = total + message[...].astype(F32)
    eye = (
        lax.broadcasted_iota(jnp.int32, (share, order), 0) + mine * share
        == lax.broadcasted_iota(jnp.int32, (share, order), 1)
    ).astype(F32)
    factor = DECAY * old[...] + (1.0 - DECAY) * total[0:share] + DAMPING * eye
    factor_out[...] = factor
    grad16 = total[share:].astype(BF16)
    squares = jnp.sum(factor * factor, axis=0, keepdims=True)
    lanes = squares[:, 0:share]
    for offset in range(1, replicas):
        lanes = lanes + squares[:, offset * share : (offset + 1) * share]
    high = lanes.astype(BF16).astype(F32)
    middle = (lanes - high).astype(BF16).astype(F32)
    low = lanes - high - middle
    spot = lax.broadcasted_iota(jnp.int32, (16, share), 0)
    digits = jnp.where(spot == 0, high, jnp.where(spot == 1, middle, jnp.where(spot == 2, low, 0.0)))
    digits16 = digits.astype(BF16)
    for offset in range(replicas):
        other = mine ^ offset
        block = factor_out[:, pl.ds(pl.multiple_of(other * share, share), share)].astype(BF16)
        rows_out[0:share, offset * share : (offset + 1) * share] = block
    rows_out[share : share + strip, :] = grad16
    rows_out[share + strip :, 0:share] = digits16
    rows_out[share + strip :, share:] = jnp.zeros((16, order - share), BF16)

    def block_of(offset):
        return rows_out[0:share, offset * share : (offset + 1) * share]

    for offset, send in zip(range(1, replicas), sends):
        pieces = [block_of(0)]
        if offset == 1:
            pieces += [block_of(2), block_of(3)[0:half, :]]
        if offset == 2:
            pieces += [block_of(1), block_of(3)[:, half:].astype(F32).T.astype(BF16)]
        for chunk in range(replicas):
            pieces.append(grad16[:, chunk * share : (chunk + 1) * share])
        pieces.append(digits16)
        start = 0
        for piece in pieces:
            send[start : start + piece.shape[0], :] = piece
            start += piece.shape[0]


def root_kernel(replicas, count, rows, near, side, far, old_root, root_out, step_out, factor, turn, grads, result):
    share = rows.shape[1] // replicas
    order = rows.shape[1]
    strip = rows.shape[0] - share - 16
    half = share // 2
    mine = lax.axis_index("dp")

    def put(row, col, block):
        factor[row * share : (row + 1) * share, col * share : (col + 1) * share] = block

    def mirror(row, col, block):
        put(row, col, block)
        put(col, row, block.astype(F32).T.astype(BF16))

    factor[0:share, :] = rows[0:share, :]
    for offset in range(1, replicas):
        put(offset, 0, rows[0:share, offset * share : (offset + 1) * share].astype(F32).T.astype(BF16))
    put(1, 1, near[0:share, :])
    put(2, 2, side[0:share, :])
    put(3, 3, far[0:share, :])
    mirror(1, 3, near[share : 2 * share, :])
    mirror(2, 3, side[share : 2 * share, :])
    middle = jnp.concatenate(
        [near[2 * share : 2 * share + half, :], side[2 * share : 2 * share + half, :]], axis=0
    )
    mirror(1, 2, middle)

    squares = rows[share + strip :, 0:share].astype(F32)
    for message in (near, side, far):
        squares = squares + message[message.shape[0] - 16 :, :].astype(F32)
    square_total = jnp.sum(squares, keepdims=True)
    scale = jnp.sqrt(square_total / order + EPSILON)
    inverse = 1.0 / scale

    for offset in range(replicas):
        band = slice(offset * share, (offset + 1) * share)
        first = (factor[band, :].astype(F32) * inverse).astype(BF16)
        factor[band, :] = first
        eye = eye_of(share, order, offset * share)
        turn[band, :] = (1.5 * eye - 0.5 * first.astype(F32)).astype(BF16)
    eye = eye_of(share, order)
    turn_rows = turn[0:share, :]
    second = jnp.dot(turn_rows, factor[...], preferred_element_type=F32).astype(BF16)
    product = jnp.dot(second, turn[...], preferred_element_type=F32)
    turn_two = (1.5 * eye - 0.5 * product).astype(BF16)
    inverse_rows = jnp.dot(turn_two, turn[...], preferred_element_type=F32)
    chosen = jnp.where(count[0, 0] == 1, turn_rows.astype(F32), inverse_rows)
    root = (chosen * lax.rsqrt(scale)).astype(BF16)
    for offset in range(replicas):
        other = mine ^ offset
        root_out[:, pl.ds(pl.multiple_of(other * share, share), share)] = root[
            :, offset * share : (offset + 1) * share
        ]

    grads[0:strip, :] = rows[share : share + strip, :]
    for offset, message in zip(range(1, replicas), (near, side, far)):
        start = message.shape[0] - 16 - replicas * strip
        for chunk in range(replicas):
            grads[offset * strip : (offset + 1) * strip, chunk * share : (chunk + 1) * share] = message[
                start + chunk * strip : start + (chunk + 1) * strip, :
            ]
    result[...] = lax.dot_general(
        grads[...], old_root[...], (((1,), (1,)), ((), ())), preferred_element_type=F32
    ).astype(BF16)
    for offset in range(replicas):
        other = mine ^ offset
        step_out[pl.ds(pl.multiple_of(other * strip, strip), strip), :] = result[
            offset * strip : (offset + 1) * strip, :
        ]


def square_plan(acts, out_grad, old_factor, old_root, iter_count):
    replicas = lax.axis_size("dp")
    inputs = acts[0]
    tokens_all = inputs.shape[0] * replicas
    order = inputs.shape[1]
    share = order // replicas
    grows = out_grad.shape[2]
    strip = grows // replicas
    half = share // 2
    params = pltpu.CompilerParams(vmem_limit_bytes=VMEM_LIMIT)
    offsets = range(1, replicas)

    received = passed_along(out_grad, "pipe", -1)[0]
    own, *sends = pl.pallas_call(
        functools.partial(products_kernel, replicas, tokens_all),
        out_shape=[jax.ShapeDtypeStruct((share + strip, order), F32)]
        + [jax.ShapeDtypeStruct((share + strip, order), BF16)] * (replicas - 1),
        in_specs=whole(2),
        out_specs=whole(replicas),
        scratch_shapes=[pltpu.VMEM((grows, order), F32)],
        compiler_params=params,
        name="products",
    )(inputs, received)
    got = [swapped(sends[offset - 1], offset) for offset in reversed(offsets)][::-1]

    tail = replicas * strip + 16
    lengths = [2 * share + half + tail, 2 * share + half + tail, share + tail]
    factor, rows, *sends = pl.pallas_call(
        functools.partial(factor_kernel, replicas),
        out_shape=[
            jax.ShapeDtypeStruct((share, order), F32),
            jax.ShapeDtypeStruct((share + strip + 16, order), BF16),
        ]
        + [jax.ShapeDtypeStruct((length, share), BF16) for length in lengths],
        in_specs=whole(replicas + 1),
        out_specs=whole(replicas + 1),
        compiler_params=params,
        name="factor",
    )(own, *got, old_factor[0, 0])
    got = [swapped(sends[offset - 1], offset) for offset in reversed(offsets)][::-1]

    root, step = pl.pallas_call(
        functools.partial(root_kernel, replicas),
        out_shape=[
            jax.ShapeDtypeStruct((share, order), BF16),
            jax.ShapeDtypeStruct((grows, share), BF16),
        ],
        in_specs=[pl.BlockSpec(memory_space=pltpu.SMEM)] + whole(replicas + 1),
        out_specs=whole(2),
        scratch_shapes=[
            pltpu.VMEM((order, order), BF16),
            pltpu.VMEM((order, order), BF16),
            pltpu.VMEM((grows, order), BF16),
            pltpu.VMEM((grows, share), BF16),
        ],
        compiler_params=params,
        name="root",
    )(iter_count, rows, *got, old_root[0, 0])
    return (factor[None, None], root[None, None], step[None, None])


def ring_plan(acts, out_grad, old_factor, old_root, iter_count):
    inputs = acts[0]
    replicas = lax.axis_size("dp")
    tokens_all = inputs.shape[0] * replicas
    order = inputs.shape[1]
    share = order // replicas
    offset = lax.axis_index("dp") * share
    received = passed_along(out_grad, "pipe", -1)[0]
    partial_grad = jnp.dot(received.T, inputs, preferred_element_type=F32) / math.sqrt(tokens_all)
    batch = lax.psum_scatter(
        jnp.dot(inputs.T, inputs, preferred_element_type=F32) / tokens_all,
        "dp",
        scatter_dimension=0,
        tiled=True,
    )
    eye_rows = eye_of(share, order, offset)
    factor = DECAY * old_factor[0, 0] + (1.0 - DECAY) * batch + DAMPING * eye_rows
    grad16 = lax.psum(partial_grad, "dp").astype(BF16)
    scale = jnp.sqrt(lax.psum(jnp.sum(factor * factor), "dp") / order + EPSILON)
    step = lax.dot_general(
        grad16, old_root[0, 0], (((1,), (1,)), ((), ())), preferred_element_type=F32
    ).astype(BF16)
    first = lax.all_gather((factor / scale).astype(BF16), "dp", axis=0, tiled=True)
    turn_one = (1.5 * eye_of(order, order) - 0.5 * first.astype(F32)).astype(BF16)
    turn_rows = lax.dynamic_slice_in_dim(turn_one, offset, share, 0)
    second = jnp.dot(turn_rows, first, preferred_element_type=F32).astype(BF16)
    product = jnp.dot(second, turn_one, preferred_element_type=F32)
    turn_two = (1.5 * eye_rows - 0.5 * product).astype(BF16)
    inverse_rows = jnp.dot(turn_two, turn_one, preferred_element_type=F32)
    chosen = jnp.where(iter_count[0, 0] == 1, turn_rows.astype(F32), inverse_rows)
    root = (chosen / jnp.sqrt(scale)).astype(BF16)
    return (factor[None, None], root[None, None], step[None, None])


def solution(mesh):
    return jax.shard_map(
        square_plan if mesh.shape["dp"] == 4 else ring_plan,
        mesh=mesh,
        in_specs=(
            P("pipe", "dp", "tensor"),
            P("pipe", "dp", "tensor"),
            P("pipe", "tensor", "dp", None),
            P("pipe", "tensor", "dp", None),
            P("pipe", "tensor"),
        ),
        out_specs=(
            P("pipe", "tensor", "dp", None),
            P("pipe", "tensor", "dp", None),
            P("pipe", "tensor", None, "dp"),
        ),
        check_vma=False,
    )
```

time: 199 us -> 62.8 us (0.32)
  waiting for transfers between devices: 121 us -> 44.9 us
  blocking collectives: 42.7 us -> 0 us
  between operations: 15.2 us -> 1.3 us
  matrix products: 11.8 us -> 0 us
  starting transfers between devices: 0.63 us -> 8.47 us
  Pallas kernels: 0 us -> 6.78 us
  other arithmetic: 5.71 us -> 0 us
    all_gather x2 -> x0, waiting for transfers between devices: 66.7 us -> none  [the longest x1 35.1 us: local(): first_full = lax.all_gather(first_rows, 'dp', axis=0, tiled=True)]
    reduce_scatter x1 -> x0, waiting for transfers between devices: 53.4 us -> none  [local(): lax.psum_scatter(jnp.dot(columns.T, inputs, preferred_element_type=jnp.fl...]
    ppermute x0 -> x6, waiting for transfers between devices: none -> 43.5 us  [swapped(): lax.ppermute(block, 'dp', [(i, i ^ offset) for i in range(lax.axis_size('...]
    psum x1 -> x0, blocking collectives: 42.7 us -> none  [local(): square_total = lax.psum(squares, 'dp')]
    dot_general x5 -> x0, matrix products: 11.8 us -> none  [the longest x1 3.76 us: local(): jnp.dot(turn_two, turn_one, preferred_element_type=jnp.float32)]
    ppermute x0 -> x6, starting transfers between devices: none -> 7.96 us  [swapped(): lax.ppermute(block, 'dp', [(i, i ^ offset) for i in range(lax.axis_size('...]
    pallas_call x0 -> x3, Pallas kernels: none -> 6.78 us  [the longest x1 3.13 us: square_plan(): pl.pallas_call(functools.partial(root_kernel, replicas), out_shape=[jax.S...]
    convert_element_type x2 -> x0, other arithmetic: 3.06 us -> none  [the longest x1 2.15 us: local(): (1.5 * eye_full - 0.5 * first_full.astype(jnp.float32)).astype(jnp.bfloat16)]
  transfers between devices with their start and end apart: 4 -> 7, of which waited for: 4 -> 5; matrix products, arithmetic and copies ran while one was open for 2% -> 0% of each run, Pallas kernels for 0% -> 0%
where the time goes in v1:
time: 62.8 us; the launch traced here: 62.7 us
  waiting for transfers between devices  44.9 us (71%)
  starting transfers between devices  8.47 us (13%)
  Pallas kernels  6.78 us (11%)
  between operations  1.3 us (2%)
  local copies, waits for them, and re-layouts  1.23 us (2%)
    ppermute x6, waiting for transfers between devices, swapped(): lax.ppermute(block, 'dp', [(i, i ^ offset) for i in range(lax.axis_size('...  43.5 us
    ppermute x6, starting transfers between devices, swapped(): lax.ppermute(block, 'dp', [(i, i ^ offset) for i in range(lax.axis_size('...  7.96 us
    pallas_call x1, Pallas kernels, square_plan(): pl.pallas_call(functools.partial(root_kernel, replicas), out_shape=[jax.S...  3.13 us
    pallas_call x1, Pallas kernels, square_plan(): pl.pallas_call(functools.partial(factor_kernel, replicas), out_shape=[jax...  2.04 us
    pallas_call x1, Pallas kernels, square_plan(): pl.pallas_call(functools.partial(products_kernel, replicas, tokens_all),...  1.61 us
    ppermute x1, waiting for transfers between devices, passed_along(): return lax.ppermute(block, axis, route)  1.37 us
  transfers between devices with their start and end apart: 7, of which 5 were waited for; matrix products, arithmetic and copies ran while one was open for 0% of the time, Pallas kernels for 0%

profile of v1, /device:TPU:0, one launch (start us, length us, event | category | flops | bytes accessed | tf_op | source)
XLA Modules:
  0.0 62.7 jit_solution(12798844933743245090)
XLA Ops:
  0.6 0.5 collective-permute-start
  1.1 1.4 %collective-permute-done = bf16[1,512,256]{2,1,0:T(8,128)(2,1)S(1)} collective-permute-done((bf16[1,512,256]{2,1,0:T(8,128)(2,1)}, bf16[1,512,256]{2,1,0:T(8,128)(2,1)S(1)}, u32[]{:S(2)}, u32[]{:S(2)}) %collective-permute-start) | collective-permute-done | bytes 262176 | tf_op jit(solution)/shard_map/ppermute | solution.py:22
  2.5 0.0 copy-start
  2.5 1.2 %copy-done = bf16[1,512,1024]{2,1,0:T(8,128)(2,1)S(1)} copy-done((bf16[1,512,1024]{2,1,0:T(8,128)(2,1)S(1)}, bf16[1,512,1024]{2,1,0:T(8,128)(2,1)}, u32[]{:S(2)}) %copy-start) | copy-done | bytes 1048600
  3.7 0.0 copy-start.1
  3.7 1.6 %products.1 = (f32[320,1024]{1,0:T(8,128)S(1)}, bf16[320,1024]{1,0:T(8,128)(2,1)S(1)}, bf16[320,1024]{1,0:T(8,128)(2,1)S(1)}, bf16[320,1024]{1,0:T(8,128)(2,1)S(1)}) custom-call(bf16[512,1024]{1,0:T(8,128)(2,1)S(1)} %bitcast.7, bf16[512,256]{1,0:T(8,128)(2,1)S(1)} %bitcast.10), custom_call_target="tpu_custom_call" | custom-call | tf_op jit(solution)/shard_map/products/pallas_call | solution.py:198
  5.4 2.9 %collective-permute-start.1 = (bf16[320,1024]{1,0:T(8,128)(2,1)S(1)}, bf16[320,1024]{1,0:T(8,128)(2,1)S(1)}, u32[]{:S(2)}, u32[]{:S(2)}) collective-permute-start(bf16[320,1024]{1,0:T(8,128)(2,1)S(1)} %get-tuple-element.15), channel_id=1, source_target_pairs={{0,4},{4,0},{8,12},{12,8},{1,5},{5,1},{9,13},{13,9},{2,6},{6,2},{1... | collective-permute-start | bytes 1966088 | tf_op jit(solution)/shard_map/ppermute | solution.py:26
  8.3 1.5 %collective-permute-start.2 = (bf16[320,1024]{1,0:T(8,128)(2,1)S(1)}, bf16[320,1024]{1,0:T(8,128)(2,1)S(1)}, u32[]{:S(2)}, u32[]{:S(2)}) collective-permute-start(bf16[320,1024]{1,0:T(8,128)(2,1)S(1)} %get-tuple-element.16), channel_id=1, source_target_pairs={{0,8},{4,12},{8,0},{12,4},{1,9},{5,13},{9,1},{13,5},{2,10},{6,14},... | collective-permute-start | bytes 1966088 | tf_op jit(solution)/shard_map/ppermute | solution.py:26
  9.8 0.0 collective-permute-start.3
  9.8 14.0 %collective-permute-done.1.rest_0_ = bf16[320,1024]{1,0:T(8,128)(2,1)S(1)} collective-permute-done((bf16[320,1024]{1,0:T(8,128)(2,1)S(1)}, bf16[320,1024]{1,0:T(8,128)(2,1)S(1)}, u32[]{:S(2)}, u32[]{:S(2)}) %collective-permute-start.1) | collective-permute-done | bytes 655392 | tf_op jit(solution)/shard_map/ppermute | solution.py:26
  23.8 15.0 %collective-permute-done.2.rest_1_ = bf16[320,1024]{1,0:T(8,128)(2,1)S(1)} collective-permute-done((bf16[320,1024]{1,0:T(8,128)(2,1)S(1)}, bf16[320,1024]{1,0:T(8,128)(2,1)S(1)}, u32[]{:S(2)}, u32[]{:S(2)}) %collective-permute-start.2) | collective-permute-done | bytes 655392 | tf_op jit(solution)/shard_map/ppermute | solution.py:26
  38.8 0.0 collective-permute-done.3.rest_2_
  38.8 0.0 copy-done.1
  38.8 0.0 copy-start.2
  38.8 2.0 %factor.1 = (f32[256,1024]{1,0:T(8,128)}, bf16[336,1024]{1,0:T(8,128)(2,1)S(1)}, bf16[912,256]{1,0:T(8,128)(2,1)S(1)}, bf16[912,256]{1,0:T(8,128)(2,1)S(1)}, bf16[528,256]{1,0:T(8,128)(2,1)S(1)}) custom-call(f32[320,1024]{1,0:T(8,128)S(1)} %get-tuple-element.14.own, bf16[320,1024]{1,0:T(8,128)(2,1)S(1)} %collective-permute-done.1.rest_0_, ...), custom_call_target="tpu_custom_call" | custom-call | tf_op jit(solution)/shard_map/factor/pallas_call | solution.py:212
  40.9 1.2 %collective-permute-start.4 = (bf16[912,256]{1,0:T(8,128)(2,1)S(1)}, bf16[912,256]{1,0:T(8,128)(2,1)S(1)}, u32[]{:S(2)}, u32[]{:S(2)}) collective-permute-start(bf16[912,256]{1,0:T(8,128)(2,1)S(1)} %get-tuple-element.20), channel_id=1, source_target_pairs={{0,4},{4,0},{8,12},{12,8},{1,5},{5,1},{9,13},{13,9},{2,6},{6,2},{1... | collective-permute-start | bytes 1400840 | tf_op jit(solution)/shard_map/ppermute | solution.py:26
  42.1 0.8 %collective-permute-start.5 = (bf16[912,256]{1,0:T(8,128)(2,1)S(1)}, bf16[912,256]{1,0:T(8,128)(2,1)S(1)}, u32[]{:S(2)}, u32[]{:S(2)}) collective-permute-start(bf16[912,256]{1,0:T(8,128)(2,1)S(1)} %get-tuple-element.21), channel_id=1, source_target_pairs={{0,8},{4,12},{8,0},{12,4},{1,9},{5,13},{9,1},{13,5},{2,10},{6,14},... | collective-permute-start | bytes 1400840 | tf_op jit(solution)/shard_map/ppermute | solution.py:26
  42.9 1.4 %collective-permute-start.6 = (bf16[528,256]{1,0:T(8,128)(2,1)S(1)}, bf16[528,256]{1,0:T(8,128)(2,1)S(1)}, u32[]{:S(2)}, u32[]{:S(2)}) collective-permute-start(bf16[528,256]{1,0:T(8,128)(2,1)S(1)} %get-tuple-element.22), channel_id=1, source_target_pairs={{0,12},{4,8},{8,4},{12,0},{1,13},{5,9},{9,5},{13,1},{2,14},{6,10},... | collective-permute-start | bytes 811016 | tf_op jit(solution)/shard_map/ppermute | solution.py:26
  45.0 14.3 %collective-permute-done.6.far = bf16[528,256]{1,0:T(8,128)(2,1)S(1)} collective-permute-done((bf16[528,256]{1,0:T(8,128)(2,1)S(1)}, bf16[528,256]{1,0:T(8,128)(2,1)S(1)}, u32[]{:S(2)}, u32[]{:S(2)}) %collective-permute-start.6) | collective-permute-done | bytes 270368 | tf_op jit(solution)/shard_map/ppermute | solution.py:26
  59.3 0.0 collective-permute-done.4.near
  59.3 0.2 collective-permute-done.5.side
  59.5 0.0 copy-done.2
  59.5 3.1 %root.1 = (bf16[256,1024]{1,0:T(8,128)(2,1)}, bf16[256,256]{1,0:T(8,128)(2,1)}) custom-call(s32[1,1]{1,0:T(1,128)S(6)} %copy.8.count, bf16[336,1024]{1,0:T(8,128)(2,1)S(1)} %get-tuple-element.19.rows, bf16[912,256]{1,0:T(8,128)(2,1)S(1)} %collective-permute-done.4.near, bf16[912,256]{1,0:T(8,128)(2,1)S(1)} %collective-permute-done.5.side, ...), custom_call_target="tpu_custom_call" | custom-call | tf_op jit(solution)/shard_map/root/pallas_call | solution.py:226
Async XLA Ops:
  0.6 1.9 %collective-permute-start = (bf16[1,512,256]{2,1,0:T(8,128)(2,1)}, bf16[1,512,256]{2,1,0:T(8,128)(2,1)S(1)}, u32[]{:S(2)}, u32[]{:S(2)}) collective-permute-start(bf16[1,512,256]{2,1,0:T(8,128)(2,1)} %param.6), channel_id=1, source_target_pairs={{16,0},{0,16},{17,1},{1,17},{18,2},{2,18},{19,3},{3,19},{20,4},{4,... | collective-permute-start | bytes 786440 | tf_op jit(solution)/shard_map/ppermute | solution.py:22
  2.5 1.2 %copy-start = (bf16[1,512,1024]{2,1,0:T(8,128)(2,1)S(1)}, bf16[1,512,1024]{2,1,0:T(8,128)(2,1)}, u32[]{:S(2)}) copy-start(bf16[1,512,1024]{2,1,0:T(8,128)(2,1)} %param.5) | copy-start | bytes 3145732
  3.7 35.1 %copy-start.1 = (f32[1,1,256,1024]{3,2,1,0:T(8,128)S(1)}, f32[1,1,256,1024]{3,2,1,0:T(8,128)}, u32[]{:S(2)}) copy-start(f32[1,1,256,1024]{3,2,1,0:T(8,128)} %param.7) | copy-start | bytes 3145732
  5.4 18.4 %collective-permute-start.1 = (bf16[320,1024]{1,0:T(8,128)(2,1)S(1)}, bf16[320,1024]{1,0:T(8,128)(2,1)S(1)}, u32[]{:S(2)}, u32[]{:S(2)}) collective-permute-start(bf16[320,1024]{1,0:T(8,128)(2,1)S(1)} %get-tuple-element.15), channel_id=1, source_target_pairs={{0,4},{4,0},{8,12},{12,8},{1,5},{5,1},{9,13},{13,9},{2,6},{6,2},{1... | collective-permute-start | bytes 1966088 | tf_op jit(solution)/shard_map/ppermute | solution.py:26
  8.3 30.5 %collective-permute-start.2 = (bf16[320,1024]{1,0:T(8,128)(2,1)S(1)}, bf16[320,1024]{1,0:T(8,128)(2,1)S(1)}, u32[]{:S(2)}, u32[]{:S(2)}) collective-permute-start(bf16[320,1024]{1,0:T(8,128)(2,1)S(1)} %get-tuple-element.16), channel_id=1, source_target_pairs={{0,8},{4,12},{8,0},{12,4},{1,9},{5,13},{9,1},{13,5},{2,10},{6,14},... | collective-permute-start | bytes 1966088 | tf_op jit(solution)/shard_map/ppermute | solution.py:26
  9.8 29.0 %collective-permute-start.3 = (bf16[320,1024]{1,0:T(8,128)(2,1)S(1)}, bf16[320,1024]{1,0:T(8,128)(2,1)S(1)}, u32[]{:S(2)}, u32[]{:S(2)}) collective-permute-start(bf16[320,1024]{1,0:T(8,128)(2,1)S(1)} %get-tuple-element.17), channel_id=1, source_target_pairs={{0,12},{4,8},{8,4},{12,0},{1,13},{5,9},{9,5},{13,1},{2,14},{6,10},... | collective-permute-start | bytes 1966088 | tf_op jit(solution)/shard_map/ppermute | solution.py:26
  38.8 20.7 %copy-start.2 = (bf16[1,1,256,1024]{3,2,1,0:T(8,128)(2,1)S(1)}, bf16[1,1,256,1024]{3,2,1,0:T(8,128)(2,1)}, u32[]{:S(2)}) copy-start(bf16[1,1,256,1024]{3,2,1,0:T(8,128)(2,1)} %param.8) | copy-start | bytes 1572868
  40.9 18.4 %collective-permute-start.4 = (bf16[912,256]{1,0:T(8,128)(2,1)S(1)}, bf16[912,256]{1,0:T(8,128)(2,1)S(1)}, u32[]{:S(2)}, u32[]{:S(2)}) collective-permute-start(bf16[912,256]{1,0:T(8,128)(2,1)S(1)} %get-tuple-element.20), channel_id=1, source_target_pairs={{0,4},{4,0},{8,12},{12,8},{1,5},{5,1},{9,13},{13,9},{2,6},{6,2},{1... | collective-permute-start | bytes 1400840 | tf_op jit(solution)/shard_map/ppermute | solution.py:26
  42.1 17.4 %collective-permute-start.5 = (bf16[912,256]{1,0:T(8,128)(2,1)S(1)}, bf16[912,256]{1,0:T(8,128)(2,1)S(1)}, u32[]{:S(2)}, u32[]{:S(2)}) collective-permute-start(bf16[912,256]{1,0:T(8,128)(2,1)S(1)} %get-tuple-element.21), channel_id=1, source_target_pairs={{0,8},{4,12},{8,0},{12,4},{1,9},{5,13},{9,1},{13,5},{2,10},{6,14},... | collective-permute-start | bytes 1400840 | tf_op jit(solution)/shard_map/ppermute | solution.py:26
  42.9 16.4 %collective-permute-start.6 = (bf16[528,256]{1,0:T(8,128)(2,1)S(1)}, bf16[528,256]{1,0:T(8,128)(2,1)S(1)}, u32[]{:S(2)}, u32[]{:S(2)}) collective-permute-start(bf16[528,256]{1,0:T(8,128)(2,1)S(1)} %get-tuple-element.22), channel_id=1, source_target_pairs={{0,12},{4,8},{8,4},{12,0},{1,13},{5,9},{9,5},{13,1},{2,14},{6,10},... | collective-permute-start | bytes 811016 | tf_op jit(solution)/shard_map/ppermute | solution.py:26

commit v2 on v0

v2 whole, which is shorter than its diff:
```python
import functools
import math

import jax
import jax.numpy as jnp
from jax import lax
from jax.experimental import pallas as pl
from jax.experimental.pallas import tpu as pltpu
from jax.sharding import PartitionSpec as P

DECAY = 0.75
DAMPING = 0.1
EPSILON = 1e-06
BF16 = jnp.bfloat16
F32 = jnp.float32
VMEM_LIMIT = 28 * 1024 * 1024


def passed_along(block, axis, distance):
    devices = range(lax.axis_size(axis))
    route = [((i - distance) % len(devices), i) for i in devices]
    return lax.ppermute(block, axis, route)


def swapped(block, offset):
    return lax.ppermute(block, "dp", [(i, i ^ offset) for i in range(lax.axis_size("dp"))])


def eye_of(rows, cols, shift=0):
    row_ids = lax.broadcasted_iota(jnp.int32, (rows, cols), 0) + shift
    col_ids = lax.broadcasted_iota(jnp.int32, (rows, cols), 1)
    return (row_ids == col_ids).astype(F32)


def whole(count):
    return [pl.BlockSpec(memory_space=pltpu.VMEM)] * count


def transposed(block):
    return block.astype(F32).T.astype(block.dtype)


def chunk_rows(share):
    half = share // 2
    return [0, half, half + half // 2] + [half + half // 2 + half * i for i in range(1, 4)]


def shared_half(owner, offset, share):
    other = owner ^ offset
    low, high = jnp.minimum(owner, other), jnp.maximum(owner, other)
    row = low * share + jnp.where(owner > other, share // 2, 0)
    return pl.multiple_of(row, share // 2), pl.multiple_of(high * share, share)


def products_kernel(replicas, tokens_all, acts, grads, relay_x, relay_y, direct_x, direct_y, keep, batch, grad_sum):
    order = acts.shape[1]
    share = order // replicas
    half = share // 2
    strip = grads.shape[1] // replicas
    starts = chunk_rows(share)
    length = relay_x.shape[0]
    mine = lax.axis_index("dp")
    over_rows = (((0,), (0,)), ((), ()))
    for i in range(replicas):
        band = slice(i * share, (i + 1) * share)
        batch[band, i * share :] = lax.dot_general(
            acts[:, band], acts[:, i * share :], over_rows, preferred_element_type=F32
        ) * (1.0 / tokens_all)
    grad_sum[...] = lax.dot_general(grads[...], acts[...], over_rows, preferred_element_type=F32) * (
        1.0 / math.sqrt(tokens_all)
    )

    def pieces(offset):
        owner = mine ^ offset
        base = pl.multiple_of(owner * share, share)
        corner = pl.multiple_of(owner * share + half, half)
        yield 0, batch[pl.ds(base, half), pl.ds(base, share)]
        low = batch[pl.ds(corner, half), pl.ds(corner, half)]
        yield starts[1], jnp.concatenate([low[0 : half // 2], low[half // 2 :]], axis=1)
        for step in range(1, replicas):
            row, col = shared_half(owner, step, share)
            yield starts[1 + step], batch[pl.ds(row, half), pl.ds(col, share)]
        rows = pl.ds(pl.multiple_of(owner * strip, strip), strip)
        for part in range(replicas):
            yield starts[-1] + part * strip, grad_sum[rows, part * share : (part + 1) * share]

    def store(offset, upper, lower):
        for start, piece in pieces(offset):
            stop = start + piece.shape[0]
            for target, low, high in ((upper, 0, length), (lower, length, 2 * length)):
                first, last = max(start, low), min(stop, high)
                if target is not None and first < last:
                    ref, at = target
                    ref[at + first - low : at + last - low, :] = piece[first - start : last - start].astype(ref.dtype)

    store(3, (relay_x, 0), (relay_y, 0))
    store(1, (direct_x, 0), (keep, 3 * length))
    store(2, (keep, 2 * length), (direct_y, 0))
    store(0, (keep, 0), (keep, length))


def relay_kernel(keep, got_x, got_y, send_x, send_y):
    length = send_x.shape[0]
    send_y[...] = (keep[2 * length : 3 * length, :] + got_x[...].astype(F32)).astype(BF16)
    send_x[...] = (keep[3 * length :, :] + got_y[...].astype(F32)).astype(BF16)


def factor_kernel(replicas, keep, direct_x, direct_y, relay_x, relay_y, old, upper, lower, exact):
    share, order = old.shape
    half = share // 2
    starts = chunk_rows(share)
    length = upper.shape[0]
    mine = lax.axis_index("dp")
    total = jnp.concatenate(
        [
            keep[0:length, :] + direct_x[...].astype(F32) + relay_y[...].astype(F32),
            keep[length : 2 * length, :] + direct_y[...].astype(F32) + relay_x[...].astype(F32),
        ],
        axis=0,
    )
    diagonal = old[:, pl.ds(pl.multiple_of(mine * share, share), share)]
    eye = eye_of(half, share)
    low_eye = eye_of(half, half)

    def packed(low):
        return jnp.concatenate([low[0 : half // 2], low[half // 2 :]], axis=1)

    terms = [
        DECAY * diagonal[0:half] + DAMPING * eye,
        packed(DECAY * diagonal[half:, half:] + DAMPING * low_eye),
    ]
    for step in range(1, replicas):
        other = mine ^ step
        block = old[:, pl.ds(pl.multiple_of(other * share, share), share)]
        terms.append(DECAY * jnp.where(mine < other, block[0:half], block[:, half:].T))
    column = lax.broadcasted_iota(jnp.int32, (1, share), 1)
    squares = jnp.zeros((1, share), F32)
    values = []
    for position, (start, term) in enumerate(zip(starts, terms)):
        value = term + (1.0 - DECAY) * total[start : start + term.shape[0]]
        exact[start : start + term.shape[0], :] = value
        summed = jnp.sum(value * value, axis=0, keepdims=True)
        if position == 0:
            summed = jnp.where(column < half, summed, 2.0 * summed)
        squares = squares + (summed if position < 2 else 2.0 * summed)
        values.append(value.astype(BF16))
    values.append(total[starts[-1] :].astype(BF16))
    high = squares.astype(BF16).astype(F32)
    middle = (squares - high).astype(BF16).astype(F32)
    rest = squares - high - middle
    spot = lax.broadcasted_iota(jnp.int32, (16, share), 0)
    digits = jnp.where(spot == 0, high, jnp.where(spot == 1, middle, jnp.where(spot == 2, rest, 0.0)))
    values.append(digits.astype(BF16))
    chunk = jnp.concatenate(values, axis=0)
    upper[...] = chunk[0:length]
    lower[...] = chunk[length:]


def root_kernel(replicas, count, exact, *rest):
    chunks = [rest[2 * i : 2 * i + 2] for i in range(replicas)]
    old_root, factor_out, root_out, step_out, factor, grads, diagonal, result = rest[2 * replicas :]
    share = root_out.shape[0]
    order = root_out.shape[1]
    half = share // 2
    strip = step_out.shape[0] // replicas
    starts = chunk_rows(share)
    length = chunks[0][0].shape[0]
    mine = lax.axis_index("dp")

    def rows_of(offset, start, count):
        upper, lower = chunks[offset]
        if start + count <= length:
            return upper[start : start + count, :]
        if start >= length:
            return lower[start - length : start - length + count, :]
        return jnp.concatenate([upper[start:, :], lower[0 : start + count - length, :]], axis=0)

    squares = jnp.zeros((16, share), F32)
    for offset in range(replicas):
        owner = mine ^ offset
        base = pl.multiple_of(owner * share, share)
        corner = pl.multiple_of(owner * share + half, half)
        top = rows_of(offset, 0, half)
        low = rows_of(offset, starts[1], half // 2)
        low = jnp.concatenate([low[:, 0:half], low[:, half:]], axis=0)
        factor[pl.ds(base, half), pl.ds(base, share)] = top
        factor[pl.ds(corner, half), pl.ds(base, half)] = transposed(top[:, half:])
        factor[pl.ds(corner, half), pl.ds(corner, half)] = low
        on_diagonal = low_eye = eye_of(half, half)
        diagonal[:, pl.ds(base, half)] = jnp.sum(
            top[:, 0:half].astype(F32) * on_diagonal, axis=0, keepdims=True
        )
        diagonal[:, pl.ds(corner, half)] = jnp.sum(low.astype(F32) * low_eye, axis=0, keepdims=True)
        for step in range(1, replicas):
            row, col = shared_half(owner, step, share)
            block = rows_of(offset, starts[1 + step], half)
            factor[pl.ds(row, half), pl.ds(col, share)] = block
            factor[pl.ds(col, share), pl.ds(row, half)] = transposed(block)
        for part in range(replicas):
            grads[offset * strip : (offset + 1) * strip, part * share : (part + 1) * share] = rows_of(
                offset, starts[-1] + part * strip, strip
            )
        squares = squares + rows_of(offset, starts[-1] + replicas * strip, 16).astype(F32)

    scale = jnp.sqrt(jnp.sum(squares, keepdims=True) / order + EPSILON)
    inverse = 1.0 / scale
    ones = diagonal[...] * inverse
    ones = ones.astype(BF16).astype(F32)
    lift = (1.5 - 0.5 * ones).astype(BF16).astype(F32) + 0.5 * (diagonal[...] * inverse)
    eye = eye_of(share, order, mine * share)
    my_rows = pl.ds(pl.multiple_of(mine * share, share), share)
    first = (factor[my_rows, :].astype(F32) * inverse).astype(BF16).astype(F32)
    turn = (1.5 * eye - 0.5 * first).astype(BF16)
    second = (jnp.dot(turn, factor[...], preferred_element_type=F32) * inverse).astype(BF16)
    product = (-0.5 * inverse) * jnp.dot(second, factor[...], preferred_element_type=F32) + second.astype(F32) * lift
    turn_two = (1.5 * eye - 0.5 * product).astype(BF16)
    inverse_rows = (-0.5 * inverse) * jnp.dot(
        turn_two, factor[...], preferred_element_type=F32
    ) + turn_two.astype(F32) * lift
    chosen = jnp.where(count[0, 0] == 1, turn.astype(F32), inverse_rows)
    root_out[...] = (chosen * lax.rsqrt(scale)).astype(BF16)

    result[...] = lax.dot_general(
        grads[...], old_root[...], (((1,), (1,)), ((), ())), preferred_element_type=F32
    ).astype(BF16)
    for offset in range(replicas):
        owner = mine ^ offset
        step_out[pl.ds(pl.multiple_of(owner * strip, strip), strip), :] = result[
            offset * strip : (offset + 1) * strip, :
        ]

    own_columns = pl.ds(pl.multiple_of(mine * share, share), share)
    top = exact[0:half, :]
    low = exact[starts[1] : starts[2], :]
    low = jnp.concatenate([low[:, 0:half], low[:, half:]], axis=0)
    factor_out[0:half, own_columns] = top
    factor_out[half:, own_columns] = jnp.concatenate([top[:, half:].T, low], axis=1)
    for step in range(1, replicas):
        other = mine ^ step
        columns = pl.ds(pl.multiple_of(other * share, share), share)
        own = exact[starts[1 + step] : starts[1 + step] + half, :]
        theirs = rows_of(step, starts[1 + step], half).astype(F32)

        @pl.when(mine < other)
        def _():
            factor_out[0:half, columns] = own
            factor_out[half:, columns] = theirs

        @pl.when(mine > other)
        def _():
            factor_out[:, columns] = jnp.concatenate([theirs.T, own.T], axis=1)


def square_plan(acts, out_grad, old_factor, old_root, iter_count):
    replicas = lax.axis_size("dp")
    inputs = acts[0]
    tokens_all = inputs.shape[0] * replicas
    order = inputs.shape[1]
    share = order // replicas
    grows = out_grad.shape[2]
    params = pltpu.CompilerParams(vmem_limit_bytes=VMEM_LIMIT)
    whole_rows = chunk_rows(share)[-1] + grows
    length = whole_rows // 2
    piece = jax.ShapeDtypeStruct((length, share), BF16)

    received = passed_along(out_grad, "pipe", -1)[0]
    relay_x, relay_y, direct_x, direct_y, keep = pl.pallas_call(
        functools.partial(products_kernel, replicas, tokens_all),
        out_shape=[piece] * 4 + [jax.ShapeDtypeStruct((4 * length, share), F32)],
        in_specs=whole(2),
        out_specs=whole(5),
        scratch_shapes=[pltpu.VMEM((order, order), F32), pltpu.VMEM((grows, order), F32)],
        compiler_params=params,
        name="products",
    )(inputs, received)
    relay_x, relay_y = swapped(relay_x, 1), swapped(relay_y, 2)
    direct_x, direct_y = swapped(direct_x, 1), swapped(direct_y, 2)
    relay_x, relay_y = pl.pallas_call(
        relay_kernel,
        out_shape=[piece] * 2,
        in_specs=whole(3),
        out_specs=whole(2),
        compiler_params=params,
        name="relay",
    )(keep, relay_x, relay_y)
    relay_x, relay_y = swapped(relay_x, 1), swapped(relay_y, 2)
    upper, lower, exact = pl.pallas_call(
        functools.partial(factor_kernel, replicas),
        out_shape=[
            piece,
            jax.ShapeDtypeStruct((length + 16, share), BF16),
            jax.ShapeDtypeStruct((chunk_rows(share)[-1], share), F32),
        ],
        in_specs=whole(6),
        out_specs=whole(3),
        compiler_params=params,
        name="factor",
    )(keep, direct_x, direct_y, relay_x, relay_y, old_factor[0, 0])
    upper_x, lower_y = swapped(upper, 1), swapped(lower, 2)
    lower_x, upper_y = swapped(lower, 1), swapped(upper, 2)
    upper_far, lower_far = swapped(upper_x, 2), swapped(lower_y, 1)
    factor, root, step = pl.pallas_call(
        functools.partial(root_kernel, replicas),
        out_shape=[
            jax.ShapeDtypeStruct((share, order), F32),
            jax.ShapeDtypeStruct((share, order), BF16),
            jax.ShapeDtypeStruct((grows, share), BF16),
        ],
        in_specs=[pl.BlockSpec(memory_space=pltpu.SMEM)] + whole(2 * replicas + 2),
        out_specs=whole(3),
        scratch_shapes=[
            pltpu.VMEM((order, order), BF16),
            pltpu.VMEM((grows, order), BF16),
            pltpu.VMEM((1, order), F32),
            pltpu.VMEM((grows, share), BF16),
        ],
        compiler_params=params,
        name="root",
    )(iter_count, exact, upper, lower, upper_x, lower_x, upper_y, lower_y, upper_far, lower_far, old_root[0, 0])
    return (factor[None, None], root[None, None], step[None, None])


def ring_plan(acts, out_grad, old_factor, old_root, iter_count):
    inputs = acts[0]
    replicas = lax.axis_size("dp")
    tokens_all = inputs.shape[0] * replicas
    order = inputs.shape[1]
    share = order // replicas
    offset = lax.axis_index("dp") * share
    received = passed_along(out_grad, "pipe", -1)[0]
    partial_grad = jnp.dot(received.T, inputs, preferred_element_type=F32) / math.sqrt(tokens_all)
    batch = lax.psum_scatter(
        jnp.dot(inputs.T, inputs, preferred_element_type=F32) / tokens_all,
        "dp",
        scatter_dimension=0,
        tiled=True,
    )
    eye_rows = eye_of(share, order, offset)
    factor = DECAY * old_factor[0, 0] + (1.0 - DECAY) * batch + DAMPING * eye_rows
    grad16 = lax.psum(partial_grad, "dp").astype(BF16)
    scale = jnp.sqrt(lax.psum(jnp.sum(factor * factor), "dp") / order + EPSILON)
    step = lax.dot_general(
        grad16, old_root[0, 0], (((1,), (1,)), ((), ())), preferred_element_type=F32
    ).astype(BF16)
    first = lax.all_gather((factor / scale).astype(BF16), "dp", axis=0, tiled=True)
    turn_one = (1.5 * eye_of(order, order) - 0.5 * first.astype(F32)).astype(BF16)
    turn_rows = lax.dynamic_slice_in_dim(turn_one, offset, share, 0)
    second = jnp.dot(turn_rows, first, preferred_element_type=F32).astype(BF16)
    product = jnp.dot(second, turn_one, preferred_element_type=F32)
    turn_two = (1.5 * eye_rows - 0.5 * product).astype(BF16)
    inverse_rows = jnp.dot(turn_two, turn_one, preferred_element_type=F32)
    chosen = jnp.where(iter_count[0, 0] == 1, turn_rows.astype(F32), inverse_rows)
    root = (chosen / jnp.sqrt(scale)).astype(BF16)
    return (factor[None, None], root[None, None], step[None, None])


def solution(mesh):
    return jax.shard_map(
        square_plan if mesh.shape["dp"] == 4 else ring_plan,
        mesh=mesh,
        in_specs=(
            P("pipe", "dp", "tensor"),
            P("pipe", "dp", "tensor"),
            P("pipe", "tensor", "dp", None),
            P("pipe", "tensor", "dp", None),
            P("pipe", "tensor"),
        ),
        out_specs=(
            P("pipe", "tensor", "dp", None),
            P("pipe", "tensor", "dp", None),
            P("pipe", "tensor", None, "dp"),
        ),
        check_vma=False,
    )
```

time: 199 us -> 45.9 us (0.23)
  waiting for transfers between devices: 121 us -> 23.2 us
  blocking collectives: 42.7 us -> 0 us
  between operations: 15.2 us -> 1.31 us
  starting transfers between devices: 0.63 us -> 13.9 us
  matrix products: 11.8 us -> 0 us
  Pallas kernels: 0 us -> 6.06 us
  other arithmetic: 5.71 us -> 0 us
    all_gather x2 -> x0, waiting for transfers between devices: 66.7 us -> none  [the longest x1 35.1 us: local(): first_full = lax.all_gather(first_rows, 'dp', axis=0, tiled=True)]
    reduce_scatter x1 -> x0, waiting for transfers between devices: 53.4 us -> none  [local(): lax.psum_scatter(jnp.dot(columns.T, inputs, preferred_element_type=jnp.fl...]
    psum x1 -> x0, blocking collectives: 42.7 us -> none  [local(): square_total = lax.psum(squares, 'dp')]
    ppermute x0 -> x12, waiting for transfers between devices: none -> 21.9 us  [swapped(): lax.ppermute(block, 'dp', [(i, i ^ offset) for i in range(lax.axis_size('...]
    ppermute x0 -> x12, starting transfers between devices: none -> 13.4 us  [swapped(): lax.ppermute(block, 'dp', [(i, i ^ offset) for i in range(lax.axis_size('...]
    dot_general x5 -> x0, matrix products: 11.8 us -> none  [the longest x1 3.76 us: local(): jnp.dot(turn_two, turn_one, preferred_element_type=jnp.float32)]
    pallas_call x0 -> x4, Pallas kernels: none -> 6.06 us  [the longest x1 4.2 us: square_plan(): pl.pallas_call(functools.partial(root_kernel, replicas), out_shape=[jax.S...]
    convert_element_type x2 -> x0, other arithmetic: 3.06 us -> none  [the longest x1 2.15 us: local(): (1.5 * eye_full - 0.5 * first_full.astype(jnp.float32)).astype(jnp.bfloat16)]
  transfers between devices with their start and end apart: 4 -> 13, of which waited for: 4 -> 12; matrix products, arithmetic and copies ran while one was open for 2% -> 0% of each run, Pallas kernels for 0% -> 0%
where the time goes in v2:
time: 45.9 us; the launch traced here: 45.7 us
  waiting for transfers between devices  23.2 us (51%)
  starting transfers between devices  13.9 us (30%)
  Pallas kernels  6.06 us (13%)
  between operations  1.31 us (3%)
  local copies, waits for them, and re-layouts  1.23 us (3%)
    ppermute x12, waiting for transfers between devices, swapped(): lax.ppermute(block, 'dp', [(i, i ^ offset) for i in range(lax.axis_size('...  21.9 us
    ppermute x12, starting transfers between devices, swapped(): lax.ppermute(block, 'dp', [(i, i ^ offset) for i in range(lax.axis_size('...  13.4 us
    pallas_call x1, Pallas kernels, square_plan(): pl.pallas_call(functools.partial(root_kernel, replicas), out_shape=[jax.S...  4.2 us
    pallas_call x1, Pallas kernels, square_plan(): pl.pallas_call(functools.partial(products_kernel, replicas, tokens_all),...  1.41 us
    ppermute x1, waiting for transfers between devices, passed_along(): return lax.ppermute(block, axis, route)  1.37 us
    unnamed x6, local copies, waits for them, and re-layouts  1.23 us
  transfers between devices with their start and end apart: 13, of which 12 were waited for; matrix products, arithmetic and copies ran while one was open for 0% of the time, Pallas kernels for 0%

profile of v2, /device:TPU:0, one launch (start us, length us, event | category | flops | bytes accessed | tf_op | source)
XLA Modules:
  0.0 45.7 jit_solution(2245656930607087575)
XLA Ops:
  0.6 0.5 %collective-permute-start = (bf16[1,512,256]{2,1,0:T(8,128)(2,1)}, bf16[1,512,256]{2,1,0:T(8,128)(2,1)S(1)}, u32[]{:S(2)}, u32[]{:S(2)}) collective-permute-start(bf16[1,512,256]{2,1,0:T(8,128)(2,1)} %param.6), channel_id=1, source_target_pairs={{16,0},{0,16},{17,1},{1,17},{18,2},{2,18},{19,3},{3,19},{20,4},{4,... | collective-permute-start | bytes 786440 | tf_op jit(solution)/shard_map/ppermute | solution.py:22
  1.1 1.4 %collective-permute-done = bf16[1,512,256]{2,1,0:T(8,128)(2,1)S(1)} collective-permute-done((bf16[1,512,256]{2,1,0:T(8,128)(2,1)}, bf16[1,512,256]{2,1,0:T(8,128)(2,1)S(1)}, u32[]{:S(2)}, u32[]{:S(2)}) %collective-permute-start) | collective-permute-done | bytes 262176 | tf_op jit(solution)/shard_map/ppermute | solution.py:22
  2.5 0.0 copy-start.1
  2.5 1.2 %copy-done.1 = bf16[1,512,1024]{2,1,0:T(8,128)(2,1)S(1)} copy-done((bf16[1,512,1024]{2,1,0:T(8,128)(2,1)S(1)}, bf16[1,512,1024]{2,1,0:T(8,128)(2,1)}, u32[]{:S(2)}) %copy-start.1) | copy-done | bytes 1048600
  3.7 0.0 copy-start
  3.7 1.4 %products.1 = (bf16[416,256]{1,0:T(8,128)(2,1)S(1)}, bf16[416,256]{1,0:T(8,128)(2,1)S(1)}, bf16[416,256]{1,0:T(8,128)(2,1)S(1)}, bf16[416,256]{1,0:T(8,128)(2,1)S(1)}, f32[1664,256]{1,0:T(8,128)S(1)}) custom-call(bf16[512,1024]{1,0:T(8,128)(2,1)S(1)} %bitcast.8, bf16[512,256]{1,0:T(8,128)(2,1)S(1)} %bitcast.10), custom_call_target="tpu_custom_call" | custom-call | tf_op jit(solution)/shard_map/products/pallas_call | solution.py:267
  5.2 2.9 %collective-permute-start.3 = (bf16[416,256]{1,0:T(8,128)(2,1)S(1)}, bf16[416,256]{1,0:T(8,128)(2,1)S(1)}, u32[]{:S(2)}, u32[]{:S(2)}) collective-permute-start(bf16[416,256]{1,0:T(8,128)(2,1)S(1)} %get-tuple-element.19), channel_id=1, source_target_pairs={{0,4},{4,0},{8,12},{12,8},{1,5},{5,1},{9,13},{13,9},{2,6},{6,2},{1... | collective-permute-start | bytes 638984 | tf_op jit(solution)/shard_map/ppermute | solution.py:26
  8.1 1.5 %collective-permute-start.4 = (bf16[416,256]{1,0:T(8,128)(2,1)S(1)}, bf16[416,256]{1,0:T(8,128)(2,1)S(1)}, u32[]{:S(2)}, u32[]{:S(2)}) collective-permute-start(bf16[416,256]{1,0:T(8,128)(2,1)S(1)} %get-tuple-element.20), channel_id=1, source_target_pairs={{0,8},{4,12},{8,0},{12,4},{1,9},{5,13},{9,1},{13,5},{2,10},{6,14},... | collective-permute-start | bytes 638984 | tf_op jit(solution)/shard_map/ppermute | solution.py:26
  9.6 0.5 %collective-permute-start.1 = (bf16[416,256]{1,0:T(8,128)(2,1)S(1)}, bf16[416,256]{1,0:T(8,128)(2,1)S(1)}, u32[]{:S(2)}, u32[]{:S(2)}) collective-permute-start(bf16[416,256]{1,0:T(8,128)(2,1)S(1)} %get-tuple-element.17), channel_id=1, source_target_pairs={{0,4},{4,0},{8,12},{12,8},{1,5},{5,1},{9,13},{13,9},{2,6},{6,2},{1... | collective-permute-start | bytes 638984 | tf_op jit(solution)/shard_map/ppermute | solution.py:26
  10.2 0.1 collective-permute-start.2
  10.2 3.9 %collective-permute-done.3.got_x = bf16[416,256]{1,0:T(8,128)(2,1)S(1)} collective-permute-done((bf16[416,256]{1,0:T(8,128)(2,1)S(1)}, bf16[416,256]{1,0:T(8,128)(2,1)S(1)}, u32[]{:S(2)}, u32[]{:S(2)}) %collective-permute-start.3) | collective-permute-done | bytes 213024 | tf_op jit(solution)/shard_map/ppermute | solution.py:26
  14.2 2.1 %collective-permute-done.4.got_y = bf16[416,256]{1,0:T(8,128)(2,1)S(1)} collective-permute-done((bf16[416,256]{1,0:T(8,128)(2,1)S(1)}, bf16[416,256]{1,0:T(8,128)(2,1)S(1)}, u32[]{:S(2)}, u32[]{:S(2)}) %collective-permute-start.4) | collective-permute-done | bytes 213024 | tf_op jit(solution)/shard_map/ppermute | solution.py:26
  16.2 0.1 relay.1
  16.3 0.1 collective-permute-start.5
  16.5 2.0 %collective-permute-start.6 = (bf16[416,256]{1,0:T(8,128)(2,1)S(1)}, bf16[416,256]{1,0:T(8,128)(2,1)S(1)}, u32[]{:S(2)}, u32[]{:S(2)}) collective-permute-start(bf16[416,256]{1,0:T(8,128)(2,1)S(1)} %get-tuple-element.22), channel_id=1, source_target_pairs={{0,8},{4,12},{8,0},{12,4},{1,9},{5,13},{9,1},{13,5},{2,10},{6,14},... | collective-permute-start | bytes 638984 | tf_op jit(solution)/shard_map/ppermute | solution.py:26
  18.5 0.3 collective-permute-done.1.direct_x
  18.7 2.1 %collective-permute-done.2.direct_y = bf16[416,256]{1,0:T(8,128)(2,1)S(1)} collective-permute-done((bf16[416,256]{1,0:T(8,128)(2,1)S(1)}, bf16[416,256]{1,0:T(8,128)(2,1)S(1)}, u32[]{:S(2)}, u32[]{:S(2)}) %collective-permute-start.2) | collective-permute-done | bytes 213024 | tf_op jit(solution)/shard_map/ppermute | solution.py:26
  20.8 2.0 %collective-permute-done.5.relay_x = bf16[416,256]{1,0:T(8,128)(2,1)S(1)} collective-permute-done((bf16[416,256]{1,0:T(8,128)(2,1)S(1)}, bf16[416,256]{1,0:T(8,128)(2,1)S(1)}, u32[]{:S(2)}, u32[]{:S(2)}) %collective-permute-start.5) | collective-permute-done | bytes 213024 | tf_op jit(solution)/shard_map/ppermute | solution.py:26
  22.8 1.5 %collective-permute-done.6.relay_y = bf16[416,256]{1,0:T(8,128)(2,1)S(1)} collective-permute-done((bf16[416,256]{1,0:T(8,128)(2,1)S(1)}, bf16[416,256]{1,0:T(8,128)(2,1)S(1)}, u32[]{:S(2)}, u32[]{:S(2)}) %collective-permute-start.6) | collective-permute-done | bytes 213024 | tf_op jit(solution)/shard_map/ppermute | solution.py:26
  24.3 0.0 copy-done
  24.3 0.0 copy-start.2
  24.3 0.3 factor.1
  24.6 1.6 %collective-permute-start.10 = (bf16[432,256]{1,0:T(8,128)(2,1)S(1)}, bf16[432,256]{1,0:T(8,128)(2,1)S(1)}, u32[]{:S(2)}, u32[]{:S(2)}) collective-permute-start(bf16[432,256]{1,0:T(8,128)(2,1)S(1)} %get-tuple-element.25.rest_1_), channel_id=1, source_target_pairs={{0,8},{4,12},{8,0},{12,4},{1,9},{5,13},{9,1},{13,5},{2,10},{6,14},... | collective-permute-start | bytes 663560 | tf_op jit(solution)/shard_map/ppermute | solution.py:26
  26.2 0.5 %collective-permute-start.7 = (bf16[416,256]{1,0:T(8,128)(2,1)S(1)}, bf16[416,256]{1,0:T(8,128)(2,1)S(1)}, u32[]{:S(2)}, u32[]{:S(2)}) collective-permute-start(bf16[416,256]{1,0:T(8,128)(2,1)S(1)} %get-tuple-element.24.rest_0_), channel_id=1, source_target_pairs={{0,4},{4,0},{8,12},{12,8},{1,5},{5,1},{9,13},{13,9},{2,6},{6,2},{1... | collective-permute-start | bytes 638984 | tf_op jit(solution)/shard_map/ppermute | solution.py:26
  26.7 1.5 %collective-permute-start.8 = (bf16[432,256]{1,0:T(8,128)(2,1)S(1)}, bf16[432,256]{1,0:T(8,128)(2,1)S(1)}, u32[]{:S(2)}, u32[]{:S(2)}) collective-permute-start(bf16[432,256]{1,0:T(8,128)(2,1)S(1)} %get-tuple-element.25.rest_1_), channel_id=1, source_target_pairs={{0,4},{4,0},{8,12},{12,8},{1,5},{5,1},{9,13},{13,9},{2,6},{6,2},{1... | collective-permute-start | bytes 663560 | tf_op jit(solution)/shard_map/ppermute | solution.py:26
  28.2 2.8 %collective-permute-done.10.rest_5_ = bf16[432,256]{1,0:T(8,128)(2,1)S(1)} collective-permute-done((bf16[432,256]{1,0:T(8,128)(2,1)S(1)}, bf16[432,256]{1,0:T(8,128)(2,1)S(1)}, u32[]{:S(2)}, u32[]{:S(2)}) %collective-permute-start.10) | collective-permute-done | bytes 221216 | tf_op jit(solution)/shard_map/ppermute | solution.py:26
  31.0 0.6 %collective-permute-start.12 = (bf16[432,256]{1,0:T(8,128)(2,1)S(1)}, bf16[432,256]{1,0:T(8,128)(2,1)S(1)}, u32[]{:S(2)}, u32[]{:S(2)}) collective-permute-start(bf16[432,256]{1,0:T(8,128)(2,1)S(1)} %collective-permute-done.10.rest_5_), channel_id=1, source_target_pairs={{0,4},{4,0},{8,12},{12,8},{1,5},{5,1},{9,13},{13,9},{2,6},{6,2},{1... | collective-permute-start | bytes 663560 | tf_op jit(solution)/shard_map/ppermute | solution.py:26
  31.6 1.5 %collective-permute-start.9 = (bf16[416,256]{1,0:T(8,128)(2,1)S(1)}, bf16[416,256]{1,0:T(8,128)(2,1)S(1)}, u32[]{:S(2)}, u32[]{:S(2)}) collective-permute-start(bf16[416,256]{1,0:T(8,128)(2,1)S(1)} %get-tuple-element.24.rest_0_), channel_id=1, source_target_pairs={{0,8},{4,12},{8,0},{12,4},{1,9},{5,13},{9,1},{13,5},{2,10},{6,14},... | collective-permute-start | bytes 638984 | tf_op jit(solution)/shard_map/ppermute | solution.py:26
  33.1 1.3 %collective-permute-done.7.rest_2_ = bf16[416,256]{1,0:T(8,128)(2,1)S(1)} collective-permute-done((bf16[416,256]{1,0:T(8,128)(2,1)S(1)}, bf16[416,256]{1,0:T(8,128)(2,1)S(1)}, u32[]{:S(2)}, u32[]{:S(2)}) %collective-permute-start.7) | collective-permute-done | bytes 213024 | tf_op jit(solution)/shard_map/ppermute | solution.py:26
  34.4 0.5 %collective-permute-start.11 = (bf16[416,256]{1,0:T(8,128)(2,1)S(1)}, bf16[416,256]{1,0:T(8,128)(2,1)S(1)}, u32[]{:S(2)}, u32[]{:S(2)}) collective-permute-start(bf16[416,256]{1,0:T(8,128)(2,1)S(1)} %collective-permute-done.7.rest_2_), channel_id=1, source_target_pairs={{0,8},{4,12},{8,0},{12,4},{1,9},{5,13},{9,1},{13,5},{2,10},{6,14},... | collective-permute-start | bytes 638984 | tf_op jit(solution)/shard_map/ppermute | solution.py:26
  35.5 3.5 %collective-permute-done.9.rest_4_ = bf16[416,256]{1,0:T(8,128)(2,1)S(1)} collective-permute-done((bf16[416,256]{1,0:T(8,128)(2,1)S(1)}, bf16[416,256]{1,0:T(8,128)(2,1)S(1)}, u32[]{:S(2)}, u32[]{:S(2)}) %collective-permute-start.9) | collective-permute-done | bytes 213024 | tf_op jit(solution)/shard_map/ppermute | solution.py:26
  39.1 0.0 collective-permute-done.8.rest_3_
  39.1 2.2 %collective-permute-done.11.rest_6_ = bf16[416,256]{1,0:T(8,128)(2,1)S(1)} collective-permute-done((bf16[416,256]{1,0:T(8,128)(2,1)S(1)}, bf16[416,256]{1,0:T(8,128)(2,1)S(1)}, u32[]{:S(2)}, u32[]{:S(2)}) %collective-permute-start.11) | collective-permute-done | bytes 213024 | tf_op jit(solution)/shard_map/ppermute | solution.py:26
  41.4 0.2 collective-permute-done.12.rest_7_
  41.5 0.0 copy-done.2
  41.5 4.2 %root.1 = (f32[256,1024]{1,0:T(8,128)}, bf16[256,1024]{1,0:T(8,128)(2,1)}, bf16[256,256]{1,0:T(8,128)(2,1)}) custom-call(s32[1,1]{1,0:T(1,128)S(6)} %copy.8.count, f32[576,256]{1,0:T(8,128)S(1)} %get-tuple-element.23.exact, bf16[416,256]{1,0:T(8,128)(2,1)S(1)} %get-tuple-element.24.rest_0_, bf16[432,256]{1,0:T(8,128)(2,1)S(1)} %get-tuple-element.25.rest_1_, ...), custom_call_target="tpu_custom_call" | custom-call | tf_op jit(solution)/shard_map/root/pallas_call | solution.py:302
Async XLA Ops:
  0.6 1.9 %collective-permute-start = (bf16[1,512,256]{2,1,0:T(8,128)(2,1)}, bf16[1,512,256]{2,1,0:T(8,128)(2,1)S(1)}, u32[]{:S(2)}, u32[]{:S(2)}) collective-permute-start(bf16[1,512,256]{2,1,0:T(8,128)(2,1)} %param.6), channel_id=1, source_target_pairs={{16,0},{0,16},{17,1},{1,17},{18,2},{2,18},{19,3},{3,19},{20,4},{4,... | collective-permute-start | bytes 786440 | tf_op jit(solution)/shard_map/ppermute | solution.py:22
  2.5 1.2 %copy-start.1 = (bf16[1,512,1024]{2,1,0:T(8,128)(2,1)S(1)}, bf16[1,512,1024]{2,1,0:T(8,128)(2,1)}, u32[]{:S(2)}) copy-start(bf16[1,512,1024]{2,1,0:T(8,128)(2,1)} %param.5) | copy-start | bytes 3145732
  3.7 20.5 %copy-start = (f32[1,1,256,1024]{3,2,1,0:T(8,128)S(1)}, f32[1,1,256,1024]{3,2,1,0:T(8,128)}, u32[]{:S(2)}) copy-start(f32[1,1,256,1024]{3,2,1,0:T(8,128)} %param.7) | copy-start | bytes 3145732
  5.2 9.0 %collective-permute-start.3 = (bf16[416,256]{1,0:T(8,128)(2,1)S(1)}, bf16[416,256]{1,0:T(8,128)(2,1)S(1)}, u32[]{:S(2)}, u32[]{:S(2)}) collective-permute-start(bf16[416,256]{1,0:T(8,128)(2,1)S(1)} %get-tuple-element.19), channel_id=1, source_target_pairs={{0,4},{4,0},{8,12},{12,8},{1,5},{5,1},{9,13},{13,9},{2,6},{6,2},{1... | collective-permute-start | bytes 638984 | tf_op jit(solution)/shard_map/ppermute | solution.py:26
  8.1 8.1 %collective-permute-start.4 = (bf16[416,256]{1,0:T(8,128)(2,1)S(1)}, bf16[416,256]{1,0:T(8,128)(2,1)S(1)}, u32[]{:S(2)}, u32[]{:S(2)}) collective-permute-start(bf16[416,256]{1,0:T(8,128)(2,1)S(1)} %get-tuple-element.20), channel_id=1, source_target_pairs={{0,8},{4,12},{8,0},{12,4},{1,9},{5,13},{9,1},{13,5},{2,10},{6,14},... | collective-permute-start | bytes 638984 | tf_op jit(solution)/shard_map/ppermute | solution.py:26
  9.6 9.1 %collective-permute-start.1 = (bf16[416,256]{1,0:T(8,128)(2,1)S(1)}, bf16[416,256]{1,0:T(8,128)(2,1)S(1)}, u32[]{:S(2)}, u32[]{:S(2)}) collective-permute-start(bf16[416,256]{1,0:T(8,128)(2,1)S(1)} %get-tuple-element.17), channel_id=1, source_target_pairs={{0,4},{4,0},{8,12},{12,8},{1,5},{5,1},{9,13},{13,9},{2,6},{6,2},{1... | collective-permute-start | bytes 638984 | tf_op jit(solution)/shard_map/ppermute | solution.py:26
  10.2 10.7 %collective-permute-start.2 = (bf16[416,256]{1,0:T(8,128)(2,1)S(1)}, bf16[416,256]{1,0:T(8,128)(2,1)S(1)}, u32[]{:S(2)}, u32[]{:S(2)}) collective-permute-start(bf16[416,256]{1,0:T(8,128)(2,1)S(1)} %get-tuple-element.18), channel_id=1, source_target_pairs={{0,8},{4,12},{8,0},{12,4},{1,9},{5,13},{9,1},{13,5},{2,10},{6,14},... | collective-permute-start | bytes 638984 | tf_op jit(solution)/shard_map/ppermute | solution.py:26
  16.3 6.5 %collective-permute-start.5 = (bf16[416,256]{1,0:T(8,128)(2,1)S(1)}, bf16[416,256]{1,0:T(8,128)(2,1)S(1)}, u32[]{:S(2)}, u32[]{:S(2)}) collective-permute-start(bf16[416,256]{1,0:T(8,128)(2,1)S(1)} %get-tuple-element.21), channel_id=1, source_target_pairs={{0,4},{4,0},{8,12},{12,8},{1,5},{5,1},{9,13},{13,9},{2,6},{6,2},{1... | collective-permute-start | bytes 638984 | tf_op jit(solution)/shard_map/ppermute | solution.py:26
  16.5 7.8 %collective-permute-start.6 = (bf16[416,256]{1,0:T(8,128)(2,1)S(1)}, bf16[416,256]{1,0:T(8,128)(2,1)S(1)}, u32[]{:S(2)}, u32[]{:S(2)}) collective-permute-start(bf16[416,256]{1,0:T(8,128)(2,1)S(1)} %get-tuple-element.22), channel_id=1, source_target_pairs={{0,8},{4,12},{8,0},{12,4},{1,9},{5,13},{9,1},{13,5},{2,10},{6,14},... | collective-permute-start | bytes 638984 | tf_op jit(solution)/shard_map/ppermute | solution.py:26
  24.3 17.3 %copy-start.2 = (bf16[1,1,256,1024]{3,2,1,0:T(8,128)(2,1)S(1)}, bf16[1,1,256,1024]{3,2,1,0:T(8,128)(2,1)}, u32[]{:S(2)}) copy-start(bf16[1,1,256,1024]{3,2,1,0:T(8,128)(2,1)} %param.8) | copy-start | bytes 1572868
  24.6 6.4 %collective-permute-start.10 = (bf16[432,256]{1,0:T(8,128)(2,1)S(1)}, bf16[432,256]{1,0:T(8,128)(2,1)S(1)}, u32[]{:S(2)}, u32[]{:S(2)}) collective-permute-start(bf16[432,256]{1,0:T(8,128)(2,1)S(1)} %get-tuple-element.25.rest_1_), channel_id=1, source_target_pairs={{0,8},{4,12},{8,0},{12,4},{1,9},{5,13},{9,1},{13,5},{2,10},{6,14},... | collective-permute-start | bytes 663560 | tf_op jit(solution)/shard_map/ppermute | solution.py:26
  26.2 8.2 %collective-permute-start.7 = (bf16[416,256]{1,0:T(8,128)(2,1)S(1)}, bf16[416,256]{1,0:T(8,128)(2,1)S(1)}, u32[]{:S(2)}, u32[]{:S(2)}) collective-permute-start(bf16[416,256]{1,0:T(8,128)(2,1)S(1)} %get-tuple-element.24.rest_0_), channel_id=1, source_target_pairs={{0,4},{4,0},{8,12},{12,8},{1,5},{5,1},{9,13},{13,9},{2,6},{6,2},{1... | collective-permute-start | bytes 638984 | tf_op jit(solution)/shard_map/ppermute | solution.py:26
  26.7 12.4 %collective-permute-start.8 = (bf16[432,256]{1,0:T(8,128)(2,1)S(1)}, bf16[432,256]{1,0:T(8,128)(2,1)S(1)}, u32[]{:S(2)}, u32[]{:S(2)}) collective-permute-start(bf16[432,256]{1,0:T(8,128)(2,1)S(1)} %get-tuple-element.25.rest_1_), channel_id=1, source_target_pairs={{0,4},{4,0},{8,12},{12,8},{1,5},{5,1},{9,13},{13,9},{2,6},{6,2},{1... | collective-permute-start | bytes 663560 | tf_op jit(solution)/shard_map/ppermute | solution.py:26
  31.0 10.5 %collective-permute-start.12 = (bf16[432,256]{1,0:T(8,128)(2,1)S(1)}, bf16[432,256]{1,0:T(8,128)(2,1)S(1)}, u32[]{:S(2)}, u32[]{:S(2)}) collective-permute-start(bf16[432,256]{1,0:T(8,128)(2,1)S(1)} %collective-permute-done.10.rest_5_), channel_id=1, source_target_pairs={{0,4},{4,0},{8,12},{12,8},{1,5},{5,1},{9,13},{13,9},{2,6},{6,2},{1... | collective-permute-start | bytes 663560 | tf_op jit(solution)/shard_map/ppermute | solution.py:26
  31.6 7.5 %collective-permute-start.9 = (bf16[416,256]{1,0:T(8,128)(2,1)S(1)}, bf16[416,256]{1,0:T(8,128)(2,1)S(1)}, u32[]{:S(2)}, u32[]{:S(2)}) collective-permute-start(bf16[416,256]{1,0:T(8,128)(2,1)S(1)} %get-tuple-element.24.rest_0_), channel_id=1, source_target_pairs={{0,8},{4,12},{8,0},{12,4},{1,9},{5,13},{9,1},{13,5},{2,10},{6,14},... | collective-permute-start | bytes 638984 | tf_op jit(solution)/shard_map/ppermute | solution.py:26
  34.4 7.0 %collective-permute-start.11 = (bf16[416,256]{1,0:T(8,128)(2,1)S(1)}, bf16[416,256]{1,0:T(8,128)(2,1)S(1)}, u32[]{:S(2)}, u32[]{:S(2)}) collective-permute-start(bf16[416,256]{1,0:T(8,128)(2,1)S(1)} %collective-permute-done.7.rest_2_), channel_id=1, source_target_pairs={{0,8},{4,12},{8,0},{12,4},{1,9},{5,13},{9,1},{13,5},{2,10},{6,14},... | collective-permute-start | bytes 638984 | tf_op jit(solution)/shard_map/ppermute | solution.py:26

commit v3 on v2

--- a/solution.py
+++ b/solution.py
@@ -52,23 +52,28 @@
     return pl.multiple_of(row, share // 2), pl.multiple_of(high * share, share)
 
 
-def products_kernel(replicas, tokens_all, acts, grads, relay_x, relay_y, direct_x, direct_y, keep, batch, grad_sum):
+def store_chunk(pieces, length, upper, lower):
+    for start, piece in pieces:
+        stop = start + piece.shape[0]
+        for target, low, high in ((upper, 0, length), (lower, length, stop)):
+            first, last = max(start, low), min(stop, high)
+            if target is not None and first < last:
+                ref, at = target
+                ref[at + first - low : at + last - low, :] = piece[first - start : last - start].astype(ref.dtype)
+
+
+def batch_kernel(replicas, tokens_all, acts, relay_x, relay_y, direct_x, direct_y, keep, batch):
     order = acts.shape[1]
     share = order // replicas
     half = share // 2
-    strip = grads.shape[1] // replicas
     starts = chunk_rows(share)
     length = relay_x.shape[0]
     mine = lax.axis_index("dp")
-    over_rows = (((0,), (0,)), ((), ()))
     for i in range(replicas):
         band = slice(i * share, (i + 1) * share)
         batch[band, i * share :] = lax.dot_general(
-            acts[:, band], acts[:, i * share :], over_rows, preferred_element_type=F32
+            acts[:, band], acts[:, i * share :], (((0,), (0,)), ((), ())), preferred_element_type=F32
         ) * (1.0 / tokens_all)
-    grad_sum[...] = lax.dot_general(grads[...], acts[...], over_rows, preferred_element_type=F32) * (
-        1.0 / math.sqrt(tokens_all)
-    )
 
     def pieces(offset):
         owner = mine ^ offset
@@ -80,29 +85,54 @@
         for step in range(1, replicas):
             row, col = shared_half(owner, step, share)
             yield starts[1 + step], batch[pl.ds(row, half), pl.ds(col, share)]
-        rows = pl.ds(pl.multiple_of(owner * strip, strip), strip)
+
+    store_chunk(pieces(3), length, (relay_x, 0), (relay_y, 0))
+    store_chunk(pieces(1), length, (direct_x, 0), (keep, 3 * length))
+    store_chunk(pieces(2), length, (keep, 2 * length), (direct_y, 0))
+    store_chunk(pieces(0), length, (keep, 0), (keep, length))
+
+
+def grad_kernel(replicas, tokens_all, acts, grads, send_x, send_y, keep, total):
+    order = acts.shape[1]
+    share = order // replicas
+    strip = grads.shape[1] // replicas
+    length = send_x.shape[0] // 2
+    mine = lax.axis_index("dp")
+    total[...] = lax.dot_general(
+        grads[...], acts[...], (((0,), (0,)), ((), ())), preferred_element_type=F32
+    ) * (1.0 / math.sqrt(tokens_all))
+
+    def pieces(offset):
+        rows = pl.ds(pl.multiple_of((mine ^ offset) * strip, strip), strip)
         for part in range(replicas):
-            yield starts[-1] + part * strip, grad_sum[rows, part * share : (part + 1) * share]
-
-    def store(offset, upper, lower):
-        for start, piece in pieces(offset):
-            stop = start + piece.shape[0]
-            for target, low, high in ((upper, 0, length), (lower, length, 2 * length)):
-                first, last = max(start, low), min(stop, high)
-                if target is not None and first < last:
-                    ref, at = target
-                    ref[at + first - low : at + last - low, :] = piece[first - start : last - start].astype(ref.dtype)
-
-    store(3, (relay_x, 0), (relay_y, 0))
-    store(1, (direct_x, 0), (keep, 3 * length))
-    store(2, (keep, 2 * length), (direct_y, 0))
-    store(0, (keep, 0), (keep, length))
+            yield part * strip, total[rows, part * share : (part + 1) * share]
+
+    store_chunk(pieces(3), length, (send_x, 0), (send_y, 0))
+    store_chunk(pieces(1), length, (send_x, length), (keep, 3 * length))
+    store_chunk(pieces(2), length, (keep, 2 * length), (send_y, length))
+    store_chunk(pieces(0), length, (keep, 0), (keep, length))
 
 
 def relay_kernel(keep, got_x, got_y, send_x, send_y):
     length = send_x.shape[0]
     send_y[...] = (keep[2 * length : 3 * length, :] + got_x[...].astype(F32)).astype(BF16)
     send_x[...] = (keep[3 * length :, :] + got_y[...].astype(F32)).astype(BF16)
+
+
+def grad_relay_kernel(keep, got_x, got_y, send_x, send_y):
+    length = send_x.shape[0]
+    send_y[...] = (keep[2 * length : 3 * length, :] + got_x[0:length, :].astype(F32)).astype(BF16)
+    send_x[...] = (keep[3 * length :, :] + got_y[0:length, :].astype(F32)).astype(BF16)
+
+
+def grad_total_kernel(keep, got_x, got_y, relay_x, relay_y, chunk):
+    length = relay_x.shape[0]
+    chunk[0:length, :] = (
+        keep[0:length, :] + got_x[length:, :].astype(F32) + relay_y[...].astype(F32)
+    ).astype(BF16)
+    chunk[length:, :] = (
+        keep[length : 2 * length, :] + got_y[length:, :].astype(F32) + relay_x[...].astype(F32)
+    ).astype(BF16)
 
 
 def factor_kernel(replicas, keep, direct_x, direct_y, relay_x, relay_y, old, upper, lower, exact):
@@ -144,7 +174,6 @@
             summed = jnp.where(column < half, summed, 2.0 * summed)
         squares = squares + (summed if position < 2 else 2.0 * summed)
         values.append(value.astype(BF16))
-    values.append(total[starts[-1] :].astype(BF16))
     high = squares.astype(BF16).astype(F32)
     middle = (squares - high).astype(BF16).astype(F32)
     rest = squares - high - middle
@@ -158,11 +187,10 @@
 
 def root_kernel(replicas, count, exact, *rest):
     chunks = [rest[2 * i : 2 * i + 2] for i in range(replicas)]
-    old_root, factor_out, root_out, step_out, factor, grads, diagonal, result = rest[2 * replicas :]
+    factor_out, root_out, finished, factor, diagonal = rest[2 * replicas :]
     share = root_out.shape[0]
     order = root_out.shape[1]
     half = share // 2
-    strip = step_out.shape[0] // replicas
     starts = chunk_rows(share)
     length = chunks[0][0].shape[0]
     mine = lax.axis_index("dp")
@@ -173,9 +201,10 @@
             return upper[start : start + count, :]
         if start >= length:
             return lower[start - length : start - length + count, :]
-        return jnp.concatenate([upper[start:, :], lower[0 : start + count - length, :]], axis=0)
+        return jnp.concatenate([upper[start:length, :], lower[0 : start + count - length, :]], axis=0)
 
     squares = jnp.zeros((16, share), F32)
+    low_eye = eye_of(half, half)
     for offset in range(replicas):
         owner = mine ^ offset
         base = pl.multiple_of(owner * share, share)
@@ -186,26 +215,18 @@
         factor[pl.ds(base, half), pl.ds(base, share)] = top
         factor[pl.ds(corner, half), pl.ds(base, half)] = transposed(top[:, half:])
         factor[pl.ds(corner, half), pl.ds(corner, half)] = low
-        on_diagonal = low_eye = eye_of(half, half)
-        diagonal[:, pl.ds(base, half)] = jnp.sum(
-            top[:, 0:half].astype(F32) * on_diagonal, axis=0, keepdims=True
-        )
+        diagonal[:, pl.ds(base, half)] = jnp.sum(top[:, 0:half].astype(F32) * low_eye, axis=0, keepdims=True)
         diagonal[:, pl.ds(corner, half)] = jnp.sum(low.astype(F32) * low_eye, axis=0, keepdims=True)
         for step in range(1, replicas):
             row, col = shared_half(owner, step, share)
             block = rows_of(offset, starts[1 + step], half)
             factor[pl.ds(row, half), pl.ds(col, share)] = block
             factor[pl.ds(col, share), pl.ds(row, half)] = transposed(block)
-        for part in range(replicas):
-            grads[offset * strip : (offset + 1) * strip, part * share : (part + 1) * share] = rows_of(
-                offset, starts[-1] + part * strip, strip
-            )
-        squares = squares + rows_of(offset, starts[-1] + replicas * strip, 16).astype(F32)
+        squares = squares + rows_of(offset, starts[-1], 16).astype(F32)
 
     scale = jnp.sqrt(jnp.sum(squares, keepdims=True) / order + EPSILON)
     inverse = 1.0 / scale
-    ones = diagonal[...] * inverse
-    ones = ones.astype(BF16).astype(F32)
+    ones = (diagonal[...] * inverse).astype(BF16).astype(F32)
     lift = (1.5 - 0.5 * ones).astype(BF16).astype(F32) + 0.5 * (diagonal[...] * inverse)
     eye = eye_of(share, order, mine * share)
     my_rows = pl.ds(pl.multiple_of(mine * share, share), share)
@@ -219,15 +240,7 @@
     ) + turn_two.astype(F32) * lift
     chosen = jnp.where(count[0, 0] == 1, turn.astype(F32), inverse_rows)
     root_out[...] = (chosen * lax.rsqrt(scale)).astype(BF16)
-
-    result[...] = lax.dot_general(
-        grads[...], old_root[...], (((1,), (1,)), ((), ())), preferred_element_type=F32
-    ).astype(BF16)
-    for offset in range(replicas):
-        owner = mine ^ offset
-        step_out[pl.ds(pl.multiple_of(owner * strip, strip), strip), :] = result[
-            offset * strip : (offset + 1) * strip, :
-        ]
+    finished[...] = jnp.zeros_like(finished)
 
     own_columns = pl.ds(pl.multiple_of(mine * share, share), share)
     top = exact[0:half, :]
@@ -251,72 +264,136 @@
             factor_out[:, columns] = jnp.concatenate([theirs.T, own.T], axis=1)
 
 
+def step_kernel(replicas, *refs):
+    chunks = refs[:replicas]
+    old_root, step_out, grads, result = refs[replicas:]
+    share = old_root.shape[0]
+    strip = step_out.shape[0] // replicas
+    mine = lax.axis_index("dp")
+    for offset, chunk in enumerate(chunks):
+        for part in range(replicas):
+            grads[offset * strip : (offset + 1) * strip, part * share : (part + 1) * share] = chunk[
+                part * strip : (part + 1) * strip, :
+            ]
+    result[...] = lax.dot_general(
+        grads[...], old_root[...], (((1,), (1,)), ((), ())), preferred_element_type=F32
+    ).astype(BF16)
+    for offset in range(replicas):
+        owner = mine ^ offset
+        step_out[pl.ds(pl.multiple_of(owner * strip, strip), strip), :] = result[
+            offset * strip : (offset + 1) * strip, :
+        ]
+
+
 def square_plan(acts, out_grad, old_factor, old_root, iter_count):
     replicas = lax.axis_size("dp")
     inputs = acts[0]
-    tokens_all = inputs.shape[0] * replicas
-    order = inputs.shape[1]
+    tokens, order = inputs.shape
     share = order // replicas
     grows = out_grad.shape[2]
     params = pltpu.CompilerParams(vmem_limit_bytes=VMEM_LIMIT)
-    whole_rows = chunk_rows(share)[-1] + grows
+    whole_rows = chunk_rows(share)[-1]
     length = whole_rows // 2
-    piece = jax.ShapeDtypeStruct((length, share), BF16)
+
+    def shape(rows, kind=BF16, columns=share):
+        return jax.ShapeDtypeStruct((rows, columns), kind)
+
+    def call(kernel, outs, name, *operands, first=None, after=(), scratch=()):
+        in_specs = whole(len(operands)) + [pl.BlockSpec(memory_space=pl.ANY)] * len(after)
+        if first is not None:
+            in_specs[0] = pl.BlockSpec(memory_space=first)
+
+        def body(*refs):
+            kernel(*refs[: len(operands)], *refs[len(operands) + len(after) :])
+
+        return pl.pallas_call(
+            body,
+            out_shape=outs,
+            in_specs=in_specs,
+            out_specs=whole(len(outs)),
+            scratch_shapes=scratch,
+            compiler_params=params,
+            name=name,
+        )(*operands, *after)
 
     received = passed_along(out_grad, "pipe", -1)[0]
-    relay_x, relay_y, direct_x, direct_y, keep = pl.pallas_call(
-        functools.partial(products_kernel, replicas, tokens_all),
-        out_shape=[piece] * 4 + [jax.ShapeDtypeStruct((4 * length, share), F32)],
-        in_specs=whole(2),
-        out_specs=whole(5),
-        scratch_shapes=[pltpu.VMEM((order, order), F32), pltpu.VMEM((grows, order), F32)],
-        compiler_params=params,
-        name="products",
-    )(inputs, received)
+    relay_x, relay_y, direct_x, direct_y, keep = call(
+        functools.partial(batch_kernel, replicas, tokens * replicas),
+        [shape(length)] * 4 + [shape(4 * length, F32)],
+        "batch",
+        inputs,
+        scratch=[pltpu.VMEM((order, order), F32)],
+    )
     relay_x, relay_y = swapped(relay_x, 1), swapped(relay_y, 2)
     direct_x, direct_y = swapped(direct_x, 1), swapped(direct_y, 2)
-    relay_x, relay_y = pl.pallas_call(
-        relay_kernel,
-        out_shape=[piece] * 2,
-        in_specs=whole(3),
-        out_specs=whole(2),
-        compiler_params=params,
-        name="relay",
-    )(keep, relay_x, relay_y)
+    relay_x, relay_y = call(relay_kernel, [shape(length)] * 2, "relay", keep, relay_x, relay_y)
+    grad_x, grad_y, grad_keep = call(
+        functools.partial(grad_kernel, replicas, tokens * replicas),
+        [shape(grows)] * 2 + [shape(2 * grows, F32)],
+        "grad",
+        inputs,
+        received,
+        after=[relay_x, relay_y],
+        scratch=[pltpu.VMEM((grows, order), F32)],
+    )
     relay_x, relay_y = swapped(relay_x, 1), swapped(relay_y, 2)
-    upper, lower, exact = pl.pallas_call(
+    grad_x, grad_y = swapped(grad_x, 1), swapped(grad_y, 2)
+    upper, lower, exact = call(
         functools.partial(factor_kernel, replicas),
-        out_shape=[
-            piece,
-            jax.ShapeDtypeStruct((length + 16, share), BF16),
-            jax.ShapeDtypeStruct((chunk_rows(share)[-1], share), F32),
-        ],
-        in_specs=whole(6),
-        out_specs=whole(3),
-        compiler_params=params,
-        name="factor",
-    )(keep, direct_x, direct_y, relay_x, relay_y, old_factor[0, 0])
+        [shape(length), shape(length + 16), shape(whole_rows, F32)],
+        "factor",
+        keep,
+        direct_x,
+        direct_y,
+        relay_x,
+        relay_y,
+        old_factor[0, 0],
+    )
     upper_x, lower_y = swapped(upper, 1), swapped(lower, 2)
     lower_x, upper_y = swapped(lower, 1), swapped(upper, 2)
+    strip_x, strip_y = call(
+        grad_relay_kernel, [shape(grows // 2)] * 2, "grad_relay", grad_keep, grad_x, grad_y, after=[upper, lower]
+    )
+    strip_x, strip_y = swapped(strip_x, 1), swapped(strip_y, 2)
     upper_far, lower_far = swapped(upper_x, 2), swapped(lower_y, 1)
-    factor, root, step = pl.pallas_call(
+    (strip,) = call(
+        grad_total_kernel,
+        [shape(grows)],
+        "grad_total",
+        grad_keep,
+        grad_x,
+        grad_y,
+        strip_x,
+        strip_y,
+        after=[upper_x, lower_y],
+    )
+    strips = [strip] + [swapped(strip, offset) for offset in range(1, replicas)]
+    factor, root, finished = call(
         functools.partial(root_kernel, replicas),
-        out_shape=[
-            jax.ShapeDtypeStruct((share, order), F32),
-            jax.ShapeDtypeStruct((share, order), BF16),
-            jax.ShapeDtypeStruct((grows, share), BF16),
-        ],
-        in_specs=[pl.BlockSpec(memory_space=pltpu.SMEM)] + whole(2 * replicas + 2),
-        out_specs=whole(3),
-        scratch_shapes=[
-            pltpu.VMEM((order, order), BF16),
-            pltpu.VMEM((grows, order), BF16),
-            pltpu.VMEM((1, order), F32),
-            pltpu.VMEM((grows, share), BF16),
-        ],
-        compiler_params=params,
-        name="root",
-    )(iter_count, exact, upper, lower, upper_x, lower_x, upper_y, lower_y, upper_far, lower_far, old_root[0, 0])
+        [shape(share, F32, order), shape(share, BF16, order), shape(8, F32, 128)],
+        "root",
+        iter_count,
+        exact,
+        upper,
+        lower,
+        upper_x,
+        lower_x,
+        upper_y,
+        lower_y,
+        upper_far,
+        lower_far,
+        first=pltpu.SMEM,
+        scratch=[pltpu.VMEM((order, order), BF16), pltpu.VMEM((1, order), F32)],
+    )
+    (step,) = call(
+        functools.partial(step_kernel, replicas),
+        [shape(grows, BF16, share)],
+        "step",
+        *strips,
+        old_root[0, 0],
+        after=[finished],
+        scratch=[pltpu.VMEM((grows, order), BF16), pltpu.VMEM((grows, share), BF16)],
+    )
     return (factor[None, None], root[None, None], step[None, None])
 
 

time: 45.9 us -> 41.7 us (0.908)
  waiting for transfers between devices: 23.2 us -> 9.61 us
  starting transfers between devices: 13.9 us -> 22.5 us
  Pallas kernels: 6.06 us -> 6.94 us
    ppermute x12 -> x19, waiting for transfers between devices: 21.9 us -> 9.61 us  [swapped(): lax.ppermute(block, 'dp', [(i, i ^ offset) for i in range(lax.axis_size('...]
    ppermute x12 -> x19, starting transfers between devices: 13.4 us -> 21.9 us  [swapped(): lax.ppermute(block, 'dp', [(i, i ^ offset) for i in range(lax.axis_size('...]
    ppermute x1, waiting for transfers between devices: 1.37 us -> 0.01 us  [passed_along(): return lax.ppermute(block, axis, route)]
    pallas_call x4 -> x8, Pallas kernels: 6.06 us -> 6.94 us  [call(): pl.pallas_call(body, out_shape=outs, in_specs=in_specs, out_specs=whole(l...]
  transfers between devices with their start and end apart: 13 -> 20, of which waited for: 12 -> 6; matrix products, arithmetic and copies ran while one was open for 0% -> 0% of each run, Pallas kernels for 0% -> 14%
where the time goes in v3:
time: 41.7 us; the launch traced here: 41.6 us
  starting transfers between devices  22.5 us (54%)
  waiting for transfers between devices  9.61 us (23%)
  Pallas kernels  6.94 us (17%)
  between operations  1.34 us (3%)
  local copies, waits for them, and re-layouts  1.23 us (3%)
    ppermute x19, starting transfers between devices, swapped(): lax.ppermute(block, 'dp', [(i, i ^ offset) for i in range(lax.axis_size('...  21.9 us
    ppermute x19, waiting for transfers between devices, swapped(): lax.ppermute(block, 'dp', [(i, i ^ offset) for i in range(lax.axis_size('...  9.61 us
    pallas_call x8, Pallas kernels, call(): pl.pallas_call(body, out_shape=outs, in_specs=in_specs, out_specs=whole(l...  6.94 us
    unnamed x6, local copies, waits for them, and re-layouts  1.23 us
  transfers between devices with their start and end apart: 20, of which 6 were waited for; matrix products, arithmetic and copies ran while one was open for 0% of the time, Pallas kernels for 14%

profile of v3, /device:TPU:0, one launch (start us, length us, event | category | flops | bytes accessed | tf_op | source)
XLA Modules:
  0.0 41.6 jit_solution(15701595255291450182)
XLA Ops:
  0.6 0.5 %collective-permute-start.12 = (bf16[1,512,256]{2,1,0:T(8,128)(2,1)}, bf16[1,512,256]{2,1,0:T(8,128)(2,1)S(1)}, u32[]{:S(2)}, u32[]{:S(2)}) collective-permute-start(bf16[1,512,256]{2,1,0:T(8,128)(2,1)} %param.6), channel_id=1, source_target_pairs={{16,0},{0,16},{17,1},{1,17},{18,2},{2,18},{19,3},{3,19},{20,4},{4,... | collective-permute-start | bytes 786440 | tf_op jit(solution)/shard_map/ppermute | solution.py:22
  1.1 0.0 copy-start
  1.1 1.2 %copy-done = bf16[1,512,1024]{2,1,0:T(8,128)(2,1)S(1)} copy-done((bf16[1,512,1024]{2,1,0:T(8,128)(2,1)S(1)}, bf16[1,512,1024]{2,1,0:T(8,128)(2,1)}, u32[]{:S(2)}) %copy-start) | copy-done | bytes 1048600
  2.4 1.1 %batch.1 = (bf16[288,256]{1,0:T(8,128)(2,1)S(1)}, bf16[288,256]{1,0:T(8,128)(2,1)S(1)}, bf16[288,256]{1,0:T(8,128)(2,1)S(1)}, bf16[288,256]{1,0:T(8,128)(2,1)S(1)}, f32[1152,256]{1,0:T(8,128)S(1)}) custom-call(bf16[512,1024]{1,0:T(8,128)(2,1)S(1)} %bitcast.7), custom_call_target="tpu_custom_call" | custom-call | tf_op jit(solution)/shard_map/batch/pallas_call | solution.py:309
  3.4 2.6 %collective-permute-start.2 = (bf16[288,256]{1,0:T(8,128)(2,1)S(1)}, bf16[288,256]{1,0:T(8,128)(2,1)S(1)}, u32[]{:S(2)}, u32[]{:S(2)}) collective-permute-start(bf16[288,256]{1,0:T(8,128)(2,1)S(1)} %get-tuple-element.24), channel_id=1, source_target_pairs={{0,4},{4,0},{8,12},{12,8},{1,5},{5,1},{9,13},{13,9},{2,6},{6,2},{1... | collective-permute-start | bytes 442376 | tf_op jit(solution)/shard_map/ppermute | solution.py:26
  6.0 1.5 %collective-permute-start.3 = (bf16[288,256]{1,0:T(8,128)(2,1)S(1)}, bf16[288,256]{1,0:T(8,128)(2,1)S(1)}, u32[]{:S(2)}, u32[]{:S(2)}) collective-permute-start(bf16[288,256]{1,0:T(8,128)(2,1)S(1)} %get-tuple-element.25), channel_id=1, source_target_pairs={{0,8},{4,12},{8,0},{12,4},{1,9},{5,13},{9,1},{13,5},{2,10},{6,14},... | collective-permute-start | bytes 442376 | tf_op jit(solution)/shard_map/ppermute | solution.py:26
  7.5 0.5 %collective-permute-start = (bf16[288,256]{1,0:T(8,128)(2,1)S(1)}, bf16[288,256]{1,0:T(8,128)(2,1)S(1)}, u32[]{:S(2)}, u32[]{:S(2)}) collective-permute-start(bf16[288,256]{1,0:T(8,128)(2,1)S(1)} %get-tuple-element.22), channel_id=1, source_target_pairs={{0,4},{4,0},{8,12},{12,8},{1,5},{5,1},{9,13},{13,9},{2,6},{6,2},{1... | collective-permute-start | bytes 442376 | tf_op jit(solution)/shard_map/ppermute | solution.py:26
  8.1 0.1 collective-permute-start.1
  8.1 2.6 %collective-permute-done.2.refs_1_ = bf16[288,256]{1,0:T(8,128)(2,1)S(1)} collective-permute-done((bf16[288,256]{1,0:T(8,128)(2,1)S(1)}, bf16[288,256]{1,0:T(8,128)(2,1)S(1)}, u32[]{:S(2)}, u32[]{:S(2)}) %collective-permute-start.2) | collective-permute-done | bytes 147488 | tf_op jit(solution)/shard_map/ppermute | solution.py:26
  10.7 2.0 %collective-permute-done.3.refs_2_ = bf16[288,256]{1,0:T(8,128)(2,1)S(1)} collective-permute-done((bf16[288,256]{1,0:T(8,128)(2,1)S(1)}, bf16[288,256]{1,0:T(8,128)(2,1)S(1)}, u32[]{:S(2)}, u32[]{:S(2)}) %collective-permute-start.3) | collective-permute-done | bytes 147488 | tf_op jit(solution)/shard_map/ppermute | solution.py:26
  12.7 0.0 copy-start.1
  12.7 0.1 relay.1
  12.8 0.1 collective-permute-start.4
  12.9 2.0 %collective-permute-start.5 = (bf16[288,256]{1,0:T(8,128)(2,1)S(1)}, bf16[288,256]{1,0:T(8,128)(2,1)S(1)}, u32[]{:S(2)}, u32[]{:S(2)}) collective-permute-start(bf16[288,256]{1,0:T(8,128)(2,1)S(1)} %get-tuple-element.27.refs_3_), channel_id=1, source_target_pairs={{0,8},{4,12},{8,0},{12,4},{1,9},{5,13},{9,1},{13,5},{2,10},{6,14},... | collective-permute-start | bytes 442376 | tf_op jit(solution)/shard_map/ppermute | solution.py:26
  14.9 0.0 collective-permute-done.12
  14.9 0.5 %grad.1 = (bf16[256,256]{1,0:T(8,128)(2,1)S(1)}, bf16[256,256]{1,0:T(8,128)(2,1)S(1)}, f32[512,256]{1,0:T(8,128)S(1)}) custom-call(bf16[512,1024]{1,0:T(8,128)(2,1)S(1)} %bitcast.8, bf16[512,256]{1,0:T(8,128)(2,1)S(1)} %bitcast.11, bf16[288,256]{1,0:T(8,128)(2,1)S(1)} %get-tuple-element.26.refs_2_, bf16[288,256]{1,0:T(8,128)(2,1)S(1)} %get-tuple-element.27.refs_3_), custom_call_target="tpu_custom_call" | custom-call | tf_op jit(solution)/shard_map/grad/pallas_call | solution.py:309
  15.4 1.6 %collective-permute-start.13 = (bf16[256,256]{1,0:T(8,128)(2,1)S(1)}, bf16[256,256]{1,0:T(8,128)(2,1)S(1)}, u32[]{:S(2)}, u32[]{:S(2)}) collective-permute-start(bf16[256,256]{1,0:T(8,128)(2,1)S(1)} %get-tuple-element.34), channel_id=1, source_target_pairs={{0,4},{4,0},{8,12},{12,8},{1,5},{5,1},{9,13},{13,9},{2,6},{6,2},{1... | collective-permute-start | bytes 393224 | tf_op jit(solution)/shard_map/ppermute | solution.py:26
  17.0 0.0 collective-permute-done.refs_1_
  17.0 0.5 %collective-permute-start.14 = (bf16[256,256]{1,0:T(8,128)(2,1)S(1)}, bf16[256,256]{1,0:T(8,128)(2,1)S(1)}, u32[]{:S(2)}, u32[]{:S(2)}) collective-permute-start(bf16[256,256]{1,0:T(8,128)(2,1)S(1)} %get-tuple-element.35), channel_id=1, source_target_pairs={{0,8},{4,12},{8,0},{12,4},{1,9},{5,13},{9,1},{13,5},{2,10},{6,14},... | collective-permute-start | bytes 393224 | tf_op jit(solution)/shard_map/ppermute | solution.py:26
  17.5 0.0 collective-permute-done.1.refs_2_
  17.5 1.8 %collective-permute-done.4.refs_3_ = bf16[288,256]{1,0:T(8,128)(2,1)S(1)} collective-permute-done((bf16[288,256]{1,0:T(8,128)(2,1)S(1)}, bf16[288,256]{1,0:T(8,128)(2,1)S(1)}, u32[]{:S(2)}, u32[]{:S(2)}) %collective-permute-start.4) | collective-permute-done | bytes 147488 | tf_op jit(solution)/shard_map/ppermute | solution.py:26
  19.2 0.0 collective-permute-done.5.refs_4_
  19.3 0.0 copy-done.1
  19.3 0.3 factor.1
  19.5 1.8 %collective-permute-start.6 = (bf16[288,256]{1,0:T(8,128)(2,1)S(1)}, bf16[288,256]{1,0:T(8,128)(2,1)S(1)}, u32[]{:S(2)}, u32[]{:S(2)}) collective-permute-start(bf16[288,256]{1,0:T(8,128)(2,1)S(1)} %get-tuple-element.29.refs_2_.refs_3_), channel_id=1, source_target_pairs={{0,4},{4,0},{8,12},{12,8},{1,5},{5,1},{9,13},{13,9},{2,6},{6,2},{1... | collective-permute-start | bytes 442376 | tf_op jit(solution)/shard_map/ppermute | solution.py:26
  21.4 1.2 %collective-permute-start.9 = (bf16[304,256]{1,0:T(8,128)(2,1)S(1)}, bf16[304,256]{1,0:T(8,128)(2,1)S(1)}, u32[]{:S(2)}, u32[]{:S(2)}) collective-permute-start(bf16[304,256]{1,0:T(8,128)(2,1)S(1)} %get-tuple-element.30.refs_3_.refs_4_), channel_id=1, source_target_pairs={{0,8},{4,12},{8,0},{12,4},{1,9},{5,13},{9,1},{13,5},{2,10},{6,14},... | collective-permute-start | bytes 466952 | tf_op jit(solution)/shard_map/ppermute | solution.py:26
  22.6 1.0 %collective-permute-start.7 = (bf16[304,256]{1,0:T(8,128)(2,1)S(1)}, bf16[304,256]{1,0:T(8,128)(2,1)S(1)}, u32[]{:S(2)}, u32[]{:S(2)}) collective-permute-start(bf16[304,256]{1,0:T(8,128)(2,1)S(1)} %get-tuple-element.30.refs_3_.refs_4_), channel_id=1, source_target_pairs={{0,4},{4,0},{8,12},{12,8},{1,5},{5,1},{9,13},{13,9},{2,6},{6,2},{1... | collective-permute-start | bytes 466952 | tf_op jit(solution)/shard_map/ppermute | solution.py:26
  23.6 0.0 collective-permute-done.13.refs_1_
  23.6 0.1 collective-permute-start.8
  23.7 0.0 collective-permute-done.14.refs_2_
  23.7 1.8 %collective-permute-start.15 = (bf16[128,256]{1,0:T(8,128)(2,1)S(1)}, bf16[128,256]{1,0:T(8,128)(2,1)S(1)}, u32[]{:S(2)}, u32[]{:S(2)}) collective-permute-start(bf16[128,256]{1,0:T(8,128)(2,1)S(1)} %get-tuple-element.36), channel_id=1, source_target_pairs={{0,4},{4,0},{8,12},{12,8},{1,5},{5,1},{9,13},{13,9},{2,6},{6,2},{1... | collective-permute-start | bytes 196616 | tf_op jit(solution)/shard_map/ppermute | solution.py:26
  25.5 0.7 %collective-permute-done.6.refs_4_.refs_5_ = bf16[288,256]{1,0:T(8,128)(2,1)S(1)} collective-permute-done((bf16[288,256]{1,0:T(8,128)(2,1)S(1)}, bf16[288,256]{1,0:T(8,128)(2,1)S(1)}, u32[]{:S(2)}, u32[]{:S(2)}) %collective-permute-start.6) | collective-permute-done | bytes 147488 | tf_op jit(solution)/shard_map/ppermute | solution.py:26
  26.2 1.3 %collective-permute-start.16 = (bf16[128,256]{1,0:T(8,128)(2,1)S(1)}, bf16[128,256]{1,0:T(8,128)(2,1)S(1)}, u32[]{:S(2)}, u32[]{:S(2)}) collective-permute-start(bf16[128,256]{1,0:T(8,128)(2,1)S(1)} %get-tuple-element.37), channel_id=1, source_target_pairs={{0,8},{4,12},{8,0},{12,4},{1,9},{5,13},{9,1},{13,5},{2,10},{6,14},... | collective-permute-start | bytes 196616 | tf_op jit(solution)/shard_map/ppermute | solution.py:26
  27.5 0.0 collective-permute-done.9.refs_7_.refs_6_
  27.5 1.6 %collective-permute-start.11 = (bf16[304,256]{1,0:T(8,128)(2,1)S(1)}, bf16[304,256]{1,0:T(8,128)(2,1)S(1)}, u32[]{:S(2)}, u32[]{:S(2)}) collective-permute-start(bf16[304,256]{1,0:T(8,128)(2,1)S(1)} %collective-permute-done.9.refs_7_.refs_6_), channel_id=1, source_target_pairs={{0,4},{4,0},{8,12},{12,8},{1,5},{5,1},{9,13},{13,9},{2,6},{6,2},{1... | collective-permute-start | bytes 466952 | tf_op jit(solution)/shard_map/ppermute | solution.py:26
  29.1 1.9 %collective-permute-done.15.refs_3_ = bf16[128,256]{1,0:T(8,128)(2,1)S(1)} collective-permute-done((bf16[128,256]{1,0:T(8,128)(2,1)S(1)}, bf16[128,256]{1,0:T(8,128)(2,1)S(1)}, u32[]{:S(2)}, u32[]{:S(2)}) %collective-permute-start.15) | collective-permute-done | bytes 65568 | tf_op jit(solution)/shard_map/ppermute | solution.py:26
  31.0 0.7 %collective-permute-start.10 = (bf16[288,256]{1,0:T(8,128)(2,1)S(1)}, bf16[288,256]{1,0:T(8,128)(2,1)S(1)}, u32[]{:S(2)}, u32[]{:S(2)}) collective-permute-start(bf16[288,256]{1,0:T(8,128)(2,1)S(1)} %collective-permute-done.6.refs_4_.refs_5_), channel_id=1, source_target_pairs={{0,8},{4,12},{8,0},{12,4},{1,9},{5,13},{9,1},{13,5},{2,10},{6,14},... | collective-permute-start | bytes 442376 | tf_op jit(solution)/shard_map/ppermute | solution.py:26
  31.7 0.0 collective-permute-done.16.refs_4_
  31.7 0.1 grad_total.1.refs_0_
  31.8 0.0 copy-start.2
  31.8 1.9 %collective-permute-start.17 = (bf16[256,256]{1,0:T(8,128)(2,1)S(1)}, bf16[256,256]{1,0:T(8,128)(2,1)S(1)}, u32[]{:S(2)}, u32[]{:S(2)}) collective-permute-start(bf16[256,256]{1,0:T(8,128)(2,1)S(1)} %grad_total.1.refs_0_), channel_id=1, source_target_pairs={{0,4},{4,0},{8,12},{12,8},{1,5},{5,1},{9,13},{13,9},{2,6},{6,2},{1... | collective-permute-start | bytes 393224 | tf_op jit(solution)/shard_map/ppermute | solution.py:26
  33.6 0.0 collective-permute-done.8.refs_6_
  33.7 1.1 %collective-permute-start.18 = (bf16[256,256]{1,0:T(8,128)(2,1)S(1)}, bf16[256,256]{1,0:T(8,128)(2,1)S(1)}, u32[]{:S(2)}, u32[]{:S(2)}) collective-permute-start(bf16[256,256]{1,0:T(8,128)(2,1)S(1)} %grad_total.1.refs_0_), channel_id=1, source_target_pairs={{0,8},{4,12},{8,0},{12,4},{1,9},{5,13},{9,1},{13,5},{2,10},{6,14},... | collective-permute-start | bytes 393224 | tf_op jit(solution)/shard_map/ppermute | solution.py:26
  34.7 0.0 collective-permute-done.7.refs_5_
  34.7 0.6 %collective-permute-start.19 = (bf16[256,256]{1,0:T(8,128)(2,1)S(1)}, bf16[256,256]{1,0:T(8,128)(2,1)S(1)}, u32[]{:S(2)}, u32[]{:S(2)}) collective-permute-start(bf16[256,256]{1,0:T(8,128)(2,1)S(1)} %grad_total.1.refs_0_), channel_id=1, source_target_pairs={{0,12},{4,8},{8,4},{12,0},{1,13},{5,9},{9,5},{13,1},{2,14},{6,10},... | collective-permute-start | bytes 393224 | tf_op jit(solution)/shard_map/ppermute | solution.py:26
  36.0 0.6 %collective-permute-done.10.refs_8_ = bf16[288,256]{1,0:T(8,128)(2,1)S(1)} collective-permute-done((bf16[288,256]{1,0:T(8,128)(2,1)S(1)}, bf16[288,256]{1,0:T(8,128)(2,1)S(1)}, u32[]{:S(2)}, u32[]{:S(2)}) %collective-permute-start.10) | collective-permute-done | bytes 147488 | tf_op jit(solution)/shard_map/ppermute | solution.py:26
  36.6 0.0 collective-permute-done.11.refs_9_
  36.6 3.9 %root.1 = (f32[256,1024]{1,0:T(8,128)}, bf16[256,1024]{1,0:T(8,128)(2,1)}, f32[8,128]{1,0:T(8,128)S(1)}) custom-call(s32[1,1]{1,0:T(1,128)S(6)} %copy.8.refs_0_, f32[576,256]{1,0:T(8,128)S(1)} %get-tuple-element.28.refs_1_, bf16[288,256]{1,0:T(8,128)(2,1)S(1)} %get-tuple-element.29.refs_2_.refs_3_, bf16[304,256]{1,0:T(8,128)(2,1)S(1)} %get-tuple-element.30.refs_3_.refs_4_, ...), custom_call_target="tpu_custom_call" | custom-call | tf_op jit(solution)/shard_map/root/pallas_call | solution.py:309
  40.5 0.0 collective-permute-done.17.refs_1_
  40.5 0.0 collective-permute-done.18.refs_2_
  40.5 0.0 collective-permute-done.19.refs_3_
  40.6 0.0 copy-done.2
  40.6 1.0 %step.1 = bf16[256,256]{1,0:T(8,128)(2,1)} custom-call(bf16[256,256]{1,0:T(8,128)(2,1)S(1)} %grad_total.1.refs_0_, bf16[256,256]{1,0:T(8,128)(2,1)S(1)} %collective-permute-done.17.refs_1_, bf16[256,256]{1,0:T(8,128)(2,1)S(1)} %collective-permute-done.18.refs_2_, bf16[256,256]{1,0:T(8,128)(2,1)S(1)} %collective-permute-done.19.refs_3_, ...), custom_call_target="tpu_custom_call" | custom-call | tf_op jit(solution)/shard_map/step/pallas_call | solution.py:309
  (1 shorter events, 0.0 us)
Async XLA Ops:
  0.6 14.2 %collective-permute-start.12 = (bf16[1,512,256]{2,1,0:T(8,128)(2,1)}, bf16[1,512,256]{2,1,0:T(8,128)(2,1)S(1)}, u32[]{:S(2)}, u32[]{:S(2)}) collective-permute-start(bf16[1,512,256]{2,1,0:T(8,128)(2,1)} %param.6), channel_id=1, source_target_pairs={{16,0},{0,16},{17,1},{1,17},{18,2},{2,18},{19,3},{3,19},{20,4},{4,... | collective-permute-start | bytes 786440 | tf_op jit(solution)/shard_map/ppermute | solution.py:22
  1.1 1.2 %copy-start = (bf16[1,512,1024]{2,1,0:T(8,128)(2,1)S(1)}, bf16[1,512,1024]{2,1,0:T(8,128)(2,1)}, u32[]{:S(2)}) copy-start(bf16[1,512,1024]{2,1,0:T(8,128)(2,1)} %param.5) | copy-start | bytes 3145732
  3.4 7.3 %collective-permute-start.2 = (bf16[288,256]{1,0:T(8,128)(2,1)S(1)}, bf16[288,256]{1,0:T(8,128)(2,1)S(1)}, u32[]{:S(2)}, u32[]{:S(2)}) collective-permute-start(bf16[288,256]{1,0:T(8,128)(2,1)S(1)} %get-tuple-element.24), channel_id=1, source_target_pairs={{0,4},{4,0},{8,12},{12,8},{1,5},{5,1},{9,13},{13,9},{2,6},{6,2},{1... | collective-permute-start | bytes 442376 | tf_op jit(solution)/shard_map/ppermute | solution.py:26
  6.0 6.7 %collective-permute-start.3 = (bf16[288,256]{1,0:T(8,128)(2,1)S(1)}, bf16[288,256]{1,0:T(8,128)(2,1)S(1)}, u32[]{:S(2)}, u32[]{:S(2)}) collective-permute-start(bf16[288,256]{1,0:T(8,128)(2,1)S(1)} %get-tuple-element.25), channel_id=1, source_target_pairs={{0,8},{4,12},{8,0},{12,4},{1,9},{5,13},{9,1},{13,5},{2,10},{6,14},... | collective-permute-start | bytes 442376 | tf_op jit(solution)/shard_map/ppermute | solution.py:26
  7.5 9.4 %collective-permute-start = (bf16[288,256]{1,0:T(8,128)(2,1)S(1)}, bf16[288,256]{1,0:T(8,128)(2,1)S(1)}, u32[]{:S(2)}, u32[]{:S(2)}) collective-permute-start(bf16[288,256]{1,0:T(8,128)(2,1)S(1)} %get-tuple-element.22), channel_id=1, source_target_pairs={{0,4},{4,0},{8,12},{12,8},{1,5},{5,1},{9,13},{13,9},{2,6},{6,2},{1... | collective-permute-start | bytes 442376 | tf_op jit(solution)/shard_map/ppermute | solution.py:26
  8.1 9.4 %collective-permute-start.1 = (bf16[288,256]{1,0:T(8,128)(2,1)S(1)}, bf16[288,256]{1,0:T(8,128)(2,1)S(1)}, u32[]{:S(2)}, u32[]{:S(2)}) collective-permute-start(bf16[288,256]{1,0:T(8,128)(2,1)S(1)} %get-tuple-element.23), channel_id=1, source_target_pairs={{0,8},{4,12},{8,0},{12,4},{1,9},{5,13},{9,1},{13,5},{2,10},{6,14},... | collective-permute-start | bytes 442376 | tf_op jit(solution)/shard_map/ppermute | solution.py:26
  12.7 6.6 %copy-start.1 = (f32[1,1,256,1024]{3,2,1,0:T(8,128)S(1)}, f32[1,1,256,1024]{3,2,1,0:T(8,128)}, u32[]{:S(2)}) copy-start(f32[1,1,256,1024]{3,2,1,0:T(8,128)} %param.7) | copy-start | bytes 3145732
  12.8 6.5 %collective-permute-start.4 = (bf16[288,256]{1,0:T(8,128)(2,1)S(1)}, bf16[288,256]{1,0:T(8,128)(2,1)S(1)}, u32[]{:S(2)}, u32[]{:S(2)}) collective-permute-start(bf16[288,256]{1,0:T(8,128)(2,1)S(1)} %get-tuple-element.26.refs_2_), channel_id=1, source_target_pairs={{0,4},{4,0},{8,12},{12,8},{1,5},{5,1},{9,13},{13,9},{2,6},{6,2},{1... | collective-permute-start | bytes 442376 | tf_op jit(solution)/shard_map/ppermute | solution.py:26
  12.9 6.4 %collective-permute-start.5 = (bf16[288,256]{1,0:T(8,128)(2,1)S(1)}, bf16[288,256]{1,0:T(8,128)(2,1)S(1)}, u32[]{:S(2)}, u32[]{:S(2)}) collective-permute-start(bf16[288,256]{1,0:T(8,128)(2,1)S(1)} %get-tuple-element.27.refs_3_), channel_id=1, source_target_pairs={{0,8},{4,12},{8,0},{12,4},{1,9},{5,13},{9,1},{13,5},{2,10},{6,14},... | collective-permute-start | bytes 442376 | tf_op jit(solution)/shard_map/ppermute | solution.py:26
  15.4 8.2 %collective-permute-start.13 = (bf16[256,256]{1,0:T(8,128)(2,1)S(1)}, bf16[256,256]{1,0:T(8,128)(2,1)S(1)}, u32[]{:S(2)}, u32[]{:S(2)}) collective-permute-start(bf16[256,256]{1,0:T(8,128)(2,1)S(1)} %get-tuple-element.34), channel_id=1, source_target_pairs={{0,4},{4,0},{8,12},{12,8},{1,5},{5,1},{9,13},{13,9},{2,6},{6,2},{1... | collective-permute-start | bytes 393224 | tf_op jit(solution)/shard_map/ppermute | solution.py:26
  17.0 6.7 %collective-permute-start.14 = (bf16[256,256]{1,0:T(8,128)(2,1)S(1)}, bf16[256,256]{1,0:T(8,128)(2,1)S(1)}, u32[]{:S(2)}, u32[]{:S(2)}) collective-permute-start(bf16[256,256]{1,0:T(8,128)(2,1)S(1)} %get-tuple-element.35), channel_id=1, source_target_pairs={{0,8},{4,12},{8,0},{12,4},{1,9},{5,13},{9,1},{13,5},{2,10},{6,14},... | collective-permute-start | bytes 393224 | tf_op jit(solution)/shard_map/ppermute | solution.py:26
  19.5 6.7 %collective-permute-start.6 = (bf16[288,256]{1,0:T(8,128)(2,1)S(1)}, bf16[288,256]{1,0:T(8,128)(2,1)S(1)}, u32[]{:S(2)}, u32[]{:S(2)}) collective-permute-start(bf16[288,256]{1,0:T(8,128)(2,1)S(1)} %get-tuple-element.29.refs_2_.refs_3_), channel_id=1, source_target_pairs={{0,4},{4,0},{8,12},{12,8},{1,5},{5,1},{9,13},{13,9},{2,6},{6,2},{1... | collective-permute-start | bytes 442376 | tf_op jit(solution)/shard_map/ppermute | solution.py:26
  21.4 6.1 %collective-permute-start.9 = (bf16[304,256]{1,0:T(8,128)(2,1)S(1)}, bf16[304,256]{1,0:T(8,128)(2,1)S(1)}, u32[]{:S(2)}, u32[]{:S(2)}) collective-permute-start(bf16[304,256]{1,0:T(8,128)(2,1)S(1)} %get-tuple-element.30.refs_3_.refs_4_), channel_id=1, source_target_pairs={{0,8},{4,12},{8,0},{12,4},{1,9},{5,13},{9,1},{13,5},{2,10},{6,14},... | collective-permute-start | bytes 466952 | tf_op jit(solution)/shard_map/ppermute | solution.py:26
  22.6 12.1 %collective-permute-start.7 = (bf16[304,256]{1,0:T(8,128)(2,1)S(1)}, bf16[304,256]{1,0:T(8,128)(2,1)S(1)}, u32[]{:S(2)}, u32[]{:S(2)}) collective-permute-start(bf16[304,256]{1,0:T(8,128)(2,1)S(1)} %get-tuple-element.30.refs_3_.refs_4_), channel_id=1, source_target_pairs={{0,4},{4,0},{8,12},{12,8},{1,5},{5,1},{9,13},{13,9},{2,6},{6,2},{1... | collective-permute-start | bytes 466952 | tf_op jit(solution)/shard_map/ppermute | solution.py:26
  23.6 10.0 %collective-permute-start.8 = (bf16[288,256]{1,0:T(8,128)(2,1)S(1)}, bf16[288,256]{1,0:T(8,128)(2,1)S(1)}, u32[]{:S(2)}, u32[]{:S(2)}) collective-permute-start(bf16[288,256]{1,0:T(8,128)(2,1)S(1)} %get-tuple-element.29.refs_2_.refs_3_), channel_id=1, source_target_pairs={{0,8},{4,12},{8,0},{12,4},{1,9},{5,13},{9,1},{13,5},{2,10},{6,14},... | collective-permute-start | bytes 442376 | tf_op jit(solution)/shard_map/ppermute | solution.py:26
  23.7 7.3 %collective-permute-start.15 = (bf16[128,256]{1,0:T(8,128)(2,1)S(1)}, bf16[128,256]{1,0:T(8,128)(2,1)S(1)}, u32[]{:S(2)}, u32[]{:S(2)}) collective-permute-start(bf16[128,256]{1,0:T(8,128)(2,1)S(1)} %get-tuple-element.36), channel_id=1, source_target_pairs={{0,4},{4,0},{8,12},{12,8},{1,5},{5,1},{9,13},{13,9},{2,6},{6,2},{1... | collective-permute-start | bytes 196616 | tf_op jit(solution)/shard_map/ppermute | solution.py:26
  26.2 5.5 %collective-permute-start.16 = (bf16[128,256]{1,0:T(8,128)(2,1)S(1)}, bf16[128,256]{1,0:T(8,128)(2,1)S(1)}, u32[]{:S(2)}, u32[]{:S(2)}) collective-permute-start(bf16[128,256]{1,0:T(8,128)(2,1)S(1)} %get-tuple-element.37), channel_id=1, source_target_pairs={{0,8},{4,12},{8,0},{12,4},{1,9},{5,13},{9,1},{13,5},{2,10},{6,14},... | collective-permute-start | bytes 196616 | tf_op jit(solution)/shard_map/ppermute | solution.py:26
  27.5 9.1 %collective-permute-start.11 = (bf16[304,256]{1,0:T(8,128)(2,1)S(1)}, bf16[304,256]{1,0:T(8,128)(2,1)S(1)}, u32[]{:S(2)}, u32[]{:S(2)}) collective-permute-start(bf16[304,256]{1,0:T(8,128)(2,1)S(1)} %collective-permute-done.9.refs_7_.refs_6_), channel_id=1, source_target_pairs={{0,4},{4,0},{8,12},{12,8},{1,5},{5,1},{9,13},{13,9},{2,6},{6,2},{1... | collective-permute-start | bytes 466952 | tf_op jit(solution)/shard_map/ppermute | solution.py:26
  31.0 5.6 %collective-permute-start.10 = (bf16[288,256]{1,0:T(8,128)(2,1)S(1)}, bf16[288,256]{1,0:T(8,128)(2,1)S(1)}, u32[]{:S(2)}, u32[]{:S(2)}) collective-permute-start(bf16[288,256]{1,0:T(8,128)(2,1)S(1)} %collective-permute-done.6.refs_4_.refs_5_), channel_id=1, source_target_pairs={{0,8},{4,12},{8,0},{12,4},{1,9},{5,13},{9,1},{13,5},{2,10},{6,14},... | collective-permute-start | bytes 442376 | tf_op jit(solution)/shard_map/ppermute | solution.py:26
  31.8 8.8 %copy-start.2 = (bf16[1,1,256,1024]{3,2,1,0:T(8,128)(2,1)S(1)}, bf16[1,1,256,1024]{3,2,1,0:T(8,128)(2,1)}, u32[]{:S(2)}) copy-start(bf16[1,1,256,1024]{3,2,1,0:T(8,128)(2,1)} %param.8) | copy-start | bytes 1572868
  31.8 8.8 %collective-permute-start.17 = (bf16[256,256]{1,0:T(8,128)(2,1)S(1)}, bf16[256,256]{1,0:T(8,128)(2,1)S(1)}, u32[]{:S(2)}, u32[]{:S(2)}) collective-permute-start(bf16[256,256]{1,0:T(8,128)(2,1)S(1)} %grad_total.1.refs_0_), channel_id=1, source_target_pairs={{0,4},{4,0},{8,12},{12,8},{1,5},{5,1},{9,13},{13,9},{2,6},{6,2},{1... | collective-permute-start | bytes 393224 | tf_op jit(solution)/shard_map/ppermute | solution.py:26
  33.7 6.9 %collective-permute-start.18 = (bf16[256,256]{1,0:T(8,128)(2,1)S(1)}, bf16[256,256]{1,0:T(8,128)(2,1)S(1)}, u32[]{:S(2)}, u32[]{:S(2)}) collective-permute-start(bf16[256,256]{1,0:T(8,128)(2,1)S(1)} %grad_total.1.refs_0_), channel_id=1, source_target_pairs={{0,8},{4,12},{8,0},{12,4},{1,9},{5,13},{9,1},{13,5},{2,10},{6,14},... | collective-permute-start | bytes 393224 | tf_op jit(solution)/shard_map/ppermute | solution.py:26
  34.7 5.9 %collective-permute-start.19 = (bf16[256,256]{1,0:T(8,128)(2,1)S(1)}, bf16[256,256]{1,0:T(8,128)(2,1)S(1)}, u32[]{:S(2)}, u32[]{:S(2)}) collective-permute-start(bf16[256,256]{1,0:T(8,128)(2,1)S(1)} %grad_total.1.refs_0_), channel_id=1, source_target_pairs={{0,12},{4,8},{8,4},{12,0},{1,13},{5,9},{9,5},{13,1},{2,14},{6,10},... | collective-permute-start | bytes 393224 | tf_op jit(solution)/shard_map/ppermute | solution.py:26

commit v4 on v3

--- a/solution.py
+++ b/solution.py
@@ -92,25 +92,11 @@
     store_chunk(pieces(0), length, (keep, 0), (keep, length))
 
 
-def grad_kernel(replicas, tokens_all, acts, grads, send_x, send_y, keep, total):
-    order = acts.shape[1]
-    share = order // replicas
-    strip = grads.shape[1] // replicas
-    length = send_x.shape[0] // 2
-    mine = lax.axis_index("dp")
-    total[...] = lax.dot_general(
-        grads[...], acts[...], (((0,), (0,)), ((), ())), preferred_element_type=F32
-    ) * (1.0 / math.sqrt(tokens_all))
-
-    def pieces(offset):
-        rows = pl.ds(pl.multiple_of((mine ^ offset) * strip, strip), strip)
-        for part in range(replicas):
-            yield part * strip, total[rows, part * share : (part + 1) * share]
-
-    store_chunk(pieces(3), length, (send_x, 0), (send_y, 0))
-    store_chunk(pieces(1), length, (send_x, length), (keep, 3 * length))
-    store_chunk(pieces(2), length, (keep, 2 * length), (send_y, length))
-    store_chunk(pieces(0), length, (keep, 0), (keep, length))
+def grad_kernel(tokens_all, acts, grads, partial):
+    partial[...] = (
+        lax.dot_general(grads[...], acts[...], (((0,), (0,)), ((), ())), preferred_element_type=F32)
+        * (1.0 / math.sqrt(tokens_all))
+    ).astype(BF16)
 
 
 def relay_kernel(keep, got_x, got_y, send_x, send_y):
@@ -119,27 +105,25 @@
     send_x[...] = (keep[3 * length :, :] + got_y[...].astype(F32)).astype(BF16)
 
 
-def grad_relay_kernel(keep, got_x, got_y, send_x, send_y):
-    length = send_x.shape[0]
-    send_y[...] = (keep[2 * length : 3 * length, :] + got_x[0:length, :].astype(F32)).astype(BF16)
-    send_x[...] = (keep[3 * length :, :] + got_y[0:length, :].astype(F32)).astype(BF16)
-
-
-def grad_total_kernel(keep, got_x, got_y, relay_x, relay_y, chunk):
-    length = relay_x.shape[0]
-    chunk[0:length, :] = (
-        keep[0:length, :] + got_x[length:, :].astype(F32) + relay_y[...].astype(F32)
-    ).astype(BF16)
-    chunk[length:, :] = (
-        keep[length : 2 * length, :] + got_y[length:, :].astype(F32) + relay_x[...].astype(F32)
-    ).astype(BF16)
-
-
-def factor_kernel(replicas, keep, direct_x, direct_y, relay_x, relay_y, old, upper, lower, exact):
+def strip_kernel(replicas, partials, copies):
+    strip = partials.shape[0] // replicas
+    total = partials[0:strip, :].astype(F32)
+    for i in range(1, replicas):
+        total = total + partials[i * strip : (i + 1) * strip, :].astype(F32)
+    for i in range(replicas):
+        copies[i * strip : (i + 1) * strip, :] = total.astype(BF16)
+
+
+def halves_kernel(got_x, got_y, send_x, send_y):
+    send_y[...] = got_x[0 : send_y.shape[0], :]
+    send_x[...] = got_y[send_y.shape[0] :, :]
+
+
+def factor_kernel(replicas, keep, direct_x, direct_y, relay_x, relay_y, old, chunk, exact):
     share, order = old.shape
     half = share // 2
     starts = chunk_rows(share)
-    length = upper.shape[0]
+    length = direct_x.shape[0]
     mine = lax.axis_index("dp")
     total = jnp.concatenate(
         [
@@ -180,23 +164,22 @@
     spot = lax.broadcasted_iota(jnp.int32, (16, share), 0)
     digits = jnp.where(spot == 0, high, jnp.where(spot == 1, middle, jnp.where(spot == 2, rest, 0.0)))
     values.append(digits.astype(BF16))
-    chunk = jnp.concatenate(values, axis=0)
-    upper[...] = chunk[0:length]
-    lower[...] = chunk[length:]
+    chunk[...] = jnp.concatenate(values, axis=0)
 
 
 def root_kernel(replicas, count, exact, *rest):
-    chunks = [rest[2 * i : 2 * i + 2] for i in range(replicas)]
-    factor_out, root_out, finished, factor, diagonal = rest[2 * replicas :]
+    own, near, side, far_upper, far_lower, factor_out, root_out, finished, factor, diagonal = rest
     share = root_out.shape[0]
     order = root_out.shape[1]
     half = share // 2
     starts = chunk_rows(share)
-    length = chunks[0][0].shape[0]
+    length = far_upper.shape[0]
     mine = lax.axis_index("dp")
 
     def rows_of(offset, start, count):
-        upper, lower = chunks[offset]
+        if offset < 3:
+            return (own, near, side)[offset][start : start + count, :]
+        upper, lower = far_upper, far_lower
         if start + count <= length:
             return upper[start : start + count, :]
         if start >= length:
@@ -264,25 +247,10 @@
             factor_out[:, columns] = jnp.concatenate([theirs.T, own.T], axis=1)
 
 
-def step_kernel(replicas, *refs):
-    chunks = refs[:replicas]
-    old_root, step_out, grads, result = refs[replicas:]
-    share = old_root.shape[0]
-    strip = step_out.shape[0] // replicas
-    mine = lax.axis_index("dp")
-    for offset, chunk in enumerate(chunks):
-        for part in range(replicas):
-            grads[offset * strip : (offset + 1) * strip, part * share : (part + 1) * share] = chunk[
-                part * strip : (part + 1) * strip, :
-            ]
-    result[...] = lax.dot_general(
+def step_kernel(grads, old_root, step_out):
+    step_out[...] = lax.dot_general(
         grads[...], old_root[...], (((1,), (1,)), ((), ())), preferred_element_type=F32
     ).astype(BF16)
-    for offset in range(replicas):
-        owner = mine ^ offset
-        step_out[pl.ds(pl.multiple_of(owner * strip, strip), strip), :] = result[
-            offset * strip : (offset + 1) * strip, :
-        ]
 
 
 def square_plan(acts, out_grad, old_factor, old_root, iter_count):
@@ -327,20 +295,19 @@
     relay_x, relay_y = swapped(relay_x, 1), swapped(relay_y, 2)
     direct_x, direct_y = swapped(direct_x, 1), swapped(direct_y, 2)
     relay_x, relay_y = call(relay_kernel, [shape(length)] * 2, "relay", keep, relay_x, relay_y)
-    grad_x, grad_y, grad_keep = call(
-        functools.partial(grad_kernel, replicas, tokens * replicas),
-        [shape(grows)] * 2 + [shape(2 * grows, F32)],
+    (partial,) = call(
+        functools.partial(grad_kernel, tokens * replicas),
+        [shape(grows, BF16, order)],
         "grad",
         inputs,
         received,
         after=[relay_x, relay_y],
-        scratch=[pltpu.VMEM((grows, order), F32)],
     )
     relay_x, relay_y = swapped(relay_x, 1), swapped(relay_y, 2)
-    grad_x, grad_y = swapped(grad_x, 1), swapped(grad_y, 2)
-    upper, lower, exact = call(
+    partials = lax.all_to_all(partial, "dp", 0, 0, tiled=True)
+    chunk, exact = call(
         functools.partial(factor_kernel, replicas),
-        [shape(length), shape(length + 16), shape(whole_rows, F32)],
+        [shape(2 * length + 16), shape(whole_rows, F32)],
         "factor",
         keep,
         direct_x,
@@ -349,51 +316,28 @@
         relay_y,
         old_factor[0, 0],
     )
-    upper_x, lower_y = swapped(upper, 1), swapped(lower, 2)
-    lower_x, upper_y = swapped(lower, 1), swapped(upper, 2)
-    strip_x, strip_y = call(
-        grad_relay_kernel, [shape(grows // 2)] * 2, "grad_relay", grad_keep, grad_x, grad_y, after=[upper, lower]
-    )
-    strip_x, strip_y = swapped(strip_x, 1), swapped(strip_y, 2)
-    upper_far, lower_far = swapped(upper_x, 2), swapped(lower_y, 1)
-    (strip,) = call(
-        grad_total_kernel,
-        [shape(grows)],
-        "grad_total",
-        grad_keep,
-        grad_x,
-        grad_y,
-        strip_x,
-        strip_y,
-        after=[upper_x, lower_y],
-    )
-    strips = [strip] + [swapped(strip, offset) for offset in range(1, replicas)]
+    near, side = swapped(chunk, 1), swapped(chunk, 2)
+    lower, upper = call(halves_kernel, [shape(length + 16), shape(length)], "halves", near, side)
+    far_upper, far_lower = swapped(upper, 2), swapped(lower, 1)
+    (strips,) = call(
+        functools.partial(strip_kernel, replicas), [shape(grows, BF16, order)], "strip", partials, after=[upper]
+    )
+    grad16 = lax.all_to_all(strips, "dp", 0, 0, tiled=True)
     factor, root, finished = call(
         functools.partial(root_kernel, replicas),
         [shape(share, F32, order), shape(share, BF16, order), shape(8, F32, 128)],
         "root",
         iter_count,
         exact,
-        upper,
-        lower,
-        upper_x,
-        lower_x,
-        upper_y,
-        lower_y,
-        upper_far,
-        lower_far,
+        chunk,
+        near,
+        side,
+        far_upper,
+        far_lower,
         first=pltpu.SMEM,
         scratch=[pltpu.VMEM((order, order), BF16), pltpu.VMEM((1, order), F32)],
     )
-    (step,) = call(
-        functools.partial(step_kernel, replicas),
-        [shape(grows, BF16, share)],
-        "step",
-        *strips,
-        old_root[0, 0],
-        after=[finished],
-        scratch=[pltpu.VMEM((grows, order), BF16), pltpu.VMEM((grows, share), BF16)],
-    )
+    (step,) = call(step_kernel, [shape(grows, BF16, share)], "step", grad16, old_root[0, 0], after=[finished])
     return (factor[None, None], root[None, None], step[None, None])
 
 

time: 41.7 us -> 53.5 us (1.28)
  local copies, waits for them, and re-layouts: 1.23 us -> 6.65 us
  waiting for transfers between devices: 9.61 us -> 14.2 us
  Pallas kernels: 6.94 us -> 9.76 us
  starting transfers between devices: 22.5 us -> 21.2 us
    ppermute x19 -> x10, starting transfers between devices: 21.9 us -> 13.6 us  [swapped(): lax.ppermute(block, 'dp', [(i, i ^ offset) for i in range(lax.axis_size('...]
    all_to_all x0 -> x2, starting transfers between devices: none -> 7.07 us  [the longest x1 3.6 us: square_plan(): grad16 = lax.all_to_all(strips, 'dp', 0, 0, tiled=True)]
    unnamed x6 -> x22, local copies, waits for them, and re-layouts: 1.23 us -> 6.65 us
    ppermute x19 -> x10, waiting for transfers between devices: 9.61 us -> 14.2 us  [swapped(): lax.ppermute(block, 'dp', [(i, i ^ offset) for i in range(lax.axis_size('...]
    pallas_call x8, Pallas kernels: 6.94 us -> 9.76 us  [call(): pl.pallas_call(body, out_shape=outs, in_specs=in_specs, out_specs=whole(l...]
  transfers between devices with their start and end apart: 20 -> 13, of which waited for: 6 -> 6; matrix products, arithmetic and copies ran while one was open for 0% -> 0% of each run, Pallas kernels for 14% -> 15%
where the time goes in v4:
time: 53.5 us; the launch traced here: 53.2 us
  starting transfers between devices  21.2 us (40%)
  waiting for transfers between devices  14.2 us (27%)
  Pallas kernels  9.76 us (18%)
  local copies, waits for them, and re-layouts  6.65 us (12%)
  between operations  1.36 us (3%)
    ppermute x10, waiting for transfers between devices, swapped(): lax.ppermute(block, 'dp', [(i, i ^ offset) for i in range(lax.axis_size('...  14.2 us
    ppermute x10, starting transfers between devices, swapped(): lax.ppermute(block, 'dp', [(i, i ^ offset) for i in range(lax.axis_size('...  13.6 us
    pallas_call x8, Pallas kernels, call(): pl.pallas_call(body, out_shape=outs, in_specs=in_specs, out_specs=whole(l...  9.76 us
    unnamed x22, local copies, waits for them, and re-layouts  6.65 us
    all_to_all x1, starting transfers between devices, square_plan(): grad16 = lax.all_to_all(strips, 'dp', 0, 0, tiled=True)  3.6 us
    all_to_all x1, starting transfers between devices, square_plan(): partials = lax.all_to_all(partial, 'dp', 0, 0, tiled=True)  3.47 us
  transfers between devices with their start and end apart: 13, of which 6 were waited for; matrix products, arithmetic and copies ran while one was open for 0% of the time, Pallas kernels for 15%

profile of v4, /device:TPU:0, one launch (start us, length us, event | category | flops | bytes accessed | tf_op | source)
XLA Modules:
  0.0 53.2 jit_solution(16098143484714075639)
XLA Ops:
  0.6 0.5 collective-permute-start.10
  1.1 0.0 copy-start
  1.1 1.2 %copy-done = bf16[1,512,1024]{2,1,0:T(8,128)(2,1)S(1)} copy-done((bf16[1,512,1024]{2,1,0:T(8,128)(2,1)S(1)}, bf16[1,512,1024]{2,1,0:T(8,128)(2,1)}, u32[]{:S(2)}) %copy-start) | copy-done | bytes 1048600
  2.4 1.7 %batch.1 = (bf16[288,256]{1,0:T(8,128)(2,1)S(1)}, bf16[288,256]{1,0:T(8,128)(2,1)S(1)}, bf16[288,256]{1,0:T(8,128)(2,1)}, bf16[288,256]{1,0:T(8,128)(2,1)}, f32[1152,256]{1,0:T(8,128)S(1)}) custom-call(bf16[512,1024]{1,0:T(8,128)(2,1)S(1)} %bitcast.11), custom_call_target="tpu_custom_call" | custom-call | tf_op jit(solution)/shard_map/batch/pallas_call | solution.py:277
  4.1 2.5 %collective-permute-start.2 = (bf16[288,256]{1,0:T(8,128)(2,1)S(1)}, bf16[288,256]{1,0:T(8,128)(2,1)S(1)}, u32[]{:S(2)}, u32[]{:S(2)}) collective-permute-start(bf16[288,256]{1,0:T(8,128)(2,1)S(1)} %get-tuple-element.20), channel_id=1, source_target_pairs={{0,4},{4,0},{8,12},{12,8},{1,5},{5,1},{9,13},{13,9},{2,6},{6,2},{1... | collective-permute-start | bytes 442376 | tf_op jit(solution)/shard_map/ppermute | solution.py:26
  6.6 1.5 %collective-permute-start.3 = (bf16[288,256]{1,0:T(8,128)(2,1)S(1)}, bf16[288,256]{1,0:T(8,128)(2,1)S(1)}, u32[]{:S(2)}, u32[]{:S(2)}) collective-permute-start(bf16[288,256]{1,0:T(8,128)(2,1)S(1)} %get-tuple-element.21), channel_id=1, source_target_pairs={{0,8},{4,12},{8,0},{12,4},{1,9},{5,13},{9,1},{13,5},{2,10},{6,14},... | collective-permute-start | bytes 442376 | tf_op jit(solution)/shard_map/ppermute | solution.py:26
  8.1 0.5 %collective-permute-start = (bf16[288,256]{1,0:T(8,128)(2,1)}, bf16[288,256]{1,0:T(8,128)(2,1)S(1)}, u32[]{:S(2)}, u32[]{:S(2)}) collective-permute-start(bf16[288,256]{1,0:T(8,128)(2,1)} %get-tuple-element.18), channel_id=1, source_target_pairs={{0,4},{4,0},{8,12},{12,8},{1,5},{5,1},{9,13},{13,9},{2,6},{6,2},{1... | collective-permute-start | bytes 442376 | tf_op jit(solution)/shard_map/ppermute | solution.py:26
  8.7 0.0 collective-permute-start.1
  8.7 2.6 %collective-permute-done.2.refs_1_ = bf16[288,256]{1,0:T(8,128)(2,1)S(1)} collective-permute-done((bf16[288,256]{1,0:T(8,128)(2,1)S(1)}, bf16[288,256]{1,0:T(8,128)(2,1)S(1)}, u32[]{:S(2)}, u32[]{:S(2)}) %collective-permute-start.2) | collective-permute-done | bytes 147488 | tf_op jit(solution)/shard_map/ppermute | solution.py:26
  11.3 2.0 %collective-permute-done.3.refs_2_ = bf16[288,256]{1,0:T(8,128)(2,1)S(1)} collective-permute-done((bf16[288,256]{1,0:T(8,128)(2,1)S(1)}, bf16[288,256]{1,0:T(8,128)(2,1)S(1)}, u32[]{:S(2)}, u32[]{:S(2)}) %collective-permute-start.3) | collective-permute-done | bytes 147488 | tf_op jit(solution)/shard_map/ppermute | solution.py:26
  13.3 0.7 %relay.1 = (bf16[288,256]{1,0:T(8,128)(2,1)}, bf16[288,256]{1,0:T(8,128)(2,1)S(1)}) custom-call(f32[1152,256]{1,0:T(8,128)S(1)} %get-tuple-element.17.refs_0_, bf16[288,256]{1,0:T(8,128)(2,1)S(1)} %collective-permute-done.2.refs_1_, bf16[288,256]{1,0:T(8,128)(2,1)S(1)} %collective-permute-done.3.refs_2_), custom_call_target="tpu_custom_call" | custom-call | tf_op jit(solution)/shard_map/relay/pallas_call | solution.py:277
  14.0 0.0 collective-permute-start.4
  14.0 2.1 %collective-permute-start.5 = (bf16[288,256]{1,0:T(8,128)(2,1)S(1)}, bf16[288,256]{1,0:T(8,128)(2,1)S(1)}, u32[]{:S(2)}, u32[]{:S(2)}) collective-permute-start(bf16[288,256]{1,0:T(8,128)(2,1)S(1)} %get-tuple-element.23.refs_3_), channel_id=1, source_target_pairs={{0,8},{4,12},{8,0},{12,4},{1,9},{5,13},{9,1},{13,5},{2,10},{6,14},... | collective-permute-start | bytes 442376 | tf_op jit(solution)/shard_map/ppermute | solution.py:26
  16.0 0.0 collective-permute-done.10
  16.0 0.0 copy-start.1
  16.0 1.3 %grad.1 = bf16[256,1024]{1,0:T(8,128)(2,1)} custom-call(bf16[512,1024]{1,0:T(8,128)(2,1)S(1)} %bitcast.12, bf16[512,256]{1,0:T(8,128)(2,1)S(1)} %bitcast.17, bf16[288,256]{1,0:T(8,128)(2,1)} %get-tuple-element.22.refs_2_, bf16[288,256]{1,0:T(8,128)(2,1)S(1)} %get-tuple-element.23.refs_3_), custom_call_target="tpu_custom_call" | custom-call | tf_op jit(solution)/shard_map/grad/pallas_call | solution.py:277
  17.3 3.5 %all-to-all-start = ((bf16[4,64,1024]{2,1,0:T(8,128)(2,1)}), bf16[4,64,1024]{2,1,0:T(8,128)(2,1)S(1)}, u32[]{:S(2)}, u32[]{:S(2)}) async-start(bf16[4,64,1024]{2,1,0:T(8,128)(2,1)} %bitcast.5), calls=%async_computation | async-start | bytes 1048576 | tf_op jit(solution)/shard_map/all_to_all | solution.py:307
  20.8 0.0 collective-permute-done.refs_1_
  20.8 0.0 collective-permute-done.1.refs_2_
  20.8 0.0 copy-start.5
  20.8 0.7 %copy-done.5 = bf16[288,256]{1,0:T(8,128)(2,1)} copy-done((bf16[288,256]{1,0:T(8,128)(2,1)}, bf16[288,256]{1,0:T(8,128)(2,1)S(1)}, u32[]{:S(2)}) %copy-start.5) | copy-done | bytes 147480
  21.5 0.0 collective-permute-done.4.refs_3_
  21.5 0.0 copy-start.7
  21.5 0.7 %copy-done.7 = bf16[288,256]{1,0:T(8,128)(2,1)} copy-done((bf16[288,256]{1,0:T(8,128)(2,1)}, bf16[288,256]{1,0:T(8,128)(2,1)S(1)}, u32[]{:S(2)}) %copy-start.7) | copy-done | bytes 147480
  22.1 0.0 collective-permute-done.5.refs_4_
  22.1 0.0 copy-start.9
  22.1 0.7 %copy-done.9 = bf16[288,256]{1,0:T(8,128)(2,1)} copy-done((bf16[288,256]{1,0:T(8,128)(2,1)}, bf16[288,256]{1,0:T(8,128)(2,1)S(1)}, u32[]{:S(2)}) %copy-start.9) | copy-done | bytes 147480
  22.8 0.0 copy-done.1
  22.8 0.0 copy-start.6
  22.8 0.9 %copy-done.6 = bf16[288,256]{1,0:T(8,128)(2,1)S(1)} copy-done((bf16[288,256]{1,0:T(8,128)(2,1)S(1)}, bf16[288,256]{1,0:T(8,128)(2,1)}, u32[]{:S(2)}) %copy-start.6) | copy-done | bytes 147480
  23.7 0.0 copy-start.8
  23.7 0.9 %copy-done.8 = bf16[288,256]{1,0:T(8,128)(2,1)S(1)} copy-done((bf16[288,256]{1,0:T(8,128)(2,1)S(1)}, bf16[288,256]{1,0:T(8,128)(2,1)}, u32[]{:S(2)}) %copy-start.8) | copy-done | bytes 147480
  24.6 0.0 copy-start.10
  24.6 0.9 %copy-done.10 = bf16[288,256]{1,0:T(8,128)(2,1)S(1)} copy-done((bf16[288,256]{1,0:T(8,128)(2,1)S(1)}, bf16[288,256]{1,0:T(8,128)(2,1)}, u32[]{:S(2)}) %copy-start.10) | copy-done | bytes 147480
  25.5 0.3 factor.1
  25.8 2.0 %collective-permute-start.6 = (bf16[592,256]{1,0:T(8,128)(2,1)S(1)}, bf16[592,256]{1,0:T(8,128)(2,1)S(1)}, u32[]{:S(2)}, u32[]{:S(2)}) collective-permute-start(bf16[592,256]{1,0:T(8,128)(2,1)S(1)} %get-tuple-element.25.refs_2_), channel_id=1, source_target_pairs={{0,4},{4,0},{8,12},{12,8},{1,5},{5,1},{9,13},{13,9},{2,6},{6,2},{1... | collective-permute-start | bytes 909320 | tf_op jit(solution)/shard_map/ppermute | solution.py:26
  27.8 1.5 %collective-permute-start.7 = (bf16[592,256]{1,0:T(8,128)(2,1)S(1)}, bf16[592,256]{1,0:T(8,128)(2,1)S(1)}, u32[]{:S(2)}, u32[]{:S(2)}) collective-permute-start(bf16[592,256]{1,0:T(8,128)(2,1)S(1)} %get-tuple-element.25.refs_2_), channel_id=1, source_target_pairs={{0,8},{4,12},{8,0},{12,4},{1,9},{5,13},{9,1},{13,5},{2,10},{6,14},... | collective-permute-start | bytes 909320 | tf_op jit(solution)/shard_map/ppermute | solution.py:26
  29.3 0.0 copy-start.3
  29.3 0.7 %copy-done.3 = bf16[592,256]{1,0:T(8,128)(2,1)} copy-done((bf16[592,256]{1,0:T(8,128)(2,1)}, bf16[592,256]{1,0:T(8,128)(2,1)S(1)}, u32[]{:S(2)}) %copy-start.3) | copy-done | bytes 303128
  30.0 3.9 %collective-permute-done.6.refs_0_.refs_3_ = bf16[592,256]{1,0:T(8,128)(2,1)S(1)} collective-permute-done((bf16[592,256]{1,0:T(8,128)(2,1)S(1)}, bf16[592,256]{1,0:T(8,128)(2,1)S(1)}, u32[]{:S(2)}, u32[]{:S(2)}) %collective-permute-start.6) | collective-permute-done | bytes 303136 | tf_op jit(solution)/shard_map/ppermute | solution.py:26
  33.9 0.7 %collective-permute-done.7.refs_1_.refs_4_ = bf16[592,256]{1,0:T(8,128)(2,1)S(1)} collective-permute-done((bf16[592,256]{1,0:T(8,128)(2,1)S(1)}, bf16[592,256]{1,0:T(8,128)(2,1)S(1)}, u32[]{:S(2)}, u32[]{:S(2)}) %collective-permute-start.7) | collective-permute-done | bytes 303136 | tf_op jit(solution)/shard_map/ppermute | solution.py:26
  34.7 0.0 copy-start.4
  34.7 0.0 all-to-all-done
  34.7 0.9 %strip.1 = bf16[256,1024]{1,0:T(8,128)(2,1)} custom-call(bf16[256,1024]{1,0:T(8,128)(2,1)S(1)} %bitcast.13, bf16[288,256]{1,0:T(8,128)(2,1)S(1)} %get-tuple-element.26.refs_1_), custom_call_target="tpu_custom_call" | custom-call | tf_op jit(solution)/shard_map/strip/pallas_call | solution.py:277
  35.6 0.0 copy-start.2
  35.6 3.6 %all-to-all-start.1 = ((bf16[4,64,1024]{2,1,0:T(8,128)(2,1)}), bf16[4,64,1024]{2,1,0:T(8,128)(2,1)S(1)}, u32[]{:S(2)}, u32[]{:S(2)}) async-start(bf16[4,64,1024]{2,1,0:T(8,128)(2,1)} %bitcast.7), calls=%async_computation.1 | async-start | bytes 1048576 | tf_op jit(solution)/shard_map/all_to_all | solution.py:325
  39.2 2.0 %collective-permute-start.9 = (bf16[304,256]{1,0:T(8,128)(2,1)S(1)}, bf16[304,256]{1,0:T(8,128)(2,1)S(1)}, u32[]{:S(2)}, u32[]{:S(2)}) collective-permute-start(bf16[304,256]{1,0:T(8,128)(2,1)S(1)} %get-tuple-element.27), channel_id=1, source_target_pairs={{0,4},{4,0},{8,12},{12,8},{1,5},{5,1},{9,13},{13,9},{2,6},{6,2},{1... | collective-permute-start | bytes 466952 | tf_op jit(solution)/shard_map/ppermute | solution.py:26
  41.2 1.5 %collective-permute-start.8 = (bf16[288,256]{1,0:T(8,128)(2,1)S(1)}, bf16[288,256]{1,0:T(8,128)(2,1)S(1)}, u32[]{:S(2)}, u32[]{:S(2)}) collective-permute-start(bf16[288,256]{1,0:T(8,128)(2,1)S(1)} %get-tuple-element.26.refs_1_), channel_id=1, source_target_pairs={{0,8},{4,12},{8,0},{12,4},{1,9},{5,13},{9,1},{13,5},{2,10},{6,14},... | collective-permute-start | bytes 442376 | tf_op jit(solution)/shard_map/ppermute | solution.py:26
  43.3 4.8 %collective-permute-done.8.refs_5_ = bf16[288,256]{1,0:T(8,128)(2,1)S(1)} collective-permute-done((bf16[288,256]{1,0:T(8,128)(2,1)S(1)}, bf16[288,256]{1,0:T(8,128)(2,1)S(1)}, u32[]{:S(2)}, u32[]{:S(2)}) %collective-permute-start.8) | collective-permute-done | bytes 147488 | tf_op jit(solution)/shard_map/ppermute | solution.py:26
  48.1 0.2 collective-permute-done.9.refs_6_
  48.3 0.0 copy-done.4
  48.3 3.9 %root.1 = (f32[256,1024]{1,0:T(8,128)}, bf16[256,1024]{1,0:T(8,128)(2,1)}, f32[8,128]{1,0:T(8,128)S(1)}) custom-call(s32[1,1]{1,0:T(1,128)S(6)} %copy.8.refs_0_, f32[576,256]{1,0:T(8,128)S(1)} %get-tuple-element.24.refs_1_, bf16[592,256]{1,0:T(8,128)(2,1)S(1)} %copy-done.4, bf16[592,256]{1,0:T(8,128)(2,1)S(1)} %collective-permute-done.6.refs_0_.refs_3_, ...), custom_call_target="tpu_custom_call" | custom-call | tf_op jit(solution)/shard_map/root/pallas_call | solution.py:277
  52.2 0.0 all-to-all-done.1
  52.2 0.0 copy-done.2
  52.2 1.0 %step.1 = bf16[256,256]{1,0:T(8,128)(2,1)} custom-call(bf16[256,1024]{1,0:T(8,128)(2,1)S(1)} %bitcast.14, bf16[256,1024]{1,0:T(8,128)(2,1)S(1)} %bitcast.16, f32[8,128]{1,0:T(8,128)S(1)} %get-tuple-element.30.refs_2_), custom_call_target="tpu_custom_call" | custom-call | tf_op jit(solution)/shard_map/step/pallas_call | solution.py:277
  (1 shorter events, 0.0 us)
Async XLA Ops:
  0.6 15.4 %collective-permute-start.10 = (bf16[1,512,256]{2,1,0:T(8,128)(2,1)}, bf16[1,512,256]{2,1,0:T(8,128)(2,1)S(1)}, u32[]{:S(2)}, u32[]{:S(2)}) collective-permute-start(bf16[1,512,256]{2,1,0:T(8,128)(2,1)} %param.6), channel_id=1, source_target_pairs={{16,0},{0,16},{17,1},{1,17},{18,2},{2,18},{19,3},{3,19},{20,4},{4,... | collective-permute-start | bytes 786440 | tf_op jit(solution)/shard_map/ppermute | solution.py:22
  1.1 1.2 %copy-start = (bf16[1,512,1024]{2,1,0:T(8,128)(2,1)S(1)}, bf16[1,512,1024]{2,1,0:T(8,128)(2,1)}, u32[]{:S(2)}) copy-start(bf16[1,512,1024]{2,1,0:T(8,128)(2,1)} %param.5) | copy-start | bytes 3145732
  4.1 7.2 %collective-permute-start.2 = (bf16[288,256]{1,0:T(8,128)(2,1)S(1)}, bf16[288,256]{1,0:T(8,128)(2,1)S(1)}, u32[]{:S(2)}, u32[]{:S(2)}) collective-permute-start(bf16[288,256]{1,0:T(8,128)(2,1)S(1)} %get-tuple-element.20), channel_id=1, source_target_pairs={{0,4},{4,0},{8,12},{12,8},{1,5},{5,1},{9,13},{13,9},{2,6},{6,2},{1... | collective-permute-start | bytes 442376 | tf_op jit(solution)/shard_map/ppermute | solution.py:26
  6.6 6.7 %collective-permute-start.3 = (bf16[288,256]{1,0:T(8,128)(2,1)S(1)}, bf16[288,256]{1,0:T(8,128)(2,1)S(1)}, u32[]{:S(2)}, u32[]{:S(2)}) collective-permute-start(bf16[288,256]{1,0:T(8,128)(2,1)S(1)} %get-tuple-element.21), channel_id=1, source_target_pairs={{0,8},{4,12},{8,0},{12,4},{1,9},{5,13},{9,1},{13,5},{2,10},{6,14},... | collective-permute-start | bytes 442376 | tf_op jit(solution)/shard_map/ppermute | solution.py:26
  8.1 12.7 %collective-permute-start = (bf16[288,256]{1,0:T(8,128)(2,1)}, bf16[288,256]{1,0:T(8,128)(2,1)S(1)}, u32[]{:S(2)}, u32[]{:S(2)}) collective-permute-start(bf16[288,256]{1,0:T(8,128)(2,1)} %get-tuple-element.18), channel_id=1, source_target_pairs={{0,4},{4,0},{8,12},{12,8},{1,5},{5,1},{9,13},{13,9},{2,6},{6,2},{1... | collective-permute-start | bytes 442376 | tf_op jit(solution)/shard_map/ppermute | solution.py:26
  8.7 12.1 %collective-permute-start.1 = (bf16[288,256]{1,0:T(8,128)(2,1)}, bf16[288,256]{1,0:T(8,128)(2,1)S(1)}, u32[]{:S(2)}, u32[]{:S(2)}) collective-permute-start(bf16[288,256]{1,0:T(8,128)(2,1)} %get-tuple-element.19), channel_id=1, source_target_pairs={{0,8},{4,12},{8,0},{12,4},{1,9},{5,13},{9,1},{13,5},{2,10},{6,14},... | collective-permute-start | bytes 442376 | tf_op jit(solution)/shard_map/ppermute | solution.py:26
  14.0 7.5 %collective-permute-start.4 = (bf16[288,256]{1,0:T(8,128)(2,1)}, bf16[288,256]{1,0:T(8,128)(2,1)S(1)}, u32[]{:S(2)}, u32[]{:S(2)}) collective-permute-start(bf16[288,256]{1,0:T(8,128)(2,1)} %get-tuple-element.22.refs_2_), channel_id=1, source_target_pairs={{0,4},{4,0},{8,12},{12,8},{1,5},{5,1},{9,13},{13,9},{2,6},{6,2},{1... | collective-permute-start | bytes 442376 | tf_op jit(solution)/shard_map/ppermute | solution.py:26
  14.0 8.1 %collective-permute-start.5 = (bf16[288,256]{1,0:T(8,128)(2,1)S(1)}, bf16[288,256]{1,0:T(8,128)(2,1)S(1)}, u32[]{:S(2)}, u32[]{:S(2)}) collective-permute-start(bf16[288,256]{1,0:T(8,128)(2,1)S(1)} %get-tuple-element.23.refs_3_), channel_id=1, source_target_pairs={{0,8},{4,12},{8,0},{12,4},{1,9},{5,13},{9,1},{13,5},{2,10},{6,14},... | collective-permute-start | bytes 442376 | tf_op jit(solution)/shard_map/ppermute | solution.py:26
  16.0 6.7 %copy-start.1 = (f32[1,1,256,1024]{3,2,1,0:T(8,128)S(1)}, f32[1,1,256,1024]{3,2,1,0:T(8,128)}, u32[]{:S(2)}) copy-start(f32[1,1,256,1024]{3,2,1,0:T(8,128)} %param.7) | copy-start | bytes 3145732
  17.3 17.4 %all-to-all-start = ((bf16[4,64,1024]{2,1,0:T(8,128)(2,1)}), bf16[4,64,1024]{2,1,0:T(8,128)(2,1)S(1)}, u32[]{:S(2)}, u32[]{:S(2)}) async-start(bf16[4,64,1024]{2,1,0:T(8,128)(2,1)} %bitcast.5), calls=%async_computation | async-start | bytes 1048576 | tf_op jit(solution)/shard_map/all_to_all | solution.py:307
  20.8 0.7 %copy-start.5 = (bf16[288,256]{1,0:T(8,128)(2,1)}, bf16[288,256]{1,0:T(8,128)(2,1)S(1)}, u32[]{:S(2)}) copy-start(bf16[288,256]{1,0:T(8,128)(2,1)S(1)} %collective-permute-done.1.refs_2_) | copy-start | bytes 442372
  21.5 0.7 %copy-start.7 = (bf16[288,256]{1,0:T(8,128)(2,1)}, bf16[288,256]{1,0:T(8,128)(2,1)S(1)}, u32[]{:S(2)}) copy-start(bf16[288,256]{1,0:T(8,128)(2,1)S(1)} %collective-permute-done.4.refs_3_) | copy-start | bytes 442372
  22.1 0.7 %copy-start.9 = (bf16[288,256]{1,0:T(8,128)(2,1)}, bf16[288,256]{1,0:T(8,128)(2,1)S(1)}, u32[]{:S(2)}) copy-start(bf16[288,256]{1,0:T(8,128)(2,1)S(1)} %collective-permute-done.5.refs_4_) | copy-start | bytes 442372
  22.8 0.9 %copy-start.6 = (bf16[288,256]{1,0:T(8,128)(2,1)S(1)}, bf16[288,256]{1,0:T(8,128)(2,1)}, u32[]{:S(2)}) copy-start(bf16[288,256]{1,0:T(8,128)(2,1)} %copy-done.5) | copy-start | bytes 442372
  23.7 0.9 %copy-start.8 = (bf16[288,256]{1,0:T(8,128)(2,1)S(1)}, bf16[288,256]{1,0:T(8,128)(2,1)}, u32[]{:S(2)}) copy-start(bf16[288,256]{1,0:T(8,128)(2,1)} %copy-done.7) | copy-start | bytes 442372
  24.6 0.9 %copy-start.10 = (bf16[288,256]{1,0:T(8,128)(2,1)S(1)}, bf16[288,256]{1,0:T(8,128)(2,1)}, u32[]{:S(2)}) copy-start(bf16[288,256]{1,0:T(8,128)(2,1)} %copy-done.9) | copy-start | bytes 442372
  25.8 8.1 %collective-permute-start.6 = (bf16[592,256]{1,0:T(8,128)(2,1)S(1)}, bf16[592,256]{1,0:T(8,128)(2,1)S(1)}, u32[]{:S(2)}, u32[]{:S(2)}) collective-permute-start(bf16[592,256]{1,0:T(8,128)(2,1)S(1)} %get-tuple-element.25.refs_2_), channel_id=1, source_target_pairs={{0,4},{4,0},{8,12},{12,8},{1,5},{5,1},{9,13},{13,9},{2,6},{6,2},{1... | collective-permute-start | bytes 909320 | tf_op jit(solution)/shard_map/ppermute | solution.py:26
  27.8 6.8 %collective-permute-start.7 = (bf16[592,256]{1,0:T(8,128)(2,1)S(1)}, bf16[592,256]{1,0:T(8,128)(2,1)S(1)}, u32[]{:S(2)}, u32[]{:S(2)}) collective-permute-start(bf16[592,256]{1,0:T(8,128)(2,1)S(1)} %get-tuple-element.25.refs_2_), channel_id=1, source_target_pairs={{0,8},{4,12},{8,0},{12,4},{1,9},{5,13},{9,1},{13,5},{2,10},{6,14},... | collective-permute-start | bytes 909320 | tf_op jit(solution)/shard_map/ppermute | solution.py:26
  29.3 0.7 %copy-start.3 = (bf16[592,256]{1,0:T(8,128)(2,1)}, bf16[592,256]{1,0:T(8,128)(2,1)S(1)}, u32[]{:S(2)}) copy-start(bf16[592,256]{1,0:T(8,128)(2,1)S(1)} %get-tuple-element.25.refs_2_) | copy-start | bytes 909316
  34.7 13.6 %copy-start.4 = (bf16[592,256]{1,0:T(8,128)(2,1)S(1)}, bf16[592,256]{1,0:T(8,128)(2,1)}, u32[]{:S(2)}) copy-start(bf16[592,256]{1,0:T(8,128)(2,1)} %copy-done.3) | copy-start | bytes 909316
  35.6 16.6 %copy-start.2 = (bf16[1,1,256,1024]{3,2,1,0:T(8,128)(2,1)S(1)}, bf16[1,1,256,1024]{3,2,1,0:T(8,128)(2,1)}, u32[]{:S(2)}) copy-start(bf16[1,1,256,1024]{3,2,1,0:T(8,128)(2,1)} %param.8) | copy-start | bytes 1572868
  35.6 16.6 %all-to-all-start.1 = ((bf16[4,64,1024]{2,1,0:T(8,128)(2,1)}), bf16[4,64,1024]{2,1,0:T(8,128)(2,1)S(1)}, u32[]{:S(2)}, u32[]{:S(2)}) async-start(bf16[4,64,1024]{2,1,0:T(8,128)(2,1)} %bitcast.7), calls=%async_computation.1 | async-start | bytes 1048576 | tf_op jit(solution)/shard_map/all_to_all | solution.py:325
  39.2 9.1 %collective-permute-start.9 = (bf16[304,256]{1,0:T(8,128)(2,1)S(1)}, bf16[304,256]{1,0:T(8,128)(2,1)S(1)}, u32[]{:S(2)}, u32[]{:S(2)}) collective-permute-start(bf16[304,256]{1,0:T(8,128)(2,1)S(1)} %get-tuple-element.27), channel_id=1, source_target_pairs={{0,4},{4,0},{8,12},{12,8},{1,5},{5,1},{9,13},{13,9},{2,6},{6,2},{1... | collective-permute-start | bytes 466952 | tf_op jit(solution)/shard_map/ppermute | solution.py:26
  41.2 6.9 %collective-permute-start.8 = (bf16[288,256]{1,0:T(8,128)(2,1)S(1)}, bf16[288,256]{1,0:T(8,128)(2,1)S(1)}, u32[]{:S(2)}, u32[]{:S(2)}) collective-permute-start(bf16[288,256]{1,0:T(8,128)(2,1)S(1)} %get-tuple-element.26.refs_1_), channel_id=1, source_target_pairs={{0,8},{4,12},{8,0},{12,4},{1,9},{5,13},{9,1},{13,5},{2,10},{6,14},... | collective-permute-start | bytes 442376 | tf_op jit(solution)/shard_map/ppermute | solution.py:26

commit v5 on v0

v5 whole, which is shorter than its diff:
```python
import functools
import math

import jax
import jax.numpy as jnp
from jax import lax
from jax.experimental import pallas as pl
from jax.experimental.pallas import tpu as pltpu
from jax.sharding import PartitionSpec as P

DECAY = 0.75
DAMPING = 0.1
EPSILON = 1e-06
BF16 = jnp.bfloat16
F32 = jnp.float32
VMEM_LIMIT = 28 * 1024 * 1024


def passed_along(block, axis, distance):
    devices = range(lax.axis_size(axis))
    route = [((i - distance) % len(devices), i) for i in devices]
    return lax.ppermute(block, axis, route)


def swapped(block, offset):
    return lax.ppermute(block, "dp", [(i, i ^ offset) for i in range(lax.axis_size("dp"))])


def eye_of(rows, cols, shift=0):
    row_ids = lax.broadcasted_iota(jnp.int32, (rows, cols), 0) + shift
    col_ids = lax.broadcasted_iota(jnp.int32, (rows, cols), 1)
    return (row_ids == col_ids).astype(F32)


def whole(count):
    return [pl.BlockSpec(memory_space=pltpu.VMEM)] * count


def transposed(block):
    return block.astype(F32).T.astype(block.dtype)


OVER_ROWS = (((0,), (0,)), ((), ()))
FIRST_WAVE = (1, 3)


def first_starts(share):
    half = share // 2
    return 0, half, half + half // 2, 2 * half + half // 2, 3 * half + half // 2


def shared_half(owner, offset, share):
    other = owner ^ offset
    low, high = jnp.minimum(owner, other), jnp.maximum(owner, other)
    row = low * share + jnp.where(owner > other, share // 2, 0)
    return pl.multiple_of(row, share // 2), pl.multiple_of(high * share, share)


def side_by_side(low):
    half = low.shape[0] // 2
    return jnp.concatenate([low[0:half], low[half:]], axis=1)


def stacked(packed):
    half = packed.shape[1] // 2
    return jnp.concatenate([packed[:, 0:half], packed[:, half:]], axis=0)


def store_wave(pieces, length, upper, lower):
    for start, piece in pieces:
        stop = start + piece.shape[0]
        for target, low, high in ((upper, 0, length), (lower, length, stop)):
            first, last = max(start, low), min(stop, high)
            if first < last:
                ref, at = target
                ref[at + first - low : at + last - low, :] = piece[first - start : last - start].astype(ref.dtype)


def store_messages(pieces, send_x, send_y, keep):
    length = send_x.shape[0] // 2
    store_wave(pieces(3), length, (send_x, 0), (send_y, 0))
    store_wave(pieces(1), length, (send_x, length), (keep, 3 * length))
    store_wave(pieces(2), length, (keep, 2 * length), (send_y, length))
    store_wave(pieces(0), length, (keep, 0), (keep, length))


def batch_kernel(replicas, tokens_all, acts, send_x, send_y, keep, rest, batch):
    order = acts.shape[1]
    share = order // replicas
    half = share // 2
    starts = first_starts(share)
    mine = lax.axis_index("dp")
    for i in range(replicas):
        band = slice(i * share, (i + 1) * share)
        batch[band, i * share :] = lax.dot_general(
            acts[:, band], acts[:, i * share :], OVER_ROWS, preferred_element_type=F32
        ) * (1.0 / tokens_all)

    def shared(owner, offset):
        row, col = shared_half(owner, offset, share)
        return batch[pl.ds(row, half), pl.ds(col, share)]

    def pieces(offset):
        owner = mine ^ offset
        base = pl.multiple_of(owner * share, share)
        corner = pl.multiple_of(owner * share + half, half)
        yield starts[0], batch[pl.ds(base, half), pl.ds(base, share)]
        yield starts[1], side_by_side(batch[pl.ds(corner, half), pl.ds(corner, half)])
        for start, step in zip(starts[2:], FIRST_WAVE):
            yield start, shared(owner, step)

    store_messages(pieces, send_x, send_y, keep)
    for offset in range(replicas):
        rest[offset * half : (offset + 1) * half, :] = shared(mine ^ offset, 2)


def grad_kernel(replicas, tokens_all, acts, grads, rest, send_x, send_y, keep, total):
    share = acts.shape[1] // replicas
    half = share // 2
    strip = grads.shape[1] // replicas
    mine = lax.axis_index("dp")
    total[...] = lax.dot_general(grads[...], acts[...], OVER_ROWS, preferred_element_type=F32) * (
        1.0 / math.sqrt(tokens_all)
    )

    def pieces(offset):
        yield 0, rest[offset * half : (offset + 1) * half, :]
        rows = pl.ds(pl.multiple_of((mine ^ offset) * strip, strip), strip)
        for part in range(replicas):
            yield half + part * strip, total[rows, part * share : (part + 1) * share]

    store_messages(pieces, send_x, send_y, keep)


def relay_kernel(keep, got_x, got_y, send_x, send_y):
    length = send_x.shape[0]
    send_y[...] = (keep[2 * length : 3 * length, :] + got_x[0:length, :].astype(F32)).astype(BF16)
    send_x[...] = (keep[3 * length :, :] + got_y[0:length, :].astype(F32)).astype(BF16)


def wave_total(keep, got_x, got_y, relay_x, relay_y):
    length = relay_x.shape[0]
    upper = keep[0:length, :] + got_x[length:, :].astype(F32) + relay_y[...].astype(F32)
    lower = keep[length : 2 * length, :] + got_y[length:, :].astype(F32) + relay_x[...].astype(F32)
    return jnp.concatenate([upper, lower], axis=0)


def old_half(old, mine, offset):
    share = old.shape[0]
    half = share // 2
    other = mine ^ offset
    block = old[:, pl.ds(pl.multiple_of(other * share, share), share)]
    return jnp.where(mine < other, block[0:half], block[:, half:].T)


def column_sums(value):
    return jnp.sum(value * value, axis=0, keepdims=True)


def first_factor_kernel(keep, got_x, got_y, relay_x, relay_y, old, chunk, exact, squares):
    share = old.shape[0]
    half = share // 2
    starts = first_starts(share)
    mine = lax.axis_index("dp")
    total = wave_total(keep, got_x, got_y, relay_x, relay_y)
    diagonal = old[:, pl.ds(pl.multiple_of(mine * share, share), share)]
    terms = [
        DECAY * diagonal[0:half] + DAMPING * eye_of(half, share),
        side_by_side(DECAY * diagonal[half:, half:] + DAMPING * eye_of(half, half)),
    ] + [DECAY * old_half(old, mine, offset) for offset in FIRST_WAVE]
    column = lax.broadcasted_iota(jnp.int32, (1, share), 1)
    weights = [jnp.where(column < half, 1.0, 2.0), 1.0, 2.0, 2.0]
    sums = jnp.zeros((1, share), F32)
    for start, term, weight in zip(starts, terms, weights):
        rows = slice(start, start + term.shape[0])
        value = term + (1.0 - DECAY) * total[rows]
        exact[rows, :] = value
        chunk[rows, :] = value.astype(BF16)
        sums = sums + weight * column_sums(value)
    squares[...] = sums


def second_factor_kernel(keep, got_x, got_y, relay_x, relay_y, old, squares, chunk, exact):
    share = old.shape[0]
    half = share // 2
    total = wave_total(keep, got_x, got_y, relay_x, relay_y)
    length = total.shape[0]
    value = DECAY * old_half(old, lax.axis_index("dp"), 2) + (1.0 - DECAY) * total[0:half]
    exact[...] = value
    chunk[0:half, :] = value.astype(BF16)
    chunk[half:length, :] = total[half:].astype(BF16)
    sums = squares[...] + 2.0 * column_sums(value)
    high = sums.astype(BF16).astype(F32)
    middle = (sums - high).astype(BF16).astype(F32)
    rest = sums - high - middle
    spot = lax.broadcasted_iota(jnp.int32, (chunk.shape[0] - length, share), 0)
    digits = jnp.where(spot == 0, high, jnp.where(spot == 1, middle, jnp.where(spot == 2, rest, 0.0)))
    chunk[length:, :] = digits.astype(BF16)


def halves_kernel(got_x, got_y, send_x, send_y):
    length = send_y.shape[0]
    send_y[...] = got_x[0:length, :]
    send_x[...] = got_y[length:, :]


def place(factor, diagonal, owner, first, second, share):
    half = share // 2
    starts = first_starts(share)
    base = pl.multiple_of(owner * share, share)
    corner = pl.multiple_of(owner * share + half, half)
    top = first(starts[0], half)
    low = stacked(first(starts[1], half // 2))
    factor[pl.ds(base, half), pl.ds(base, share)] = top
    factor[pl.ds(corner, half), pl.ds(base, half)] = transposed(top[:, half:])
    factor[pl.ds(corner, half), pl.ds(corner, half)] = low
    eye = eye_of(half, half)
    diagonal[:, pl.ds(base, half)] = jnp.sum(top[:, 0:half].astype(F32) * eye, axis=0, keepdims=True)
    diagonal[:, pl.ds(corner, half)] = jnp.sum(low.astype(F32) * eye, axis=0, keepdims=True)
    blocks = [(step, first(start, half)) for start, step in zip(starts[2:], FIRST_WAVE)]
    for step, block in blocks + [(2, second(0, half))]:
        row, col = shared_half(owner, step, share)
        factor[pl.ds(row, half), pl.ds(col, share)] = block
        factor[pl.ds(col, share), pl.ds(row, half)] = transposed(block)


def rows_of(upper, lower=None):
    def read(start, count):
        if lower is None:
            return upper[start : start + count, :]
        length = upper.shape[0]
        if start + count <= length:
            return upper[start : start + count, :]
        if start >= length:
            return lower[start - length : start - length + count, :]
        return jnp.concatenate([upper[start:, :], lower[0 : start + count - length, :]], axis=0)

    return read


def near_kernel(own, own_rest, x, x_rest, y, y_rest, factor, diagonal):
    share = own.shape[1]
    mine = lax.axis_index("dp")
    for offset, (first, second) in enumerate([(own, own_rest), (x, x_rest), (y, y_rest)]):
        place(factor, diagonal, mine ^ offset, rows_of(first), rows_of(second), share)


def new_rows_kernel(exact, exact_rest, x, y_rest, far_upper, far_lower, factor_out):
    share = factor_out.shape[0]
    half = share // 2
    starts = first_starts(share)
    mine = lax.axis_index("dp")
    own_columns = pl.ds(pl.multiple_of(mine * share, share), share)
    top = exact[0:half, :]
    factor_out[0:half, own_columns] = top
    factor_out[half:, own_columns] = jnp.concatenate(
        [top[:, half:].T, stacked(exact[starts[1] : starts[2], :])], axis=1
    )
    pairs = [
        (1, exact[starts[2] : starts[3], :], x[starts[2] : starts[3], :]),
        (2, exact_rest[...], y_rest[0:half, :]),
        (3, exact[starts[3] : starts[4], :], rows_of(far_upper, far_lower)(starts[3], half)),
    ]
    for step, own, theirs in pairs:
        other = mine ^ step
        columns = pl.ds(pl.multiple_of(other * share, share), share)
        theirs = theirs.astype(F32)

        @pl.when(mine < other)
        def _():
            factor_out[0:half, columns] = own
            factor_out[half:, columns] = theirs

        @pl.when(mine > other)
        def _():
            factor_out[:, columns] = jnp.concatenate([theirs.T, own.T], axis=1)


def root_kernel(
    replicas, count, known, known_diagonal, upper, lower, own_rest, x_rest, y_rest, upper_rest, lower_rest, old_root,
    root_out, step_out, factor, diagonal, grads, result,
):
    share = root_out.shape[0]
    order = root_out.shape[1]
    half = share // 2
    strip = step_out.shape[0] // replicas
    digits = half + replicas * strip
    mine = lax.axis_index("dp")
    diagonal[...] = known_diagonal[...]
    seconds = [rows_of(own_rest), rows_of(x_rest), rows_of(y_rest), rows_of(upper_rest, lower_rest)]
    place(factor, diagonal, mine ^ 3, rows_of(upper, lower), seconds[3], share)
    squares = jnp.zeros((16, share), F32)
    for second in seconds:
        squares = squares + second(digits, 16).astype(F32)
    scale = jnp.sqrt(jnp.sum(squares, keepdims=True) / order + EPSILON)
    inverse = 1.0 / scale
    ones = (diagonal[...] * inverse).astype(BF16).astype(F32)
    lift = (1.5 - 0.5 * ones).astype(BF16).astype(F32) + 0.5 * (diagonal[...] * inverse)
    eye = eye_of(share, order, mine * share)
    my_rows = pl.ds(pl.multiple_of(mine * share, share), share)
    first = (factor[my_rows, :].astype(F32) * inverse).astype(BF16).astype(F32)
    turn = (1.5 * eye - 0.5 * first).astype(BF16)
    second = (jnp.dot(turn, factor[...], preferred_element_type=F32) * inverse).astype(BF16)
    product = (-0.5 * inverse) * jnp.dot(second, factor[...], preferred_element_type=F32) + second.astype(F32) * lift
    turn_two = (1.5 * eye - 0.5 * product).astype(BF16)
    inverse_rows = (-0.5 * inverse) * jnp.dot(
        turn_two, factor[...], preferred_element_type=F32
    ) + turn_two.astype(F32) * lift
    chosen = jnp.where(count[0, 0] == 1, turn.astype(F32), inverse_rows)
    root_out[...] = (chosen * lax.rsqrt(scale)).astype(BF16)

    for offset, second in enumerate(seconds):
        for part in range(replicas):
            grads[offset * strip : (offset + 1) * strip, part * share : (part + 1) * share] = second(
                half + part * strip, strip
            )
    result[...] = lax.dot_general(
        grads[...], old_root[...], (((1,), (1,)), ((), ())), preferred_element_type=F32
    ).astype(BF16)
    for offset in range(replicas):
        owner = mine ^ offset
        step_out[pl.ds(pl.multiple_of(owner * strip, strip), strip), :] = result[
            offset * strip : (offset + 1) * strip, :
        ]


def square_plan(acts, out_grad, old_factor, old_root, iter_count):
    replicas = lax.axis_size("dp")
    inputs = acts[0]
    tokens, order = inputs.shape
    share = order // replicas
    half = share // 2
    grows = out_grad.shape[2]
    old = old_factor[0, 0]
    params = pltpu.CompilerParams(vmem_limit_bytes=VMEM_LIMIT)
    first = first_starts(share)[-1]
    second = half + grows
    digits = 16

    def shape(rows, kind=BF16, columns=share):
        return jax.ShapeDtypeStruct((rows, columns), kind)

    def call(kernel, outs, name, *operands, in_smem=(), aliases=None, after=(), scratch=()):
        in_specs = whole(len(operands)) + [pl.BlockSpec(memory_space=pl.ANY)] * len(after)
        for i in in_smem:
            in_specs[i] = pl.BlockSpec(memory_space=pltpu.SMEM)

        def body(*refs):
            kernel(*refs[: len(operands)], *refs[len(operands) + len(after) :])

        return pl.pallas_call(
            body,
            out_shape=outs,
            in_specs=in_specs,
            out_specs=whole(len(outs)),
            scratch_shapes=scratch,
            input_output_aliases=aliases or {},
            compiler_params=params,
            name=name,
        )(*operands, *after)

    def both(x, y):
        return swapped(x, 1), swapped(y, 2)

    received = passed_along(out_grad, "pipe", -1)[0]
    x1, y1, keep1, rest = call(
        functools.partial(batch_kernel, replicas, tokens * replicas),
        [shape(first)] * 2 + [shape(2 * first, F32), shape(replicas * half, F32)],
        "batch",
        inputs,
        scratch=[pltpu.VMEM((order, order), F32)],
    )
    x1, y1 = both(x1, y1)
    x2, y2, keep2 = call(
        functools.partial(grad_kernel, replicas, tokens * replicas),
        [shape(second)] * 2 + [shape(2 * second, F32)],
        "grad",
        inputs,
        received,
        rest,
        scratch=[pltpu.VMEM((grows, order), F32)],
    )
    x2, y2 = both(x2, y2)
    relay_x1, relay_y1 = both(*call(relay_kernel, [shape(first // 2)] * 2, "relay", keep1, x1, y1))
    relay_x2, relay_y2 = both(*call(relay_kernel, [shape(second // 2)] * 2, "relay_rest", keep2, x2, y2))
    own1, exact1, squares = call(
        first_factor_kernel,
        [shape(first), shape(first, F32), shape(1, F32)],
        "factor",
        keep1,
        x1,
        y1,
        relay_x1,
        relay_y1,
        old,
    )
    near1, side1 = both(own1, own1)
    own2, exact2 = call(
        second_factor_kernel,
        [shape(second + digits), shape(half, F32)],
        "factor_rest",
        keep2,
        x2,
        y2,
        relay_x2,
        relay_y2,
        old,
        squares,
    )
    near2, side2 = both(own2, own2)
    on_x1, on_y1 = call(halves_kernel, [shape(first // 2)] * 2, "halves", near1, side1)
    lower1, upper1 = both(on_x1, on_y1)
    on_x2, on_y2 = call(
        halves_kernel,
        [shape(second // 2 + digits), shape(second // 2)],
        "halves_rest",
        near2,
        side2,
        after=[on_x1],
    )
    lower2, upper2 = both(on_x2, on_y2)
    known, diagonal = call(
        near_kernel,
        [shape(order, BF16, order), shape(1, F32, order)],
        "near",
        own1,
        own2,
        near1,
        near2,
        side1,
        side2,
        after=[on_x2],
    )
    (factor,) = call(
        new_rows_kernel,
        [shape(share, F32, order)],
        "new_rows",
        exact1,
        exact2,
        near1,
        side2,
        upper1,
        lower1,
        after=[diagonal],
    )
    root, step, _ = call(
        functools.partial(root_kernel, replicas),
        [shape(share, BF16, order), shape(grows), shape(order, BF16, order)],
        "root",
        iter_count,
        known,
        diagonal,
        upper1,
        lower1,
        own2,
        near2,
        side2,
        upper2,
        lower2,
        old_root[0, 0],
        in_smem=[0],
        aliases={1: 2},
        scratch=[
            pltpu.VMEM((1, order), F32),
            pltpu.VMEM((grows, order), BF16),
            pltpu.VMEM((grows, share), BF16),
        ],
    )
    return (factor[None, None], root[None, None], step[None, None])


def ring_plan(acts, out_grad, old_factor, old_root, iter_count):
    inputs = acts[0]
    replicas = lax.axis_size("dp")
    tokens_all = inputs.shape[0] * replicas
    order = inputs.shape[1]
    share = order // replicas
    offset = lax.axis_index("dp") * share
    received = passed_along(out_grad, "pipe", -1)[0]
    partial_grad = jnp.dot(received.T, inputs, preferred_element_type=F32) / math.sqrt(tokens_all)
    batch = lax.psum_scatter(
        jnp.dot(inputs.T, inputs, preferred_element_type=F32) / tokens_all,
        "dp",
        scatter_dimension=0,
        tiled=True,
    )
    eye_rows = eye_of(share, order, offset)
    factor = DECAY * old_factor[0, 0] + (1.0 - DECAY) * batch + DAMPING * eye_rows
    grad16 = lax.psum(partial_grad, "dp").astype(BF16)
    scale = jnp.sqrt(lax.psum(jnp.sum(factor * factor), "dp") / order + EPSILON)
    step = lax.dot_general(
        grad16, old_root[0, 0], (((1,), (1,)), ((), ())), preferred_element_type=F32
    ).astype(BF16)
    first = lax.all_gather((factor / scale).astype(BF16), "dp", axis=0, tiled=True)
    turn_one = (1.5 * eye_of(order, order) - 0.5 * first.astype(F32)).astype(BF16)
    turn_rows = lax.dynamic_slice_in_dim(turn_one, offset, share, 0)
    second = jnp.dot(turn_rows, first, preferred_element_type=F32).astype(BF16)
    product = jnp.dot(second, turn_one, preferred_element_type=F32)
    turn_two = (1.5 * eye_rows - 0.5 * product).astype(BF16)
    inverse_rows = jnp.dot(turn_two, turn_one, preferred_element_type=F32)
    chosen = jnp.where(iter_count[0, 0] == 1, turn_rows.astype(F32), inverse_rows)
    root = (chosen / jnp.sqrt(scale)).astype(BF16)
    return (factor[None, None], root[None, None], step[None, None])


def solution(mesh):
    return jax.shard_map(
        square_plan if mesh.shape["dp"] == 4 else ring_plan,
        mesh=mesh,
        in_specs=(
            P("pipe", "dp", "tensor"),
            P("pipe", "dp", "tensor"),
            P("pipe", "tensor", "dp", None),
            P("pipe", "tensor", "dp", None),
            P("pipe", "tensor"),
        ),
        out_specs=(
            P("pipe", "tensor", "dp", None),
            P("pipe", "tensor", "dp", None),
            P("pipe", "tensor", None, "dp"),
        ),
        check_vma=False,
    )
```

time: 199 us -> 43.6 us (0.22)
  waiting for transfers between devices: 121 us -> 14.4 us
  blocking collectives: 42.7 us -> 0 us
  starting transfers between devices: 0.63 us -> 19.4 us
  between operations: 15.2 us -> 1.36 us
  matrix products: 11.8 us -> 0 us
  Pallas kernels: 0 us -> 6.99 us
  other arithmetic: 5.71 us -> 0 us
    all_gather x2 -> x0, waiting for transfers between devices: 66.7 us -> none  [the longest x1 35.1 us: local(): first_full = lax.all_gather(first_rows, 'dp', axis=0, tiled=True)]
    reduce_scatter x1 -> x0, waiting for transfers between devices: 53.4 us -> none  [local(): lax.psum_scatter(jnp.dot(columns.T, inputs, preferred_element_type=jnp.fl...]
    psum x1 -> x0, blocking collectives: 42.7 us -> none  [local(): square_total = lax.psum(squares, 'dp')]
    ppermute x0 -> x16, starting transfers between devices: none -> 18.9 us  [swapped(): lax.ppermute(block, 'dp', [(i, i ^ offset) for i in range(lax.axis_size('...]
    ppermute x0 -> x16, waiting for transfers between devices: none -> 14.4 us  [swapped(): lax.ppermute(block, 'dp', [(i, i ^ offset) for i in range(lax.axis_size('...]
    dot_general x5 -> x0, matrix products: 11.8 us -> none  [the longest x1 3.76 us: local(): jnp.dot(turn_two, turn_one, preferred_element_type=jnp.float32)]
    pallas_call x0 -> x11, Pallas kernels: none -> 6.99 us  [call(): pl.pallas_call(body, out_shape=outs, in_specs=in_specs, out_specs=whole(l...]
    convert_element_type x2 -> x0, other arithmetic: 3.06 us -> none  [the longest x1 2.15 us: local(): (1.5 * eye_full - 0.5 * first_full.astype(jnp.float32)).astype(jnp.bfloat16)]
  transfers between devices with their start and end apart: 4 -> 17, of which waited for: 4 -> 10; matrix products, arithmetic and copies ran while one was open for 2% -> 0% of each run, Pallas kernels for 0% -> 9%
where the time goes in v5:
time: 43.6 us; the launch traced here: 43.4 us
  starting transfers between devices  19.4 us (44%)
  waiting for transfers between devices  14.4 us (33%)
  Pallas kernels  6.99 us (16%)
  between operations  1.36 us (3%)
  local copies, waits for them, and re-layouts  1.23 us (3%)
    ppermute x16, starting transfers between devices, swapped(): lax.ppermute(block, 'dp', [(i, i ^ offset) for i in range(lax.axis_size('...  18.9 us
    ppermute x16, waiting for transfers between devices, swapped(): lax.ppermute(block, 'dp', [(i, i ^ offset) for i in range(lax.axis_size('...  14.4 us
    pallas_call x11, Pallas kernels, call(): pl.pallas_call(body, out_shape=outs, in_specs=in_specs, out_specs=whole(l...  6.99 us
    unnamed x6, local copies, waits for them, and re-layouts  1.23 us
  transfers between devices with their start and end apart: 17, of which 10 were waited for; matrix products, arithmetic and copies ran while one was open for 0% of the time, Pallas kernels for 9%

profile of v5, /device:TPU:0, one launch (start us, length us, event | category | flops | bytes accessed | tf_op | source)
XLA Modules:
  0.0 43.4 jit_solution(14121434575716313182)
XLA Ops:
  0.6 0.5 %collective-permute-start.4 = (bf16[1,512,256]{2,1,0:T(8,128)(2,1)}, bf16[1,512,256]{2,1,0:T(8,128)(2,1)S(1)}, u32[]{:S(2)}, u32[]{:S(2)}) collective-permute-start(bf16[1,512,256]{2,1,0:T(8,128)(2,1)} %param.6), channel_id=1, source_target_pairs={{16,0},{0,16},{17,1},{1,17},{18,2},{2,18},{19,3},{3,19},{20,4},{4,... | collective-permute-start | bytes 786440 | tf_op jit(solution)/shard_map/ppermute | solution.py:22
  1.1 0.0 copy-start
  1.1 1.2 %copy-done = bf16[1,512,1024]{2,1,0:T(8,128)(2,1)S(1)} copy-done((bf16[1,512,1024]{2,1,0:T(8,128)(2,1)S(1)}, bf16[1,512,1024]{2,1,0:T(8,128)(2,1)}, u32[]{:S(2)}) %copy-start) | copy-done | bytes 1048600
  2.4 1.1 %batch.1 = (bf16[448,256]{1,0:T(8,128)(2,1)S(1)}, bf16[448,256]{1,0:T(8,128)(2,1)S(1)}, f32[896,256]{1,0:T(8,128)S(1)}, f32[512,256]{1,0:T(8,128)S(1)}) custom-call(bf16[512,1024]{1,0:T(8,128)(2,1)S(1)} %bitcast.7), custom_call_target="tpu_custom_call" | custom-call | tf_op jit(solution)/shard_map/batch/pallas_call | solution.py:351
  3.4 2.6 %collective-permute-start = (bf16[448,256]{1,0:T(8,128)(2,1)S(1)}, bf16[448,256]{1,0:T(8,128)(2,1)S(1)}, u32[]{:S(2)}, u32[]{:S(2)}) collective-permute-start(bf16[448,256]{1,0:T(8,128)(2,1)S(1)} %get-tuple-element.28), channel_id=1, source_target_pairs={{0,4},{4,0},{8,12},{12,8},{1,5},{5,1},{9,13},{13,9},{2,6},{6,2},{1... | collective-permute-start | bytes 688136 | tf_op jit(solution)/shard_map/ppermute | solution.py:26
  6.0 1.5 %collective-permute-start.1 = (bf16[448,256]{1,0:T(8,128)(2,1)S(1)}, bf16[448,256]{1,0:T(8,128)(2,1)S(1)}, u32[]{:S(2)}, u32[]{:S(2)}) collective-permute-start(bf16[448,256]{1,0:T(8,128)(2,1)S(1)} %get-tuple-element.29), channel_id=1, source_target_pairs={{0,8},{4,12},{8,0},{12,4},{1,9},{5,13},{9,1},{13,5},{2,10},{6,14},... | collective-permute-start | bytes 688136 | tf_op jit(solution)/shard_map/ppermute | solution.py:26
  7.5 0.0 collective-permute-done.4
  7.5 0.0 copy-start.1
  7.5 0.5 %grad.1 = (bf16[384,256]{1,0:T(8,128)(2,1)S(1)}, bf16[384,256]{1,0:T(8,128)(2,1)S(1)}, f32[768,256]{1,0:T(8,128)S(1)}) custom-call(bf16[512,1024]{1,0:T(8,128)(2,1)S(1)} %bitcast.8, bf16[512,256]{1,0:T(8,128)(2,1)S(1)} %bitcast.12, f32[512,256]{1,0:T(8,128)S(1)} %get-tuple-element.33.refs_2_), custom_call_target="tpu_custom_call" | custom-call | tf_op jit(solution)/shard_map/grad/pallas_call | solution.py:351
  8.1 0.6 %collective-permute-start.5 = (bf16[384,256]{1,0:T(8,128)(2,1)S(1)}, bf16[384,256]{1,0:T(8,128)(2,1)S(1)}, u32[]{:S(2)}, u32[]{:S(2)}) collective-permute-start(bf16[384,256]{1,0:T(8,128)(2,1)S(1)} %get-tuple-element.35), channel_id=1, source_target_pairs={{0,4},{4,0},{8,12},{12,8},{1,5},{5,1},{9,13},{13,9},{2,6},{6,2},{1... | collective-permute-start | bytes 589832 | tf_op jit(solution)/shard_map/ppermute | solution.py:26
  8.7 0.1 collective-permute-start.6
  8.7 3.7 %collective-permute-done.refs_1_ = bf16[448,256]{1,0:T(8,128)(2,1)S(1)} collective-permute-done((bf16[448,256]{1,0:T(8,128)(2,1)S(1)}, bf16[448,256]{1,0:T(8,128)(2,1)S(1)}, u32[]{:S(2)}, u32[]{:S(2)}) %collective-permute-start) | collective-permute-done | bytes 229408 | tf_op jit(solution)/shard_map/ppermute | solution.py:26
  12.5 2.0 %collective-permute-done.1.refs_2_ = bf16[448,256]{1,0:T(8,128)(2,1)S(1)} collective-permute-done((bf16[448,256]{1,0:T(8,128)(2,1)S(1)}, bf16[448,256]{1,0:T(8,128)(2,1)S(1)}, u32[]{:S(2)}, u32[]{:S(2)}) %collective-permute-start.1) | collective-permute-done | bytes 229408 | tf_op jit(solution)/shard_map/ppermute | solution.py:26
  14.5 0.1 collective-permute-start.2
  14.6 2.0 %collective-permute-start.3 = (bf16[224,256]{1,0:T(8,128)(2,1)S(1)}, bf16[224,256]{1,0:T(8,128)(2,1)S(1)}, u32[]{:S(2)}, u32[]{:S(2)}) collective-permute-start(bf16[224,256]{1,0:T(8,128)(2,1)S(1)} %get-tuple-element.31), channel_id=1, source_target_pairs={{0,8},{4,12},{8,0},{12,4},{1,9},{5,13},{9,1},{13,5},{2,10},{6,14},... | collective-permute-start | bytes 344072 | tf_op jit(solution)/shard_map/ppermute | solution.py:26
  16.6 0.1 collective-permute-done.5.refs_1_
  16.7 2.0 %collective-permute-done.6.refs_2_ = bf16[384,256]{1,0:T(8,128)(2,1)S(1)} collective-permute-done((bf16[384,256]{1,0:T(8,128)(2,1)S(1)}, bf16[384,256]{1,0:T(8,128)(2,1)S(1)}, u32[]{:S(2)}, u32[]{:S(2)}) %collective-permute-start.6) | collective-permute-done | bytes 196640 | tf_op jit(solution)/shard_map/ppermute | solution.py:26
  18.7 0.1 collective-permute-start.7
  18.8 2.0 %collective-permute-start.8 = (bf16[192,256]{1,0:T(8,128)(2,1)S(1)}, bf16[192,256]{1,0:T(8,128)(2,1)S(1)}, u32[]{:S(2)}, u32[]{:S(2)}) collective-permute-start(bf16[192,256]{1,0:T(8,128)(2,1)S(1)} %get-tuple-element.38), channel_id=1, source_target_pairs={{0,8},{4,12},{8,0},{12,4},{1,9},{5,13},{9,1},{13,5},{2,10},{6,14},... | collective-permute-start | bytes 294920 | tf_op jit(solution)/shard_map/ppermute | solution.py:26
  20.8 0.0 collective-permute-done.2.refs_3_
  20.8 0.0 collective-permute-done.3.refs_4_
  20.8 0.0 copy-done.1
  20.8 0.2 factor.1
  21.1 1.1 %collective-permute-start.11 = (bf16[448,256]{1,0:T(8,128)(2,1)S(1)}, bf16[448,256]{1,0:T(8,128)(2,1)S(1)}, u32[]{:S(2)}, u32[]{:S(2)}) collective-permute-start(bf16[448,256]{1,0:T(8,128)(2,1)S(1)} %get-tuple-element.41.refs_0_), channel_id=1, source_target_pairs={{0,8},{4,12},{8,0},{12,4},{1,9},{5,13},{9,1},{13,5},{2,10},{6,14},... | collective-permute-start | bytes 688136 | tf_op jit(solution)/shard_map/ppermute | solution.py:26
  22.2 1.0 %collective-permute-start.9 = (bf16[448,256]{1,0:T(8,128)(2,1)S(1)}, bf16[448,256]{1,0:T(8,128)(2,1)S(1)}, u32[]{:S(2)}, u32[]{:S(2)}) collective-permute-start(bf16[448,256]{1,0:T(8,128)(2,1)S(1)} %get-tuple-element.41.refs_0_), channel_id=1, source_target_pairs={{0,4},{4,0},{8,12},{12,8},{1,5},{5,1},{9,13},{13,9},{2,6},{6,2},{1... | collective-permute-start | bytes 688136 | tf_op jit(solution)/shard_map/ppermute | solution.py:26
  23.2 0.2 collective-permute-done.7.refs_3_
  23.4 0.8 %collective-permute-done.8.refs_4_ = bf16[192,256]{1,0:T(8,128)(2,1)S(1)} collective-permute-done((bf16[192,256]{1,0:T(8,128)(2,1)S(1)}, bf16[192,256]{1,0:T(8,128)(2,1)S(1)}, u32[]{:S(2)}, u32[]{:S(2)}) %collective-permute-start.8) | collective-permute-done | bytes 98336 | tf_op jit(solution)/shard_map/ppermute | solution.py:26
  24.2 0.1 factor_rest.1
  24.4 2.3 %collective-permute-start.14 = (bf16[400,256]{1,0:T(8,128)(2,1)S(1)}, bf16[400,256]{1,0:T(8,128)(2,1)S(1)}, u32[]{:S(2)}, u32[]{:S(2)}) collective-permute-start(bf16[400,256]{1,0:T(8,128)(2,1)S(1)} %get-tuple-element.42.refs_1_.refs_5_), channel_id=1, source_target_pairs={{0,4},{4,0},{8,12},{12,8},{1,5},{5,1},{9,13},{13,9},{2,6},{6,2},{1... | collective-permute-start | bytes 614408 | tf_op jit(solution)/shard_map/ppermute | solution.py:26
  26.7 1.5 %collective-permute-start.10 = (bf16[400,256]{1,0:T(8,128)(2,1)S(1)}, bf16[400,256]{1,0:T(8,128)(2,1)S(1)}, u32[]{:S(2)}, u32[]{:S(2)}) collective-permute-start(bf16[400,256]{1,0:T(8,128)(2,1)S(1)} %get-tuple-element.42.refs_1_.refs_5_), channel_id=1, source_target_pairs={{0,8},{4,12},{8,0},{12,4},{1,9},{5,13},{9,1},{13,5},{2,10},{6,14},... | collective-permute-start | bytes 614408 | tf_op jit(solution)/shard_map/ppermute | solution.py:26
  28.2 1.5 %collective-permute-done.11.refs_1_.refs_4_ = bf16[448,256]{1,0:T(8,128)(2,1)S(1)} collective-permute-done((bf16[448,256]{1,0:T(8,128)(2,1)S(1)}, bf16[448,256]{1,0:T(8,128)(2,1)S(1)}, u32[]{:S(2)}, u32[]{:S(2)}) %collective-permute-start.11) | collective-permute-done | bytes 229408 | tf_op jit(solution)/shard_map/ppermute | solution.py:26
  29.7 1.1 %collective-permute-done.9.refs_0_.refs_2_ = bf16[448,256]{1,0:T(8,128)(2,1)S(1)} collective-permute-done((bf16[448,256]{1,0:T(8,128)(2,1)S(1)}, bf16[448,256]{1,0:T(8,128)(2,1)S(1)}, u32[]{:S(2)}, u32[]{:S(2)}) %collective-permute-start.9) | collective-permute-done | bytes 229408 | tf_op jit(solution)/shard_map/ppermute | solution.py:26
  30.8 1.0 %collective-permute-start.12 = (bf16[224,256]{1,0:T(8,128)(2,1)S(1)}, bf16[224,256]{1,0:T(8,128)(2,1)S(1)}, u32[]{:S(2)}, u32[]{:S(2)}) collective-permute-start(bf16[224,256]{1,0:T(8,128)(2,1)S(1)} %get-tuple-element.43), channel_id=1, source_target_pairs={{0,8},{4,12},{8,0},{12,4},{1,9},{5,13},{9,1},{13,5},{2,10},{6,14},... | collective-permute-start | bytes 344072 | tf_op jit(solution)/shard_map/ppermute | solution.py:26
  31.8 0.0 copy-start.2
  31.8 1.3 %collective-permute-start.13 = (bf16[224,256]{1,0:T(8,128)(2,1)S(1)}, bf16[224,256]{1,0:T(8,128)(2,1)S(1)}, u32[]{:S(2)}, u32[]{:S(2)}) collective-permute-start(bf16[224,256]{1,0:T(8,128)(2,1)S(1)} %get-tuple-element.44.refs_2_), channel_id=1, source_target_pairs={{0,4},{4,0},{8,12},{12,8},{1,5},{5,1},{9,13},{13,9},{2,6},{6,2},{1... | collective-permute-start | bytes 344072 | tf_op jit(solution)/shard_map/ppermute | solution.py:26
  33.1 1.6 %collective-permute-done.14.refs_0_.refs_3_.refs_6_ = bf16[400,256]{1,0:T(8,128)(2,1)S(1)} collective-permute-done((bf16[400,256]{1,0:T(8,128)(2,1)S(1)}, bf16[400,256]{1,0:T(8,128)(2,1)S(1)}, u32[]{:S(2)}, u32[]{:S(2)}) %collective-permute-start.14) | collective-permute-done | bytes 204832 | tf_op jit(solution)/shard_map/ppermute | solution.py:26
  34.8 0.0 collective-permute-done.10.refs_1_.refs_5_.refs_3_.refs_7_
  34.8 0.7 %collective-permute-start.16 = (bf16[208,256]{1,0:T(8,128)(2,1)S(1)}, bf16[208,256]{1,0:T(8,128)(2,1)S(1)}, u32[]{:S(2)}, u32[]{:S(2)}) collective-permute-start(bf16[208,256]{1,0:T(8,128)(2,1)S(1)} %get-tuple-element.45.refs_6_), channel_id=1, source_target_pairs={{0,4},{4,0},{8,12},{12,8},{1,5},{5,1},{9,13},{13,9},{2,6},{6,2},{1... | collective-permute-start | bytes 319496 | tf_op jit(solution)/shard_map/ppermute | solution.py:26
  35.5 0.9 %collective-permute-start.15 = (bf16[192,256]{1,0:T(8,128)(2,1)S(1)}, bf16[192,256]{1,0:T(8,128)(2,1)S(1)}, u32[]{:S(2)}, u32[]{:S(2)}) collective-permute-start(bf16[192,256]{1,0:T(8,128)(2,1)S(1)} %get-tuple-element.48), channel_id=1, source_target_pairs={{0,8},{4,12},{8,0},{12,4},{1,9},{5,13},{9,1},{13,5},{2,10},{6,14},... | collective-permute-start | bytes 294920 | tf_op jit(solution)/shard_map/ppermute | solution.py:26
  37.0 0.5 %near.1 = (bf16[1024,1024]{1,0:T(8,128)(2,1)S(1)}, f32[1,1024]{1,0:T(1,128)S(1)}) custom-call(bf16[448,256]{1,0:T(8,128)(2,1)S(1)} %get-tuple-element.41.refs_0_, bf16[400,256]{1,0:T(8,128)(2,1)S(1)} %get-tuple-element.42.refs_1_.refs_5_, bf16[448,256]{1,0:T(8,128)(2,1)S(1)} %collective-permute-done.9.refs_0_.refs_2_, ...), custom_call_target="tpu_custom_call" | custom-call | tf_op jit(solution)/shard_map/near/pallas_call | solution.py:351
  37.5 0.0 collective-permute-done.12.refs_4_.refs_3_
  37.5 0.0 collective-permute-done.13.refs_5_.refs_4_
  37.5 1.1 %new_rows.1 = f32[256,1024]{1,0:T(8,128)} custom-call(f32[448,256]{1,0:T(8,128)S(1)} %get-tuple-element.32.refs_0_, f32[128,256]{1,0:T(8,128)S(1)} %get-tuple-element.40.refs_1_, bf16[448,256]{1,0:T(8,128)(2,1)S(1)} %collective-permute-done.9.refs_0_.refs_2_, bf16[400,256]{1,0:T(8,128)(2,1)S(1)} %collective-permute-done.10.refs_1_.refs_5_.refs_3_.refs_7_, ...), custom_call_target="tpu_custom_call" | custom-call | tf_op jit(solution)/shard_map/new_rows/pallas_call | solution.py:351
  38.7 1.4 %collective-permute-done.15.refs_8_ = bf16[192,256]{1,0:T(8,128)(2,1)S(1)} collective-permute-done((bf16[192,256]{1,0:T(8,128)(2,1)S(1)}, bf16[192,256]{1,0:T(8,128)(2,1)S(1)}, u32[]{:S(2)}, u32[]{:S(2)}) %collective-permute-start.15) | collective-permute-done | bytes 98336 | tf_op jit(solution)/shard_map/ppermute | solution.py:26
  40.1 0.0 collective-permute-done.16.refs_9_
  40.1 0.0 copy-done.2
  40.1 3.3 %root.1 = (bf16[256,1024]{1,0:T(8,128)(2,1)}, bf16[256,256]{1,0:T(8,128)(2,1)}, bf16[1024,1024]{1,0:T(8,128)(2,1)S(1)}) custom-call(s32[1,1]{1,0:T(1,128)S(6)} %copy.10.refs_0_, bf16[1024,1024]{1,0:T(8,128)(2,1)S(1)} %get-tuple-element.47.refs_1_, f32[1,1024]{1,0:T(1,128)S(1)} %get-tuple-element.46.refs_6_.refs_2_, ...), custom_call_target="tpu_custom_call", output_to_operand_aliasing={{2}: (1, {})} | custom-call | tf_op jit(solution)/shard_map/root/pallas_call | solution.py:351
  (4 shorter events, 0.1 us)
Async XLA Ops:
  0.6 6.9 %collective-permute-start.4 = (bf16[1,512,256]{2,1,0:T(8,128)(2,1)}, bf16[1,512,256]{2,1,0:T(8,128)(2,1)S(1)}, u32[]{:S(2)}, u32[]{:S(2)}) collective-permute-start(bf16[1,512,256]{2,1,0:T(8,128)(2,1)} %param.6), channel_id=1, source_target_pairs={{16,0},{0,16},{17,1},{1,17},{18,2},{2,18},{19,3},{3,19},{20,4},{4,... | collective-permute-start | bytes 786440 | tf_op jit(solution)/shard_map/ppermute | solution.py:22
  1.1 1.2 %copy-start = (bf16[1,512,1024]{2,1,0:T(8,128)(2,1)S(1)}, bf16[1,512,1024]{2,1,0:T(8,128)(2,1)}, u32[]{:S(2)}) copy-start(bf16[1,512,1024]{2,1,0:T(8,128)(2,1)} %param.5) | copy-start | bytes 3145732
  3.4 9.0 %collective-permute-start = (bf16[448,256]{1,0:T(8,128)(2,1)S(1)}, bf16[448,256]{1,0:T(8,128)(2,1)S(1)}, u32[]{:S(2)}, u32[]{:S(2)}) collective-permute-start(bf16[448,256]{1,0:T(8,128)(2,1)S(1)} %get-tuple-element.28), channel_id=1, source_target_pairs={{0,4},{4,0},{8,12},{12,8},{1,5},{5,1},{9,13},{13,9},{2,6},{6,2},{1... | collective-permute-start | bytes 688136 | tf_op jit(solution)/shard_map/ppermute | solution.py:26
  6.0 8.4 %collective-permute-start.1 = (bf16[448,256]{1,0:T(8,128)(2,1)S(1)}, bf16[448,256]{1,0:T(8,128)(2,1)S(1)}, u32[]{:S(2)}, u32[]{:S(2)}) collective-permute-start(bf16[448,256]{1,0:T(8,128)(2,1)S(1)} %get-tuple-element.29), channel_id=1, source_target_pairs={{0,8},{4,12},{8,0},{12,4},{1,9},{5,13},{9,1},{13,5},{2,10},{6,14},... | collective-permute-start | bytes 688136 | tf_op jit(solution)/shard_map/ppermute | solution.py:26
  7.5 13.3 %copy-start.1 = (f32[1,1,256,1024]{3,2,1,0:T(8,128)S(1)}, f32[1,1,256,1024]{3,2,1,0:T(8,128)}, u32[]{:S(2)}) copy-start(f32[1,1,256,1024]{3,2,1,0:T(8,128)} %param.7) | copy-start | bytes 3145732
  8.1 8.6 %collective-permute-start.5 = (bf16[384,256]{1,0:T(8,128)(2,1)S(1)}, bf16[384,256]{1,0:T(8,128)(2,1)S(1)}, u32[]{:S(2)}, u32[]{:S(2)}) collective-permute-start(bf16[384,256]{1,0:T(8,128)(2,1)S(1)} %get-tuple-element.35), channel_id=1, source_target_pairs={{0,4},{4,0},{8,12},{12,8},{1,5},{5,1},{9,13},{13,9},{2,6},{6,2},{1... | collective-permute-start | bytes 589832 | tf_op jit(solution)/shard_map/ppermute | solution.py:26
  8.7 10.0 %collective-permute-start.6 = (bf16[384,256]{1,0:T(8,128)(2,1)S(1)}, bf16[384,256]{1,0:T(8,128)(2,1)S(1)}, u32[]{:S(2)}, u32[]{:S(2)}) collective-permute-start(bf16[384,256]{1,0:T(8,128)(2,1)S(1)} %get-tuple-element.36), channel_id=1, source_target_pairs={{0,8},{4,12},{8,0},{12,4},{1,9},{5,13},{9,1},{13,5},{2,10},{6,14},... | collective-permute-start | bytes 589832 | tf_op jit(solution)/shard_map/ppermute | solution.py:26
  14.5 6.3 %collective-permute-start.2 = (bf16[224,256]{1,0:T(8,128)(2,1)S(1)}, bf16[224,256]{1,0:T(8,128)(2,1)S(1)}, u32[]{:S(2)}, u32[]{:S(2)}) collective-permute-start(bf16[224,256]{1,0:T(8,128)(2,1)S(1)} %get-tuple-element.30), channel_id=1, source_target_pairs={{0,4},{4,0},{8,12},{12,8},{1,5},{5,1},{9,13},{13,9},{2,6},{6,2},{1... | collective-permute-start | bytes 344072 | tf_op jit(solution)/shard_map/ppermute | solution.py:26
  14.6 6.2 %collective-permute-start.3 = (bf16[224,256]{1,0:T(8,128)(2,1)S(1)}, bf16[224,256]{1,0:T(8,128)(2,1)S(1)}, u32[]{:S(2)}, u32[]{:S(2)}) collective-permute-start(bf16[224,256]{1,0:T(8,128)(2,1)S(1)} %get-tuple-element.31), channel_id=1, source_target_pairs={{0,8},{4,12},{8,0},{12,4},{1,9},{5,13},{9,1},{13,5},{2,10},{6,14},... | collective-permute-start | bytes 344072 | tf_op jit(solution)/shard_map/ppermute | solution.py:26
  18.7 4.7 %collective-permute-start.7 = (bf16[192,256]{1,0:T(8,128)(2,1)S(1)}, bf16[192,256]{1,0:T(8,128)(2,1)S(1)}, u32[]{:S(2)}, u32[]{:S(2)}) collective-permute-start(bf16[192,256]{1,0:T(8,128)(2,1)S(1)} %get-tuple-element.37), channel_id=1, source_target_pairs={{0,4},{4,0},{8,12},{12,8},{1,5},{5,1},{9,13},{13,9},{2,6},{6,2},{1... | collective-permute-start | bytes 294920 | tf_op jit(solution)/shard_map/ppermute | solution.py:26
  18.8 5.4 %collective-permute-start.8 = (bf16[192,256]{1,0:T(8,128)(2,1)S(1)}, bf16[192,256]{1,0:T(8,128)(2,1)S(1)}, u32[]{:S(2)}, u32[]{:S(2)}) collective-permute-start(bf16[192,256]{1,0:T(8,128)(2,1)S(1)} %get-tuple-element.38), channel_id=1, source_target_pairs={{0,8},{4,12},{8,0},{12,4},{1,9},{5,13},{9,1},{13,5},{2,10},{6,14},... | collective-permute-start | bytes 294920 | tf_op jit(solution)/shard_map/ppermute | solution.py:26
  21.1 8.6 %collective-permute-start.11 = (bf16[448,256]{1,0:T(8,128)(2,1)S(1)}, bf16[448,256]{1,0:T(8,128)(2,1)S(1)}, u32[]{:S(2)}, u32[]{:S(2)}) collective-permute-start(bf16[448,256]{1,0:T(8,128)(2,1)S(1)} %get-tuple-element.41.refs_0_), channel_id=1, source_target_pairs={{0,8},{4,12},{8,0},{12,4},{1,9},{5,13},{9,1},{13,5},{2,10},{6,14},... | collective-permute-start | bytes 688136 | tf_op jit(solution)/shard_map/ppermute | solution.py:26
  22.2 8.5 %collective-permute-start.9 = (bf16[448,256]{1,0:T(8,128)(2,1)S(1)}, bf16[448,256]{1,0:T(8,128)(2,1)S(1)}, u32[]{:S(2)}, u32[]{:S(2)}) collective-permute-start(bf16[448,256]{1,0:T(8,128)(2,1)S(1)} %get-tuple-element.41.refs_0_), channel_id=1, source_target_pairs={{0,4},{4,0},{8,12},{12,8},{1,5},{5,1},{9,13},{13,9},{2,6},{6,2},{1... | collective-permute-start | bytes 688136 | tf_op jit(solution)/shard_map/ppermute | solution.py:26
  24.4 10.4 %collective-permute-start.14 = (bf16[400,256]{1,0:T(8,128)(2,1)S(1)}, bf16[400,256]{1,0:T(8,128)(2,1)S(1)}, u32[]{:S(2)}, u32[]{:S(2)}) collective-permute-start(bf16[400,256]{1,0:T(8,128)(2,1)S(1)} %get-tuple-element.42.refs_1_.refs_5_), channel_id=1, source_target_pairs={{0,4},{4,0},{8,12},{12,8},{1,5},{5,1},{9,13},{13,9},{2,6},{6,2},{1... | collective-permute-start | bytes 614408 | tf_op jit(solution)/shard_map/ppermute | solution.py:26
  26.7 8.1 %collective-permute-start.10 = (bf16[400,256]{1,0:T(8,128)(2,1)S(1)}, bf16[400,256]{1,0:T(8,128)(2,1)S(1)}, u32[]{:S(2)}, u32[]{:S(2)}) collective-permute-start(bf16[400,256]{1,0:T(8,128)(2,1)S(1)} %get-tuple-element.42.refs_1_.refs_5_), channel_id=1, source_target_pairs={{0,8},{4,12},{8,0},{12,4},{1,9},{5,13},{9,1},{13,5},{2,10},{6,14},... | collective-permute-start | bytes 614408 | tf_op jit(solution)/shard_map/ppermute | solution.py:26
  30.8 6.7 %collective-permute-start.12 = (bf16[224,256]{1,0:T(8,128)(2,1)S(1)}, bf16[224,256]{1,0:T(8,128)(2,1)S(1)}, u32[]{:S(2)}, u32[]{:S(2)}) collective-permute-start(bf16[224,256]{1,0:T(8,128)(2,1)S(1)} %get-tuple-element.43), channel_id=1, source_target_pairs={{0,8},{4,12},{8,0},{12,4},{1,9},{5,13},{9,1},{13,5},{2,10},{6,14},... | collective-permute-start | bytes 344072 | tf_op jit(solution)/shard_map/ppermute | solution.py:26
  31.8 8.3 %copy-start.2 = (bf16[1,1,256,1024]{3,2,1,0:T(8,128)(2,1)S(1)}, bf16[1,1,256,1024]{3,2,1,0:T(8,128)(2,1)}, u32[]{:S(2)}) copy-start(bf16[1,1,256,1024]{3,2,1,0:T(8,128)(2,1)} %param.8) | copy-start | bytes 1572868
  31.8 5.7 %collective-permute-start.13 = (bf16[224,256]{1,0:T(8,128)(2,1)S(1)}, bf16[224,256]{1,0:T(8,128)(2,1)S(1)}, u32[]{:S(2)}, u32[]{:S(2)}) collective-permute-start(bf16[224,256]{1,0:T(8,128)(2,1)S(1)} %get-tuple-element.44.refs_2_), channel_id=1, source_target_pairs={{0,4},{4,0},{8,12},{12,8},{1,5},{5,1},{9,13},{13,9},{2,6},{6,2},{1... | collective-permute-start | bytes 344072 | tf_op jit(solution)/shard_map/ppermute | solution.py:26
  34.8 5.3 %collective-permute-start.16 = (bf16[208,256]{1,0:T(8,128)(2,1)S(1)}, bf16[208,256]{1,0:T(8,128)(2,1)S(1)}, u32[]{:S(2)}, u32[]{:S(2)}) collective-permute-start(bf16[208,256]{1,0:T(8,128)(2,1)S(1)} %get-tuple-element.45.refs_6_), channel_id=1, source_target_pairs={{0,4},{4,0},{8,12},{12,8},{1,5},{5,1},{9,13},{13,9},{2,6},{6,2},{1... | collective-permute-start | bytes 319496 | tf_op jit(solution)/shard_map/ppermute | solution.py:26
  35.5 4.6 %collective-permute-start.15 = (bf16[192,256]{1,0:T(8,128)(2,1)S(1)}, bf16[192,256]{1,0:T(8,128)(2,1)S(1)}, u32[]{:S(2)}, u32[]{:S(2)}) collective-permute-start(bf16[192,256]{1,0:T(8,128)(2,1)S(1)} %get-tuple-element.48), channel_id=1, source_target_pairs={{0,8},{4,12},{8,0},{12,4},{1,9},{5,13},{9,1},{13,5},{2,10},{6,14},... | collective-permute-start | bytes 294920 | tf_op jit(solution)/shard_map/ppermute | solution.py:26

commit v6 on v5

v6 whole, which is shorter than its diff:
```python
import functools
import math

import jax
import jax.numpy as jnp
from jax import lax
from jax.experimental import pallas as pl
from jax.experimental.pallas import tpu as pltpu
from jax.sharding import PartitionSpec as P

DECAY = 0.75
DAMPING = 0.1
EPSILON = 1e-06
BF16 = jnp.bfloat16
F32 = jnp.float32
VMEM_LIMIT = 28 * 1024 * 1024


def passed_along(block, axis, distance):
    devices = range(lax.axis_size(axis))
    route = [((i - distance) % len(devices), i) for i in devices]
    return lax.ppermute(block, axis, route)


def along(axis_turn):
    return jnp.where(lax.axis_index("pipe") == axis_turn, 1, 2)


def swapped(block, axis_turn):
    replicas = lax.axis_size("dp")
    route = []
    for section in range(lax.axis_size("pipe")):
        offset = 1 if section == axis_turn else 2
        route += [(section * replicas + i, section * replicas + (i ^ offset)) for i in range(replicas)]
    return lax.ppermute(block, ("pipe", "dp"), route)


def eye_of(rows, cols, shift=0):
    row_ids = lax.broadcasted_iota(jnp.int32, (rows, cols), 0) + shift
    col_ids = lax.broadcasted_iota(jnp.int32, (rows, cols), 1)
    return (row_ids == col_ids).astype(F32)


def whole(count):
    return [pl.BlockSpec(memory_space=pltpu.VMEM)] * count


def transposed(block):
    return block.astype(F32).T.astype(block.dtype)


OVER_ROWS = (((0,), (0,)), ((), ()))


def first_starts(share):
    half = share // 2
    return 0, half, half + half // 2, 2 * half + half // 2, 3 * half + half // 2


def shared_half(owner, offset, share):
    other = owner ^ offset
    low, high = jnp.minimum(owner, other), jnp.maximum(owner, other)
    row = low * share + jnp.where(owner > other, share // 2, 0)
    return pl.multiple_of(row, share // 2), pl.multiple_of(high * share, share)


def side_by_side(low):
    half = low.shape[0] // 2
    return jnp.concatenate([low[0:half], low[half:]], axis=1)


def stacked(packed):
    half = packed.shape[1] // 2
    return jnp.concatenate([packed[:, 0:half], packed[:, half:]], axis=0)


def store_messages(pieces, send, keep):
    for ref, offsets in ((send, (along(0), 3)), (keep, (0, along(1)))):
        length = ref.shape[0] // 2
        for at, offset in zip((0, length), offsets):
            for start, piece in pieces(offset):
                ref[at + start : at + start + piece.shape[0], :] = piece.astype(ref.dtype)


def batch_kernel(replicas, tokens_all, acts, send, keep, rest, batch):
    order = acts.shape[1]
    share = order // replicas
    half = share // 2
    starts = first_starts(share)
    mine = lax.axis_index("dp")
    for i in range(replicas):
        band = slice(i * share, (i + 1) * share)
        batch[band, i * share :] = lax.dot_general(
            acts[:, band], acts[:, i * share :], OVER_ROWS, preferred_element_type=F32
        ) * (1.0 / tokens_all)

    def shared(owner, offset):
        row, col = shared_half(owner, offset, share)
        return batch[pl.ds(row, half), pl.ds(col, share)]

    def pieces(offset):
        owner = mine ^ offset
        base = pl.multiple_of(owner * share, share)
        corner = pl.multiple_of(owner * share + half, half)
        yield starts[0], batch[pl.ds(base, half), pl.ds(base, share)]
        yield starts[1], side_by_side(batch[pl.ds(corner, half), pl.ds(corner, half)])
        for start, step in zip(starts[2:], (along(0), 3)):
            yield start, shared(owner, step)

    store_messages(pieces, send, keep)
    for owner in range(replicas):
        rest[owner * half : (owner + 1) * half, :] = shared(owner, along(1))


def grad_kernel(replicas, tokens_all, acts, grads, rest, send, keep, total):
    share = acts.shape[1] // replicas
    half = share // 2
    strip = grads.shape[1] // replicas
    mine = lax.axis_index("dp")
    total[...] = lax.dot_general(grads[...], acts[...], OVER_ROWS, preferred_element_type=F32) * (
        1.0 / math.sqrt(tokens_all)
    )

    def pieces(offset):
        owner = mine ^ offset
        yield 0, rest[pl.ds(pl.multiple_of(owner * half, half), half), :]
        rows = pl.ds(pl.multiple_of(owner * strip, strip), strip)
        for part in range(replicas):
            yield half + part * strip, total[rows, part * share : (part + 1) * share]

    store_messages(pieces, send, keep)


def relay_kernel(keep, got, send):
    length = send.shape[0]
    send[...] = (keep[length:, :] + got[length:, :].astype(F32)).astype(BF16)


def wave_total(keep, got, relayed):
    length = relayed.shape[0]
    return keep[0:length, :] + got[0:length, :].astype(F32) + relayed[...].astype(F32)


def old_half(old, mine, offset):
    share = old.shape[0]
    half = share // 2
    other = mine ^ offset
    block = old[:, pl.ds(pl.multiple_of(other * share, share), share)]
    return jnp.where(mine < other, block[0:half], block[:, half:].T)


def column_sums(value):
    return jnp.sum(value * value, axis=0, keepdims=True)


def first_factor_kernel(keep, got, relayed, old, chunk, exact, squares):
    share = old.shape[0]
    half = share // 2
    starts = first_starts(share)
    mine = lax.axis_index("dp")
    total = wave_total(keep, got, relayed)
    diagonal = old[:, pl.ds(pl.multiple_of(mine * share, share), share)]
    terms = [
        DECAY * diagonal[0:half] + DAMPING * eye_of(half, share),
        side_by_side(DECAY * diagonal[half:, half:] + DAMPING * eye_of(half, half)),
    ] + [DECAY * old_half(old, mine, offset) for offset in (along(0), 3)]
    column = lax.broadcasted_iota(jnp.int32, (1, share), 1)
    weights = [jnp.where(column < half, 1.0, 2.0), 1.0, 2.0, 2.0]
    sums = jnp.zeros((1, share), F32)
    for start, term, weight in zip(starts, terms, weights):
        rows = slice(start, start + term.shape[0])
        value = term + (1.0 - DECAY) * total[rows]
        exact[rows, :] = value
        chunk[rows, :] = value.astype(BF16)
        sums = sums + weight * column_sums(value)
    squares[...] = sums


def second_factor_kernel(keep, got, relayed, old, squares, chunk, exact):
    share = old.shape[0]
    half = share // 2
    total = wave_total(keep, got, relayed)
    length = total.shape[0]
    value = DECAY * old_half(old, lax.axis_index("dp"), along(1)) + (1.0 - DECAY) * total[0:half]
    exact[...] = value
    chunk[0:half, :] = value.astype(BF16)
    chunk[half:length, :] = total[half:].astype(BF16)
    sums = squares[...] + 2.0 * column_sums(value)
    high = sums.astype(BF16).astype(F32)
    middle = (sums - high).astype(BF16).astype(F32)
    rest = sums - high - middle
    spot = lax.broadcasted_iota(jnp.int32, (chunk.shape[0] - length, share), 0)
    digits = jnp.where(spot == 0, high, jnp.where(spot == 1, middle, jnp.where(spot == 2, rest, 0.0)))
    chunk[length:, :] = digits.astype(BF16)


def pair_kernel(own, got, send):
    length = own.shape[0]
    send[0:length, :] = own[...]
    send[length:, :] = got[...]


def place_half(factor, owner, offset, block):
    row, col = shared_half(owner, offset, block.shape[1])
    factor[pl.ds(row, block.shape[0]), pl.ds(col, block.shape[1])] = block
    factor[pl.ds(col, block.shape[1]), pl.ds(row, block.shape[0])] = transposed(block)


def place_first(factor, diagonal, owner, wave, at=0):
    share = wave.shape[1]
    half = share // 2
    starts = [at + start for start in first_starts(share)]
    base = pl.multiple_of(owner * share, share)
    corner = pl.multiple_of(owner * share + half, half)
    top = wave[at : at + half, :]
    low = stacked(wave[starts[1] : starts[2], :])
    factor[pl.ds(base, half), pl.ds(base, share)] = top
    factor[pl.ds(corner, half), pl.ds(base, half)] = transposed(top[:, half:])
    factor[pl.ds(corner, half), pl.ds(corner, half)] = low
    eye = eye_of(half, half)
    diagonal[:, pl.ds(base, half)] = jnp.sum(top[:, 0:half].astype(F32) * eye, axis=0, keepdims=True)
    diagonal[:, pl.ds(corner, half)] = jnp.sum(low.astype(F32) * eye, axis=0, keepdims=True)
    for start, offset in zip(starts[2:], (along(0), 3)):
        place_half(factor, owner, offset, wave[start : start + half, :])


def matrix_kernel(pair, pair_rest, far, factor, diagonal):
    share = pair.shape[1]
    half = share // 2
    mine = lax.axis_index("dp")
    for offset, wave, at in (
        (0, pair, 0),
        (along(1), pair, pair.shape[0] // 2),
        (along(0), far, 0),
        (3, far, far.shape[0] // 2),
    ):
        place_first(factor, diagonal, mine ^ offset, wave, at)
    for i, offset in enumerate((0, along(1))):
        start = i * (pair_rest.shape[0] // 2)
        place_half(factor, mine ^ offset, along(1), pair_rest[start : start + half, :])
    bands = [pl.ds(pl.multiple_of((mine ^ offset) * share, share), share) for offset in (along(0), 3)]
    for rows, columns in (bands, bands[::-1]):
        factor[rows, columns] = jnp.zeros((share, share), BF16)


def new_rows_kernel(exact, exact_rest, far, pair_rest, factor_out):
    share = factor_out.shape[0]
    half = share // 2
    starts = first_starts(share)
    across = far.shape[0] // 2 + starts[3]
    second = pair_rest.shape[0] // 2
    mine = lax.axis_index("dp")
    own_columns = pl.ds(pl.multiple_of(mine * share, share), share)
    top = exact[0:half, :]
    factor_out[0:half, own_columns] = top
    factor_out[half:, own_columns] = jnp.concatenate(
        [top[:, half:].T, stacked(exact[starts[1] : starts[2], :])], axis=1
    )
    shared = [
        (along(0), exact[starts[2] : starts[3], :], far[starts[2] : starts[3], :]),
        (along(1), exact_rest[...], pair_rest[second : second + half, :]),
        (3, exact[starts[3] : starts[4], :], far[across : across + half, :]),
    ]
    for offset, own, theirs in shared:
        other = mine ^ offset
        columns = pl.ds(pl.multiple_of(other * share, share), share)
        theirs = theirs.astype(F32)

        @pl.when(mine < other)
        def _():
            factor_out[0:half, columns] = own
            factor_out[half:, columns] = theirs

        @pl.when(mine > other)
        def _():
            factor_out[:, columns] = jnp.concatenate([theirs.T, own.T], axis=1)


def root_kernel(replicas, count, known, diagonal, pair, far, old_root, root_out, step_out, left, right, grads, result):
    share = root_out.shape[0]
    order = root_out.shape[1]
    half = share // 2
    strip = step_out.shape[0] // replicas
    digits = half + replicas * strip
    length = pair.shape[0] // 2
    mine = lax.axis_index("dp")
    waves = [(pair, 0, 0), (pair, length, along(1)), (far, 0, along(0)), (far, length, 3)]
    squares = jnp.zeros((length - digits, share), F32)
    for wave, at, _ in waves:
        squares = squares + wave[at + digits : at + length, :].astype(F32)
    scale = jnp.sqrt(jnp.sum(squares, keepdims=True) / order + EPSILON)
    inverse = 1.0 / scale
    neighbour, across = mine ^ along(0), mine ^ 3
    ours, theirs = far[0:half, :], far[length : length + half, :]
    ordered = jnp.where(neighbour < across, 1.0, 0.0).astype(F32)
    upper = ordered * ours.astype(F32) + (1.0 - ordered) * theirs.astype(F32)
    lower = ordered * theirs.astype(F32) + (1.0 - ordered) * ours.astype(F32)
    block = jnp.concatenate([upper, lower], axis=0).astype(BF16)
    low = pl.ds(pl.multiple_of(jnp.minimum(neighbour, across) * share, share), share)
    high = pl.ds(pl.multiple_of(jnp.maximum(neighbour, across) * share, share), share)

    def times_factor(value):
        left[...] = value
        right[...] = jnp.dot(value, known[...], preferred_element_type=F32)
        right[:, high] += jnp.dot(left[:, low], block, preferred_element_type=F32)
        right[:, low] += lax.dot_general(
            left[:, high], block, (((1,), (1,)), ((), ())), preferred_element_type=F32
        )
        return right[...]

    ones = (diagonal[...] * inverse).astype(BF16).astype(F32)
    lift = (1.5 - 0.5 * ones).astype(BF16).astype(F32) + 0.5 * (diagonal[...] * inverse)
    eye = eye_of(share, order, mine * share)
    my_rows = pl.ds(pl.multiple_of(mine * share, share), share)
    first = (known[my_rows, :].astype(F32) * inverse).astype(BF16).astype(F32)
    turn = (1.5 * eye - 0.5 * first).astype(BF16)
    second = (times_factor(turn) * inverse).astype(BF16)
    product = (-0.5 * inverse) * times_factor(second) + second.astype(F32) * lift
    turn_two = (1.5 * eye - 0.5 * product).astype(BF16)
    inverse_rows = (-0.5 * inverse) * times_factor(turn_two) + turn_two.astype(F32) * lift
    chosen = jnp.where(count[0, 0] == 1, turn.astype(F32), inverse_rows)
    root_out[...] = (chosen * lax.rsqrt(scale)).astype(BF16)

    for i, (wave, at, _) in enumerate(waves):
        for part in range(replicas):
            start = at + half + part * strip
            grads[i * strip : (i + 1) * strip, part * share : (part + 1) * share] = wave[start : start + strip, :]
    result[...] = lax.dot_general(
        grads[...], old_root[...], (((1,), (1,)), ((), ())), preferred_element_type=F32
    ).astype(BF16)
    for i, (_, _, offset) in enumerate(waves):
        rows = pl.ds(pl.multiple_of((mine ^ offset) * strip, strip), strip)
        step_out[rows, :] = result[i * strip : (i + 1) * strip, :]


def square_plan(acts, out_grad, old_factor, old_root, iter_count):
    replicas = lax.axis_size("dp")
    inputs = acts[0]
    tokens, order = inputs.shape
    share = order // replicas
    half = share // 2
    grows = out_grad.shape[2]
    old = old_factor[0, 0]
    params = pltpu.CompilerParams(vmem_limit_bytes=VMEM_LIMIT)
    first = first_starts(share)[-1]
    second = half + grows
    digits = 16

    def shape(rows, kind=BF16, columns=share):
        return jax.ShapeDtypeStruct((rows, columns), kind)

    def call(kernel, outs, name, *operands, in_smem=(), after=(), scratch=()):
        in_specs = whole(len(operands)) + [pl.BlockSpec(memory_space=pl.ANY)] * len(after)
        for i in in_smem:
            in_specs[i] = pl.BlockSpec(memory_space=pltpu.SMEM)

        def body(*refs):
            kernel(*refs[: len(operands)], *refs[len(operands) + len(after) :])

        return pl.pallas_call(
            body,
            out_shape=outs,
            in_specs=in_specs,
            out_specs=whole(len(outs)),
            scratch_shapes=scratch,
            compiler_params=params,
            name=name,
        )(*operands, *after)

    received = passed_along(out_grad, "pipe", -1)[0]
    send1, keep1, rest = call(
        functools.partial(batch_kernel, replicas, tokens * replicas),
        [shape(2 * first), shape(2 * first, F32), shape(replicas * half, F32)],
        "batch",
        inputs,
        scratch=[pltpu.VMEM((order, order), F32)],
    )
    got1 = swapped(send1, 0)
    send2, keep2 = call(
        functools.partial(grad_kernel, replicas, tokens * replicas),
        [shape(2 * second), shape(2 * second, F32)],
        "grad",
        inputs,
        received,
        rest,
        scratch=[pltpu.VMEM((grows, order), F32)],
    )
    got2 = swapped(send2, 0)
    (send1,) = call(relay_kernel, [shape(first)], "relay", keep1, got1)
    relayed1 = swapped(send1, 1)
    (send2,) = call(relay_kernel, [shape(second)], "relay_rest", keep2, got2)
    relayed2 = swapped(send2, 1)
    own1, exact1, squares = call(
        first_factor_kernel,
        [shape(first), shape(first, F32), shape(1, F32)],
        "factor",
        keep1,
        got1,
        relayed1,
        old,
    )
    near1 = swapped(own1, 1)
    own2, exact2 = call(
        second_factor_kernel,
        [shape(second + digits), shape(half, F32)],
        "factor_rest",
        keep2,
        got2,
        relayed2,
        old,
        squares,
    )
    near2 = swapped(own2, 1)
    (pair1,) = call(pair_kernel, [shape(2 * first)], "pair", own1, near1)
    far1 = swapped(pair1, 0)
    (pair2,) = call(pair_kernel, [shape(2 * (second + digits))], "pair_rest", own2, near2, after=[pair1])
    far2 = swapped(pair2, 0)
    known, diagonal = call(
        matrix_kernel, [shape(order, BF16, order), shape(1, F32, order)], "matrix", pair1, pair2, far1
    )
    (factor,) = call(
        new_rows_kernel, [shape(share, F32, order)], "new_rows", exact1, exact2, far1, pair2, after=[diagonal]
    )
    root, step = call(
        functools.partial(root_kernel, replicas),
        [shape(share, BF16, order), shape(grows)],
        "root",
        iter_count,
        known,
        diagonal,
        pair2,
        far2,
        old_root[0, 0],
        in_smem=[0],
        scratch=[
            pltpu.VMEM((share, order), BF16),
            pltpu.VMEM((share, order), F32),
            pltpu.VMEM((grows, order), BF16),
            pltpu.VMEM((grows, share), BF16),
        ],
    )
    return (factor[None, None], root[None, None], step[None, None])


def ring_plan(acts, out_grad, old_factor, old_root, iter_count):
    inputs = acts[0]
    replicas = lax.axis_size("dp")
    tokens_all = inputs.shape[0] * replicas
    order = inputs.shape[1]
    share = order // replicas
    offset = lax.axis_index("dp") * share
    received = passed_along(out_grad, "pipe", -1)[0]
    partial_grad = jnp.dot(received.T, inputs, preferred_element_type=F32) / math.sqrt(tokens_all)
    batch = lax.psum_scatter(
        jnp.dot(inputs.T, inputs, preferred_element_type=F32) / tokens_all,
        "dp",
        scatter_dimension=0,
        tiled=True,
    )
    eye_rows = eye_of(share, order, offset)
    factor = DECAY * old_factor[0, 0] + (1.0 - DECAY) * batch + DAMPING * eye_rows
    grad16 = lax.psum(partial_grad, "dp").astype(BF16)
    scale = jnp.sqrt(lax.psum(jnp.sum(factor * factor), "dp") / order + EPSILON)
    step = lax.dot_general(
        grad16, old_root[0, 0], (((1,), (1,)), ((), ())), preferred_element_type=F32
    ).astype(BF16)
    first = lax.all_gather((factor / scale).astype(BF16), "dp", axis=0, tiled=True)
    turn_one = (1.5 * eye_of(order, order) - 0.5 * first.astype(F32)).astype(BF16)
    turn_rows = lax.dynamic_slice_in_dim(turn_one, offset, share, 0)
    second = jnp.dot(turn_rows, first, preferred_element_type=F32).astype(BF16)
    product = jnp.dot(second, turn_one, preferred_element_type=F32)
    turn_two = (1.5 * eye_rows - 0.5 * product).astype(BF16)
    inverse_rows = jnp.dot(turn_two, turn_one, preferred_element_type=F32)
    chosen = jnp.where(iter_count[0, 0] == 1, turn_rows.astype(F32), inverse_rows)
    root = (chosen / jnp.sqrt(scale)).astype(BF16)
    return (factor[None, None], root[None, None], step[None, None])


def solution(mesh):
    return jax.shard_map(
        square_plan if mesh.shape["dp"] == 4 and mesh.shape["pipe"] == 2 else ring_plan,
        mesh=mesh,
        in_specs=(
            P("pipe", "dp", "tensor"),
            P("pipe", "dp", "tensor"),
            P("pipe", "tensor", "dp", None),
            P("pipe", "tensor", "dp", None),
            P("pipe", "tensor"),
        ),
        out_specs=(
            P("pipe", "tensor", "dp", None),
            P("pipe", "tensor", "dp", None),
            P("pipe", "tensor", None, "dp"),
        ),
        check_vma=False,
    )
```

time: 43.6 us -> 44.9 us (1.030)
  waiting for transfers between devices: 14.4 us -> 20.2 us
  starting transfers between devices: 19.4 us -> 13.9 us
  Pallas kernels: 6.99 us -> 8.08 us
    ppermute x16 -> x8, waiting for transfers between devices: 14.4 us -> 20.2 us  [swapped(): return lax.ppermute(block, ('pipe', 'dp'), route)]
    ppermute x16 -> x8, starting transfers between devices: 18.9 us -> 13.4 us  [swapped(): return lax.ppermute(block, ('pipe', 'dp'), route)]
    pallas_call x11, Pallas kernels: 6.99 us -> 8.08 us  [call(): pl.pallas_call(body, out_shape=outs, in_specs=in_specs, out_specs=whole(l...]
  transfers between devices with their start and end apart: 17 -> 9, of which waited for: 10 -> 7; matrix products, arithmetic and copies ran while one was open for 0% -> 0% of each run, Pallas kernels for 9% -> 9%
where the time goes in v6:
time: 44.9 us; the launch traced here: 44.8 us
  waiting for transfers between devices  20.2 us (45%)
  starting transfers between devices  13.9 us (31%)
  Pallas kernels  8.08 us (18%)
  between operations  1.34 us (3%)
  local copies, waits for them, and re-layouts  1.23 us (3%)
    ppermute x8, waiting for transfers between devices, swapped(): return lax.ppermute(block, ('pipe', 'dp'), route)  20.2 us
    ppermute x8, starting transfers between devices, swapped(): return lax.ppermute(block, ('pipe', 'dp'), route)  13.4 us
    pallas_call x11, Pallas kernels, call(): pl.pallas_call(body, out_shape=outs, in_specs=in_specs, out_specs=whole(l...  8.08 us
    unnamed x6, local copies, waits for them, and re-layouts  1.23 us
  transfers between devices with their start and end apart: 9, of which 7 were waited for; matrix products, arithmetic and copies ran while one was open for 0% of the time, Pallas kernels for 9%

profile of v6, /device:TPU:0, one launch (start us, length us, event | category | flops | bytes accessed | tf_op | source)
XLA Modules:
  0.0 44.8 jit_solution(2045315932372883913)
XLA Ops:
  0.6 0.5 %collective-permute-start.2 = (bf16[1,512,256]{2,1,0:T(8,128)(2,1)}, bf16[1,512,256]{2,1,0:T(8,128)(2,1)S(1)}, u32[]{:S(2)}, u32[]{:S(2)}) collective-permute-start(bf16[1,512,256]{2,1,0:T(8,128)(2,1)} %param.6), channel_id=1, source_target_pairs={{16,0},{0,16},{17,1},{1,17},{18,2},{2,18},{19,3},{3,19},{20,4},{4,... | collective-permute-start | bytes 786440 | tf_op jit(solution)/shard_map/ppermute | solution.py:22
  1.1 0.0 copy-start
  1.1 1.2 %copy-done = bf16[1,512,1024]{2,1,0:T(8,128)(2,1)S(1)} copy-done((bf16[1,512,1024]{2,1,0:T(8,128)(2,1)S(1)}, bf16[1,512,1024]{2,1,0:T(8,128)(2,1)}, u32[]{:S(2)}) %copy-start) | copy-done | bytes 1048600
  2.4 1.1 %batch.1 = (bf16[896,256]{1,0:T(8,128)(2,1)S(1)}, f32[896,256]{1,0:T(8,128)S(1)}, f32[512,256]{1,0:T(8,128)S(1)}) custom-call(bf16[512,1024]{1,0:T(8,128)(2,1)S(1)} %bitcast.7), custom_call_target="tpu_custom_call" | custom-call | tf_op jit(solution)/shard_map/batch/pallas_call | solution.py:360
  3.4 2.6 %collective-permute-start = (bf16[896,256]{1,0:T(8,128)(2,1)S(1)}, bf16[896,256]{1,0:T(8,128)(2,1)S(1)}, u32[]{:S(2)}, u32[]{:S(2)}) collective-permute-start(bf16[896,256]{1,0:T(8,128)(2,1)S(1)} %get-tuple-element.18), channel_id=1, source_target_pairs={{0,4},{4,0},{8,12},{12,8},{16,24},{20,28},{24,16},{28,20},{1,5},{5... | collective-permute-start | bytes 1376264 | tf_op jit(solution)/shard_map/ppermute | solution.py:35
  6.0 0.0 collective-permute-done.2
  6.0 0.0 copy-start.1
  6.0 0.5 %grad.1 = (bf16[768,256]{1,0:T(8,128)(2,1)S(1)}, f32[768,256]{1,0:T(8,128)S(1)}) custom-call(bf16[512,1024]{1,0:T(8,128)(2,1)S(1)} %bitcast.8, bf16[512,256]{1,0:T(8,128)(2,1)S(1)} %bitcast.12, f32[512,256]{1,0:T(8,128)S(1)} %get-tuple-element.20.refs_2_), custom_call_target="tpu_custom_call" | custom-call | tf_op jit(solution)/shard_map/grad/pallas_call | solution.py:360
  6.5 0.1 collective-permute-start.3
  6.6 5.8 %collective-permute-done.refs_1_ = bf16[896,256]{1,0:T(8,128)(2,1)S(1)} collective-permute-done((bf16[896,256]{1,0:T(8,128)(2,1)S(1)}, bf16[896,256]{1,0:T(8,128)(2,1)S(1)}, u32[]{:S(2)}, u32[]{:S(2)}) %collective-permute-start) | collective-permute-done | bytes 458784 | tf_op jit(solution)/shard_map/ppermute | solution.py:35
  12.5 2.1 %collective-permute-start.1 = (bf16[448,256]{1,0:T(8,128)(2,1)S(1)}, bf16[448,256]{1,0:T(8,128)(2,1)S(1)}, u32[]{:S(2)}, u32[]{:S(2)}) collective-permute-start(bf16[448,256]{1,0:T(8,128)(2,1)S(1)} %relay.1), channel_id=1, source_target_pairs={{0,8},{4,12},{8,0},{12,4},{16,20},{20,16},{24,28},{28,24},{1,9},{5... | collective-permute-start | bytes 688136 | tf_op jit(solution)/shard_map/ppermute | solution.py:35
  14.6 3.5 %collective-permute-done.3.refs_1_ = bf16[768,256]{1,0:T(8,128)(2,1)S(1)} collective-permute-done((bf16[768,256]{1,0:T(8,128)(2,1)S(1)}, bf16[768,256]{1,0:T(8,128)(2,1)S(1)}, u32[]{:S(2)}, u32[]{:S(2)}) %collective-permute-start.3) | collective-permute-done | bytes 393248 | tf_op jit(solution)/shard_map/ppermute | solution.py:35
  18.2 2.4 %collective-permute-start.4 = (bf16[384,256]{1,0:T(8,128)(2,1)S(1)}, bf16[384,256]{1,0:T(8,128)(2,1)S(1)}, u32[]{:S(2)}, u32[]{:S(2)}) collective-permute-start(bf16[384,256]{1,0:T(8,128)(2,1)S(1)} %relay_rest.1), channel_id=1, source_target_pairs={{0,8},{4,12},{8,0},{12,4},{16,20},{20,16},{24,28},{28,24},{1,9},{5... | collective-permute-start | bytes 589832 | tf_op jit(solution)/shard_map/ppermute | solution.py:35
  20.6 0.0 collective-permute-done.1.refs_2_
  20.6 0.0 copy-done.1
  20.6 0.2 factor.1
  20.9 0.2 collective-permute-start.5
  21.0 3.2 %collective-permute-done.4.refs_2_ = bf16[384,256]{1,0:T(8,128)(2,1)S(1)} collective-permute-done((bf16[384,256]{1,0:T(8,128)(2,1)S(1)}, bf16[384,256]{1,0:T(8,128)(2,1)S(1)}, u32[]{:S(2)}, u32[]{:S(2)}) %collective-permute-start.4) | collective-permute-done | bytes 196640 | tf_op jit(solution)/shard_map/ppermute | solution.py:35
  24.3 0.2 factor_rest.1
  24.4 2.1 %collective-permute-start.7 = (bf16[400,256]{1,0:T(8,128)(2,1)S(1)}, bf16[400,256]{1,0:T(8,128)(2,1)S(1)}, u32[]{:S(2)}, u32[]{:S(2)}) collective-permute-start(bf16[400,256]{1,0:T(8,128)(2,1)S(1)} %get-tuple-element.26.refs_0_), channel_id=1, source_target_pairs={{0,8},{4,12},{8,0},{12,4},{16,20},{20,16},{24,28},{28,24},{1,9},{5... | collective-permute-start | bytes 614408 | tf_op jit(solution)/shard_map/ppermute | solution.py:35
  26.5 0.4 collective-permute-done.5.refs_1_
  27.0 1.8 %collective-permute-start.6 = (bf16[896,256]{1,0:T(8,128)(2,1)S(1)}, bf16[896,256]{1,0:T(8,128)(2,1)S(1)}, u32[]{:S(2)}, u32[]{:S(2)}) collective-permute-start(bf16[896,256]{1,0:T(8,128)(2,1)S(1)} %pair.1.refs_2_.refs_0_), channel_id=1, source_target_pairs={{0,4},{4,0},{8,12},{12,8},{16,24},{20,28},{24,16},{28,20},{1,5},{5... | collective-permute-start | bytes 1376264 | tf_op jit(solution)/shard_map/ppermute | solution.py:35
  28.8 3.6 %collective-permute-done.7.refs_1_ = bf16[400,256]{1,0:T(8,128)(2,1)S(1)} collective-permute-done((bf16[400,256]{1,0:T(8,128)(2,1)S(1)}, bf16[400,256]{1,0:T(8,128)(2,1)S(1)}, u32[]{:S(2)}, u32[]{:S(2)}) %collective-permute-start.7) | collective-permute-done | bytes 204832 | tf_op jit(solution)/shard_map/ppermute | solution.py:35
  32.4 0.0 copy-start.2
  32.4 2.1 %collective-permute-start.8 = (bf16[800,256]{1,0:T(8,128)(2,1)S(1)}, bf16[800,256]{1,0:T(8,128)(2,1)S(1)}, u32[]{:S(2)}, u32[]{:S(2)}) collective-permute-start(bf16[800,256]{1,0:T(8,128)(2,1)S(1)} %pair_rest.1.refs_1_.refs_3_), channel_id=1, source_target_pairs={{0,4},{4,0},{8,12},{12,8},{16,24},{20,28},{24,16},{28,20},{1,5},{5... | collective-permute-start | bytes 1228808 | tf_op jit(solution)/shard_map/ppermute | solution.py:35
  35.2 0.3 collective-permute-done.6.refs_2_
  35.5 0.5 %matrix.1 = (bf16[1024,1024]{1,0:T(8,128)(2,1)S(1)}, f32[1,1024]{1,0:T(1,128)S(1)}) custom-call(bf16[896,256]{1,0:T(8,128)(2,1)S(1)} %pair.1.refs_2_.refs_0_, bf16[800,256]{1,0:T(8,128)(2,1)S(1)} %pair_rest.1.refs_1_.refs_3_, bf16[896,256]{1,0:T(8,128)(2,1)S(1)} %collective-permute-done.6.refs_2_), custom_call_target="tpu_custom_call" | custom-call | tf_op jit(solution)/shard_map/matrix/pallas_call | solution.py:360
  36.1 1.2 %new_rows.1 = f32[256,1024]{1,0:T(8,128)} custom-call(f32[448,256]{1,0:T(8,128)S(1)} %get-tuple-element.19.refs_0_, f32[128,256]{1,0:T(8,128)S(1)} %get-tuple-element.24.refs_1_, bf16[896,256]{1,0:T(8,128)(2,1)S(1)} %collective-permute-done.6.refs_2_, bf16[800,256]{1,0:T(8,128)(2,1)S(1)} %pair_rest.1.refs_1_.refs_3_, ...), custom_call_target="tpu_custom_call" | custom-call | tf_op jit(solution)/shard_map/new_rows/pallas_call | solution.py:360
  37.2 3.2 %collective-permute-done.8.refs_4_ = bf16[800,256]{1,0:T(8,128)(2,1)S(1)} collective-permute-done((bf16[800,256]{1,0:T(8,128)(2,1)S(1)}, bf16[800,256]{1,0:T(8,128)(2,1)S(1)}, u32[]{:S(2)}, u32[]{:S(2)}) %collective-permute-start.8) | collective-permute-done | bytes 409632 | tf_op jit(solution)/shard_map/ppermute | solution.py:35
  40.5 0.0 copy-done.2
  40.5 4.3 %root.1 = (bf16[256,1024]{1,0:T(8,128)(2,1)}, bf16[256,256]{1,0:T(8,128)(2,1)}) custom-call(s32[1,1]{1,0:T(1,128)S(6)} %copy.8.refs_0_, bf16[1024,1024]{1,0:T(8,128)(2,1)S(1)} %get-tuple-element.28.refs_1_, f32[1,1024]{1,0:T(1,128)S(1)} %get-tuple-element.27.refs_4_.refs_2_, bf16[800,256]{1,0:T(8,128)(2,1)S(1)} %pair_rest.1.refs_1_.refs_3_, ...), custom_call_target="tpu_custom_call" | custom-call | tf_op jit(solution)/shard_map/root/pallas_call | solution.py:360
  (4 shorter events, 0.1 us)
Async XLA Ops:
  0.6 5.4 %collective-permute-start.2 = (bf16[1,512,256]{2,1,0:T(8,128)(2,1)}, bf16[1,512,256]{2,1,0:T(8,128)(2,1)S(1)}, u32[]{:S(2)}, u32[]{:S(2)}) collective-permute-start(bf16[1,512,256]{2,1,0:T(8,128)(2,1)} %param.6), channel_id=1, source_target_pairs={{16,0},{0,16},{17,1},{1,17},{18,2},{2,18},{19,3},{3,19},{20,4},{4,... | collective-permute-start | bytes 786440 | tf_op jit(solution)/shard_map/ppermute | solution.py:22
  1.1 1.2 %copy-start = (bf16[1,512,1024]{2,1,0:T(8,128)(2,1)S(1)}, bf16[1,512,1024]{2,1,0:T(8,128)(2,1)}, u32[]{:S(2)}) copy-start(bf16[1,512,1024]{2,1,0:T(8,128)(2,1)} %param.5) | copy-start | bytes 3145732
  3.4 9.0 %collective-permute-start = (bf16[896,256]{1,0:T(8,128)(2,1)S(1)}, bf16[896,256]{1,0:T(8,128)(2,1)S(1)}, u32[]{:S(2)}, u32[]{:S(2)}) collective-permute-start(bf16[896,256]{1,0:T(8,128)(2,1)S(1)} %get-tuple-element.18), channel_id=1, source_target_pairs={{0,4},{4,0},{8,12},{12,8},{16,24},{20,28},{24,16},{28,20},{1,5},{5... | collective-permute-start | bytes 1376264 | tf_op jit(solution)/shard_map/ppermute | solution.py:35
  6.0 14.6 %copy-start.1 = (f32[1,1,256,1024]{3,2,1,0:T(8,128)S(1)}, f32[1,1,256,1024]{3,2,1,0:T(8,128)}, u32[]{:S(2)}) copy-start(f32[1,1,256,1024]{3,2,1,0:T(8,128)} %param.7) | copy-start | bytes 3145732
  6.5 11.6 %collective-permute-start.3 = (bf16[768,256]{1,0:T(8,128)(2,1)S(1)}, bf16[768,256]{1,0:T(8,128)(2,1)S(1)}, u32[]{:S(2)}, u32[]{:S(2)}) collective-permute-start(bf16[768,256]{1,0:T(8,128)(2,1)S(1)} %get-tuple-element.22), channel_id=1, source_target_pairs={{0,4},{4,0},{8,12},{12,8},{16,24},{20,28},{24,16},{28,20},{1,5},{5... | collective-permute-start | bytes 1179656 | tf_op jit(solution)/shard_map/ppermute | solution.py:35
  12.5 8.1 %collective-permute-start.1 = (bf16[448,256]{1,0:T(8,128)(2,1)S(1)}, bf16[448,256]{1,0:T(8,128)(2,1)S(1)}, u32[]{:S(2)}, u32[]{:S(2)}) collective-permute-start(bf16[448,256]{1,0:T(8,128)(2,1)S(1)} %relay.1), channel_id=1, source_target_pairs={{0,8},{4,12},{8,0},{12,4},{16,20},{20,16},{24,28},{28,24},{1,9},{5... | collective-permute-start | bytes 688136 | tf_op jit(solution)/shard_map/ppermute | solution.py:35
  18.2 6.1 %collective-permute-start.4 = (bf16[384,256]{1,0:T(8,128)(2,1)S(1)}, bf16[384,256]{1,0:T(8,128)(2,1)S(1)}, u32[]{:S(2)}, u32[]{:S(2)}) collective-permute-start(bf16[384,256]{1,0:T(8,128)(2,1)S(1)} %relay_rest.1), channel_id=1, source_target_pairs={{0,8},{4,12},{8,0},{12,4},{16,20},{20,16},{24,28},{28,24},{1,9},{5... | collective-permute-start | bytes 589832 | tf_op jit(solution)/shard_map/ppermute | solution.py:35
  20.9 6.1 %collective-permute-start.5 = (bf16[448,256]{1,0:T(8,128)(2,1)S(1)}, bf16[448,256]{1,0:T(8,128)(2,1)S(1)}, u32[]{:S(2)}, u32[]{:S(2)}) collective-permute-start(bf16[448,256]{1,0:T(8,128)(2,1)S(1)} %get-tuple-element.25.refs_0_), channel_id=1, source_target_pairs={{0,8},{4,12},{8,0},{12,4},{16,20},{20,16},{24,28},{28,24},{1,9},{5... | collective-permute-start | bytes 688136 | tf_op jit(solution)/shard_map/ppermute | solution.py:35
  24.4 8.0 %collective-permute-start.7 = (bf16[400,256]{1,0:T(8,128)(2,1)S(1)}, bf16[400,256]{1,0:T(8,128)(2,1)S(1)}, u32[]{:S(2)}, u32[]{:S(2)}) collective-permute-start(bf16[400,256]{1,0:T(8,128)(2,1)S(1)} %get-tuple-element.26.refs_0_), channel_id=1, source_target_pairs={{0,8},{4,12},{8,0},{12,4},{16,20},{20,16},{24,28},{28,24},{1,9},{5... | collective-permute-start | bytes 614408 | tf_op jit(solution)/shard_map/ppermute | solution.py:35
  27.0 8.5 %collective-permute-start.6 = (bf16[896,256]{1,0:T(8,128)(2,1)S(1)}, bf16[896,256]{1,0:T(8,128)(2,1)S(1)}, u32[]{:S(2)}, u32[]{:S(2)}) collective-permute-start(bf16[896,256]{1,0:T(8,128)(2,1)S(1)} %pair.1.refs_2_.refs_0_), channel_id=1, source_target_pairs={{0,4},{4,0},{8,12},{12,8},{16,24},{20,28},{24,16},{28,20},{1,5},{5... | collective-permute-start | bytes 1376264 | tf_op jit(solution)/shard_map/ppermute | solution.py:35
  32.4 8.0 %copy-start.2 = (bf16[1,1,256,1024]{3,2,1,0:T(8,128)(2,1)S(1)}, bf16[1,1,256,1024]{3,2,1,0:T(8,128)(2,1)}, u32[]{:S(2)}) copy-start(bf16[1,1,256,1024]{3,2,1,0:T(8,128)(2,1)} %param.8) | copy-start | bytes 1572868
  32.4 8.0 %collective-permute-start.8 = (bf16[800,256]{1,0:T(8,128)(2,1)S(1)}, bf16[800,256]{1,0:T(8,128)(2,1)S(1)}, u32[]{:S(2)}, u32[]{:S(2)}) collective-permute-start(bf16[800,256]{1,0:T(8,128)(2,1)S(1)} %pair_rest.1.refs_1_.refs_3_), channel_id=1, source_target_pairs={{0,4},{4,0},{8,12},{12,8},{16,24},{20,28},{24,16},{28,20},{1,5},{5... | collective-permute-start | bytes 1228808 | tf_op jit(solution)/shard_map/ppermute | solution.py:35

commit v7 on v0

v7 whole, which is shorter than its diff:
```python
import functools
import math

import jax
import jax.numpy as jnp
from jax import lax
from jax.experimental import pallas as pl
from jax.experimental.pallas import tpu as pltpu
from jax.sharding import PartitionSpec as P

DECAY = 0.75
DAMPING = 0.1
EPSILON = 1e-06
BF16 = jnp.bfloat16
F32 = jnp.float32
VMEM_LIMIT = 28 * 1024 * 1024


def passed_along(block, axis, distance):
    devices = range(lax.axis_size(axis))
    route = [((i - distance) % len(devices), i) for i in devices]
    return lax.ppermute(block, axis, route)


def swapped(block, offset):
    return lax.ppermute(block, "dp", [(i, i ^ offset) for i in range(lax.axis_size("dp"))])


def along(turn):
    return jnp.where(lax.axis_index("pipe") == turn, 1, 2)


def swapped_along(block, turn):
    replicas = lax.axis_size("dp")
    route = []
    for section in range(lax.axis_size("pipe")):
        offset = 1 if section == turn else 2
        route += [(section * replicas + i, section * replicas + (i ^ offset)) for i in range(replicas)]
    return lax.ppermute(block, ("pipe", "dp"), route)


def eye_of(rows, cols, shift=0):
    row_ids = lax.broadcasted_iota(jnp.int32, (rows, cols), 0) + shift
    col_ids = lax.broadcasted_iota(jnp.int32, (rows, cols), 1)
    return (row_ids == col_ids).astype(F32)


def whole(count):
    return [pl.BlockSpec(memory_space=pltpu.VMEM)] * count


def transposed(block):
    return block.astype(F32).T.astype(block.dtype)


OVER_ROWS = (((0,), (0,)), ((), ()))


def chunk_starts(share):
    half = share // 2
    return (0, half) + tuple(half + half // 2 + half * i for i in range(4))


def shared_half(owner, offset, share):
    other = owner ^ offset
    low, high = jnp.minimum(owner, other), jnp.maximum(owner, other)
    row = low * share + jnp.where(owner > other, share // 2, 0)
    return pl.multiple_of(row, share // 2), pl.multiple_of(high * share, share)


def band(index, size):
    return pl.ds(pl.multiple_of(index * size, size), size)


def side_by_side(low):
    half = low.shape[0] // 2
    return jnp.concatenate([low[0:half], low[half:]], axis=1)


def stacked(packed):
    half = packed.shape[1] // 2
    return jnp.concatenate([packed[:, 0:half], packed[:, half:]], axis=0)


def store_chunk(pieces, length, upper, lower):
    for start, piece in pieces:
        stop = start + piece.shape[0]
        for target, low, high in ((upper, 0, length), (lower, length, stop)):
            first, last = max(start, low), min(stop, high)
            if first < last:
                ref, at = target
                ref[at + first - low : at + last - low, :] = piece[first - start : last - start].astype(ref.dtype)


def batch_kernel(replicas, tokens_all, acts, send_x, send_y, keep, batch):
    order = acts.shape[1]
    share = order // replicas
    half = share // 2
    starts = chunk_starts(share)
    length = send_x.shape[0] // 2
    mine = lax.axis_index("dp")
    for i in range(replicas):
        rows = slice(i * share, (i + 1) * share)
        batch[rows, i * share :] = lax.dot_general(
            acts[:, rows], acts[:, i * share :], OVER_ROWS, preferred_element_type=F32
        ) * (1.0 / tokens_all)

    def pieces(offset):
        owner = mine ^ offset
        corner = pl.ds(pl.multiple_of(owner * share + half, half), half)
        yield starts[0], batch[pl.ds(pl.multiple_of(owner * share, share), half), band(owner, share)]
        yield starts[1], side_by_side(batch[corner, corner])
        for step in range(1, replicas):
            row, col = shared_half(owner, step, share)
            yield starts[1 + step], batch[pl.ds(row, half), pl.ds(col, share)]

    store_chunk(pieces(3), length, (send_x, 0), (send_y, 0))
    store_chunk(pieces(1), length, (send_x, length), (keep, 3 * length))
    store_chunk(pieces(2), length, (keep, 2 * length), (send_y, length))
    store_chunk(pieces(0), length, (keep, 0), (keep, length))


def relay_kernel(keep, got_x, got_y, send_x, send_y):
    length = send_x.shape[0]
    send_y[...] = (keep[2 * length : 3 * length, :] + got_x[0:length, :].astype(F32)).astype(BF16)
    send_x[...] = (keep[3 * length :, :] + got_y[0:length, :].astype(F32)).astype(BF16)


def grad_kernel(replicas, tokens_all, acts, grads, send, keep, total):
    share = acts.shape[1] // replicas
    strip = grads.shape[1] // replicas
    mine = lax.axis_index("dp")
    total[...] = lax.dot_general(grads[...], acts[...], OVER_ROWS, preferred_element_type=F32) * (
        1.0 / math.sqrt(tokens_all)
    )
    for ref, offsets in ((send, (along(0), 3)), (keep, (0, along(1)))):
        for i, offset in enumerate(offsets):
            for part in range(replicas):
                start = (i * replicas + part) * strip
                piece = total[band(mine ^ offset, strip), part * share : (part + 1) * share]
                ref[start : start + strip, :] = piece.astype(ref.dtype)


def strip_relay_kernel(keep, got, send):
    length = send.shape[0]
    send[...] = (keep[length:, :] + got[length:, :].astype(F32)).astype(BF16)


def strip_kernel(keep, got, relayed, strip):
    length = strip.shape[0]
    strip[...] = (keep[0:length, :] + got[0:length, :].astype(F32) + relayed[...].astype(F32)).astype(BF16)


def pair_kernel(own, got, send):
    length = own.shape[0]
    send[0:length, :] = own[...]
    send[length:, :] = got[...]


def factor_kernel(keep, got_x, got_y, relay_x, relay_y, old, chunk, exact):
    share = old.shape[0]
    half = share // 2
    starts = chunk_starts(share)
    length = relay_x.shape[0]
    mine = lax.axis_index("dp")
    upper = keep[0:length, :] + got_x[length:, :].astype(F32) + relay_y[...].astype(F32)
    lower = keep[length : 2 * length, :] + got_y[length:, :].astype(F32) + relay_x[...].astype(F32)
    total = jnp.concatenate([upper, lower], axis=0)
    diagonal = old[:, band(mine, share)]
    terms = [
        DECAY * diagonal[0:half] + DAMPING * eye_of(half, share),
        side_by_side(DECAY * diagonal[half:, half:] + DAMPING * eye_of(half, half)),
    ]
    for offset in range(1, 4):
        block = old[:, band(mine ^ offset, share)]
        terms.append(DECAY * jnp.where(mine < mine ^ offset, block[0:half], block[:, half:].T))
    column = lax.broadcasted_iota(jnp.int32, (1, share), 1)
    weights = [jnp.where(column < half, 1.0, 2.0), 1.0, 2.0, 2.0, 2.0]
    sums = jnp.zeros((1, share), F32)
    for start, term, weight in zip(starts, terms, weights):
        rows = slice(start, start + term.shape[0])
        value = term + (1.0 - DECAY) * total[rows]
        exact[rows, :] = value
        chunk[rows, :] = value.astype(BF16)
        sums = sums + weight * jnp.sum(value * value, axis=0, keepdims=True)
    high = sums.astype(BF16).astype(F32)
    middle = (sums - high).astype(BF16).astype(F32)
    rest = sums - high - middle
    spot = lax.broadcasted_iota(jnp.int32, (chunk.shape[0] - 2 * length, share), 0)
    digits = jnp.where(spot == 0, high, jnp.where(spot == 1, middle, jnp.where(spot == 2, rest, 0.0)))
    chunk[2 * length :, :] = digits.astype(BF16)


def halves_kernel(got_x, got_y, send_x, send_y):
    length = send_y.shape[0]
    send_y[...] = got_x[0:length, :]
    send_x[...] = got_y[length:, :]


def place(factor, diagonal, owner, read, share):
    half = share // 2
    starts = chunk_starts(share)
    base = pl.ds(pl.multiple_of(owner * share, share), half)
    corner = pl.ds(pl.multiple_of(owner * share + half, half), half)
    top = read(starts[0], half)
    low = stacked(read(starts[1], half // 2))
    factor[base, band(owner, share)] = top
    factor[corner, base] = transposed(top[:, half:])
    factor[corner, corner] = low
    eye = eye_of(half, half)
    diagonal[:, base] = jnp.sum(top[:, 0:half].astype(F32) * eye, axis=0, keepdims=True)
    diagonal[:, corner] = jnp.sum(low.astype(F32) * eye, axis=0, keepdims=True)
    for offset in range(1, 4):
        row, col = shared_half(owner, offset, share)
        block = read(starts[1 + offset], half)
        factor[pl.ds(row, half), pl.ds(col, share)] = block
        factor[pl.ds(col, share), pl.ds(row, half)] = transposed(block)


def rows_of(upper, lower=None):
    def read(start, count):
        if lower is None:
            return upper[start : start + count, :]
        length = upper.shape[0]
        if start + count <= length:
            return upper[start : start + count, :]
        if start >= length:
            return lower[start - length : start - length + count, :]
        return jnp.concatenate([upper[start:, :], lower[0 : start + count - length, :]], axis=0)

    return read


def store_shared(target, columns, own_is_upper, own, theirs):
    half = own.shape[0]

    @pl.when(own_is_upper)
    def _():
        target[0:half, columns] = own
        target[half:, columns] = theirs

    @pl.when(jnp.logical_not(own_is_upper))
    def _():
        target[:, columns] = jnp.concatenate([theirs.T, own.T], axis=1)


def matrix_kernel(exact, chunk, near, side, old_root, factor, diagonal, squares, rows, old_columns):
    share = exact.shape[1]
    half = share // 2
    starts = chunk_starts(share)
    mine = lax.axis_index("dp")
    factor[...] = jnp.zeros_like(factor)
    diagonal[...] = jnp.zeros_like(diagonal)
    sums = jnp.zeros((chunk.shape[0] - starts[-1], share), F32)
    for offset, ref in enumerate((chunk, near, side)):
        place(factor, diagonal, mine ^ offset, rows_of(ref), share)
        sums = sums + ref[starts[-1] :, :].astype(F32)
    squares[...] = sums
    top = exact[0:half, :]
    low = stacked(exact[starts[1] : starts[2], :])
    rows[0:half, band(mine, share)] = top
    rows[half:, band(mine, share)] = jnp.concatenate([top[:, half:].T, low], axis=1)
    for offset, ref in ((1, near), (2, side)):
        part = slice(starts[1 + offset], starts[1 + offset] + half)
        other = mine ^ offset
        store_shared(rows, band(other, share), mine < other, exact[part, :], ref[part, :].astype(F32))
    rows[:, band(mine ^ 3, share)] = jnp.zeros((share, share), F32)
    old_columns[...] = transposed(old_root[...])


def root_kernel(
    count, known, known_diagonal, squares, rows, exact, upper, lower, factor_out, root_out, finished, factor, diagonal,
    shared, sent,
):
    share, order = root_out.shape
    half = share // 2
    starts = chunk_starts(share)
    mine = lax.axis_index("dp")
    read = rows_of(upper, lower)
    last = slice(starts[4], starts[5])
    store_shared(shared, slice(None), mine < mine ^ 3, exact[last, :], read(starts[4], half).astype(F32))
    copies = []
    for offset in range(4):
        columns = band(mine ^ offset, share)
        source = shared if offset == 3 else rows.at[:, columns]
        copies.append(pltpu.make_async_copy(source, factor_out.at[:, columns], sent.at[offset]))
        copies[-1].start()

    factor[...] = known[...]
    diagonal[...] = known_diagonal[...]
    place(factor, diagonal, mine ^ 3, read, share)
    total = squares[...] + lower[lower.shape[0] - squares.shape[0] :, :].astype(F32)
    scale = jnp.sqrt(jnp.sum(total, keepdims=True) / order + EPSILON)
    inverse = 1.0 / scale
    ones = (diagonal[...] * inverse).astype(BF16).astype(F32)
    lift = (1.5 - 0.5 * ones).astype(BF16).astype(F32) + 0.5 * (diagonal[...] * inverse)
    eye = eye_of(share, order, mine * share)
    first = (factor[band(mine, share), :].astype(F32) * inverse).astype(BF16).astype(F32)
    turn = (1.5 * eye - 0.5 * first).astype(BF16)
    second = (jnp.dot(turn, factor[...], preferred_element_type=F32) * inverse).astype(BF16)
    product = (-0.5 * inverse) * jnp.dot(second, factor[...], preferred_element_type=F32) + second.astype(F32) * lift
    turn_two = (1.5 * eye - 0.5 * product).astype(BF16)
    inverse_rows = (-0.5 * inverse) * jnp.dot(
        turn_two, factor[...], preferred_element_type=F32
    ) + turn_two.astype(F32) * lift
    chosen = jnp.where(count[0, 0] == 1, turn.astype(F32), inverse_rows)
    root_out[...] = (chosen * lax.rsqrt(scale)).astype(BF16)
    finished[...] = jnp.zeros_like(finished)
    for copy in copies:
        copy.wait()


def step_kernel(replicas, pair, far, old_columns, step_out, grads, result):
    share = old_columns.shape[1]
    strip = step_out.shape[0] // replicas
    length = pair.shape[0] // 2
    mine = lax.axis_index("dp")
    strips = [(pair, 0, 0), (pair, length, along(1)), (far, 0, along(0)), (far, length, 3)]
    for i, (ref, at, _) in enumerate(strips):
        for part in range(replicas):
            start = at + part * strip
            grads[i * strip : (i + 1) * strip, part * share : (part + 1) * share] = ref[start : start + strip, :]
    result[...] = jnp.dot(grads[...], old_columns[...], preferred_element_type=F32).astype(BF16)
    for i, (_, _, offset) in enumerate(strips):
        step_out[band(mine ^ offset, strip), :] = result[i * strip : (i + 1) * strip, :]


def square_plan(acts, out_grad, old_factor, old_root, iter_count):
    replicas = lax.axis_size("dp")
    inputs = acts[0]
    tokens, order = inputs.shape
    share = order // replicas
    grows = out_grad.shape[2]
    params = pltpu.CompilerParams(vmem_limit_bytes=VMEM_LIMIT)
    length = chunk_starts(share)[-1]
    digits = 16

    def shape(rows, kind=BF16, columns=share):
        return jax.ShapeDtypeStruct((rows, columns), kind)

    def call(kernel, outs, name, *operands, flops=0, scalar=False, first_out=None, after=(), scratch=()):
        in_specs = whole(len(operands)) + [pl.BlockSpec(memory_space=pl.ANY)] * len(after)
        out_specs = whole(len(outs))
        if scalar:
            in_specs[0] = pl.BlockSpec(memory_space=pltpu.SMEM)
        if first_out is not None:
            out_specs[0] = pl.BlockSpec(memory_space=first_out)

        def body(*refs):
            kernel(*refs[: len(operands)], *refs[len(operands) + len(after) :])

        return pl.pallas_call(
            body,
            out_shape=outs,
            in_specs=in_specs,
            out_specs=out_specs,
            scratch_shapes=scratch,
            compiler_params=params,
            cost_estimate=pl.CostEstimate(
                flops=flops,
                bytes_accessed=sum(x.size * x.dtype.itemsize for x in (*operands, *outs)),
                transcendentals=0,
            ),
            name=name,
        )(*operands, *after)

    def both(x, y):
        return swapped(x, 1), swapped(y, 2)

    received = passed_along(out_grad, "pipe", -1)[0]
    send_x, send_y, keep = call(
        functools.partial(batch_kernel, replicas, tokens * replicas),
        [shape(length)] * 2 + [shape(2 * length, F32)],
        "batch",
        inputs,
        flops=5 * tokens * order * order // 4,
        scratch=[pltpu.VMEM((order, order), F32)],
    )
    got_x, got_y = both(send_x, send_y)
    on_x, on_y = call(relay_kernel, [shape(length // 2)] * 2, "relay", keep, got_x, got_y)
    relay_x, relay_y = both(on_x, on_y)
    strips, strips_keep = call(
        functools.partial(grad_kernel, replicas, tokens * replicas),
        [shape(2 * grows), shape(2 * grows, F32)],
        "grad",
        inputs,
        received,
        flops=2 * tokens * order * grows,
        scratch=[pltpu.VMEM((grows, order), F32)],
    )
    strips_got = swapped_along(strips, 0)
    chunk, exact = call(
        factor_kernel,
        [shape(length + digits), shape(length, F32)],
        "factor",
        keep,
        got_x,
        got_y,
        relay_x,
        relay_y,
        old_factor[0, 0],
    )
    near, side = both(chunk, chunk)
    (strip_on,) = call(strip_relay_kernel, [shape(grows)], "strip_relay", strips_keep, strips_got, after=[chunk])
    strip_relayed = swapped_along(strip_on, 1)
    (strip,) = call(strip_kernel, [shape(grows)], "strip", strips_keep, strips_got, strip_relayed)
    strip_near = swapped_along(strip, 1)
    on_x, on_y = call(halves_kernel, [shape(length // 2 + digits), shape(length // 2)], "halves", near, side)
    lower, upper = both(on_x, on_y)
    known, diagonal, squares, rows, old_columns = call(
        matrix_kernel,
        [shape(order, BF16, order), shape(1, F32, order), shape(digits, F32), shape(share, F32, order), shape(order)],
        "matrix",
        exact,
        chunk,
        near,
        side,
        old_root[0, 0],
        after=[on_x],
    )
    (pair,) = call(pair_kernel, [shape(2 * grows)], "pair", strip, strip_near, after=[diagonal])
    pair_far = swapped_along(pair, 0)
    factor, root, finished = call(
        root_kernel,
        [shape(share, F32, order), shape(share, BF16, order), shape(8, F32, 128)],
        "root",
        iter_count,
        known,
        diagonal,
        squares,
        rows,
        exact,
        upper,
        lower,
        flops=6 * share * order * order,
        scalar=True,
        first_out=pl.ANY,
        scratch=[
            pltpu.VMEM((order, order), BF16),
            pltpu.VMEM((1, order), F32),
            pltpu.VMEM((share, share), F32),
            pltpu.SemaphoreType.DMA((replicas,)),
        ],
    )
    (step,) = call(
        functools.partial(step_kernel, replicas),
        [shape(grows)],
        "step",
        pair,
        pair_far,
        old_columns,
        flops=2 * grows * order * share,
        after=[finished],
        scratch=[pltpu.VMEM((grows, order), BF16), pltpu.VMEM((grows, share), BF16)],
    )
    return (factor[None, None], root[None, None], step[None, None])


def ring_plan(acts, out_grad, old_factor, old_root, iter_count):
    inputs = acts[0]
    replicas = lax.axis_size("dp")
    tokens_all = inputs.shape[0] * replicas
    order = inputs.shape[1]
    share = order // replicas
    offset = lax.axis_index("dp") * share
    received = passed_along(out_grad, "pipe", -1)[0]
    partial_grad = jnp.dot(received.T, inputs, preferred_element_type=F32) / math.sqrt(tokens_all)
    batch = lax.psum_scatter(
        jnp.dot(inputs.T, inputs, preferred_element_type=F32) / tokens_all,
        "dp",
        scatter_dimension=0,
        tiled=True,
    )
    eye_rows = eye_of(share, order, offset)
    factor = DECAY * old_factor[0, 0] + (1.0 - DECAY) * batch + DAMPING * eye_rows
    grad16 = lax.psum(partial_grad, "dp").astype(BF16)
    scale = jnp.sqrt(lax.psum(jnp.sum(factor * factor), "dp") / order + EPSILON)
    step = lax.dot_general(
        grad16, old_root[0, 0], (((1,), (1,)), ((), ())), preferred_element_type=F32
    ).astype(BF16)
    first = lax.all_gather((factor / scale).astype(BF16), "dp", axis=0, tiled=True)
    turn_one = (1.5 * eye_of(order, order) - 0.5 * first.astype(F32)).astype(BF16)
    turn_rows = lax.dynamic_slice_in_dim(turn_one, offset, share, 0)
    second = jnp.dot(turn_rows, first, preferred_element_type=F32).astype(BF16)
    product = jnp.dot(second, turn_one, preferred_element_type=F32)
    turn_two = (1.5 * eye_rows - 0.5 * product).astype(BF16)
    inverse_rows = jnp.dot(turn_two, turn_one, preferred_element_type=F32)
    chosen = jnp.where(iter_count[0, 0] == 1, turn_rows.astype(F32), inverse_rows)
    root = (chosen / jnp.sqrt(scale)).astype(BF16)
    return (factor[None, None], root[None, None], step[None, None])


def solution(mesh):
    return jax.shard_map(
        square_plan if mesh.shape["dp"] == 4 and mesh.shape["pipe"] == 2 else ring_plan,
        mesh=mesh,
        in_specs=(
            P("pipe", "dp", "tensor"),
            P("pipe", "dp", "tensor"),
            P("pipe", "tensor", "dp", None),
            P("pipe", "tensor", "dp", None),
            P("pipe", "tensor"),
        ),
        out_specs=(
            P("pipe", "tensor", "dp", None),
            P("pipe", "tensor", "dp", None),
            P("pipe", "tensor", None, "dp"),
        ),
        check_vma=False,
    )
```

time: 199 us -> 45 us (0.23)
  waiting for transfers between devices: 121 us -> 18.1 us
  blocking collectives: 42.7 us -> 0 us
  starting transfers between devices: 0.63 us -> 16.6 us
  between operations: 15.2 us -> 1.37 us
  matrix products: 11.8 us -> 0 us
  Pallas kernels: 0 us -> 7.48 us
  other arithmetic: 5.71 us -> 0 us
    all_gather x2 -> x0, waiting for transfers between devices: 66.7 us -> none  [the longest x1 35.1 us: local(): first_full = lax.all_gather(first_rows, 'dp', axis=0, tiled=True)]
    reduce_scatter x1 -> x0, waiting for transfers between devices: 53.4 us -> none  [local(): lax.psum_scatter(jnp.dot(columns.T, inputs, preferred_element_type=jnp.fl...]
    psum x1 -> x0, blocking collectives: 42.7 us -> none  [local(): square_total = lax.psum(squares, 'dp')]
    ppermute x0 -> x12, waiting for transfers between devices: none -> 18.1 us  [the longest x8 11.7 us: swapped(): lax.ppermute(block, 'dp', [(i, i ^ offset) for i in range(lax.axis_size('...]
    ppermute x0 -> x12, starting transfers between devices: none -> 16.1 us  [the longest x8 11.8 us: swapped(): lax.ppermute(block, 'dp', [(i, i ^ offset) for i in range(lax.axis_size('...]
    dot_general x5 -> x0, matrix products: 11.8 us -> none  [the longest x1 3.76 us: local(): jnp.dot(turn_two, turn_one, preferred_element_type=jnp.float32)]
    pallas_call x0 -> x11, Pallas kernels: none -> 7.48 us  [call(): pl.pallas_call(body, out_shape=outs, in_specs=in_specs, out_specs=out_spe...]
    convert_element_type x2 -> x0, other arithmetic: 3.06 us -> none  [the longest x1 2.15 us: local(): (1.5 * eye_full - 0.5 * first_full.astype(jnp.float32)).astype(jnp.bfloat16)]
  transfers between devices with their start and end apart: 4 -> 13, of which waited for: 4 -> 7; matrix products, arithmetic and copies ran while one was open for 2% -> 0% of each run, Pallas kernels for 0% -> 14%
where the time goes in v7:
time: 45 us; the launch traced here: 44.9 us
  waiting for transfers between devices  18.1 us (40%)
  starting transfers between devices  16.6 us (37%)
  Pallas kernels  7.48 us (17%)
  between operations  1.37 us (3%)
  local copies, waits for them, and re-layouts  1.24 us (3%)
    ppermute x8, starting transfers between devices, swapped(): lax.ppermute(block, 'dp', [(i, i ^ offset) for i in range(lax.axis_size('...  11.8 us
    ppermute x8, waiting for transfers between devices, swapped(): lax.ppermute(block, 'dp', [(i, i ^ offset) for i in range(lax.axis_size('...  11.7 us
    pallas_call x11, Pallas kernels, call(): pl.pallas_call(body, out_shape=outs, in_specs=in_specs, out_specs=out_spe...  7.48 us
    ppermute x4, waiting for transfers between devices, swapped_along(): return lax.ppermute(block, ('pipe', 'dp'), route)  6.41 us
    ppermute x4, starting transfers between devices, swapped_along(): return lax.ppermute(block, ('pipe', 'dp'), route)  4.31 us
    unnamed x6, local copies, waits for them, and re-layouts  1.24 us
  transfers between devices with their start and end apart: 13, of which 7 were waited for; matrix products, arithmetic and copies ran while one was open for 0% of the time, Pallas kernels for 14%

profile of v7, /device:TPU:0, one launch (start us, length us, event | category | flops | bytes accessed | tf_op | source)
XLA Modules:
  0.0 44.9 jit_solution(10333644638934063035)
XLA Ops:
  0.6 0.5 %collective-permute-start.8 = (bf16[1,512,256]{2,1,0:T(8,128)(2,1)}, bf16[1,512,256]{2,1,0:T(8,128)(2,1)S(1)}, u32[]{:S(2)}, u32[]{:S(2)}) collective-permute-start(bf16[1,512,256]{2,1,0:T(8,128)(2,1)} %param.6), channel_id=1, source_target_pairs={{16,0},{0,16},{17,1},{1,17},{18,2},{2,18},{19,3},{3,19},{20,4},{4,... | collective-permute-start | bytes 786440 | tf_op jit(solution)/shard_map/ppermute | solution.py:22
  1.1 0.0 copy-start.1
  1.1 1.2 %copy-done.1 = bf16[1,512,1024]{2,1,0:T(8,128)(2,1)S(1)} copy-done((bf16[1,512,1024]{2,1,0:T(8,128)(2,1)S(1)}, bf16[1,512,1024]{2,1,0:T(8,128)(2,1)}, u32[]{:S(2)}) %copy-start.1) | copy-done | bytes 1048600
  2.4 1.1 %batch.1 = (bf16[576,256]{1,0:T(8,128)(2,1)S(1)}, bf16[576,256]{1,0:T(8,128)(2,1)S(1)}, f32[1152,256]{1,0:T(8,128)S(1)}) custom-call(bf16[512,1024]{1,0:T(8,128)(2,1)S(1)} %bitcast.8), custom_call_target="tpu_custom_call" | custom-call | flops 671088640 | bytes 2818048 | tf_op jit(solution)/shard_map/batch/pallas_call | solution.py:352
  3.4 0.0 copy-start
  3.4 2.6 %collective-permute-start = (bf16[576,256]{1,0:T(8,128)(2,1)S(1)}, bf16[576,256]{1,0:T(8,128)(2,1)S(1)}, u32[]{:S(2)}, u32[]{:S(2)}) collective-permute-start(bf16[576,256]{1,0:T(8,128)(2,1)S(1)} %get-tuple-element.23), channel_id=1, source_target_pairs={{0,4},{4,0},{8,12},{12,8},{1,5},{5,1},{9,13},{13,9},{2,6},{6,2},{1... | collective-permute-start | bytes 884744 | tf_op jit(solution)/shard_map/ppermute | solution.py:26
  6.0 1.5 %collective-permute-start.1 = (bf16[576,256]{1,0:T(8,128)(2,1)S(1)}, bf16[576,256]{1,0:T(8,128)(2,1)S(1)}, u32[]{:S(2)}, u32[]{:S(2)}) collective-permute-start(bf16[576,256]{1,0:T(8,128)(2,1)S(1)} %get-tuple-element.24), channel_id=1, source_target_pairs={{0,8},{4,12},{8,0},{12,4},{1,9},{5,13},{9,1},{13,5},{2,10},{6,14},... | collective-permute-start | bytes 884744 | tf_op jit(solution)/shard_map/ppermute | solution.py:26
  7.5 0.0 collective-permute-done.8
  7.5 0.5 %grad.1 = (bf16[512,256]{1,0:T(8,128)(2,1)S(1)}, f32[512,256]{1,0:T(8,128)S(1)}) custom-call(bf16[512,1024]{1,0:T(8,128)(2,1)S(1)} %bitcast.9, bf16[512,256]{1,0:T(8,128)(2,1)S(1)} %bitcast.11), custom_call_target="tpu_custom_call" | custom-call | flops 268435456 | bytes 2097152 | tf_op jit(solution)/shard_map/grad/pallas_call | solution.py:352
  8.1 0.6 %collective-permute-start.9 = (bf16[512,256]{1,0:T(8,128)(2,1)S(1)}, bf16[512,256]{1,0:T(8,128)(2,1)S(1)}, u32[]{:S(2)}, u32[]{:S(2)}) collective-permute-start(bf16[512,256]{1,0:T(8,128)(2,1)S(1)} %get-tuple-element.38), channel_id=1, source_target_pairs={{0,4},{4,0},{8,12},{12,8},{16,24},{20,28},{24,16},{28,20},{1,5},{5... | collective-permute-start | bytes 786440 | tf_op jit(solution)/shard_map/ppermute | solution.py:39
  8.7 5.0 %collective-permute-done.refs_1_ = bf16[576,256]{1,0:T(8,128)(2,1)S(1)} collective-permute-done((bf16[576,256]{1,0:T(8,128)(2,1)S(1)}, bf16[576,256]{1,0:T(8,128)(2,1)S(1)}, u32[]{:S(2)}, u32[]{:S(2)}) %collective-permute-start) | collective-permute-done | bytes 294944 | tf_op jit(solution)/shard_map/ppermute | solution.py:26
  13.7 2.2 %collective-permute-done.1.refs_2_ = bf16[576,256]{1,0:T(8,128)(2,1)S(1)} collective-permute-done((bf16[576,256]{1,0:T(8,128)(2,1)S(1)}, bf16[576,256]{1,0:T(8,128)(2,1)S(1)}, u32[]{:S(2)}, u32[]{:S(2)}) %collective-permute-start.1) | collective-permute-done | bytes 294944 | tf_op jit(solution)/shard_map/ppermute | solution.py:26
  15.9 0.1 relay.1
  15.9 0.1 collective-permute-start.2
  16.0 2.0 %collective-permute-start.3 = (bf16[288,256]{1,0:T(8,128)(2,1)S(1)}, bf16[288,256]{1,0:T(8,128)(2,1)S(1)}, u32[]{:S(2)}, u32[]{:S(2)}) collective-permute-start(bf16[288,256]{1,0:T(8,128)(2,1)S(1)} %get-tuple-element.26), channel_id=1, source_target_pairs={{0,8},{4,12},{8,0},{12,4},{1,9},{5,13},{9,1},{13,5},{2,10},{6,14},... | collective-permute-start | bytes 442376 | tf_op jit(solution)/shard_map/ppermute | solution.py:26
  18.0 3.1 %collective-permute-done.2.refs_3_ = bf16[288,256]{1,0:T(8,128)(2,1)S(1)} collective-permute-done((bf16[288,256]{1,0:T(8,128)(2,1)S(1)}, bf16[288,256]{1,0:T(8,128)(2,1)S(1)}, u32[]{:S(2)}, u32[]{:S(2)}) %collective-permute-start.2) | collective-permute-done | bytes 147488 | tf_op jit(solution)/shard_map/ppermute | solution.py:26
  21.1 0.1 collective-permute-done.3.refs_4_
  21.2 0.0 copy-done
  21.2 0.3 factor.1
  21.5 0.0 copy-start.2
  21.5 2.0 %collective-permute-start.5 = (bf16[592,256]{1,0:T(8,128)(2,1)S(1)}, bf16[592,256]{1,0:T(8,128)(2,1)S(1)}, u32[]{:S(2)}, u32[]{:S(2)}) collective-permute-start(bf16[592,256]{1,0:T(8,128)(2,1)S(1)} %get-tuple-element.28.refs_1_.refs_2_), channel_id=1, source_target_pairs={{0,8},{4,12},{8,0},{12,4},{1,9},{5,13},{9,1},{13,5},{2,10},{6,14},... | collective-permute-start | bytes 909320 | tf_op jit(solution)/shard_map/ppermute | solution.py:26
  23.6 1.5 %collective-permute-start.4 = (bf16[592,256]{1,0:T(8,128)(2,1)S(1)}, bf16[592,256]{1,0:T(8,128)(2,1)S(1)}, u32[]{:S(2)}, u32[]{:S(2)}) collective-permute-start(bf16[592,256]{1,0:T(8,128)(2,1)S(1)} %get-tuple-element.28.refs_1_.refs_2_), channel_id=1, source_target_pairs={{0,4},{4,0},{8,12},{12,8},{1,5},{5,1},{9,13},{13,9},{2,6},{6,2},{1... | collective-permute-start | bytes 909320 | tf_op jit(solution)/shard_map/ppermute | solution.py:26
  25.1 0.0 collective-permute-done.9.refs_1_
  25.1 0.6 %collective-permute-start.10 = (bf16[256,256]{1,0:T(8,128)(2,1)S(1)}, bf16[256,256]{1,0:T(8,128)(2,1)S(1)}, u32[]{:S(2)}, u32[]{:S(2)}) collective-permute-start(bf16[256,256]{1,0:T(8,128)(2,1)S(1)} %strip_relay.1), channel_id=1, source_target_pairs={{0,8},{4,12},{8,0},{12,4},{16,20},{20,16},{24,28},{28,24},{1,9},{5... | collective-permute-start | bytes 393224 | tf_op jit(solution)/shard_map/ppermute | solution.py:39
  25.7 4.6 %collective-permute-done.10.refs_2_ = bf16[256,256]{1,0:T(8,128)(2,1)S(1)} collective-permute-done((bf16[256,256]{1,0:T(8,128)(2,1)S(1)}, bf16[256,256]{1,0:T(8,128)(2,1)S(1)}, u32[]{:S(2)}, u32[]{:S(2)}) %collective-permute-start.10) | collective-permute-done | bytes 131104 | tf_op jit(solution)/shard_map/ppermute | solution.py:39
  30.2 0.1 strip.1.refs_0_
  30.3 1.6 %collective-permute-start.11 = (bf16[256,256]{1,0:T(8,128)(2,1)S(1)}, bf16[256,256]{1,0:T(8,128)(2,1)S(1)}, u32[]{:S(2)}, u32[]{:S(2)}) collective-permute-start(bf16[256,256]{1,0:T(8,128)(2,1)S(1)} %strip.1.refs_0_), channel_id=1, source_target_pairs={{0,8},{4,12},{8,0},{12,4},{16,20},{20,16},{24,28},{28,24},{1,9},{5... | collective-permute-start | bytes 393224 | tf_op jit(solution)/shard_map/ppermute | solution.py:39
  31.9 0.0 collective-permute-done.5.refs_1_.refs_3_
  31.9 0.0 collective-permute-done.4.refs_0_.refs_2_
  31.9 1.6 %collective-permute-start.7 = (bf16[304,256]{1,0:T(8,128)(2,1)S(1)}, bf16[304,256]{1,0:T(8,128)(2,1)S(1)}, u32[]{:S(2)}, u32[]{:S(2)}) collective-permute-start(bf16[304,256]{1,0:T(8,128)(2,1)S(1)} %get-tuple-element.29.refs_5_), channel_id=1, source_target_pairs={{0,4},{4,0},{8,12},{12,8},{1,5},{5,1},{9,13},{13,9},{2,6},{6,2},{1... | collective-permute-start | bytes 466952 | tf_op jit(solution)/shard_map/ppermute | solution.py:26
  33.5 0.5 %collective-permute-start.6 = (bf16[288,256]{1,0:T(8,128)(2,1)S(1)}, bf16[288,256]{1,0:T(8,128)(2,1)S(1)}, u32[]{:S(2)}, u32[]{:S(2)}) collective-permute-start(bf16[288,256]{1,0:T(8,128)(2,1)S(1)} %get-tuple-element.34), channel_id=1, source_target_pairs={{0,8},{4,12},{8,0},{12,4},{1,9},{5,13},{9,1},{13,5},{2,10},{6,14},... | collective-permute-start | bytes 442376 | tf_op jit(solution)/shard_map/ppermute | solution.py:26
  34.0 0.0 copy-done.2
  34.0 0.9 %matrix.1 = (bf16[1024,1024]{1,0:T(8,128)(2,1)S(1)}, f32[1,1024]{1,0:T(1,128)S(1)}, f32[16,256]{1,0:T(8,128)S(1)}, f32[256,1024]{1,0:T(8,128)S(1)}, bf16[1024,256]{1,0:T(8,128)(2,1)S(1)}) custom-call(f32[576,256]{1,0:T(8,128)S(1)} %get-tuple-element.27.refs_0_.refs_5_, bf16[592,256]{1,0:T(8,128)(2,1)S(1)} %get-tuple-element.28.refs_1_.refs_2_, ...), custom_call_target="tpu_custom_call" | custom-call | bytes 5713920 | tf_op jit(solution)/shard_map/matrix/pallas_call | solution.py:352
  34.9 1.8 %collective-permute-done.11.refs_1_ = bf16[256,256]{1,0:T(8,128)(2,1)S(1)} collective-permute-done((bf16[256,256]{1,0:T(8,128)(2,1)S(1)}, bf16[256,256]{1,0:T(8,128)(2,1)S(1)}, u32[]{:S(2)}, u32[]{:S(2)}) %collective-permute-start.11) | collective-permute-done | bytes 131104 | tf_op jit(solution)/shard_map/ppermute | solution.py:39
  36.8 1.5 %collective-permute-start.12 = (bf16[512,256]{1,0:T(8,128)(2,1)S(1)}, bf16[512,256]{1,0:T(8,128)(2,1)S(1)}, u32[]{:S(2)}, u32[]{:S(2)}) collective-permute-start(bf16[512,256]{1,0:T(8,128)(2,1)S(1)} %pair.1.refs_0_), channel_id=1, source_target_pairs={{0,4},{4,0},{8,12},{12,8},{16,24},{20,28},{24,16},{28,20},{1,5},{5... | collective-permute-start | bytes 786440 | tf_op jit(solution)/shard_map/ppermute | solution.py:39
  39.0 1.3 %collective-permute-done.6.refs_6_ = bf16[288,256]{1,0:T(8,128)(2,1)S(1)} collective-permute-done((bf16[288,256]{1,0:T(8,128)(2,1)S(1)}, bf16[288,256]{1,0:T(8,128)(2,1)S(1)}, u32[]{:S(2)}, u32[]{:S(2)}) %collective-permute-start.6) | collective-permute-done | bytes 147488 | tf_op jit(solution)/shard_map/ppermute | solution.py:26
  40.3 0.0 collective-permute-done.7.refs_7_
  40.3 3.6 %root.1 = (f32[256,1024]{1,0:T(8,128)}, bf16[256,1024]{1,0:T(8,128)(2,1)}, f32[8,128]{1,0:T(8,128)S(1)}) custom-call(s32[1,1]{1,0:T(1,128)S(6)} %copy.8.refs_0_, bf16[1024,1024]{1,0:T(8,128)(2,1)S(1)} %get-tuple-element.30.refs_1_, f32[1,1024]{1,0:T(1,128)S(1)} %get-tuple-element.31.refs_2_, f32[16,256]{1,0:T(8,128)S(1)} %get-tuple-element.32.refs_3_, ...), custom_call_target="tpu_custom_call" | custom-call | flops 1610612736 | bytes 5636100 | tf_op jit(solution)/shard_map/root/pallas_call | solution.py:352
  43.9 0.0 collective-permute-done.12.refs_1_
  43.9 1.0 %step.1 = bf16[256,256]{1,0:T(8,128)(2,1)} custom-call(bf16[512,256]{1,0:T(8,128)(2,1)S(1)} %pair.1.refs_0_, bf16[512,256]{1,0:T(8,128)(2,1)S(1)} %collective-permute-done.12.refs_1_, bf16[1024,256]{1,0:T(8,128)(2,1)S(1)} %get-tuple-element.39.refs_2_, f32[8,128]{1,0:T(8,128)S(1)} %get-tuple-element.40.refs_3_), custom_call_target="tpu_custom_call" | custom-call | flops 134217728 | bytes 1179648 | tf_op jit(solution)/shard_map/step/pallas_call | solution.py:352
  (3 shorter events, 0.1 us)
Async XLA Ops:
  0.6 6.9 %collective-permute-start.8 = (bf16[1,512,256]{2,1,0:T(8,128)(2,1)}, bf16[1,512,256]{2,1,0:T(8,128)(2,1)S(1)}, u32[]{:S(2)}, u32[]{:S(2)}) collective-permute-start(bf16[1,512,256]{2,1,0:T(8,128)(2,1)} %param.6), channel_id=1, source_target_pairs={{16,0},{0,16},{17,1},{1,17},{18,2},{2,18},{19,3},{3,19},{20,4},{4,... | collective-permute-start | bytes 786440 | tf_op jit(solution)/shard_map/ppermute | solution.py:22
  1.1 1.2 %copy-start.1 = (bf16[1,512,1024]{2,1,0:T(8,128)(2,1)S(1)}, bf16[1,512,1024]{2,1,0:T(8,128)(2,1)}, u32[]{:S(2)}) copy-start(bf16[1,512,1024]{2,1,0:T(8,128)(2,1)} %param.5) | copy-start | bytes 3145732
  3.4 17.8 %copy-start = (f32[1,1,256,1024]{3,2,1,0:T(8,128)S(1)}, f32[1,1,256,1024]{3,2,1,0:T(8,128)}, u32[]{:S(2)}) copy-start(f32[1,1,256,1024]{3,2,1,0:T(8,128)} %param.7) | copy-start | bytes 3145732
  3.4 10.2 %collective-permute-start = (bf16[576,256]{1,0:T(8,128)(2,1)S(1)}, bf16[576,256]{1,0:T(8,128)(2,1)S(1)}, u32[]{:S(2)}, u32[]{:S(2)}) collective-permute-start(bf16[576,256]{1,0:T(8,128)(2,1)S(1)} %get-tuple-element.23), channel_id=1, source_target_pairs={{0,4},{4,0},{8,12},{12,8},{1,5},{5,1},{9,13},{13,9},{2,6},{6,2},{1... | collective-permute-start | bytes 884744 | tf_op jit(solution)/shard_map/ppermute | solution.py:26
  6.0 9.8 %collective-permute-start.1 = (bf16[576,256]{1,0:T(8,128)(2,1)S(1)}, bf16[576,256]{1,0:T(8,128)(2,1)S(1)}, u32[]{:S(2)}, u32[]{:S(2)}) collective-permute-start(bf16[576,256]{1,0:T(8,128)(2,1)S(1)} %get-tuple-element.24), channel_id=1, source_target_pairs={{0,8},{4,12},{8,0},{12,4},{1,9},{5,13},{9,1},{13,5},{2,10},{6,14},... | collective-permute-start | bytes 884744 | tf_op jit(solution)/shard_map/ppermute | solution.py:26
  8.1 17.0 %collective-permute-start.9 = (bf16[512,256]{1,0:T(8,128)(2,1)S(1)}, bf16[512,256]{1,0:T(8,128)(2,1)S(1)}, u32[]{:S(2)}, u32[]{:S(2)}) collective-permute-start(bf16[512,256]{1,0:T(8,128)(2,1)S(1)} %get-tuple-element.38), channel_id=1, source_target_pairs={{0,4},{4,0},{8,12},{12,8},{16,24},{20,28},{24,16},{28,20},{1,5},{5... | collective-permute-start | bytes 786440 | tf_op jit(solution)/shard_map/ppermute | solution.py:39
  15.9 5.2 %collective-permute-start.2 = (bf16[288,256]{1,0:T(8,128)(2,1)S(1)}, bf16[288,256]{1,0:T(8,128)(2,1)S(1)}, u32[]{:S(2)}, u32[]{:S(2)}) collective-permute-start(bf16[288,256]{1,0:T(8,128)(2,1)S(1)} %get-tuple-element.25), channel_id=1, source_target_pairs={{0,4},{4,0},{8,12},{12,8},{1,5},{5,1},{9,13},{13,9},{2,6},{6,2},{1... | collective-permute-start | bytes 442376 | tf_op jit(solution)/shard_map/ppermute | solution.py:26
  16.0 5.2 %collective-permute-start.3 = (bf16[288,256]{1,0:T(8,128)(2,1)S(1)}, bf16[288,256]{1,0:T(8,128)(2,1)S(1)}, u32[]{:S(2)}, u32[]{:S(2)}) collective-permute-start(bf16[288,256]{1,0:T(8,128)(2,1)S(1)} %get-tuple-element.26), channel_id=1, source_target_pairs={{0,8},{4,12},{8,0},{12,4},{1,9},{5,13},{9,1},{13,5},{2,10},{6,14},... | collective-permute-start | bytes 442376 | tf_op jit(solution)/shard_map/ppermute | solution.py:26
  21.5 12.5 %copy-start.2 = (bf16[1,1,256,1024]{3,2,1,0:T(8,128)(2,1)S(1)}, bf16[1,1,256,1024]{3,2,1,0:T(8,128)(2,1)}, u32[]{:S(2)}) copy-start(bf16[1,1,256,1024]{3,2,1,0:T(8,128)(2,1)} %param.8) | copy-start | bytes 1572868
  21.5 10.4 %collective-permute-start.5 = (bf16[592,256]{1,0:T(8,128)(2,1)S(1)}, bf16[592,256]{1,0:T(8,128)(2,1)S(1)}, u32[]{:S(2)}, u32[]{:S(2)}) collective-permute-start(bf16[592,256]{1,0:T(8,128)(2,1)S(1)} %get-tuple-element.28.refs_1_.refs_2_), channel_id=1, source_target_pairs={{0,8},{4,12},{8,0},{12,4},{1,9},{5,13},{9,1},{13,5},{2,10},{6,14},... | collective-permute-start | bytes 909320 | tf_op jit(solution)/shard_map/ppermute | solution.py:26
  23.6 8.4 %collective-permute-start.4 = (bf16[592,256]{1,0:T(8,128)(2,1)S(1)}, bf16[592,256]{1,0:T(8,128)(2,1)S(1)}, u32[]{:S(2)}, u32[]{:S(2)}) collective-permute-start(bf16[592,256]{1,0:T(8,128)(2,1)S(1)} %get-tuple-element.28.refs_1_.refs_2_), channel_id=1, source_target_pairs={{0,4},{4,0},{8,12},{12,8},{1,5},{5,1},{9,13},{13,9},{2,6},{6,2},{1... | collective-permute-start | bytes 909320 | tf_op jit(solution)/shard_map/ppermute | solution.py:26
  25.1 5.1 %collective-permute-start.10 = (bf16[256,256]{1,0:T(8,128)(2,1)S(1)}, bf16[256,256]{1,0:T(8,128)(2,1)S(1)}, u32[]{:S(2)}, u32[]{:S(2)}) collective-permute-start(bf16[256,256]{1,0:T(8,128)(2,1)S(1)} %strip_relay.1), channel_id=1, source_target_pairs={{0,8},{4,12},{8,0},{12,4},{16,20},{20,16},{24,28},{28,24},{1,9},{5... | collective-permute-start | bytes 393224 | tf_op jit(solution)/shard_map/ppermute | solution.py:39
  30.3 6.4 %collective-permute-start.11 = (bf16[256,256]{1,0:T(8,128)(2,1)S(1)}, bf16[256,256]{1,0:T(8,128)(2,1)S(1)}, u32[]{:S(2)}, u32[]{:S(2)}) collective-permute-start(bf16[256,256]{1,0:T(8,128)(2,1)S(1)} %strip.1.refs_0_), channel_id=1, source_target_pairs={{0,8},{4,12},{8,0},{12,4},{16,20},{20,16},{24,28},{28,24},{1,9},{5... | collective-permute-start | bytes 393224 | tf_op jit(solution)/shard_map/ppermute | solution.py:39
  31.9 8.3 %collective-permute-start.7 = (bf16[304,256]{1,0:T(8,128)(2,1)S(1)}, bf16[304,256]{1,0:T(8,128)(2,1)S(1)}, u32[]{:S(2)}, u32[]{:S(2)}) collective-permute-start(bf16[304,256]{1,0:T(8,128)(2,1)S(1)} %get-tuple-element.29.refs_5_), channel_id=1, source_target_pairs={{0,4},{4,0},{8,12},{12,8},{1,5},{5,1},{9,13},{13,9},{2,6},{6,2},{1... | collective-permute-start | bytes 466952 | tf_op jit(solution)/shard_map/ppermute | solution.py:26
  33.5 6.8 %collective-permute-start.6 = (bf16[288,256]{1,0:T(8,128)(2,1)S(1)}, bf16[288,256]{1,0:T(8,128)(2,1)S(1)}, u32[]{:S(2)}, u32[]{:S(2)}) collective-permute-start(bf16[288,256]{1,0:T(8,128)(2,1)S(1)} %get-tuple-element.34), channel_id=1, source_target_pairs={{0,8},{4,12},{8,0},{12,4},{1,9},{5,13},{9,1},{13,5},{2,10},{6,14},... | collective-permute-start | bytes 442376 | tf_op jit(solution)/shard_map/ppermute | solution.py:26
  36.8 7.1 %collective-permute-start.12 = (bf16[512,256]{1,0:T(8,128)(2,1)S(1)}, bf16[512,256]{1,0:T(8,128)(2,1)S(1)}, u32[]{:S(2)}, u32[]{:S(2)}) collective-permute-start(bf16[512,256]{1,0:T(8,128)(2,1)S(1)} %pair.1.refs_0_), channel_id=1, source_target_pairs={{0,4},{4,0},{8,12},{12,8},{16,24},{20,28},{24,16},{28,20},{1,5},{5... | collective-permute-start | bytes 786440 | tf_op jit(solution)/shard_map/ppermute | solution.py:39

commit v8 on v7

--- a/solution.py
+++ b/solution.py
@@ -92,12 +92,12 @@
                 ref[at + first - low : at + last - low, :] = piece[first - start : last - start].astype(ref.dtype)
 
 
-def batch_kernel(replicas, tokens_all, acts, send_x, send_y, keep, batch):
+def batch_kernel(replicas, tokens_all, acts, relay_x, relay_y, direct_x, direct_y, keep, batch):
     order = acts.shape[1]
     share = order // replicas
     half = share // 2
     starts = chunk_starts(share)
-    length = send_x.shape[0] // 2
+    length = relay_x.shape[0]
     mine = lax.axis_index("dp")
     for i in range(replicas):
         rows = slice(i * share, (i + 1) * share)
@@ -114,16 +114,16 @@
             row, col = shared_half(owner, step, share)
             yield starts[1 + step], batch[pl.ds(row, half), pl.ds(col, share)]
 
-    store_chunk(pieces(3), length, (send_x, 0), (send_y, 0))
-    store_chunk(pieces(1), length, (send_x, length), (keep, 3 * length))
-    store_chunk(pieces(2), length, (keep, 2 * length), (send_y, length))
+    store_chunk(pieces(3), length, (relay_x, 0), (relay_y, 0))
+    store_chunk(pieces(1), length, (direct_x, 0), (keep, 3 * length))
+    store_chunk(pieces(2), length, (keep, 2 * length), (direct_y, 0))
     store_chunk(pieces(0), length, (keep, 0), (keep, length))
 
 
 def relay_kernel(keep, got_x, got_y, send_x, send_y):
     length = send_x.shape[0]
-    send_y[...] = (keep[2 * length : 3 * length, :] + got_x[0:length, :].astype(F32)).astype(BF16)
-    send_x[...] = (keep[3 * length :, :] + got_y[0:length, :].astype(F32)).astype(BF16)
+    send_y[...] = (keep[2 * length : 3 * length, :] + got_x[...].astype(F32)).astype(BF16)
+    send_x[...] = (keep[3 * length :, :] + got_y[...].astype(F32)).astype(BF16)
 
 
 def grad_kernel(replicas, tokens_all, acts, grads, send, keep, total):
@@ -141,6 +141,10 @@
                 ref[start : start + strip, :] = piece.astype(ref.dtype)
 
 
+def copy_kernel(source, target):
+    target[...] = source[...]
+
+
 def strip_relay_kernel(keep, got, send):
     length = send.shape[0]
     send[...] = (keep[length:, :] + got[length:, :].astype(F32)).astype(BF16)
@@ -157,14 +161,14 @@
     send[length:, :] = got[...]
 
 
-def factor_kernel(keep, got_x, got_y, relay_x, relay_y, old, chunk, exact):
+def factor_kernel(keep, direct_x, direct_y, relay_x, relay_y, old, chunk_upper, chunk_lower, exact):
     share = old.shape[0]
     half = share // 2
     starts = chunk_starts(share)
     length = relay_x.shape[0]
     mine = lax.axis_index("dp")
-    upper = keep[0:length, :] + got_x[length:, :].astype(F32) + relay_y[...].astype(F32)
-    lower = keep[length : 2 * length, :] + got_y[length:, :].astype(F32) + relay_x[...].astype(F32)
+    upper = keep[0:length, :] + direct_x[...].astype(F32) + relay_y[...].astype(F32)
+    lower = keep[length : 2 * length, :] + direct_y[...].astype(F32) + relay_x[...].astype(F32)
     total = jnp.concatenate([upper, lower], axis=0)
     diagonal = old[:, band(mine, share)]
     terms = [
@@ -181,20 +185,15 @@
         rows = slice(start, start + term.shape[0])
         value = term + (1.0 - DECAY) * total[rows]
         exact[rows, :] = value
-        chunk[rows, :] = value.astype(BF16)
         sums = sums + weight * jnp.sum(value * value, axis=0, keepdims=True)
     high = sums.astype(BF16).astype(F32)
     middle = (sums - high).astype(BF16).astype(F32)
     rest = sums - high - middle
-    spot = lax.broadcasted_iota(jnp.int32, (chunk.shape[0] - 2 * length, share), 0)
+    spot = lax.broadcasted_iota(jnp.int32, (chunk_lower.shape[0] - length, share), 0)
     digits = jnp.where(spot == 0, high, jnp.where(spot == 1, middle, jnp.where(spot == 2, rest, 0.0)))
-    chunk[2 * length :, :] = digits.astype(BF16)
-
-
-def halves_kernel(got_x, got_y, send_x, send_y):
-    length = send_y.shape[0]
-    send_y[...] = got_x[0:length, :]
-    send_x[...] = got_y[length:, :]
+    chunk_upper[...] = exact[0:length, :].astype(BF16)
+    chunk_lower[0:length, :] = exact[length:, :].astype(BF16)
+    chunk_lower[length:, :] = digits.astype(BF16)
 
 
 def place(factor, diagonal, owner, read, share):
@@ -217,10 +216,8 @@
         factor[pl.ds(col, share), pl.ds(row, half)] = transposed(block)
 
 
-def rows_of(upper, lower=None):
+def rows_of(upper, lower):
     def read(start, count):
-        if lower is None:
-            return upper[start : start + count, :]
         length = upper.shape[0]
         if start + count <= length:
             return upper[start : start + count, :]
@@ -244,26 +241,32 @@
         target[:, columns] = jnp.concatenate([theirs.T, own.T], axis=1)
 
 
-def matrix_kernel(exact, chunk, near, side, old_root, factor, diagonal, squares, rows, old_columns):
+def matrix_kernel(
+    exact, own_upper, own_lower, near_upper, near_lower, side_upper, side_lower, old_root, factor, diagonal, squares, rows,
+    old_columns,
+):
     share = exact.shape[1]
     half = share // 2
     starts = chunk_starts(share)
     mine = lax.axis_index("dp")
     factor[...] = jnp.zeros_like(factor)
     diagonal[...] = jnp.zeros_like(diagonal)
-    sums = jnp.zeros((chunk.shape[0] - starts[-1], share), F32)
-    for offset, ref in enumerate((chunk, near, side)):
-        place(factor, diagonal, mine ^ offset, rows_of(ref), share)
-        sums = sums + ref[starts[-1] :, :].astype(F32)
+    count = squares.shape[0]
+    reads = [rows_of(own_upper, own_lower), rows_of(near_upper, near_lower), rows_of(side_upper, side_lower)]
+    sums = jnp.zeros((count, share), F32)
+    for offset, read in enumerate(reads):
+        place(factor, diagonal, mine ^ offset, read, share)
+        sums = sums + read(starts[-1], count).astype(F32)
     squares[...] = sums
     top = exact[0:half, :]
     low = stacked(exact[starts[1] : starts[2], :])
     rows[0:half, band(mine, share)] = top
     rows[half:, band(mine, share)] = jnp.concatenate([top[:, half:].T, low], axis=1)
-    for offset, ref in ((1, near), (2, side)):
-        part = slice(starts[1 + offset], starts[1 + offset] + half)
+    for offset in (1, 2):
+        start = starts[1 + offset]
         other = mine ^ offset
-        store_shared(rows, band(other, share), mine < other, exact[part, :], ref[part, :].astype(F32))
+        theirs = reads[offset](start, half).astype(F32)
+        store_shared(rows, band(other, share), mine < other, exact[start : start + half, :], theirs)
     rows[:, band(mine ^ 3, share)] = jnp.zeros((share, share), F32)
     old_columns[...] = transposed(old_root[...])
 
@@ -360,7 +363,9 @@
                 flops=flops,
                 bytes_accessed=sum(x.size * x.dtype.itemsize for x in (*operands, *outs)),
                 transcendentals=0,
-            ),
+            )
+            if flops
+            else None,
             name=name,
         )(*operands, *after)
 
@@ -368,16 +373,16 @@
         return swapped(x, 1), swapped(y, 2)
 
     received = passed_along(out_grad, "pipe", -1)[0]
-    send_x, send_y, keep = call(
+    relay_x, relay_y, direct_x, direct_y, keep = call(
         functools.partial(batch_kernel, replicas, tokens * replicas),
-        [shape(length)] * 2 + [shape(2 * length, F32)],
+        [shape(length // 2)] * 4 + [shape(2 * length, F32)],
         "batch",
         inputs,
-        flops=5 * tokens * order * order // 4,
         scratch=[pltpu.VMEM((order, order), F32)],
     )
-    got_x, got_y = both(send_x, send_y)
-    on_x, on_y = call(relay_kernel, [shape(length // 2)] * 2, "relay", keep, got_x, got_y)
+    relay_x, relay_y = both(relay_x, relay_y)
+    direct_x, direct_y = both(direct_x, direct_y)
+    on_x, on_y = call(relay_kernel, [shape(length // 2)] * 2, "relay", keep, relay_x, relay_y)
     relay_x, relay_y = both(on_x, on_y)
     strips, strips_keep = call(
         functools.partial(grad_kernel, replicas, tokens * replicas),
@@ -385,40 +390,43 @@
         "grad",
         inputs,
         received,
-        flops=2 * tokens * order * grows,
         scratch=[pltpu.VMEM((grows, order), F32)],
     )
-    strips_got = swapped_along(strips, 0)
-    chunk, exact = call(
+    (strips_now,) = call(copy_kernel, [shape(2 * grows)], "release", strips, after=[relay_x, relay_y, direct_x, direct_y])
+    strips_got = swapped_along(strips_now, 0)
+    upper, lower, exact = call(
         factor_kernel,
-        [shape(length + digits), shape(length, F32)],
+        [shape(length // 2), shape(length // 2 + digits), shape(length, F32)],
         "factor",
         keep,
-        got_x,
-        got_y,
+        direct_x,
+        direct_y,
         relay_x,
         relay_y,
         old_factor[0, 0],
     )
-    near, side = both(chunk, chunk)
-    (strip_on,) = call(strip_relay_kernel, [shape(grows)], "strip_relay", strips_keep, strips_got, after=[chunk])
+    near_upper, side_lower = both(upper, lower)
+    near_lower, side_upper = both(lower, upper)
+    far_lower, far_upper = both(side_lower, near_upper)
+    (strip_on,) = call(strip_relay_kernel, [shape(grows)], "strip_relay", strips_keep, strips_got, after=[upper])
     strip_relayed = swapped_along(strip_on, 1)
     (strip,) = call(strip_kernel, [shape(grows)], "strip", strips_keep, strips_got, strip_relayed)
     strip_near = swapped_along(strip, 1)
-    on_x, on_y = call(halves_kernel, [shape(length // 2 + digits), shape(length // 2)], "halves", near, side)
-    lower, upper = both(on_x, on_y)
     known, diagonal, squares, rows, old_columns = call(
         matrix_kernel,
         [shape(order, BF16, order), shape(1, F32, order), shape(digits, F32), shape(share, F32, order), shape(order)],
         "matrix",
         exact,
-        chunk,
-        near,
-        side,
+        upper,
+        lower,
+        near_upper,
+        near_lower,
+        side_upper,
+        side_lower,
         old_root[0, 0],
-        after=[on_x],
-    )
-    (pair,) = call(pair_kernel, [shape(2 * grows)], "pair", strip, strip_near, after=[diagonal])
+        flops=order * order,
+    )
+    (pair,) = call(pair_kernel, [shape(2 * grows)], "pair", strip, strip_near, after=[diagonal, far_lower, far_upper])
     pair_far = swapped_along(pair, 0)
     factor, root, finished = call(
         root_kernel,
@@ -430,8 +438,8 @@
         squares,
         rows,
         exact,
-        upper,
-        lower,
+        far_upper,
+        far_lower,
         flops=6 * share * order * order,
         scalar=True,
         first_out=pl.ANY,
@@ -449,7 +457,6 @@
         pair,
         pair_far,
         old_columns,
-        flops=2 * grows * order * share,
         after=[finished],
         scratch=[pltpu.VMEM((grows, order), BF16), pltpu.VMEM((grows, share), BF16)],
     )

time: 45 us -> 47.7 us (1.060)
  starting transfers between devices: 16.6 us -> 22.3 us
  waiting for transfers between devices: 18.1 us -> 15.2 us
    ppermute x4, starting transfers between devices: 4.31 us -> 7.44 us  [swapped_along(): return lax.ppermute(block, ('pipe', 'dp'), route)]
    ppermute x8 -> x12, starting transfers between devices: 11.8 us -> 14.9 us  [swapped(): lax.ppermute(block, 'dp', [(i, i ^ offset) for i in range(lax.axis_size('...]
    ppermute x8 -> x12, waiting for transfers between devices: 11.7 us -> 9.57 us  [swapped(): lax.ppermute(block, 'dp', [(i, i ^ offset) for i in range(lax.axis_size('...]
    ppermute x4, waiting for transfers between devices: 6.41 us -> 5.59 us  [swapped_along(): return lax.ppermute(block, ('pipe', 'dp'), route)]
    ppermute x1, starting transfers between devices: 0.52 us -> 0.01 us  [passed_along(): return lax.ppermute(block, axis, route)]
  transfers between devices with their start and end apart: 13 -> 17, of which waited for: 7 -> 9; matrix products, arithmetic and copies ran while one was open for 0% -> 0% of each run, Pallas kernels for 14% -> 11%
where the time goes in v8:
time: 47.7 us; the launch traced here: 47.5 us
  starting transfers between devices  22.3 us (47%)
  waiting for transfers between devices  15.2 us (32%)
  Pallas kernels  7.47 us (16%)
  between operations  1.38 us (3%)
  local copies, waits for them, and re-layouts  1.23 us (3%)
    ppermute x12, starting transfers between devices, swapped(): lax.ppermute(block, 'dp', [(i, i ^ offset) for i in range(lax.axis_size('...  14.9 us
    ppermute x12, waiting for transfers between devices, swapped(): lax.ppermute(block, 'dp', [(i, i ^ offset) for i in range(lax.axis_size('...  9.57 us
    pallas_call x11, Pallas kernels, call(): pl.pallas_call(body, out_shape=outs, in_specs=in_specs, out_specs=out_spe...  7.47 us
    ppermute x4, starting transfers between devices, swapped_along(): return lax.ppermute(block, ('pipe', 'dp'), route)  7.44 us
    ppermute x4, waiting for transfers between devices, swapped_along(): return lax.ppermute(block, ('pipe', 'dp'), route)  5.59 us
    unnamed x6, local copies, waits for them, and re-layouts  1.23 us
  transfers between devices with their start and end apart: 17, of which 9 were waited for; matrix products, arithmetic and copies ran while one was open for 0% of the time, Pallas kernels for 11%

profile of v8, /device:TPU:0, one launch (start us, length us, event | category | flops | bytes accessed | tf_op | source)
XLA Modules:
  0.0 47.5 jit_solution(894257612319625349)
XLA Ops:
  0.6 0.0 copy-start
  0.6 1.2 %copy-done = bf16[1,512,1024]{2,1,0:T(8,128)(2,1)S(1)} copy-done((bf16[1,512,1024]{2,1,0:T(8,128)(2,1)S(1)}, bf16[1,512,1024]{2,1,0:T(8,128)(2,1)}, u32[]{:S(2)}) %copy-start) | copy-done | bytes 1048600
  1.9 1.1 %batch.1 = (bf16[288,256]{1,0:T(8,128)(2,1)S(1)}, bf16[288,256]{1,0:T(8,128)(2,1)S(1)}, bf16[288,256]{1,0:T(8,128)(2,1)S(1)}, bf16[288,256]{1,0:T(8,128)(2,1)S(1)}, f32[1152,256]{1,0:T(8,128)S(1)}) custom-call(bf16[512,1024]{1,0:T(8,128)(2,1)S(1)} %bitcast.7), custom_call_target="tpu_custom_call" | custom-call | tf_op jit(solution)/shard_map/batch/pallas_call | solution.py:355
  2.9 0.0 copy-start.1
  2.9 3.0 %collective-permute-start.2 = (bf16[288,256]{1,0:T(8,128)(2,1)S(1)}, bf16[288,256]{1,0:T(8,128)(2,1)S(1)}, u32[]{:S(2)}, u32[]{:S(2)}) collective-permute-start(bf16[288,256]{1,0:T(8,128)(2,1)S(1)} %get-tuple-element.26), channel_id=1, source_target_pairs={{0,4},{4,0},{8,12},{12,8},{1,5},{5,1},{9,13},{13,9},{2,6},{6,2},{1... | collective-permute-start | bytes 442376 | tf_op jit(solution)/shard_map/ppermute | solution.py:26
  5.9 1.5 %collective-permute-start.3 = (bf16[288,256]{1,0:T(8,128)(2,1)S(1)}, bf16[288,256]{1,0:T(8,128)(2,1)S(1)}, u32[]{:S(2)}, u32[]{:S(2)}) collective-permute-start(bf16[288,256]{1,0:T(8,128)(2,1)S(1)} %get-tuple-element.27), channel_id=1, source_target_pairs={{0,8},{4,12},{8,0},{12,4},{1,9},{5,13},{9,1},{13,5},{2,10},{6,14},... | collective-permute-start | bytes 442376 | tf_op jit(solution)/shard_map/ppermute | solution.py:26
  7.5 0.0 collective-permute-start.12
  7.5 0.5 %collective-permute-start = (bf16[288,256]{1,0:T(8,128)(2,1)S(1)}, bf16[288,256]{1,0:T(8,128)(2,1)S(1)}, u32[]{:S(2)}, u32[]{:S(2)}) collective-permute-start(bf16[288,256]{1,0:T(8,128)(2,1)S(1)} %get-tuple-element.24), channel_id=1, source_target_pairs={{0,4},{4,0},{8,12},{12,8},{1,5},{5,1},{9,13},{13,9},{2,6},{6,2},{1... | collective-permute-start | bytes 442376 | tf_op jit(solution)/shard_map/ppermute | solution.py:26
  8.0 0.1 collective-permute-start.1
  8.1 1.7 %collective-permute-done.2.refs_1_ = bf16[288,256]{1,0:T(8,128)(2,1)S(1)} collective-permute-done((bf16[288,256]{1,0:T(8,128)(2,1)S(1)}, bf16[288,256]{1,0:T(8,128)(2,1)S(1)}, u32[]{:S(2)}, u32[]{:S(2)}) %collective-permute-start.2) | collective-permute-done | bytes 147488 | tf_op jit(solution)/shard_map/ppermute | solution.py:26
  9.8 2.0 %collective-permute-done.3.refs_2_ = bf16[288,256]{1,0:T(8,128)(2,1)S(1)} collective-permute-done((bf16[288,256]{1,0:T(8,128)(2,1)S(1)}, bf16[288,256]{1,0:T(8,128)(2,1)S(1)}, u32[]{:S(2)}, u32[]{:S(2)}) %collective-permute-start.3) | collective-permute-done | bytes 147488 | tf_op jit(solution)/shard_map/ppermute | solution.py:26
  11.8 0.1 relay.1
  11.8 0.2 collective-permute-start.4
  12.0 2.4 %collective-permute-start.5 = (bf16[288,256]{1,0:T(8,128)(2,1)S(1)}, bf16[288,256]{1,0:T(8,128)(2,1)S(1)}, u32[]{:S(2)}, u32[]{:S(2)}) collective-permute-start(bf16[288,256]{1,0:T(8,128)(2,1)S(1)} %get-tuple-element.29), channel_id=1, source_target_pairs={{0,8},{4,12},{8,0},{12,4},{1,9},{5,13},{9,1},{13,5},{2,10},{6,14},... | collective-permute-start | bytes 442376 | tf_op jit(solution)/shard_map/ppermute | solution.py:26
  14.4 0.0 collective-permute-done.12
  14.4 0.5 %grad.1 = (bf16[512,256]{1,0:T(8,128)(2,1)S(1)}, f32[512,256]{1,0:T(8,128)S(1)}) custom-call(bf16[512,1024]{1,0:T(8,128)(2,1)S(1)} %bitcast.8, bf16[512,256]{1,0:T(8,128)(2,1)S(1)} %bitcast.11), custom_call_target="tpu_custom_call" | custom-call | tf_op jit(solution)/shard_map/grad/pallas_call | solution.py:355
  15.0 0.0 collective-permute-done.refs_1_.refs_3_
  15.0 0.0 collective-permute-done.1.refs_2_.refs_4_
  15.0 2.0 %collective-permute-done.4.refs_3_.refs_1_ = bf16[288,256]{1,0:T(8,128)(2,1)S(1)} collective-permute-done((bf16[288,256]{1,0:T(8,128)(2,1)S(1)}, bf16[288,256]{1,0:T(8,128)(2,1)S(1)}, u32[]{:S(2)}, u32[]{:S(2)}) %collective-permute-start.4) | collective-permute-done | bytes 147488 | tf_op jit(solution)/shard_map/ppermute | solution.py:26
  17.0 0.6 %collective-permute-done.5.refs_4_.refs_2_ = bf16[288,256]{1,0:T(8,128)(2,1)S(1)} collective-permute-done((bf16[288,256]{1,0:T(8,128)(2,1)S(1)}, bf16[288,256]{1,0:T(8,128)(2,1)S(1)}, u32[]{:S(2)}, u32[]{:S(2)}) %collective-permute-start.5) | collective-permute-done | bytes 147488 | tf_op jit(solution)/shard_map/ppermute | solution.py:26
  17.6 2.3 %collective-permute-start.13 = (bf16[512,256]{1,0:T(8,128)(2,1)S(1)}, bf16[512,256]{1,0:T(8,128)(2,1)S(1)}, u32[]{:S(2)}, u32[]{:S(2)}) collective-permute-start(bf16[512,256]{1,0:T(8,128)(2,1)S(1)} %release.1), channel_id=1, source_target_pairs={{0,4},{4,0},{8,12},{12,8},{16,24},{20,28},{24,16},{28,20},{1,5},{5... | collective-permute-start | bytes 786440 | tf_op jit(solution)/shard_map/ppermute | solution.py:39
  19.9 0.0 copy-done.1
  19.9 0.0 copy-start.2
  19.9 0.3 factor.1
  20.2 2.5 %collective-permute-start.9 = (bf16[304,256]{1,0:T(8,128)(2,1)S(1)}, bf16[304,256]{1,0:T(8,128)(2,1)S(1)}, u32[]{:S(2)}, u32[]{:S(2)}) collective-permute-start(bf16[304,256]{1,0:T(8,128)(2,1)S(1)} %get-tuple-element.32.refs_2_), channel_id=1, source_target_pairs={{0,8},{4,12},{8,0},{12,4},{1,9},{5,13},{9,1},{13,5},{2,10},{6,14},... | collective-permute-start | bytes 466952 | tf_op jit(solution)/shard_map/ppermute | solution.py:26
  22.7 0.0 collective-permute-start.6
  22.7 2.8 %collective-permute-done.13.refs_1_ = bf16[512,256]{1,0:T(8,128)(2,1)S(1)} collective-permute-done((bf16[512,256]{1,0:T(8,128)(2,1)S(1)}, bf16[512,256]{1,0:T(8,128)(2,1)S(1)}, u32[]{:S(2)}, u32[]{:S(2)}) %collective-permute-start.13) | collective-permute-done | bytes 262176 | tf_op jit(solution)/shard_map/ppermute | solution.py:39
  25.6 2.6 %collective-permute-start.14 = (bf16[256,256]{1,0:T(8,128)(2,1)S(1)}, bf16[256,256]{1,0:T(8,128)(2,1)S(1)}, u32[]{:S(2)}, u32[]{:S(2)}) collective-permute-start(bf16[256,256]{1,0:T(8,128)(2,1)S(1)} %strip_relay.1), channel_id=1, source_target_pairs={{0,8},{4,12},{8,0},{12,4},{16,20},{20,16},{24,28},{28,24},{1,9},{5... | collective-permute-start | bytes 393224 | tf_op jit(solution)/shard_map/ppermute | solution.py:39
  28.2 2.5 %collective-permute-start.7 = (bf16[304,256]{1,0:T(8,128)(2,1)S(1)}, bf16[304,256]{1,0:T(8,128)(2,1)S(1)}, u32[]{:S(2)}, u32[]{:S(2)}) collective-permute-start(bf16[304,256]{1,0:T(8,128)(2,1)S(1)} %get-tuple-element.32.refs_2_), channel_id=1, source_target_pairs={{0,4},{4,0},{8,12},{12,8},{1,5},{5,1},{9,13},{13,9},{2,6},{6,2},{1... | collective-permute-start | bytes 466952 | tf_op jit(solution)/shard_map/ppermute | solution.py:26
  30.7 0.0 collective-permute-done.9.refs_6_
  30.7 0.0 collective-permute-start.11
  30.7 0.1 collective-permute-start.8
  30.9 0.0 collective-permute-done.6.refs_3_
  30.9 1.9 %collective-permute-start.10 = (bf16[288,256]{1,0:T(8,128)(2,1)S(1)}, bf16[288,256]{1,0:T(8,128)(2,1)S(1)}, u32[]{:S(2)}, u32[]{:S(2)}) collective-permute-start(bf16[288,256]{1,0:T(8,128)(2,1)S(1)} %collective-permute-done.6.refs_3_), channel_id=1, source_target_pairs={{0,8},{4,12},{8,0},{12,4},{1,9},{5,13},{9,1},{13,5},{2,10},{6,14},... | collective-permute-start | bytes 442376 | tf_op jit(solution)/shard_map/ppermute | solution.py:26
  32.8 0.0 collective-permute-done.14.refs_2_
  32.8 0.1 strip.1.refs_0_
  32.8 0.5 %collective-permute-start.15 = (bf16[256,256]{1,0:T(8,128)(2,1)S(1)}, bf16[256,256]{1,0:T(8,128)(2,1)S(1)}, u32[]{:S(2)}, u32[]{:S(2)}) collective-permute-start(bf16[256,256]{1,0:T(8,128)(2,1)S(1)} %strip.1.refs_0_), channel_id=1, source_target_pairs={{0,8},{4,12},{8,0},{12,4},{16,20},{20,16},{24,28},{28,24},{1,9},{5... | collective-permute-start | bytes 393224 | tf_op jit(solution)/shard_map/ppermute | solution.py:39
  33.3 2.6 %collective-permute-done.8.refs_5_ = bf16[288,256]{1,0:T(8,128)(2,1)S(1)} collective-permute-done((bf16[288,256]{1,0:T(8,128)(2,1)S(1)}, bf16[288,256]{1,0:T(8,128)(2,1)S(1)}, u32[]{:S(2)}, u32[]{:S(2)}) %collective-permute-start.8) | collective-permute-done | bytes 147488 | tf_op jit(solution)/shard_map/ppermute | solution.py:26
  35.9 0.0 collective-permute-done.7.refs_4_
  35.9 0.0 copy-done.2
  35.9 0.9 %matrix.1 = (bf16[1024,1024]{1,0:T(8,128)(2,1)S(1)}, f32[1,1024]{1,0:T(1,128)S(1)}, f32[16,256]{1,0:T(8,128)S(1)}, f32[256,1024]{1,0:T(8,128)S(1)}, bf16[1024,256]{1,0:T(8,128)(2,1)S(1)}) custom-call(f32[576,256]{1,0:T(8,128)S(1)} %get-tuple-element.30.refs_0_.refs_5_, bf16[288,256]{1,0:T(8,128)(2,1)S(1)} %get-tuple-element.31.refs_1_.refs_2_, ...), custom_call_target="tpu_custom_call" | custom-call | flops 1048576 | bytes 5713920 | tf_op jit(solution)/shard_map/matrix/pallas_call | solution.py:355
  36.7 0.7 %collective-permute-done.10.refs_6_.refs_4_ = bf16[288,256]{1,0:T(8,128)(2,1)S(1)} collective-permute-done((bf16[288,256]{1,0:T(8,128)(2,1)S(1)}, bf16[288,256]{1,0:T(8,128)(2,1)S(1)}, u32[]{:S(2)}, u32[]{:S(2)}) %collective-permute-start.10) | collective-permute-done | bytes 147488 | tf_op jit(solution)/shard_map/ppermute | solution.py:26
  37.4 0.0 collective-permute-done.11.refs_7_.refs_3_
  37.4 2.7 %collective-permute-done.15.refs_1_ = bf16[256,256]{1,0:T(8,128)(2,1)S(1)} collective-permute-done((bf16[256,256]{1,0:T(8,128)(2,1)S(1)}, bf16[256,256]{1,0:T(8,128)(2,1)S(1)}, u32[]{:S(2)}, u32[]{:S(2)}) %collective-permute-start.15) | collective-permute-done | bytes 131104 | tf_op jit(solution)/shard_map/ppermute | solution.py:39
  40.1 2.0 %collective-permute-start.16 = (bf16[512,256]{1,0:T(8,128)(2,1)S(1)}, bf16[512,256]{1,0:T(8,128)(2,1)S(1)}, u32[]{:S(2)}, u32[]{:S(2)}) collective-permute-start(bf16[512,256]{1,0:T(8,128)(2,1)S(1)} %pair.1.refs_0_), channel_id=1, source_target_pairs={{0,4},{4,0},{8,12},{12,8},{16,24},{20,28},{24,16},{28,20},{1,5},{5... | collective-permute-start | bytes 786440 | tf_op jit(solution)/shard_map/ppermute | solution.py:39
  42.8 3.6 %root.1 = (f32[256,1024]{1,0:T(8,128)}, bf16[256,1024]{1,0:T(8,128)(2,1)}, f32[8,128]{1,0:T(8,128)S(1)}) custom-call(s32[1,1]{1,0:T(1,128)S(6)} %copy.8.refs_0_, bf16[1024,1024]{1,0:T(8,128)(2,1)S(1)} %get-tuple-element.33.refs_1_, f32[1,1024]{1,0:T(1,128)S(1)} %get-tuple-element.34.refs_2_, f32[16,256]{1,0:T(8,128)S(1)} %get-tuple-element.35.refs_3_, ...), custom_call_target="tpu_custom_call" | custom-call | flops 1610612736 | bytes 5636100 | tf_op jit(solution)/shard_map/root/pallas_call | solution.py:355
  46.4 0.1 collective-permute-done.16.refs_1_
  46.6 1.0 %step.1 = bf16[256,256]{1,0:T(8,128)(2,1)} custom-call(bf16[512,256]{1,0:T(8,128)(2,1)S(1)} %pair.1.refs_0_, bf16[512,256]{1,0:T(8,128)(2,1)S(1)} %collective-permute-done.16.refs_1_, bf16[1024,256]{1,0:T(8,128)(2,1)S(1)} %get-tuple-element.41.refs_2_, f32[8,128]{1,0:T(8,128)S(1)} %get-tuple-element.42.refs_3_), custom_call_target="tpu_custom_call" | custom-call | tf_op jit(solution)/shard_map/step/pallas_call | solution.py:355
  (3 shorter events, 0.1 us)
Async XLA Ops:
  0.6 1.2 %copy-start = (bf16[1,512,1024]{2,1,0:T(8,128)(2,1)S(1)}, bf16[1,512,1024]{2,1,0:T(8,128)(2,1)}, u32[]{:S(2)}) copy-start(bf16[1,512,1024]{2,1,0:T(8,128)(2,1)} %param.5) | copy-start | bytes 3145732
  2.9 16.9 %copy-start.1 = (f32[1,1,256,1024]{3,2,1,0:T(8,128)S(1)}, f32[1,1,256,1024]{3,2,1,0:T(8,128)}, u32[]{:S(2)}) copy-start(f32[1,1,256,1024]{3,2,1,0:T(8,128)} %param.7) | copy-start | bytes 3145732
  2.9 6.9 %collective-permute-start.2 = (bf16[288,256]{1,0:T(8,128)(2,1)S(1)}, bf16[288,256]{1,0:T(8,128)(2,1)S(1)}, u32[]{:S(2)}, u32[]{:S(2)}) collective-permute-start(bf16[288,256]{1,0:T(8,128)(2,1)S(1)} %get-tuple-element.26), channel_id=1, source_target_pairs={{0,4},{4,0},{8,12},{12,8},{1,5},{5,1},{9,13},{13,9},{2,6},{6,2},{1... | collective-permute-start | bytes 442376 | tf_op jit(solution)/shard_map/ppermute | solution.py:26
  5.9 5.8 %collective-permute-start.3 = (bf16[288,256]{1,0:T(8,128)(2,1)S(1)}, bf16[288,256]{1,0:T(8,128)(2,1)S(1)}, u32[]{:S(2)}, u32[]{:S(2)}) collective-permute-start(bf16[288,256]{1,0:T(8,128)(2,1)S(1)} %get-tuple-element.27), channel_id=1, source_target_pairs={{0,8},{4,12},{8,0},{12,4},{1,9},{5,13},{9,1},{13,5},{2,10},{6,14},... | collective-permute-start | bytes 442376 | tf_op jit(solution)/shard_map/ppermute | solution.py:26
  7.5 7.0 %collective-permute-start.12 = (bf16[1,512,256]{2,1,0:T(8,128)(2,1)}, bf16[1,512,256]{2,1,0:T(8,128)(2,1)S(1)}, u32[]{:S(2)}, u32[]{:S(2)}) collective-permute-start(bf16[1,512,256]{2,1,0:T(8,128)(2,1)} %param.6), channel_id=1, source_target_pairs={{16,0},{0,16},{17,1},{1,17},{18,2},{2,18},{19,3},{3,19},{20,4},{4,... | collective-permute-start | bytes 786440 | tf_op jit(solution)/shard_map/ppermute | solution.py:22
  7.5 7.5 %collective-permute-start = (bf16[288,256]{1,0:T(8,128)(2,1)S(1)}, bf16[288,256]{1,0:T(8,128)(2,1)S(1)}, u32[]{:S(2)}, u32[]{:S(2)}) collective-permute-start(bf16[288,256]{1,0:T(8,128)(2,1)S(1)} %get-tuple-element.24), channel_id=1, source_target_pairs={{0,4},{4,0},{8,12},{12,8},{1,5},{5,1},{9,13},{13,9},{2,6},{6,2},{1... | collective-permute-start | bytes 442376 | tf_op jit(solution)/shard_map/ppermute | solution.py:26
  8.0 7.0 %collective-permute-start.1 = (bf16[288,256]{1,0:T(8,128)(2,1)S(1)}, bf16[288,256]{1,0:T(8,128)(2,1)S(1)}, u32[]{:S(2)}, u32[]{:S(2)}) collective-permute-start(bf16[288,256]{1,0:T(8,128)(2,1)S(1)} %get-tuple-element.25), channel_id=1, source_target_pairs={{0,8},{4,12},{8,0},{12,4},{1,9},{5,13},{9,1},{13,5},{2,10},{6,14},... | collective-permute-start | bytes 442376 | tf_op jit(solution)/shard_map/ppermute | solution.py:26
  11.8 5.2 %collective-permute-start.4 = (bf16[288,256]{1,0:T(8,128)(2,1)S(1)}, bf16[288,256]{1,0:T(8,128)(2,1)S(1)}, u32[]{:S(2)}, u32[]{:S(2)}) collective-permute-start(bf16[288,256]{1,0:T(8,128)(2,1)S(1)} %get-tuple-element.28), channel_id=1, source_target_pairs={{0,4},{4,0},{8,12},{12,8},{1,5},{5,1},{9,13},{13,9},{2,6},{6,2},{1... | collective-permute-start | bytes 442376 | tf_op jit(solution)/shard_map/ppermute | solution.py:26
  12.0 5.5 %collective-permute-start.5 = (bf16[288,256]{1,0:T(8,128)(2,1)S(1)}, bf16[288,256]{1,0:T(8,128)(2,1)S(1)}, u32[]{:S(2)}, u32[]{:S(2)}) collective-permute-start(bf16[288,256]{1,0:T(8,128)(2,1)S(1)} %get-tuple-element.29), channel_id=1, source_target_pairs={{0,8},{4,12},{8,0},{12,4},{1,9},{5,13},{9,1},{13,5},{2,10},{6,14},... | collective-permute-start | bytes 442376 | tf_op jit(solution)/shard_map/ppermute | solution.py:26
  17.6 7.9 %collective-permute-start.13 = (bf16[512,256]{1,0:T(8,128)(2,1)S(1)}, bf16[512,256]{1,0:T(8,128)(2,1)S(1)}, u32[]{:S(2)}, u32[]{:S(2)}) collective-permute-start(bf16[512,256]{1,0:T(8,128)(2,1)S(1)} %release.1), channel_id=1, source_target_pairs={{0,4},{4,0},{8,12},{12,8},{16,24},{20,28},{24,16},{28,20},{1,5},{5... | collective-permute-start | bytes 786440 | tf_op jit(solution)/shard_map/ppermute | solution.py:39
  19.9 16.0 %copy-start.2 = (bf16[1,1,256,1024]{3,2,1,0:T(8,128)(2,1)S(1)}, bf16[1,1,256,1024]{3,2,1,0:T(8,128)(2,1)}, u32[]{:S(2)}) copy-start(bf16[1,1,256,1024]{3,2,1,0:T(8,128)(2,1)} %param.8) | copy-start | bytes 1572868
  20.2 10.5 %collective-permute-start.9 = (bf16[304,256]{1,0:T(8,128)(2,1)S(1)}, bf16[304,256]{1,0:T(8,128)(2,1)S(1)}, u32[]{:S(2)}, u32[]{:S(2)}) collective-permute-start(bf16[304,256]{1,0:T(8,128)(2,1)S(1)} %get-tuple-element.32.refs_2_), channel_id=1, source_target_pairs={{0,8},{4,12},{8,0},{12,4},{1,9},{5,13},{9,1},{13,5},{2,10},{6,14},... | collective-permute-start | bytes 466952 | tf_op jit(solution)/shard_map/ppermute | solution.py:26
  22.7 8.2 %collective-permute-start.6 = (bf16[288,256]{1,0:T(8,128)(2,1)S(1)}, bf16[288,256]{1,0:T(8,128)(2,1)S(1)}, u32[]{:S(2)}, u32[]{:S(2)}) collective-permute-start(bf16[288,256]{1,0:T(8,128)(2,1)S(1)} %get-tuple-element.31.refs_1_.refs_2_), channel_id=1, source_target_pairs={{0,4},{4,0},{8,12},{12,8},{1,5},{5,1},{9,13},{13,9},{2,6},{6,2},{1... | collective-permute-start | bytes 442376 | tf_op jit(solution)/shard_map/ppermute | solution.py:26
  25.6 7.2 %collective-permute-start.14 = (bf16[256,256]{1,0:T(8,128)(2,1)S(1)}, bf16[256,256]{1,0:T(8,128)(2,1)S(1)}, u32[]{:S(2)}, u32[]{:S(2)}) collective-permute-start(bf16[256,256]{1,0:T(8,128)(2,1)S(1)} %strip_relay.1), channel_id=1, source_target_pairs={{0,8},{4,12},{8,0},{12,4},{16,20},{20,16},{24,28},{28,24},{1,9},{5... | collective-permute-start | bytes 393224 | tf_op jit(solution)/shard_map/ppermute | solution.py:39
  28.2 7.7 %collective-permute-start.7 = (bf16[304,256]{1,0:T(8,128)(2,1)S(1)}, bf16[304,256]{1,0:T(8,128)(2,1)S(1)}, u32[]{:S(2)}, u32[]{:S(2)}) collective-permute-start(bf16[304,256]{1,0:T(8,128)(2,1)S(1)} %get-tuple-element.32.refs_2_), channel_id=1, source_target_pairs={{0,4},{4,0},{8,12},{12,8},{1,5},{5,1},{9,13},{13,9},{2,6},{6,2},{1... | collective-permute-start | bytes 466952 | tf_op jit(solution)/shard_map/ppermute | solution.py:26
  30.7 6.8 %collective-permute-start.11 = (bf16[304,256]{1,0:T(8,128)(2,1)S(1)}, bf16[304,256]{1,0:T(8,128)(2,1)S(1)}, u32[]{:S(2)}, u32[]{:S(2)}) collective-permute-start(bf16[304,256]{1,0:T(8,128)(2,1)S(1)} %collective-permute-done.9.refs_6_), channel_id=1, source_target_pairs={{0,4},{4,0},{8,12},{12,8},{1,5},{5,1},{9,13},{13,9},{2,6},{6,2},{1... | collective-permute-start | bytes 466952 | tf_op jit(solution)/shard_map/ppermute | solution.py:26
  30.7 5.1 %collective-permute-start.8 = (bf16[288,256]{1,0:T(8,128)(2,1)S(1)}, bf16[288,256]{1,0:T(8,128)(2,1)S(1)}, u32[]{:S(2)}, u32[]{:S(2)}) collective-permute-start(bf16[288,256]{1,0:T(8,128)(2,1)S(1)} %get-tuple-element.31.refs_1_.refs_2_), channel_id=1, source_target_pairs={{0,8},{4,12},{8,0},{12,4},{1,9},{5,13},{9,1},{13,5},{2,10},{6,14},... | collective-permute-start | bytes 442376 | tf_op jit(solution)/shard_map/ppermute | solution.py:26
  30.9 6.6 %collective-permute-start.10 = (bf16[288,256]{1,0:T(8,128)(2,1)S(1)}, bf16[288,256]{1,0:T(8,128)(2,1)S(1)}, u32[]{:S(2)}, u32[]{:S(2)}) collective-permute-start(bf16[288,256]{1,0:T(8,128)(2,1)S(1)} %collective-permute-done.6.refs_3_), channel_id=1, source_target_pairs={{0,8},{4,12},{8,0},{12,4},{1,9},{5,13},{9,1},{13,5},{2,10},{6,14},... | collective-permute-start | bytes 442376 | tf_op jit(solution)/shard_map/ppermute | solution.py:26
  32.8 7.3 %collective-permute-start.15 = (bf16[256,256]{1,0:T(8,128)(2,1)S(1)}, bf16[256,256]{1,0:T(8,128)(2,1)S(1)}, u32[]{:S(2)}, u32[]{:S(2)}) collective-permute-start(bf16[256,256]{1,0:T(8,128)(2,1)S(1)} %strip.1.refs_0_), channel_id=1, source_target_pairs={{0,8},{4,12},{8,0},{12,4},{16,20},{20,16},{24,28},{28,24},{1,9},{5... | collective-permute-start | bytes 393224 | tf_op jit(solution)/shard_map/ppermute | solution.py:39
  40.1 6.4 %collective-permute-start.16 = (bf16[512,256]{1,0:T(8,128)(2,1)S(1)}, bf16[512,256]{1,0:T(8,128)(2,1)S(1)}, u32[]{:S(2)}, u32[]{:S(2)}) collective-permute-start(bf16[512,256]{1,0:T(8,128)(2,1)S(1)} %pair.1.refs_0_), channel_id=1, source_target_pairs={{0,4},{4,0},{8,12},{12,8},{16,24},{20,28},{24,16},{28,20},{1,5},{5... | collective-permute-start | bytes 786440 | tf_op jit(solution)/shard_map/ppermute | solution.py:39

commit v9 on v3

--- a/solution.py
+++ b/solution.py
@@ -22,8 +22,21 @@
     return lax.ppermute(block, axis, route)
 
 
-def swapped(block, offset):
-    return lax.ppermute(block, "dp", [(i, i ^ offset) for i in range(lax.axis_size("dp"))])
+def along(turn):
+    return jnp.where(lax.axis_index("pipe") == turn, 1, 2)
+
+
+def swapped(block, turn):
+    replicas = lax.axis_size("dp")
+    route = []
+    for section in range(lax.axis_size("pipe")):
+        offset = 1 if section == turn else 2
+        route += [(section * replicas + i, section * replicas + (i ^ offset)) for i in range(replicas)]
+    return lax.ppermute(block, ("pipe", "dp"), route)
+
+
+def swapped_across(block):
+    return lax.ppermute(block, "dp", [(i, i ^ 3) for i in range(lax.axis_size("dp"))])
 
 
 def eye_of(rows, cols, shift=0):
@@ -38,6 +51,10 @@
 
 def transposed(block):
     return block.astype(F32).T.astype(block.dtype)
+
+
+def offsets():
+    return 0, along(0), along(1), 3
 
 
 def chunk_rows(share):
@@ -82,13 +99,13 @@
         yield 0, batch[pl.ds(base, half), pl.ds(base, share)]
         low = batch[pl.ds(corner, half), pl.ds(corner, half)]
         yield starts[1], jnp.concatenate([low[0 : half // 2], low[half // 2 :]], axis=1)
-        for step in range(1, replicas):
+        for start, step in zip(starts[2:], offsets()[1:]):
             row, col = shared_half(owner, step, share)
-            yield starts[1 + step], batch[pl.ds(row, half), pl.ds(col, share)]
+            yield start, batch[pl.ds(row, half), pl.ds(col, share)]
 
     store_chunk(pieces(3), length, (relay_x, 0), (relay_y, 0))
-    store_chunk(pieces(1), length, (direct_x, 0), (keep, 3 * length))
-    store_chunk(pieces(2), length, (keep, 2 * length), (direct_y, 0))
+    store_chunk(pieces(along(0)), length, (direct_x, 0), (keep, 3 * length))
+    store_chunk(pieces(along(1)), length, (keep, 2 * length), (direct_y, 0))
     store_chunk(pieces(0), length, (keep, 0), (keep, length))
 
 
@@ -108,8 +125,8 @@
             yield part * strip, total[rows, part * share : (part + 1) * share]
 
     store_chunk(pieces(3), length, (send_x, 0), (send_y, 0))
-    store_chunk(pieces(1), length, (send_x, length), (keep, 3 * length))
-    store_chunk(pieces(2), length, (keep, 2 * length), (send_y, length))
+    store_chunk(pieces(along(0)), length, (send_x, length), (keep, 3 * length))
+    store_chunk(pieces(along(1)), length, (keep, 2 * length), (send_y, length))
     store_chunk(pieces(0), length, (keep, 0), (keep, length))
 
 
@@ -159,7 +176,7 @@
         DECAY * diagonal[0:half] + DAMPING * eye,
         packed(DECAY * diagonal[half:, half:] + DAMPING * low_eye),
     ]
-    for step in range(1, replicas):
+    for step in offsets()[1:]:
         other = mine ^ step
         block = old[:, pl.ds(pl.multiple_of(other * share, share), share)]
         terms.append(DECAY * jnp.where(mine < other, block[0:half], block[:, half:].T))
@@ -185,44 +202,71 @@
     lower[...] = chunk[length:]
 
 
-def root_kernel(replicas, count, exact, *rest):
-    chunks = [rest[2 * i : 2 * i + 2] for i in range(replicas)]
-    factor_out, root_out, finished, factor, diagonal = rest[2 * replicas :]
-    share = root_out.shape[0]
-    order = root_out.shape[1]
+def root_kernel(count, exact, *rest):
+    chunks = [rest[2 * i : 2 * i + 2] for i in range(4)]
+    factor_out, root_out, finished, factor, diagonal, rows, sent = rest[8:]
+    share, order = root_out.shape
     half = share // 2
     starts = chunk_rows(share)
     length = chunks[0][0].shape[0]
     mine = lax.axis_index("dp")
 
-    def rows_of(offset, start, count):
-        upper, lower = chunks[offset]
+    def rows_of(position, start, count):
+        upper, lower = chunks[position]
         if start + count <= length:
             return upper[start : start + count, :]
         if start >= length:
             return lower[start - length : start - length + count, :]
         return jnp.concatenate([upper[start:length, :], lower[0 : start + count - length, :]], axis=0)
 
+    top = exact[0:half, :]
+    low = exact[starts[1] : starts[2], :]
+    low = jnp.concatenate([low[:, 0:half], low[:, half:]], axis=0)
+    copies = []
+    for position, step in enumerate(offsets()):
+        other = mine ^ step
+        target = rows.at[position]
+        if position == 0:
+            target[0:half, :] = top
+            target[half:, :] = jnp.concatenate([top[:, half:].T, low], axis=1)
+        else:
+            start = starts[1 + position]
+            own = exact[start : start + half, :]
+            theirs = rows_of(position, start, half).astype(F32)
+
+            @pl.when(mine < other)
+            def _():
+                target[0:half, :] = own
+                target[half:, :] = theirs
+
+            @pl.when(mine > other)
+            def _():
+                target[...] = jnp.concatenate([theirs.T, own.T], axis=1)
+
+        columns = pl.ds(pl.multiple_of(other * share, share), share)
+        copies.append(pltpu.make_async_copy(target, factor_out.at[:, columns], sent.at[position]))
+        copies[-1].start()
+
     squares = jnp.zeros((16, share), F32)
     low_eye = eye_of(half, half)
-    for offset in range(replicas):
+    for position, offset in enumerate(offsets()):
         owner = mine ^ offset
         base = pl.multiple_of(owner * share, share)
         corner = pl.multiple_of(owner * share + half, half)
-        top = rows_of(offset, 0, half)
-        low = rows_of(offset, starts[1], half // 2)
+        top = rows_of(position, 0, half)
+        low = rows_of(position, starts[1], half // 2)
         low = jnp.concatenate([low[:, 0:half], low[:, half:]], axis=0)
         factor[pl.ds(base, half), pl.ds(base, share)] = top
         factor[pl.ds(corner, half), pl.ds(base, half)] = transposed(top[:, half:])
         factor[pl.ds(corner, half), pl.ds(corner, half)] = low
         diagonal[:, pl.ds(base, half)] = jnp.sum(top[:, 0:half].astype(F32) * low_eye, axis=0, keepdims=True)
         diagonal[:, pl.ds(corner, half)] = jnp.sum(low.astype(F32) * low_eye, axis=0, keepdims=True)
-        for step in range(1, replicas):
+        for start, step in zip(starts[2:], offsets()[1:]):
             row, col = shared_half(owner, step, share)
-            block = rows_of(offset, starts[1 + step], half)
+            block = rows_of(position, start, half)
             factor[pl.ds(row, half), pl.ds(col, share)] = block
             factor[pl.ds(col, share), pl.ds(row, half)] = transposed(block)
-        squares = squares + rows_of(offset, starts[-1], 16).astype(F32)
+        squares = squares + rows_of(position, starts[-1], 16).astype(F32)
 
     scale = jnp.sqrt(jnp.sum(squares, keepdims=True) / order + EPSILON)
     inverse = 1.0 / scale
@@ -241,27 +285,8 @@
     chosen = jnp.where(count[0, 0] == 1, turn.astype(F32), inverse_rows)
     root_out[...] = (chosen * lax.rsqrt(scale)).astype(BF16)
     finished[...] = jnp.zeros_like(finished)
-
-    own_columns = pl.ds(pl.multiple_of(mine * share, share), share)
-    top = exact[0:half, :]
-    low = exact[starts[1] : starts[2], :]
-    low = jnp.concatenate([low[:, 0:half], low[:, half:]], axis=0)
-    factor_out[0:half, own_columns] = top
-    factor_out[half:, own_columns] = jnp.concatenate([top[:, half:].T, low], axis=1)
-    for step in range(1, replicas):
-        other = mine ^ step
-        columns = pl.ds(pl.multiple_of(other * share, share), share)
-        own = exact[starts[1 + step] : starts[1 + step] + half, :]
-        theirs = rows_of(step, starts[1 + step], half).astype(F32)
-
-        @pl.when(mine < other)
-        def _():
-            factor_out[0:half, columns] = own
-            factor_out[half:, columns] = theirs
-
-        @pl.when(mine > other)
-        def _():
-            factor_out[:, columns] = jnp.concatenate([theirs.T, own.T], axis=1)
+    for copy in copies:
+        copy.wait()
 
 
 def step_kernel(replicas, *refs):
@@ -278,11 +303,9 @@
     result[...] = lax.dot_general(
         grads[...], old_root[...], (((1,), (1,)), ((), ())), preferred_element_type=F32
     ).astype(BF16)
-    for offset in range(replicas):
-        owner = mine ^ offset
-        step_out[pl.ds(pl.multiple_of(owner * strip, strip), strip), :] = result[
-            offset * strip : (offset + 1) * strip, :
-        ]
+    for position, offset in enumerate(offsets()):
+        rows = pl.ds(pl.multiple_of((mine ^ offset) * strip, strip), strip)
+        step_out[rows, :] = result[position * strip : (position + 1) * strip, :]
 
 
 def square_plan(acts, out_grad, old_factor, old_root, iter_count):
@@ -298,10 +321,13 @@
     def shape(rows, kind=BF16, columns=share):
         return jax.ShapeDtypeStruct((rows, columns), kind)
 
-    def call(kernel, outs, name, *operands, first=None, after=(), scratch=()):
+    def call(kernel, outs, name, *operands, first=None, first_out=None, after=(), scratch=()):
         in_specs = whole(len(operands)) + [pl.BlockSpec(memory_space=pl.ANY)] * len(after)
         if first is not None:
             in_specs[0] = pl.BlockSpec(memory_space=first)
+        out_specs = whole(len(outs))
+        if first_out is not None:
+            out_specs[0] = pl.BlockSpec(memory_space=first_out)
 
         def body(*refs):
             kernel(*refs[: len(operands)], *refs[len(operands) + len(after) :])
@@ -310,7 +336,7 @@
             body,
             out_shape=outs,
             in_specs=in_specs,
-            out_specs=whole(len(outs)),
+            out_specs=out_specs,
             scratch_shapes=scratch,
             compiler_params=params,
             name=name,
@@ -324,8 +350,8 @@
         inputs,
         scratch=[pltpu.VMEM((order, order), F32)],
     )
-    relay_x, relay_y = swapped(relay_x, 1), swapped(relay_y, 2)
-    direct_x, direct_y = swapped(direct_x, 1), swapped(direct_y, 2)
+    relay_x, relay_y = swapped(relay_x, 0), swapped(relay_y, 1)
+    direct_x, direct_y = swapped(direct_x, 0), swapped(direct_y, 1)
     relay_x, relay_y = call(relay_kernel, [shape(length)] * 2, "relay", keep, relay_x, relay_y)
     grad_x, grad_y, grad_keep = call(
         functools.partial(grad_kernel, replicas, tokens * replicas),
@@ -336,8 +362,8 @@
         after=[relay_x, relay_y],
         scratch=[pltpu.VMEM((grows, order), F32)],
     )
-    relay_x, relay_y = swapped(relay_x, 1), swapped(relay_y, 2)
-    grad_x, grad_y = swapped(grad_x, 1), swapped(grad_y, 2)
+    relay_x, relay_y = swapped(relay_x, 0), swapped(relay_y, 1)
+    grad_x, grad_y = swapped(grad_x, 0), swapped(grad_y, 1)
     upper, lower, exact = call(
         functools.partial(factor_kernel, replicas),
         [shape(length), shape(length + 16), shape(whole_rows, F32)],
@@ -349,13 +375,13 @@
         relay_y,
         old_factor[0, 0],
     )
-    upper_x, lower_y = swapped(upper, 1), swapped(lower, 2)
-    lower_x, upper_y = swapped(lower, 1), swapped(upper, 2)
+    upper_x, lower_y = swapped(upper, 0), swapped(lower, 1)
+    lower_x, upper_y = swapped(lower, 0), swapped(upper, 1)
     strip_x, strip_y = call(
         grad_relay_kernel, [shape(grows // 2)] * 2, "grad_relay", grad_keep, grad_x, grad_y, after=[upper, lower]
     )
-    strip_x, strip_y = swapped(strip_x, 1), swapped(strip_y, 2)
-    upper_far, lower_far = swapped(upper_x, 2), swapped(lower_y, 1)
+    strip_x, strip_y = swapped(strip_x, 0), swapped(strip_y, 1)
+    upper_far, lower_far = swapped(upper_x, 1), swapped(lower_y, 0)
     (strip,) = call(
         grad_total_kernel,
         [shape(grows)],
@@ -367,9 +393,9 @@
         strip_y,
         after=[upper_x, lower_y],
     )
-    strips = [strip] + [swapped(strip, offset) for offset in range(1, replicas)]
+    strips = [strip, swapped(strip, 0), swapped(strip, 1), swapped_across(strip)]
     factor, root, finished = call(
-        functools.partial(root_kernel, replicas),
+        root_kernel,
         [shape(share, F32, order), shape(share, BF16, order), shape(8, F32, 128)],
         "root",
         iter_count,
@@ -383,7 +409,13 @@
         upper_far,
         lower_far,
         first=pltpu.SMEM,
-        scratch=[pltpu.VMEM((order, order), BF16), pltpu.VMEM((1, order), F32)],
+        first_out=pl.ANY,
+        scratch=[
+            pltpu.VMEM((order, order), BF16),
+            pltpu.VMEM((1, order), F32),
+            pltpu.VMEM((replicas, share, share), F32),
+            pltpu.SemaphoreType.DMA((replicas,)),
+        ],
     )
     (step,) = call(
         functools.partial(step_kernel, replicas),
@@ -433,7 +465,7 @@
 
 def solution(mesh):
     return jax.shard_map(
-        square_plan if mesh.shape["dp"] == 4 else ring_plan,
+        square_plan if mesh.shape["dp"] == 4 and mesh.shape["pipe"] == 2 else ring_plan,
         mesh=mesh,
         in_specs=(
             P("pipe", "dp", "tensor"),

time: 41.7 us -> 41.9 us (level)
  starting transfers between devices: 22.5 us -> 23 us
    ppermute x19, starting transfers between devices: 21.9 us -> 22.4 us  [the longest x18 21.5 us: swapped(): return lax.ppermute(block, ('pipe', 'dp'), route)]
  transfers between devices with their start and end apart: 20 -> 20, of which waited for: 6 -> 7; matrix products, arithmetic and copies ran while one was open for 0% -> 0% of each run, Pallas kernels for 14% -> 14%
where the time goes in v9:
time: 41.9 us; the launch traced here: 41.8 us
  starting transfers between devices  23 us (55%)
  waiting for transfers between devices  9.43 us (23%)
  Pallas kernels  6.75 us (16%)
  between operations  1.38 us (3%)
  local copies, waits for them, and re-layouts  1.23 us (3%)
    ppermute x18, starting transfers between devices, swapped(): return lax.ppermute(block, ('pipe', 'dp'), route)  21.5 us
    ppermute x18, waiting for transfers between devices, swapped(): return lax.ppermute(block, ('pipe', 'dp'), route)  8.97 us
    pallas_call x8, Pallas kernels, call(): pl.pallas_call(body, out_shape=outs, in_specs=in_specs, out_specs=out_spe...  6.75 us
    unnamed x6, local copies, waits for them, and re-layouts  1.23 us
    ppermute x1, starting transfers between devices, swapped_across(): lax.ppermute(block, 'dp', [(i, i ^ 3) for i in range(lax.axis_size('dp'))])  0.99 us
  transfers between devices with their start and end apart: 20, of which 7 were waited for; matrix products, arithmetic and copies ran while one was open for 0% of the time, Pallas kernels for 14%

profile of v9, /device:TPU:0, one launch (start us, length us, event | category | flops | bytes accessed | tf_op | source)
XLA Modules:
  0.0 41.8 jit_solution(12144637558681009722)
XLA Ops:
  0.6 0.5 %collective-permute-start.12 = (bf16[1,512,256]{2,1,0:T(8,128)(2,1)}, bf16[1,512,256]{2,1,0:T(8,128)(2,1)S(1)}, u32[]{:S(2)}, u32[]{:S(2)}) collective-permute-start(bf16[1,512,256]{2,1,0:T(8,128)(2,1)} %param.6), channel_id=1, source_target_pairs={{16,0},{0,16},{17,1},{1,17},{18,2},{2,18},{19,3},{3,19},{20,4},{4,... | collective-permute-start | bytes 786440 | tf_op jit(solution)/shard_map/ppermute | solution.py:22
  1.1 0.0 copy-start
  1.1 1.2 %copy-done = bf16[1,512,1024]{2,1,0:T(8,128)(2,1)S(1)} copy-done((bf16[1,512,1024]{2,1,0:T(8,128)(2,1)S(1)}, bf16[1,512,1024]{2,1,0:T(8,128)(2,1)}, u32[]{:S(2)}) %copy-start) | copy-done | bytes 1048600
  2.4 1.1 %batch.1 = (bf16[288,256]{1,0:T(8,128)(2,1)S(1)}, bf16[288,256]{1,0:T(8,128)(2,1)S(1)}, bf16[288,256]{1,0:T(8,128)(2,1)S(1)}, bf16[288,256]{1,0:T(8,128)(2,1)S(1)}, f32[1152,256]{1,0:T(8,128)S(1)}) custom-call(bf16[512,1024]{1,0:T(8,128)(2,1)S(1)} %bitcast.7), custom_call_target="tpu_custom_call" | custom-call | tf_op jit(solution)/shard_map/batch/pallas_call | solution.py:335
  3.4 2.6 %collective-permute-start.2 = (bf16[288,256]{1,0:T(8,128)(2,1)S(1)}, bf16[288,256]{1,0:T(8,128)(2,1)S(1)}, u32[]{:S(2)}, u32[]{:S(2)}) collective-permute-start(bf16[288,256]{1,0:T(8,128)(2,1)S(1)} %get-tuple-element.24), channel_id=1, source_target_pairs={{0,4},{4,0},{8,12},{12,8},{16,24},{20,28},{24,16},{28,20},{1,5},{5... | collective-permute-start | bytes 442376 | tf_op jit(solution)/shard_map/ppermute | solution.py:35
  6.0 1.5 %collective-permute-start.3 = (bf16[288,256]{1,0:T(8,128)(2,1)S(1)}, bf16[288,256]{1,0:T(8,128)(2,1)S(1)}, u32[]{:S(2)}, u32[]{:S(2)}) collective-permute-start(bf16[288,256]{1,0:T(8,128)(2,1)S(1)} %get-tuple-element.25), channel_id=1, source_target_pairs={{0,8},{4,12},{8,0},{12,4},{16,20},{20,16},{24,28},{28,24},{1,9},{5... | collective-permute-start | bytes 442376 | tf_op jit(solution)/shard_map/ppermute | solution.py:35
  7.5 0.5 %collective-permute-start = (bf16[288,256]{1,0:T(8,128)(2,1)S(1)}, bf16[288,256]{1,0:T(8,128)(2,1)S(1)}, u32[]{:S(2)}, u32[]{:S(2)}) collective-permute-start(bf16[288,256]{1,0:T(8,128)(2,1)S(1)} %get-tuple-element.22), channel_id=1, source_target_pairs={{0,4},{4,0},{8,12},{12,8},{16,24},{20,28},{24,16},{28,20},{1,5},{5... | collective-permute-start | bytes 442376 | tf_op jit(solution)/shard_map/ppermute | solution.py:35
  8.1 0.1 collective-permute-start.1
  8.1 1.4 %collective-permute-done.2.refs_1_ = bf16[288,256]{1,0:T(8,128)(2,1)S(1)} collective-permute-done((bf16[288,256]{1,0:T(8,128)(2,1)S(1)}, bf16[288,256]{1,0:T(8,128)(2,1)S(1)}, u32[]{:S(2)}, u32[]{:S(2)}) %collective-permute-start.2) | collective-permute-done | bytes 147488 | tf_op jit(solution)/shard_map/ppermute | solution.py:35
  9.5 2.8 %collective-permute-done.3.refs_2_ = bf16[288,256]{1,0:T(8,128)(2,1)S(1)} collective-permute-done((bf16[288,256]{1,0:T(8,128)(2,1)S(1)}, bf16[288,256]{1,0:T(8,128)(2,1)S(1)}, u32[]{:S(2)}, u32[]{:S(2)}) %collective-permute-start.3) | collective-permute-done | bytes 147488 | tf_op jit(solution)/shard_map/ppermute | solution.py:35
  12.3 0.0 copy-start.1
  12.3 0.1 relay.1
  12.4 0.5 %collective-permute-start.4 = (bf16[288,256]{1,0:T(8,128)(2,1)S(1)}, bf16[288,256]{1,0:T(8,128)(2,1)S(1)}, u32[]{:S(2)}, u32[]{:S(2)}) collective-permute-start(bf16[288,256]{1,0:T(8,128)(2,1)S(1)} %get-tuple-element.26.refs_2_), channel_id=1, source_target_pairs={{0,4},{4,0},{8,12},{12,8},{16,24},{20,28},{24,16},{28,20},{1,5},{5... | collective-permute-start | bytes 442376 | tf_op jit(solution)/shard_map/ppermute | solution.py:35
  12.9 2.0 %collective-permute-start.5 = (bf16[288,256]{1,0:T(8,128)(2,1)S(1)}, bf16[288,256]{1,0:T(8,128)(2,1)S(1)}, u32[]{:S(2)}, u32[]{:S(2)}) collective-permute-start(bf16[288,256]{1,0:T(8,128)(2,1)S(1)} %get-tuple-element.27.refs_3_), channel_id=1, source_target_pairs={{0,8},{4,12},{8,0},{12,4},{16,20},{20,16},{24,28},{28,24},{1,9},{5... | collective-permute-start | bytes 442376 | tf_op jit(solution)/shard_map/ppermute | solution.py:35
  14.9 0.0 collective-permute-done.12
  14.9 0.5 %grad.1 = (bf16[256,256]{1,0:T(8,128)(2,1)S(1)}, bf16[256,256]{1,0:T(8,128)(2,1)S(1)}, f32[512,256]{1,0:T(8,128)S(1)}) custom-call(bf16[512,1024]{1,0:T(8,128)(2,1)S(1)} %bitcast.8, bf16[512,256]{1,0:T(8,128)(2,1)S(1)} %bitcast.11, bf16[288,256]{1,0:T(8,128)(2,1)S(1)} %get-tuple-element.26.refs_2_, bf16[288,256]{1,0:T(8,128)(2,1)S(1)} %get-tuple-element.27.refs_3_), custom_call_target="tpu_custom_call" | custom-call | tf_op jit(solution)/shard_map/grad/pallas_call | solution.py:335
  15.4 1.2 %collective-permute-start.13 = (bf16[256,256]{1,0:T(8,128)(2,1)S(1)}, bf16[256,256]{1,0:T(8,128)(2,1)S(1)}, u32[]{:S(2)}, u32[]{:S(2)}) collective-permute-start(bf16[256,256]{1,0:T(8,128)(2,1)S(1)} %get-tuple-element.34), channel_id=1, source_target_pairs={{0,4},{4,0},{8,12},{12,8},{16,24},{20,28},{24,16},{28,20},{1,5},{5... | collective-permute-start | bytes 393224 | tf_op jit(solution)/shard_map/ppermute | solution.py:35
  16.6 0.0 collective-permute-done.refs_1_
  16.6 0.5 %collective-permute-start.14 = (bf16[256,256]{1,0:T(8,128)(2,1)S(1)}, bf16[256,256]{1,0:T(8,128)(2,1)S(1)}, u32[]{:S(2)}, u32[]{:S(2)}) collective-permute-start(bf16[256,256]{1,0:T(8,128)(2,1)S(1)} %get-tuple-element.35), channel_id=1, source_target_pairs={{0,8},{4,12},{8,0},{12,4},{16,20},{20,16},{24,28},{28,24},{1,9},{5... | collective-permute-start | bytes 393224 | tf_op jit(solution)/shard_map/ppermute | solution.py:35
  17.1 0.0 collective-permute-done.1.refs_2_
  17.1 0.7 %collective-permute-done.4.refs_3_ = bf16[288,256]{1,0:T(8,128)(2,1)S(1)} collective-permute-done((bf16[288,256]{1,0:T(8,128)(2,1)S(1)}, bf16[288,256]{1,0:T(8,128)(2,1)S(1)}, u32[]{:S(2)}, u32[]{:S(2)}) %collective-permute-start.4) | collective-permute-done | bytes 147488 | tf_op jit(solution)/shard_map/ppermute | solution.py:35
  17.8 1.5 %collective-permute-done.5.refs_4_ = bf16[288,256]{1,0:T(8,128)(2,1)S(1)} collective-permute-done((bf16[288,256]{1,0:T(8,128)(2,1)S(1)}, bf16[288,256]{1,0:T(8,128)(2,1)S(1)}, u32[]{:S(2)}, u32[]{:S(2)}) %collective-permute-start.5) | collective-permute-done | bytes 147488 | tf_op jit(solution)/shard_map/ppermute | solution.py:35
  19.3 0.0 copy-done.1
  19.3 0.3 factor.1
  19.6 1.6 %collective-permute-start.6 = (bf16[288,256]{1,0:T(8,128)(2,1)S(1)}, bf16[288,256]{1,0:T(8,128)(2,1)S(1)}, u32[]{:S(2)}, u32[]{:S(2)}) collective-permute-start(bf16[288,256]{1,0:T(8,128)(2,1)S(1)} %get-tuple-element.29.refs_2_.refs_3_), channel_id=1, source_target_pairs={{0,4},{4,0},{8,12},{12,8},{16,24},{20,28},{24,16},{28,20},{1,5},{5... | collective-permute-start | bytes 442376 | tf_op jit(solution)/shard_map/ppermute | solution.py:35
  21.3 0.8 %collective-permute-start.9 = (bf16[304,256]{1,0:T(8,128)(2,1)S(1)}, bf16[304,256]{1,0:T(8,128)(2,1)S(1)}, u32[]{:S(2)}, u32[]{:S(2)}) collective-permute-start(bf16[304,256]{1,0:T(8,128)(2,1)S(1)} %get-tuple-element.30.refs_3_.refs_4_), channel_id=1, source_target_pairs={{0,8},{4,12},{8,0},{12,4},{16,20},{20,16},{24,28},{28,24},{1,9},{5... | collective-permute-start | bytes 466952 | tf_op jit(solution)/shard_map/ppermute | solution.py:35
  22.0 1.7 %collective-permute-start.7 = (bf16[304,256]{1,0:T(8,128)(2,1)S(1)}, bf16[304,256]{1,0:T(8,128)(2,1)S(1)}, u32[]{:S(2)}, u32[]{:S(2)}) collective-permute-start(bf16[304,256]{1,0:T(8,128)(2,1)S(1)} %get-tuple-element.30.refs_3_.refs_4_), channel_id=1, source_target_pairs={{0,4},{4,0},{8,12},{12,8},{16,24},{20,28},{24,16},{28,20},{1,5},{5... | collective-permute-start | bytes 466952 | tf_op jit(solution)/shard_map/ppermute | solution.py:35
  23.8 0.0 collective-permute-done.13.refs_1_
  23.8 0.0 collective-permute-start.8
  23.8 0.0 collective-permute-done.14.refs_2_
  23.8 1.6 %collective-permute-start.15 = (bf16[128,256]{1,0:T(8,128)(2,1)S(1)}, bf16[128,256]{1,0:T(8,128)(2,1)S(1)}, u32[]{:S(2)}, u32[]{:S(2)}) collective-permute-start(bf16[128,256]{1,0:T(8,128)(2,1)S(1)} %get-tuple-element.36), channel_id=1, source_target_pairs={{0,4},{4,0},{8,12},{12,8},{16,24},{20,28},{24,16},{28,20},{1,5},{5... | collective-permute-start | bytes 196616 | tf_op jit(solution)/shard_map/ppermute | solution.py:35
  25.4 1.0 %collective-permute-done.6.refs_4_.refs_5_ = bf16[288,256]{1,0:T(8,128)(2,1)S(1)} collective-permute-done((bf16[288,256]{1,0:T(8,128)(2,1)S(1)}, bf16[288,256]{1,0:T(8,128)(2,1)S(1)}, u32[]{:S(2)}, u32[]{:S(2)}) %collective-permute-start.6) | collective-permute-done | bytes 147488 | tf_op jit(solution)/shard_map/ppermute | solution.py:35
  26.5 2.0 %collective-permute-start.16 = (bf16[128,256]{1,0:T(8,128)(2,1)S(1)}, bf16[128,256]{1,0:T(8,128)(2,1)S(1)}, u32[]{:S(2)}, u32[]{:S(2)}) collective-permute-start(bf16[128,256]{1,0:T(8,128)(2,1)S(1)} %get-tuple-element.37), channel_id=1, source_target_pairs={{0,8},{4,12},{8,0},{12,4},{16,20},{20,16},{24,28},{28,24},{1,9},{5... | collective-permute-start | bytes 196616 | tf_op jit(solution)/shard_map/ppermute | solution.py:35
  28.4 0.0 collective-permute-done.9.refs_7_.refs_6_
  28.5 0.3 collective-permute-start.11
  28.8 1.5 %collective-permute-done.15.refs_3_ = bf16[128,256]{1,0:T(8,128)(2,1)S(1)} collective-permute-done((bf16[128,256]{1,0:T(8,128)(2,1)S(1)}, bf16[128,256]{1,0:T(8,128)(2,1)S(1)}, u32[]{:S(2)}, u32[]{:S(2)}) %collective-permute-start.15) | collective-permute-done | bytes 65568 | tf_op jit(solution)/shard_map/ppermute | solution.py:35
  30.2 2.0 %collective-permute-start.10 = (bf16[288,256]{1,0:T(8,128)(2,1)S(1)}, bf16[288,256]{1,0:T(8,128)(2,1)S(1)}, u32[]{:S(2)}, u32[]{:S(2)}) collective-permute-start(bf16[288,256]{1,0:T(8,128)(2,1)S(1)} %collective-permute-done.6.refs_4_.refs_5_), channel_id=1, source_target_pairs={{0,8},{4,12},{8,0},{12,4},{16,20},{20,16},{24,28},{28,24},{1,9},{5... | collective-permute-start | bytes 442376 | tf_op jit(solution)/shard_map/ppermute | solution.py:35
  32.2 0.0 collective-permute-done.16.refs_4_
  32.2 0.1 grad_total.1.refs_0_
  32.3 0.0 copy-start.2
  32.3 1.0 %collective-permute-start.17 = (bf16[256,256]{1,0:T(8,128)(2,1)S(1)}, bf16[256,256]{1,0:T(8,128)(2,1)S(1)}, u32[]{:S(2)}, u32[]{:S(2)}) collective-permute-start(bf16[256,256]{1,0:T(8,128)(2,1)S(1)} %grad_total.1.refs_0_), channel_id=1, source_target_pairs={{0,4},{4,0},{8,12},{12,8},{16,24},{20,28},{24,16},{28,20},{1,5},{5... | collective-permute-start | bytes 393224 | tf_op jit(solution)/shard_map/ppermute | solution.py:35
  33.3 0.0 collective-permute-done.8.refs_6_
  33.3 1.5 %collective-permute-start.18 = (bf16[256,256]{1,0:T(8,128)(2,1)S(1)}, bf16[256,256]{1,0:T(8,128)(2,1)S(1)}, u32[]{:S(2)}, u32[]{:S(2)}) collective-permute-start(bf16[256,256]{1,0:T(8,128)(2,1)S(1)} %grad_total.1.refs_0_), channel_id=1, source_target_pairs={{0,8},{4,12},{8,0},{12,4},{16,20},{20,16},{24,28},{28,24},{1,9},{5... | collective-permute-start | bytes 393224 | tf_op jit(solution)/shard_map/ppermute | solution.py:35
  34.9 0.0 collective-permute-done.7.refs_5_
  34.9 1.0 %collective-permute-start.19 = (bf16[256,256]{1,0:T(8,128)(2,1)S(1)}, bf16[256,256]{1,0:T(8,128)(2,1)S(1)}, u32[]{:S(2)}, u32[]{:S(2)}) collective-permute-start(bf16[256,256]{1,0:T(8,128)(2,1)S(1)} %grad_total.1.refs_0_), channel_id=1, source_target_pairs={{0,12},{4,8},{8,4},{12,0},{1,13},{5,9},{9,5},{13,1},{2,14},{6,10},... | collective-permute-start | bytes 393224 | tf_op jit(solution)/shard_map/ppermute | solution.py:39
  36.5 0.0 collective-permute-done.10.refs_8_
  36.5 0.0 collective-permute-done.11.refs_9_
  36.5 3.7 %root.1 = (f32[256,1024]{1,0:T(8,128)}, bf16[256,1024]{1,0:T(8,128)(2,1)}, f32[8,128]{1,0:T(8,128)S(1)}) custom-call(s32[1,1]{1,0:T(1,128)S(6)} %copy.8.refs_0_, f32[576,256]{1,0:T(8,128)S(1)} %get-tuple-element.28.refs_1_, bf16[288,256]{1,0:T(8,128)(2,1)S(1)} %get-tuple-element.29.refs_2_.refs_3_, bf16[304,256]{1,0:T(8,128)(2,1)S(1)} %get-tuple-element.30.refs_3_.refs_4_, ...), custom_call_target="tpu_custom_call" | custom-call | tf_op jit(solution)/shard_map/root/pallas_call | solution.py:335
  40.3 0.0 collective-permute-done.17.refs_1_
  40.3 0.0 collective-permute-done.18.refs_2_
  40.3 0.5 %collective-permute-done.19.refs_3_ = bf16[256,256]{1,0:T(8,128)(2,1)S(1)} collective-permute-done((bf16[256,256]{1,0:T(8,128)(2,1)S(1)}, bf16[256,256]{1,0:T(8,128)(2,1)S(1)}, u32[]{:S(2)}, u32[]{:S(2)}) %collective-permute-start.19) | collective-permute-done | bytes 131104 | tf_op jit(solution)/shard_map/ppermute | solution.py:39
  40.8 0.0 copy-done.2
  40.8 1.0 %step.1 = bf16[256,256]{1,0:T(8,128)(2,1)} custom-call(bf16[256,256]{1,0:T(8,128)(2,1)S(1)} %grad_total.1.refs_0_, bf16[256,256]{1,0:T(8,128)(2,1)S(1)} %collective-permute-done.17.refs_1_, bf16[256,256]{1,0:T(8,128)(2,1)S(1)} %collective-permute-done.18.refs_2_, bf16[256,256]{1,0:T(8,128)(2,1)S(1)} %collective-permute-done.19.refs_3_, ...), custom_call_target="tpu_custom_call" | custom-call | tf_op jit(solution)/shard_map/step/pallas_call | solution.py:335
  (1 shorter events, 0.0 us)
Async XLA Ops:
  0.6 14.3 %collective-permute-start.12 = (bf16[1,512,256]{2,1,0:T(8,128)(2,1)}, bf16[1,512,256]{2,1,0:T(8,128)(2,1)S(1)}, u32[]{:S(2)}, u32[]{:S(2)}) collective-permute-start(bf16[1,512,256]{2,1,0:T(8,128)(2,1)} %param.6), channel_id=1, source_target_pairs={{16,0},{0,16},{17,1},{1,17},{18,2},{2,18},{19,3},{3,19},{20,4},{4,... | collective-permute-start | bytes 786440 | tf_op jit(solution)/shard_map/ppermute | solution.py:22
  1.1 1.2 %copy-start = (bf16[1,512,1024]{2,1,0:T(8,128)(2,1)S(1)}, bf16[1,512,1024]{2,1,0:T(8,128)(2,1)}, u32[]{:S(2)}) copy-start(bf16[1,512,1024]{2,1,0:T(8,128)(2,1)} %param.5) | copy-start | bytes 3145732
  3.4 6.1 %collective-permute-start.2 = (bf16[288,256]{1,0:T(8,128)(2,1)S(1)}, bf16[288,256]{1,0:T(8,128)(2,1)S(1)}, u32[]{:S(2)}, u32[]{:S(2)}) collective-permute-start(bf16[288,256]{1,0:T(8,128)(2,1)S(1)} %get-tuple-element.24), channel_id=1, source_target_pairs={{0,4},{4,0},{8,12},{12,8},{16,24},{20,28},{24,16},{28,20},{1,5},{5... | collective-permute-start | bytes 442376 | tf_op jit(solution)/shard_map/ppermute | solution.py:35
  6.0 6.3 %collective-permute-start.3 = (bf16[288,256]{1,0:T(8,128)(2,1)S(1)}, bf16[288,256]{1,0:T(8,128)(2,1)S(1)}, u32[]{:S(2)}, u32[]{:S(2)}) collective-permute-start(bf16[288,256]{1,0:T(8,128)(2,1)S(1)} %get-tuple-element.25), channel_id=1, source_target_pairs={{0,8},{4,12},{8,0},{12,4},{16,20},{20,16},{24,28},{28,24},{1,9},{5... | collective-permute-start | bytes 442376 | tf_op jit(solution)/shard_map/ppermute | solution.py:35
  7.5 9.1 %collective-permute-start = (bf16[288,256]{1,0:T(8,128)(2,1)S(1)}, bf16[288,256]{1,0:T(8,128)(2,1)S(1)}, u32[]{:S(2)}, u32[]{:S(2)}) collective-permute-start(bf16[288,256]{1,0:T(8,128)(2,1)S(1)} %get-tuple-element.22), channel_id=1, source_target_pairs={{0,4},{4,0},{8,12},{12,8},{16,24},{20,28},{24,16},{28,20},{1,5},{5... | collective-permute-start | bytes 442376 | tf_op jit(solution)/shard_map/ppermute | solution.py:35
  8.1 9.0 %collective-permute-start.1 = (bf16[288,256]{1,0:T(8,128)(2,1)S(1)}, bf16[288,256]{1,0:T(8,128)(2,1)S(1)}, u32[]{:S(2)}, u32[]{:S(2)}) collective-permute-start(bf16[288,256]{1,0:T(8,128)(2,1)S(1)} %get-tuple-element.23), channel_id=1, source_target_pairs={{0,8},{4,12},{8,0},{12,4},{16,20},{20,16},{24,28},{28,24},{1,9},{5... | collective-permute-start | bytes 442376 | tf_op jit(solution)/shard_map/ppermute | solution.py:35
  12.3 7.0 %copy-start.1 = (f32[1,1,256,1024]{3,2,1,0:T(8,128)S(1)}, f32[1,1,256,1024]{3,2,1,0:T(8,128)}, u32[]{:S(2)}) copy-start(f32[1,1,256,1024]{3,2,1,0:T(8,128)} %param.7) | copy-start | bytes 3145732
  12.4 5.4 %collective-permute-start.4 = (bf16[288,256]{1,0:T(8,128)(2,1)S(1)}, bf16[288,256]{1,0:T(8,128)(2,1)S(1)}, u32[]{:S(2)}, u32[]{:S(2)}) collective-permute-start(bf16[288,256]{1,0:T(8,128)(2,1)S(1)} %get-tuple-element.26.refs_2_), channel_id=1, source_target_pairs={{0,4},{4,0},{8,12},{12,8},{16,24},{20,28},{24,16},{28,20},{1,5},{5... | collective-permute-start | bytes 442376 | tf_op jit(solution)/shard_map/ppermute | solution.py:35
  12.9 6.5 %collective-permute-start.5 = (bf16[288,256]{1,0:T(8,128)(2,1)S(1)}, bf16[288,256]{1,0:T(8,128)(2,1)S(1)}, u32[]{:S(2)}, u32[]{:S(2)}) collective-permute-start(bf16[288,256]{1,0:T(8,128)(2,1)S(1)} %get-tuple-element.27.refs_3_), channel_id=1, source_target_pairs={{0,8},{4,12},{8,0},{12,4},{16,20},{20,16},{24,28},{28,24},{1,9},{5... | collective-permute-start | bytes 442376 | tf_op jit(solution)/shard_map/ppermute | solution.py:35
  15.4 8.3 %collective-permute-start.13 = (bf16[256,256]{1,0:T(8,128)(2,1)S(1)}, bf16[256,256]{1,0:T(8,128)(2,1)S(1)}, u32[]{:S(2)}, u32[]{:S(2)}) collective-permute-start(bf16[256,256]{1,0:T(8,128)(2,1)S(1)} %get-tuple-element.34), channel_id=1, source_target_pairs={{0,4},{4,0},{8,12},{12,8},{16,24},{20,28},{24,16},{28,20},{1,5},{5... | collective-permute-start | bytes 393224 | tf_op jit(solution)/shard_map/ppermute | solution.py:35
  16.6 7.1 %collective-permute-start.14 = (bf16[256,256]{1,0:T(8,128)(2,1)S(1)}, bf16[256,256]{1,0:T(8,128)(2,1)S(1)}, u32[]{:S(2)}, u32[]{:S(2)}) collective-permute-start(bf16[256,256]{1,0:T(8,128)(2,1)S(1)} %get-tuple-element.35), channel_id=1, source_target_pairs={{0,8},{4,12},{8,0},{12,4},{16,20},{20,16},{24,28},{28,24},{1,9},{5... | collective-permute-start | bytes 393224 | tf_op jit(solution)/shard_map/ppermute | solution.py:35
  19.6 6.8 %collective-permute-start.6 = (bf16[288,256]{1,0:T(8,128)(2,1)S(1)}, bf16[288,256]{1,0:T(8,128)(2,1)S(1)}, u32[]{:S(2)}, u32[]{:S(2)}) collective-permute-start(bf16[288,256]{1,0:T(8,128)(2,1)S(1)} %get-tuple-element.29.refs_2_.refs_3_), channel_id=1, source_target_pairs={{0,4},{4,0},{8,12},{12,8},{16,24},{20,28},{24,16},{28,20},{1,5},{5... | collective-permute-start | bytes 442376 | tf_op jit(solution)/shard_map/ppermute | solution.py:35
  21.3 7.2 %collective-permute-start.9 = (bf16[304,256]{1,0:T(8,128)(2,1)S(1)}, bf16[304,256]{1,0:T(8,128)(2,1)S(1)}, u32[]{:S(2)}, u32[]{:S(2)}) collective-permute-start(bf16[304,256]{1,0:T(8,128)(2,1)S(1)} %get-tuple-element.30.refs_3_.refs_4_), channel_id=1, source_target_pairs={{0,8},{4,12},{8,0},{12,4},{16,20},{20,16},{24,28},{28,24},{1,9},{5... | collective-permute-start | bytes 466952 | tf_op jit(solution)/shard_map/ppermute | solution.py:35
  22.0 12.9 %collective-permute-start.7 = (bf16[304,256]{1,0:T(8,128)(2,1)S(1)}, bf16[304,256]{1,0:T(8,128)(2,1)S(1)}, u32[]{:S(2)}, u32[]{:S(2)}) collective-permute-start(bf16[304,256]{1,0:T(8,128)(2,1)S(1)} %get-tuple-element.30.refs_3_.refs_4_), channel_id=1, source_target_pairs={{0,4},{4,0},{8,12},{12,8},{16,24},{20,28},{24,16},{28,20},{1,5},{5... | collective-permute-start | bytes 466952 | tf_op jit(solution)/shard_map/ppermute | solution.py:35
  23.8 9.6 %collective-permute-start.8 = (bf16[288,256]{1,0:T(8,128)(2,1)S(1)}, bf16[288,256]{1,0:T(8,128)(2,1)S(1)}, u32[]{:S(2)}, u32[]{:S(2)}) collective-permute-start(bf16[288,256]{1,0:T(8,128)(2,1)S(1)} %get-tuple-element.29.refs_2_.refs_3_), channel_id=1, source_target_pairs={{0,8},{4,12},{8,0},{12,4},{16,20},{20,16},{24,28},{28,24},{1,9},{5... | collective-permute-start | bytes 442376 | tf_op jit(solution)/shard_map/ppermute | solution.py:35
  23.8 6.4 %collective-permute-start.15 = (bf16[128,256]{1,0:T(8,128)(2,1)S(1)}, bf16[128,256]{1,0:T(8,128)(2,1)S(1)}, u32[]{:S(2)}, u32[]{:S(2)}) collective-permute-start(bf16[128,256]{1,0:T(8,128)(2,1)S(1)} %get-tuple-element.36), channel_id=1, source_target_pairs={{0,4},{4,0},{8,12},{12,8},{16,24},{20,28},{24,16},{28,20},{1,5},{5... | collective-permute-start | bytes 196616 | tf_op jit(solution)/shard_map/ppermute | solution.py:35
  26.5 5.8 %collective-permute-start.16 = (bf16[128,256]{1,0:T(8,128)(2,1)S(1)}, bf16[128,256]{1,0:T(8,128)(2,1)S(1)}, u32[]{:S(2)}, u32[]{:S(2)}) collective-permute-start(bf16[128,256]{1,0:T(8,128)(2,1)S(1)} %get-tuple-element.37), channel_id=1, source_target_pairs={{0,8},{4,12},{8,0},{12,4},{16,20},{20,16},{24,28},{28,24},{1,9},{5... | collective-permute-start | bytes 196616 | tf_op jit(solution)/shard_map/ppermute | solution.py:35
  28.5 8.1 %collective-permute-start.11 = (bf16[304,256]{1,0:T(8,128)(2,1)S(1)}, bf16[304,256]{1,0:T(8,128)(2,1)S(1)}, u32[]{:S(2)}, u32[]{:S(2)}) collective-permute-start(bf16[304,256]{1,0:T(8,128)(2,1)S(1)} %collective-permute-done.9.refs_7_.refs_6_), channel_id=1, source_target_pairs={{0,4},{4,0},{8,12},{12,8},{16,24},{20,28},{24,16},{28,20},{1,5},{5... | collective-permute-start | bytes 466952 | tf_op jit(solution)/shard_map/ppermute | solution.py:35
  30.2 6.3 %collective-permute-start.10 = (bf16[288,256]{1,0:T(8,128)(2,1)S(1)}, bf16[288,256]{1,0:T(8,128)(2,1)S(1)}, u32[]{:S(2)}, u32[]{:S(2)}) collective-permute-start(bf16[288,256]{1,0:T(8,128)(2,1)S(1)} %collective-permute-done.6.refs_4_.refs_5_), channel_id=1, source_target_pairs={{0,8},{4,12},{8,0},{12,4},{16,20},{20,16},{24,28},{28,24},{1,9},{5... | collective-permute-start | bytes 442376 | tf_op jit(solution)/shard_map/ppermute | solution.py:35
  32.3 8.5 %copy-start.2 = (bf16[1,1,256,1024]{3,2,1,0:T(8,128)(2,1)S(1)}, bf16[1,1,256,1024]{3,2,1,0:T(8,128)(2,1)}, u32[]{:S(2)}) copy-start(bf16[1,1,256,1024]{3,2,1,0:T(8,128)(2,1)} %param.8) | copy-start | bytes 1572868
  32.3 8.0 %collective-permute-start.17 = (bf16[256,256]{1,0:T(8,128)(2,1)S(1)}, bf16[256,256]{1,0:T(8,128)(2,1)S(1)}, u32[]{:S(2)}, u32[]{:S(2)}) collective-permute-start(bf16[256,256]{1,0:T(8,128)(2,1)S(1)} %grad_total.1.refs_0_), channel_id=1, source_target_pairs={{0,4},{4,0},{8,12},{12,8},{16,24},{20,28},{24,16},{28,20},{1,5},{5... | collective-permute-start | bytes 393224 | tf_op jit(solution)/shard_map/ppermute | solution.py:35
  33.3 7.0 %collective-permute-start.18 = (bf16[256,256]{1,0:T(8,128)(2,1)S(1)}, bf16[256,256]{1,0:T(8,128)(2,1)S(1)}, u32[]{:S(2)}, u32[]{:S(2)}) collective-permute-start(bf16[256,256]{1,0:T(8,128)(2,1)S(1)} %grad_total.1.refs_0_), channel_id=1, source_target_pairs={{0,8},{4,12},{8,0},{12,4},{16,20},{20,16},{24,28},{28,24},{1,9},{5... | collective-permute-start | bytes 393224 | tf_op jit(solution)/shard_map/ppermute | solution.py:35
  34.9 5.9 %collective-permute-start.19 = (bf16[256,256]{1,0:T(8,128)(2,1)S(1)}, bf16[256,256]{1,0:T(8,128)(2,1)S(1)}, u32[]{:S(2)}, u32[]{:S(2)}) collective-permute-start(bf16[256,256]{1,0:T(8,128)(2,1)S(1)} %grad_total.1.refs_0_), channel_id=1, source_target_pairs={{0,12},{4,8},{8,4},{12,0},{1,13},{5,9},{9,5},{13,1},{2,14},{6,10},... | collective-permute-start | bytes 393224 | tf_op jit(solution)/shard_map/ppermute | solution.py:39

commit v10 on v9

--- a/solution.py
+++ b/solution.py
@@ -136,19 +136,27 @@
     send_x[...] = (keep[3 * length :, :] + got_y[...].astype(F32)).astype(BF16)
 
 
-def grad_relay_kernel(keep, got_x, got_y, send_x, send_y):
-    length = send_x.shape[0]
-    send_y[...] = (keep[2 * length : 3 * length, :] + got_x[0:length, :].astype(F32)).astype(BF16)
-    send_x[...] = (keep[3 * length :, :] + got_y[0:length, :].astype(F32)).astype(BF16)
-
-
-def grad_total_kernel(keep, got_x, got_y, relay_x, relay_y, chunk):
-    length = relay_x.shape[0]
-    chunk[0:length, :] = (
-        keep[0:length, :] + got_x[length:, :].astype(F32) + relay_y[...].astype(F32)
+def gather_kernel(keep, got_x, got_y, upper, lower, send_x, send_y):
+    length = got_x.shape[0] // 2
+    send_x[0 : upper.shape[0], :] = upper[...]
+    send_x[upper.shape[0] :, :] = (keep[3 * length :, :] + got_y[0:length, :].astype(F32)).astype(BF16)
+    send_y[0 : lower.shape[0], :] = lower[...]
+    send_y[lower.shape[0] :, :] = (keep[2 * length : 3 * length, :] + got_x[0:length, :].astype(F32)).astype(BF16)
+
+
+def halves_kernel(got_x, got_y, send_x, send_y):
+    send_y[...] = got_x[0 : send_y.shape[0], :]
+    send_x[...] = got_y[0 : send_x.shape[0], :]
+
+
+def strip_kernel(keep, got_x, got_y, relay_x, relay_y, strip):
+    length = got_x.shape[0] // 2
+    first_x, first_y = relay_x.shape[0] - length, relay_y.shape[0] - length
+    strip[0:length, :] = (
+        keep[0:length, :] + got_x[length:, :].astype(F32) + relay_y[first_y:, :].astype(F32)
     ).astype(BF16)
-    chunk[length:, :] = (
-        keep[length : 2 * length, :] + got_y[length:, :].astype(F32) + relay_x[...].astype(F32)
+    strip[length:, :] = (
+        keep[length : 2 * length, :] + got_y[length:, :].astype(F32) + relay_x[first_x:, :].astype(F32)
     ).astype(BF16)
 
 
@@ -375,23 +383,22 @@
         relay_y,
         old_factor[0, 0],
     )
-    upper_x, lower_y = swapped(upper, 0), swapped(lower, 1)
-    lower_x, upper_y = swapped(lower, 0), swapped(upper, 1)
-    strip_x, strip_y = call(
-        grad_relay_kernel, [shape(grows // 2)] * 2, "grad_relay", grad_keep, grad_x, grad_y, after=[upper, lower]
-    )
-    strip_x, strip_y = swapped(strip_x, 0), swapped(strip_y, 1)
-    upper_far, lower_far = swapped(upper_x, 1), swapped(lower_y, 0)
-    (strip,) = call(
-        grad_total_kernel,
-        [shape(grows)],
-        "grad_total",
+    on_x, on_y = call(
+        gather_kernel,
+        [shape(length + grows // 2), shape(length + 16 + grows // 2)],
+        "gather",
         grad_keep,
         grad_x,
         grad_y,
-        strip_x,
-        strip_y,
-        after=[upper_x, lower_y],
+        upper,
+        lower,
+    )
+    upper_x, lower_y = swapped(on_x, 0), swapped(on_y, 1)
+    lower_x, upper_y = swapped(lower, 0), swapped(upper, 1)
+    on_x, on_y = call(halves_kernel, [shape(length + 16), shape(length)], "halves", upper_x, lower_y)
+    lower_far, upper_far = swapped(on_x, 0), swapped(on_y, 1)
+    (strip,) = call(
+        strip_kernel, [shape(grows)], "strip", grad_keep, grad_x, grad_y, upper_x, lower_y, after=[on_x]
     )
     strips = [strip, swapped(strip, 0), swapped(strip, 1), swapped_across(strip)]
     factor, root, finished = call(

time: 41.9 us -> 45.1 us (1.076)
  waiting for transfers between devices: 9.43 us -> 15.7 us
  starting transfers between devices: 23 us -> 19.9 us
    ppermute x18 -> x16, waiting for transfers between devices: 8.97 us -> 15.7 us  [swapped(): return lax.ppermute(block, ('pipe', 'dp'), route)]
    ppermute x18 -> x16, starting transfers between devices: 21.5 us -> 18.6 us  [swapped(): return lax.ppermute(block, ('pipe', 'dp'), route)]
    ppermute x1, waiting for transfers between devices: 0.46 us -> 0.01 us  [swapped_across(): lax.ppermute(block, 'dp', [(i, i ^ 3) for i in range(lax.axis_size('dp'))])]
    pallas_call x8 -> x9, Pallas kernels: 6.75 us -> 6.78 us  [call(): pl.pallas_call(body, out_shape=outs, in_specs=in_specs, out_specs=out_spe...]
  transfers between devices with their start and end apart: 20 -> 18, of which waited for: 7 -> 9; matrix products, arithmetic and copies ran while one was open for 0% -> 0% of each run, Pallas kernels for 14% -> 13%
where the time goes in v10:
time: 45.1 us; the launch traced here: 45 us
  starting transfers between devices  19.9 us (44%)
  waiting for transfers between devices  15.7 us (35%)
  Pallas kernels  6.78 us (15%)
  between operations  1.37 us (3%)
  local copies, waits for them, and re-layouts  1.23 us (3%)
    ppermute x16, starting transfers between devices, swapped(): return lax.ppermute(block, ('pipe', 'dp'), route)  18.6 us
    ppermute x16, waiting for transfers between devices, swapped(): return lax.ppermute(block, ('pipe', 'dp'), route)  15.7 us
    pallas_call x9, Pallas kernels, call(): pl.pallas_call(body, out_shape=outs, in_specs=in_specs, out_specs=out_spe...  6.78 us
    unnamed x6, local copies, waits for them, and re-layouts  1.23 us
  transfers between devices with their start and end apart: 18, of which 9 were waited for; matrix products, arithmetic and copies ran while one was open for 0% of the time, Pallas kernels for 13%

profile of v10, /device:TPU:0, one launch (start us, length us, event | category | flops | bytes accessed | tf_op | source)
XLA Modules:
  0.0 45.0 jit_solution(17940724739143492177)
XLA Ops:
  0.6 0.5 %collective-permute-start.6 = (bf16[1,512,256]{2,1,0:T(8,128)(2,1)}, bf16[1,512,256]{2,1,0:T(8,128)(2,1)S(1)}, u32[]{:S(2)}, u32[]{:S(2)}) collective-permute-start(bf16[1,512,256]{2,1,0:T(8,128)(2,1)} %param.6), channel_id=1, source_target_pairs={{16,0},{0,16},{17,1},{1,17},{18,2},{2,18},{19,3},{3,19},{20,4},{4,... | collective-permute-start | bytes 786440 | tf_op jit(solution)/shard_map/ppermute | solution.py:22
  1.1 0.0 copy-start
  1.1 1.2 %copy-done = bf16[1,512,1024]{2,1,0:T(8,128)(2,1)S(1)} copy-done((bf16[1,512,1024]{2,1,0:T(8,128)(2,1)S(1)}, bf16[1,512,1024]{2,1,0:T(8,128)(2,1)}, u32[]{:S(2)}) %copy-start) | copy-done | bytes 1048600
  2.4 1.1 %batch.1 = (bf16[288,256]{1,0:T(8,128)(2,1)S(1)}, bf16[288,256]{1,0:T(8,128)(2,1)S(1)}, bf16[288,256]{1,0:T(8,128)(2,1)S(1)}, bf16[288,256]{1,0:T(8,128)(2,1)S(1)}, f32[1152,256]{1,0:T(8,128)S(1)}) custom-call(bf16[512,1024]{1,0:T(8,128)(2,1)S(1)} %bitcast.7), custom_call_target="tpu_custom_call" | custom-call | tf_op jit(solution)/shard_map/batch/pallas_call | solution.py:343
  3.4 2.6 %collective-permute-start.2 = (bf16[288,256]{1,0:T(8,128)(2,1)S(1)}, bf16[288,256]{1,0:T(8,128)(2,1)S(1)}, u32[]{:S(2)}, u32[]{:S(2)}) collective-permute-start(bf16[288,256]{1,0:T(8,128)(2,1)S(1)} %get-tuple-element.26), channel_id=1, source_target_pairs={{0,4},{4,0},{8,12},{12,8},{16,24},{20,28},{24,16},{28,20},{1,5},{5... | collective-permute-start | bytes 442376 | tf_op jit(solution)/shard_map/ppermute | solution.py:35
  6.0 1.5 %collective-permute-start.3 = (bf16[288,256]{1,0:T(8,128)(2,1)S(1)}, bf16[288,256]{1,0:T(8,128)(2,1)S(1)}, u32[]{:S(2)}, u32[]{:S(2)}) collective-permute-start(bf16[288,256]{1,0:T(8,128)(2,1)S(1)} %get-tuple-element.27), channel_id=1, source_target_pairs={{0,8},{4,12},{8,0},{12,4},{16,20},{20,16},{24,28},{28,24},{1,9},{5... | collective-permute-start | bytes 442376 | tf_op jit(solution)/shard_map/ppermute | solution.py:35
  7.5 0.5 %collective-permute-start = (bf16[288,256]{1,0:T(8,128)(2,1)S(1)}, bf16[288,256]{1,0:T(8,128)(2,1)S(1)}, u32[]{:S(2)}, u32[]{:S(2)}) collective-permute-start(bf16[288,256]{1,0:T(8,128)(2,1)S(1)} %get-tuple-element.24), channel_id=1, source_target_pairs={{0,4},{4,0},{8,12},{12,8},{16,24},{20,28},{24,16},{28,20},{1,5},{5... | collective-permute-start | bytes 442376 | tf_op jit(solution)/shard_map/ppermute | solution.py:35
  8.1 0.1 collective-permute-start.1
  8.1 1.4 %collective-permute-done.2.refs_1_ = bf16[288,256]{1,0:T(8,128)(2,1)S(1)} collective-permute-done((bf16[288,256]{1,0:T(8,128)(2,1)S(1)}, bf16[288,256]{1,0:T(8,128)(2,1)S(1)}, u32[]{:S(2)}, u32[]{:S(2)}) %collective-permute-start.2) | collective-permute-done | bytes 147488 | tf_op jit(solution)/shard_map/ppermute | solution.py:35
  9.5 2.8 %collective-permute-done.3.refs_2_ = bf16[288,256]{1,0:T(8,128)(2,1)S(1)} collective-permute-done((bf16[288,256]{1,0:T(8,128)(2,1)S(1)}, bf16[288,256]{1,0:T(8,128)(2,1)S(1)}, u32[]{:S(2)}, u32[]{:S(2)}) %collective-permute-start.3) | collective-permute-done | bytes 147488 | tf_op jit(solution)/shard_map/ppermute | solution.py:35
  12.3 0.0 copy-start.1
  12.3 0.1 relay.1
  12.4 0.5 %collective-permute-start.4 = (bf16[288,256]{1,0:T(8,128)(2,1)S(1)}, bf16[288,256]{1,0:T(8,128)(2,1)S(1)}, u32[]{:S(2)}, u32[]{:S(2)}) collective-permute-start(bf16[288,256]{1,0:T(8,128)(2,1)S(1)} %get-tuple-element.28.refs_2_), channel_id=1, source_target_pairs={{0,4},{4,0},{8,12},{12,8},{16,24},{20,28},{24,16},{28,20},{1,5},{5... | collective-permute-start | bytes 442376 | tf_op jit(solution)/shard_map/ppermute | solution.py:35
  12.9 2.0 %collective-permute-start.5 = (bf16[288,256]{1,0:T(8,128)(2,1)S(1)}, bf16[288,256]{1,0:T(8,128)(2,1)S(1)}, u32[]{:S(2)}, u32[]{:S(2)}) collective-permute-start(bf16[288,256]{1,0:T(8,128)(2,1)S(1)} %get-tuple-element.29.refs_3_), channel_id=1, source_target_pairs={{0,8},{4,12},{8,0},{12,4},{16,20},{20,16},{24,28},{28,24},{1,9},{5... | collective-permute-start | bytes 442376 | tf_op jit(solution)/shard_map/ppermute | solution.py:35
  14.9 0.0 collective-permute-done.6
  14.9 0.5 %grad.1 = (bf16[256,256]{1,0:T(8,128)(2,1)S(1)}, bf16[256,256]{1,0:T(8,128)(2,1)S(1)}, f32[512,256]{1,0:T(8,128)S(1)}) custom-call(bf16[512,1024]{1,0:T(8,128)(2,1)S(1)} %bitcast.8, bf16[512,256]{1,0:T(8,128)(2,1)S(1)} %bitcast.11, bf16[288,256]{1,0:T(8,128)(2,1)S(1)} %get-tuple-element.28.refs_2_, bf16[288,256]{1,0:T(8,128)(2,1)S(1)} %get-tuple-element.29.refs_3_), custom_call_target="tpu_custom_call" | custom-call | tf_op jit(solution)/shard_map/grad/pallas_call | solution.py:343
  15.4 1.2 %collective-permute-start.7 = (bf16[256,256]{1,0:T(8,128)(2,1)S(1)}, bf16[256,256]{1,0:T(8,128)(2,1)S(1)}, u32[]{:S(2)}, u32[]{:S(2)}) collective-permute-start(bf16[256,256]{1,0:T(8,128)(2,1)S(1)} %get-tuple-element.34), channel_id=1, source_target_pairs={{0,4},{4,0},{8,12},{12,8},{16,24},{20,28},{24,16},{28,20},{1,5},{5... | collective-permute-start | bytes 393224 | tf_op jit(solution)/shard_map/ppermute | solution.py:35
  16.6 0.0 collective-permute-done.refs_1_
  16.6 0.5 %collective-permute-start.8 = (bf16[256,256]{1,0:T(8,128)(2,1)S(1)}, bf16[256,256]{1,0:T(8,128)(2,1)S(1)}, u32[]{:S(2)}, u32[]{:S(2)}) collective-permute-start(bf16[256,256]{1,0:T(8,128)(2,1)S(1)} %get-tuple-element.35), channel_id=1, source_target_pairs={{0,8},{4,12},{8,0},{12,4},{16,20},{20,16},{24,28},{28,24},{1,9},{5... | collective-permute-start | bytes 393224 | tf_op jit(solution)/shard_map/ppermute | solution.py:35
  17.1 0.0 collective-permute-done.1.refs_2_
  17.1 0.7 %collective-permute-done.4.refs_3_ = bf16[288,256]{1,0:T(8,128)(2,1)S(1)} collective-permute-done((bf16[288,256]{1,0:T(8,128)(2,1)S(1)}, bf16[288,256]{1,0:T(8,128)(2,1)S(1)}, u32[]{:S(2)}, u32[]{:S(2)}) %collective-permute-start.4) | collective-permute-done | bytes 147488 | tf_op jit(solution)/shard_map/ppermute | solution.py:35
  17.8 1.5 %collective-permute-done.5.refs_4_ = bf16[288,256]{1,0:T(8,128)(2,1)S(1)} collective-permute-done((bf16[288,256]{1,0:T(8,128)(2,1)S(1)}, bf16[288,256]{1,0:T(8,128)(2,1)S(1)}, u32[]{:S(2)}, u32[]{:S(2)}) %collective-permute-start.5) | collective-permute-done | bytes 147488 | tf_op jit(solution)/shard_map/ppermute | solution.py:35
  19.3 0.0 copy-done.1
  19.3 0.3 factor.1
  19.6 1.3 %collective-permute-done.7.refs_1_ = bf16[256,256]{1,0:T(8,128)(2,1)S(1)} collective-permute-done((bf16[256,256]{1,0:T(8,128)(2,1)S(1)}, bf16[256,256]{1,0:T(8,128)(2,1)S(1)}, u32[]{:S(2)}, u32[]{:S(2)}) %collective-permute-start.7) | collective-permute-done | bytes 131104 | tf_op jit(solution)/shard_map/ppermute | solution.py:35
  20.9 0.7 %collective-permute-done.8.refs_2_ = bf16[256,256]{1,0:T(8,128)(2,1)S(1)} collective-permute-done((bf16[256,256]{1,0:T(8,128)(2,1)S(1)}, bf16[256,256]{1,0:T(8,128)(2,1)S(1)}, u32[]{:S(2)}, u32[]{:S(2)}) %collective-permute-start.8) | collective-permute-done | bytes 131104 | tf_op jit(solution)/shard_map/ppermute | solution.py:35
  21.6 0.1 gather.1
  21.7 1.2 %collective-permute-start.12 = (bf16[432,256]{1,0:T(8,128)(2,1)S(1)}, bf16[432,256]{1,0:T(8,128)(2,1)S(1)}, u32[]{:S(2)}, u32[]{:S(2)}) collective-permute-start(bf16[432,256]{1,0:T(8,128)(2,1)S(1)} %get-tuple-element.37), channel_id=1, source_target_pairs={{0,8},{4,12},{8,0},{12,4},{16,20},{20,16},{24,28},{28,24},{1,9},{5... | collective-permute-start | bytes 663560 | tf_op jit(solution)/shard_map/ppermute | solution.py:35
  22.9 1.3 %collective-permute-start.9 = (bf16[416,256]{1,0:T(8,128)(2,1)S(1)}, bf16[416,256]{1,0:T(8,128)(2,1)S(1)}, u32[]{:S(2)}, u32[]{:S(2)}) collective-permute-start(bf16[416,256]{1,0:T(8,128)(2,1)S(1)} %get-tuple-element.36), channel_id=1, source_target_pairs={{0,4},{4,0},{8,12},{12,8},{16,24},{20,28},{24,16},{28,20},{1,5},{5... | collective-permute-start | bytes 638984 | tf_op jit(solution)/shard_map/ppermute | solution.py:35
  24.2 0.8 %collective-permute-start.10 = (bf16[304,256]{1,0:T(8,128)(2,1)S(1)}, bf16[304,256]{1,0:T(8,128)(2,1)S(1)}, u32[]{:S(2)}, u32[]{:S(2)}) collective-permute-start(bf16[304,256]{1,0:T(8,128)(2,1)S(1)} %get-tuple-element.32.refs_4_.refs_3_), channel_id=1, source_target_pairs={{0,4},{4,0},{8,12},{12,8},{16,24},{20,28},{24,16},{28,20},{1,5},{5... | collective-permute-start | bytes 466952 | tf_op jit(solution)/shard_map/ppermute | solution.py:35
  24.9 0.9 %collective-permute-start.11 = (bf16[288,256]{1,0:T(8,128)(2,1)S(1)}, bf16[288,256]{1,0:T(8,128)(2,1)S(1)}, u32[]{:S(2)}, u32[]{:S(2)}) collective-permute-start(bf16[288,256]{1,0:T(8,128)(2,1)S(1)} %get-tuple-element.31.refs_3_.refs_2_), channel_id=1, source_target_pairs={{0,8},{4,12},{8,0},{12,4},{16,20},{20,16},{24,28},{28,24},{1,9},{5... | collective-permute-start | bytes 442376 | tf_op jit(solution)/shard_map/ppermute | solution.py:35
  25.8 4.1 %collective-permute-done.9.refs_0_.refs_4_.refs_3_ = bf16[416,256]{1,0:T(8,128)(2,1)S(1)} collective-permute-done((bf16[416,256]{1,0:T(8,128)(2,1)S(1)}, bf16[416,256]{1,0:T(8,128)(2,1)S(1)}, u32[]{:S(2)}, u32[]{:S(2)}) %collective-permute-start.9) | collective-permute-done | bytes 213024 | tf_op jit(solution)/shard_map/ppermute | solution.py:35
  29.9 0.1 collective-permute-done.12.refs_1_.refs_7_.refs_4_
  30.0 1.0 %collective-permute-start.14 = (bf16[304,256]{1,0:T(8,128)(2,1)S(1)}, bf16[304,256]{1,0:T(8,128)(2,1)S(1)}, u32[]{:S(2)}, u32[]{:S(2)}) collective-permute-start(bf16[304,256]{1,0:T(8,128)(2,1)S(1)} %get-tuple-element.39.refs_5_), channel_id=1, source_target_pairs={{0,4},{4,0},{8,12},{12,8},{16,24},{20,28},{24,16},{28,20},{1,5},{5... | collective-permute-start | bytes 466952 | tf_op jit(solution)/shard_map/ppermute | solution.py:35
  31.1 1.8 %collective-permute-start.13 = (bf16[288,256]{1,0:T(8,128)(2,1)S(1)}, bf16[288,256]{1,0:T(8,128)(2,1)S(1)}, u32[]{:S(2)}, u32[]{:S(2)}) collective-permute-start(bf16[288,256]{1,0:T(8,128)(2,1)S(1)} %get-tuple-element.38), channel_id=1, source_target_pairs={{0,8},{4,12},{8,0},{12,4},{16,20},{20,16},{24,28},{28,24},{1,9},{5... | collective-permute-start | bytes 442376 | tf_op jit(solution)/shard_map/ppermute | solution.py:35
  32.9 0.0 copy-start.2
  32.9 0.8 %collective-permute-start.17 = (bf16[256,256]{1,0:T(8,128)(2,1)S(1)}, bf16[256,256]{1,0:T(8,128)(2,1)S(1)}, u32[]{:S(2)}, u32[]{:S(2)}) collective-permute-start(bf16[256,256]{1,0:T(8,128)(2,1)S(1)} %strip.1.refs_0_), channel_id=1, source_target_pairs={{0,12},{4,8},{8,4},{12,0},{1,13},{5,9},{9,5},{13,1},{2,14},{6,10},... | collective-permute-start | bytes 393224 | tf_op jit(solution)/shard_map/ppermute | solution.py:39
  33.7 0.0 collective-permute-done.11.refs_6_
  33.7 1.2 %collective-permute-start.16 = (bf16[256,256]{1,0:T(8,128)(2,1)S(1)}, bf16[256,256]{1,0:T(8,128)(2,1)S(1)}, u32[]{:S(2)}, u32[]{:S(2)}) collective-permute-start(bf16[256,256]{1,0:T(8,128)(2,1)S(1)} %strip.1.refs_0_), channel_id=1, source_target_pairs={{0,8},{4,12},{8,0},{12,4},{16,20},{20,16},{24,28},{28,24},{1,9},{5... | collective-permute-start | bytes 393224 | tf_op jit(solution)/shard_map/ppermute | solution.py:35
  34.9 0.0 collective-permute-done.10.refs_5_
  34.9 1.6 %collective-permute-start.15 = (bf16[256,256]{1,0:T(8,128)(2,1)S(1)}, bf16[256,256]{1,0:T(8,128)(2,1)S(1)}, u32[]{:S(2)}, u32[]{:S(2)}) collective-permute-start(bf16[256,256]{1,0:T(8,128)(2,1)S(1)} %strip.1.refs_0_), channel_id=1, source_target_pairs={{0,4},{4,0},{8,12},{12,8},{16,24},{20,28},{24,16},{28,20},{1,5},{5... | collective-permute-start | bytes 393224 | tf_op jit(solution)/shard_map/ppermute | solution.py:35
  37.2 3.0 %collective-permute-done.13.refs_8_ = bf16[288,256]{1,0:T(8,128)(2,1)S(1)} collective-permute-done((bf16[288,256]{1,0:T(8,128)(2,1)S(1)}, bf16[288,256]{1,0:T(8,128)(2,1)S(1)}, u32[]{:S(2)}, u32[]{:S(2)}) %collective-permute-start.13) | collective-permute-done | bytes 147488 | tf_op jit(solution)/shard_map/ppermute | solution.py:35
  40.2 0.0 collective-permute-done.14.refs_9_
  40.2 3.7 %root.1 = (f32[256,1024]{1,0:T(8,128)}, bf16[256,1024]{1,0:T(8,128)(2,1)}, f32[8,128]{1,0:T(8,128)S(1)}) custom-call(s32[1,1]{1,0:T(1,128)S(6)} %copy.8.refs_0_, f32[576,256]{1,0:T(8,128)S(1)} %get-tuple-element.30.refs_1_, bf16[288,256]{1,0:T(8,128)(2,1)S(1)} %get-tuple-element.31.refs_3_.refs_2_, bf16[304,256]{1,0:T(8,128)(2,1)S(1)} %get-tuple-element.32.refs_4_.refs_3_, ...), custom_call_target="tpu_custom_call" | custom-call | tf_op jit(solution)/shard_map/root/pallas_call | solution.py:343
  43.9 0.0 collective-permute-done.17.refs_3_
  43.9 0.0 collective-permute-done.16.refs_2_
  44.0 0.0 collective-permute-done.15.refs_1_
  44.0 0.0 copy-done.2
  44.0 1.0 %step.1 = bf16[256,256]{1,0:T(8,128)(2,1)} custom-call(bf16[256,256]{1,0:T(8,128)(2,1)S(1)} %strip.1.refs_0_, bf16[256,256]{1,0:T(8,128)(2,1)S(1)} %collective-permute-done.15.refs_1_, bf16[256,256]{1,0:T(8,128)(2,1)S(1)} %collective-permute-done.16.refs_2_, bf16[256,256]{1,0:T(8,128)(2,1)S(1)} %collective-permute-done.17.refs_3_, ...), custom_call_target="tpu_custom_call" | custom-call | tf_op jit(solution)/shard_map/step/pallas_call | solution.py:343
  (2 shorter events, 0.1 us)
Async XLA Ops:
  0.6 14.3 %collective-permute-start.6 = (bf16[1,512,256]{2,1,0:T(8,128)(2,1)}, bf16[1,512,256]{2,1,0:T(8,128)(2,1)S(1)}, u32[]{:S(2)}, u32[]{:S(2)}) collective-permute-start(bf16[1,512,256]{2,1,0:T(8,128)(2,1)} %param.6), channel_id=1, source_target_pairs={{16,0},{0,16},{17,1},{1,17},{18,2},{2,18},{19,3},{3,19},{20,4},{4,... | collective-permute-start | bytes 786440 | tf_op jit(solution)/shard_map/ppermute | solution.py:22
  1.1 1.2 %copy-start = (bf16[1,512,1024]{2,1,0:T(8,128)(2,1)S(1)}, bf16[1,512,1024]{2,1,0:T(8,128)(2,1)}, u32[]{:S(2)}) copy-start(bf16[1,512,1024]{2,1,0:T(8,128)(2,1)} %param.5) | copy-start | bytes 3145732
  3.4 6.1 %collective-permute-start.2 = (bf16[288,256]{1,0:T(8,128)(2,1)S(1)}, bf16[288,256]{1,0:T(8,128)(2,1)S(1)}, u32[]{:S(2)}, u32[]{:S(2)}) collective-permute-start(bf16[288,256]{1,0:T(8,128)(2,1)S(1)} %get-tuple-element.26), channel_id=1, source_target_pairs={{0,4},{4,0},{8,12},{12,8},{16,24},{20,28},{24,16},{28,20},{1,5},{5... | collective-permute-start | bytes 442376 | tf_op jit(solution)/shard_map/ppermute | solution.py:35
  6.0 6.3 %collective-permute-start.3 = (bf16[288,256]{1,0:T(8,128)(2,1)S(1)}, bf16[288,256]{1,0:T(8,128)(2,1)S(1)}, u32[]{:S(2)}, u32[]{:S(2)}) collective-permute-start(bf16[288,256]{1,0:T(8,128)(2,1)S(1)} %get-tuple-element.27), channel_id=1, source_target_pairs={{0,8},{4,12},{8,0},{12,4},{16,20},{20,16},{24,28},{28,24},{1,9},{5... | collective-permute-start | bytes 442376 | tf_op jit(solution)/shard_map/ppermute | solution.py:35
  7.5 9.1 %collective-permute-start = (bf16[288,256]{1,0:T(8,128)(2,1)S(1)}, bf16[288,256]{1,0:T(8,128)(2,1)S(1)}, u32[]{:S(2)}, u32[]{:S(2)}) collective-permute-start(bf16[288,256]{1,0:T(8,128)(2,1)S(1)} %get-tuple-element.24), channel_id=1, source_target_pairs={{0,4},{4,0},{8,12},{12,8},{16,24},{20,28},{24,16},{28,20},{1,5},{5... | collective-permute-start | bytes 442376 | tf_op jit(solution)/shard_map/ppermute | solution.py:35
  8.1 9.0 %collective-permute-start.1 = (bf16[288,256]{1,0:T(8,128)(2,1)S(1)}, bf16[288,256]{1,0:T(8,128)(2,1)S(1)}, u32[]{:S(2)}, u32[]{:S(2)}) collective-permute-start(bf16[288,256]{1,0:T(8,128)(2,1)S(1)} %get-tuple-element.25), channel_id=1, source_target_pairs={{0,8},{4,12},{8,0},{12,4},{16,20},{20,16},{24,28},{28,24},{1,9},{5... | collective-permute-start | bytes 442376 | tf_op jit(solution)/shard_map/ppermute | solution.py:35
  12.3 7.0 %copy-start.1 = (f32[1,1,256,1024]{3,2,1,0:T(8,128)S(1)}, f32[1,1,256,1024]{3,2,1,0:T(8,128)}, u32[]{:S(2)}) copy-start(f32[1,1,256,1024]{3,2,1,0:T(8,128)} %param.7) | copy-start | bytes 3145732
  12.4 5.4 %collective-permute-start.4 = (bf16[288,256]{1,0:T(8,128)(2,1)S(1)}, bf16[288,256]{1,0:T(8,128)(2,1)S(1)}, u32[]{:S(2)}, u32[]{:S(2)}) collective-permute-start(bf16[288,256]{1,0:T(8,128)(2,1)S(1)} %get-tuple-element.28.refs_2_), channel_id=1, source_target_pairs={{0,4},{4,0},{8,12},{12,8},{16,24},{20,28},{24,16},{28,20},{1,5},{5... | collective-permute-start | bytes 442376 | tf_op jit(solution)/shard_map/ppermute | solution.py:35
  12.9 6.5 %collective-permute-start.5 = (bf16[288,256]{1,0:T(8,128)(2,1)S(1)}, bf16[288,256]{1,0:T(8,128)(2,1)S(1)}, u32[]{:S(2)}, u32[]{:S(2)}) collective-permute-start(bf16[288,256]{1,0:T(8,128)(2,1)S(1)} %get-tuple-element.29.refs_3_), channel_id=1, source_target_pairs={{0,8},{4,12},{8,0},{12,4},{16,20},{20,16},{24,28},{28,24},{1,9},{5... | collective-permute-start | bytes 442376 | tf_op jit(solution)/shard_map/ppermute | solution.py:35
  15.4 5.5 %collective-permute-start.7 = (bf16[256,256]{1,0:T(8,128)(2,1)S(1)}, bf16[256,256]{1,0:T(8,128)(2,1)S(1)}, u32[]{:S(2)}, u32[]{:S(2)}) collective-permute-start(bf16[256,256]{1,0:T(8,128)(2,1)S(1)} %get-tuple-element.34), channel_id=1, source_target_pairs={{0,4},{4,0},{8,12},{12,8},{16,24},{20,28},{24,16},{28,20},{1,5},{5... | collective-permute-start | bytes 393224 | tf_op jit(solution)/shard_map/ppermute | solution.py:35
  16.6 5.0 %collective-permute-start.8 = (bf16[256,256]{1,0:T(8,128)(2,1)S(1)}, bf16[256,256]{1,0:T(8,128)(2,1)S(1)}, u32[]{:S(2)}, u32[]{:S(2)}) collective-permute-start(bf16[256,256]{1,0:T(8,128)(2,1)S(1)} %get-tuple-element.35), channel_id=1, source_target_pairs={{0,8},{4,12},{8,0},{12,4},{16,20},{20,16},{24,28},{28,24},{1,9},{5... | collective-permute-start | bytes 393224 | tf_op jit(solution)/shard_map/ppermute | solution.py:35
  21.7 8.3 %collective-permute-start.12 = (bf16[432,256]{1,0:T(8,128)(2,1)S(1)}, bf16[432,256]{1,0:T(8,128)(2,1)S(1)}, u32[]{:S(2)}, u32[]{:S(2)}) collective-permute-start(bf16[432,256]{1,0:T(8,128)(2,1)S(1)} %get-tuple-element.37), channel_id=1, source_target_pairs={{0,8},{4,12},{8,0},{12,4},{16,20},{20,16},{24,28},{28,24},{1,9},{5... | collective-permute-start | bytes 663560 | tf_op jit(solution)/shard_map/ppermute | solution.py:35
  22.9 7.0 %collective-permute-start.9 = (bf16[416,256]{1,0:T(8,128)(2,1)S(1)}, bf16[416,256]{1,0:T(8,128)(2,1)S(1)}, u32[]{:S(2)}, u32[]{:S(2)}) collective-permute-start(bf16[416,256]{1,0:T(8,128)(2,1)S(1)} %get-tuple-element.36), channel_id=1, source_target_pairs={{0,4},{4,0},{8,12},{12,8},{16,24},{20,28},{24,16},{28,20},{1,5},{5... | collective-permute-start | bytes 638984 | tf_op jit(solution)/shard_map/ppermute | solution.py:35
  24.2 10.7 %collective-permute-start.10 = (bf16[304,256]{1,0:T(8,128)(2,1)S(1)}, bf16[304,256]{1,0:T(8,128)(2,1)S(1)}, u32[]{:S(2)}, u32[]{:S(2)}) collective-permute-start(bf16[304,256]{1,0:T(8,128)(2,1)S(1)} %get-tuple-element.32.refs_4_.refs_3_), channel_id=1, source_target_pairs={{0,4},{4,0},{8,12},{12,8},{16,24},{20,28},{24,16},{28,20},{1,5},{5... | collective-permute-start | bytes 466952 | tf_op jit(solution)/shard_map/ppermute | solution.py:35
  24.9 8.8 %collective-permute-start.11 = (bf16[288,256]{1,0:T(8,128)(2,1)S(1)}, bf16[288,256]{1,0:T(8,128)(2,1)S(1)}, u32[]{:S(2)}, u32[]{:S(2)}) collective-permute-start(bf16[288,256]{1,0:T(8,128)(2,1)S(1)} %get-tuple-element.31.refs_3_.refs_2_), channel_id=1, source_target_pairs={{0,8},{4,12},{8,0},{12,4},{16,20},{20,16},{24,28},{28,24},{1,9},{5... | collective-permute-start | bytes 442376 | tf_op jit(solution)/shard_map/ppermute | solution.py:35
  30.0 10.2 %collective-permute-start.14 = (bf16[304,256]{1,0:T(8,128)(2,1)S(1)}, bf16[304,256]{1,0:T(8,128)(2,1)S(1)}, u32[]{:S(2)}, u32[]{:S(2)}) collective-permute-start(bf16[304,256]{1,0:T(8,128)(2,1)S(1)} %get-tuple-element.39.refs_5_), channel_id=1, source_target_pairs={{0,4},{4,0},{8,12},{12,8},{16,24},{20,28},{24,16},{28,20},{1,5},{5... | collective-permute-start | bytes 466952 | tf_op jit(solution)/shard_map/ppermute | solution.py:35
  31.1 9.1 %collective-permute-start.13 = (bf16[288,256]{1,0:T(8,128)(2,1)S(1)}, bf16[288,256]{1,0:T(8,128)(2,1)S(1)}, u32[]{:S(2)}, u32[]{:S(2)}) collective-permute-start(bf16[288,256]{1,0:T(8,128)(2,1)S(1)} %get-tuple-element.38), channel_id=1, source_target_pairs={{0,8},{4,12},{8,0},{12,4},{16,20},{20,16},{24,28},{28,24},{1,9},{5... | collective-permute-start | bytes 442376 | tf_op jit(solution)/shard_map/ppermute | solution.py:35
  32.9 11.0 %copy-start.2 = (bf16[1,1,256,1024]{3,2,1,0:T(8,128)(2,1)S(1)}, bf16[1,1,256,1024]{3,2,1,0:T(8,128)(2,1)}, u32[]{:S(2)}) copy-start(bf16[1,1,256,1024]{3,2,1,0:T(8,128)(2,1)} %param.8) | copy-start | bytes 1572868
  32.9 11.0 %collective-permute-start.17 = (bf16[256,256]{1,0:T(8,128)(2,1)S(1)}, bf16[256,256]{1,0:T(8,128)(2,1)S(1)}, u32[]{:S(2)}, u32[]{:S(2)}) collective-permute-start(bf16[256,256]{1,0:T(8,128)(2,1)S(1)} %strip.1.refs_0_), channel_id=1, source_target_pairs={{0,12},{4,8},{8,4},{12,0},{1,13},{5,9},{9,5},{13,1},{2,14},{6,10},... | collective-permute-start | bytes 393224 | tf_op jit(solution)/shard_map/ppermute | solution.py:39
  33.7 10.2 %collective-permute-start.16 = (bf16[256,256]{1,0:T(8,128)(2,1)S(1)}, bf16[256,256]{1,0:T(8,128)(2,1)S(1)}, u32[]{:S(2)}, u32[]{:S(2)}) collective-permute-start(bf16[256,256]{1,0:T(8,128)(2,1)S(1)} %strip.1.refs_0_), channel_id=1, source_target_pairs={{0,8},{4,12},{8,0},{12,4},{16,20},{20,16},{24,28},{28,24},{1,9},{5... | collective-permute-start | bytes 393224 | tf_op jit(solution)/shard_map/ppermute | solution.py:35
  34.9 9.1 %collective-permute-start.15 = (bf16[256,256]{1,0:T(8,128)(2,1)S(1)}, bf16[256,256]{1,0:T(8,128)(2,1)S(1)}, u32[]{:S(2)}, u32[]{:S(2)}) collective-permute-start(bf16[256,256]{1,0:T(8,128)(2,1)S(1)} %strip.1.refs_0_), channel_id=1, source_target_pairs={{0,4},{4,0},{8,12},{12,8},{16,24},{20,28},{24,16},{28,20},{1,5},{5... | collective-permute-start | bytes 393224 | tf_op jit(solution)/shard_map/ppermute | solution.py:35

commit v11 on v9

--- a/solution.py
+++ b/solution.py
@@ -58,8 +58,44 @@
 
 
 def chunk_rows(share):
-    half = share // 2
-    return [0, half, half + half // 2] + [half + half // 2 + half * i for i in range(1, 4)]
+    half, packed = share // 2, 5 * share // 8
+    return [0] + [packed + half * i for i in range(4)]
+
+
+def packed_upper(block):
+    quarter = block.shape[0] // 4
+    column = lax.broadcasted_iota(jnp.int32, (quarter, 4 * quarter), 1)
+    second = pltpu.roll(block[quarter : 2 * quarter], 3 * quarter, 1)
+    third = block[2 * quarter : 3 * quarter, 2 * quarter :]
+    return jnp.concatenate(
+        [
+            block[0:quarter],
+            jnp.where(column < 3 * quarter, second, block[3 * quarter :]),
+            jnp.concatenate([third[0 : quarter // 2], third[quarter // 2 :]], axis=1),
+        ],
+        axis=0,
+    )
+
+
+def unpacked(packed):
+    share = packed.shape[1]
+    quarter = share // 4
+    column = lax.broadcasted_iota(jnp.int32, (quarter, share), 1)
+    second = packed[quarter : 2 * quarter]
+    third = packed[2 * quarter :]
+    third = jnp.concatenate([third[:, 0 : 2 * quarter], third[:, 2 * quarter :]], axis=0)
+    upper = jnp.concatenate(
+        [
+            packed[0:quarter],
+            jnp.where(column < quarter, 0.0, pltpu.roll(second, quarter, 1)),
+            jnp.concatenate([jnp.zeros((quarter, 2 * quarter), F32), third], axis=1),
+            jnp.where(column < 3 * quarter, 0.0, second),
+        ],
+        axis=0,
+    )
+    rows = lax.broadcasted_iota(jnp.int32, (share, share), 0) // quarter
+    columns = lax.broadcasted_iota(jnp.int32, (share, share), 1) // quarter
+    return upper + jnp.where(rows == columns, 0.0, upper).T
 
 
 def shared_half(owner, offset, share):
@@ -95,11 +131,8 @@
     def pieces(offset):
         owner = mine ^ offset
         base = pl.multiple_of(owner * share, share)
-        corner = pl.multiple_of(owner * share + half, half)
-        yield 0, batch[pl.ds(base, half), pl.ds(base, share)]
-        low = batch[pl.ds(corner, half), pl.ds(corner, half)]
-        yield starts[1], jnp.concatenate([low[0 : half // 2], low[half // 2 :]], axis=1)
-        for start, step in zip(starts[2:], offsets()[1:]):
+        yield 0, packed_upper(batch[pl.ds(base, share), pl.ds(base, share)])
+        for start, step in zip(starts[1:], offsets()[1:]):
             row, col = shared_half(owner, step, share)
             yield start, batch[pl.ds(row, half), pl.ds(col, share)]
 
@@ -166,30 +199,19 @@
         axis=0,
     )
     diagonal = old[:, pl.ds(pl.multiple_of(mine * share, share), share)]
-    eye = eye_of(half, share)
-    low_eye = eye_of(half, half)
-
-    def packed(low):
-        return jnp.concatenate([low[0 : half // 2], low[half // 2 :]], axis=1)
-
-    terms = [
-        DECAY * diagonal[0:half] + DAMPING * eye,
-        packed(DECAY * diagonal[half:, half:] + DAMPING * low_eye),
-    ]
-    for step in offsets()[1:]:
+    block_sum = unpacked(total[0 : starts[1]])
+    value = DECAY * diagonal + (1.0 - DECAY) * block_sum + DAMPING * eye_of(share, share)
+    exact[0:share, :] = value
+    squares = jnp.sum(value * value, axis=0, keepdims=True)
+    values = [packed_upper(value).astype(BF16)]
+    for position, step in enumerate(offsets()[1:]):
         other = mine ^ step
         block = old[:, pl.ds(pl.multiple_of(other * share, share), share)]
-        terms.append(DECAY * jnp.where(mine < other, block[0:half], block[:, half:].T))
-    column = lax.broadcasted_iota(jnp.int32, (1, share), 1)
-    squares = jnp.zeros((1, share), F32)
-    values = []
-    for position, (start, term) in enumerate(zip(starts, terms)):
-        value = term + (1.0 - DECAY) * total[start : start + term.shape[0]]
-        exact[start : start + term.shape[0], :] = value
-        summed = jnp.sum(value * value, axis=0, keepdims=True)
-        if position == 0:
-            summed = jnp.where(column < half, summed, 2.0 * summed)
-        squares = squares + (summed if position < 2 else 2.0 * summed)
+        term = DECAY * jnp.where(mine < other, block[0:half], block[:, half:].T)
+        start = starts[1 + position]
+        value = term + (1.0 - DECAY) * total[start : start + half]
+        exact[share + position * half : share + (position + 1) * half, :] = value
+        squares = squares + 2.0 * jnp.sum(value * value, axis=0, keepdims=True)
         values.append(value.astype(BF16))
     high = squares.astype(BF16).astype(F32)
     middle = (squares - high).astype(BF16).astype(F32)
@@ -219,19 +241,15 @@
             return lower[start - length : start - length + count, :]
         return jnp.concatenate([upper[start:length, :], lower[0 : start + count - length, :]], axis=0)
 
-    top = exact[0:half, :]
-    low = exact[starts[1] : starts[2], :]
-    low = jnp.concatenate([low[:, 0:half], low[:, half:]], axis=0)
     copies = []
     for position, step in enumerate(offsets()):
         other = mine ^ step
         target = rows.at[position]
         if position == 0:
-            target[0:half, :] = top
-            target[half:, :] = jnp.concatenate([top[:, half:].T, low], axis=1)
+            target[...] = exact[0:share, :]
         else:
-            start = starts[1 + position]
-            own = exact[start : start + half, :]
+            start = starts[position]
+            own = exact[share + (position - 1) * half : share + position * half, :]
             theirs = rows_of(position, start, half).astype(F32)
 
             @pl.when(mine < other)
@@ -248,20 +266,14 @@
         copies[-1].start()
 
     squares = jnp.zeros((16, share), F32)
-    low_eye = eye_of(half, half)
+    block_eye = eye_of(share, share)
     for position, offset in enumerate(offsets()):
         owner = mine ^ offset
-        base = pl.multiple_of(owner * share, share)
-        corner = pl.multiple_of(owner * share + half, half)
-        top = rows_of(position, 0, half)
-        low = rows_of(position, starts[1], half // 2)
-        low = jnp.concatenate([low[:, 0:half], low[:, half:]], axis=0)
-        factor[pl.ds(base, half), pl.ds(base, share)] = top
-        factor[pl.ds(corner, half), pl.ds(base, half)] = transposed(top[:, half:])
-        factor[pl.ds(corner, half), pl.ds(corner, half)] = low
-        diagonal[:, pl.ds(base, half)] = jnp.sum(top[:, 0:half].astype(F32) * low_eye, axis=0, keepdims=True)
-        diagonal[:, pl.ds(corner, half)] = jnp.sum(low.astype(F32) * low_eye, axis=0, keepdims=True)
-        for start, step in zip(starts[2:], offsets()[1:]):
+        own_band = pl.ds(pl.multiple_of(owner * share, share), share)
+        block = unpacked(rows_of(position, 0, starts[1]).astype(F32))
+        factor[own_band, own_band] = block.astype(BF16)
+        diagonal[:, own_band] = jnp.sum(block * block_eye, axis=0, keepdims=True)
+        for start, step in zip(starts[1:], offsets()[1:]):
             row, col = shared_half(owner, step, share)
             block = rows_of(position, start, half)
             factor[pl.ds(row, half), pl.ds(col, share)] = block
@@ -366,7 +378,7 @@
     grad_x, grad_y = swapped(grad_x, 0), swapped(grad_y, 1)
     upper, lower, exact = call(
         functools.partial(factor_kernel, replicas),
-        [shape(length), shape(length + 16), shape(whole_rows, F32)],
+        [shape(length), shape(length + 16), shape(5 * share // 2, F32)],
         "factor",
         keep,
         direct_x,
@@ -391,7 +403,7 @@
         grad_y,
         strip_x,
         strip_y,
-        after=[upper_x, lower_y],
+        after=[lower_x, upper_y],
     )
     strips = [strip, swapped(strip, 0), swapped(strip, 1), swapped_across(strip)]
     factor, root, finished = call(

time: 41.9 us -> 44.2 us (1.055)
  waiting for transfers between devices: 9.43 us -> 13.9 us
  starting transfers between devices: 23 us -> 20.6 us
    ppermute x18, waiting for transfers between devices: 8.97 us -> 13.9 us  [swapped(): return lax.ppermute(block, ('pipe', 'dp'), route)]
    ppermute x18, starting transfers between devices: 21.5 us -> 17.3 us  [swapped(): return lax.ppermute(block, ('pipe', 'dp'), route)]
    ppermute x1, starting transfers between devices: 0.99 us -> 2.77 us  [swapped_across(): lax.ppermute(block, 'dp', [(i, i ^ 3) for i in range(lax.axis_size('dp'))])]
    ppermute x1, waiting for transfers between devices: 0.46 us -> 0.01 us  [swapped_across(): lax.ppermute(block, 'dp', [(i, i ^ 3) for i in range(lax.axis_size('dp'))])]
  transfers between devices with their start and end apart: 20 -> 20, of which waited for: 7 -> 8; matrix products, arithmetic and copies ran while one was open for 0% -> 0% of each run, Pallas kernels for 14% -> 14%
where the time goes in v11:
time: 44.2 us; the launch traced here: 44.1 us
  starting transfers between devices  20.6 us (47%)
  waiting for transfers between devices  13.9 us (31%)
  Pallas kernels  6.99 us (16%)
  between operations  1.41 us (3%)
  local copies, waits for them, and re-layouts  1.24 us (3%)
    ppermute x18, starting transfers between devices, swapped(): return lax.ppermute(block, ('pipe', 'dp'), route)  17.3 us
    ppermute x18, waiting for transfers between devices, swapped(): return lax.ppermute(block, ('pipe', 'dp'), route)  13.9 us
    pallas_call x8, Pallas kernels, call(): pl.pallas_call(body, out_shape=outs, in_specs=in_specs, out_specs=out_spe...  6.99 us
    ppermute x1, starting transfers between devices, swapped_across(): lax.ppermute(block, 'dp', [(i, i ^ 3) for i in range(lax.axis_size('dp'))])  2.77 us
    unnamed x6, local copies, waits for them, and re-layouts  1.24 us
  transfers between devices with their start and end apart: 20, of which 8 were waited for; matrix products, arithmetic and copies ran while one was open for 0% of the time, Pallas kernels for 14%

profile of v11, /device:TPU:0, one launch (start us, length us, event | category | flops | bytes accessed | tf_op | source)
XLA Modules:
  0.0 44.1 jit_solution(12328043583587416340)
XLA Ops:
  0.6 0.5 %collective-permute-start.12 = (bf16[1,512,256]{2,1,0:T(8,128)(2,1)}, bf16[1,512,256]{2,1,0:T(8,128)(2,1)S(1)}, u32[]{:S(2)}, u32[]{:S(2)}) collective-permute-start(bf16[1,512,256]{2,1,0:T(8,128)(2,1)} %param.6), channel_id=1, source_target_pairs={{16,0},{0,16},{17,1},{1,17},{18,2},{2,18},{19,3},{3,19},{20,4},{4,... | collective-permute-start | bytes 786440 | tf_op jit(solution)/shard_map/ppermute | solution.py:22
  1.1 0.0 copy-start
  1.1 1.2 %copy-done = bf16[1,512,1024]{2,1,0:T(8,128)(2,1)S(1)} copy-done((bf16[1,512,1024]{2,1,0:T(8,128)(2,1)S(1)}, bf16[1,512,1024]{2,1,0:T(8,128)(2,1)}, u32[]{:S(2)}) %copy-start) | copy-done | bytes 1048600
  2.4 1.1 %batch.1 = (bf16[272,256]{1,0:T(8,128)(2,1)S(1)}, bf16[272,256]{1,0:T(8,128)(2,1)S(1)}, bf16[272,256]{1,0:T(8,128)(2,1)S(1)}, bf16[272,256]{1,0:T(8,128)(2,1)S(1)}, f32[1088,256]{1,0:T(8,128)S(1)}) custom-call(bf16[512,1024]{1,0:T(8,128)(2,1)S(1)} %bitcast.7), custom_call_target="tpu_custom_call" | custom-call | tf_op jit(solution)/shard_map/batch/pallas_call | solution.py:347
  3.5 2.6 %collective-permute-start.2 = (bf16[272,256]{1,0:T(8,128)(2,1)S(1)}, bf16[272,256]{1,0:T(8,128)(2,1)S(1)}, u32[]{:S(2)}, u32[]{:S(2)}) collective-permute-start(bf16[272,256]{1,0:T(8,128)(2,1)S(1)} %get-tuple-element.24), channel_id=1, source_target_pairs={{0,4},{4,0},{8,12},{12,8},{16,24},{20,28},{24,16},{28,20},{1,5},{5... | collective-permute-start | bytes 417800 | tf_op jit(solution)/shard_map/ppermute | solution.py:35
  6.1 1.5 %collective-permute-start.3 = (bf16[272,256]{1,0:T(8,128)(2,1)S(1)}, bf16[272,256]{1,0:T(8,128)(2,1)S(1)}, u32[]{:S(2)}, u32[]{:S(2)}) collective-permute-start(bf16[272,256]{1,0:T(8,128)(2,1)S(1)} %get-tuple-element.25), channel_id=1, source_target_pairs={{0,8},{4,12},{8,0},{12,4},{16,20},{20,16},{24,28},{28,24},{1,9},{5... | collective-permute-start | bytes 417800 | tf_op jit(solution)/shard_map/ppermute | solution.py:35
  7.6 0.5 %collective-permute-start = (bf16[272,256]{1,0:T(8,128)(2,1)S(1)}, bf16[272,256]{1,0:T(8,128)(2,1)S(1)}, u32[]{:S(2)}, u32[]{:S(2)}) collective-permute-start(bf16[272,256]{1,0:T(8,128)(2,1)S(1)} %get-tuple-element.22), channel_id=1, source_target_pairs={{0,4},{4,0},{8,12},{12,8},{16,24},{20,28},{24,16},{28,20},{1,5},{5... | collective-permute-start | bytes 417800 | tf_op jit(solution)/shard_map/ppermute | solution.py:35
  8.1 0.1 collective-permute-start.1
  8.2 1.2 %collective-permute-done.2.refs_1_ = bf16[272,256]{1,0:T(8,128)(2,1)S(1)} collective-permute-done((bf16[272,256]{1,0:T(8,128)(2,1)S(1)}, bf16[272,256]{1,0:T(8,128)(2,1)S(1)}, u32[]{:S(2)}, u32[]{:S(2)}) %collective-permute-start.2) | collective-permute-done | bytes 139296 | tf_op jit(solution)/shard_map/ppermute | solution.py:35
  9.4 2.8 %collective-permute-done.3.refs_2_ = bf16[272,256]{1,0:T(8,128)(2,1)S(1)} collective-permute-done((bf16[272,256]{1,0:T(8,128)(2,1)S(1)}, bf16[272,256]{1,0:T(8,128)(2,1)S(1)}, u32[]{:S(2)}, u32[]{:S(2)}) %collective-permute-start.3) | collective-permute-done | bytes 139296 | tf_op jit(solution)/shard_map/ppermute | solution.py:35
  12.2 0.1 relay.1
  12.2 0.0 copy-start.1
  12.3 0.5 %collective-permute-start.4 = (bf16[272,256]{1,0:T(8,128)(2,1)S(1)}, bf16[272,256]{1,0:T(8,128)(2,1)S(1)}, u32[]{:S(2)}, u32[]{:S(2)}) collective-permute-start(bf16[272,256]{1,0:T(8,128)(2,1)S(1)} %get-tuple-element.26.refs_2_), channel_id=1, source_target_pairs={{0,4},{4,0},{8,12},{12,8},{16,24},{20,28},{24,16},{28,20},{1,5},{5... | collective-permute-start | bytes 417800 | tf_op jit(solution)/shard_map/ppermute | solution.py:35
  12.7 2.0 %collective-permute-start.5 = (bf16[272,256]{1,0:T(8,128)(2,1)S(1)}, bf16[272,256]{1,0:T(8,128)(2,1)S(1)}, u32[]{:S(2)}, u32[]{:S(2)}) collective-permute-start(bf16[272,256]{1,0:T(8,128)(2,1)S(1)} %get-tuple-element.27.refs_3_), channel_id=1, source_target_pairs={{0,8},{4,12},{8,0},{12,4},{16,20},{20,16},{24,28},{28,24},{1,9},{5... | collective-permute-start | bytes 417800 | tf_op jit(solution)/shard_map/ppermute | solution.py:35
  14.8 0.0 collective-permute-done.12
  14.8 0.5 %grad.1 = (bf16[256,256]{1,0:T(8,128)(2,1)S(1)}, bf16[256,256]{1,0:T(8,128)(2,1)S(1)}, f32[512,256]{1,0:T(8,128)S(1)}) custom-call(bf16[512,1024]{1,0:T(8,128)(2,1)S(1)} %bitcast.8, bf16[512,256]{1,0:T(8,128)(2,1)S(1)} %bitcast.11, bf16[272,256]{1,0:T(8,128)(2,1)S(1)} %get-tuple-element.26.refs_2_, bf16[272,256]{1,0:T(8,128)(2,1)S(1)} %get-tuple-element.27.refs_3_), custom_call_target="tpu_custom_call" | custom-call | tf_op jit(solution)/shard_map/grad/pallas_call | solution.py:347
  15.3 1.1 %collective-permute-start.13 = (bf16[256,256]{1,0:T(8,128)(2,1)S(1)}, bf16[256,256]{1,0:T(8,128)(2,1)S(1)}, u32[]{:S(2)}, u32[]{:S(2)}) collective-permute-start(bf16[256,256]{1,0:T(8,128)(2,1)S(1)} %get-tuple-element.34), channel_id=1, source_target_pairs={{0,4},{4,0},{8,12},{12,8},{16,24},{20,28},{24,16},{28,20},{1,5},{5... | collective-permute-start | bytes 393224 | tf_op jit(solution)/shard_map/ppermute | solution.py:35
  16.4 0.0 collective-permute-done.refs_1_
  16.4 0.0 collective-permute-done.1.refs_2_
  16.4 1.1 %collective-permute-done.4.refs_3_ = bf16[272,256]{1,0:T(8,128)(2,1)S(1)} collective-permute-done((bf16[272,256]{1,0:T(8,128)(2,1)S(1)}, bf16[272,256]{1,0:T(8,128)(2,1)S(1)}, u32[]{:S(2)}, u32[]{:S(2)}) %collective-permute-start.4) | collective-permute-done | bytes 139296 | tf_op jit(solution)/shard_map/ppermute | solution.py:35
  17.5 1.6 %collective-permute-done.5.refs_4_ = bf16[272,256]{1,0:T(8,128)(2,1)S(1)} collective-permute-done((bf16[272,256]{1,0:T(8,128)(2,1)S(1)}, bf16[272,256]{1,0:T(8,128)(2,1)S(1)}, u32[]{:S(2)}, u32[]{:S(2)}) %collective-permute-start.5) | collective-permute-done | bytes 139296 | tf_op jit(solution)/shard_map/ppermute | solution.py:35
  19.1 0.0 copy-done.1
  19.1 0.4 factor.1
  19.5 1.6 %collective-permute-start.6 = (bf16[272,256]{1,0:T(8,128)(2,1)S(1)}, bf16[272,256]{1,0:T(8,128)(2,1)S(1)}, u32[]{:S(2)}, u32[]{:S(2)}) collective-permute-start(bf16[272,256]{1,0:T(8,128)(2,1)S(1)} %get-tuple-element.29.refs_2_.refs_3_), channel_id=1, source_target_pairs={{0,4},{4,0},{8,12},{12,8},{16,24},{20,28},{24,16},{28,20},{1,5},{5... | collective-permute-start | bytes 417800 | tf_op jit(solution)/shard_map/ppermute | solution.py:35
  21.1 0.9 %collective-permute-start.14 = (bf16[256,256]{1,0:T(8,128)(2,1)S(1)}, bf16[256,256]{1,0:T(8,128)(2,1)S(1)}, u32[]{:S(2)}, u32[]{:S(2)}) collective-permute-start(bf16[256,256]{1,0:T(8,128)(2,1)S(1)} %get-tuple-element.35), channel_id=1, source_target_pairs={{0,8},{4,12},{8,0},{12,4},{16,20},{20,16},{24,28},{28,24},{1,9},{5... | collective-permute-start | bytes 393224 | tf_op jit(solution)/shard_map/ppermute | solution.py:35
  21.9 1.2 %collective-permute-start.9 = (bf16[288,256]{1,0:T(8,128)(2,1)S(1)}, bf16[288,256]{1,0:T(8,128)(2,1)S(1)}, u32[]{:S(2)}, u32[]{:S(2)}) collective-permute-start(bf16[288,256]{1,0:T(8,128)(2,1)S(1)} %get-tuple-element.30.refs_3_.refs_4_), channel_id=1, source_target_pairs={{0,8},{4,12},{8,0},{12,4},{16,20},{20,16},{24,28},{28,24},{1,9},{5... | collective-permute-start | bytes 442376 | tf_op jit(solution)/shard_map/ppermute | solution.py:35
  23.1 0.9 %collective-permute-start.8 = (bf16[272,256]{1,0:T(8,128)(2,1)S(1)}, bf16[272,256]{1,0:T(8,128)(2,1)S(1)}, u32[]{:S(2)}, u32[]{:S(2)}) collective-permute-start(bf16[272,256]{1,0:T(8,128)(2,1)S(1)} %get-tuple-element.29.refs_2_.refs_3_), channel_id=1, source_target_pairs={{0,8},{4,12},{8,0},{12,4},{16,20},{20,16},{24,28},{28,24},{1,9},{5... | collective-permute-start | bytes 417800 | tf_op jit(solution)/shard_map/ppermute | solution.py:35
  23.9 0.0 collective-permute-done.13.refs_1_
  23.9 1.7 %collective-permute-start.7 = (bf16[288,256]{1,0:T(8,128)(2,1)S(1)}, bf16[288,256]{1,0:T(8,128)(2,1)S(1)}, u32[]{:S(2)}, u32[]{:S(2)}) collective-permute-start(bf16[288,256]{1,0:T(8,128)(2,1)S(1)} %get-tuple-element.30.refs_3_.refs_4_), channel_id=1, source_target_pairs={{0,4},{4,0},{8,12},{12,8},{16,24},{20,28},{24,16},{28,20},{1,5},{5... | collective-permute-start | bytes 442376 | tf_op jit(solution)/shard_map/ppermute | solution.py:35
  25.7 1.7 %collective-permute-done.14.refs_2_ = bf16[256,256]{1,0:T(8,128)(2,1)S(1)} collective-permute-done((bf16[256,256]{1,0:T(8,128)(2,1)S(1)}, bf16[256,256]{1,0:T(8,128)(2,1)S(1)}, u32[]{:S(2)}, u32[]{:S(2)}) %collective-permute-start.14) | collective-permute-done | bytes 131104 | tf_op jit(solution)/shard_map/ppermute | solution.py:35
  27.4 0.7 %collective-permute-start.15 = (bf16[128,256]{1,0:T(8,128)(2,1)S(1)}, bf16[128,256]{1,0:T(8,128)(2,1)S(1)}, u32[]{:S(2)}, u32[]{:S(2)}) collective-permute-start(bf16[128,256]{1,0:T(8,128)(2,1)S(1)} %get-tuple-element.36), channel_id=1, source_target_pairs={{0,4},{4,0},{8,12},{12,8},{16,24},{20,28},{24,16},{28,20},{1,5},{5... | collective-permute-start | bytes 196616 | tf_op jit(solution)/shard_map/ppermute | solution.py:35
  28.1 0.0 collective-permute-done.6.refs_4_
  28.1 1.0 %collective-permute-start.16 = (bf16[128,256]{1,0:T(8,128)(2,1)S(1)}, bf16[128,256]{1,0:T(8,128)(2,1)S(1)}, u32[]{:S(2)}, u32[]{:S(2)}) collective-permute-start(bf16[128,256]{1,0:T(8,128)(2,1)S(1)} %get-tuple-element.37), channel_id=1, source_target_pairs={{0,8},{4,12},{8,0},{12,4},{16,20},{20,16},{24,28},{28,24},{1,9},{5... | collective-permute-start | bytes 196616 | tf_op jit(solution)/shard_map/ppermute | solution.py:35
  29.1 1.4 %collective-permute-done.9.refs_7_ = bf16[288,256]{1,0:T(8,128)(2,1)S(1)} collective-permute-done((bf16[288,256]{1,0:T(8,128)(2,1)S(1)}, bf16[288,256]{1,0:T(8,128)(2,1)S(1)}, u32[]{:S(2)}, u32[]{:S(2)}) %collective-permute-start.9) | collective-permute-done | bytes 147488 | tf_op jit(solution)/shard_map/ppermute | solution.py:35
  30.5 0.0 collective-permute-start.11
  30.5 3.0 %collective-permute-done.8.refs_6_ = bf16[272,256]{1,0:T(8,128)(2,1)S(1)} collective-permute-done((bf16[272,256]{1,0:T(8,128)(2,1)S(1)}, bf16[272,256]{1,0:T(8,128)(2,1)S(1)}, u32[]{:S(2)}, u32[]{:S(2)}) %collective-permute-start.8) | collective-permute-done | bytes 139296 | tf_op jit(solution)/shard_map/ppermute | solution.py:35
  33.5 0.3 collective-permute-start.10
  33.8 0.0 collective-permute-done.7.refs_5_
  33.8 0.0 collective-permute-done.15.refs_3_
  33.8 1.1 %collective-permute-done.16.refs_4_ = bf16[128,256]{1,0:T(8,128)(2,1)S(1)} collective-permute-done((bf16[128,256]{1,0:T(8,128)(2,1)S(1)}, bf16[128,256]{1,0:T(8,128)(2,1)S(1)}, u32[]{:S(2)}, u32[]{:S(2)}) %collective-permute-start.16) | collective-permute-done | bytes 65568 | tf_op jit(solution)/shard_map/ppermute | solution.py:35
  35.0 0.0 copy-start.2
  35.0 0.1 collective-permute-start.17
  35.1 0.7 %collective-permute-start.18 = (bf16[256,256]{1,0:T(8,128)(2,1)S(1)}, bf16[256,256]{1,0:T(8,128)(2,1)S(1)}, u32[]{:S(2)}, u32[]{:S(2)}) collective-permute-start(bf16[256,256]{1,0:T(8,128)(2,1)S(1)} %grad_total.1.refs_0_), channel_id=1, source_target_pairs={{0,8},{4,12},{8,0},{12,4},{16,20},{20,16},{24,28},{28,24},{1,9},{5... | collective-permute-start | bytes 393224 | tf_op jit(solution)/shard_map/ppermute | solution.py:35
  35.8 2.8 %collective-permute-start.19 = (bf16[256,256]{1,0:T(8,128)(2,1)S(1)}, bf16[256,256]{1,0:T(8,128)(2,1)S(1)}, u32[]{:S(2)}, u32[]{:S(2)}) collective-permute-start(bf16[256,256]{1,0:T(8,128)(2,1)S(1)} %grad_total.1.refs_0_), channel_id=1, source_target_pairs={{0,12},{4,8},{8,4},{12,0},{1,13},{5,9},{9,5},{13,1},{2,14},{6,10},... | collective-permute-start | bytes 393224 | tf_op jit(solution)/shard_map/ppermute | solution.py:39
  39.2 0.0 collective-permute-done.10.refs_8_
  39.2 0.0 collective-permute-done.11.refs_9_
  39.2 3.8 %root.1 = (f32[256,1024]{1,0:T(8,128)}, bf16[256,1024]{1,0:T(8,128)(2,1)}, f32[8,128]{1,0:T(8,128)S(1)}) custom-call(s32[1,1]{1,0:T(1,128)S(6)} %copy.8.refs_0_, f32[640,256]{1,0:T(8,128)S(1)} %get-tuple-element.28.refs_1_, bf16[272,256]{1,0:T(8,128)(2,1)S(1)} %get-tuple-element.29.refs_2_.refs_3_, bf16[288,256]{1,0:T(8,128)(2,1)S(1)} %get-tuple-element.30.refs_3_.refs_4_, ...), custom_call_target="tpu_custom_call" | custom-call | tf_op jit(solution)/shard_map/root/pallas_call | solution.py:347
  43.0 0.0 collective-permute-done.17.refs_1_
  43.0 0.0 collective-permute-done.18.refs_2_
  43.1 0.0 collective-permute-done.19.refs_3_
  43.1 0.0 copy-done.2
  43.1 1.0 %step.1 = bf16[256,256]{1,0:T(8,128)(2,1)} custom-call(bf16[256,256]{1,0:T(8,128)(2,1)S(1)} %grad_total.1.refs_0_, bf16[256,256]{1,0:T(8,128)(2,1)S(1)} %collective-permute-done.17.refs_1_, bf16[256,256]{1,0:T(8,128)(2,1)S(1)} %collective-permute-done.18.refs_2_, bf16[256,256]{1,0:T(8,128)(2,1)S(1)} %collective-permute-done.19.refs_3_, ...), custom_call_target="tpu_custom_call" | custom-call | tf_op jit(solution)/shard_map/step/pallas_call | solution.py:347
  (2 shorter events, 0.1 us)
Async XLA Ops:
  0.6 14.2 %collective-permute-start.12 = (bf16[1,512,256]{2,1,0:T(8,128)(2,1)}, bf16[1,512,256]{2,1,0:T(8,128)(2,1)S(1)}, u32[]{:S(2)}, u32[]{:S(2)}) collective-permute-start(bf16[1,512,256]{2,1,0:T(8,128)(2,1)} %param.6), channel_id=1, source_target_pairs={{16,0},{0,16},{17,1},{1,17},{18,2},{2,18},{19,3},{3,19},{20,4},{4,... | collective-permute-start | bytes 786440 | tf_op jit(solution)/shard_map/ppermute | solution.py:22
  1.1 1.2 %copy-start = (bf16[1,512,1024]{2,1,0:T(8,128)(2,1)S(1)}, bf16[1,512,1024]{2,1,0:T(8,128)(2,1)}, u32[]{:S(2)}) copy-start(bf16[1,512,1024]{2,1,0:T(8,128)(2,1)} %param.5) | copy-start | bytes 3145732
  3.5 5.9 %collective-permute-start.2 = (bf16[272,256]{1,0:T(8,128)(2,1)S(1)}, bf16[272,256]{1,0:T(8,128)(2,1)S(1)}, u32[]{:S(2)}, u32[]{:S(2)}) collective-permute-start(bf16[272,256]{1,0:T(8,128)(2,1)S(1)} %get-tuple-element.24), channel_id=1, source_target_pairs={{0,4},{4,0},{8,12},{12,8},{16,24},{20,28},{24,16},{28,20},{1,5},{5... | collective-permute-start | bytes 417800 | tf_op jit(solution)/shard_map/ppermute | solution.py:35
  6.1 6.1 %collective-permute-start.3 = (bf16[272,256]{1,0:T(8,128)(2,1)S(1)}, bf16[272,256]{1,0:T(8,128)(2,1)S(1)}, u32[]{:S(2)}, u32[]{:S(2)}) collective-permute-start(bf16[272,256]{1,0:T(8,128)(2,1)S(1)} %get-tuple-element.25), channel_id=1, source_target_pairs={{0,8},{4,12},{8,0},{12,4},{16,20},{20,16},{24,28},{28,24},{1,9},{5... | collective-permute-start | bytes 417800 | tf_op jit(solution)/shard_map/ppermute | solution.py:35
  7.6 8.8 %collective-permute-start = (bf16[272,256]{1,0:T(8,128)(2,1)S(1)}, bf16[272,256]{1,0:T(8,128)(2,1)S(1)}, u32[]{:S(2)}, u32[]{:S(2)}) collective-permute-start(bf16[272,256]{1,0:T(8,128)(2,1)S(1)} %get-tuple-element.22), channel_id=1, source_target_pairs={{0,4},{4,0},{8,12},{12,8},{16,24},{20,28},{24,16},{28,20},{1,5},{5... | collective-permute-start | bytes 417800 | tf_op jit(solution)/shard_map/ppermute | solution.py:35
  8.1 8.3 %collective-permute-start.1 = (bf16[272,256]{1,0:T(8,128)(2,1)S(1)}, bf16[272,256]{1,0:T(8,128)(2,1)S(1)}, u32[]{:S(2)}, u32[]{:S(2)}) collective-permute-start(bf16[272,256]{1,0:T(8,128)(2,1)S(1)} %get-tuple-element.23), channel_id=1, source_target_pairs={{0,8},{4,12},{8,0},{12,4},{16,20},{20,16},{24,28},{28,24},{1,9},{5... | collective-permute-start | bytes 417800 | tf_op jit(solution)/shard_map/ppermute | solution.py:35
  12.2 6.8 %copy-start.1 = (f32[1,1,256,1024]{3,2,1,0:T(8,128)S(1)}, f32[1,1,256,1024]{3,2,1,0:T(8,128)}, u32[]{:S(2)}) copy-start(f32[1,1,256,1024]{3,2,1,0:T(8,128)} %param.7) | copy-start | bytes 3145732
  12.3 5.2 %collective-permute-start.4 = (bf16[272,256]{1,0:T(8,128)(2,1)S(1)}, bf16[272,256]{1,0:T(8,128)(2,1)S(1)}, u32[]{:S(2)}, u32[]{:S(2)}) collective-permute-start(bf16[272,256]{1,0:T(8,128)(2,1)S(1)} %get-tuple-element.26.refs_2_), channel_id=1, source_target_pairs={{0,4},{4,0},{8,12},{12,8},{16,24},{20,28},{24,16},{28,20},{1,5},{5... | collective-permute-start | bytes 417800 | tf_op jit(solution)/shard_map/ppermute | solution.py:35
  12.7 6.3 %collective-permute-start.5 = (bf16[272,256]{1,0:T(8,128)(2,1)S(1)}, bf16[272,256]{1,0:T(8,128)(2,1)S(1)}, u32[]{:S(2)}, u32[]{:S(2)}) collective-permute-start(bf16[272,256]{1,0:T(8,128)(2,1)S(1)} %get-tuple-element.27.refs_3_), channel_id=1, source_target_pairs={{0,8},{4,12},{8,0},{12,4},{16,20},{20,16},{24,28},{28,24},{1,9},{5... | collective-permute-start | bytes 417800 | tf_op jit(solution)/shard_map/ppermute | solution.py:35
  15.3 8.6 %collective-permute-start.13 = (bf16[256,256]{1,0:T(8,128)(2,1)S(1)}, bf16[256,256]{1,0:T(8,128)(2,1)S(1)}, u32[]{:S(2)}, u32[]{:S(2)}) collective-permute-start(bf16[256,256]{1,0:T(8,128)(2,1)S(1)} %get-tuple-element.34), channel_id=1, source_target_pairs={{0,4},{4,0},{8,12},{12,8},{16,24},{20,28},{24,16},{28,20},{1,5},{5... | collective-permute-start | bytes 393224 | tf_op jit(solution)/shard_map/ppermute | solution.py:35
  19.5 8.6 %collective-permute-start.6 = (bf16[272,256]{1,0:T(8,128)(2,1)S(1)}, bf16[272,256]{1,0:T(8,128)(2,1)S(1)}, u32[]{:S(2)}, u32[]{:S(2)}) collective-permute-start(bf16[272,256]{1,0:T(8,128)(2,1)S(1)} %get-tuple-element.29.refs_2_.refs_3_), channel_id=1, source_target_pairs={{0,4},{4,0},{8,12},{12,8},{16,24},{20,28},{24,16},{28,20},{1,5},{5... | collective-permute-start | bytes 417800 | tf_op jit(solution)/shard_map/ppermute | solution.py:35
  21.1 6.3 %collective-permute-start.14 = (bf16[256,256]{1,0:T(8,128)(2,1)S(1)}, bf16[256,256]{1,0:T(8,128)(2,1)S(1)}, u32[]{:S(2)}, u32[]{:S(2)}) collective-permute-start(bf16[256,256]{1,0:T(8,128)(2,1)S(1)} %get-tuple-element.35), channel_id=1, source_target_pairs={{0,8},{4,12},{8,0},{12,4},{16,20},{20,16},{24,28},{28,24},{1,9},{5... | collective-permute-start | bytes 393224 | tf_op jit(solution)/shard_map/ppermute | solution.py:35
  21.9 8.6 %collective-permute-start.9 = (bf16[288,256]{1,0:T(8,128)(2,1)S(1)}, bf16[288,256]{1,0:T(8,128)(2,1)S(1)}, u32[]{:S(2)}, u32[]{:S(2)}) collective-permute-start(bf16[288,256]{1,0:T(8,128)(2,1)S(1)} %get-tuple-element.30.refs_3_.refs_4_), channel_id=1, source_target_pairs={{0,8},{4,12},{8,0},{12,4},{16,20},{20,16},{24,28},{28,24},{1,9},{5... | collective-permute-start | bytes 442376 | tf_op jit(solution)/shard_map/ppermute | solution.py:35
  23.1 10.4 %collective-permute-start.8 = (bf16[272,256]{1,0:T(8,128)(2,1)S(1)}, bf16[272,256]{1,0:T(8,128)(2,1)S(1)}, u32[]{:S(2)}, u32[]{:S(2)}) collective-permute-start(bf16[272,256]{1,0:T(8,128)(2,1)S(1)} %get-tuple-element.29.refs_2_.refs_3_), channel_id=1, source_target_pairs={{0,8},{4,12},{8,0},{12,4},{16,20},{20,16},{24,28},{28,24},{1,9},{5... | collective-permute-start | bytes 417800 | tf_op jit(solution)/shard_map/ppermute | solution.py:35
  23.9 9.9 %collective-permute-start.7 = (bf16[288,256]{1,0:T(8,128)(2,1)S(1)}, bf16[288,256]{1,0:T(8,128)(2,1)S(1)}, u32[]{:S(2)}, u32[]{:S(2)}) collective-permute-start(bf16[288,256]{1,0:T(8,128)(2,1)S(1)} %get-tuple-element.30.refs_3_.refs_4_), channel_id=1, source_target_pairs={{0,4},{4,0},{8,12},{12,8},{16,24},{20,28},{24,16},{28,20},{1,5},{5... | collective-permute-start | bytes 442376 | tf_op jit(solution)/shard_map/ppermute | solution.py:35
  27.4 6.4 %collective-permute-start.15 = (bf16[128,256]{1,0:T(8,128)(2,1)S(1)}, bf16[128,256]{1,0:T(8,128)(2,1)S(1)}, u32[]{:S(2)}, u32[]{:S(2)}) collective-permute-start(bf16[128,256]{1,0:T(8,128)(2,1)S(1)} %get-tuple-element.36), channel_id=1, source_target_pairs={{0,4},{4,0},{8,12},{12,8},{16,24},{20,28},{24,16},{28,20},{1,5},{5... | collective-permute-start | bytes 196616 | tf_op jit(solution)/shard_map/ppermute | solution.py:35
  28.1 6.8 %collective-permute-start.16 = (bf16[128,256]{1,0:T(8,128)(2,1)S(1)}, bf16[128,256]{1,0:T(8,128)(2,1)S(1)}, u32[]{:S(2)}, u32[]{:S(2)}) collective-permute-start(bf16[128,256]{1,0:T(8,128)(2,1)S(1)} %get-tuple-element.37), channel_id=1, source_target_pairs={{0,8},{4,12},{8,0},{12,4},{16,20},{20,16},{24,28},{28,24},{1,9},{5... | collective-permute-start | bytes 196616 | tf_op jit(solution)/shard_map/ppermute | solution.py:35
  30.5 8.7 %collective-permute-start.11 = (bf16[288,256]{1,0:T(8,128)(2,1)S(1)}, bf16[288,256]{1,0:T(8,128)(2,1)S(1)}, u32[]{:S(2)}, u32[]{:S(2)}) collective-permute-start(bf16[288,256]{1,0:T(8,128)(2,1)S(1)} %collective-permute-done.9.refs_7_), channel_id=1, source_target_pairs={{0,4},{4,0},{8,12},{12,8},{16,24},{20,28},{24,16},{28,20},{1,5},{5... | collective-permute-start | bytes 442376 | tf_op jit(solution)/shard_map/ppermute | solution.py:35
  33.5 5.7 %collective-permute-start.10 = (bf16[272,256]{1,0:T(8,128)(2,1)S(1)}, bf16[272,256]{1,0:T(8,128)(2,1)S(1)}, u32[]{:S(2)}, u32[]{:S(2)}) collective-permute-start(bf16[272,256]{1,0:T(8,128)(2,1)S(1)} %collective-permute-done.6.refs_4_), channel_id=1, source_target_pairs={{0,8},{4,12},{8,0},{12,4},{16,20},{20,16},{24,28},{28,24},{1,9},{5... | collective-permute-start | bytes 417800 | tf_op jit(solution)/shard_map/ppermute | solution.py:35
  35.0 8.1 %copy-start.2 = (bf16[1,1,256,1024]{3,2,1,0:T(8,128)(2,1)S(1)}, bf16[1,1,256,1024]{3,2,1,0:T(8,128)(2,1)}, u32[]{:S(2)}) copy-start(bf16[1,1,256,1024]{3,2,1,0:T(8,128)(2,1)} %param.8) | copy-start | bytes 1572868
  35.0 8.1 %collective-permute-start.17 = (bf16[256,256]{1,0:T(8,128)(2,1)S(1)}, bf16[256,256]{1,0:T(8,128)(2,1)S(1)}, u32[]{:S(2)}, u32[]{:S(2)}) collective-permute-start(bf16[256,256]{1,0:T(8,128)(2,1)S(1)} %grad_total.1.refs_0_), channel_id=1, source_target_pairs={{0,4},{4,0},{8,12},{12,8},{16,24},{20,28},{24,16},{28,20},{1,5},{5... | collective-permute-start | bytes 393224 | tf_op jit(solution)/shard_map/ppermute | solution.py:35
  35.1 8.0 %collective-permute-start.18 = (bf16[256,256]{1,0:T(8,128)(2,1)S(1)}, bf16[256,256]{1,0:T(8,128)(2,1)S(1)}, u32[]{:S(2)}, u32[]{:S(2)}) collective-permute-start(bf16[256,256]{1,0:T(8,128)(2,1)S(1)} %grad_total.1.refs_0_), channel_id=1, source_target_pairs={{0,8},{4,12},{8,0},{12,4},{16,20},{20,16},{24,28},{28,24},{1,9},{5... | collective-permute-start | bytes 393224 | tf_op jit(solution)/shard_map/ppermute | solution.py:35
  35.8 7.3 %collective-permute-start.19 = (bf16[256,256]{1,0:T(8,128)(2,1)S(1)}, bf16[256,256]{1,0:T(8,128)(2,1)S(1)}, u32[]{:S(2)}, u32[]{:S(2)}) collective-permute-start(bf16[256,256]{1,0:T(8,128)(2,1)S(1)} %grad_total.1.refs_0_), channel_id=1, source_target_pairs={{0,12},{4,8},{8,4},{12,0},{1,13},{5,9},{9,5},{13,1},{2,14},{6,10},... | collective-permute-start | bytes 393224 | tf_op jit(solution)/shard_map/ppermute | solution.py:39

commit v12 on v11

--- a/solution.py
+++ b/solution.py
@@ -371,11 +371,14 @@
         "grad",
         inputs,
         received,
-        after=[relay_x, relay_y],
         scratch=[pltpu.VMEM((grows, order), F32)],
     )
     relay_x, relay_y = swapped(relay_x, 0), swapped(relay_y, 1)
     grad_x, grad_y = swapped(grad_x, 0), swapped(grad_y, 1)
+    strip_x, strip_y = call(
+        grad_relay_kernel, [shape(grows // 2)] * 2, "grad_relay", grad_keep, grad_x, grad_y
+    )
+    strip_x, strip_y = swapped(strip_x, 0), swapped(strip_y, 1)
     upper, lower, exact = call(
         functools.partial(factor_kernel, replicas),
         [shape(length), shape(length + 16), shape(5 * share // 2, F32)],
@@ -386,13 +389,10 @@
         relay_x,
         relay_y,
         old_factor[0, 0],
+        after=[strip_x, strip_y],
     )
     upper_x, lower_y = swapped(upper, 0), swapped(lower, 1)
     lower_x, upper_y = swapped(lower, 0), swapped(upper, 1)
-    strip_x, strip_y = call(
-        grad_relay_kernel, [shape(grows // 2)] * 2, "grad_relay", grad_keep, grad_x, grad_y, after=[upper, lower]
-    )
-    strip_x, strip_y = swapped(strip_x, 0), swapped(strip_y, 1)
     upper_far, lower_far = swapped(upper_x, 1), swapped(lower_y, 0)
     (strip,) = call(
         grad_total_kernel,
@@ -403,7 +403,7 @@
         grad_y,
         strip_x,
         strip_y,
-        after=[lower_x, upper_y],
+        after=[upper_x, lower_y],
     )
     strips = [strip, swapped(strip, 0), swapped(strip, 1), swapped_across(strip)]
     factor, root, finished = call(

time: 44.2 us -> 43.9 us (level)
  waiting for transfers between devices: 13.9 us -> 11.8 us
  starting transfers between devices: 20.6 us -> 22.4 us
    ppermute x18, starting transfers between devices: 17.3 us -> 20.6 us  [swapped(): return lax.ppermute(block, ('pipe', 'dp'), route)]
    ppermute x18, waiting for transfers between devices: 13.9 us -> 11.8 us  [swapped(): return lax.ppermute(block, ('pipe', 'dp'), route)]
    ppermute x1, starting transfers between devices: 2.77 us -> 1.26 us  [swapped_across(): lax.ppermute(block, 'dp', [(i, i ^ 3) for i in range(lax.axis_size('dp'))])]
  transfers between devices with their start and end apart: 20 -> 20, of which waited for: 8 -> 7; matrix products, arithmetic and copies ran while one was open for 0% -> 0% of each run, Pallas kernels for 14% -> 13%
where the time goes in v12:
time: 43.9 us; the launch traced here: 43.8 us
  starting transfers between devices  22.4 us (51%)
  waiting for transfers between devices  11.8 us (27%)
  Pallas kernels  6.98 us (16%)
  between operations  1.38 us (3%)
  local copies, waits for them, and re-layouts  1.24 us (3%)
    ppermute x18, starting transfers between devices, swapped(): return lax.ppermute(block, ('pipe', 'dp'), route)  20.6 us
    ppermute x18, waiting for transfers between devices, swapped(): return lax.ppermute(block, ('pipe', 'dp'), route)  11.8 us
    pallas_call x8, Pallas kernels, call(): pl.pallas_call(body, out_shape=outs, in_specs=in_specs, out_specs=out_spe...  6.98 us
    ppermute x1, starting transfers between devices, swapped_across(): lax.ppermute(block, 'dp', [(i, i ^ 3) for i in range(lax.axis_size('dp'))])  1.26 us
    unnamed x6, local copies, waits for them, and re-layouts  1.24 us
  transfers between devices with their start and end apart: 20, of which 7 were waited for; matrix products, arithmetic and copies ran while one was open for 0% of the time, Pallas kernels for 13%

profile of v12, /device:TPU:0, one launch (start us, length us, event | category | flops | bytes accessed | tf_op | source)
XLA Modules:
  0.0 43.8 jit_solution(4103294362591036083)
XLA Ops:
  0.6 0.5 %collective-permute-start.6 = (bf16[1,512,256]{2,1,0:T(8,128)(2,1)}, bf16[1,512,256]{2,1,0:T(8,128)(2,1)S(1)}, u32[]{:S(2)}, u32[]{:S(2)}) collective-permute-start(bf16[1,512,256]{2,1,0:T(8,128)(2,1)} %param.6), channel_id=1, source_target_pairs={{16,0},{0,16},{17,1},{1,17},{18,2},{2,18},{19,3},{3,19},{20,4},{4,... | collective-permute-start | bytes 786440 | tf_op jit(solution)/shard_map/ppermute | solution.py:22
  1.1 0.0 copy-start
  1.1 1.2 %copy-done = bf16[1,512,1024]{2,1,0:T(8,128)(2,1)S(1)} copy-done((bf16[1,512,1024]{2,1,0:T(8,128)(2,1)S(1)}, bf16[1,512,1024]{2,1,0:T(8,128)(2,1)}, u32[]{:S(2)}) %copy-start) | copy-done | bytes 1048600
  2.4 1.1 %batch.1 = (bf16[272,256]{1,0:T(8,128)(2,1)S(1)}, bf16[272,256]{1,0:T(8,128)(2,1)S(1)}, bf16[272,256]{1,0:T(8,128)(2,1)S(1)}, bf16[272,256]{1,0:T(8,128)(2,1)S(1)}, f32[1088,256]{1,0:T(8,128)S(1)}) custom-call(bf16[512,1024]{1,0:T(8,128)(2,1)S(1)} %bitcast.7), custom_call_target="tpu_custom_call" | custom-call | tf_op jit(solution)/shard_map/batch/pallas_call | solution.py:347
  3.5 2.6 %collective-permute-start.2 = (bf16[272,256]{1,0:T(8,128)(2,1)S(1)}, bf16[272,256]{1,0:T(8,128)(2,1)S(1)}, u32[]{:S(2)}, u32[]{:S(2)}) collective-permute-start(bf16[272,256]{1,0:T(8,128)(2,1)S(1)} %get-tuple-element.24), channel_id=1, source_target_pairs={{0,4},{4,0},{8,12},{12,8},{16,24},{20,28},{24,16},{28,20},{1,5},{5... | collective-permute-start | bytes 417800 | tf_op jit(solution)/shard_map/ppermute | solution.py:35
  6.0 1.5 %collective-permute-start.3 = (bf16[272,256]{1,0:T(8,128)(2,1)S(1)}, bf16[272,256]{1,0:T(8,128)(2,1)S(1)}, u32[]{:S(2)}, u32[]{:S(2)}) collective-permute-start(bf16[272,256]{1,0:T(8,128)(2,1)S(1)} %get-tuple-element.25), channel_id=1, source_target_pairs={{0,8},{4,12},{8,0},{12,4},{16,20},{20,16},{24,28},{28,24},{1,9},{5... | collective-permute-start | bytes 417800 | tf_op jit(solution)/shard_map/ppermute | solution.py:35
  7.6 0.0 collective-permute-done.6
  7.6 0.5 %grad.1 = (bf16[256,256]{1,0:T(8,128)(2,1)S(1)}, bf16[256,256]{1,0:T(8,128)(2,1)S(1)}, f32[512,256]{1,0:T(8,128)S(1)}) custom-call(bf16[512,1024]{1,0:T(8,128)(2,1)S(1)} %bitcast.8, bf16[512,256]{1,0:T(8,128)(2,1)S(1)} %bitcast.11), custom_call_target="tpu_custom_call" | custom-call | tf_op jit(solution)/shard_map/grad/pallas_call | solution.py:347
  8.1 0.0 copy-start.1
  8.1 0.6 %collective-permute-start.7 = (bf16[256,256]{1,0:T(8,128)(2,1)S(1)}, bf16[256,256]{1,0:T(8,128)(2,1)S(1)}, u32[]{:S(2)}, u32[]{:S(2)}) collective-permute-start(bf16[256,256]{1,0:T(8,128)(2,1)S(1)} %get-tuple-element.29), channel_id=1, source_target_pairs={{0,4},{4,0},{8,12},{12,8},{16,24},{20,28},{24,16},{28,20},{1,5},{5... | collective-permute-start | bytes 393224 | tf_op jit(solution)/shard_map/ppermute | solution.py:35
  8.7 1.5 %collective-permute-start = (bf16[272,256]{1,0:T(8,128)(2,1)S(1)}, bf16[272,256]{1,0:T(8,128)(2,1)S(1)}, u32[]{:S(2)}, u32[]{:S(2)}) collective-permute-start(bf16[272,256]{1,0:T(8,128)(2,1)S(1)} %get-tuple-element.22), channel_id=1, source_target_pairs={{0,4},{4,0},{8,12},{12,8},{16,24},{20,28},{24,16},{28,20},{1,5},{5... | collective-permute-start | bytes 417800 | tf_op jit(solution)/shard_map/ppermute | solution.py:35
  10.2 0.5 %collective-permute-start.8 = (bf16[256,256]{1,0:T(8,128)(2,1)S(1)}, bf16[256,256]{1,0:T(8,128)(2,1)S(1)}, u32[]{:S(2)}, u32[]{:S(2)}) collective-permute-start(bf16[256,256]{1,0:T(8,128)(2,1)S(1)} %get-tuple-element.30), channel_id=1, source_target_pairs={{0,8},{4,12},{8,0},{12,4},{16,20},{20,16},{24,28},{28,24},{1,9},{5... | collective-permute-start | bytes 393224 | tf_op jit(solution)/shard_map/ppermute | solution.py:35
  10.7 0.0 collective-permute-done.2.refs_1_
  10.7 1.5 %collective-permute-start.1 = (bf16[272,256]{1,0:T(8,128)(2,1)S(1)}, bf16[272,256]{1,0:T(8,128)(2,1)S(1)}, u32[]{:S(2)}, u32[]{:S(2)}) collective-permute-start(bf16[272,256]{1,0:T(8,128)(2,1)S(1)} %get-tuple-element.23), channel_id=1, source_target_pairs={{0,8},{4,12},{8,0},{12,4},{16,20},{20,16},{24,28},{28,24},{1,9},{5... | collective-permute-start | bytes 417800 | tf_op jit(solution)/shard_map/ppermute | solution.py:35
  12.2 0.0 collective-permute-done.3.refs_2_
  12.3 0.1 relay.1
  12.3 1.9 %collective-permute-start.4 = (bf16[272,256]{1,0:T(8,128)(2,1)S(1)}, bf16[272,256]{1,0:T(8,128)(2,1)S(1)}, u32[]{:S(2)}, u32[]{:S(2)}) collective-permute-start(bf16[272,256]{1,0:T(8,128)(2,1)S(1)} %get-tuple-element.26), channel_id=1, source_target_pairs={{0,4},{4,0},{8,12},{12,8},{16,24},{20,28},{24,16},{28,20},{1,5},{5... | collective-permute-start | bytes 417800 | tf_op jit(solution)/shard_map/ppermute | solution.py:35
  14.3 0.0 collective-permute-done.7.refs_1_
  14.3 0.5 %collective-permute-start.5 = (bf16[272,256]{1,0:T(8,128)(2,1)S(1)}, bf16[272,256]{1,0:T(8,128)(2,1)S(1)}, u32[]{:S(2)}, u32[]{:S(2)}) collective-permute-start(bf16[272,256]{1,0:T(8,128)(2,1)S(1)} %get-tuple-element.27), channel_id=1, source_target_pairs={{0,8},{4,12},{8,0},{12,4},{16,20},{20,16},{24,28},{28,24},{1,9},{5... | collective-permute-start | bytes 417800 | tf_op jit(solution)/shard_map/ppermute | solution.py:35
  14.8 1.8 %collective-permute-done.8.refs_2_ = bf16[256,256]{1,0:T(8,128)(2,1)S(1)} collective-permute-done((bf16[256,256]{1,0:T(8,128)(2,1)S(1)}, bf16[256,256]{1,0:T(8,128)(2,1)S(1)}, u32[]{:S(2)}, u32[]{:S(2)}) %collective-permute-start.8) | collective-permute-done | bytes 131104 | tf_op jit(solution)/shard_map/ppermute | solution.py:35
  16.6 0.7 %collective-permute-start.9 = (bf16[128,256]{1,0:T(8,128)(2,1)S(1)}, bf16[128,256]{1,0:T(8,128)(2,1)S(1)}, u32[]{:S(2)}, u32[]{:S(2)}) collective-permute-start(bf16[128,256]{1,0:T(8,128)(2,1)S(1)} %get-tuple-element.31), channel_id=1, source_target_pairs={{0,4},{4,0},{8,12},{12,8},{16,24},{20,28},{24,16},{28,20},{1,5},{5... | collective-permute-start | bytes 196616 | tf_op jit(solution)/shard_map/ppermute | solution.py:35
  17.3 0.0 collective-permute-done.refs_1_
  17.3 0.4 collective-permute-start.10
  17.7 1.4 %collective-permute-done.1.refs_2_ = bf16[272,256]{1,0:T(8,128)(2,1)S(1)} collective-permute-done((bf16[272,256]{1,0:T(8,128)(2,1)S(1)}, bf16[272,256]{1,0:T(8,128)(2,1)S(1)}, u32[]{:S(2)}, u32[]{:S(2)}) %collective-permute-start.1) | collective-permute-done | bytes 139296 | tf_op jit(solution)/shard_map/ppermute | solution.py:35
  19.0 1.1 %collective-permute-done.4.refs_3_ = bf16[272,256]{1,0:T(8,128)(2,1)S(1)} collective-permute-done((bf16[272,256]{1,0:T(8,128)(2,1)S(1)}, bf16[272,256]{1,0:T(8,128)(2,1)S(1)}, u32[]{:S(2)}, u32[]{:S(2)}) %collective-permute-start.4) | collective-permute-done | bytes 139296 | tf_op jit(solution)/shard_map/ppermute | solution.py:35
  20.2 0.4 collective-permute-done.5.refs_4_
  20.6 1.1 %collective-permute-done.9.refs_6_.refs_3_ = bf16[128,256]{1,0:T(8,128)(2,1)S(1)} collective-permute-done((bf16[128,256]{1,0:T(8,128)(2,1)S(1)}, bf16[128,256]{1,0:T(8,128)(2,1)S(1)}, u32[]{:S(2)}, u32[]{:S(2)}) %collective-permute-start.9) | collective-permute-done | bytes 65568 | tf_op jit(solution)/shard_map/ppermute | solution.py:35
  21.7 0.0 collective-permute-done.10.refs_7_.refs_4_
  21.7 0.0 copy-done.1
  21.7 0.4 factor.1
  22.1 1.2 %collective-permute-start.14 = (bf16[288,256]{1,0:T(8,128)(2,1)S(1)}, bf16[288,256]{1,0:T(8,128)(2,1)S(1)}, u32[]{:S(2)}, u32[]{:S(2)}) collective-permute-start(bf16[288,256]{1,0:T(8,128)(2,1)S(1)} %get-tuple-element.35.refs_3_), channel_id=1, source_target_pairs={{0,8},{4,12},{8,0},{12,4},{16,20},{20,16},{24,28},{28,24},{1,9},{5... | collective-permute-start | bytes 442376 | tf_op jit(solution)/shard_map/ppermute | solution.py:35
  23.3 1.4 %collective-permute-start.11 = (bf16[272,256]{1,0:T(8,128)(2,1)S(1)}, bf16[272,256]{1,0:T(8,128)(2,1)S(1)}, u32[]{:S(2)}, u32[]{:S(2)}) collective-permute-start(bf16[272,256]{1,0:T(8,128)(2,1)S(1)} %get-tuple-element.34.refs_2_), channel_id=1, source_target_pairs={{0,4},{4,0},{8,12},{12,8},{16,24},{20,28},{24,16},{28,20},{1,5},{5... | collective-permute-start | bytes 417800 | tf_op jit(solution)/shard_map/ppermute | solution.py:35
  24.7 0.7 %collective-permute-start.12 = (bf16[288,256]{1,0:T(8,128)(2,1)S(1)}, bf16[288,256]{1,0:T(8,128)(2,1)S(1)}, u32[]{:S(2)}, u32[]{:S(2)}) collective-permute-start(bf16[288,256]{1,0:T(8,128)(2,1)S(1)} %get-tuple-element.35.refs_3_), channel_id=1, source_target_pairs={{0,4},{4,0},{8,12},{12,8},{16,24},{20,28},{24,16},{28,20},{1,5},{5... | collective-permute-start | bytes 442376 | tf_op jit(solution)/shard_map/ppermute | solution.py:35
  25.3 0.9 %collective-permute-start.13 = (bf16[272,256]{1,0:T(8,128)(2,1)S(1)}, bf16[272,256]{1,0:T(8,128)(2,1)S(1)}, u32[]{:S(2)}, u32[]{:S(2)}) collective-permute-start(bf16[272,256]{1,0:T(8,128)(2,1)S(1)} %get-tuple-element.34.refs_2_), channel_id=1, source_target_pairs={{0,8},{4,12},{8,0},{12,4},{16,20},{20,16},{24,28},{28,24},{1,9},{5... | collective-permute-start | bytes 417800 | tf_op jit(solution)/shard_map/ppermute | solution.py:35
  26.2 2.7 %collective-permute-done.14.refs_7_.refs_6_ = bf16[288,256]{1,0:T(8,128)(2,1)S(1)} collective-permute-done((bf16[288,256]{1,0:T(8,128)(2,1)S(1)}, bf16[288,256]{1,0:T(8,128)(2,1)S(1)}, u32[]{:S(2)}, u32[]{:S(2)}) %collective-permute-start.14) | collective-permute-done | bytes 147488 | tf_op jit(solution)/shard_map/ppermute | solution.py:35
  28.9 1.2 %collective-permute-start.16 = (bf16[288,256]{1,0:T(8,128)(2,1)S(1)}, bf16[288,256]{1,0:T(8,128)(2,1)S(1)}, u32[]{:S(2)}, u32[]{:S(2)}) collective-permute-start(bf16[288,256]{1,0:T(8,128)(2,1)S(1)} %collective-permute-done.14.refs_7_.refs_6_), channel_id=1, source_target_pairs={{0,4},{4,0},{8,12},{12,8},{16,24},{20,28},{24,16},{28,20},{1,5},{5... | collective-permute-start | bytes 442376 | tf_op jit(solution)/shard_map/ppermute | solution.py:35
  30.1 0.0 collective-permute-done.11.refs_4_.refs_5_
  30.1 1.3 %collective-permute-start.15 = (bf16[272,256]{1,0:T(8,128)(2,1)S(1)}, bf16[272,256]{1,0:T(8,128)(2,1)S(1)}, u32[]{:S(2)}, u32[]{:S(2)}) collective-permute-start(bf16[272,256]{1,0:T(8,128)(2,1)S(1)} %collective-permute-done.11.refs_4_.refs_5_), channel_id=1, source_target_pairs={{0,8},{4,12},{8,0},{12,4},{16,20},{20,16},{24,28},{28,24},{1,9},{5... | collective-permute-start | bytes 417800 | tf_op jit(solution)/shard_map/ppermute | solution.py:35
  31.4 0.1 grad_total.1.refs_0_
  31.4 0.0 copy-start.2
  31.4 1.3 %collective-permute-start.19 = (bf16[256,256]{1,0:T(8,128)(2,1)S(1)}, bf16[256,256]{1,0:T(8,128)(2,1)S(1)}, u32[]{:S(2)}, u32[]{:S(2)}) collective-permute-start(bf16[256,256]{1,0:T(8,128)(2,1)S(1)} %grad_total.1.refs_0_), channel_id=1, source_target_pairs={{0,12},{4,8},{8,4},{12,0},{1,13},{5,9},{9,5},{13,1},{2,14},{6,10},... | collective-permute-start | bytes 393224 | tf_op jit(solution)/shard_map/ppermute | solution.py:39
  32.7 0.0 collective-permute-done.13.refs_6_
  32.7 1.0 %collective-permute-start.18 = (bf16[256,256]{1,0:T(8,128)(2,1)S(1)}, bf16[256,256]{1,0:T(8,128)(2,1)S(1)}, u32[]{:S(2)}, u32[]{:S(2)}) collective-permute-start(bf16[256,256]{1,0:T(8,128)(2,1)S(1)} %grad_total.1.refs_0_), channel_id=1, source_target_pairs={{0,8},{4,12},{8,0},{12,4},{16,20},{20,16},{24,28},{28,24},{1,9},{5... | collective-permute-start | bytes 393224 | tf_op jit(solution)/shard_map/ppermute | solution.py:35
  33.6 0.0 collective-permute-done.12.refs_5_
  33.6 1.3 %collective-permute-start.17 = (bf16[256,256]{1,0:T(8,128)(2,1)S(1)}, bf16[256,256]{1,0:T(8,128)(2,1)S(1)}, u32[]{:S(2)}, u32[]{:S(2)}) collective-permute-start(bf16[256,256]{1,0:T(8,128)(2,1)S(1)} %grad_total.1.refs_0_), channel_id=1, source_target_pairs={{0,4},{4,0},{8,12},{12,8},{16,24},{20,28},{24,16},{28,20},{1,5},{5... | collective-permute-start | bytes 393224 | tf_op jit(solution)/shard_map/ppermute | solution.py:35
  35.6 3.3 %collective-permute-done.15.refs_8_ = bf16[272,256]{1,0:T(8,128)(2,1)S(1)} collective-permute-done((bf16[272,256]{1,0:T(8,128)(2,1)S(1)}, bf16[272,256]{1,0:T(8,128)(2,1)S(1)}, u32[]{:S(2)}, u32[]{:S(2)}) %collective-permute-start.15) | collective-permute-done | bytes 139296 | tf_op jit(solution)/shard_map/ppermute | solution.py:35
  38.9 0.0 collective-permute-done.16.refs_9_
  38.9 3.8 %root.1 = (f32[256,1024]{1,0:T(8,128)}, bf16[256,1024]{1,0:T(8,128)(2,1)}, f32[8,128]{1,0:T(8,128)S(1)}) custom-call(s32[1,1]{1,0:T(1,128)S(6)} %copy.8.refs_0_, f32[640,256]{1,0:T(8,128)S(1)} %get-tuple-element.33.refs_1_, bf16[272,256]{1,0:T(8,128)(2,1)S(1)} %get-tuple-element.34.refs_2_, bf16[288,256]{1,0:T(8,128)(2,1)S(1)} %get-tuple-element.35.refs_3_, ...), custom_call_target="tpu_custom_call" | custom-call | tf_op jit(solution)/shard_map/root/pallas_call | solution.py:347
  42.7 0.0 collective-permute-done.19.refs_3_
  42.8 0.0 collective-permute-done.18.refs_2_
  42.8 0.0 collective-permute-done.17.refs_1_
  42.8 0.0 copy-done.2
  42.8 1.0 %step.1 = bf16[256,256]{1,0:T(8,128)(2,1)} custom-call(bf16[256,256]{1,0:T(8,128)(2,1)S(1)} %grad_total.1.refs_0_, bf16[256,256]{1,0:T(8,128)(2,1)S(1)} %collective-permute-done.17.refs_1_, bf16[256,256]{1,0:T(8,128)(2,1)S(1)} %collective-permute-done.18.refs_2_, bf16[256,256]{1,0:T(8,128)(2,1)S(1)} %collective-permute-done.19.refs_3_, ...), custom_call_target="tpu_custom_call" | custom-call | tf_op jit(solution)/shard_map/step/pallas_call | solution.py:347
  (1 shorter events, 0.0 us)
Async XLA Ops:
  0.6 6.9 %collective-permute-start.6 = (bf16[1,512,256]{2,1,0:T(8,128)(2,1)}, bf16[1,512,256]{2,1,0:T(8,128)(2,1)S(1)}, u32[]{:S(2)}, u32[]{:S(2)}) collective-permute-start(bf16[1,512,256]{2,1,0:T(8,128)(2,1)} %param.6), channel_id=1, source_target_pairs={{16,0},{0,16},{17,1},{1,17},{18,2},{2,18},{19,3},{3,19},{20,4},{4,... | collective-permute-start | bytes 786440 | tf_op jit(solution)/shard_map/ppermute | solution.py:22
  1.1 1.2 %copy-start = (bf16[1,512,1024]{2,1,0:T(8,128)(2,1)S(1)}, bf16[1,512,1024]{2,1,0:T(8,128)(2,1)}, u32[]{:S(2)}) copy-start(bf16[1,512,1024]{2,1,0:T(8,128)(2,1)} %param.5) | copy-start | bytes 3145732
  3.5 7.2 %collective-permute-start.2 = (bf16[272,256]{1,0:T(8,128)(2,1)S(1)}, bf16[272,256]{1,0:T(8,128)(2,1)S(1)}, u32[]{:S(2)}, u32[]{:S(2)}) collective-permute-start(bf16[272,256]{1,0:T(8,128)(2,1)S(1)} %get-tuple-element.24), channel_id=1, source_target_pairs={{0,4},{4,0},{8,12},{12,8},{16,24},{20,28},{24,16},{28,20},{1,5},{5... | collective-permute-start | bytes 417800 | tf_op jit(solution)/shard_map/ppermute | solution.py:35
  6.0 6.2 %collective-permute-start.3 = (bf16[272,256]{1,0:T(8,128)(2,1)S(1)}, bf16[272,256]{1,0:T(8,128)(2,1)S(1)}, u32[]{:S(2)}, u32[]{:S(2)}) collective-permute-start(bf16[272,256]{1,0:T(8,128)(2,1)S(1)} %get-tuple-element.25), channel_id=1, source_target_pairs={{0,8},{4,12},{8,0},{12,4},{16,20},{20,16},{24,28},{28,24},{1,9},{5... | collective-permute-start | bytes 417800 | tf_op jit(solution)/shard_map/ppermute | solution.py:35
  8.1 13.6 %copy-start.1 = (f32[1,1,256,1024]{3,2,1,0:T(8,128)S(1)}, f32[1,1,256,1024]{3,2,1,0:T(8,128)}, u32[]{:S(2)}) copy-start(f32[1,1,256,1024]{3,2,1,0:T(8,128)} %param.7) | copy-start | bytes 3145732
  8.1 6.2 %collective-permute-start.7 = (bf16[256,256]{1,0:T(8,128)(2,1)S(1)}, bf16[256,256]{1,0:T(8,128)(2,1)S(1)}, u32[]{:S(2)}, u32[]{:S(2)}) collective-permute-start(bf16[256,256]{1,0:T(8,128)(2,1)S(1)} %get-tuple-element.29), channel_id=1, source_target_pairs={{0,4},{4,0},{8,12},{12,8},{16,24},{20,28},{24,16},{28,20},{1,5},{5... | collective-permute-start | bytes 393224 | tf_op jit(solution)/shard_map/ppermute | solution.py:35
  8.7 8.6 %collective-permute-start = (bf16[272,256]{1,0:T(8,128)(2,1)S(1)}, bf16[272,256]{1,0:T(8,128)(2,1)S(1)}, u32[]{:S(2)}, u32[]{:S(2)}) collective-permute-start(bf16[272,256]{1,0:T(8,128)(2,1)S(1)} %get-tuple-element.22), channel_id=1, source_target_pairs={{0,4},{4,0},{8,12},{12,8},{16,24},{20,28},{24,16},{28,20},{1,5},{5... | collective-permute-start | bytes 417800 | tf_op jit(solution)/shard_map/ppermute | solution.py:35
  10.2 6.4 %collective-permute-start.8 = (bf16[256,256]{1,0:T(8,128)(2,1)S(1)}, bf16[256,256]{1,0:T(8,128)(2,1)S(1)}, u32[]{:S(2)}, u32[]{:S(2)}) collective-permute-start(bf16[256,256]{1,0:T(8,128)(2,1)S(1)} %get-tuple-element.30), channel_id=1, source_target_pairs={{0,8},{4,12},{8,0},{12,4},{16,20},{20,16},{24,28},{28,24},{1,9},{5... | collective-permute-start | bytes 393224 | tf_op jit(solution)/shard_map/ppermute | solution.py:35
  10.7 8.3 %collective-permute-start.1 = (bf16[272,256]{1,0:T(8,128)(2,1)S(1)}, bf16[272,256]{1,0:T(8,128)(2,1)S(1)}, u32[]{:S(2)}, u32[]{:S(2)}) collective-permute-start(bf16[272,256]{1,0:T(8,128)(2,1)S(1)} %get-tuple-element.23), channel_id=1, source_target_pairs={{0,8},{4,12},{8,0},{12,4},{16,20},{20,16},{24,28},{28,24},{1,9},{5... | collective-permute-start | bytes 417800 | tf_op jit(solution)/shard_map/ppermute | solution.py:35
  12.3 7.8 %collective-permute-start.4 = (bf16[272,256]{1,0:T(8,128)(2,1)S(1)}, bf16[272,256]{1,0:T(8,128)(2,1)S(1)}, u32[]{:S(2)}, u32[]{:S(2)}) collective-permute-start(bf16[272,256]{1,0:T(8,128)(2,1)S(1)} %get-tuple-element.26), channel_id=1, source_target_pairs={{0,4},{4,0},{8,12},{12,8},{16,24},{20,28},{24,16},{28,20},{1,5},{5... | collective-permute-start | bytes 417800 | tf_op jit(solution)/shard_map/ppermute | solution.py:35
  14.3 6.3 %collective-permute-start.5 = (bf16[272,256]{1,0:T(8,128)(2,1)S(1)}, bf16[272,256]{1,0:T(8,128)(2,1)S(1)}, u32[]{:S(2)}, u32[]{:S(2)}) collective-permute-start(bf16[272,256]{1,0:T(8,128)(2,1)S(1)} %get-tuple-element.27), channel_id=1, source_target_pairs={{0,8},{4,12},{8,0},{12,4},{16,20},{20,16},{24,28},{28,24},{1,9},{5... | collective-permute-start | bytes 417800 | tf_op jit(solution)/shard_map/ppermute | solution.py:35
  16.6 5.1 %collective-permute-start.9 = (bf16[128,256]{1,0:T(8,128)(2,1)S(1)}, bf16[128,256]{1,0:T(8,128)(2,1)S(1)}, u32[]{:S(2)}, u32[]{:S(2)}) collective-permute-start(bf16[128,256]{1,0:T(8,128)(2,1)S(1)} %get-tuple-element.31), channel_id=1, source_target_pairs={{0,4},{4,0},{8,12},{12,8},{16,24},{20,28},{24,16},{28,20},{1,5},{5... | collective-permute-start | bytes 196616 | tf_op jit(solution)/shard_map/ppermute | solution.py:35
  17.3 4.4 %collective-permute-start.10 = (bf16[128,256]{1,0:T(8,128)(2,1)S(1)}, bf16[128,256]{1,0:T(8,128)(2,1)S(1)}, u32[]{:S(2)}, u32[]{:S(2)}) collective-permute-start(bf16[128,256]{1,0:T(8,128)(2,1)S(1)} %get-tuple-element.32), channel_id=1, source_target_pairs={{0,8},{4,12},{8,0},{12,4},{16,20},{20,16},{24,28},{28,24},{1,9},{5... | collective-permute-start | bytes 196616 | tf_op jit(solution)/shard_map/ppermute | solution.py:35
  22.1 6.8 %collective-permute-start.14 = (bf16[288,256]{1,0:T(8,128)(2,1)S(1)}, bf16[288,256]{1,0:T(8,128)(2,1)S(1)}, u32[]{:S(2)}, u32[]{:S(2)}) collective-permute-start(bf16[288,256]{1,0:T(8,128)(2,1)S(1)} %get-tuple-element.35.refs_3_), channel_id=1, source_target_pairs={{0,8},{4,12},{8,0},{12,4},{16,20},{20,16},{24,28},{28,24},{1,9},{5... | collective-permute-start | bytes 442376 | tf_op jit(solution)/shard_map/ppermute | solution.py:35
  23.3 6.8 %collective-permute-start.11 = (bf16[272,256]{1,0:T(8,128)(2,1)S(1)}, bf16[272,256]{1,0:T(8,128)(2,1)S(1)}, u32[]{:S(2)}, u32[]{:S(2)}) collective-permute-start(bf16[272,256]{1,0:T(8,128)(2,1)S(1)} %get-tuple-element.34.refs_2_), channel_id=1, source_target_pairs={{0,4},{4,0},{8,12},{12,8},{16,24},{20,28},{24,16},{28,20},{1,5},{5... | collective-permute-start | bytes 417800 | tf_op jit(solution)/shard_map/ppermute | solution.py:35
  24.7 9.0 %collective-permute-start.12 = (bf16[288,256]{1,0:T(8,128)(2,1)S(1)}, bf16[288,256]{1,0:T(8,128)(2,1)S(1)}, u32[]{:S(2)}, u32[]{:S(2)}) collective-permute-start(bf16[288,256]{1,0:T(8,128)(2,1)S(1)} %get-tuple-element.35.refs_3_), channel_id=1, source_target_pairs={{0,4},{4,0},{8,12},{12,8},{16,24},{20,28},{24,16},{28,20},{1,5},{5... | collective-permute-start | bytes 442376 | tf_op jit(solution)/shard_map/ppermute | solution.py:35
  25.3 7.4 %collective-permute-start.13 = (bf16[272,256]{1,0:T(8,128)(2,1)S(1)}, bf16[272,256]{1,0:T(8,128)(2,1)S(1)}, u32[]{:S(2)}, u32[]{:S(2)}) collective-permute-start(bf16[272,256]{1,0:T(8,128)(2,1)S(1)} %get-tuple-element.34.refs_2_), channel_id=1, source_target_pairs={{0,8},{4,12},{8,0},{12,4},{16,20},{20,16},{24,28},{28,24},{1,9},{5... | collective-permute-start | bytes 417800 | tf_op jit(solution)/shard_map/ppermute | solution.py:35
  28.9 10.0 %collective-permute-start.16 = (bf16[288,256]{1,0:T(8,128)(2,1)S(1)}, bf16[288,256]{1,0:T(8,128)(2,1)S(1)}, u32[]{:S(2)}, u32[]{:S(2)}) collective-permute-start(bf16[288,256]{1,0:T(8,128)(2,1)S(1)} %collective-permute-done.14.refs_7_.refs_6_), channel_id=1, source_target_pairs={{0,4},{4,0},{8,12},{12,8},{16,24},{20,28},{24,16},{28,20},{1,5},{5... | collective-permute-start | bytes 442376 | tf_op jit(solution)/shard_map/ppermute | solution.py:35
  30.1 8.8 %collective-permute-start.15 = (bf16[272,256]{1,0:T(8,128)(2,1)S(1)}, bf16[272,256]{1,0:T(8,128)(2,1)S(1)}, u32[]{:S(2)}, u32[]{:S(2)}) collective-permute-start(bf16[272,256]{1,0:T(8,128)(2,1)S(1)} %collective-permute-done.11.refs_4_.refs_5_), channel_id=1, source_target_pairs={{0,8},{4,12},{8,0},{12,4},{16,20},{20,16},{24,28},{28,24},{1,9},{5... | collective-permute-start | bytes 417800 | tf_op jit(solution)/shard_map/ppermute | solution.py:35
  31.4 11.4 %copy-start.2 = (bf16[1,1,256,1024]{3,2,1,0:T(8,128)(2,1)S(1)}, bf16[1,1,256,1024]{3,2,1,0:T(8,128)(2,1)}, u32[]{:S(2)}) copy-start(bf16[1,1,256,1024]{3,2,1,0:T(8,128)(2,1)} %param.8) | copy-start | bytes 1572868
  31.4 11.3 %collective-permute-start.19 = (bf16[256,256]{1,0:T(8,128)(2,1)S(1)}, bf16[256,256]{1,0:T(8,128)(2,1)S(1)}, u32[]{:S(2)}, u32[]{:S(2)}) collective-permute-start(bf16[256,256]{1,0:T(8,128)(2,1)S(1)} %grad_total.1.refs_0_), channel_id=1, source_target_pairs={{0,12},{4,8},{8,4},{12,0},{1,13},{5,9},{9,5},{13,1},{2,14},{6,10},... | collective-permute-start | bytes 393224 | tf_op jit(solution)/shard_map/ppermute | solution.py:39
  32.7 10.1 %collective-permute-start.18 = (bf16[256,256]{1,0:T(8,128)(2,1)S(1)}, bf16[256,256]{1,0:T(8,128)(2,1)S(1)}, u32[]{:S(2)}, u32[]{:S(2)}) collective-permute-start(bf16[256,256]{1,0:T(8,128)(2,1)S(1)} %grad_total.1.refs_0_), channel_id=1, source_target_pairs={{0,8},{4,12},{8,0},{12,4},{16,20},{20,16},{24,28},{28,24},{1,9},{5... | collective-permute-start | bytes 393224 | tf_op jit(solution)/shard_map/ppermute | solution.py:35
  33.6 9.1 %collective-permute-start.17 = (bf16[256,256]{1,0:T(8,128)(2,1)S(1)}, bf16[256,256]{1,0:T(8,128)(2,1)S(1)}, u32[]{:S(2)}, u32[]{:S(2)}) collective-permute-start(bf16[256,256]{1,0:T(8,128)(2,1)S(1)} %grad_total.1.refs_0_), channel_id=1, source_target_pairs={{0,4},{4,0},{8,12},{12,8},{16,24},{20,28},{24,16},{28,20},{1,5},{5... | collective-permute-start | bytes 393224 | tf_op jit(solution)/shard_map/ppermute | solution.py:35

commit v13 on v12

--- a/solution.py
+++ b/solution.py
@@ -33,10 +33,6 @@
         offset = 1 if section == turn else 2
         route += [(section * replicas + i, section * replicas + (i ^ offset)) for i in range(replicas)]
     return lax.ppermute(block, ("pipe", "dp"), route)
-
-
-def swapped_across(block):
-    return lax.ppermute(block, "dp", [(i, i ^ 3) for i in range(lax.axis_size("dp"))])
 
 
 def eye_of(rows, cols, shift=0):
@@ -142,25 +138,23 @@
     store_chunk(pieces(0), length, (keep, 0), (keep, length))
 
 
-def grad_kernel(replicas, tokens_all, acts, grads, send_x, send_y, keep, total):
-    order = acts.shape[1]
-    share = order // replicas
+def band(index, size):
+    return pl.ds(pl.multiple_of(index * size, size), size)
+
+
+def grad_kernel(replicas, tokens_all, acts, grads, send, keep, total):
+    share = acts.shape[1] // replicas
     strip = grads.shape[1] // replicas
-    length = send_x.shape[0] // 2
     mine = lax.axis_index("dp")
-    total[...] = lax.dot_general(
-        grads[...], acts[...], (((0,), (0,)), ((), ())), preferred_element_type=F32
-    ) * (1.0 / math.sqrt(tokens_all))
-
-    def pieces(offset):
-        rows = pl.ds(pl.multiple_of((mine ^ offset) * strip, strip), strip)
-        for part in range(replicas):
-            yield part * strip, total[rows, part * share : (part + 1) * share]
-
-    store_chunk(pieces(3), length, (send_x, 0), (send_y, 0))
-    store_chunk(pieces(along(0)), length, (send_x, length), (keep, 3 * length))
-    store_chunk(pieces(along(1)), length, (keep, 2 * length), (send_y, length))
-    store_chunk(pieces(0), length, (keep, 0), (keep, length))
+    total[...] = lax.dot_general(grads[...], acts[...], (((0,), (0,)), ((), ())), preferred_element_type=F32) * (
+        1.0 / math.sqrt(tokens_all)
+    )
+    for ref, offsets in ((send, (along(0), 3)), (keep, (0, along(1)))):
+        for i, offset in enumerate(offsets):
+            for part in range(replicas):
+                start = (i * replicas + part) * strip
+                piece = total[band(mine ^ offset, strip), part * share : (part + 1) * share]
+                ref[start : start + strip, :] = piece.astype(ref.dtype)
 
 
 def relay_kernel(keep, got_x, got_y, send_x, send_y):
@@ -169,20 +163,20 @@
     send_x[...] = (keep[3 * length :, :] + got_y[...].astype(F32)).astype(BF16)
 
 
-def grad_relay_kernel(keep, got_x, got_y, send_x, send_y):
-    length = send_x.shape[0]
-    send_y[...] = (keep[2 * length : 3 * length, :] + got_x[0:length, :].astype(F32)).astype(BF16)
-    send_x[...] = (keep[3 * length :, :] + got_y[0:length, :].astype(F32)).astype(BF16)
-
-
-def grad_total_kernel(keep, got_x, got_y, relay_x, relay_y, chunk):
-    length = relay_x.shape[0]
-    chunk[0:length, :] = (
-        keep[0:length, :] + got_x[length:, :].astype(F32) + relay_y[...].astype(F32)
-    ).astype(BF16)
-    chunk[length:, :] = (
-        keep[length : 2 * length, :] + got_y[length:, :].astype(F32) + relay_x[...].astype(F32)
-    ).astype(BF16)
+def strip_relay_kernel(keep, got, send):
+    length = send.shape[0]
+    send[...] = (keep[length:, :] + got[length:, :].astype(F32)).astype(BF16)
+
+
+def strip_kernel(keep, got, relayed, strip):
+    length = strip.shape[0]
+    strip[...] = (keep[0:length, :] + got[0:length, :].astype(F32) + relayed[...].astype(F32)).astype(BF16)
+
+
+def pair_kernel(own, got, send):
+    length = own.shape[0]
+    send[0:length, :] = own[...]
+    send[length:, :] = got[...]
 
 
 def factor_kernel(replicas, keep, direct_x, direct_y, relay_x, relay_y, old, upper, lower, exact):
@@ -301,23 +295,21 @@
         copy.wait()
 
 
-def step_kernel(replicas, *refs):
-    chunks = refs[:replicas]
-    old_root, step_out, grads, result = refs[replicas:]
+def step_kernel(replicas, pair, far, old_root, step_out, grads, result):
     share = old_root.shape[0]
     strip = step_out.shape[0] // replicas
+    length = pair.shape[0] // 2
     mine = lax.axis_index("dp")
-    for offset, chunk in enumerate(chunks):
+    strips = [(pair, 0, 0), (pair, length, along(1)), (far, 0, along(0)), (far, length, 3)]
+    for i, (ref, at, _) in enumerate(strips):
         for part in range(replicas):
-            grads[offset * strip : (offset + 1) * strip, part * share : (part + 1) * share] = chunk[
-                part * strip : (part + 1) * strip, :
-            ]
+            start = at + part * strip
+            grads[i * strip : (i + 1) * strip, part * share : (part + 1) * share] = ref[start : start + strip, :]
     result[...] = lax.dot_general(
         grads[...], old_root[...], (((1,), (1,)), ((), ())), preferred_element_type=F32
     ).astype(BF16)
-    for position, offset in enumerate(offsets()):
-        rows = pl.ds(pl.multiple_of((mine ^ offset) * strip, strip), strip)
-        step_out[rows, :] = result[position * strip : (position + 1) * strip, :]
+    for i, (_, _, offset) in enumerate(strips):
+        step_out[band(mine ^ offset, strip), :] = result[i * strip : (i + 1) * strip, :]
 
 
 def square_plan(acts, out_grad, old_factor, old_root, iter_count):
@@ -365,20 +357,18 @@
     relay_x, relay_y = swapped(relay_x, 0), swapped(relay_y, 1)
     direct_x, direct_y = swapped(direct_x, 0), swapped(direct_y, 1)
     relay_x, relay_y = call(relay_kernel, [shape(length)] * 2, "relay", keep, relay_x, relay_y)
-    grad_x, grad_y, grad_keep = call(
+    strips, strips_keep = call(
         functools.partial(grad_kernel, replicas, tokens * replicas),
-        [shape(grows)] * 2 + [shape(2 * grows, F32)],
+        [shape(2 * grows), shape(2 * grows, F32)],
         "grad",
         inputs,
         received,
         scratch=[pltpu.VMEM((grows, order), F32)],
     )
     relay_x, relay_y = swapped(relay_x, 0), swapped(relay_y, 1)
-    grad_x, grad_y = swapped(grad_x, 0), swapped(grad_y, 1)
-    strip_x, strip_y = call(
-        grad_relay_kernel, [shape(grows // 2)] * 2, "grad_relay", grad_keep, grad_x, grad_y
-    )
-    strip_x, strip_y = swapped(strip_x, 0), swapped(strip_y, 1)
+    strips_got = swapped(strips, 0)
+    (strip_on,) = call(strip_relay_kernel, [shape(grows)], "strip_relay", strips_keep, strips_got)
+    strip_relayed = swapped(strip_on, 1)
     upper, lower, exact = call(
         functools.partial(factor_kernel, replicas),
         [shape(length), shape(length + 16), shape(5 * share // 2, F32)],
@@ -389,23 +379,17 @@
         relay_x,
         relay_y,
         old_factor[0, 0],
-        after=[strip_x, strip_y],
+        after=[strip_relayed],
     )
     upper_x, lower_y = swapped(upper, 0), swapped(lower, 1)
     lower_x, upper_y = swapped(lower, 0), swapped(upper, 1)
     upper_far, lower_far = swapped(upper_x, 1), swapped(lower_y, 0)
     (strip,) = call(
-        grad_total_kernel,
-        [shape(grows)],
-        "grad_total",
-        grad_keep,
-        grad_x,
-        grad_y,
-        strip_x,
-        strip_y,
-        after=[upper_x, lower_y],
-    )
-    strips = [strip, swapped(strip, 0), swapped(strip, 1), swapped_across(strip)]
+        strip_kernel, [shape(grows)], "strip", strips_keep, strips_got, strip_relayed, after=[upper_x, lower_y, lower_x, upper_y]
+    )
+    strip_near = swapped(strip, 1)
+    (pair,) = call(pair_kernel, [shape(2 * grows)], "pair", strip, strip_near, after=[upper_far, lower_far])
+    pair_far = swapped(pair, 0)
     factor, root, finished = call(
         root_kernel,
         [shape(share, F32, order), shape(share, BF16, order), shape(8, F32, 128)],
@@ -433,7 +417,8 @@
         functools.partial(step_kernel, replicas),
         [shape(grows, BF16, share)],
         "step",
-        *strips,
+        pair,
+        pair_far,
         old_root[0, 0],
         after=[finished],
         scratch=[pltpu.VMEM((grows, order), BF16), pltpu.VMEM((grows, share), BF16)],

time: 43.9 us -> 47.3 us (1.077)
  waiting for transfers between devices: 11.8 us -> 17.6 us
  starting transfers between devices: 22.4 us -> 20 us
    ppermute x18 -> x16, waiting for transfers between devices: 11.8 us -> 16.2 us  [swapped(): return lax.ppermute(block, ('pipe', 'dp'), route)]
    ppermute x1, waiting for transfers between devices: 0.01 us -> 1.37 us  [passed_along(): return lax.ppermute(block, axis, route)]
    ppermute x1 -> x0, starting transfers between devices: 1.26 us -> none  [swapped_across(): lax.ppermute(block, 'dp', [(i, i ^ 3) for i in range(lax.axis_size('dp'))])]
    ppermute x18 -> x16, starting transfers between devices: 20.6 us -> 19.5 us  [swapped(): return lax.ppermute(block, ('pipe', 'dp'), route)]
    pallas_call x8 -> x9, Pallas kernels: 6.98 us -> 6.98 us  [call(): pl.pallas_call(body, out_shape=outs, in_specs=in_specs, out_specs=out_spe...]
  transfers between devices with their start and end apart: 20 -> 17, of which waited for: 7 -> 11; matrix products, arithmetic and copies ran while one was open for 0% -> 0% of each run, Pallas kernels for 13% -> 11%
where the time goes in v13:
time: 47.3 us; the launch traced here: 47.1 us
  starting transfers between devices  20 us (42%)
  waiting for transfers between devices  17.6 us (37%)
  Pallas kernels  6.98 us (15%)
  between operations  1.35 us (3%)
  local copies, waits for them, and re-layouts  1.23 us (3%)
    ppermute x16, starting transfers between devices, swapped(): return lax.ppermute(block, ('pipe', 'dp'), route)  19.5 us
    ppermute x16, waiting for transfers between devices, swapped(): return lax.ppermute(block, ('pipe', 'dp'), route)  16.2 us
    pallas_call x9, Pallas kernels, call(): pl.pallas_call(body, out_shape=outs, in_specs=in_specs, out_specs=out_spe...  6.98 us
    ppermute x1, waiting for transfers between devices, passed_along(): return lax.ppermute(block, axis, route)  1.37 us
    unnamed x6, local copies, waits for them, and re-layouts  1.23 us
  transfers between devices with their start and end apart: 17, of which 11 were waited for; matrix products, arithmetic and copies ran while one was open for 0% of the time, Pallas kernels for 11%

profile of v13, /device:TPU:0, one launch (start us, length us, event | category | flops | bytes accessed | tf_op | source)
XLA Modules:
  0.0 47.1 jit_solution(1674545409467153159)
XLA Ops:
  0.6 0.5 %collective-permute-start.6 = (bf16[1,512,256]{2,1,0:T(8,128)(2,1)}, bf16[1,512,256]{2,1,0:T(8,128)(2,1)S(1)}, u32[]{:S(2)}, u32[]{:S(2)}) collective-permute-start(bf16[1,512,256]{2,1,0:T(8,128)(2,1)} %param.6), channel_id=1, source_target_pairs={{16,0},{0,16},{17,1},{1,17},{18,2},{2,18},{19,3},{3,19},{20,4},{4,... | collective-permute-start | bytes 786440 | tf_op jit(solution)/shard_map/ppermute | solution.py:22
  1.1 1.4 %collective-permute-done.6 = bf16[1,512,256]{2,1,0:T(8,128)(2,1)S(1)} collective-permute-done((bf16[1,512,256]{2,1,0:T(8,128)(2,1)}, bf16[1,512,256]{2,1,0:T(8,128)(2,1)S(1)}, u32[]{:S(2)}, u32[]{:S(2)}) %collective-permute-start.6) | collective-permute-done | bytes 262176 | tf_op jit(solution)/shard_map/ppermute | solution.py:22
  2.5 0.0 copy-start
  2.5 1.2 %copy-done = bf16[1,512,1024]{2,1,0:T(8,128)(2,1)S(1)} copy-done((bf16[1,512,1024]{2,1,0:T(8,128)(2,1)S(1)}, bf16[1,512,1024]{2,1,0:T(8,128)(2,1)}, u32[]{:S(2)}) %copy-start) | copy-done | bytes 1048600
  3.7 0.5 %grad.1 = (bf16[512,256]{1,0:T(8,128)(2,1)S(1)}, f32[512,256]{1,0:T(8,128)S(1)}) custom-call(bf16[512,1024]{1,0:T(8,128)(2,1)S(1)} %bitcast.7, bf16[512,256]{1,0:T(8,128)(2,1)S(1)} %bitcast.11), custom_call_target="tpu_custom_call" | custom-call | tf_op jit(solution)/shard_map/grad/pallas_call | solution.py:339
  4.3 2.9 %collective-permute-start.7 = (bf16[512,256]{1,0:T(8,128)(2,1)S(1)}, bf16[512,256]{1,0:T(8,128)(2,1)S(1)}, u32[]{:S(2)}, u32[]{:S(2)}) collective-permute-start(bf16[512,256]{1,0:T(8,128)(2,1)S(1)} %get-tuple-element.26), channel_id=1, source_target_pairs={{0,4},{4,0},{8,12},{12,8},{16,24},{20,28},{24,16},{28,20},{1,5},{5... | collective-permute-start | bytes 786440 | tf_op jit(solution)/shard_map/ppermute | solution.py:35
  7.2 1.1 %batch.1 = (bf16[272,256]{1,0:T(8,128)(2,1)S(1)}, bf16[272,256]{1,0:T(8,128)(2,1)S(1)}, bf16[272,256]{1,0:T(8,128)(2,1)S(1)}, bf16[272,256]{1,0:T(8,128)(2,1)S(1)}, f32[1088,256]{1,0:T(8,128)S(1)}) custom-call(bf16[512,1024]{1,0:T(8,128)(2,1)S(1)} %bitcast.8), custom_call_target="tpu_custom_call" | custom-call | tf_op jit(solution)/shard_map/batch/pallas_call | solution.py:339
  8.3 0.1 collective-permute-start.2
  8.4 2.0 %collective-permute-start.3 = (bf16[272,256]{1,0:T(8,128)(2,1)S(1)}, bf16[272,256]{1,0:T(8,128)(2,1)S(1)}, u32[]{:S(2)}, u32[]{:S(2)}) collective-permute-start(bf16[272,256]{1,0:T(8,128)(2,1)S(1)} %get-tuple-element.22), channel_id=1, source_target_pairs={{0,8},{4,12},{8,0},{12,4},{16,20},{20,16},{24,28},{28,24},{1,9},{5... | collective-permute-start | bytes 417800 | tf_op jit(solution)/shard_map/ppermute | solution.py:35
  10.4 1.5 %collective-permute-start = (bf16[272,256]{1,0:T(8,128)(2,1)S(1)}, bf16[272,256]{1,0:T(8,128)(2,1)S(1)}, u32[]{:S(2)}, u32[]{:S(2)}) collective-permute-start(bf16[272,256]{1,0:T(8,128)(2,1)S(1)} %get-tuple-element.19), channel_id=1, source_target_pairs={{0,4},{4,0},{8,12},{12,8},{16,24},{20,28},{24,16},{28,20},{1,5},{5... | collective-permute-start | bytes 417800 | tf_op jit(solution)/shard_map/ppermute | solution.py:35
  11.9 0.5 %collective-permute-start.1 = (bf16[272,256]{1,0:T(8,128)(2,1)S(1)}, bf16[272,256]{1,0:T(8,128)(2,1)S(1)}, u32[]{:S(2)}, u32[]{:S(2)}) collective-permute-start(bf16[272,256]{1,0:T(8,128)(2,1)S(1)} %get-tuple-element.20), channel_id=1, source_target_pairs={{0,8},{4,12},{8,0},{12,4},{16,20},{20,16},{24,28},{28,24},{1,9},{5... | collective-permute-start | bytes 417800 | tf_op jit(solution)/shard_map/ppermute | solution.py:35
  12.4 2.7 %collective-permute-done.2.refs_1_ = bf16[272,256]{1,0:T(8,128)(2,1)S(1)} collective-permute-done((bf16[272,256]{1,0:T(8,128)(2,1)S(1)}, bf16[272,256]{1,0:T(8,128)(2,1)S(1)}, u32[]{:S(2)}, u32[]{:S(2)}) %collective-permute-start.2) | collective-permute-done | bytes 139296 | tf_op jit(solution)/shard_map/ppermute | solution.py:35
  15.1 0.0 collective-permute-done.3.refs_2_
  15.1 0.0 copy-start.1
  15.1 2.5 %collective-permute-start.4 = (bf16[272,256]{1,0:T(8,128)(2,1)S(1)}, bf16[272,256]{1,0:T(8,128)(2,1)S(1)}, u32[]{:S(2)}, u32[]{:S(2)}) collective-permute-start(bf16[272,256]{1,0:T(8,128)(2,1)S(1)} %get-tuple-element.23), channel_id=1, source_target_pairs={{0,4},{4,0},{8,12},{12,8},{16,24},{20,28},{24,16},{28,20},{1,5},{5... | collective-permute-start | bytes 417800 | tf_op jit(solution)/shard_map/ppermute | solution.py:35
  17.6 1.5 %collective-permute-start.5 = (bf16[272,256]{1,0:T(8,128)(2,1)S(1)}, bf16[272,256]{1,0:T(8,128)(2,1)S(1)}, u32[]{:S(2)}, u32[]{:S(2)}) collective-permute-start(bf16[272,256]{1,0:T(8,128)(2,1)S(1)} %get-tuple-element.24), channel_id=1, source_target_pairs={{0,8},{4,12},{8,0},{12,4},{16,20},{20,16},{24,28},{28,24},{1,9},{5... | collective-permute-start | bytes 417800 | tf_op jit(solution)/shard_map/ppermute | solution.py:35
  19.1 0.0 collective-permute-done.7.refs_1_
  19.2 0.6 %collective-permute-start.8 = (bf16[256,256]{1,0:T(8,128)(2,1)S(1)}, bf16[256,256]{1,0:T(8,128)(2,1)S(1)}, u32[]{:S(2)}, u32[]{:S(2)}) collective-permute-start(bf16[256,256]{1,0:T(8,128)(2,1)S(1)} %strip_relay.1), channel_id=1, source_target_pairs={{0,8},{4,12},{8,0},{12,4},{16,20},{20,16},{24,28},{28,24},{1,9},{5... | collective-permute-start | bytes 393224 | tf_op jit(solution)/shard_map/ppermute | solution.py:35
  19.7 0.0 collective-permute-done.refs_1_
  19.7 0.0 collective-permute-done.1.refs_2_
  19.7 2.4 %collective-permute-done.4.refs_3_ = bf16[272,256]{1,0:T(8,128)(2,1)S(1)} collective-permute-done((bf16[272,256]{1,0:T(8,128)(2,1)S(1)}, bf16[272,256]{1,0:T(8,128)(2,1)S(1)}, u32[]{:S(2)}, u32[]{:S(2)}) %collective-permute-start.4) | collective-permute-done | bytes 139296 | tf_op jit(solution)/shard_map/ppermute | solution.py:35
  22.1 0.5 %collective-permute-done.5.refs_4_ = bf16[272,256]{1,0:T(8,128)(2,1)S(1)} collective-permute-done((bf16[272,256]{1,0:T(8,128)(2,1)S(1)}, bf16[272,256]{1,0:T(8,128)(2,1)S(1)}, u32[]{:S(2)}, u32[]{:S(2)}) %collective-permute-start.5) | collective-permute-done | bytes 139296 | tf_op jit(solution)/shard_map/ppermute | solution.py:35
  22.7 1.5 %collective-permute-done.8.refs_6_.refs_2_ = bf16[256,256]{1,0:T(8,128)(2,1)S(1)} collective-permute-done((bf16[256,256]{1,0:T(8,128)(2,1)S(1)}, bf16[256,256]{1,0:T(8,128)(2,1)S(1)}, u32[]{:S(2)}, u32[]{:S(2)}) %collective-permute-start.8) | collective-permute-done | bytes 131104 | tf_op jit(solution)/shard_map/ppermute | solution.py:35
  24.2 0.0 copy-done.1
  24.2 0.4 factor.1
  24.6 1.5 %collective-permute-start.12 = (bf16[288,256]{1,0:T(8,128)(2,1)S(1)}, bf16[288,256]{1,0:T(8,128)(2,1)S(1)}, u32[]{:S(2)}, u32[]{:S(2)}) collective-permute-start(bf16[288,256]{1,0:T(8,128)(2,1)S(1)} %get-tuple-element.29.refs_3_), channel_id=1, source_target_pairs={{0,8},{4,12},{8,0},{12,4},{16,20},{20,16},{24,28},{28,24},{1,9},{5... | collective-permute-start | bytes 442376 | tf_op jit(solution)/shard_map/ppermute | solution.py:35
  26.1 0.5 %collective-permute-start.10 = (bf16[288,256]{1,0:T(8,128)(2,1)S(1)}, bf16[288,256]{1,0:T(8,128)(2,1)S(1)}, u32[]{:S(2)}, u32[]{:S(2)}) collective-permute-start(bf16[288,256]{1,0:T(8,128)(2,1)S(1)} %get-tuple-element.29.refs_3_), channel_id=1, source_target_pairs={{0,4},{4,0},{8,12},{12,8},{16,24},{20,28},{24,16},{28,20},{1,5},{5... | collective-permute-start | bytes 442376 | tf_op jit(solution)/shard_map/ppermute | solution.py:35
  26.6 1.5 %collective-permute-start.9 = (bf16[272,256]{1,0:T(8,128)(2,1)S(1)}, bf16[272,256]{1,0:T(8,128)(2,1)S(1)}, u32[]{:S(2)}, u32[]{:S(2)}) collective-permute-start(bf16[272,256]{1,0:T(8,128)(2,1)S(1)} %get-tuple-element.28.refs_2_), channel_id=1, source_target_pairs={{0,4},{4,0},{8,12},{12,8},{16,24},{20,28},{24,16},{28,20},{1,5},{5... | collective-permute-start | bytes 417800 | tf_op jit(solution)/shard_map/ppermute | solution.py:35
  28.1 0.6 %collective-permute-start.11 = (bf16[272,256]{1,0:T(8,128)(2,1)S(1)}, bf16[272,256]{1,0:T(8,128)(2,1)S(1)}, u32[]{:S(2)}, u32[]{:S(2)}) collective-permute-start(bf16[272,256]{1,0:T(8,128)(2,1)S(1)} %get-tuple-element.28.refs_2_), channel_id=1, source_target_pairs={{0,8},{4,12},{8,0},{12,4},{16,20},{20,16},{24,28},{28,24},{1,9},{5... | collective-permute-start | bytes 417800 | tf_op jit(solution)/shard_map/ppermute | solution.py:35
  28.7 2.7 %collective-permute-done.12.refs_7_.refs_4_ = bf16[288,256]{1,0:T(8,128)(2,1)S(1)} collective-permute-done((bf16[288,256]{1,0:T(8,128)(2,1)S(1)}, bf16[288,256]{1,0:T(8,128)(2,1)S(1)}, u32[]{:S(2)}, u32[]{:S(2)}) %collective-permute-start.12) | collective-permute-done | bytes 147488 | tf_op jit(solution)/shard_map/ppermute | solution.py:35
  31.5 0.5 %collective-permute-start.14 = (bf16[288,256]{1,0:T(8,128)(2,1)S(1)}, bf16[288,256]{1,0:T(8,128)(2,1)S(1)}, u32[]{:S(2)}, u32[]{:S(2)}) collective-permute-start(bf16[288,256]{1,0:T(8,128)(2,1)S(1)} %collective-permute-done.12.refs_7_.refs_4_), channel_id=1, source_target_pairs={{0,4},{4,0},{8,12},{12,8},{16,24},{20,28},{24,16},{28,20},{1,5},{5... | collective-permute-start | bytes 442376 | tf_op jit(solution)/shard_map/ppermute | solution.py:35
  32.0 0.9 %collective-permute-done.9.refs_4_.refs_3_ = bf16[272,256]{1,0:T(8,128)(2,1)S(1)} collective-permute-done((bf16[272,256]{1,0:T(8,128)(2,1)S(1)}, bf16[272,256]{1,0:T(8,128)(2,1)S(1)}, u32[]{:S(2)}, u32[]{:S(2)}) %collective-permute-start.9) | collective-permute-done | bytes 139296 | tf_op jit(solution)/shard_map/ppermute | solution.py:35
  32.9 1.2 %collective-permute-start.13 = (bf16[272,256]{1,0:T(8,128)(2,1)S(1)}, bf16[272,256]{1,0:T(8,128)(2,1)S(1)}, u32[]{:S(2)}, u32[]{:S(2)}) collective-permute-start(bf16[272,256]{1,0:T(8,128)(2,1)S(1)} %collective-permute-done.9.refs_4_.refs_3_), channel_id=1, source_target_pairs={{0,8},{4,12},{8,0},{12,4},{16,20},{20,16},{24,28},{28,24},{1,9},{5... | collective-permute-start | bytes 417800 | tf_op jit(solution)/shard_map/ppermute | solution.py:35
  34.1 0.5 %collective-permute-done.11.refs_6_ = bf16[272,256]{1,0:T(8,128)(2,1)S(1)} collective-permute-done((bf16[272,256]{1,0:T(8,128)(2,1)S(1)}, bf16[272,256]{1,0:T(8,128)(2,1)S(1)}, u32[]{:S(2)}, u32[]{:S(2)}) %collective-permute-start.11) | collective-permute-done | bytes 139296 | tf_op jit(solution)/shard_map/ppermute | solution.py:35
  34.6 0.0 collective-permute-done.10.refs_5_
  34.6 0.0 copy-start.2
  34.6 1.3 %collective-permute-start.15 = (bf16[256,256]{1,0:T(8,128)(2,1)S(1)}, bf16[256,256]{1,0:T(8,128)(2,1)S(1)}, u32[]{:S(2)}, u32[]{:S(2)}) collective-permute-start(bf16[256,256]{1,0:T(8,128)(2,1)S(1)} %strip.1.refs_0_), channel_id=1, source_target_pairs={{0,8},{4,12},{8,0},{12,4},{16,20},{20,16},{24,28},{28,24},{1,9},{5... | collective-permute-start | bytes 393224 | tf_op jit(solution)/shard_map/ppermute | solution.py:35
  35.9 2.0 %collective-permute-done.13.refs_8_.refs_2_ = bf16[272,256]{1,0:T(8,128)(2,1)S(1)} collective-permute-done((bf16[272,256]{1,0:T(8,128)(2,1)S(1)}, bf16[272,256]{1,0:T(8,128)(2,1)S(1)}, u32[]{:S(2)}, u32[]{:S(2)}) %collective-permute-start.13) | collective-permute-done | bytes 139296 | tf_op jit(solution)/shard_map/ppermute | solution.py:35
  37.9 1.7 %collective-permute-done.15.refs_1_ = bf16[256,256]{1,0:T(8,128)(2,1)S(1)} collective-permute-done((bf16[256,256]{1,0:T(8,128)(2,1)S(1)}, bf16[256,256]{1,0:T(8,128)(2,1)S(1)}, u32[]{:S(2)}, u32[]{:S(2)}) %collective-permute-start.15) | collective-permute-done | bytes 131104 | tf_op jit(solution)/shard_map/ppermute | solution.py:35
  39.7 0.0 collective-permute-done.14.refs_9_.refs_3_
  39.7 0.7 %collective-permute-start.16 = (bf16[512,256]{1,0:T(8,128)(2,1)S(1)}, bf16[512,256]{1,0:T(8,128)(2,1)S(1)}, u32[]{:S(2)}, u32[]{:S(2)}) collective-permute-start(bf16[512,256]{1,0:T(8,128)(2,1)S(1)} %pair.1.refs_0_), channel_id=1, source_target_pairs={{0,4},{4,0},{8,12},{12,8},{16,24},{20,28},{24,16},{28,20},{1,5},{5... | collective-permute-start | bytes 786440 | tf_op jit(solution)/shard_map/ppermute | solution.py:35
  41.1 3.8 %root.1 = (f32[256,1024]{1,0:T(8,128)}, bf16[256,1024]{1,0:T(8,128)(2,1)}, f32[8,128]{1,0:T(8,128)S(1)}) custom-call(s32[1,1]{1,0:T(1,128)S(6)} %copy.8.refs_0_, f32[640,256]{1,0:T(8,128)S(1)} %get-tuple-element.27.refs_1_, bf16[272,256]{1,0:T(8,128)(2,1)S(1)} %get-tuple-element.28.refs_2_, bf16[288,256]{1,0:T(8,128)(2,1)S(1)} %get-tuple-element.29.refs_3_, ...), custom_call_target="tpu_custom_call" | custom-call | tf_op jit(solution)/shard_map/root/pallas_call | solution.py:339
  44.9 1.2 %collective-permute-done.16.refs_1_ = bf16[512,256]{1,0:T(8,128)(2,1)S(1)} collective-permute-done((bf16[512,256]{1,0:T(8,128)(2,1)S(1)}, bf16[512,256]{1,0:T(8,128)(2,1)S(1)}, u32[]{:S(2)}, u32[]{:S(2)}) %collective-permute-start.16) | collective-permute-done | bytes 262176 | tf_op jit(solution)/shard_map/ppermute | solution.py:35
  46.1 0.0 copy-done.2
  46.1 1.0 %step.1 = bf16[256,256]{1,0:T(8,128)(2,1)} custom-call(bf16[512,256]{1,0:T(8,128)(2,1)S(1)} %pair.1.refs_0_, bf16[512,256]{1,0:T(8,128)(2,1)S(1)} %collective-permute-done.16.refs_1_, bf16[256,1024]{1,0:T(8,128)(2,1)S(1)} %bitcast.10, f32[8,128]{1,0:T(8,128)S(1)} %get-tuple-element.32.refs_3_), custom_call_target="tpu_custom_call" | custom-call | tf_op jit(solution)/shard_map/step/pallas_call | solution.py:339
  (4 shorter events, 0.1 us)
Async XLA Ops:
  0.6 1.9 %collective-permute-start.6 = (bf16[1,512,256]{2,1,0:T(8,128)(2,1)}, bf16[1,512,256]{2,1,0:T(8,128)(2,1)S(1)}, u32[]{:S(2)}, u32[]{:S(2)}) collective-permute-start(bf16[1,512,256]{2,1,0:T(8,128)(2,1)} %param.6), channel_id=1, source_target_pairs={{16,0},{0,16},{17,1},{1,17},{18,2},{2,18},{19,3},{3,19},{20,4},{4,... | collective-permute-start | bytes 786440 | tf_op jit(solution)/shard_map/ppermute | solution.py:22
  2.5 1.2 %copy-start = (bf16[1,512,1024]{2,1,0:T(8,128)(2,1)S(1)}, bf16[1,512,1024]{2,1,0:T(8,128)(2,1)}, u32[]{:S(2)}) copy-start(bf16[1,512,1024]{2,1,0:T(8,128)(2,1)} %param.5) | copy-start | bytes 3145732
  4.3 14.9 %collective-permute-start.7 = (bf16[512,256]{1,0:T(8,128)(2,1)S(1)}, bf16[512,256]{1,0:T(8,128)(2,1)S(1)}, u32[]{:S(2)}, u32[]{:S(2)}) collective-permute-start(bf16[512,256]{1,0:T(8,128)(2,1)S(1)} %get-tuple-element.26), channel_id=1, source_target_pairs={{0,4},{4,0},{8,12},{12,8},{16,24},{20,28},{24,16},{28,20},{1,5},{5... | collective-permute-start | bytes 786440 | tf_op jit(solution)/shard_map/ppermute | solution.py:35
  8.3 6.8 %collective-permute-start.2 = (bf16[272,256]{1,0:T(8,128)(2,1)S(1)}, bf16[272,256]{1,0:T(8,128)(2,1)S(1)}, u32[]{:S(2)}, u32[]{:S(2)}) collective-permute-start(bf16[272,256]{1,0:T(8,128)(2,1)S(1)} %get-tuple-element.21), channel_id=1, source_target_pairs={{0,4},{4,0},{8,12},{12,8},{16,24},{20,28},{24,16},{28,20},{1,5},{5... | collective-permute-start | bytes 417800 | tf_op jit(solution)/shard_map/ppermute | solution.py:35
  8.4 6.7 %collective-permute-start.3 = (bf16[272,256]{1,0:T(8,128)(2,1)S(1)}, bf16[272,256]{1,0:T(8,128)(2,1)S(1)}, u32[]{:S(2)}, u32[]{:S(2)}) collective-permute-start(bf16[272,256]{1,0:T(8,128)(2,1)S(1)} %get-tuple-element.22), channel_id=1, source_target_pairs={{0,8},{4,12},{8,0},{12,4},{16,20},{20,16},{24,28},{28,24},{1,9},{5... | collective-permute-start | bytes 417800 | tf_op jit(solution)/shard_map/ppermute | solution.py:35
  10.4 9.3 %collective-permute-start = (bf16[272,256]{1,0:T(8,128)(2,1)S(1)}, bf16[272,256]{1,0:T(8,128)(2,1)S(1)}, u32[]{:S(2)}, u32[]{:S(2)}) collective-permute-start(bf16[272,256]{1,0:T(8,128)(2,1)S(1)} %get-tuple-element.19), channel_id=1, source_target_pairs={{0,4},{4,0},{8,12},{12,8},{16,24},{20,28},{24,16},{28,20},{1,5},{5... | collective-permute-start | bytes 417800 | tf_op jit(solution)/shard_map/ppermute | solution.py:35
  11.9 7.8 %collective-permute-start.1 = (bf16[272,256]{1,0:T(8,128)(2,1)S(1)}, bf16[272,256]{1,0:T(8,128)(2,1)S(1)}, u32[]{:S(2)}, u32[]{:S(2)}) collective-permute-start(bf16[272,256]{1,0:T(8,128)(2,1)S(1)} %get-tuple-element.20), channel_id=1, source_target_pairs={{0,8},{4,12},{8,0},{12,4},{16,20},{20,16},{24,28},{28,24},{1,9},{5... | collective-permute-start | bytes 417800 | tf_op jit(solution)/shard_map/ppermute | solution.py:35
  15.1 9.1 %copy-start.1 = (f32[1,1,256,1024]{3,2,1,0:T(8,128)S(1)}, f32[1,1,256,1024]{3,2,1,0:T(8,128)}, u32[]{:S(2)}) copy-start(f32[1,1,256,1024]{3,2,1,0:T(8,128)} %param.7) | copy-start | bytes 3145732
  15.1 7.0 %collective-permute-start.4 = (bf16[272,256]{1,0:T(8,128)(2,1)S(1)}, bf16[272,256]{1,0:T(8,128)(2,1)S(1)}, u32[]{:S(2)}, u32[]{:S(2)}) collective-permute-start(bf16[272,256]{1,0:T(8,128)(2,1)S(1)} %get-tuple-element.23), channel_id=1, source_target_pairs={{0,4},{4,0},{8,12},{12,8},{16,24},{20,28},{24,16},{28,20},{1,5},{5... | collective-permute-start | bytes 417800 | tf_op jit(solution)/shard_map/ppermute | solution.py:35
  17.6 5.1 %collective-permute-start.5 = (bf16[272,256]{1,0:T(8,128)(2,1)S(1)}, bf16[272,256]{1,0:T(8,128)(2,1)S(1)}, u32[]{:S(2)}, u32[]{:S(2)}) collective-permute-start(bf16[272,256]{1,0:T(8,128)(2,1)S(1)} %get-tuple-element.24), channel_id=1, source_target_pairs={{0,8},{4,12},{8,0},{12,4},{16,20},{20,16},{24,28},{28,24},{1,9},{5... | collective-permute-start | bytes 417800 | tf_op jit(solution)/shard_map/ppermute | solution.py:35
  19.2 5.0 %collective-permute-start.8 = (bf16[256,256]{1,0:T(8,128)(2,1)S(1)}, bf16[256,256]{1,0:T(8,128)(2,1)S(1)}, u32[]{:S(2)}, u32[]{:S(2)}) collective-permute-start(bf16[256,256]{1,0:T(8,128)(2,1)S(1)} %strip_relay.1), channel_id=1, source_target_pairs={{0,8},{4,12},{8,0},{12,4},{16,20},{20,16},{24,28},{28,24},{1,9},{5... | collective-permute-start | bytes 393224 | tf_op jit(solution)/shard_map/ppermute | solution.py:35
  24.6 6.8 %collective-permute-start.12 = (bf16[288,256]{1,0:T(8,128)(2,1)S(1)}, bf16[288,256]{1,0:T(8,128)(2,1)S(1)}, u32[]{:S(2)}, u32[]{:S(2)}) collective-permute-start(bf16[288,256]{1,0:T(8,128)(2,1)S(1)} %get-tuple-element.29.refs_3_), channel_id=1, source_target_pairs={{0,8},{4,12},{8,0},{12,4},{16,20},{20,16},{24,28},{28,24},{1,9},{5... | collective-permute-start | bytes 442376 | tf_op jit(solution)/shard_map/ppermute | solution.py:35
  26.1 8.5 %collective-permute-start.10 = (bf16[288,256]{1,0:T(8,128)(2,1)S(1)}, bf16[288,256]{1,0:T(8,128)(2,1)S(1)}, u32[]{:S(2)}, u32[]{:S(2)}) collective-permute-start(bf16[288,256]{1,0:T(8,128)(2,1)S(1)} %get-tuple-element.29.refs_3_), channel_id=1, source_target_pairs={{0,4},{4,0},{8,12},{12,8},{16,24},{20,28},{24,16},{28,20},{1,5},{5... | collective-permute-start | bytes 442376 | tf_op jit(solution)/shard_map/ppermute | solution.py:35
  26.6 6.3 %collective-permute-start.9 = (bf16[272,256]{1,0:T(8,128)(2,1)S(1)}, bf16[272,256]{1,0:T(8,128)(2,1)S(1)}, u32[]{:S(2)}, u32[]{:S(2)}) collective-permute-start(bf16[272,256]{1,0:T(8,128)(2,1)S(1)} %get-tuple-element.28.refs_2_), channel_id=1, source_target_pairs={{0,4},{4,0},{8,12},{12,8},{16,24},{20,28},{24,16},{28,20},{1,5},{5... | collective-permute-start | bytes 417800 | tf_op jit(solution)/shard_map/ppermute | solution.py:35
  28.1 6.5 %collective-permute-start.11 = (bf16[272,256]{1,0:T(8,128)(2,1)S(1)}, bf16[272,256]{1,0:T(8,128)(2,1)S(1)}, u32[]{:S(2)}, u32[]{:S(2)}) collective-permute-start(bf16[272,256]{1,0:T(8,128)(2,1)S(1)} %get-tuple-element.28.refs_2_), channel_id=1, source_target_pairs={{0,8},{4,12},{8,0},{12,4},{16,20},{20,16},{24,28},{28,24},{1,9},{5... | collective-permute-start | bytes 417800 | tf_op jit(solution)/shard_map/ppermute | solution.py:35
  31.5 8.2 %collective-permute-start.14 = (bf16[288,256]{1,0:T(8,128)(2,1)S(1)}, bf16[288,256]{1,0:T(8,128)(2,1)S(1)}, u32[]{:S(2)}, u32[]{:S(2)}) collective-permute-start(bf16[288,256]{1,0:T(8,128)(2,1)S(1)} %collective-permute-done.12.refs_7_.refs_4_), channel_id=1, source_target_pairs={{0,4},{4,0},{8,12},{12,8},{16,24},{20,28},{24,16},{28,20},{1,5},{5... | collective-permute-start | bytes 442376 | tf_op jit(solution)/shard_map/ppermute | solution.py:35
  32.9 5.1 %collective-permute-start.13 = (bf16[272,256]{1,0:T(8,128)(2,1)S(1)}, bf16[272,256]{1,0:T(8,128)(2,1)S(1)}, u32[]{:S(2)}, u32[]{:S(2)}) collective-permute-start(bf16[272,256]{1,0:T(8,128)(2,1)S(1)} %collective-permute-done.9.refs_4_.refs_3_), channel_id=1, source_target_pairs={{0,8},{4,12},{8,0},{12,4},{16,20},{20,16},{24,28},{28,24},{1,9},{5... | collective-permute-start | bytes 417800 | tf_op jit(solution)/shard_map/ppermute | solution.py:35
  34.6 11.5 %copy-start.2 = (bf16[1,1,256,1024]{3,2,1,0:T(8,128)(2,1)S(1)}, bf16[1,1,256,1024]{3,2,1,0:T(8,128)(2,1)}, u32[]{:S(2)}) copy-start(bf16[1,1,256,1024]{3,2,1,0:T(8,128)(2,1)} %param.8) | copy-start | bytes 1572868
  34.6 5.0 %collective-permute-start.15 = (bf16[256,256]{1,0:T(8,128)(2,1)S(1)}, bf16[256,256]{1,0:T(8,128)(2,1)S(1)}, u32[]{:S(2)}, u32[]{:S(2)}) collective-permute-start(bf16[256,256]{1,0:T(8,128)(2,1)S(1)} %strip.1.refs_0_), channel_id=1, source_target_pairs={{0,8},{4,12},{8,0},{12,4},{16,20},{20,16},{24,28},{28,24},{1,9},{5... | collective-permute-start | bytes 393224 | tf_op jit(solution)/shard_map/ppermute | solution.py:35
  39.7 6.4 %collective-permute-start.16 = (bf16[512,256]{1,0:T(8,128)(2,1)S(1)}, bf16[512,256]{1,0:T(8,128)(2,1)S(1)}, u32[]{:S(2)}, u32[]{:S(2)}) collective-permute-start(bf16[512,256]{1,0:T(8,128)(2,1)S(1)} %pair.1.refs_0_), channel_id=1, source_target_pairs={{0,4},{4,0},{8,12},{12,8},{16,24},{20,28},{24,16},{28,20},{1,5},{5... | collective-permute-start | bytes 786440 | tf_op jit(solution)/shard_map/ppermute | solution.py:35

commit v14 on v11

--- a/solution.py
+++ b/solution.py
@@ -33,10 +33,6 @@
         offset = 1 if section == turn else 2
         route += [(section * replicas + i, section * replicas + (i ^ offset)) for i in range(replicas)]
     return lax.ppermute(block, ("pipe", "dp"), route)
-
-
-def swapped_across(block):
-    return lax.ppermute(block, "dp", [(i, i ^ 3) for i in range(lax.axis_size("dp"))])
 
 
 def eye_of(rows, cols, shift=0):
@@ -183,6 +179,23 @@
     chunk[length:, :] = (
         keep[length : 2 * length, :] + got_y[length:, :].astype(F32) + relay_x[...].astype(F32)
     ).astype(BF16)
+
+
+def band(index, size):
+    return pl.ds(pl.multiple_of(index * size, size), size)
+
+
+def pair_kernel(own, got, send):
+    length = own.shape[0]
+    send[0:length, :] = own[...]
+    send[length:, :] = got[...]
+
+
+def second_kernel(upper, lower, got_x, got_y, send_x, send_y):
+    send_x[0 : lower.shape[0], :] = lower[...]
+    send_x[lower.shape[0] :, :] = got_y[...]
+    send_y[0 : upper.shape[0], :] = upper[...]
+    send_y[upper.shape[0] :, :] = got_x[...]
 
 
 def factor_kernel(replicas, keep, direct_x, direct_y, relay_x, relay_y, old, upper, lower, exact):
@@ -225,21 +238,27 @@
 
 
 def root_kernel(count, exact, *rest):
-    chunks = [rest[2 * i : 2 * i + 2] for i in range(4)]
-    factor_out, root_out, finished, factor, diagonal, rows, sent = rest[8:]
+    upper, lower, upper_x, lower_y, second_x, second_y = rest[:6]
+    factor_out, root_out, finished, factor, diagonal, rows, sent = rest[6:]
     share, order = root_out.shape
     half = share // 2
     starts = chunk_rows(share)
-    length = chunks[0][0].shape[0]
+    length, rest_length = upper.shape[0], lower.shape[0]
     mine = lax.axis_index("dp")
+    chunks = [
+        ((upper, 0), (lower, 0)),
+        ((upper_x, 0), (second_x, 0)),
+        ((second_y, 0), (lower_y, 0)),
+        ((second_y, length), (second_x, rest_length)),
+    ]
 
     def rows_of(position, start, count):
-        upper, lower = chunks[position]
-        if start + count <= length:
-            return upper[start : start + count, :]
-        if start >= length:
-            return lower[start - length : start - length + count, :]
-        return jnp.concatenate([upper[start:length, :], lower[0 : start + count - length, :]], axis=0)
+        parts = []
+        for (ref, at), low, high in zip(chunks[position], (0, length), (length, length + rest_length)):
+            first, last = max(start, low), min(start + count, high)
+            if first < last:
+                parts.append(ref[at + first - low : at + last - low, :])
+        return parts[0] if len(parts) == 1 else jnp.concatenate(parts, axis=0)
 
     copies = []
     for position, step in enumerate(offsets()):
@@ -301,23 +320,21 @@
         copy.wait()
 
 
-def step_kernel(replicas, *refs):
-    chunks = refs[:replicas]
-    old_root, step_out, grads, result = refs[replicas:]
+def step_kernel(replicas, pair, far, old_root, step_out, grads, result):
     share = old_root.shape[0]
     strip = step_out.shape[0] // replicas
+    length = pair.shape[0] // 2
     mine = lax.axis_index("dp")
-    for offset, chunk in enumerate(chunks):
+    strips = [(pair, 0, 0), (pair, length, along(1)), (far, 0, along(0)), (far, length, 3)]
+    for i, (ref, at, _) in enumerate(strips):
         for part in range(replicas):
-            grads[offset * strip : (offset + 1) * strip, part * share : (part + 1) * share] = chunk[
-                part * strip : (part + 1) * strip, :
-            ]
+            start = at + part * strip
+            grads[i * strip : (i + 1) * strip, part * share : (part + 1) * share] = ref[start : start + strip, :]
     result[...] = lax.dot_general(
         grads[...], old_root[...], (((1,), (1,)), ((), ())), preferred_element_type=F32
     ).astype(BF16)
-    for position, offset in enumerate(offsets()):
-        rows = pl.ds(pl.multiple_of((mine ^ offset) * strip, strip), strip)
-        step_out[rows, :] = result[position * strip : (position + 1) * strip, :]
+    for i, (_, _, offset) in enumerate(strips):
+        step_out[band(mine ^ offset, strip), :] = result[i * strip : (i + 1) * strip, :]
 
 
 def square_plan(acts, out_grad, old_factor, old_root, iter_count):
@@ -388,12 +405,14 @@
         old_factor[0, 0],
     )
     upper_x, lower_y = swapped(upper, 0), swapped(lower, 1)
-    lower_x, upper_y = swapped(lower, 0), swapped(upper, 1)
     strip_x, strip_y = call(
         grad_relay_kernel, [shape(grows // 2)] * 2, "grad_relay", grad_keep, grad_x, grad_y, after=[upper, lower]
     )
     strip_x, strip_y = swapped(strip_x, 0), swapped(strip_y, 1)
-    upper_far, lower_far = swapped(upper_x, 1), swapped(lower_y, 0)
+    on_x, on_y = call(
+        second_kernel, [shape(2 * length + 32), shape(2 * length)], "second", upper, lower, upper_x, lower_y
+    )
+    second_x, second_y = swapped(on_x, 0), swapped(on_y, 1)
     (strip,) = call(
         grad_total_kernel,
         [shape(grows)],
@@ -403,9 +422,11 @@
         grad_y,
         strip_x,
         strip_y,
-        after=[lower_x, upper_y],
-    )
-    strips = [strip, swapped(strip, 0), swapped(strip, 1), swapped_across(strip)]
+        after=[on_x],
+    )
+    strip_near = swapped(strip, 1)
+    (pair,) = call(pair_kernel, [shape(2 * grows)], "pair", strip, strip_near, after=[second_x, second_y])
+    pair_far = swapped(pair, 0)
     factor, root, finished = call(
         root_kernel,
         [shape(share, F32, order), shape(share, BF16, order), shape(8, F32, 128)],
@@ -415,11 +436,9 @@
         upper,
         lower,
         upper_x,
-        lower_x,
-        upper_y,
         lower_y,
-        upper_far,
-        lower_far,
+        second_x,
+        second_y,
         first=pltpu.SMEM,
         first_out=pl.ANY,
         scratch=[
@@ -433,7 +452,8 @@
         functools.partial(step_kernel, replicas),
         [shape(grows, BF16, share)],
         "step",
-        *strips,
+        pair,
+        pair_far,
         old_root[0, 0],
         after=[finished],
         scratch=[pltpu.VMEM((grows, order), BF16), pltpu.VMEM((grows, share), BF16)],

time: 44.2 us -> 49 us (1.11)
  waiting for transfers between devices: 13.9 us -> 22.1 us
  starting transfers between devices: 20.6 us -> 17.1 us
    ppermute x18 -> x16, waiting for transfers between devices: 13.9 us -> 22.1 us  [swapped(): return lax.ppermute(block, ('pipe', 'dp'), route)]
    ppermute x1 -> x0, starting transfers between devices: 2.77 us -> none  [swapped_across(): lax.ppermute(block, 'dp', [(i, i ^ 3) for i in range(lax.axis_size('dp'))])]
    ppermute x1, starting transfers between devices: 0.52 us -> 0.01 us  [passed_along(): return lax.ppermute(block, axis, route)]
    ppermute x18 -> x16, starting transfers between devices: 17.3 us -> 17.1 us  [swapped(): return lax.ppermute(block, ('pipe', 'dp'), route)]
    pallas_call x8 -> x10, Pallas kernels: 6.99 us -> 7.05 us  [call(): pl.pallas_call(body, out_shape=outs, in_specs=in_specs, out_specs=out_spe...]
  transfers between devices with their start and end apart: 20 -> 17, of which waited for: 8 -> 11; matrix products, arithmetic and copies ran while one was open for 0% -> 0% of each run, Pallas kernels for 14% -> 10%
where the time goes in v14:
time: 49 us; the launch traced here: 48.8 us
  waiting for transfers between devices  22.1 us (45%)
  starting transfers between devices  17.1 us (35%)
  Pallas kernels  7.05 us (14%)
  between operations  1.36 us (3%)
  local copies, waits for them, and re-layouts  1.23 us (3%)
    ppermute x16, waiting for transfers between devices, swapped(): return lax.ppermute(block, ('pipe', 'dp'), route)  22.1 us
    ppermute x16, starting transfers between devices, swapped(): return lax.ppermute(block, ('pipe', 'dp'), route)  17.1 us
    pallas_call x10, Pallas kernels, call(): pl.pallas_call(body, out_shape=outs, in_specs=in_specs, out_specs=out_spe...  7.05 us
    unnamed x6, local copies, waits for them, and re-layouts  1.23 us
  transfers between devices with their start and end apart: 17, of which 11 were waited for; matrix products, arithmetic and copies ran while one was open for 0% of the time, Pallas kernels for 10%

profile of v14, /device:TPU:0, one launch (start us, length us, event | category | flops | bytes accessed | tf_op | source)
XLA Modules:
  0.0 48.8 jit_solution(6044908129322008621)
XLA Ops:
  0.6 0.0 copy-start
  0.6 1.2 %copy-done = bf16[1,512,1024]{2,1,0:T(8,128)(2,1)S(1)} copy-done((bf16[1,512,1024]{2,1,0:T(8,128)(2,1)S(1)}, bf16[1,512,1024]{2,1,0:T(8,128)(2,1)}, u32[]{:S(2)}) %copy-start) | copy-done | bytes 1048600
  1.9 0.0 copy-start.1
  1.9 1.1 %batch.1 = (bf16[272,256]{1,0:T(8,128)(2,1)S(1)}, bf16[272,256]{1,0:T(8,128)(2,1)S(1)}, bf16[272,256]{1,0:T(8,128)(2,1)S(1)}, bf16[272,256]{1,0:T(8,128)(2,1)S(1)}, f32[1088,256]{1,0:T(8,128)S(1)}) custom-call(bf16[512,1024]{1,0:T(8,128)(2,1)S(1)} %bitcast.7), custom_call_target="tpu_custom_call" | custom-call | tf_op jit(solution)/shard_map/batch/pallas_call | solution.py:364
  3.0 3.0 %collective-permute-start.2 = (bf16[272,256]{1,0:T(8,128)(2,1)S(1)}, bf16[272,256]{1,0:T(8,128)(2,1)S(1)}, u32[]{:S(2)}, u32[]{:S(2)}) collective-permute-start(bf16[272,256]{1,0:T(8,128)(2,1)S(1)} %get-tuple-element.26), channel_id=1, source_target_pairs={{0,4},{4,0},{8,12},{12,8},{16,24},{20,28},{24,16},{28,20},{1,5},{5... | collective-permute-start | bytes 417800 | tf_op jit(solution)/shard_map/ppermute | solution.py:35
  6.0 1.5 %collective-permute-start.3 = (bf16[272,256]{1,0:T(8,128)(2,1)S(1)}, bf16[272,256]{1,0:T(8,128)(2,1)S(1)}, u32[]{:S(2)}, u32[]{:S(2)}) collective-permute-start(bf16[272,256]{1,0:T(8,128)(2,1)S(1)} %get-tuple-element.27), channel_id=1, source_target_pairs={{0,8},{4,12},{8,0},{12,4},{16,20},{20,16},{24,28},{28,24},{1,9},{5... | collective-permute-start | bytes 417800 | tf_op jit(solution)/shard_map/ppermute | solution.py:35
  7.5 0.0 collective-permute-start.10
  7.5 0.5 %collective-permute-start = (bf16[272,256]{1,0:T(8,128)(2,1)S(1)}, bf16[272,256]{1,0:T(8,128)(2,1)S(1)}, u32[]{:S(2)}, u32[]{:S(2)}) collective-permute-start(bf16[272,256]{1,0:T(8,128)(2,1)S(1)} %get-tuple-element.24), channel_id=1, source_target_pairs={{0,4},{4,0},{8,12},{12,8},{16,24},{20,28},{24,16},{28,20},{1,5},{5... | collective-permute-start | bytes 417800 | tf_op jit(solution)/shard_map/ppermute | solution.py:35
  8.0 0.1 collective-permute-start.1
  8.1 1.9 %collective-permute-done.2.refs_1_ = bf16[272,256]{1,0:T(8,128)(2,1)S(1)} collective-permute-done((bf16[272,256]{1,0:T(8,128)(2,1)S(1)}, bf16[272,256]{1,0:T(8,128)(2,1)S(1)}, u32[]{:S(2)}, u32[]{:S(2)}) %collective-permute-start.2) | collective-permute-done | bytes 139296 | tf_op jit(solution)/shard_map/ppermute | solution.py:35
  9.9 1.6 %collective-permute-done.3.refs_2_ = bf16[272,256]{1,0:T(8,128)(2,1)S(1)} collective-permute-done((bf16[272,256]{1,0:T(8,128)(2,1)S(1)}, bf16[272,256]{1,0:T(8,128)(2,1)S(1)}, u32[]{:S(2)}, u32[]{:S(2)}) %collective-permute-start.3) | collective-permute-done | bytes 139296 | tf_op jit(solution)/shard_map/ppermute | solution.py:35
  11.5 0.1 relay.1
  11.6 1.0 %collective-permute-start.4 = (bf16[272,256]{1,0:T(8,128)(2,1)S(1)}, bf16[272,256]{1,0:T(8,128)(2,1)S(1)}, u32[]{:S(2)}, u32[]{:S(2)}) collective-permute-start(bf16[272,256]{1,0:T(8,128)(2,1)S(1)} %get-tuple-element.28.refs_2_), channel_id=1, source_target_pairs={{0,4},{4,0},{8,12},{12,8},{16,24},{20,28},{24,16},{28,20},{1,5},{5... | collective-permute-start | bytes 417800 | tf_op jit(solution)/shard_map/ppermute | solution.py:35
  12.6 1.9 %collective-permute-start.5 = (bf16[272,256]{1,0:T(8,128)(2,1)S(1)}, bf16[272,256]{1,0:T(8,128)(2,1)S(1)}, u32[]{:S(2)}, u32[]{:S(2)}) collective-permute-start(bf16[272,256]{1,0:T(8,128)(2,1)S(1)} %get-tuple-element.29.refs_3_), channel_id=1, source_target_pairs={{0,8},{4,12},{8,0},{12,4},{16,20},{20,16},{24,28},{28,24},{1,9},{5... | collective-permute-start | bytes 417800 | tf_op jit(solution)/shard_map/ppermute | solution.py:35
  14.5 0.0 collective-permute-done.refs_1_
  14.5 0.0 collective-permute-done.1.refs_2_
  14.6 2.2 %collective-permute-done.4.refs_3_ = bf16[272,256]{1,0:T(8,128)(2,1)S(1)} collective-permute-done((bf16[272,256]{1,0:T(8,128)(2,1)S(1)}, bf16[272,256]{1,0:T(8,128)(2,1)S(1)}, u32[]{:S(2)}, u32[]{:S(2)}) %collective-permute-start.4) | collective-permute-done | bytes 139296 | tf_op jit(solution)/shard_map/ppermute | solution.py:35
  16.8 0.8 %collective-permute-done.5.refs_4_ = bf16[272,256]{1,0:T(8,128)(2,1)S(1)} collective-permute-done((bf16[272,256]{1,0:T(8,128)(2,1)S(1)}, bf16[272,256]{1,0:T(8,128)(2,1)S(1)}, u32[]{:S(2)}, u32[]{:S(2)}) %collective-permute-start.5) | collective-permute-done | bytes 139296 | tf_op jit(solution)/shard_map/ppermute | solution.py:35
  17.6 0.0 copy-done.1
  17.6 0.4 factor.1
  18.1 2.0 %collective-permute-start.7 = (bf16[288,256]{1,0:T(8,128)(2,1)S(1)}, bf16[288,256]{1,0:T(8,128)(2,1)S(1)}, u32[]{:S(2)}, u32[]{:S(2)}) collective-permute-start(bf16[288,256]{1,0:T(8,128)(2,1)S(1)} %get-tuple-element.32.refs_1_.refs_3_.refs_4_), channel_id=1, source_target_pairs={{0,8},{4,12},{8,0},{12,4},{16,20},{20,16},{24,28},{28,24},{1,9},{5... | collective-permute-start | bytes 442376 | tf_op jit(solution)/shard_map/ppermute | solution.py:35
  20.1 1.6 %collective-permute-start.6 = (bf16[272,256]{1,0:T(8,128)(2,1)S(1)}, bf16[272,256]{1,0:T(8,128)(2,1)S(1)}, u32[]{:S(2)}, u32[]{:S(2)}) collective-permute-start(bf16[272,256]{1,0:T(8,128)(2,1)S(1)} %get-tuple-element.31.refs_0_.refs_2_.refs_3_), channel_id=1, source_target_pairs={{0,4},{4,0},{8,12},{12,8},{16,24},{20,28},{24,16},{28,20},{1,5},{5... | collective-permute-start | bytes 417800 | tf_op jit(solution)/shard_map/ppermute | solution.py:35
  21.7 0.0 collective-permute-done.10
  21.7 0.5 %grad.1 = (bf16[256,256]{1,0:T(8,128)(2,1)S(1)}, bf16[256,256]{1,0:T(8,128)(2,1)S(1)}, f32[512,256]{1,0:T(8,128)S(1)}) custom-call(bf16[512,1024]{1,0:T(8,128)(2,1)S(1)} %bitcast.8, bf16[512,256]{1,0:T(8,128)(2,1)S(1)} %bitcast.11, bf16[272,256]{1,0:T(8,128)(2,1)S(1)} %get-tuple-element.28.refs_2_, bf16[272,256]{1,0:T(8,128)(2,1)S(1)} %get-tuple-element.29.refs_3_), custom_call_target="tpu_custom_call" | custom-call | tf_op jit(solution)/shard_map/grad/pallas_call | solution.py:364
  22.2 0.5 %collective-permute-start.11 = (bf16[256,256]{1,0:T(8,128)(2,1)S(1)}, bf16[256,256]{1,0:T(8,128)(2,1)S(1)}, u32[]{:S(2)}, u32[]{:S(2)}) collective-permute-start(bf16[256,256]{1,0:T(8,128)(2,1)S(1)} %get-tuple-element.38), channel_id=1, source_target_pairs={{0,4},{4,0},{8,12},{12,8},{16,24},{20,28},{24,16},{28,20},{1,5},{5... | collective-permute-start | bytes 393224 | tf_op jit(solution)/shard_map/ppermute | solution.py:35
  22.7 0.1 collective-permute-start.12
  22.8 3.1 %collective-permute-done.6.refs_2_.refs_4_ = bf16[272,256]{1,0:T(8,128)(2,1)S(1)} collective-permute-done((bf16[272,256]{1,0:T(8,128)(2,1)S(1)}, bf16[272,256]{1,0:T(8,128)(2,1)S(1)}, u32[]{:S(2)}, u32[]{:S(2)}) %collective-permute-start.6) | collective-permute-done | bytes 139296 | tf_op jit(solution)/shard_map/ppermute | solution.py:35
  25.9 0.0 collective-permute-done.7.refs_3_.refs_5_
  25.9 1.0 %collective-permute-start.8 = (bf16[576,256]{1,0:T(8,128)(2,1)S(1)}, bf16[576,256]{1,0:T(8,128)(2,1)S(1)}, u32[]{:S(2)}, u32[]{:S(2)}) collective-permute-start(bf16[576,256]{1,0:T(8,128)(2,1)S(1)} %get-tuple-element.33.refs_5_), channel_id=1, source_target_pairs={{0,4},{4,0},{8,12},{12,8},{16,24},{20,28},{24,16},{28,20},{1,5},{5... | collective-permute-start | bytes 884744 | tf_op jit(solution)/shard_map/ppermute | solution.py:35
  26.9 0.7 %collective-permute-start.9 = (bf16[544,256]{1,0:T(8,128)(2,1)S(1)}, bf16[544,256]{1,0:T(8,128)(2,1)S(1)}, u32[]{:S(2)}, u32[]{:S(2)}) collective-permute-start(bf16[544,256]{1,0:T(8,128)(2,1)S(1)} %get-tuple-element.34), channel_id=1, source_target_pairs={{0,8},{4,12},{8,0},{12,4},{16,20},{20,16},{24,28},{28,24},{1,9},{5... | collective-permute-start | bytes 835592 | tf_op jit(solution)/shard_map/ppermute | solution.py:35
  27.7 0.5 collective-permute-done.11.refs_1_
  28.1 0.8 %collective-permute-done.12.refs_2_ = bf16[256,256]{1,0:T(8,128)(2,1)S(1)} collective-permute-done((bf16[256,256]{1,0:T(8,128)(2,1)S(1)}, bf16[256,256]{1,0:T(8,128)(2,1)S(1)}, u32[]{:S(2)}, u32[]{:S(2)}) %collective-permute-start.12) | collective-permute-done | bytes 131104 | tf_op jit(solution)/shard_map/ppermute | solution.py:35
  29.0 1.8 %collective-permute-start.13 = (bf16[128,256]{1,0:T(8,128)(2,1)S(1)}, bf16[128,256]{1,0:T(8,128)(2,1)S(1)}, u32[]{:S(2)}, u32[]{:S(2)}) collective-permute-start(bf16[128,256]{1,0:T(8,128)(2,1)S(1)} %get-tuple-element.40), channel_id=1, source_target_pairs={{0,4},{4,0},{8,12},{12,8},{16,24},{20,28},{24,16},{28,20},{1,5},{5... | collective-permute-start | bytes 196616 | tf_op jit(solution)/shard_map/ppermute | solution.py:35
  30.8 0.1 collective-permute-start.14
  30.9 3.9 %collective-permute-done.13.refs_3_ = bf16[128,256]{1,0:T(8,128)(2,1)S(1)} collective-permute-done((bf16[128,256]{1,0:T(8,128)(2,1)S(1)}, bf16[128,256]{1,0:T(8,128)(2,1)S(1)}, u32[]{:S(2)}, u32[]{:S(2)}) %collective-permute-start.13) | collective-permute-done | bytes 65568 | tf_op jit(solution)/shard_map/ppermute | solution.py:35
  34.8 0.3 collective-permute-done.14.refs_4_
  35.1 0.6 %collective-permute-start.15 = (bf16[256,256]{1,0:T(8,128)(2,1)S(1)}, bf16[256,256]{1,0:T(8,128)(2,1)S(1)}, u32[]{:S(2)}, u32[]{:S(2)}) collective-permute-start(bf16[256,256]{1,0:T(8,128)(2,1)S(1)} %grad_total.1.refs_0_), channel_id=1, source_target_pairs={{0,8},{4,12},{8,0},{12,4},{16,20},{20,16},{24,28},{28,24},{1,9},{5... | collective-permute-start | bytes 393224 | tf_op jit(solution)/shard_map/ppermute | solution.py:35
  35.8 5.5 %collective-permute-done.15.refs_1_ = bf16[256,256]{1,0:T(8,128)(2,1)S(1)} collective-permute-done((bf16[256,256]{1,0:T(8,128)(2,1)S(1)}, bf16[256,256]{1,0:T(8,128)(2,1)S(1)}, u32[]{:S(2)}, u32[]{:S(2)}) %collective-permute-start.15) | collective-permute-done | bytes 131104 | tf_op jit(solution)/shard_map/ppermute | solution.py:35
  41.3 0.0 collective-permute-done.9.refs_7_.refs_3_
  41.3 0.0 collective-permute-done.8.refs_6_.refs_2_
  41.3 0.0 copy-start.2
  41.3 0.5 %collective-permute-start.16 = (bf16[512,256]{1,0:T(8,128)(2,1)S(1)}, bf16[512,256]{1,0:T(8,128)(2,1)S(1)}, u32[]{:S(2)}, u32[]{:S(2)}) collective-permute-start(bf16[512,256]{1,0:T(8,128)(2,1)S(1)} %pair.1.refs_0_), channel_id=1, source_target_pairs={{0,4},{4,0},{8,12},{12,8},{16,24},{20,28},{24,16},{28,20},{1,5},{5... | collective-permute-start | bytes 786440 | tf_op jit(solution)/shard_map/ppermute | solution.py:35
  42.5 3.8 %root.1 = (f32[256,1024]{1,0:T(8,128)}, bf16[256,1024]{1,0:T(8,128)(2,1)}, f32[8,128]{1,0:T(8,128)S(1)}) custom-call(s32[1,1]{1,0:T(1,128)S(6)} %copy.8.refs_0_, f32[640,256]{1,0:T(8,128)S(1)} %get-tuple-element.30.refs_1_, bf16[272,256]{1,0:T(8,128)(2,1)S(1)} %get-tuple-element.31.refs_0_.refs_2_.refs_3_, ...), custom_call_target="tpu_custom_call" | custom-call | tf_op jit(solution)/shard_map/root/pallas_call | solution.py:364
  46.4 1.4 %collective-permute-done.16.refs_1_ = bf16[512,256]{1,0:T(8,128)(2,1)S(1)} collective-permute-done((bf16[512,256]{1,0:T(8,128)(2,1)S(1)}, bf16[512,256]{1,0:T(8,128)(2,1)S(1)}, u32[]{:S(2)}, u32[]{:S(2)}) %collective-permute-start.16) | collective-permute-done | bytes 262176 | tf_op jit(solution)/shard_map/ppermute | solution.py:35
  47.8 0.0 copy-done.2
  47.8 1.0 %step.1 = bf16[256,256]{1,0:T(8,128)(2,1)} custom-call(bf16[512,256]{1,0:T(8,128)(2,1)S(1)} %pair.1.refs_0_, bf16[512,256]{1,0:T(8,128)(2,1)S(1)} %collective-permute-done.16.refs_1_, bf16[256,1024]{1,0:T(8,128)(2,1)S(1)} %bitcast.10, f32[8,128]{1,0:T(8,128)S(1)} %get-tuple-element.42.refs_3_), custom_call_target="tpu_custom_call" | custom-call | tf_op jit(solution)/shard_map/step/pallas_call | solution.py:364
  (4 shorter events, 0.1 us)
Async XLA Ops:
  0.6 1.2 %copy-start = (bf16[1,512,1024]{2,1,0:T(8,128)(2,1)S(1)}, bf16[1,512,1024]{2,1,0:T(8,128)(2,1)}, u32[]{:S(2)}) copy-start(bf16[1,512,1024]{2,1,0:T(8,128)(2,1)} %param.5) | copy-start | bytes 3145732
  1.9 15.8 %copy-start.1 = (f32[1,1,256,1024]{3,2,1,0:T(8,128)S(1)}, f32[1,1,256,1024]{3,2,1,0:T(8,128)}, u32[]{:S(2)}) copy-start(f32[1,1,256,1024]{3,2,1,0:T(8,128)} %param.7) | copy-start | bytes 3145732
  3.0 7.0 %collective-permute-start.2 = (bf16[272,256]{1,0:T(8,128)(2,1)S(1)}, bf16[272,256]{1,0:T(8,128)(2,1)S(1)}, u32[]{:S(2)}, u32[]{:S(2)}) collective-permute-start(bf16[272,256]{1,0:T(8,128)(2,1)S(1)} %get-tuple-element.26), channel_id=1, source_target_pairs={{0,4},{4,0},{8,12},{12,8},{16,24},{20,28},{24,16},{28,20},{1,5},{5... | collective-permute-start | bytes 417800 | tf_op jit(solution)/shard_map/ppermute | solution.py:35
  6.0 5.5 %collective-permute-start.3 = (bf16[272,256]{1,0:T(8,128)(2,1)S(1)}, bf16[272,256]{1,0:T(8,128)(2,1)S(1)}, u32[]{:S(2)}, u32[]{:S(2)}) collective-permute-start(bf16[272,256]{1,0:T(8,128)(2,1)S(1)} %get-tuple-element.27), channel_id=1, source_target_pairs={{0,8},{4,12},{8,0},{12,4},{16,20},{20,16},{24,28},{28,24},{1,9},{5... | collective-permute-start | bytes 417800 | tf_op jit(solution)/shard_map/ppermute | solution.py:35
  7.5 14.2 %collective-permute-start.10 = (bf16[1,512,256]{2,1,0:T(8,128)(2,1)}, bf16[1,512,256]{2,1,0:T(8,128)(2,1)S(1)}, u32[]{:S(2)}, u32[]{:S(2)}) collective-permute-start(bf16[1,512,256]{2,1,0:T(8,128)(2,1)} %param.6), channel_id=1, source_target_pairs={{16,0},{0,16},{17,1},{1,17},{18,2},{2,18},{19,3},{3,19},{20,4},{4,... | collective-permute-start | bytes 786440 | tf_op jit(solution)/shard_map/ppermute | solution.py:22
  7.5 7.0 %collective-permute-start = (bf16[272,256]{1,0:T(8,128)(2,1)S(1)}, bf16[272,256]{1,0:T(8,128)(2,1)S(1)}, u32[]{:S(2)}, u32[]{:S(2)}) collective-permute-start(bf16[272,256]{1,0:T(8,128)(2,1)S(1)} %get-tuple-element.24), channel_id=1, source_target_pairs={{0,4},{4,0},{8,12},{12,8},{16,24},{20,28},{24,16},{28,20},{1,5},{5... | collective-permute-start | bytes 417800 | tf_op jit(solution)/shard_map/ppermute | solution.py:35
  8.0 6.5 %collective-permute-start.1 = (bf16[272,256]{1,0:T(8,128)(2,1)S(1)}, bf16[272,256]{1,0:T(8,128)(2,1)S(1)}, u32[]{:S(2)}, u32[]{:S(2)}) collective-permute-start(bf16[272,256]{1,0:T(8,128)(2,1)S(1)} %get-tuple-element.25), channel_id=1, source_target_pairs={{0,8},{4,12},{8,0},{12,4},{16,20},{20,16},{24,28},{28,24},{1,9},{5... | collective-permute-start | bytes 417800 | tf_op jit(solution)/shard_map/ppermute | solution.py:35
  11.6 5.3 %collective-permute-start.4 = (bf16[272,256]{1,0:T(8,128)(2,1)S(1)}, bf16[272,256]{1,0:T(8,128)(2,1)S(1)}, u32[]{:S(2)}, u32[]{:S(2)}) collective-permute-start(bf16[272,256]{1,0:T(8,128)(2,1)S(1)} %get-tuple-element.28.refs_2_), channel_id=1, source_target_pairs={{0,4},{4,0},{8,12},{12,8},{16,24},{20,28},{24,16},{28,20},{1,5},{5... | collective-permute-start | bytes 417800 | tf_op jit(solution)/shard_map/ppermute | solution.py:35
  12.6 5.1 %collective-permute-start.5 = (bf16[272,256]{1,0:T(8,128)(2,1)S(1)}, bf16[272,256]{1,0:T(8,128)(2,1)S(1)}, u32[]{:S(2)}, u32[]{:S(2)}) collective-permute-start(bf16[272,256]{1,0:T(8,128)(2,1)S(1)} %get-tuple-element.29.refs_3_), channel_id=1, source_target_pairs={{0,8},{4,12},{8,0},{12,4},{16,20},{20,16},{24,28},{28,24},{1,9},{5... | collective-permute-start | bytes 417800 | tf_op jit(solution)/shard_map/ppermute | solution.py:35
  18.1 7.8 %collective-permute-start.7 = (bf16[288,256]{1,0:T(8,128)(2,1)S(1)}, bf16[288,256]{1,0:T(8,128)(2,1)S(1)}, u32[]{:S(2)}, u32[]{:S(2)}) collective-permute-start(bf16[288,256]{1,0:T(8,128)(2,1)S(1)} %get-tuple-element.32.refs_1_.refs_3_.refs_4_), channel_id=1, source_target_pairs={{0,8},{4,12},{8,0},{12,4},{16,20},{20,16},{24,28},{28,24},{1,9},{5... | collective-permute-start | bytes 442376 | tf_op jit(solution)/shard_map/ppermute | solution.py:35
  20.1 5.8 %collective-permute-start.6 = (bf16[272,256]{1,0:T(8,128)(2,1)S(1)}, bf16[272,256]{1,0:T(8,128)(2,1)S(1)}, u32[]{:S(2)}, u32[]{:S(2)}) collective-permute-start(bf16[272,256]{1,0:T(8,128)(2,1)S(1)} %get-tuple-element.31.refs_0_.refs_2_.refs_3_), channel_id=1, source_target_pairs={{0,4},{4,0},{8,12},{12,8},{16,24},{20,28},{24,16},{28,20},{1,5},{5... | collective-permute-start | bytes 417800 | tf_op jit(solution)/shard_map/ppermute | solution.py:35
  22.2 5.9 %collective-permute-start.11 = (bf16[256,256]{1,0:T(8,128)(2,1)S(1)}, bf16[256,256]{1,0:T(8,128)(2,1)S(1)}, u32[]{:S(2)}, u32[]{:S(2)}) collective-permute-start(bf16[256,256]{1,0:T(8,128)(2,1)S(1)} %get-tuple-element.38), channel_id=1, source_target_pairs={{0,4},{4,0},{8,12},{12,8},{16,24},{20,28},{24,16},{28,20},{1,5},{5... | collective-permute-start | bytes 393224 | tf_op jit(solution)/shard_map/ppermute | solution.py:35
  22.7 6.3 %collective-permute-start.12 = (bf16[256,256]{1,0:T(8,128)(2,1)S(1)}, bf16[256,256]{1,0:T(8,128)(2,1)S(1)}, u32[]{:S(2)}, u32[]{:S(2)}) collective-permute-start(bf16[256,256]{1,0:T(8,128)(2,1)S(1)} %get-tuple-element.39), channel_id=1, source_target_pairs={{0,8},{4,12},{8,0},{12,4},{16,20},{20,16},{24,28},{28,24},{1,9},{5... | collective-permute-start | bytes 393224 | tf_op jit(solution)/shard_map/ppermute | solution.py:35
  25.9 15.4 %collective-permute-start.8 = (bf16[576,256]{1,0:T(8,128)(2,1)S(1)}, bf16[576,256]{1,0:T(8,128)(2,1)S(1)}, u32[]{:S(2)}, u32[]{:S(2)}) collective-permute-start(bf16[576,256]{1,0:T(8,128)(2,1)S(1)} %get-tuple-element.33.refs_5_), channel_id=1, source_target_pairs={{0,4},{4,0},{8,12},{12,8},{16,24},{20,28},{24,16},{28,20},{1,5},{5... | collective-permute-start | bytes 884744 | tf_op jit(solution)/shard_map/ppermute | solution.py:35
  26.9 14.4 %collective-permute-start.9 = (bf16[544,256]{1,0:T(8,128)(2,1)S(1)}, bf16[544,256]{1,0:T(8,128)(2,1)S(1)}, u32[]{:S(2)}, u32[]{:S(2)}) collective-permute-start(bf16[544,256]{1,0:T(8,128)(2,1)S(1)} %get-tuple-element.34), channel_id=1, source_target_pairs={{0,8},{4,12},{8,0},{12,4},{16,20},{20,16},{24,28},{28,24},{1,9},{5... | collective-permute-start | bytes 835592 | tf_op jit(solution)/shard_map/ppermute | solution.py:35
  29.0 5.8 %collective-permute-start.13 = (bf16[128,256]{1,0:T(8,128)(2,1)S(1)}, bf16[128,256]{1,0:T(8,128)(2,1)S(1)}, u32[]{:S(2)}, u32[]{:S(2)}) collective-permute-start(bf16[128,256]{1,0:T(8,128)(2,1)S(1)} %get-tuple-element.40), channel_id=1, source_target_pairs={{0,4},{4,0},{8,12},{12,8},{16,24},{20,28},{24,16},{28,20},{1,5},{5... | collective-permute-start | bytes 196616 | tf_op jit(solution)/shard_map/ppermute | solution.py:35
  30.8 4.3 %collective-permute-start.14 = (bf16[128,256]{1,0:T(8,128)(2,1)S(1)}, bf16[128,256]{1,0:T(8,128)(2,1)S(1)}, u32[]{:S(2)}, u32[]{:S(2)}) collective-permute-start(bf16[128,256]{1,0:T(8,128)(2,1)S(1)} %get-tuple-element.41), channel_id=1, source_target_pairs={{0,8},{4,12},{8,0},{12,4},{16,20},{20,16},{24,28},{28,24},{1,9},{5... | collective-permute-start | bytes 196616 | tf_op jit(solution)/shard_map/ppermute | solution.py:35
  35.1 6.2 %collective-permute-start.15 = (bf16[256,256]{1,0:T(8,128)(2,1)S(1)}, bf16[256,256]{1,0:T(8,128)(2,1)S(1)}, u32[]{:S(2)}, u32[]{:S(2)}) collective-permute-start(bf16[256,256]{1,0:T(8,128)(2,1)S(1)} %grad_total.1.refs_0_), channel_id=1, source_target_pairs={{0,8},{4,12},{8,0},{12,4},{16,20},{20,16},{24,28},{28,24},{1,9},{5... | collective-permute-start | bytes 393224 | tf_op jit(solution)/shard_map/ppermute | solution.py:35
  41.3 6.5 %copy-start.2 = (bf16[1,1,256,1024]{3,2,1,0:T(8,128)(2,1)S(1)}, bf16[1,1,256,1024]{3,2,1,0:T(8,128)(2,1)}, u32[]{:S(2)}) copy-start(bf16[1,1,256,1024]{3,2,1,0:T(8,128)(2,1)} %param.8) | copy-start | bytes 1572868
  41.3 6.4 %collective-permute-start.16 = (bf16[512,256]{1,0:T(8,128)(2,1)S(1)}, bf16[512,256]{1,0:T(8,128)(2,1)S(1)}, u32[]{:S(2)}, u32[]{:S(2)}) collective-permute-start(bf16[512,256]{1,0:T(8,128)(2,1)S(1)} %pair.1.refs_0_), channel_id=1, source_target_pairs={{0,4},{4,0},{8,12},{12,8},{16,24},{20,28},{24,16},{28,20},{1,5},{5... | collective-permute-start | bytes 786440 | tf_op jit(solution)/shard_map/ppermute | solution.py:35

commit v15 on v12

--- a/solution.py
+++ b/solution.py
@@ -33,10 +33,6 @@
         offset = 1 if section == turn else 2
         route += [(section * replicas + i, section * replicas + (i ^ offset)) for i in range(replicas)]
     return lax.ppermute(block, ("pipe", "dp"), route)
-
-
-def swapped_across(block):
-    return lax.ppermute(block, "dp", [(i, i ^ 3) for i in range(lax.axis_size("dp"))])
 
 
 def eye_of(rows, cols, shift=0):
@@ -183,6 +179,16 @@
     chunk[length:, :] = (
         keep[length : 2 * length, :] + got_y[length:, :].astype(F32) + relay_x[...].astype(F32)
     ).astype(BF16)
+
+
+def band(index, size):
+    return pl.ds(pl.multiple_of(index * size, size), size)
+
+
+def pair_kernel(own, got, send):
+    length = own.shape[0]
+    send[0:length, :] = own[...]
+    send[length:, :] = got[...]
 
 
 def factor_kernel(replicas, keep, direct_x, direct_y, relay_x, relay_y, old, upper, lower, exact):
@@ -301,23 +307,21 @@
         copy.wait()
 
 
-def step_kernel(replicas, *refs):
-    chunks = refs[:replicas]
-    old_root, step_out, grads, result = refs[replicas:]
+def step_kernel(replicas, pair, far, old_root, step_out, grads, result):
     share = old_root.shape[0]
     strip = step_out.shape[0] // replicas
+    length = pair.shape[0] // 2
     mine = lax.axis_index("dp")
-    for offset, chunk in enumerate(chunks):
+    strips = [(pair, 0, 0), (pair, length, along(1)), (far, 0, along(0)), (far, length, 3)]
+    for i, (ref, at, _) in enumerate(strips):
         for part in range(replicas):
-            grads[offset * strip : (offset + 1) * strip, part * share : (part + 1) * share] = chunk[
-                part * strip : (part + 1) * strip, :
-            ]
+            start = at + part * strip
+            grads[i * strip : (i + 1) * strip, part * share : (part + 1) * share] = ref[start : start + strip, :]
     result[...] = lax.dot_general(
         grads[...], old_root[...], (((1,), (1,)), ((), ())), preferred_element_type=F32
     ).astype(BF16)
-    for position, offset in enumerate(offsets()):
-        rows = pl.ds(pl.multiple_of((mine ^ offset) * strip, strip), strip)
-        step_out[rows, :] = result[position * strip : (position + 1) * strip, :]
+    for i, (_, _, offset) in enumerate(strips):
+        step_out[band(mine ^ offset, strip), :] = result[i * strip : (i + 1) * strip, :]
 
 
 def square_plan(acts, out_grad, old_factor, old_root, iter_count):
@@ -403,9 +407,11 @@
         grad_y,
         strip_x,
         strip_y,
-        after=[upper_x, lower_y],
-    )
-    strips = [strip, swapped(strip, 0), swapped(strip, 1), swapped_across(strip)]
+        after=[upper],
+    )
+    strip_near = swapped(strip, 1)
+    (pair,) = call(pair_kernel, [shape(2 * grows)], "pair", strip, strip_near, after=[upper_far, lower_far, lower_x, upper_y])
+    pair_far = swapped(pair, 0)
     factor, root, finished = call(
         root_kernel,
         [shape(share, F32, order), shape(share, BF16, order), shape(8, F32, 128)],
@@ -433,7 +439,8 @@
         functools.partial(step_kernel, replicas),
         [shape(grows, BF16, share)],
         "step",
-        *strips,
+        pair,
+        pair_far,
         old_root[0, 0],
         after=[finished],
         scratch=[pltpu.VMEM((grows, order), BF16), pltpu.VMEM((grows, share), BF16)],

time: 43.9 us -> 45.7 us (1.041)
  waiting for transfers between devices: 11.8 us -> 15 us
  starting transfers between devices: 22.4 us -> 20.9 us
    ppermute x18, waiting for transfers between devices: 11.8 us -> 15 us  [swapped(): return lax.ppermute(block, ('pipe', 'dp'), route)]
    ppermute x1 -> x0, starting transfers between devices: 1.26 us -> none  [swapped_across(): lax.ppermute(block, 'dp', [(i, i ^ 3) for i in range(lax.axis_size('dp'))])]
    pallas_call x8 -> x9, Pallas kernels: 6.98 us -> 7.01 us  [call(): pl.pallas_call(body, out_shape=outs, in_specs=in_specs, out_specs=out_spe...]
  transfers between devices with their start and end apart: 20 -> 19, of which waited for: 7 -> 8; matrix products, arithmetic and copies ran while one was open for 0% -> 0% of each run, Pallas kernels for 13% -> 12%
where the time goes in v15:
time: 45.7 us; the launch traced here: 45.6 us
  starting transfers between devices  20.9 us (46%)
  waiting for transfers between devices  15 us (33%)
  Pallas kernels  7.01 us (15%)
  between operations  1.37 us (3%)
  local copies, waits for them, and re-layouts  1.24 us (3%)
    ppermute x18, starting transfers between devices, swapped(): return lax.ppermute(block, ('pipe', 'dp'), route)  20.4 us
    ppermute x18, waiting for transfers between devices, swapped(): return lax.ppermute(block, ('pipe', 'dp'), route)  15 us
    pallas_call x9, Pallas kernels, call(): pl.pallas_call(body, out_shape=outs, in_specs=in_specs, out_specs=out_spe...  7.01 us
    unnamed x6, local copies, waits for them, and re-layouts  1.24 us
  transfers between devices with their start and end apart: 19, of which 8 were waited for; matrix products, arithmetic and copies ran while one was open for 0% of the time, Pallas kernels for 12%

profile of v15, /device:TPU:0, one launch (start us, length us, event | category | flops | bytes accessed | tf_op | source)
XLA Modules:
  0.0 45.6 jit_solution(7999917169111289449)
XLA Ops:
  0.6 0.5 %collective-permute-start.6 = (bf16[1,512,256]{2,1,0:T(8,128)(2,1)}, bf16[1,512,256]{2,1,0:T(8,128)(2,1)S(1)}, u32[]{:S(2)}, u32[]{:S(2)}) collective-permute-start(bf16[1,512,256]{2,1,0:T(8,128)(2,1)} %param.6), channel_id=1, source_target_pairs={{16,0},{0,16},{17,1},{1,17},{18,2},{2,18},{19,3},{3,19},{20,4},{4,... | collective-permute-start | bytes 786440 | tf_op jit(solution)/shard_map/ppermute | solution.py:22
  1.1 0.0 copy-start
  1.1 1.2 %copy-done = bf16[1,512,1024]{2,1,0:T(8,128)(2,1)S(1)} copy-done((bf16[1,512,1024]{2,1,0:T(8,128)(2,1)S(1)}, bf16[1,512,1024]{2,1,0:T(8,128)(2,1)}, u32[]{:S(2)}) %copy-start) | copy-done | bytes 1048600
  2.4 1.1 %batch.1 = (bf16[272,256]{1,0:T(8,128)(2,1)S(1)}, bf16[272,256]{1,0:T(8,128)(2,1)S(1)}, bf16[272,256]{1,0:T(8,128)(2,1)S(1)}, bf16[272,256]{1,0:T(8,128)(2,1)S(1)}, f32[1088,256]{1,0:T(8,128)S(1)}) custom-call(bf16[512,1024]{1,0:T(8,128)(2,1)S(1)} %bitcast.7), custom_call_target="tpu_custom_call" | custom-call | tf_op jit(solution)/shard_map/batch/pallas_call | solution.py:351
  3.5 2.6 %collective-permute-start.2 = (bf16[272,256]{1,0:T(8,128)(2,1)S(1)}, bf16[272,256]{1,0:T(8,128)(2,1)S(1)}, u32[]{:S(2)}, u32[]{:S(2)}) collective-permute-start(bf16[272,256]{1,0:T(8,128)(2,1)S(1)} %get-tuple-element.24), channel_id=1, source_target_pairs={{0,4},{4,0},{8,12},{12,8},{16,24},{20,28},{24,16},{28,20},{1,5},{5... | collective-permute-start | bytes 417800 | tf_op jit(solution)/shard_map/ppermute | solution.py:35
  6.0 1.5 %collective-permute-start.3 = (bf16[272,256]{1,0:T(8,128)(2,1)S(1)}, bf16[272,256]{1,0:T(8,128)(2,1)S(1)}, u32[]{:S(2)}, u32[]{:S(2)}) collective-permute-start(bf16[272,256]{1,0:T(8,128)(2,1)S(1)} %get-tuple-element.25), channel_id=1, source_target_pairs={{0,8},{4,12},{8,0},{12,4},{16,20},{20,16},{24,28},{28,24},{1,9},{5... | collective-permute-start | bytes 417800 | tf_op jit(solution)/shard_map/ppermute | solution.py:35
  7.6 0.0 collective-permute-done.6
  7.6 0.5 %grad.1 = (bf16[256,256]{1,0:T(8,128)(2,1)S(1)}, bf16[256,256]{1,0:T(8,128)(2,1)S(1)}, f32[512,256]{1,0:T(8,128)S(1)}) custom-call(bf16[512,1024]{1,0:T(8,128)(2,1)S(1)} %bitcast.8, bf16[512,256]{1,0:T(8,128)(2,1)S(1)} %bitcast.11), custom_call_target="tpu_custom_call" | custom-call | tf_op jit(solution)/shard_map/grad/pallas_call | solution.py:351
  8.1 0.0 copy-start.1
  8.1 0.6 %collective-permute-start.7 = (bf16[256,256]{1,0:T(8,128)(2,1)S(1)}, bf16[256,256]{1,0:T(8,128)(2,1)S(1)}, u32[]{:S(2)}, u32[]{:S(2)}) collective-permute-start(bf16[256,256]{1,0:T(8,128)(2,1)S(1)} %get-tuple-element.29), channel_id=1, source_target_pairs={{0,4},{4,0},{8,12},{12,8},{16,24},{20,28},{24,16},{28,20},{1,5},{5... | collective-permute-start | bytes 393224 | tf_op jit(solution)/shard_map/ppermute | solution.py:35
  8.7 1.5 %collective-permute-start = (bf16[272,256]{1,0:T(8,128)(2,1)S(1)}, bf16[272,256]{1,0:T(8,128)(2,1)S(1)}, u32[]{:S(2)}, u32[]{:S(2)}) collective-permute-start(bf16[272,256]{1,0:T(8,128)(2,1)S(1)} %get-tuple-element.22), channel_id=1, source_target_pairs={{0,4},{4,0},{8,12},{12,8},{16,24},{20,28},{24,16},{28,20},{1,5},{5... | collective-permute-start | bytes 417800 | tf_op jit(solution)/shard_map/ppermute | solution.py:35
  10.2 0.5 %collective-permute-start.8 = (bf16[256,256]{1,0:T(8,128)(2,1)S(1)}, bf16[256,256]{1,0:T(8,128)(2,1)S(1)}, u32[]{:S(2)}, u32[]{:S(2)}) collective-permute-start(bf16[256,256]{1,0:T(8,128)(2,1)S(1)} %get-tuple-element.30), channel_id=1, source_target_pairs={{0,8},{4,12},{8,0},{12,4},{16,20},{20,16},{24,28},{28,24},{1,9},{5... | collective-permute-start | bytes 393224 | tf_op jit(solution)/shard_map/ppermute | solution.py:35
  10.7 0.0 collective-permute-done.2.refs_1_
  10.7 1.5 %collective-permute-start.1 = (bf16[272,256]{1,0:T(8,128)(2,1)S(1)}, bf16[272,256]{1,0:T(8,128)(2,1)S(1)}, u32[]{:S(2)}, u32[]{:S(2)}) collective-permute-start(bf16[272,256]{1,0:T(8,128)(2,1)S(1)} %get-tuple-element.23), channel_id=1, source_target_pairs={{0,8},{4,12},{8,0},{12,4},{16,20},{20,16},{24,28},{28,24},{1,9},{5... | collective-permute-start | bytes 417800 | tf_op jit(solution)/shard_map/ppermute | solution.py:35
  12.2 0.0 collective-permute-done.3.refs_2_
  12.3 0.1 relay.1
  12.3 1.9 %collective-permute-start.4 = (bf16[272,256]{1,0:T(8,128)(2,1)S(1)}, bf16[272,256]{1,0:T(8,128)(2,1)S(1)}, u32[]{:S(2)}, u32[]{:S(2)}) collective-permute-start(bf16[272,256]{1,0:T(8,128)(2,1)S(1)} %get-tuple-element.26), channel_id=1, source_target_pairs={{0,4},{4,0},{8,12},{12,8},{16,24},{20,28},{24,16},{28,20},{1,5},{5... | collective-permute-start | bytes 417800 | tf_op jit(solution)/shard_map/ppermute | solution.py:35
  14.3 0.0 collective-permute-done.7.refs_1_
  14.3 0.5 %collective-permute-start.5 = (bf16[272,256]{1,0:T(8,128)(2,1)S(1)}, bf16[272,256]{1,0:T(8,128)(2,1)S(1)}, u32[]{:S(2)}, u32[]{:S(2)}) collective-permute-start(bf16[272,256]{1,0:T(8,128)(2,1)S(1)} %get-tuple-element.27), channel_id=1, source_target_pairs={{0,8},{4,12},{8,0},{12,4},{16,20},{20,16},{24,28},{28,24},{1,9},{5... | collective-permute-start | bytes 417800 | tf_op jit(solution)/shard_map/ppermute | solution.py:35
  14.8 1.8 %collective-permute-done.8.refs_2_ = bf16[256,256]{1,0:T(8,128)(2,1)S(1)} collective-permute-done((bf16[256,256]{1,0:T(8,128)(2,1)S(1)}, bf16[256,256]{1,0:T(8,128)(2,1)S(1)}, u32[]{:S(2)}, u32[]{:S(2)}) %collective-permute-start.8) | collective-permute-done | bytes 131104 | tf_op jit(solution)/shard_map/ppermute | solution.py:35
  16.6 0.7 %collective-permute-start.9 = (bf16[128,256]{1,0:T(8,128)(2,1)S(1)}, bf16[128,256]{1,0:T(8,128)(2,1)S(1)}, u32[]{:S(2)}, u32[]{:S(2)}) collective-permute-start(bf16[128,256]{1,0:T(8,128)(2,1)S(1)} %get-tuple-element.31), channel_id=1, source_target_pairs={{0,4},{4,0},{8,12},{12,8},{16,24},{20,28},{24,16},{28,20},{1,5},{5... | collective-permute-start | bytes 196616 | tf_op jit(solution)/shard_map/ppermute | solution.py:35
  17.3 0.0 collective-permute-done.refs_1_
  17.3 0.4 collective-permute-start.10
  17.7 1.3 %collective-permute-done.1.refs_2_ = bf16[272,256]{1,0:T(8,128)(2,1)S(1)} collective-permute-done((bf16[272,256]{1,0:T(8,128)(2,1)S(1)}, bf16[272,256]{1,0:T(8,128)(2,1)S(1)}, u32[]{:S(2)}, u32[]{:S(2)}) %collective-permute-start.1) | collective-permute-done | bytes 139296 | tf_op jit(solution)/shard_map/ppermute | solution.py:35
  19.0 1.1 %collective-permute-done.4.refs_3_ = bf16[272,256]{1,0:T(8,128)(2,1)S(1)} collective-permute-done((bf16[272,256]{1,0:T(8,128)(2,1)S(1)}, bf16[272,256]{1,0:T(8,128)(2,1)S(1)}, u32[]{:S(2)}, u32[]{:S(2)}) %collective-permute-start.4) | collective-permute-done | bytes 139296 | tf_op jit(solution)/shard_map/ppermute | solution.py:35
  20.2 0.4 collective-permute-done.5.refs_4_
  20.6 1.1 %collective-permute-done.9.refs_6_.refs_3_ = bf16[128,256]{1,0:T(8,128)(2,1)S(1)} collective-permute-done((bf16[128,256]{1,0:T(8,128)(2,1)S(1)}, bf16[128,256]{1,0:T(8,128)(2,1)S(1)}, u32[]{:S(2)}, u32[]{:S(2)}) %collective-permute-start.9) | collective-permute-done | bytes 65568 | tf_op jit(solution)/shard_map/ppermute | solution.py:35
  21.7 0.0 collective-permute-done.10.refs_7_.refs_4_
  21.7 0.0 copy-done.1
  21.7 0.4 factor.1
  22.1 1.2 %collective-permute-start.14 = (bf16[288,256]{1,0:T(8,128)(2,1)S(1)}, bf16[288,256]{1,0:T(8,128)(2,1)S(1)}, u32[]{:S(2)}, u32[]{:S(2)}) collective-permute-start(bf16[288,256]{1,0:T(8,128)(2,1)S(1)} %get-tuple-element.35.refs_3_), channel_id=1, source_target_pairs={{0,8},{4,12},{8,0},{12,4},{16,20},{20,16},{24,28},{28,24},{1,9},{5... | collective-permute-start | bytes 442376 | tf_op jit(solution)/shard_map/ppermute | solution.py:35
  23.3 1.4 %collective-permute-start.11 = (bf16[272,256]{1,0:T(8,128)(2,1)S(1)}, bf16[272,256]{1,0:T(8,128)(2,1)S(1)}, u32[]{:S(2)}, u32[]{:S(2)}) collective-permute-start(bf16[272,256]{1,0:T(8,128)(2,1)S(1)} %get-tuple-element.34.refs_2_.refs_5_), channel_id=1, source_target_pairs={{0,4},{4,0},{8,12},{12,8},{16,24},{20,28},{24,16},{28,20},{1,5},{5... | collective-permute-start | bytes 417800 | tf_op jit(solution)/shard_map/ppermute | solution.py:35
  24.7 0.6 %collective-permute-start.12 = (bf16[288,256]{1,0:T(8,128)(2,1)S(1)}, bf16[288,256]{1,0:T(8,128)(2,1)S(1)}, u32[]{:S(2)}, u32[]{:S(2)}) collective-permute-start(bf16[288,256]{1,0:T(8,128)(2,1)S(1)} %get-tuple-element.35.refs_3_), channel_id=1, source_target_pairs={{0,4},{4,0},{8,12},{12,8},{16,24},{20,28},{24,16},{28,20},{1,5},{5... | collective-permute-start | bytes 442376 | tf_op jit(solution)/shard_map/ppermute | solution.py:35
  25.3 3.6 %collective-permute-done.14.refs_7_ = bf16[288,256]{1,0:T(8,128)(2,1)S(1)} collective-permute-done((bf16[288,256]{1,0:T(8,128)(2,1)S(1)}, bf16[288,256]{1,0:T(8,128)(2,1)S(1)}, u32[]{:S(2)}, u32[]{:S(2)}) %collective-permute-start.14) | collective-permute-done | bytes 147488 | tf_op jit(solution)/shard_map/ppermute | solution.py:35
  28.9 1.2 %collective-permute-start.16 = (bf16[288,256]{1,0:T(8,128)(2,1)S(1)}, bf16[288,256]{1,0:T(8,128)(2,1)S(1)}, u32[]{:S(2)}, u32[]{:S(2)}) collective-permute-start(bf16[288,256]{1,0:T(8,128)(2,1)S(1)} %collective-permute-done.14.refs_7_), channel_id=1, source_target_pairs={{0,4},{4,0},{8,12},{12,8},{16,24},{20,28},{24,16},{28,20},{1,5},{5... | collective-permute-start | bytes 442376 | tf_op jit(solution)/shard_map/ppermute | solution.py:35
  30.1 1.3 %collective-permute-start.13 = (bf16[272,256]{1,0:T(8,128)(2,1)S(1)}, bf16[272,256]{1,0:T(8,128)(2,1)S(1)}, u32[]{:S(2)}, u32[]{:S(2)}) collective-permute-start(bf16[272,256]{1,0:T(8,128)(2,1)S(1)} %get-tuple-element.34.refs_2_.refs_5_), channel_id=1, source_target_pairs={{0,8},{4,12},{8,0},{12,4},{16,20},{20,16},{24,28},{28,24},{1,9},{5... | collective-permute-start | bytes 417800 | tf_op jit(solution)/shard_map/ppermute | solution.py:35
  31.4 0.0 collective-permute-done.11.refs_4_
  31.4 0.8 %collective-permute-start.15 = (bf16[272,256]{1,0:T(8,128)(2,1)S(1)}, bf16[272,256]{1,0:T(8,128)(2,1)S(1)}, u32[]{:S(2)}, u32[]{:S(2)}) collective-permute-start(bf16[272,256]{1,0:T(8,128)(2,1)S(1)} %collective-permute-done.11.refs_4_), channel_id=1, source_target_pairs={{0,8},{4,12},{8,0},{12,4},{16,20},{20,16},{24,28},{28,24},{1,9},{5... | collective-permute-start | bytes 417800 | tf_op jit(solution)/shard_map/ppermute | solution.py:35
  32.1 0.1 grad_total.1.refs_0_
  32.2 1.3 %collective-permute-start.17 = (bf16[256,256]{1,0:T(8,128)(2,1)S(1)}, bf16[256,256]{1,0:T(8,128)(2,1)S(1)}, u32[]{:S(2)}, u32[]{:S(2)}) collective-permute-start(bf16[256,256]{1,0:T(8,128)(2,1)S(1)} %grad_total.1.refs_0_), channel_id=1, source_target_pairs={{0,8},{4,12},{8,0},{12,4},{16,20},{20,16},{24,28},{28,24},{1,9},{5... | collective-permute-start | bytes 393224 | tf_op jit(solution)/shard_map/ppermute | solution.py:35
  33.5 4.5 %collective-permute-done.17.refs_1_ = bf16[256,256]{1,0:T(8,128)(2,1)S(1)} collective-permute-done((bf16[256,256]{1,0:T(8,128)(2,1)S(1)}, bf16[256,256]{1,0:T(8,128)(2,1)S(1)}, u32[]{:S(2)}, u32[]{:S(2)}) %collective-permute-start.17) | collective-permute-done | bytes 131104 | tf_op jit(solution)/shard_map/ppermute | solution.py:35
  38.1 0.0 collective-permute-done.13.refs_6_.refs_5_
  38.1 0.0 collective-permute-done.12.refs_5_.refs_4_
  38.1 0.0 collective-permute-done.15.refs_8_.refs_2_
  38.1 0.0 collective-permute-done.16.refs_9_.refs_3_
  38.1 0.0 copy-start.2
  38.1 0.9 %collective-permute-start.18 = (bf16[512,256]{1,0:T(8,128)(2,1)S(1)}, bf16[512,256]{1,0:T(8,128)(2,1)S(1)}, u32[]{:S(2)}, u32[]{:S(2)}) collective-permute-start(bf16[512,256]{1,0:T(8,128)(2,1)S(1)} %pair.1.refs_0_), channel_id=1, source_target_pairs={{0,4},{4,0},{8,12},{12,8},{16,24},{20,28},{24,16},{28,20},{1,5},{5... | collective-permute-start | bytes 786440 | tf_op jit(solution)/shard_map/ppermute | solution.py:35
  39.7 3.8 %root.1 = (f32[256,1024]{1,0:T(8,128)}, bf16[256,1024]{1,0:T(8,128)(2,1)}, f32[8,128]{1,0:T(8,128)S(1)}) custom-call(s32[1,1]{1,0:T(1,128)S(6)} %copy.8.refs_0_, f32[640,256]{1,0:T(8,128)S(1)} %get-tuple-element.33.refs_1_, bf16[272,256]{1,0:T(8,128)(2,1)S(1)} %get-tuple-element.34.refs_2_.refs_5_, bf16[288,256]{1,0:T(8,128)(2,1)S(1)} %get-tuple-element.35.refs_3_, ...), custom_call_target="tpu_custom_call" | custom-call | tf_op jit(solution)/shard_map/root/pallas_call | solution.py:351
  43.5 1.0 %collective-permute-done.18.refs_1_ = bf16[512,256]{1,0:T(8,128)(2,1)S(1)} collective-permute-done((bf16[512,256]{1,0:T(8,128)(2,1)S(1)}, bf16[512,256]{1,0:T(8,128)(2,1)S(1)}, u32[]{:S(2)}, u32[]{:S(2)}) %collective-permute-start.18) | collective-permute-done | bytes 262176 | tf_op jit(solution)/shard_map/ppermute | solution.py:35
  44.6 0.0 copy-done.2
  44.6 1.0 %step.1 = bf16[256,256]{1,0:T(8,128)(2,1)} custom-call(bf16[512,256]{1,0:T(8,128)(2,1)S(1)} %pair.1.refs_0_, bf16[512,256]{1,0:T(8,128)(2,1)S(1)} %collective-permute-done.18.refs_1_, bf16[256,1024]{1,0:T(8,128)(2,1)S(1)} %bitcast.10, f32[8,128]{1,0:T(8,128)S(1)} %get-tuple-element.38.refs_3_), custom_call_target="tpu_custom_call" | custom-call | tf_op jit(solution)/shard_map/step/pallas_call | solution.py:351
  (2 shorter events, 0.1 us)
Async XLA Ops:
  0.6 6.9 %collective-permute-start.6 = (bf16[1,512,256]{2,1,0:T(8,128)(2,1)}, bf16[1,512,256]{2,1,0:T(8,128)(2,1)S(1)}, u32[]{:S(2)}, u32[]{:S(2)}) collective-permute-start(bf16[1,512,256]{2,1,0:T(8,128)(2,1)} %param.6), channel_id=1, source_target_pairs={{16,0},{0,16},{17,1},{1,17},{18,2},{2,18},{19,3},{3,19},{20,4},{4,... | collective-permute-start | bytes 786440 | tf_op jit(solution)/shard_map/ppermute | solution.py:22
  1.1 1.2 %copy-start = (bf16[1,512,1024]{2,1,0:T(8,128)(2,1)S(1)}, bf16[1,512,1024]{2,1,0:T(8,128)(2,1)}, u32[]{:S(2)}) copy-start(bf16[1,512,1024]{2,1,0:T(8,128)(2,1)} %param.5) | copy-start | bytes 3145732
  3.5 7.2 %collective-permute-start.2 = (bf16[272,256]{1,0:T(8,128)(2,1)S(1)}, bf16[272,256]{1,0:T(8,128)(2,1)S(1)}, u32[]{:S(2)}, u32[]{:S(2)}) collective-permute-start(bf16[272,256]{1,0:T(8,128)(2,1)S(1)} %get-tuple-element.24), channel_id=1, source_target_pairs={{0,4},{4,0},{8,12},{12,8},{16,24},{20,28},{24,16},{28,20},{1,5},{5... | collective-permute-start | bytes 417800 | tf_op jit(solution)/shard_map/ppermute | solution.py:35
  6.0 6.2 %collective-permute-start.3 = (bf16[272,256]{1,0:T(8,128)(2,1)S(1)}, bf16[272,256]{1,0:T(8,128)(2,1)S(1)}, u32[]{:S(2)}, u32[]{:S(2)}) collective-permute-start(bf16[272,256]{1,0:T(8,128)(2,1)S(1)} %get-tuple-element.25), channel_id=1, source_target_pairs={{0,8},{4,12},{8,0},{12,4},{16,20},{20,16},{24,28},{28,24},{1,9},{5... | collective-permute-start | bytes 417800 | tf_op jit(solution)/shard_map/ppermute | solution.py:35
  8.1 13.6 %copy-start.1 = (f32[1,1,256,1024]{3,2,1,0:T(8,128)S(1)}, f32[1,1,256,1024]{3,2,1,0:T(8,128)}, u32[]{:S(2)}) copy-start(f32[1,1,256,1024]{3,2,1,0:T(8,128)} %param.7) | copy-start | bytes 3145732
  8.1 6.2 %collective-permute-start.7 = (bf16[256,256]{1,0:T(8,128)(2,1)S(1)}, bf16[256,256]{1,0:T(8,128)(2,1)S(1)}, u32[]{:S(2)}, u32[]{:S(2)}) collective-permute-start(bf16[256,256]{1,0:T(8,128)(2,1)S(1)} %get-tuple-element.29), channel_id=1, source_target_pairs={{0,4},{4,0},{8,12},{12,8},{16,24},{20,28},{24,16},{28,20},{1,5},{5... | collective-permute-start | bytes 393224 | tf_op jit(solution)/shard_map/ppermute | solution.py:35
  8.7 8.6 %collective-permute-start = (bf16[272,256]{1,0:T(8,128)(2,1)S(1)}, bf16[272,256]{1,0:T(8,128)(2,1)S(1)}, u32[]{:S(2)}, u32[]{:S(2)}) collective-permute-start(bf16[272,256]{1,0:T(8,128)(2,1)S(1)} %get-tuple-element.22), channel_id=1, source_target_pairs={{0,4},{4,0},{8,12},{12,8},{16,24},{20,28},{24,16},{28,20},{1,5},{5... | collective-permute-start | bytes 417800 | tf_op jit(solution)/shard_map/ppermute | solution.py:35
  10.2 6.4 %collective-permute-start.8 = (bf16[256,256]{1,0:T(8,128)(2,1)S(1)}, bf16[256,256]{1,0:T(8,128)(2,1)S(1)}, u32[]{:S(2)}, u32[]{:S(2)}) collective-permute-start(bf16[256,256]{1,0:T(8,128)(2,1)S(1)} %get-tuple-element.30), channel_id=1, source_target_pairs={{0,8},{4,12},{8,0},{12,4},{16,20},{20,16},{24,28},{28,24},{1,9},{5... | collective-permute-start | bytes 393224 | tf_op jit(solution)/shard_map/ppermute | solution.py:35
  10.7 8.3 %collective-permute-start.1 = (bf16[272,256]{1,0:T(8,128)(2,1)S(1)}, bf16[272,256]{1,0:T(8,128)(2,1)S(1)}, u32[]{:S(2)}, u32[]{:S(2)}) collective-permute-start(bf16[272,256]{1,0:T(8,128)(2,1)S(1)} %get-tuple-element.23), channel_id=1, source_target_pairs={{0,8},{4,12},{8,0},{12,4},{16,20},{20,16},{24,28},{28,24},{1,9},{5... | collective-permute-start | bytes 417800 | tf_op jit(solution)/shard_map/ppermute | solution.py:35
  12.3 7.8 %collective-permute-start.4 = (bf16[272,256]{1,0:T(8,128)(2,1)S(1)}, bf16[272,256]{1,0:T(8,128)(2,1)S(1)}, u32[]{:S(2)}, u32[]{:S(2)}) collective-permute-start(bf16[272,256]{1,0:T(8,128)(2,1)S(1)} %get-tuple-element.26), channel_id=1, source_target_pairs={{0,4},{4,0},{8,12},{12,8},{16,24},{20,28},{24,16},{28,20},{1,5},{5... | collective-permute-start | bytes 417800 | tf_op jit(solution)/shard_map/ppermute | solution.py:35
  14.3 6.3 %collective-permute-start.5 = (bf16[272,256]{1,0:T(8,128)(2,1)S(1)}, bf16[272,256]{1,0:T(8,128)(2,1)S(1)}, u32[]{:S(2)}, u32[]{:S(2)}) collective-permute-start(bf16[272,256]{1,0:T(8,128)(2,1)S(1)} %get-tuple-element.27), channel_id=1, source_target_pairs={{0,8},{4,12},{8,0},{12,4},{16,20},{20,16},{24,28},{28,24},{1,9},{5... | collective-permute-start | bytes 417800 | tf_op jit(solution)/shard_map/ppermute | solution.py:35
  16.6 5.1 %collective-permute-start.9 = (bf16[128,256]{1,0:T(8,128)(2,1)S(1)}, bf16[128,256]{1,0:T(8,128)(2,1)S(1)}, u32[]{:S(2)}, u32[]{:S(2)}) collective-permute-start(bf16[128,256]{1,0:T(8,128)(2,1)S(1)} %get-tuple-element.31), channel_id=1, source_target_pairs={{0,4},{4,0},{8,12},{12,8},{16,24},{20,28},{24,16},{28,20},{1,5},{5... | collective-permute-start | bytes 196616 | tf_op jit(solution)/shard_map/ppermute | solution.py:35
  17.3 4.4 %collective-permute-start.10 = (bf16[128,256]{1,0:T(8,128)(2,1)S(1)}, bf16[128,256]{1,0:T(8,128)(2,1)S(1)}, u32[]{:S(2)}, u32[]{:S(2)}) collective-permute-start(bf16[128,256]{1,0:T(8,128)(2,1)S(1)} %get-tuple-element.32), channel_id=1, source_target_pairs={{0,8},{4,12},{8,0},{12,4},{16,20},{20,16},{24,28},{28,24},{1,9},{5... | collective-permute-start | bytes 196616 | tf_op jit(solution)/shard_map/ppermute | solution.py:35
  22.1 6.8 %collective-permute-start.14 = (bf16[288,256]{1,0:T(8,128)(2,1)S(1)}, bf16[288,256]{1,0:T(8,128)(2,1)S(1)}, u32[]{:S(2)}, u32[]{:S(2)}) collective-permute-start(bf16[288,256]{1,0:T(8,128)(2,1)S(1)} %get-tuple-element.35.refs_3_), channel_id=1, source_target_pairs={{0,8},{4,12},{8,0},{12,4},{16,20},{20,16},{24,28},{28,24},{1,9},{5... | collective-permute-start | bytes 442376 | tf_op jit(solution)/shard_map/ppermute | solution.py:35
  23.3 8.1 %collective-permute-start.11 = (bf16[272,256]{1,0:T(8,128)(2,1)S(1)}, bf16[272,256]{1,0:T(8,128)(2,1)S(1)}, u32[]{:S(2)}, u32[]{:S(2)}) collective-permute-start(bf16[272,256]{1,0:T(8,128)(2,1)S(1)} %get-tuple-element.34.refs_2_.refs_5_), channel_id=1, source_target_pairs={{0,4},{4,0},{8,12},{12,8},{16,24},{20,28},{24,16},{28,20},{1,5},{5... | collective-permute-start | bytes 417800 | tf_op jit(solution)/shard_map/ppermute | solution.py:35
  24.7 13.4 %collective-permute-start.12 = (bf16[288,256]{1,0:T(8,128)(2,1)S(1)}, bf16[288,256]{1,0:T(8,128)(2,1)S(1)}, u32[]{:S(2)}, u32[]{:S(2)}) collective-permute-start(bf16[288,256]{1,0:T(8,128)(2,1)S(1)} %get-tuple-element.35.refs_3_), channel_id=1, source_target_pairs={{0,4},{4,0},{8,12},{12,8},{16,24},{20,28},{24,16},{28,20},{1,5},{5... | collective-permute-start | bytes 442376 | tf_op jit(solution)/shard_map/ppermute | solution.py:35
  28.9 9.1 %collective-permute-start.16 = (bf16[288,256]{1,0:T(8,128)(2,1)S(1)}, bf16[288,256]{1,0:T(8,128)(2,1)S(1)}, u32[]{:S(2)}, u32[]{:S(2)}) collective-permute-start(bf16[288,256]{1,0:T(8,128)(2,1)S(1)} %collective-permute-done.14.refs_7_), channel_id=1, source_target_pairs={{0,4},{4,0},{8,12},{12,8},{16,24},{20,28},{24,16},{28,20},{1,5},{5... | collective-permute-start | bytes 442376 | tf_op jit(solution)/shard_map/ppermute | solution.py:35
  30.1 8.0 %collective-permute-start.13 = (bf16[272,256]{1,0:T(8,128)(2,1)S(1)}, bf16[272,256]{1,0:T(8,128)(2,1)S(1)}, u32[]{:S(2)}, u32[]{:S(2)}) collective-permute-start(bf16[272,256]{1,0:T(8,128)(2,1)S(1)} %get-tuple-element.34.refs_2_.refs_5_), channel_id=1, source_target_pairs={{0,8},{4,12},{8,0},{12,4},{16,20},{20,16},{24,28},{28,24},{1,9},{5... | collective-permute-start | bytes 417800 | tf_op jit(solution)/shard_map/ppermute | solution.py:35
  31.4 6.7 %collective-permute-start.15 = (bf16[272,256]{1,0:T(8,128)(2,1)S(1)}, bf16[272,256]{1,0:T(8,128)(2,1)S(1)}, u32[]{:S(2)}, u32[]{:S(2)}) collective-permute-start(bf16[272,256]{1,0:T(8,128)(2,1)S(1)} %collective-permute-done.11.refs_4_), channel_id=1, source_target_pairs={{0,8},{4,12},{8,0},{12,4},{16,20},{20,16},{24,28},{28,24},{1,9},{5... | collective-permute-start | bytes 417800 | tf_op jit(solution)/shard_map/ppermute | solution.py:35
  32.2 5.9 %collective-permute-start.17 = (bf16[256,256]{1,0:T(8,128)(2,1)S(1)}, bf16[256,256]{1,0:T(8,128)(2,1)S(1)}, u32[]{:S(2)}, u32[]{:S(2)}) collective-permute-start(bf16[256,256]{1,0:T(8,128)(2,1)S(1)} %grad_total.1.refs_0_), channel_id=1, source_target_pairs={{0,8},{4,12},{8,0},{12,4},{16,20},{20,16},{24,28},{28,24},{1,9},{5... | collective-permute-start | bytes 393224 | tf_op jit(solution)/shard_map/ppermute | solution.py:35
  38.1 6.5 %copy-start.2 = (bf16[1,1,256,1024]{3,2,1,0:T(8,128)(2,1)S(1)}, bf16[1,1,256,1024]{3,2,1,0:T(8,128)(2,1)}, u32[]{:S(2)}) copy-start(bf16[1,1,256,1024]{3,2,1,0:T(8,128)(2,1)} %param.8) | copy-start | bytes 1572868
  38.1 6.4 %collective-permute-start.18 = (bf16[512,256]{1,0:T(8,128)(2,1)S(1)}, bf16[512,256]{1,0:T(8,128)(2,1)S(1)}, u32[]{:S(2)}, u32[]{:S(2)}) collective-permute-start(bf16[512,256]{1,0:T(8,128)(2,1)S(1)} %pair.1.refs_0_), channel_id=1, source_target_pairs={{0,4},{4,0},{8,12},{12,8},{16,24},{20,28},{24,16},{28,20},{1,5},{5... | collective-permute-start | bytes 786440 | tf_op jit(solution)/shard_map/ppermute | solution.py:35

commit v16 on v11

--- a/solution.py
+++ b/solution.py
@@ -22,21 +22,8 @@
     return lax.ppermute(block, axis, route)
 
 
-def along(turn):
-    return jnp.where(lax.axis_index("pipe") == turn, 1, 2)
-
-
-def swapped(block, turn):
-    replicas = lax.axis_size("dp")
-    route = []
-    for section in range(lax.axis_size("pipe")):
-        offset = 1 if section == turn else 2
-        route += [(section * replicas + i, section * replicas + (i ^ offset)) for i in range(replicas)]
-    return lax.ppermute(block, ("pipe", "dp"), route)
-
-
-def swapped_across(block):
-    return lax.ppermute(block, "dp", [(i, i ^ 3) for i in range(lax.axis_size("dp"))])
+def swapped(block, offset):
+    return lax.ppermute(block, "dp", [(i, i ^ offset) for i in range(lax.axis_size("dp"))])
 
 
 def eye_of(rows, cols, shift=0):
@@ -53,8 +40,7 @@
     return block.astype(F32).T.astype(block.dtype)
 
 
-def offsets():
-    return 0, along(0), along(1), 3
+OFFSETS = (0, 1, 2, 3)
 
 
 def chunk_rows(share):
@@ -132,13 +118,13 @@
         owner = mine ^ offset
         base = pl.multiple_of(owner * share, share)
         yield 0, packed_upper(batch[pl.ds(base, share), pl.ds(base, share)])
-        for start, step in zip(starts[1:], offsets()[1:]):
+        for start, step in zip(starts[1:], OFFSETS[1:]):
             row, col = shared_half(owner, step, share)
             yield start, batch[pl.ds(row, half), pl.ds(col, share)]
 
     store_chunk(pieces(3), length, (relay_x, 0), (relay_y, 0))
-    store_chunk(pieces(along(0)), length, (direct_x, 0), (keep, 3 * length))
-    store_chunk(pieces(along(1)), length, (keep, 2 * length), (direct_y, 0))
+    store_chunk(pieces(1), length, (direct_x, 0), (keep, 3 * length))
+    store_chunk(pieces(2), length, (keep, 2 * length), (direct_y, 0))
     store_chunk(pieces(0), length, (keep, 0), (keep, length))
 
 
@@ -158,8 +144,8 @@
             yield part * strip, total[rows, part * share : (part + 1) * share]
 
     store_chunk(pieces(3), length, (send_x, 0), (send_y, 0))
-    store_chunk(pieces(along(0)), length, (send_x, length), (keep, 3 * length))
-    store_chunk(pieces(along(1)), length, (keep, 2 * length), (send_y, length))
+    store_chunk(pieces(1), length, (send_x, length), (keep, 3 * length))
+    store_chunk(pieces(2), length, (keep, 2 * length), (send_y, length))
     store_chunk(pieces(0), length, (keep, 0), (keep, length))
 
 
@@ -204,7 +190,7 @@
     exact[0:share, :] = value
     squares = jnp.sum(value * value, axis=0, keepdims=True)
     values = [packed_upper(value).astype(BF16)]
-    for position, step in enumerate(offsets()[1:]):
+    for position, step in enumerate(OFFSETS[1:]):
         other = mine ^ step
         block = old[:, pl.ds(pl.multiple_of(other * share, share), share)]
         term = DECAY * jnp.where(mine < other, block[0:half], block[:, half:].T)
@@ -242,7 +228,7 @@
         return jnp.concatenate([upper[start:length, :], lower[0 : start + count - length, :]], axis=0)
 
     copies = []
-    for position, step in enumerate(offsets()):
+    for position, step in enumerate(OFFSETS):
         other = mine ^ step
         target = rows.at[position]
         if position == 0:
@@ -267,13 +253,13 @@
 
     squares = jnp.zeros((16, share), F32)
     block_eye = eye_of(share, share)
-    for position, offset in enumerate(offsets()):
+    for position, offset in enumerate(OFFSETS):
         owner = mine ^ offset
         own_band = pl.ds(pl.multiple_of(owner * share, share), share)
         block = unpacked(rows_of(position, 0, starts[1]).astype(F32))
         factor[own_band, own_band] = block.astype(BF16)
         diagonal[:, own_band] = jnp.sum(block * block_eye, axis=0, keepdims=True)
-        for start, step in zip(starts[1:], offsets()[1:]):
+        for start, step in zip(starts[1:], OFFSETS[1:]):
             row, col = shared_half(owner, step, share)
             block = rows_of(position, start, half)
             factor[pl.ds(row, half), pl.ds(col, share)] = block
@@ -315,7 +301,7 @@
     result[...] = lax.dot_general(
         grads[...], old_root[...], (((1,), (1,)), ((), ())), preferred_element_type=F32
     ).astype(BF16)
-    for position, offset in enumerate(offsets()):
+    for position, offset in enumerate(OFFSETS):
         rows = pl.ds(pl.multiple_of((mine ^ offset) * strip, strip), strip)
         step_out[rows, :] = result[position * strip : (position + 1) * strip, :]
 
@@ -362,8 +348,8 @@
         inputs,
         scratch=[pltpu.VMEM((order, order), F32)],
     )
-    relay_x, relay_y = swapped(relay_x, 0), swapped(relay_y, 1)
-    direct_x, direct_y = swapped(direct_x, 0), swapped(direct_y, 1)
+    relay_x, relay_y = swapped(relay_x, 1), swapped(relay_y, 2)
+    direct_x, direct_y = swapped(direct_x, 1), swapped(direct_y, 2)
     relay_x, relay_y = call(relay_kernel, [shape(length)] * 2, "relay", keep, relay_x, relay_y)
     grad_x, grad_y, grad_keep = call(
         functools.partial(grad_kernel, replicas, tokens * replicas),
@@ -374,8 +360,8 @@
         after=[relay_x, relay_y],
         scratch=[pltpu.VMEM((grows, order), F32)],
     )
-    relay_x, relay_y = swapped(relay_x, 0), swapped(relay_y, 1)
-    grad_x, grad_y = swapped(grad_x, 0), swapped(grad_y, 1)
+    relay_x, relay_y = swapped(relay_x, 1), swapped(relay_y, 2)
+    grad_x, grad_y = swapped(grad_x, 1), swapped(grad_y, 2)
     upper, lower, exact = call(
         functools.partial(factor_kernel, replicas),
         [shape(length), shape(length + 16), shape(5 * share // 2, F32)],
@@ -387,13 +373,13 @@
         relay_y,
         old_factor[0, 0],
     )
-    upper_x, lower_y = swapped(upper, 0), swapped(lower, 1)
-    lower_x, upper_y = swapped(lower, 0), swapped(upper, 1)
+    upper_x, lower_y = swapped(upper, 1), swapped(lower, 2)
+    lower_x, upper_y = swapped(lower, 1), swapped(upper, 2)
     strip_x, strip_y = call(
         grad_relay_kernel, [shape(grows // 2)] * 2, "grad_relay", grad_keep, grad_x, grad_y, after=[upper, lower]
     )
-    strip_x, strip_y = swapped(strip_x, 0), swapped(strip_y, 1)
-    upper_far, lower_far = swapped(upper_x, 1), swapped(lower_y, 0)
+    strip_x, strip_y = swapped(strip_x, 1), swapped(strip_y, 2)
+    upper_far, lower_far = swapped(upper_x, 2), swapped(lower_y, 1)
     (strip,) = call(
         grad_total_kernel,
         [shape(grows)],
@@ -403,9 +389,9 @@
         grad_y,
         strip_x,
         strip_y,
-        after=[lower_x, upper_y],
-    )
-    strips = [strip, swapped(strip, 0), swapped(strip, 1), swapped_across(strip)]
+        after=[upper_x, lower_y],
+    )
+    strips = [strip, swapped(strip, 1), swapped(strip, 2), swapped(strip, 3)]
     factor, root, finished = call(
         root_kernel,
         [shape(share, F32, order), shape(share, BF16, order), shape(8, F32, 128)],
@@ -477,7 +463,7 @@
 
 def solution(mesh):
     return jax.shard_map(
-        square_plan if mesh.shape["dp"] == 4 and mesh.shape["pipe"] == 2 else ring_plan,
+        square_plan if mesh.shape["dp"] == 4 else ring_plan,
         mesh=mesh,
         in_specs=(
             P("pipe", "dp", "tensor"),

time: 44.2 us -> 41.2 us (0.932)
  waiting for transfers between devices: 13.9 us -> 9.66 us
  starting transfers between devices: 20.6 us -> 21.7 us
    ppermute x19, waiting for transfers between devices: 13.9 us -> 9.66 us  [swapped(): lax.ppermute(block, 'dp', [(i, i ^ offset) for i in range(lax.axis_size('...]
    ppermute x19, starting transfers between devices: 20 us -> 21.2 us  [swapped(): lax.ppermute(block, 'dp', [(i, i ^ offset) for i in range(lax.axis_size('...]
  transfers between devices with their start and end apart: 20 -> 20, of which waited for: 8 -> 7; matrix products, arithmetic and copies ran while one was open for 0% -> 0% of each run, Pallas kernels for 14% -> 15%
where the time goes in v16:
time: 41.2 us; the launch traced here: 41 us
  starting transfers between devices  21.7 us (53%)
  waiting for transfers between devices  9.66 us (23%)
  Pallas kernels  7 us (17%)
  between operations  1.38 us (3%)
  local copies, waits for them, and re-layouts  1.24 us (3%)
    ppermute x19, starting transfers between devices, swapped(): lax.ppermute(block, 'dp', [(i, i ^ offset) for i in range(lax.axis_size('...  21.2 us
    ppermute x19, waiting for transfers between devices, swapped(): lax.ppermute(block, 'dp', [(i, i ^ offset) for i in range(lax.axis_size('...  9.66 us
    pallas_call x8, Pallas kernels, call(): pl.pallas_call(body, out_shape=outs, in_specs=in_specs, out_specs=out_spe...  7 us
    unnamed x6, local copies, waits for them, and re-layouts  1.24 us
  transfers between devices with their start and end apart: 20, of which 7 were waited for; matrix products, arithmetic and copies ran while one was open for 0% of the time, Pallas kernels for 15%

profile of v16, /device:TPU:0, one launch (start us, length us, event | category | flops | bytes accessed | tf_op | source)
XLA Modules:
  0.0 41.0 jit_solution(8007452557831488340)
XLA Ops:
  0.6 0.5 %collective-permute-start.12 = (bf16[1,512,256]{2,1,0:T(8,128)(2,1)}, bf16[1,512,256]{2,1,0:T(8,128)(2,1)S(1)}, u32[]{:S(2)}, u32[]{:S(2)}) collective-permute-start(bf16[1,512,256]{2,1,0:T(8,128)(2,1)} %param.6), channel_id=1, source_target_pairs={{16,0},{0,16},{17,1},{1,17},{18,2},{2,18},{19,3},{3,19},{20,4},{4,... | collective-permute-start | bytes 786440 | tf_op jit(solution)/shard_map/ppermute | solution.py:22
  1.1 0.0 copy-start
  1.1 1.2 %copy-done = bf16[1,512,1024]{2,1,0:T(8,128)(2,1)S(1)} copy-done((bf16[1,512,1024]{2,1,0:T(8,128)(2,1)S(1)}, bf16[1,512,1024]{2,1,0:T(8,128)(2,1)}, u32[]{:S(2)}) %copy-start) | copy-done | bytes 1048600
  2.4 1.1 %batch.1 = (bf16[272,256]{1,0:T(8,128)(2,1)S(1)}, bf16[272,256]{1,0:T(8,128)(2,1)S(1)}, bf16[272,256]{1,0:T(8,128)(2,1)S(1)}, bf16[272,256]{1,0:T(8,128)(2,1)S(1)}, f32[1088,256]{1,0:T(8,128)S(1)}) custom-call(bf16[512,1024]{1,0:T(8,128)(2,1)S(1)} %bitcast.7), custom_call_target="tpu_custom_call" | custom-call | tf_op jit(solution)/shard_map/batch/pallas_call | solution.py:333
  3.5 2.6 %collective-permute-start.2 = (bf16[272,256]{1,0:T(8,128)(2,1)S(1)}, bf16[272,256]{1,0:T(8,128)(2,1)S(1)}, u32[]{:S(2)}, u32[]{:S(2)}) collective-permute-start(bf16[272,256]{1,0:T(8,128)(2,1)S(1)} %get-tuple-element.24), channel_id=1, source_target_pairs={{0,4},{4,0},{8,12},{12,8},{1,5},{5,1},{9,13},{13,9},{2,6},{6,2},{1... | collective-permute-start | bytes 417800 | tf_op jit(solution)/shard_map/ppermute | solution.py:26
  6.0 1.5 %collective-permute-start.3 = (bf16[272,256]{1,0:T(8,128)(2,1)S(1)}, bf16[272,256]{1,0:T(8,128)(2,1)S(1)}, u32[]{:S(2)}, u32[]{:S(2)}) collective-permute-start(bf16[272,256]{1,0:T(8,128)(2,1)S(1)} %get-tuple-element.25), channel_id=1, source_target_pairs={{0,8},{4,12},{8,0},{12,4},{1,9},{5,13},{9,1},{13,5},{2,10},{6,14},... | collective-permute-start | bytes 417800 | tf_op jit(solution)/shard_map/ppermute | solution.py:26
  7.6 0.5 %collective-permute-start = (bf16[272,256]{1,0:T(8,128)(2,1)S(1)}, bf16[272,256]{1,0:T(8,128)(2,1)S(1)}, u32[]{:S(2)}, u32[]{:S(2)}) collective-permute-start(bf16[272,256]{1,0:T(8,128)(2,1)S(1)} %get-tuple-element.22), channel_id=1, source_target_pairs={{0,4},{4,0},{8,12},{12,8},{1,5},{5,1},{9,13},{13,9},{2,6},{6,2},{1... | collective-permute-start | bytes 417800 | tf_op jit(solution)/shard_map/ppermute | solution.py:26
  8.1 0.1 collective-permute-start.1
  8.2 2.4 %collective-permute-done.2.refs_1_ = bf16[272,256]{1,0:T(8,128)(2,1)S(1)} collective-permute-done((bf16[272,256]{1,0:T(8,128)(2,1)S(1)}, bf16[272,256]{1,0:T(8,128)(2,1)S(1)}, u32[]{:S(2)}, u32[]{:S(2)}) %collective-permute-start.2) | collective-permute-done | bytes 139296 | tf_op jit(solution)/shard_map/ppermute | solution.py:26
  10.6 2.0 %collective-permute-done.3.refs_2_ = bf16[272,256]{1,0:T(8,128)(2,1)S(1)} collective-permute-done((bf16[272,256]{1,0:T(8,128)(2,1)S(1)}, bf16[272,256]{1,0:T(8,128)(2,1)S(1)}, u32[]{:S(2)}, u32[]{:S(2)}) %collective-permute-start.3) | collective-permute-done | bytes 139296 | tf_op jit(solution)/shard_map/ppermute | solution.py:26
  12.6 0.1 relay.1
  12.6 0.0 copy-start.1
  12.6 0.1 collective-permute-start.4
  12.7 2.0 %collective-permute-start.5 = (bf16[272,256]{1,0:T(8,128)(2,1)S(1)}, bf16[272,256]{1,0:T(8,128)(2,1)S(1)}, u32[]{:S(2)}, u32[]{:S(2)}) collective-permute-start(bf16[272,256]{1,0:T(8,128)(2,1)S(1)} %get-tuple-element.27.refs_3_), channel_id=1, source_target_pairs={{0,8},{4,12},{8,0},{12,4},{1,9},{5,13},{9,1},{13,5},{2,10},{6,14},... | collective-permute-start | bytes 417800 | tf_op jit(solution)/shard_map/ppermute | solution.py:26
  14.7 0.0 collective-permute-done.12
  14.8 0.5 %grad.1 = (bf16[256,256]{1,0:T(8,128)(2,1)S(1)}, bf16[256,256]{1,0:T(8,128)(2,1)S(1)}, f32[512,256]{1,0:T(8,128)S(1)}) custom-call(bf16[512,1024]{1,0:T(8,128)(2,1)S(1)} %bitcast.8, bf16[512,256]{1,0:T(8,128)(2,1)S(1)} %bitcast.11, bf16[272,256]{1,0:T(8,128)(2,1)S(1)} %get-tuple-element.26.refs_2_, bf16[272,256]{1,0:T(8,128)(2,1)S(1)} %get-tuple-element.27.refs_3_), custom_call_target="tpu_custom_call" | custom-call | tf_op jit(solution)/shard_map/grad/pallas_call | solution.py:333
  15.3 1.6 %collective-permute-start.13 = (bf16[256,256]{1,0:T(8,128)(2,1)S(1)}, bf16[256,256]{1,0:T(8,128)(2,1)S(1)}, u32[]{:S(2)}, u32[]{:S(2)}) collective-permute-start(bf16[256,256]{1,0:T(8,128)(2,1)S(1)} %get-tuple-element.34), channel_id=1, source_target_pairs={{0,4},{4,0},{8,12},{12,8},{1,5},{5,1},{9,13},{13,9},{2,6},{6,2},{1... | collective-permute-start | bytes 393224 | tf_op jit(solution)/shard_map/ppermute | solution.py:26
  16.8 0.0 collective-permute-done.refs_1_
  16.8 0.5 %collective-permute-start.14 = (bf16[256,256]{1,0:T(8,128)(2,1)S(1)}, bf16[256,256]{1,0:T(8,128)(2,1)S(1)}, u32[]{:S(2)}, u32[]{:S(2)}) collective-permute-start(bf16[256,256]{1,0:T(8,128)(2,1)S(1)} %get-tuple-element.35), channel_id=1, source_target_pairs={{0,8},{4,12},{8,0},{12,4},{1,9},{5,13},{9,1},{13,5},{2,10},{6,14},... | collective-permute-start | bytes 393224 | tf_op jit(solution)/shard_map/ppermute | solution.py:26
  17.4 0.0 collective-permute-done.1.refs_2_
  17.4 1.7 %collective-permute-done.4.refs_3_ = bf16[272,256]{1,0:T(8,128)(2,1)S(1)} collective-permute-done((bf16[272,256]{1,0:T(8,128)(2,1)S(1)}, bf16[272,256]{1,0:T(8,128)(2,1)S(1)}, u32[]{:S(2)}, u32[]{:S(2)}) %collective-permute-start.4) | collective-permute-done | bytes 139296 | tf_op jit(solution)/shard_map/ppermute | solution.py:26
  19.0 0.0 collective-permute-done.5.refs_4_
  19.0 0.0 copy-done.1
  19.0 0.4 %factor.1 = (bf16[272,256]{1,0:T(8,128)(2,1)S(1)}, bf16[288,256]{1,0:T(8,128)(2,1)S(1)}, f32[640,256]{1,0:T(8,128)S(1)}) custom-call(f32[1088,256]{1,0:T(8,128)S(1)} %get-tuple-element.21.refs_0_, bf16[272,256]{1,0:T(8,128)(2,1)S(1)} %collective-permute-done.refs_1_, bf16[272,256]{1,0:T(8,128)(2,1)S(1)} %collective-permute-done.1.refs_2_, ...), custom_call_target="tpu_custom_call" | custom-call | tf_op jit(solution)/shard_map/factor/pallas_call | solution.py:333
  19.4 1.8 %collective-permute-start.6 = (bf16[272,256]{1,0:T(8,128)(2,1)S(1)}, bf16[272,256]{1,0:T(8,128)(2,1)S(1)}, u32[]{:S(2)}, u32[]{:S(2)}) collective-permute-start(bf16[272,256]{1,0:T(8,128)(2,1)S(1)} %get-tuple-element.29.refs_2_.refs_3_), channel_id=1, source_target_pairs={{0,4},{4,0},{8,12},{12,8},{1,5},{5,1},{9,13},{13,9},{2,6},{6,2},{1... | collective-permute-start | bytes 417800 | tf_op jit(solution)/shard_map/ppermute | solution.py:26
  21.3 1.1 %collective-permute-start.9 = (bf16[288,256]{1,0:T(8,128)(2,1)S(1)}, bf16[288,256]{1,0:T(8,128)(2,1)S(1)}, u32[]{:S(2)}, u32[]{:S(2)}) collective-permute-start(bf16[288,256]{1,0:T(8,128)(2,1)S(1)} %get-tuple-element.30.refs_3_.refs_4_), channel_id=1, source_target_pairs={{0,8},{4,12},{8,0},{12,4},{1,9},{5,13},{9,1},{13,5},{2,10},{6,14},... | collective-permute-start | bytes 442376 | tf_op jit(solution)/shard_map/ppermute | solution.py:26
  22.3 0.9 %collective-permute-start.7 = (bf16[288,256]{1,0:T(8,128)(2,1)S(1)}, bf16[288,256]{1,0:T(8,128)(2,1)S(1)}, u32[]{:S(2)}, u32[]{:S(2)}) collective-permute-start(bf16[288,256]{1,0:T(8,128)(2,1)S(1)} %get-tuple-element.30.refs_3_.refs_4_), channel_id=1, source_target_pairs={{0,4},{4,0},{8,12},{12,8},{1,5},{5,1},{9,13},{13,9},{2,6},{6,2},{1... | collective-permute-start | bytes 442376 | tf_op jit(solution)/shard_map/ppermute | solution.py:26
  23.3 0.0 collective-permute-done.13.refs_1_
  23.3 0.3 collective-permute-start.8
  23.6 0.0 collective-permute-done.14.refs_2_
  23.6 1.8 %collective-permute-start.15 = (bf16[128,256]{1,0:T(8,128)(2,1)S(1)}, bf16[128,256]{1,0:T(8,128)(2,1)S(1)}, u32[]{:S(2)}, u32[]{:S(2)}) collective-permute-start(bf16[128,256]{1,0:T(8,128)(2,1)S(1)} %get-tuple-element.36), channel_id=1, source_target_pairs={{0,4},{4,0},{8,12},{12,8},{1,5},{5,1},{9,13},{13,9},{2,6},{6,2},{1... | collective-permute-start | bytes 196616 | tf_op jit(solution)/shard_map/ppermute | solution.py:26
  25.4 0.3 collective-permute-done.6.refs_4_.refs_5_
  25.7 1.0 %collective-permute-start.16 = (bf16[128,256]{1,0:T(8,128)(2,1)S(1)}, bf16[128,256]{1,0:T(8,128)(2,1)S(1)}, u32[]{:S(2)}, u32[]{:S(2)}) collective-permute-start(bf16[128,256]{1,0:T(8,128)(2,1)S(1)} %get-tuple-element.37), channel_id=1, source_target_pairs={{0,8},{4,12},{8,0},{12,4},{1,9},{5,13},{9,1},{13,5},{2,10},{6,14},... | collective-permute-start | bytes 196616 | tf_op jit(solution)/shard_map/ppermute | solution.py:26
  26.7 0.3 collective-permute-done.9.refs_7_.refs_6_
  26.9 0.8 %collective-permute-start.11 = (bf16[288,256]{1,0:T(8,128)(2,1)S(1)}, bf16[288,256]{1,0:T(8,128)(2,1)S(1)}, u32[]{:S(2)}, u32[]{:S(2)}) collective-permute-start(bf16[288,256]{1,0:T(8,128)(2,1)S(1)} %collective-permute-done.9.refs_7_.refs_6_), channel_id=1, source_target_pairs={{0,4},{4,0},{8,12},{12,8},{1,5},{5,1},{9,13},{13,9},{2,6},{6,2},{1... | collective-permute-start | bytes 442376 | tf_op jit(solution)/shard_map/ppermute | solution.py:26
  27.7 2.7 %collective-permute-done.15.refs_3_ = bf16[128,256]{1,0:T(8,128)(2,1)S(1)} collective-permute-done((bf16[128,256]{1,0:T(8,128)(2,1)S(1)}, bf16[128,256]{1,0:T(8,128)(2,1)S(1)}, u32[]{:S(2)}, u32[]{:S(2)}) %collective-permute-start.15) | collective-permute-done | bytes 65568 | tf_op jit(solution)/shard_map/ppermute | solution.py:26
  30.4 0.5 %collective-permute-start.10 = (bf16[272,256]{1,0:T(8,128)(2,1)S(1)}, bf16[272,256]{1,0:T(8,128)(2,1)S(1)}, u32[]{:S(2)}, u32[]{:S(2)}) collective-permute-start(bf16[272,256]{1,0:T(8,128)(2,1)S(1)} %collective-permute-done.6.refs_4_.refs_5_), channel_id=1, source_target_pairs={{0,8},{4,12},{8,0},{12,4},{1,9},{5,13},{9,1},{13,5},{2,10},{6,14},... | collective-permute-start | bytes 417800 | tf_op jit(solution)/shard_map/ppermute | solution.py:26
  30.9 0.0 collective-permute-done.16.refs_4_
  30.9 0.1 grad_total.1.refs_0_
  31.0 0.0 copy-start.2
  31.0 2.7 %collective-permute-start.17 = (bf16[256,256]{1,0:T(8,128)(2,1)S(1)}, bf16[256,256]{1,0:T(8,128)(2,1)S(1)}, u32[]{:S(2)}, u32[]{:S(2)}) collective-permute-start(bf16[256,256]{1,0:T(8,128)(2,1)S(1)} %grad_total.1.refs_0_), channel_id=1, source_target_pairs={{0,4},{4,0},{8,12},{12,8},{1,5},{5,1},{9,13},{13,9},{2,6},{6,2},{1... | collective-permute-start | bytes 393224 | tf_op jit(solution)/shard_map/ppermute | solution.py:26
  33.6 0.0 collective-permute-done.8.refs_6_
  33.6 0.1 collective-permute-start.18
  33.7 0.0 collective-permute-done.7.refs_5_
  33.7 1.5 %collective-permute-start.19 = (bf16[256,256]{1,0:T(8,128)(2,1)S(1)}, bf16[256,256]{1,0:T(8,128)(2,1)S(1)}, u32[]{:S(2)}, u32[]{:S(2)}) collective-permute-start(bf16[256,256]{1,0:T(8,128)(2,1)S(1)} %grad_total.1.refs_0_), channel_id=1, source_target_pairs={{0,12},{4,8},{8,4},{12,0},{1,13},{5,9},{9,5},{13,1},{2,14},{6,10},... | collective-permute-start | bytes 393224 | tf_op jit(solution)/shard_map/ppermute | solution.py:26
  35.8 0.0 collective-permute-done.10.refs_8_
  35.9 0.0 collective-permute-done.11.refs_9_
  35.9 3.8 %root.1 = (f32[256,1024]{1,0:T(8,128)}, bf16[256,1024]{1,0:T(8,128)(2,1)}, f32[8,128]{1,0:T(8,128)S(1)}) custom-call(s32[1,1]{1,0:T(1,128)S(6)} %copy.8.refs_0_, f32[640,256]{1,0:T(8,128)S(1)} %get-tuple-element.28.refs_1_, bf16[272,256]{1,0:T(8,128)(2,1)S(1)} %get-tuple-element.29.refs_2_.refs_3_, bf16[288,256]{1,0:T(8,128)(2,1)S(1)} %get-tuple-element.30.refs_3_.refs_4_, ...), custom_call_target="tpu_custom_call" | custom-call | tf_op jit(solution)/shard_map/root/pallas_call | solution.py:333
  39.7 0.0 collective-permute-done.17.refs_1_
  39.7 0.3 collective-permute-done.18.refs_2_
  40.0 0.0 collective-permute-done.19.refs_3_
  40.0 0.0 copy-done.2
  40.0 1.0 %step.1 = bf16[256,256]{1,0:T(8,128)(2,1)} custom-call(bf16[256,256]{1,0:T(8,128)(2,1)S(1)} %grad_total.1.refs_0_, bf16[256,256]{1,0:T(8,128)(2,1)S(1)} %collective-permute-done.17.refs_1_, bf16[256,256]{1,0:T(8,128)(2,1)S(1)} %collective-permute-done.18.refs_2_, bf16[256,256]{1,0:T(8,128)(2,1)S(1)} %collective-permute-done.19.refs_3_, ...), custom_call_target="tpu_custom_call" | custom-call | tf_op jit(solution)/shard_map/step/pallas_call | solution.py:333
  (1 shorter events, 0.0 us)
Async XLA Ops:
  0.6 14.1 %collective-permute-start.12 = (bf16[1,512,256]{2,1,0:T(8,128)(2,1)}, bf16[1,512,256]{2,1,0:T(8,128)(2,1)S(1)}, u32[]{:S(2)}, u32[]{:S(2)}) collective-permute-start(bf16[1,512,256]{2,1,0:T(8,128)(2,1)} %param.6), channel_id=1, source_target_pairs={{16,0},{0,16},{17,1},{1,17},{18,2},{2,18},{19,3},{3,19},{20,4},{4,... | collective-permute-start | bytes 786440 | tf_op jit(solution)/shard_map/ppermute | solution.py:22
  1.1 1.2 %copy-start = (bf16[1,512,1024]{2,1,0:T(8,128)(2,1)S(1)}, bf16[1,512,1024]{2,1,0:T(8,128)(2,1)}, u32[]{:S(2)}) copy-start(bf16[1,512,1024]{2,1,0:T(8,128)(2,1)} %param.5) | copy-start | bytes 3145732
  3.5 7.1 %collective-permute-start.2 = (bf16[272,256]{1,0:T(8,128)(2,1)S(1)}, bf16[272,256]{1,0:T(8,128)(2,1)S(1)}, u32[]{:S(2)}, u32[]{:S(2)}) collective-permute-start(bf16[272,256]{1,0:T(8,128)(2,1)S(1)} %get-tuple-element.24), channel_id=1, source_target_pairs={{0,4},{4,0},{8,12},{12,8},{1,5},{5,1},{9,13},{13,9},{2,6},{6,2},{1... | collective-permute-start | bytes 417800 | tf_op jit(solution)/shard_map/ppermute | solution.py:26
  6.0 6.5 %collective-permute-start.3 = (bf16[272,256]{1,0:T(8,128)(2,1)S(1)}, bf16[272,256]{1,0:T(8,128)(2,1)S(1)}, u32[]{:S(2)}, u32[]{:S(2)}) collective-permute-start(bf16[272,256]{1,0:T(8,128)(2,1)S(1)} %get-tuple-element.25), channel_id=1, source_target_pairs={{0,8},{4,12},{8,0},{12,4},{1,9},{5,13},{9,1},{13,5},{2,10},{6,14},... | collective-permute-start | bytes 417800 | tf_op jit(solution)/shard_map/ppermute | solution.py:26
  7.6 9.3 %collective-permute-start = (bf16[272,256]{1,0:T(8,128)(2,1)S(1)}, bf16[272,256]{1,0:T(8,128)(2,1)S(1)}, u32[]{:S(2)}, u32[]{:S(2)}) collective-permute-start(bf16[272,256]{1,0:T(8,128)(2,1)S(1)} %get-tuple-element.22), channel_id=1, source_target_pairs={{0,4},{4,0},{8,12},{12,8},{1,5},{5,1},{9,13},{13,9},{2,6},{6,2},{1... | collective-permute-start | bytes 417800 | tf_op jit(solution)/shard_map/ppermute | solution.py:26
  8.1 9.3 %collective-permute-start.1 = (bf16[272,256]{1,0:T(8,128)(2,1)S(1)}, bf16[272,256]{1,0:T(8,128)(2,1)S(1)}, u32[]{:S(2)}, u32[]{:S(2)}) collective-permute-start(bf16[272,256]{1,0:T(8,128)(2,1)S(1)} %get-tuple-element.23), channel_id=1, source_target_pairs={{0,8},{4,12},{8,0},{12,4},{1,9},{5,13},{9,1},{13,5},{2,10},{6,14},... | collective-permute-start | bytes 417800 | tf_op jit(solution)/shard_map/ppermute | solution.py:26
  12.6 6.4 %copy-start.1 = (f32[1,1,256,1024]{3,2,1,0:T(8,128)S(1)}, f32[1,1,256,1024]{3,2,1,0:T(8,128)}, u32[]{:S(2)}) copy-start(f32[1,1,256,1024]{3,2,1,0:T(8,128)} %param.7) | copy-start | bytes 3145732
  12.6 6.4 %collective-permute-start.4 = (bf16[272,256]{1,0:T(8,128)(2,1)S(1)}, bf16[272,256]{1,0:T(8,128)(2,1)S(1)}, u32[]{:S(2)}, u32[]{:S(2)}) collective-permute-start(bf16[272,256]{1,0:T(8,128)(2,1)S(1)} %get-tuple-element.26.refs_2_), channel_id=1, source_target_pairs={{0,4},{4,0},{8,12},{12,8},{1,5},{5,1},{9,13},{13,9},{2,6},{6,2},{1... | collective-permute-start | bytes 417800 | tf_op jit(solution)/shard_map/ppermute | solution.py:26
  12.7 6.3 %collective-permute-start.5 = (bf16[272,256]{1,0:T(8,128)(2,1)S(1)}, bf16[272,256]{1,0:T(8,128)(2,1)S(1)}, u32[]{:S(2)}, u32[]{:S(2)}) collective-permute-start(bf16[272,256]{1,0:T(8,128)(2,1)S(1)} %get-tuple-element.27.refs_3_), channel_id=1, source_target_pairs={{0,8},{4,12},{8,0},{12,4},{1,9},{5,13},{9,1},{13,5},{2,10},{6,14},... | collective-permute-start | bytes 417800 | tf_op jit(solution)/shard_map/ppermute | solution.py:26
  15.3 8.0 %collective-permute-start.13 = (bf16[256,256]{1,0:T(8,128)(2,1)S(1)}, bf16[256,256]{1,0:T(8,128)(2,1)S(1)}, u32[]{:S(2)}, u32[]{:S(2)}) collective-permute-start(bf16[256,256]{1,0:T(8,128)(2,1)S(1)} %get-tuple-element.34), channel_id=1, source_target_pairs={{0,4},{4,0},{8,12},{12,8},{1,5},{5,1},{9,13},{13,9},{2,6},{6,2},{1... | collective-permute-start | bytes 393224 | tf_op jit(solution)/shard_map/ppermute | solution.py:26
  16.8 6.7 %collective-permute-start.14 = (bf16[256,256]{1,0:T(8,128)(2,1)S(1)}, bf16[256,256]{1,0:T(8,128)(2,1)S(1)}, u32[]{:S(2)}, u32[]{:S(2)}) collective-permute-start(bf16[256,256]{1,0:T(8,128)(2,1)S(1)} %get-tuple-element.35), channel_id=1, source_target_pairs={{0,8},{4,12},{8,0},{12,4},{1,9},{5,13},{9,1},{13,5},{2,10},{6,14},... | collective-permute-start | bytes 393224 | tf_op jit(solution)/shard_map/ppermute | solution.py:26
  19.4 6.2 %collective-permute-start.6 = (bf16[272,256]{1,0:T(8,128)(2,1)S(1)}, bf16[272,256]{1,0:T(8,128)(2,1)S(1)}, u32[]{:S(2)}, u32[]{:S(2)}) collective-permute-start(bf16[272,256]{1,0:T(8,128)(2,1)S(1)} %get-tuple-element.29.refs_2_.refs_3_), channel_id=1, source_target_pairs={{0,4},{4,0},{8,12},{12,8},{1,5},{5,1},{9,13},{13,9},{2,6},{6,2},{1... | collective-permute-start | bytes 417800 | tf_op jit(solution)/shard_map/ppermute | solution.py:26
  21.3 5.6 %collective-permute-start.9 = (bf16[288,256]{1,0:T(8,128)(2,1)S(1)}, bf16[288,256]{1,0:T(8,128)(2,1)S(1)}, u32[]{:S(2)}, u32[]{:S(2)}) collective-permute-start(bf16[288,256]{1,0:T(8,128)(2,1)S(1)} %get-tuple-element.30.refs_3_.refs_4_), channel_id=1, source_target_pairs={{0,8},{4,12},{8,0},{12,4},{1,9},{5,13},{9,1},{13,5},{2,10},{6,14},... | collective-permute-start | bytes 442376 | tf_op jit(solution)/shard_map/ppermute | solution.py:26
  22.3 11.4 %collective-permute-start.7 = (bf16[288,256]{1,0:T(8,128)(2,1)S(1)}, bf16[288,256]{1,0:T(8,128)(2,1)S(1)}, u32[]{:S(2)}, u32[]{:S(2)}) collective-permute-start(bf16[288,256]{1,0:T(8,128)(2,1)S(1)} %get-tuple-element.30.refs_3_.refs_4_), channel_id=1, source_target_pairs={{0,4},{4,0},{8,12},{12,8},{1,5},{5,1},{9,13},{13,9},{2,6},{6,2},{1... | collective-permute-start | bytes 442376 | tf_op jit(solution)/shard_map/ppermute | solution.py:26
  23.3 10.4 %collective-permute-start.8 = (bf16[272,256]{1,0:T(8,128)(2,1)S(1)}, bf16[272,256]{1,0:T(8,128)(2,1)S(1)}, u32[]{:S(2)}, u32[]{:S(2)}) collective-permute-start(bf16[272,256]{1,0:T(8,128)(2,1)S(1)} %get-tuple-element.29.refs_2_.refs_3_), channel_id=1, source_target_pairs={{0,8},{4,12},{8,0},{12,4},{1,9},{5,13},{9,1},{13,5},{2,10},{6,14},... | collective-permute-start | bytes 417800 | tf_op jit(solution)/shard_map/ppermute | solution.py:26
  23.6 6.8 %collective-permute-start.15 = (bf16[128,256]{1,0:T(8,128)(2,1)S(1)}, bf16[128,256]{1,0:T(8,128)(2,1)S(1)}, u32[]{:S(2)}, u32[]{:S(2)}) collective-permute-start(bf16[128,256]{1,0:T(8,128)(2,1)S(1)} %get-tuple-element.36), channel_id=1, source_target_pairs={{0,4},{4,0},{8,12},{12,8},{1,5},{5,1},{9,13},{13,9},{2,6},{6,2},{1... | collective-permute-start | bytes 196616 | tf_op jit(solution)/shard_map/ppermute | solution.py:26
  25.7 5.2 %collective-permute-start.16 = (bf16[128,256]{1,0:T(8,128)(2,1)S(1)}, bf16[128,256]{1,0:T(8,128)(2,1)S(1)}, u32[]{:S(2)}, u32[]{:S(2)}) collective-permute-start(bf16[128,256]{1,0:T(8,128)(2,1)S(1)} %get-tuple-element.37), channel_id=1, source_target_pairs={{0,8},{4,12},{8,0},{12,4},{1,9},{5,13},{9,1},{13,5},{2,10},{6,14},... | collective-permute-start | bytes 196616 | tf_op jit(solution)/shard_map/ppermute | solution.py:26
  26.9 9.0 %collective-permute-start.11 = (bf16[288,256]{1,0:T(8,128)(2,1)S(1)}, bf16[288,256]{1,0:T(8,128)(2,1)S(1)}, u32[]{:S(2)}, u32[]{:S(2)}) collective-permute-start(bf16[288,256]{1,0:T(8,128)(2,1)S(1)} %collective-permute-done.9.refs_7_.refs_6_), channel_id=1, source_target_pairs={{0,4},{4,0},{8,12},{12,8},{1,5},{5,1},{9,13},{13,9},{2,6},{6,2},{1... | collective-permute-start | bytes 442376 | tf_op jit(solution)/shard_map/ppermute | solution.py:26
  30.4 5.4 %collective-permute-start.10 = (bf16[272,256]{1,0:T(8,128)(2,1)S(1)}, bf16[272,256]{1,0:T(8,128)(2,1)S(1)}, u32[]{:S(2)}, u32[]{:S(2)}) collective-permute-start(bf16[272,256]{1,0:T(8,128)(2,1)S(1)} %collective-permute-done.6.refs_4_.refs_5_), channel_id=1, source_target_pairs={{0,8},{4,12},{8,0},{12,4},{1,9},{5,13},{9,1},{13,5},{2,10},{6,14},... | collective-permute-start | bytes 417800 | tf_op jit(solution)/shard_map/ppermute | solution.py:26
  31.0 9.1 %copy-start.2 = (bf16[1,1,256,1024]{3,2,1,0:T(8,128)(2,1)S(1)}, bf16[1,1,256,1024]{3,2,1,0:T(8,128)(2,1)}, u32[]{:S(2)}) copy-start(bf16[1,1,256,1024]{3,2,1,0:T(8,128)(2,1)} %param.8) | copy-start | bytes 1572868
  31.0 8.7 %collective-permute-start.17 = (bf16[256,256]{1,0:T(8,128)(2,1)S(1)}, bf16[256,256]{1,0:T(8,128)(2,1)S(1)}, u32[]{:S(2)}, u32[]{:S(2)}) collective-permute-start(bf16[256,256]{1,0:T(8,128)(2,1)S(1)} %grad_total.1.refs_0_), channel_id=1, source_target_pairs={{0,4},{4,0},{8,12},{12,8},{1,5},{5,1},{9,13},{13,9},{2,6},{6,2},{1... | collective-permute-start | bytes 393224 | tf_op jit(solution)/shard_map/ppermute | solution.py:26
  33.6 6.4 %collective-permute-start.18 = (bf16[256,256]{1,0:T(8,128)(2,1)S(1)}, bf16[256,256]{1,0:T(8,128)(2,1)S(1)}, u32[]{:S(2)}, u32[]{:S(2)}) collective-permute-start(bf16[256,256]{1,0:T(8,128)(2,1)S(1)} %grad_total.1.refs_0_), channel_id=1, source_target_pairs={{0,8},{4,12},{8,0},{12,4},{1,9},{5,13},{9,1},{13,5},{2,10},{6,14},... | collective-permute-start | bytes 393224 | tf_op jit(solution)/shard_map/ppermute | solution.py:26
  33.7 6.3 %collective-permute-start.19 = (bf16[256,256]{1,0:T(8,128)(2,1)S(1)}, bf16[256,256]{1,0:T(8,128)(2,1)S(1)}, u32[]{:S(2)}, u32[]{:S(2)}) collective-permute-start(bf16[256,256]{1,0:T(8,128)(2,1)S(1)} %grad_total.1.refs_0_), channel_id=1, source_target_pairs={{0,12},{4,8},{8,4},{12,0},{1,13},{5,9},{9,5},{13,1},{2,14},{6,10},... | collective-permute-start | bytes 393224 | tf_op jit(solution)/shard_map/ppermute | solution.py:26

commit v17 on v16

--- a/solution.py
+++ b/solution.py
@@ -101,12 +101,31 @@
                 ref[at + first - low : at + last - low, :] = piece[first - start : last - start].astype(ref.dtype)
 
 
-def batch_kernel(replicas, tokens_all, acts, relay_x, relay_y, direct_x, direct_y, keep, batch):
+def across_kernel(tokens_all, acts, relay_x, relay_y):
+    share = relay_x.shape[1]
+    half = share // 2
+    starts = chunk_rows(share)
+    owner = lax.axis_index("dp") ^ 3
+
+    def product(left, right):
+        return lax.dot_general(
+            acts[:, left], acts[:, right], (((0,), (0,)), ((), ())), preferred_element_type=F32
+        ) * (1.0 / tokens_all)
+
+    columns = pl.ds(pl.multiple_of(owner * share, share), share)
+    pieces = [(0, packed_upper(product(columns, columns)))]
+    for start, step in zip(starts[1:], OFFSETS[1:]):
+        row, col = shared_half(owner, step, share)
+        pieces.append((start, product(pl.ds(row, half), pl.ds(col, share))))
+    store_chunk(pieces, relay_x.shape[0], (relay_x, 0), (relay_y, 0))
+
+
+def batch_kernel(replicas, tokens_all, acts, direct_x, direct_y, keep, batch):
     order = acts.shape[1]
     share = order // replicas
     half = share // 2
     starts = chunk_rows(share)
-    length = relay_x.shape[0]
+    length = direct_x.shape[0]
     mine = lax.axis_index("dp")
     for i in range(replicas):
         band = slice(i * share, (i + 1) * share)
@@ -122,7 +141,6 @@
             row, col = shared_half(owner, step, share)
             yield start, batch[pl.ds(row, half), pl.ds(col, share)]
 
-    store_chunk(pieces(3), length, (relay_x, 0), (relay_y, 0))
     store_chunk(pieces(1), length, (direct_x, 0), (keep, 3 * length))
     store_chunk(pieces(2), length, (keep, 2 * length), (direct_y, 0))
     store_chunk(pieces(0), length, (keep, 0), (keep, length))
@@ -341,11 +359,15 @@
         )(*operands, *after)
 
     received = passed_along(out_grad, "pipe", -1)[0]
-    relay_x, relay_y, direct_x, direct_y, keep = call(
+    relay_x, relay_y = call(
+        functools.partial(across_kernel, tokens * replicas), [shape(length)] * 2, "across", inputs
+    )
+    direct_x, direct_y, keep = call(
         functools.partial(batch_kernel, replicas, tokens * replicas),
-        [shape(length)] * 4 + [shape(4 * length, F32)],
+        [shape(length)] * 2 + [shape(4 * length, F32)],
         "batch",
         inputs,
+        after=[relay_x],
         scratch=[pltpu.VMEM((order, order), F32)],
     )
     relay_x, relay_y = swapped(relay_x, 1), swapped(relay_y, 2)

time: 41.2 us -> 40.7 us (0.988)
  waiting for transfers between devices: 9.66 us -> 7.4 us
  starting transfers between devices: 21.7 us -> 23.1 us
  Pallas kernels: 7 us -> 7.42 us
    ppermute x19, waiting for transfers between devices: 9.66 us -> 7.4 us  [swapped(): lax.ppermute(block, 'dp', [(i, i ^ offset) for i in range(lax.axis_size('...]
    ppermute x19, starting transfers between devices: 21.2 us -> 22.6 us  [swapped(): lax.ppermute(block, 'dp', [(i, i ^ offset) for i in range(lax.axis_size('...]
    pallas_call x8 -> x9, Pallas kernels: 7 us -> 7.42 us  [call(): pl.pallas_call(body, out_shape=outs, in_specs=in_specs, out_specs=out_spe...]
    unnamed x6 -> x8, local copies, waits for them, and re-layouts: 1.24 us -> 1.24 us
  transfers between devices with their start and end apart: 20 -> 20, of which waited for: 7 -> 6; matrix products, arithmetic and copies ran while one was open for 0% -> 0% of each run, Pallas kernels for 15% -> 16%
where the time goes in v17:
time: 40.7 us; the launch traced here: 40.5 us
  starting transfers between devices  23.1 us (57%)
  Pallas kernels  7.42 us (18%)
  waiting for transfers between devices  7.4 us (18%)
  between operations  1.38 us (3%)
  local copies, waits for them, and re-layouts  1.24 us (3%)
    ppermute x19, starting transfers between devices, swapped(): lax.ppermute(block, 'dp', [(i, i ^ offset) for i in range(lax.axis_size('...  22.6 us
    pallas_call x9, Pallas kernels, call(): pl.pallas_call(body, out_shape=outs, in_specs=in_specs, out_specs=out_spe...  7.42 us
    ppermute x19, waiting for transfers between devices, swapped(): lax.ppermute(block, 'dp', [(i, i ^ offset) for i in range(lax.axis_size('...  7.4 us
    unnamed x8, local copies, waits for them, and re-layouts  1.24 us
  transfers between devices with their start and end apart: 20, of which 6 were waited for; matrix products, arithmetic and copies ran while one was open for 0% of the time, Pallas kernels for 16%

profile of v17, /device:TPU:0, one launch (start us, length us, event | category | flops | bytes accessed | tf_op | source)
XLA Modules:
  0.0 40.5 jit_solution(10140463130107092738)
XLA Ops:
  0.6 0.5 %collective-permute-start.12 = (bf16[1,512,256]{2,1,0:T(8,128)(2,1)}, bf16[1,512,256]{2,1,0:T(8,128)(2,1)S(1)}, u32[]{:S(2)}, u32[]{:S(2)}) collective-permute-start(bf16[1,512,256]{2,1,0:T(8,128)(2,1)} %param.6), channel_id=1, source_target_pairs={{16,0},{0,16},{17,1},{1,17},{18,2},{2,18},{19,3},{3,19},{20,4},{4,... | collective-permute-start | bytes 786440 | tf_op jit(solution)/shard_map/ppermute | solution.py:22
  1.1 0.0 copy-start
  1.1 1.2 %copy-done = bf16[1,512,1024]{2,1,0:T(8,128)(2,1)S(1)} copy-done((bf16[1,512,1024]{2,1,0:T(8,128)(2,1)S(1)}, bf16[1,512,1024]{2,1,0:T(8,128)(2,1)}, u32[]{:S(2)}) %copy-start) | copy-done | bytes 1048600
  2.4 0.5 %across.1 = (bf16[272,256]{1,0:T(8,128)(2,1)S(1)}, bf16[272,256]{1,0:T(8,128)(2,1)S(1)}) custom-call(bf16[512,1024]{1,0:T(8,128)(2,1)S(1)} %bitcast.7), custom_call_target="tpu_custom_call" | custom-call | tf_op jit(solution)/shard_map/across/pallas_call | solution.py:351
  2.8 2.6 %collective-permute-start.2 = (bf16[272,256]{1,0:T(8,128)(2,1)S(1)}, bf16[272,256]{1,0:T(8,128)(2,1)S(1)}, u32[]{:S(2)}, u32[]{:S(2)}) collective-permute-start(bf16[272,256]{1,0:T(8,128)(2,1)S(1)} %get-tuple-element.21.refs_1_), channel_id=1, source_target_pairs={{0,4},{4,0},{8,12},{12,8},{1,5},{5,1},{9,13},{13,9},{2,6},{6,2},{1... | collective-permute-start | bytes 417800 | tf_op jit(solution)/shard_map/ppermute | solution.py:26
  5.4 0.0 copy-start.1
  5.4 1.5 %collective-permute-start.3 = (bf16[272,256]{1,0:T(8,128)(2,1)S(1)}, bf16[272,256]{1,0:T(8,128)(2,1)S(1)}, u32[]{:S(2)}, u32[]{:S(2)}) collective-permute-start(bf16[272,256]{1,0:T(8,128)(2,1)S(1)} %get-tuple-element.25), channel_id=1, source_target_pairs={{0,8},{4,12},{8,0},{12,4},{1,9},{5,13},{9,1},{13,5},{2,10},{6,14},... | collective-permute-start | bytes 417800 | tf_op jit(solution)/shard_map/ppermute | solution.py:26
  6.9 1.1 %batch.1 = (bf16[272,256]{1,0:T(8,128)(2,1)S(1)}, bf16[272,256]{1,0:T(8,128)(2,1)S(1)}, f32[1088,256]{1,0:T(8,128)S(1)}) custom-call(bf16[512,1024]{1,0:T(8,128)(2,1)S(1)} %bitcast.8, bf16[272,256]{1,0:T(8,128)(2,1)S(1)} %get-tuple-element.21.refs_1_), custom_call_target="tpu_custom_call" | custom-call | tf_op jit(solution)/shard_map/batch/pallas_call | solution.py:351
  8.0 0.6 %collective-permute-start = (bf16[272,256]{1,0:T(8,128)(2,1)S(1)}, bf16[272,256]{1,0:T(8,128)(2,1)S(1)}, u32[]{:S(2)}, u32[]{:S(2)}) collective-permute-start(bf16[272,256]{1,0:T(8,128)(2,1)S(1)} %get-tuple-element.23), channel_id=1, source_target_pairs={{0,4},{4,0},{8,12},{12,8},{1,5},{5,1},{9,13},{13,9},{2,6},{6,2},{1... | collective-permute-start | bytes 417800 | tf_op jit(solution)/shard_map/ppermute | solution.py:26
  8.6 0.1 collective-permute-start.1
  8.7 1.1 %collective-permute-done.2.refs_1_ = bf16[272,256]{1,0:T(8,128)(2,1)S(1)} collective-permute-done((bf16[272,256]{1,0:T(8,128)(2,1)S(1)}, bf16[272,256]{1,0:T(8,128)(2,1)S(1)}, u32[]{:S(2)}, u32[]{:S(2)}) %collective-permute-start.2) | collective-permute-done | bytes 139296 | tf_op jit(solution)/shard_map/ppermute | solution.py:26
  9.7 1.7 %collective-permute-done.3.refs_2_ = bf16[272,256]{1,0:T(8,128)(2,1)S(1)} collective-permute-done((bf16[272,256]{1,0:T(8,128)(2,1)S(1)}, bf16[272,256]{1,0:T(8,128)(2,1)S(1)}, u32[]{:S(2)}, u32[]{:S(2)}) %collective-permute-start.3) | collective-permute-done | bytes 139296 | tf_op jit(solution)/shard_map/ppermute | solution.py:26
  11.5 0.1 relay.1
  11.5 0.0 copy-start.2
  11.6 0.3 collective-permute-start.4
  11.9 1.8 %collective-permute-start.5 = (bf16[272,256]{1,0:T(8,128)(2,1)S(1)}, bf16[272,256]{1,0:T(8,128)(2,1)S(1)}, u32[]{:S(2)}, u32[]{:S(2)}) collective-permute-start(bf16[272,256]{1,0:T(8,128)(2,1)S(1)} %get-tuple-element.27.refs_3_), channel_id=1, source_target_pairs={{0,8},{4,12},{8,0},{12,4},{1,9},{5,13},{9,1},{13,5},{2,10},{6,14},... | collective-permute-start | bytes 417800 | tf_op jit(solution)/shard_map/ppermute | solution.py:26
  13.7 0.0 collective-permute-done.12
  13.7 0.0 copy-done.1
  13.7 0.5 %grad.1 = (bf16[256,256]{1,0:T(8,128)(2,1)S(1)}, bf16[256,256]{1,0:T(8,128)(2,1)S(1)}, f32[512,256]{1,0:T(8,128)S(1)}) custom-call(bf16[512,1024]{1,0:T(8,128)(2,1)S(1)} %bitcast.9, bf16[512,256]{1,0:T(8,128)(2,1)S(1)} %bitcast.12, bf16[272,256]{1,0:T(8,128)(2,1)S(1)} %get-tuple-element.26.refs_2_, bf16[272,256]{1,0:T(8,128)(2,1)S(1)} %get-tuple-element.27.refs_3_), custom_call_target="tpu_custom_call" | custom-call | tf_op jit(solution)/shard_map/grad/pallas_call | solution.py:351
  14.3 1.9 %collective-permute-start.13 = (bf16[256,256]{1,0:T(8,128)(2,1)S(1)}, bf16[256,256]{1,0:T(8,128)(2,1)S(1)}, u32[]{:S(2)}, u32[]{:S(2)}) collective-permute-start(bf16[256,256]{1,0:T(8,128)(2,1)S(1)} %get-tuple-element.34), channel_id=1, source_target_pairs={{0,4},{4,0},{8,12},{12,8},{1,5},{5,1},{9,13},{13,9},{2,6},{6,2},{1... | collective-permute-start | bytes 393224 | tf_op jit(solution)/shard_map/ppermute | solution.py:26
  16.2 0.0 collective-permute-done.refs_1_
  16.2 0.1 collective-permute-start.14
  16.3 0.0 collective-permute-done.1.refs_2_
  16.3 1.6 %collective-permute-done.4.refs_3_ = bf16[272,256]{1,0:T(8,128)(2,1)S(1)} collective-permute-done((bf16[272,256]{1,0:T(8,128)(2,1)S(1)}, bf16[272,256]{1,0:T(8,128)(2,1)S(1)}, u32[]{:S(2)}, u32[]{:S(2)}) %collective-permute-start.4) | collective-permute-done | bytes 139296 | tf_op jit(solution)/shard_map/ppermute | solution.py:26
  17.9 0.0 collective-permute-done.5.refs_4_
  17.9 0.0 copy-done.2
  17.9 0.4 %factor.1 = (bf16[272,256]{1,0:T(8,128)(2,1)S(1)}, bf16[288,256]{1,0:T(8,128)(2,1)S(1)}, f32[640,256]{1,0:T(8,128)S(1)}) custom-call(f32[1088,256]{1,0:T(8,128)S(1)} %get-tuple-element.22.refs_0_, bf16[272,256]{1,0:T(8,128)(2,1)S(1)} %collective-permute-done.refs_1_, bf16[272,256]{1,0:T(8,128)(2,1)S(1)} %collective-permute-done.1.refs_2_, ...), custom_call_target="tpu_custom_call" | custom-call | tf_op jit(solution)/shard_map/factor/pallas_call | solution.py:351
  18.3 2.3 %collective-permute-start.6 = (bf16[272,256]{1,0:T(8,128)(2,1)S(1)}, bf16[272,256]{1,0:T(8,128)(2,1)S(1)}, u32[]{:S(2)}, u32[]{:S(2)}) collective-permute-start(bf16[272,256]{1,0:T(8,128)(2,1)S(1)} %get-tuple-element.29.refs_2_.refs_3_), channel_id=1, source_target_pairs={{0,4},{4,0},{8,12},{12,8},{1,5},{5,1},{9,13},{13,9},{2,6},{6,2},{1... | collective-permute-start | bytes 417800 | tf_op jit(solution)/shard_map/ppermute | solution.py:26
  20.6 1.1 %collective-permute-start.9 = (bf16[288,256]{1,0:T(8,128)(2,1)S(1)}, bf16[288,256]{1,0:T(8,128)(2,1)S(1)}, u32[]{:S(2)}, u32[]{:S(2)}) collective-permute-start(bf16[288,256]{1,0:T(8,128)(2,1)S(1)} %get-tuple-element.30.refs_3_.refs_4_), channel_id=1, source_target_pairs={{0,8},{4,12},{8,0},{12,4},{1,9},{5,13},{9,1},{13,5},{2,10},{6,14},... | collective-permute-start | bytes 442376 | tf_op jit(solution)/shard_map/ppermute | solution.py:26
  21.7 0.9 %collective-permute-start.7 = (bf16[288,256]{1,0:T(8,128)(2,1)S(1)}, bf16[288,256]{1,0:T(8,128)(2,1)S(1)}, u32[]{:S(2)}, u32[]{:S(2)}) collective-permute-start(bf16[288,256]{1,0:T(8,128)(2,1)S(1)} %get-tuple-element.30.refs_3_.refs_4_), channel_id=1, source_target_pairs={{0,4},{4,0},{8,12},{12,8},{1,5},{5,1},{9,13},{13,9},{2,6},{6,2},{1... | collective-permute-start | bytes 442376 | tf_op jit(solution)/shard_map/ppermute | solution.py:26
  22.6 0.0 collective-permute-done.13.refs_1_
  22.6 0.1 collective-permute-start.8
  22.7 0.0 collective-permute-done.14.refs_2_
  22.7 2.0 %collective-permute-start.15 = (bf16[128,256]{1,0:T(8,128)(2,1)S(1)}, bf16[128,256]{1,0:T(8,128)(2,1)S(1)}, u32[]{:S(2)}, u32[]{:S(2)}) collective-permute-start(bf16[128,256]{1,0:T(8,128)(2,1)S(1)} %get-tuple-element.36), channel_id=1, source_target_pairs={{0,4},{4,0},{8,12},{12,8},{1,5},{5,1},{9,13},{13,9},{2,6},{6,2},{1... | collective-permute-start | bytes 196616 | tf_op jit(solution)/shard_map/ppermute | solution.py:26
  24.8 0.0 collective-permute-done.6.refs_4_.refs_5_
  24.8 1.5 %collective-permute-start.16 = (bf16[128,256]{1,0:T(8,128)(2,1)S(1)}, bf16[128,256]{1,0:T(8,128)(2,1)S(1)}, u32[]{:S(2)}, u32[]{:S(2)}) collective-permute-start(bf16[128,256]{1,0:T(8,128)(2,1)S(1)} %get-tuple-element.37), channel_id=1, source_target_pairs={{0,8},{4,12},{8,0},{12,4},{1,9},{5,13},{9,1},{13,5},{2,10},{6,14},... | collective-permute-start | bytes 196616 | tf_op jit(solution)/shard_map/ppermute | solution.py:26
  26.3 0.2 collective-permute-done.9.refs_7_.refs_6_
  26.5 0.7 %collective-permute-start.11 = (bf16[288,256]{1,0:T(8,128)(2,1)S(1)}, bf16[288,256]{1,0:T(8,128)(2,1)S(1)}, u32[]{:S(2)}, u32[]{:S(2)}) collective-permute-start(bf16[288,256]{1,0:T(8,128)(2,1)S(1)} %collective-permute-done.9.refs_7_.refs_6_), channel_id=1, source_target_pairs={{0,4},{4,0},{8,12},{12,8},{1,5},{5,1},{9,13},{13,9},{2,6},{6,2},{1... | collective-permute-start | bytes 442376 | tf_op jit(solution)/shard_map/ppermute | solution.py:26
  27.2 2.4 %collective-permute-done.15.refs_3_ = bf16[128,256]{1,0:T(8,128)(2,1)S(1)} collective-permute-done((bf16[128,256]{1,0:T(8,128)(2,1)S(1)}, bf16[128,256]{1,0:T(8,128)(2,1)S(1)}, u32[]{:S(2)}, u32[]{:S(2)}) %collective-permute-start.15) | collective-permute-done | bytes 65568 | tf_op jit(solution)/shard_map/ppermute | solution.py:26
  29.6 0.9 %collective-permute-start.10 = (bf16[272,256]{1,0:T(8,128)(2,1)S(1)}, bf16[272,256]{1,0:T(8,128)(2,1)S(1)}, u32[]{:S(2)}, u32[]{:S(2)}) collective-permute-start(bf16[272,256]{1,0:T(8,128)(2,1)S(1)} %collective-permute-done.6.refs_4_.refs_5_), channel_id=1, source_target_pairs={{0,8},{4,12},{8,0},{12,4},{1,9},{5,13},{9,1},{13,5},{2,10},{6,14},... | collective-permute-start | bytes 417800 | tf_op jit(solution)/shard_map/ppermute | solution.py:26
  30.6 0.0 collective-permute-done.16.refs_4_
  30.6 0.1 grad_total.1.refs_0_
  30.6 0.0 copy-start.3
  30.6 2.5 %collective-permute-start.17 = (bf16[256,256]{1,0:T(8,128)(2,1)S(1)}, bf16[256,256]{1,0:T(8,128)(2,1)S(1)}, u32[]{:S(2)}, u32[]{:S(2)}) collective-permute-start(bf16[256,256]{1,0:T(8,128)(2,1)S(1)} %grad_total.1.refs_0_), channel_id=1, source_target_pairs={{0,4},{4,0},{8,12},{12,8},{1,5},{5,1},{9,13},{13,9},{2,6},{6,2},{1... | collective-permute-start | bytes 393224 | tf_op jit(solution)/shard_map/ppermute | solution.py:26
  33.2 0.0 collective-permute-done.8.refs_6_
  33.2 0.2 collective-permute-start.18
  33.4 0.0 collective-permute-done.7.refs_5_
  33.4 1.3 %collective-permute-start.19 = (bf16[256,256]{1,0:T(8,128)(2,1)S(1)}, bf16[256,256]{1,0:T(8,128)(2,1)S(1)}, u32[]{:S(2)}, u32[]{:S(2)}) collective-permute-start(bf16[256,256]{1,0:T(8,128)(2,1)S(1)} %grad_total.1.refs_0_), channel_id=1, source_target_pairs={{0,12},{4,8},{8,4},{12,0},{1,13},{5,9},{9,5},{13,1},{2,14},{6,10},... | collective-permute-start | bytes 393224 | tf_op jit(solution)/shard_map/ppermute | solution.py:26
  35.4 0.0 collective-permute-done.10.refs_8_
  35.4 0.0 collective-permute-done.11.refs_9_
  35.4 3.8 %root.1 = (f32[256,1024]{1,0:T(8,128)}, bf16[256,1024]{1,0:T(8,128)(2,1)}, f32[8,128]{1,0:T(8,128)S(1)}) custom-call(s32[1,1]{1,0:T(1,128)S(6)} %copy.8.refs_0_, f32[640,256]{1,0:T(8,128)S(1)} %get-tuple-element.28.refs_1_, bf16[272,256]{1,0:T(8,128)(2,1)S(1)} %get-tuple-element.29.refs_2_.refs_3_, bf16[288,256]{1,0:T(8,128)(2,1)S(1)} %get-tuple-element.30.refs_3_.refs_4_, ...), custom_call_target="tpu_custom_call" | custom-call | tf_op jit(solution)/shard_map/root/pallas_call | solution.py:351
  39.2 0.0 collective-permute-done.17.refs_1_
  39.2 0.3 collective-permute-done.18.refs_2_
  39.5 0.0 collective-permute-done.19.refs_3_
  39.5 0.0 copy-done.3
  39.5 1.0 %step.1 = bf16[256,256]{1,0:T(8,128)(2,1)} custom-call(bf16[256,256]{1,0:T(8,128)(2,1)S(1)} %grad_total.1.refs_0_, bf16[256,256]{1,0:T(8,128)(2,1)S(1)} %collective-permute-done.17.refs_1_, bf16[256,256]{1,0:T(8,128)(2,1)S(1)} %collective-permute-done.18.refs_2_, bf16[256,256]{1,0:T(8,128)(2,1)S(1)} %collective-permute-done.19.refs_3_, ...), custom_call_target="tpu_custom_call" | custom-call | tf_op jit(solution)/shard_map/step/pallas_call | solution.py:351
  (1 shorter events, 0.0 us)
Async XLA Ops:
  0.6 13.1 %collective-permute-start.12 = (bf16[1,512,256]{2,1,0:T(8,128)(2,1)}, bf16[1,512,256]{2,1,0:T(8,128)(2,1)S(1)}, u32[]{:S(2)}, u32[]{:S(2)}) collective-permute-start(bf16[1,512,256]{2,1,0:T(8,128)(2,1)} %param.6), channel_id=1, source_target_pairs={{16,0},{0,16},{17,1},{1,17},{18,2},{2,18},{19,3},{3,19},{20,4},{4,... | collective-permute-start | bytes 786440 | tf_op jit(solution)/shard_map/ppermute | solution.py:22
  1.1 1.2 %copy-start = (bf16[1,512,1024]{2,1,0:T(8,128)(2,1)S(1)}, bf16[1,512,1024]{2,1,0:T(8,128)(2,1)}, u32[]{:S(2)}) copy-start(bf16[1,512,1024]{2,1,0:T(8,128)(2,1)} %param.5) | copy-start | bytes 3145732
  2.8 6.9 %collective-permute-start.2 = (bf16[272,256]{1,0:T(8,128)(2,1)S(1)}, bf16[272,256]{1,0:T(8,128)(2,1)S(1)}, u32[]{:S(2)}, u32[]{:S(2)}) collective-permute-start(bf16[272,256]{1,0:T(8,128)(2,1)S(1)} %get-tuple-element.21.refs_1_), channel_id=1, source_target_pairs={{0,4},{4,0},{8,12},{12,8},{1,5},{5,1},{9,13},{13,9},{2,6},{6,2},{1... | collective-permute-start | bytes 417800 | tf_op jit(solution)/shard_map/ppermute | solution.py:26
  5.4 8.3 %copy-start.1 = (bf16[1,512,1024]{2,1,0:T(8,128)(2,1)S(1)}, bf16[1,512,1024]{2,1,0:T(8,128)(2,1)}, u32[]{:S(2)}) copy-start(bf16[1,512,1024]{2,1,0:T(8,128)(2,1)} %param.5) | copy-start | bytes 3145732
  5.4 6.1 %collective-permute-start.3 = (bf16[272,256]{1,0:T(8,128)(2,1)S(1)}, bf16[272,256]{1,0:T(8,128)(2,1)S(1)}, u32[]{:S(2)}, u32[]{:S(2)}) collective-permute-start(bf16[272,256]{1,0:T(8,128)(2,1)S(1)} %get-tuple-element.25), channel_id=1, source_target_pairs={{0,8},{4,12},{8,0},{12,4},{1,9},{5,13},{9,1},{13,5},{2,10},{6,14},... | collective-permute-start | bytes 417800 | tf_op jit(solution)/shard_map/ppermute | solution.py:26
  8.0 8.2 %collective-permute-start = (bf16[272,256]{1,0:T(8,128)(2,1)S(1)}, bf16[272,256]{1,0:T(8,128)(2,1)S(1)}, u32[]{:S(2)}, u32[]{:S(2)}) collective-permute-start(bf16[272,256]{1,0:T(8,128)(2,1)S(1)} %get-tuple-element.23), channel_id=1, source_target_pairs={{0,4},{4,0},{8,12},{12,8},{1,5},{5,1},{9,13},{13,9},{2,6},{6,2},{1... | collective-permute-start | bytes 417800 | tf_op jit(solution)/shard_map/ppermute | solution.py:26
  8.6 7.7 %collective-permute-start.1 = (bf16[272,256]{1,0:T(8,128)(2,1)S(1)}, bf16[272,256]{1,0:T(8,128)(2,1)S(1)}, u32[]{:S(2)}, u32[]{:S(2)}) collective-permute-start(bf16[272,256]{1,0:T(8,128)(2,1)S(1)} %get-tuple-element.24), channel_id=1, source_target_pairs={{0,8},{4,12},{8,0},{12,4},{1,9},{5,13},{9,1},{13,5},{2,10},{6,14},... | collective-permute-start | bytes 417800 | tf_op jit(solution)/shard_map/ppermute | solution.py:26
  11.5 6.3 %copy-start.2 = (f32[1,1,256,1024]{3,2,1,0:T(8,128)S(1)}, f32[1,1,256,1024]{3,2,1,0:T(8,128)}, u32[]{:S(2)}) copy-start(f32[1,1,256,1024]{3,2,1,0:T(8,128)} %param.7) | copy-start | bytes 3145732
  11.6 6.3 %collective-permute-start.4 = (bf16[272,256]{1,0:T(8,128)(2,1)S(1)}, bf16[272,256]{1,0:T(8,128)(2,1)S(1)}, u32[]{:S(2)}, u32[]{:S(2)}) collective-permute-start(bf16[272,256]{1,0:T(8,128)(2,1)S(1)} %get-tuple-element.26.refs_2_), channel_id=1, source_target_pairs={{0,4},{4,0},{8,12},{12,8},{1,5},{5,1},{9,13},{13,9},{2,6},{6,2},{1... | collective-permute-start | bytes 417800 | tf_op jit(solution)/shard_map/ppermute | solution.py:26
  11.9 6.0 %collective-permute-start.5 = (bf16[272,256]{1,0:T(8,128)(2,1)S(1)}, bf16[272,256]{1,0:T(8,128)(2,1)S(1)}, u32[]{:S(2)}, u32[]{:S(2)}) collective-permute-start(bf16[272,256]{1,0:T(8,128)(2,1)S(1)} %get-tuple-element.27.refs_3_), channel_id=1, source_target_pairs={{0,8},{4,12},{8,0},{12,4},{1,9},{5,13},{9,1},{13,5},{2,10},{6,14},... | collective-permute-start | bytes 417800 | tf_op jit(solution)/shard_map/ppermute | solution.py:26
  14.3 8.3 %collective-permute-start.13 = (bf16[256,256]{1,0:T(8,128)(2,1)S(1)}, bf16[256,256]{1,0:T(8,128)(2,1)S(1)}, u32[]{:S(2)}, u32[]{:S(2)}) collective-permute-start(bf16[256,256]{1,0:T(8,128)(2,1)S(1)} %get-tuple-element.34), channel_id=1, source_target_pairs={{0,4},{4,0},{8,12},{12,8},{1,5},{5,1},{9,13},{13,9},{2,6},{6,2},{1... | collective-permute-start | bytes 393224 | tf_op jit(solution)/shard_map/ppermute | solution.py:26
  16.2 6.5 %collective-permute-start.14 = (bf16[256,256]{1,0:T(8,128)(2,1)S(1)}, bf16[256,256]{1,0:T(8,128)(2,1)S(1)}, u32[]{:S(2)}, u32[]{:S(2)}) collective-permute-start(bf16[256,256]{1,0:T(8,128)(2,1)S(1)} %get-tuple-element.35), channel_id=1, source_target_pairs={{0,8},{4,12},{8,0},{12,4},{1,9},{5,13},{9,1},{13,5},{2,10},{6,14},... | collective-permute-start | bytes 393224 | tf_op jit(solution)/shard_map/ppermute | solution.py:26
  18.3 6.5 %collective-permute-start.6 = (bf16[272,256]{1,0:T(8,128)(2,1)S(1)}, bf16[272,256]{1,0:T(8,128)(2,1)S(1)}, u32[]{:S(2)}, u32[]{:S(2)}) collective-permute-start(bf16[272,256]{1,0:T(8,128)(2,1)S(1)} %get-tuple-element.29.refs_2_.refs_3_), channel_id=1, source_target_pairs={{0,4},{4,0},{8,12},{12,8},{1,5},{5,1},{9,13},{13,9},{2,6},{6,2},{1... | collective-permute-start | bytes 417800 | tf_op jit(solution)/shard_map/ppermute | solution.py:26
  20.6 5.9 %collective-permute-start.9 = (bf16[288,256]{1,0:T(8,128)(2,1)S(1)}, bf16[288,256]{1,0:T(8,128)(2,1)S(1)}, u32[]{:S(2)}, u32[]{:S(2)}) collective-permute-start(bf16[288,256]{1,0:T(8,128)(2,1)S(1)} %get-tuple-element.30.refs_3_.refs_4_), channel_id=1, source_target_pairs={{0,8},{4,12},{8,0},{12,4},{1,9},{5,13},{9,1},{13,5},{2,10},{6,14},... | collective-permute-start | bytes 442376 | tf_op jit(solution)/shard_map/ppermute | solution.py:26
  21.7 11.7 %collective-permute-start.7 = (bf16[288,256]{1,0:T(8,128)(2,1)S(1)}, bf16[288,256]{1,0:T(8,128)(2,1)S(1)}, u32[]{:S(2)}, u32[]{:S(2)}) collective-permute-start(bf16[288,256]{1,0:T(8,128)(2,1)S(1)} %get-tuple-element.30.refs_3_.refs_4_), channel_id=1, source_target_pairs={{0,4},{4,0},{8,12},{12,8},{1,5},{5,1},{9,13},{13,9},{2,6},{6,2},{1... | collective-permute-start | bytes 442376 | tf_op jit(solution)/shard_map/ppermute | solution.py:26
  22.6 10.6 %collective-permute-start.8 = (bf16[272,256]{1,0:T(8,128)(2,1)S(1)}, bf16[272,256]{1,0:T(8,128)(2,1)S(1)}, u32[]{:S(2)}, u32[]{:S(2)}) collective-permute-start(bf16[272,256]{1,0:T(8,128)(2,1)S(1)} %get-tuple-element.29.refs_2_.refs_3_), channel_id=1, source_target_pairs={{0,8},{4,12},{8,0},{12,4},{1,9},{5,13},{9,1},{13,5},{2,10},{6,14},... | collective-permute-start | bytes 417800 | tf_op jit(solution)/shard_map/ppermute | solution.py:26
  22.7 6.9 %collective-permute-start.15 = (bf16[128,256]{1,0:T(8,128)(2,1)S(1)}, bf16[128,256]{1,0:T(8,128)(2,1)S(1)}, u32[]{:S(2)}, u32[]{:S(2)}) collective-permute-start(bf16[128,256]{1,0:T(8,128)(2,1)S(1)} %get-tuple-element.36), channel_id=1, source_target_pairs={{0,4},{4,0},{8,12},{12,8},{1,5},{5,1},{9,13},{13,9},{2,6},{6,2},{1... | collective-permute-start | bytes 196616 | tf_op jit(solution)/shard_map/ppermute | solution.py:26
  24.8 5.8 %collective-permute-start.16 = (bf16[128,256]{1,0:T(8,128)(2,1)S(1)}, bf16[128,256]{1,0:T(8,128)(2,1)S(1)}, u32[]{:S(2)}, u32[]{:S(2)}) collective-permute-start(bf16[128,256]{1,0:T(8,128)(2,1)S(1)} %get-tuple-element.37), channel_id=1, source_target_pairs={{0,8},{4,12},{8,0},{12,4},{1,9},{5,13},{9,1},{13,5},{2,10},{6,14},... | collective-permute-start | bytes 196616 | tf_op jit(solution)/shard_map/ppermute | solution.py:26
  26.5 8.9 %collective-permute-start.11 = (bf16[288,256]{1,0:T(8,128)(2,1)S(1)}, bf16[288,256]{1,0:T(8,128)(2,1)S(1)}, u32[]{:S(2)}, u32[]{:S(2)}) collective-permute-start(bf16[288,256]{1,0:T(8,128)(2,1)S(1)} %collective-permute-done.9.refs_7_.refs_6_), channel_id=1, source_target_pairs={{0,4},{4,0},{8,12},{12,8},{1,5},{5,1},{9,13},{13,9},{2,6},{6,2},{1... | collective-permute-start | bytes 442376 | tf_op jit(solution)/shard_map/ppermute | solution.py:26
  29.6 5.7 %collective-permute-start.10 = (bf16[272,256]{1,0:T(8,128)(2,1)S(1)}, bf16[272,256]{1,0:T(8,128)(2,1)S(1)}, u32[]{:S(2)}, u32[]{:S(2)}) collective-permute-start(bf16[272,256]{1,0:T(8,128)(2,1)S(1)} %collective-permute-done.6.refs_4_.refs_5_), channel_id=1, source_target_pairs={{0,8},{4,12},{8,0},{12,4},{1,9},{5,13},{9,1},{13,5},{2,10},{6,14},... | collective-permute-start | bytes 417800 | tf_op jit(solution)/shard_map/ppermute | solution.py:26
  30.6 8.9 %copy-start.3 = (bf16[1,1,256,1024]{3,2,1,0:T(8,128)(2,1)S(1)}, bf16[1,1,256,1024]{3,2,1,0:T(8,128)(2,1)}, u32[]{:S(2)}) copy-start(bf16[1,1,256,1024]{3,2,1,0:T(8,128)(2,1)} %param.8) | copy-start | bytes 1572868
  30.6 8.6 %collective-permute-start.17 = (bf16[256,256]{1,0:T(8,128)(2,1)S(1)}, bf16[256,256]{1,0:T(8,128)(2,1)S(1)}, u32[]{:S(2)}, u32[]{:S(2)}) collective-permute-start(bf16[256,256]{1,0:T(8,128)(2,1)S(1)} %grad_total.1.refs_0_), channel_id=1, source_target_pairs={{0,4},{4,0},{8,12},{12,8},{1,5},{5,1},{9,13},{13,9},{2,6},{6,2},{1... | collective-permute-start | bytes 393224 | tf_op jit(solution)/shard_map/ppermute | solution.py:26
  33.2 6.4 %collective-permute-start.18 = (bf16[256,256]{1,0:T(8,128)(2,1)S(1)}, bf16[256,256]{1,0:T(8,128)(2,1)S(1)}, u32[]{:S(2)}, u32[]{:S(2)}) collective-permute-start(bf16[256,256]{1,0:T(8,128)(2,1)S(1)} %grad_total.1.refs_0_), channel_id=1, source_target_pairs={{0,8},{4,12},{8,0},{12,4},{1,9},{5,13},{9,1},{13,5},{2,10},{6,14},... | collective-permute-start | bytes 393224 | tf_op jit(solution)/shard_map/ppermute | solution.py:26
  33.4 6.1 %collective-permute-start.19 = (bf16[256,256]{1,0:T(8,128)(2,1)S(1)}, bf16[256,256]{1,0:T(8,128)(2,1)S(1)}, u32[]{:S(2)}, u32[]{:S(2)}) collective-permute-start(bf16[256,256]{1,0:T(8,128)(2,1)S(1)} %grad_total.1.refs_0_), channel_id=1, source_target_pairs={{0,12},{4,8},{8,4},{12,0},{1,13},{5,9},{9,5},{13,1},{2,14},{6,10},... | collective-permute-start | bytes 393224 | tf_op jit(solution)/shard_map/ppermute | solution.py:26

commit v18 on v17

--- a/solution.py
+++ b/solution.py
@@ -37,7 +37,7 @@
 
 
 def transposed(block):
-    return block.astype(F32).T.astype(block.dtype)
+    return block.T
 
 
 OFFSETS = (0, 1, 2, 3)
@@ -146,7 +146,8 @@
     store_chunk(pieces(0), length, (keep, 0), (keep, length))
 
 
-def grad_kernel(replicas, tokens_all, acts, grads, send_x, send_y, keep, total):
+def grad_kernel(replicas, tokens_all, acts, grads, old_root, send_x, send_y, keep, old_columns, total):
+    old_columns[...] = old_root[...].T
     order = acts.shape[1]
     share = order // replicas
     strip = grads.shape[1] // replicas
@@ -307,8 +308,8 @@
 
 def step_kernel(replicas, *refs):
     chunks = refs[:replicas]
-    old_root, step_out, grads, result = refs[replicas:]
-    share = old_root.shape[0]
+    old_columns, step_out, grads, result = refs[replicas:]
+    share = old_columns.shape[1]
     strip = step_out.shape[0] // replicas
     mine = lax.axis_index("dp")
     for offset, chunk in enumerate(chunks):
@@ -316,9 +317,7 @@
             grads[offset * strip : (offset + 1) * strip, part * share : (part + 1) * share] = chunk[
                 part * strip : (part + 1) * strip, :
             ]
-    result[...] = lax.dot_general(
-        grads[...], old_root[...], (((1,), (1,)), ((), ())), preferred_element_type=F32
-    ).astype(BF16)
+    result[...] = jnp.dot(grads[...], old_columns[...], preferred_element_type=F32).astype(BF16)
     for position, offset in enumerate(OFFSETS):
         rows = pl.ds(pl.multiple_of((mine ^ offset) * strip, strip), strip)
         step_out[rows, :] = result[position * strip : (position + 1) * strip, :]
@@ -373,12 +372,13 @@
     relay_x, relay_y = swapped(relay_x, 1), swapped(relay_y, 2)
     direct_x, direct_y = swapped(direct_x, 1), swapped(direct_y, 2)
     relay_x, relay_y = call(relay_kernel, [shape(length)] * 2, "relay", keep, relay_x, relay_y)
-    grad_x, grad_y, grad_keep = call(
+    grad_x, grad_y, grad_keep, old_columns = call(
         functools.partial(grad_kernel, replicas, tokens * replicas),
-        [shape(grows)] * 2 + [shape(2 * grows, F32)],
+        [shape(grows)] * 2 + [shape(2 * grows, F32), shape(order)],
         "grad",
         inputs,
         received,
+        old_root[0, 0],
         after=[relay_x, relay_y],
         scratch=[pltpu.VMEM((grows, order), F32)],
     )
@@ -442,7 +442,7 @@
         [shape(grows, BF16, share)],
         "step",
         *strips,
-        old_root[0, 0],
+        old_columns,
         after=[finished],
         scratch=[pltpu.VMEM((grows, order), BF16), pltpu.VMEM((grows, share), BF16)],
     )

time: 40.7 us -> 41.2 us (1.012)
  waiting for transfers between devices: 7.4 us -> 8.85 us
  starting transfers between devices: 23.1 us -> 22.2 us
    ppermute x19, waiting for transfers between devices: 7.4 us -> 8.85 us  [swapped(): lax.ppermute(block, 'dp', [(i, i ^ offset) for i in range(lax.axis_size('...]
    ppermute x19, starting transfers between devices: 22.6 us -> 21.7 us  [swapped(): lax.ppermute(block, 'dp', [(i, i ^ offset) for i in range(lax.axis_size('...]
  transfers between devices with their start and end apart: 20 -> 20, of which waited for: 6 -> 8; matrix products, arithmetic and copies ran while one was open for 0% -> 0% of each run, Pallas kernels for 16% -> 16%
where the time goes in v18:
time: 41.2 us; the launch traced here: 41 us
  starting transfers between devices  22.2 us (54%)
  waiting for transfers between devices  8.85 us (21%)
  Pallas kernels  7.33 us (18%)
  between operations  1.39 us (3%)
  local copies, waits for them, and re-layouts  1.24 us (3%)
    ppermute x19, starting transfers between devices, swapped(): lax.ppermute(block, 'dp', [(i, i ^ offset) for i in range(lax.axis_size('...  21.7 us
    ppermute x19, waiting for transfers between devices, swapped(): lax.ppermute(block, 'dp', [(i, i ^ offset) for i in range(lax.axis_size('...  8.85 us
    pallas_call x9, Pallas kernels, call(): pl.pallas_call(body, out_shape=outs, in_specs=in_specs, out_specs=out_spe...  7.33 us
    unnamed x8, local copies, waits for them, and re-layouts  1.24 us
  transfers between devices with their start and end apart: 20, of which 8 were waited for; matrix products, arithmetic and copies ran while one was open for 0% of the time, Pallas kernels for 16%

profile of v18, /device:TPU:0, one launch (start us, length us, event | category | flops | bytes accessed | tf_op | source)
XLA Modules:
  0.0 41.0 jit_solution(4340076673428266728)
XLA Ops:
  0.6 0.5 %collective-permute-start.12 = (bf16[1,512,256]{2,1,0:T(8,128)(2,1)}, bf16[1,512,256]{2,1,0:T(8,128)(2,1)S(1)}, u32[]{:S(2)}, u32[]{:S(2)}) collective-permute-start(bf16[1,512,256]{2,1,0:T(8,128)(2,1)} %param.6), channel_id=1, source_target_pairs={{16,0},{0,16},{17,1},{1,17},{18,2},{2,18},{19,3},{3,19},{20,4},{4,... | collective-permute-start | bytes 786440 | tf_op jit(solution)/shard_map/ppermute | solution.py:22
  1.1 0.0 copy-start
  1.1 1.2 %copy-done = bf16[1,512,1024]{2,1,0:T(8,128)(2,1)S(1)} copy-done((bf16[1,512,1024]{2,1,0:T(8,128)(2,1)S(1)}, bf16[1,512,1024]{2,1,0:T(8,128)(2,1)}, u32[]{:S(2)}) %copy-start) | copy-done | bytes 1048600
  2.4 0.5 %across.1 = (bf16[272,256]{1,0:T(8,128)(2,1)S(1)}, bf16[272,256]{1,0:T(8,128)(2,1)S(1)}) custom-call(bf16[512,1024]{1,0:T(8,128)(2,1)S(1)} %bitcast.7), custom_call_target="tpu_custom_call" | custom-call | tf_op jit(solution)/shard_map/across/pallas_call | solution.py:350
  2.8 2.6 %collective-permute-start.3 = (bf16[272,256]{1,0:T(8,128)(2,1)S(1)}, bf16[272,256]{1,0:T(8,128)(2,1)S(1)}, u32[]{:S(2)}, u32[]{:S(2)}) collective-permute-start(bf16[272,256]{1,0:T(8,128)(2,1)S(1)} %get-tuple-element.26), channel_id=1, source_target_pairs={{0,8},{4,12},{8,0},{12,4},{1,9},{5,13},{9,1},{13,5},{2,10},{6,14},... | collective-permute-start | bytes 417800 | tf_op jit(solution)/shard_map/ppermute | solution.py:26
  5.4 0.0 copy-start.1
  5.4 0.0 copy-start.3
  5.4 1.5 %collective-permute-start.2 = (bf16[272,256]{1,0:T(8,128)(2,1)S(1)}, bf16[272,256]{1,0:T(8,128)(2,1)S(1)}, u32[]{:S(2)}, u32[]{:S(2)}) collective-permute-start(bf16[272,256]{1,0:T(8,128)(2,1)S(1)} %get-tuple-element.22.refs_1_), channel_id=1, source_target_pairs={{0,4},{4,0},{8,12},{12,8},{1,5},{5,1},{9,13},{13,9},{2,6},{6,2},{1... | collective-permute-start | bytes 417800 | tf_op jit(solution)/shard_map/ppermute | solution.py:26
  6.9 1.1 %batch.1 = (bf16[272,256]{1,0:T(8,128)(2,1)S(1)}, bf16[272,256]{1,0:T(8,128)(2,1)S(1)}, f32[1088,256]{1,0:T(8,128)S(1)}) custom-call(bf16[512,1024]{1,0:T(8,128)(2,1)S(1)} %bitcast.8, bf16[272,256]{1,0:T(8,128)(2,1)S(1)} %get-tuple-element.22.refs_1_), custom_call_target="tpu_custom_call" | custom-call | tf_op jit(solution)/shard_map/batch/pallas_call | solution.py:350
  8.0 0.6 %collective-permute-start = (bf16[272,256]{1,0:T(8,128)(2,1)S(1)}, bf16[272,256]{1,0:T(8,128)(2,1)S(1)}, u32[]{:S(2)}, u32[]{:S(2)}) collective-permute-start(bf16[272,256]{1,0:T(8,128)(2,1)S(1)} %get-tuple-element.24), channel_id=1, source_target_pairs={{0,4},{4,0},{8,12},{12,8},{1,5},{5,1},{9,13},{13,9},{2,6},{6,2},{1... | collective-permute-start | bytes 417800 | tf_op jit(solution)/shard_map/ppermute | solution.py:26
  8.6 0.1 collective-permute-start.1
  8.7 1.1 %collective-permute-done.3.refs_2_ = bf16[272,256]{1,0:T(8,128)(2,1)S(1)} collective-permute-done((bf16[272,256]{1,0:T(8,128)(2,1)S(1)}, bf16[272,256]{1,0:T(8,128)(2,1)S(1)}, u32[]{:S(2)}, u32[]{:S(2)}) %collective-permute-start.3) | collective-permute-done | bytes 139296 | tf_op jit(solution)/shard_map/ppermute | solution.py:26
  9.8 2.0 %collective-permute-done.2.refs_1_ = bf16[272,256]{1,0:T(8,128)(2,1)S(1)} collective-permute-done((bf16[272,256]{1,0:T(8,128)(2,1)S(1)}, bf16[272,256]{1,0:T(8,128)(2,1)S(1)}, u32[]{:S(2)}, u32[]{:S(2)}) %collective-permute-start.2) | collective-permute-done | bytes 139296 | tf_op jit(solution)/shard_map/ppermute | solution.py:26
  11.8 0.1 relay.1
  11.9 0.0 copy-start.2
  11.9 1.7 %collective-permute-start.4 = (bf16[272,256]{1,0:T(8,128)(2,1)S(1)}, bf16[272,256]{1,0:T(8,128)(2,1)S(1)}, u32[]{:S(2)}, u32[]{:S(2)}) collective-permute-start(bf16[272,256]{1,0:T(8,128)(2,1)S(1)} %get-tuple-element.27.refs_3_), channel_id=1, source_target_pairs={{0,4},{4,0},{8,12},{12,8},{1,5},{5,1},{9,13},{13,9},{2,6},{6,2},{1... | collective-permute-start | bytes 417800 | tf_op jit(solution)/shard_map/ppermute | solution.py:26
  13.6 0.5 %collective-permute-start.5 = (bf16[272,256]{1,0:T(8,128)(2,1)S(1)}, bf16[272,256]{1,0:T(8,128)(2,1)S(1)}, u32[]{:S(2)}, u32[]{:S(2)}) collective-permute-start(bf16[272,256]{1,0:T(8,128)(2,1)S(1)} %get-tuple-element.28.refs_4_), channel_id=1, source_target_pairs={{0,8},{4,12},{8,0},{12,4},{1,9},{5,13},{9,1},{13,5},{2,10},{6,14},... | collective-permute-start | bytes 417800 | tf_op jit(solution)/shard_map/ppermute | solution.py:26
  14.1 0.0 collective-permute-done.12
  14.1 0.0 copy-done.1
  14.1 0.0 copy-done.3
  14.1 0.5 %grad.1 = (bf16[256,256]{1,0:T(8,128)(2,1)S(1)}, bf16[256,256]{1,0:T(8,128)(2,1)S(1)}, f32[512,256]{1,0:T(8,128)S(1)}, bf16[1024,256]{1,0:T(8,128)(2,1)S(1)}) custom-call(bf16[512,1024]{1,0:T(8,128)(2,1)S(1)} %bitcast.9, bf16[512,256]{1,0:T(8,128)(2,1)S(1)} %bitcast.12, bf16[256,1024]{1,0:T(8,128)(2,1)S(1)} %bitcast.11, ...), custom_call_target="tpu_custom_call" | custom-call | tf_op jit(solution)/shard_map/grad/pallas_call | solution.py:350
  14.6 0.2 collective-permute-start.13
  14.8 0.0 collective-permute-done.refs_1_
  14.8 1.8 %collective-permute-start.14 = (bf16[256,256]{1,0:T(8,128)(2,1)S(1)}, bf16[256,256]{1,0:T(8,128)(2,1)S(1)}, u32[]{:S(2)}, u32[]{:S(2)}) collective-permute-start(bf16[256,256]{1,0:T(8,128)(2,1)S(1)} %get-tuple-element.36), channel_id=1, source_target_pairs={{0,8},{4,12},{8,0},{12,4},{1,9},{5,13},{9,1},{13,5},{2,10},{6,14},... | collective-permute-start | bytes 393224 | tf_op jit(solution)/shard_map/ppermute | solution.py:26
  16.6 0.0 collective-permute-done.1.refs_2_
  16.6 1.9 %collective-permute-done.4.refs_3_ = bf16[272,256]{1,0:T(8,128)(2,1)S(1)} collective-permute-done((bf16[272,256]{1,0:T(8,128)(2,1)S(1)}, bf16[272,256]{1,0:T(8,128)(2,1)S(1)}, u32[]{:S(2)}, u32[]{:S(2)}) %collective-permute-start.4) | collective-permute-done | bytes 139296 | tf_op jit(solution)/shard_map/ppermute | solution.py:26
  18.5 0.7 %collective-permute-done.5.refs_4_ = bf16[272,256]{1,0:T(8,128)(2,1)S(1)} collective-permute-done((bf16[272,256]{1,0:T(8,128)(2,1)S(1)}, bf16[272,256]{1,0:T(8,128)(2,1)S(1)}, u32[]{:S(2)}, u32[]{:S(2)}) %collective-permute-start.5) | collective-permute-done | bytes 139296 | tf_op jit(solution)/shard_map/ppermute | solution.py:26
  19.2 0.0 copy-done.2
  19.2 0.4 %factor.1 = (bf16[272,256]{1,0:T(8,128)(2,1)S(1)}, bf16[288,256]{1,0:T(8,128)(2,1)S(1)}, f32[640,256]{1,0:T(8,128)S(1)}) custom-call(f32[1088,256]{1,0:T(8,128)S(1)} %get-tuple-element.23.refs_0_, bf16[272,256]{1,0:T(8,128)(2,1)S(1)} %collective-permute-done.refs_1_, bf16[272,256]{1,0:T(8,128)(2,1)S(1)} %collective-permute-done.1.refs_2_, ...), custom_call_target="tpu_custom_call" | custom-call | tf_op jit(solution)/shard_map/factor/pallas_call | solution.py:350
  19.7 1.2 %collective-permute-start.6 = (bf16[272,256]{1,0:T(8,128)(2,1)S(1)}, bf16[272,256]{1,0:T(8,128)(2,1)S(1)}, u32[]{:S(2)}, u32[]{:S(2)}) collective-permute-start(bf16[272,256]{1,0:T(8,128)(2,1)S(1)} %get-tuple-element.30.refs_2_.refs_3_), channel_id=1, source_target_pairs={{0,4},{4,0},{8,12},{12,8},{1,5},{5,1},{9,13},{13,9},{2,6},{6,2},{1... | collective-permute-start | bytes 417800 | tf_op jit(solution)/shard_map/ppermute | solution.py:26
  20.8 0.3 collective-permute-start.9
  21.1 1.5 %collective-permute-start.7 = (bf16[288,256]{1,0:T(8,128)(2,1)S(1)}, bf16[288,256]{1,0:T(8,128)(2,1)S(1)}, u32[]{:S(2)}, u32[]{:S(2)}) collective-permute-start(bf16[288,256]{1,0:T(8,128)(2,1)S(1)} %get-tuple-element.31.refs_3_.refs_4_), channel_id=1, source_target_pairs={{0,4},{4,0},{8,12},{12,8},{1,5},{5,1},{9,13},{13,9},{2,6},{6,2},{1... | collective-permute-start | bytes 442376 | tf_op jit(solution)/shard_map/ppermute | solution.py:26
  22.6 0.0 collective-permute-done.13.refs_1_
  22.6 1.2 %collective-permute-start.8 = (bf16[272,256]{1,0:T(8,128)(2,1)S(1)}, bf16[272,256]{1,0:T(8,128)(2,1)S(1)}, u32[]{:S(2)}, u32[]{:S(2)}) collective-permute-start(bf16[272,256]{1,0:T(8,128)(2,1)S(1)} %get-tuple-element.30.refs_2_.refs_3_), channel_id=1, source_target_pairs={{0,8},{4,12},{8,0},{12,4},{1,9},{5,13},{9,1},{13,5},{2,10},{6,14},... | collective-permute-start | bytes 417800 | tf_op jit(solution)/shard_map/ppermute | solution.py:26
  23.8 0.0 collective-permute-done.14.refs_2_
  23.8 1.2 %collective-permute-start.15 = (bf16[128,256]{1,0:T(8,128)(2,1)S(1)}, bf16[128,256]{1,0:T(8,128)(2,1)S(1)}, u32[]{:S(2)}, u32[]{:S(2)}) collective-permute-start(bf16[128,256]{1,0:T(8,128)(2,1)S(1)} %get-tuple-element.37), channel_id=1, source_target_pairs={{0,4},{4,0},{8,12},{12,8},{1,5},{5,1},{9,13},{13,9},{2,6},{6,2},{1... | collective-permute-start | bytes 196616 | tf_op jit(solution)/shard_map/ppermute | solution.py:26
  25.0 0.4 collective-permute-done.6.refs_4_.refs_5_
  25.4 1.6 %collective-permute-start.16 = (bf16[128,256]{1,0:T(8,128)(2,1)S(1)}, bf16[128,256]{1,0:T(8,128)(2,1)S(1)}, u32[]{:S(2)}, u32[]{:S(2)}) collective-permute-start(bf16[128,256]{1,0:T(8,128)(2,1)S(1)} %get-tuple-element.38), channel_id=1, source_target_pairs={{0,8},{4,12},{8,0},{12,4},{1,9},{5,13},{9,1},{13,5},{2,10},{6,14},... | collective-permute-start | bytes 196616 | tf_op jit(solution)/shard_map/ppermute | solution.py:26
  26.9 0.0 collective-permute-done.9.refs_7_.refs_6_
  26.9 0.7 %collective-permute-start.11 = (bf16[288,256]{1,0:T(8,128)(2,1)S(1)}, bf16[288,256]{1,0:T(8,128)(2,1)S(1)}, u32[]{:S(2)}, u32[]{:S(2)}) collective-permute-start(bf16[288,256]{1,0:T(8,128)(2,1)S(1)} %collective-permute-done.9.refs_7_.refs_6_), channel_id=1, source_target_pairs={{0,4},{4,0},{8,12},{12,8},{1,5},{5,1},{9,13},{13,9},{2,6},{6,2},{1... | collective-permute-start | bytes 442376 | tf_op jit(solution)/shard_map/ppermute | solution.py:26
  27.6 1.6 %collective-permute-done.15.refs_3_ = bf16[128,256]{1,0:T(8,128)(2,1)S(1)} collective-permute-done((bf16[128,256]{1,0:T(8,128)(2,1)S(1)}, bf16[128,256]{1,0:T(8,128)(2,1)S(1)}, u32[]{:S(2)}, u32[]{:S(2)}) %collective-permute-start.15) | collective-permute-done | bytes 65568 | tf_op jit(solution)/shard_map/ppermute | solution.py:26
  29.2 1.6 %collective-permute-start.10 = (bf16[272,256]{1,0:T(8,128)(2,1)S(1)}, bf16[272,256]{1,0:T(8,128)(2,1)S(1)}, u32[]{:S(2)}, u32[]{:S(2)}) collective-permute-start(bf16[272,256]{1,0:T(8,128)(2,1)S(1)} %collective-permute-done.6.refs_4_.refs_5_), channel_id=1, source_target_pairs={{0,8},{4,12},{8,0},{12,4},{1,9},{5,13},{9,1},{13,5},{2,10},{6,14},... | collective-permute-start | bytes 417800 | tf_op jit(solution)/shard_map/ppermute | solution.py:26
  30.8 1.0 %collective-permute-done.16.refs_4_ = bf16[128,256]{1,0:T(8,128)(2,1)S(1)} collective-permute-done((bf16[128,256]{1,0:T(8,128)(2,1)S(1)}, bf16[128,256]{1,0:T(8,128)(2,1)S(1)}, u32[]{:S(2)}, u32[]{:S(2)}) %collective-permute-start.16) | collective-permute-done | bytes 65568 | tf_op jit(solution)/shard_map/ppermute | solution.py:26
  31.9 1.1 %collective-permute-start.19 = (bf16[256,256]{1,0:T(8,128)(2,1)S(1)}, bf16[256,256]{1,0:T(8,128)(2,1)S(1)}, u32[]{:S(2)}, u32[]{:S(2)}) collective-permute-start(bf16[256,256]{1,0:T(8,128)(2,1)S(1)} %grad_total.1.refs_0_), channel_id=1, source_target_pairs={{0,12},{4,8},{8,4},{12,0},{1,13},{5,9},{9,5},{13,1},{2,14},{6,10},... | collective-permute-start | bytes 393224 | tf_op jit(solution)/shard_map/ppermute | solution.py:26
  33.0 0.0 collective-permute-done.8.refs_6_
  33.0 2.1 %collective-permute-start.18 = (bf16[256,256]{1,0:T(8,128)(2,1)S(1)}, bf16[256,256]{1,0:T(8,128)(2,1)S(1)}, u32[]{:S(2)}, u32[]{:S(2)}) collective-permute-start(bf16[256,256]{1,0:T(8,128)(2,1)S(1)} %grad_total.1.refs_0_), channel_id=1, source_target_pairs={{0,8},{4,12},{8,0},{12,4},{1,9},{5,13},{9,1},{13,5},{2,10},{6,14},... | collective-permute-start | bytes 393224 | tf_op jit(solution)/shard_map/ppermute | solution.py:26
  35.1 0.0 collective-permute-done.7.refs_5_
  35.1 0.4 collective-permute-start.17
  36.1 0.0 collective-permute-done.10.refs_8_
  36.1 0.0 collective-permute-done.11.refs_9_
  36.1 3.8 %root.1 = (f32[256,1024]{1,0:T(8,128)}, bf16[256,1024]{1,0:T(8,128)(2,1)}, f32[8,128]{1,0:T(8,128)S(1)}) custom-call(s32[1,1]{1,0:T(1,128)S(6)} %copy.8.refs_0_, f32[640,256]{1,0:T(8,128)S(1)} %get-tuple-element.29.refs_1_, bf16[272,256]{1,0:T(8,128)(2,1)S(1)} %get-tuple-element.30.refs_2_.refs_3_, bf16[288,256]{1,0:T(8,128)(2,1)S(1)} %get-tuple-element.31.refs_3_.refs_4_, ...), custom_call_target="tpu_custom_call" | custom-call | tf_op jit(solution)/shard_map/root/pallas_call | solution.py:350
  39.9 0.0 collective-permute-done.19.refs_3_
  39.9 0.0 collective-permute-done.18.refs_2_
  39.9 0.2 collective-permute-done.17.refs_1_
  40.0 1.0 %step.1 = bf16[256,256]{1,0:T(8,128)(2,1)} custom-call(bf16[256,256]{1,0:T(8,128)(2,1)S(1)} %grad_total.1.refs_0_, bf16[256,256]{1,0:T(8,128)(2,1)S(1)} %collective-permute-done.17.refs_1_, bf16[256,256]{1,0:T(8,128)(2,1)S(1)} %collective-permute-done.18.refs_2_, bf16[256,256]{1,0:T(8,128)(2,1)S(1)} %collective-permute-done.19.refs_3_, ...), custom_call_target="tpu_custom_call" | custom-call | tf_op jit(solution)/shard_map/step/pallas_call | solution.py:350
  (2 shorter events, 0.1 us)
Async XLA Ops:
  0.6 13.4 %collective-permute-start.12 = (bf16[1,512,256]{2,1,0:T(8,128)(2,1)}, bf16[1,512,256]{2,1,0:T(8,128)(2,1)S(1)}, u32[]{:S(2)}, u32[]{:S(2)}) collective-permute-start(bf16[1,512,256]{2,1,0:T(8,128)(2,1)} %param.6), channel_id=1, source_target_pairs={{16,0},{0,16},{17,1},{1,17},{18,2},{2,18},{19,3},{3,19},{20,4},{4,... | collective-permute-start | bytes 786440 | tf_op jit(solution)/shard_map/ppermute | solution.py:22
  1.1 1.2 %copy-start = (bf16[1,512,1024]{2,1,0:T(8,128)(2,1)S(1)}, bf16[1,512,1024]{2,1,0:T(8,128)(2,1)}, u32[]{:S(2)}) copy-start(bf16[1,512,1024]{2,1,0:T(8,128)(2,1)} %param.5) | copy-start | bytes 3145732
  2.8 6.9 %collective-permute-start.3 = (bf16[272,256]{1,0:T(8,128)(2,1)S(1)}, bf16[272,256]{1,0:T(8,128)(2,1)S(1)}, u32[]{:S(2)}, u32[]{:S(2)}) collective-permute-start(bf16[272,256]{1,0:T(8,128)(2,1)S(1)} %get-tuple-element.26), channel_id=1, source_target_pairs={{0,8},{4,12},{8,0},{12,4},{1,9},{5,13},{9,1},{13,5},{2,10},{6,14},... | collective-permute-start | bytes 417800 | tf_op jit(solution)/shard_map/ppermute | solution.py:26
  5.4 8.7 %copy-start.1 = (bf16[1,512,1024]{2,1,0:T(8,128)(2,1)S(1)}, bf16[1,512,1024]{2,1,0:T(8,128)(2,1)}, u32[]{:S(2)}) copy-start(bf16[1,512,1024]{2,1,0:T(8,128)(2,1)} %param.5) | copy-start | bytes 3145732
  5.4 8.7 %copy-start.3 = (bf16[1,1,256,1024]{3,2,1,0:T(8,128)(2,1)S(1)}, bf16[1,1,256,1024]{3,2,1,0:T(8,128)(2,1)}, u32[]{:S(2)}) copy-start(bf16[1,1,256,1024]{3,2,1,0:T(8,128)(2,1)} %param.8) | copy-start | bytes 1572868
  5.4 6.4 %collective-permute-start.2 = (bf16[272,256]{1,0:T(8,128)(2,1)S(1)}, bf16[272,256]{1,0:T(8,128)(2,1)S(1)}, u32[]{:S(2)}, u32[]{:S(2)}) collective-permute-start(bf16[272,256]{1,0:T(8,128)(2,1)S(1)} %get-tuple-element.22.refs_1_), channel_id=1, source_target_pairs={{0,4},{4,0},{8,12},{12,8},{1,5},{5,1},{9,13},{13,9},{2,6},{6,2},{1... | collective-permute-start | bytes 417800 | tf_op jit(solution)/shard_map/ppermute | solution.py:26
  8.0 6.8 %collective-permute-start = (bf16[272,256]{1,0:T(8,128)(2,1)S(1)}, bf16[272,256]{1,0:T(8,128)(2,1)S(1)}, u32[]{:S(2)}, u32[]{:S(2)}) collective-permute-start(bf16[272,256]{1,0:T(8,128)(2,1)S(1)} %get-tuple-element.24), channel_id=1, source_target_pairs={{0,4},{4,0},{8,12},{12,8},{1,5},{5,1},{9,13},{13,9},{2,6},{6,2},{1... | collective-permute-start | bytes 417800 | tf_op jit(solution)/shard_map/ppermute | solution.py:26
  8.6 8.0 %collective-permute-start.1 = (bf16[272,256]{1,0:T(8,128)(2,1)S(1)}, bf16[272,256]{1,0:T(8,128)(2,1)S(1)}, u32[]{:S(2)}, u32[]{:S(2)}) collective-permute-start(bf16[272,256]{1,0:T(8,128)(2,1)S(1)} %get-tuple-element.25), channel_id=1, source_target_pairs={{0,8},{4,12},{8,0},{12,4},{1,9},{5,13},{9,1},{13,5},{2,10},{6,14},... | collective-permute-start | bytes 417800 | tf_op jit(solution)/shard_map/ppermute | solution.py:26
  11.9 7.4 %copy-start.2 = (f32[1,1,256,1024]{3,2,1,0:T(8,128)S(1)}, f32[1,1,256,1024]{3,2,1,0:T(8,128)}, u32[]{:S(2)}) copy-start(f32[1,1,256,1024]{3,2,1,0:T(8,128)} %param.7) | copy-start | bytes 3145732
  11.9 6.7 %collective-permute-start.4 = (bf16[272,256]{1,0:T(8,128)(2,1)S(1)}, bf16[272,256]{1,0:T(8,128)(2,1)S(1)}, u32[]{:S(2)}, u32[]{:S(2)}) collective-permute-start(bf16[272,256]{1,0:T(8,128)(2,1)S(1)} %get-tuple-element.27.refs_3_), channel_id=1, source_target_pairs={{0,4},{4,0},{8,12},{12,8},{1,5},{5,1},{9,13},{13,9},{2,6},{6,2},{1... | collective-permute-start | bytes 417800 | tf_op jit(solution)/shard_map/ppermute | solution.py:26
  13.6 5.7 %collective-permute-start.5 = (bf16[272,256]{1,0:T(8,128)(2,1)S(1)}, bf16[272,256]{1,0:T(8,128)(2,1)S(1)}, u32[]{:S(2)}, u32[]{:S(2)}) collective-permute-start(bf16[272,256]{1,0:T(8,128)(2,1)S(1)} %get-tuple-element.28.refs_4_), channel_id=1, source_target_pairs={{0,8},{4,12},{8,0},{12,4},{1,9},{5,13},{9,1},{13,5},{2,10},{6,14},... | collective-permute-start | bytes 417800 | tf_op jit(solution)/shard_map/ppermute | solution.py:26
  14.6 8.0 %collective-permute-start.13 = (bf16[256,256]{1,0:T(8,128)(2,1)S(1)}, bf16[256,256]{1,0:T(8,128)(2,1)S(1)}, u32[]{:S(2)}, u32[]{:S(2)}) collective-permute-start(bf16[256,256]{1,0:T(8,128)(2,1)S(1)} %get-tuple-element.35), channel_id=1, source_target_pairs={{0,4},{4,0},{8,12},{12,8},{1,5},{5,1},{9,13},{13,9},{2,6},{6,2},{1... | collective-permute-start | bytes 393224 | tf_op jit(solution)/shard_map/ppermute | solution.py:26
  14.8 9.0 %collective-permute-start.14 = (bf16[256,256]{1,0:T(8,128)(2,1)S(1)}, bf16[256,256]{1,0:T(8,128)(2,1)S(1)}, u32[]{:S(2)}, u32[]{:S(2)}) collective-permute-start(bf16[256,256]{1,0:T(8,128)(2,1)S(1)} %get-tuple-element.36), channel_id=1, source_target_pairs={{0,8},{4,12},{8,0},{12,4},{1,9},{5,13},{9,1},{13,5},{2,10},{6,14},... | collective-permute-start | bytes 393224 | tf_op jit(solution)/shard_map/ppermute | solution.py:26
  19.7 5.7 %collective-permute-start.6 = (bf16[272,256]{1,0:T(8,128)(2,1)S(1)}, bf16[272,256]{1,0:T(8,128)(2,1)S(1)}, u32[]{:S(2)}, u32[]{:S(2)}) collective-permute-start(bf16[272,256]{1,0:T(8,128)(2,1)S(1)} %get-tuple-element.30.refs_2_.refs_3_), channel_id=1, source_target_pairs={{0,4},{4,0},{8,12},{12,8},{1,5},{5,1},{9,13},{13,9},{2,6},{6,2},{1... | collective-permute-start | bytes 417800 | tf_op jit(solution)/shard_map/ppermute | solution.py:26
  20.8 6.1 %collective-permute-start.9 = (bf16[288,256]{1,0:T(8,128)(2,1)S(1)}, bf16[288,256]{1,0:T(8,128)(2,1)S(1)}, u32[]{:S(2)}, u32[]{:S(2)}) collective-permute-start(bf16[288,256]{1,0:T(8,128)(2,1)S(1)} %get-tuple-element.31.refs_3_.refs_4_), channel_id=1, source_target_pairs={{0,8},{4,12},{8,0},{12,4},{1,9},{5,13},{9,1},{13,5},{2,10},{6,14},... | collective-permute-start | bytes 442376 | tf_op jit(solution)/shard_map/ppermute | solution.py:26
  21.1 14.0 %collective-permute-start.7 = (bf16[288,256]{1,0:T(8,128)(2,1)S(1)}, bf16[288,256]{1,0:T(8,128)(2,1)S(1)}, u32[]{:S(2)}, u32[]{:S(2)}) collective-permute-start(bf16[288,256]{1,0:T(8,128)(2,1)S(1)} %get-tuple-element.31.refs_3_.refs_4_), channel_id=1, source_target_pairs={{0,4},{4,0},{8,12},{12,8},{1,5},{5,1},{9,13},{13,9},{2,6},{6,2},{1... | collective-permute-start | bytes 442376 | tf_op jit(solution)/shard_map/ppermute | solution.py:26
  22.6 10.4 %collective-permute-start.8 = (bf16[272,256]{1,0:T(8,128)(2,1)S(1)}, bf16[272,256]{1,0:T(8,128)(2,1)S(1)}, u32[]{:S(2)}, u32[]{:S(2)}) collective-permute-start(bf16[272,256]{1,0:T(8,128)(2,1)S(1)} %get-tuple-element.30.refs_2_.refs_3_), channel_id=1, source_target_pairs={{0,8},{4,12},{8,0},{12,4},{1,9},{5,13},{9,1},{13,5},{2,10},{6,14},... | collective-permute-start | bytes 417800 | tf_op jit(solution)/shard_map/ppermute | solution.py:26
  23.8 5.4 %collective-permute-start.15 = (bf16[128,256]{1,0:T(8,128)(2,1)S(1)}, bf16[128,256]{1,0:T(8,128)(2,1)S(1)}, u32[]{:S(2)}, u32[]{:S(2)}) collective-permute-start(bf16[128,256]{1,0:T(8,128)(2,1)S(1)} %get-tuple-element.37), channel_id=1, source_target_pairs={{0,4},{4,0},{8,12},{12,8},{1,5},{5,1},{9,13},{13,9},{2,6},{6,2},{1... | collective-permute-start | bytes 196616 | tf_op jit(solution)/shard_map/ppermute | solution.py:26
  25.4 6.4 %collective-permute-start.16 = (bf16[128,256]{1,0:T(8,128)(2,1)S(1)}, bf16[128,256]{1,0:T(8,128)(2,1)S(1)}, u32[]{:S(2)}, u32[]{:S(2)}) collective-permute-start(bf16[128,256]{1,0:T(8,128)(2,1)S(1)} %get-tuple-element.38), channel_id=1, source_target_pairs={{0,8},{4,12},{8,0},{12,4},{1,9},{5,13},{9,1},{13,5},{2,10},{6,14},... | collective-permute-start | bytes 196616 | tf_op jit(solution)/shard_map/ppermute | solution.py:26
  26.9 9.1 %collective-permute-start.11 = (bf16[288,256]{1,0:T(8,128)(2,1)S(1)}, bf16[288,256]{1,0:T(8,128)(2,1)S(1)}, u32[]{:S(2)}, u32[]{:S(2)}) collective-permute-start(bf16[288,256]{1,0:T(8,128)(2,1)S(1)} %collective-permute-done.9.refs_7_.refs_6_), channel_id=1, source_target_pairs={{0,4},{4,0},{8,12},{12,8},{1,5},{5,1},{9,13},{13,9},{2,6},{6,2},{1... | collective-permute-start | bytes 442376 | tf_op jit(solution)/shard_map/ppermute | solution.py:26
  29.2 6.9 %collective-permute-start.10 = (bf16[272,256]{1,0:T(8,128)(2,1)S(1)}, bf16[272,256]{1,0:T(8,128)(2,1)S(1)}, u32[]{:S(2)}, u32[]{:S(2)}) collective-permute-start(bf16[272,256]{1,0:T(8,128)(2,1)S(1)} %collective-permute-done.6.refs_4_.refs_5_), channel_id=1, source_target_pairs={{0,8},{4,12},{8,0},{12,4},{1,9},{5,13},{9,1},{13,5},{2,10},{6,14},... | collective-permute-start | bytes 417800 | tf_op jit(solution)/shard_map/ppermute | solution.py:26
  31.9 8.0 %collective-permute-start.19 = (bf16[256,256]{1,0:T(8,128)(2,1)S(1)}, bf16[256,256]{1,0:T(8,128)(2,1)S(1)}, u32[]{:S(2)}, u32[]{:S(2)}) collective-permute-start(bf16[256,256]{1,0:T(8,128)(2,1)S(1)} %grad_total.1.refs_0_), channel_id=1, source_target_pairs={{0,12},{4,8},{8,4},{12,0},{1,13},{5,9},{9,5},{13,1},{2,14},{6,10},... | collective-permute-start | bytes 393224 | tf_op jit(solution)/shard_map/ppermute | solution.py:26
  33.0 6.9 %collective-permute-start.18 = (bf16[256,256]{1,0:T(8,128)(2,1)S(1)}, bf16[256,256]{1,0:T(8,128)(2,1)S(1)}, u32[]{:S(2)}, u32[]{:S(2)}) collective-permute-start(bf16[256,256]{1,0:T(8,128)(2,1)S(1)} %grad_total.1.refs_0_), channel_id=1, source_target_pairs={{0,8},{4,12},{8,0},{12,4},{1,9},{5,13},{9,1},{13,5},{2,10},{6,14},... | collective-permute-start | bytes 393224 | tf_op jit(solution)/shard_map/ppermute | solution.py:26
  35.1 5.0 %collective-permute-start.17 = (bf16[256,256]{1,0:T(8,128)(2,1)S(1)}, bf16[256,256]{1,0:T(8,128)(2,1)S(1)}, u32[]{:S(2)}, u32[]{:S(2)}) collective-permute-start(bf16[256,256]{1,0:T(8,128)(2,1)S(1)} %grad_total.1.refs_0_), channel_id=1, source_target_pairs={{0,4},{4,0},{8,12},{12,8},{1,5},{5,1},{9,13},{13,9},{2,6},{6,2},{1... | collective-permute-start | bytes 393224 | tf_op jit(solution)/shard_map/ppermute | solution.py:26

commit v19 on v17

--- a/solution.py
+++ b/solution.py
@@ -230,7 +230,7 @@
 
 def root_kernel(count, exact, *rest):
     chunks = [rest[2 * i : 2 * i + 2] for i in range(4)]
-    factor_out, root_out, finished, factor, diagonal, rows, sent = rest[8:]
+    factor_out, root_out, finished, factor, diagonal, rows, roots, sent, root_sent = rest[8:]
     share, order = root_out.shape
     half = share // 2
     starts = chunk_rows(share)
@@ -295,11 +295,16 @@
     second = (jnp.dot(turn, factor[...], preferred_element_type=F32) * inverse).astype(BF16)
     product = (-0.5 * inverse) * jnp.dot(second, factor[...], preferred_element_type=F32) + second.astype(F32) * lift
     turn_two = (1.5 * eye - 0.5 * product).astype(BF16)
-    inverse_rows = (-0.5 * inverse) * jnp.dot(
-        turn_two, factor[...], preferred_element_type=F32
-    ) + turn_two.astype(F32) * lift
-    chosen = jnp.where(count[0, 0] == 1, turn.astype(F32), inverse_rows)
-    root_out[...] = (chosen * lax.rsqrt(scale)).astype(BF16)
+    root_scale = lax.rsqrt(scale)
+    for i in range(order // share):
+        part = slice(i * share, (i + 1) * share)
+        inverse_rows = (-0.5 * inverse) * jnp.dot(
+            turn_two, factor[:, part], preferred_element_type=F32
+        ) + turn_two[:, part].astype(F32) * lift[:, part]
+        chosen = jnp.where(count[0, 0] == 1, turn[:, part].astype(F32), inverse_rows)
+        roots[i] = (chosen * root_scale).astype(BF16)
+        copies.append(pltpu.make_async_copy(roots.at[i], root_out.at[:, part], root_sent.at[i]))
+        copies[-1].start()
     finished[...] = jnp.zeros_like(finished)
     for copy in copies:
         copy.wait()
@@ -337,13 +342,12 @@
     def shape(rows, kind=BF16, columns=share):
         return jax.ShapeDtypeStruct((rows, columns), kind)
 
-    def call(kernel, outs, name, *operands, first=None, first_out=None, after=(), scratch=()):
+    def call(kernel, outs, name, *operands, first=None, copied_out=0, after=(), scratch=()):
         in_specs = whole(len(operands)) + [pl.BlockSpec(memory_space=pl.ANY)] * len(after)
         if first is not None:
             in_specs[0] = pl.BlockSpec(memory_space=first)
         out_specs = whole(len(outs))
-        if first_out is not None:
-            out_specs[0] = pl.BlockSpec(memory_space=first_out)
+        out_specs[:copied_out] = [pl.BlockSpec(memory_space=pl.ANY)] * copied_out
 
         def body(*refs):
             kernel(*refs[: len(operands)], *refs[len(operands) + len(after) :])
@@ -429,11 +433,13 @@
         upper_far,
         lower_far,
         first=pltpu.SMEM,
-        first_out=pl.ANY,
+        copied_out=2,
         scratch=[
             pltpu.VMEM((order, order), BF16),
             pltpu.VMEM((1, order), F32),
             pltpu.VMEM((replicas, share, share), F32),
+            pltpu.VMEM((replicas, share, share), BF16),
+            pltpu.SemaphoreType.DMA((replicas,)),
             pltpu.SemaphoreType.DMA((replicas,)),
         ],
     )

time: 40.7 us -> 40.7 us (level)
  no operation moved by 1% of the time
where the time goes in v19:
time: 40.7 us; the launch traced here: 40.5 us
  starting transfers between devices  23.1 us (57%)
  waiting for transfers between devices  7.44 us (18%)
  Pallas kernels  7.38 us (18%)
  between operations  1.38 us (3%)
  local copies, waits for them, and re-layouts  1.24 us (3%)
    ppermute x19, starting transfers between devices, swapped(): lax.ppermute(block, 'dp', [(i, i ^ offset) for i in range(lax.axis_size('...  22.6 us
    ppermute x19, waiting for transfers between devices, swapped(): lax.ppermute(block, 'dp', [(i, i ^ offset) for i in range(lax.axis_size('...  7.44 us
    pallas_call x9, Pallas kernels, call(): pl.pallas_call(body, out_shape=outs, in_specs=in_specs, out_specs=out_spe...  7.38 us
    unnamed x8, local copies, waits for them, and re-layouts  1.24 us
  transfers between devices with their start and end apart: 20, of which 6 were waited for; matrix products, arithmetic and copies ran while one was open for 0% of the time, Pallas kernels for 16%

profile of v19, /device:TPU:0, one launch (start us, length us, event | category | flops | bytes accessed | tf_op | source)
XLA Modules:
  0.0 40.5 jit_solution(8017002820288911632)
XLA Ops:
  0.6 0.5 %collective-permute-start.12 = (bf16[1,512,256]{2,1,0:T(8,128)(2,1)}, bf16[1,512,256]{2,1,0:T(8,128)(2,1)S(1)}, u32[]{:S(2)}, u32[]{:S(2)}) collective-permute-start(bf16[1,512,256]{2,1,0:T(8,128)(2,1)} %param.6), channel_id=1, source_target_pairs={{16,0},{0,16},{17,1},{1,17},{18,2},{2,18},{19,3},{3,19},{20,4},{4,... | collective-permute-start | bytes 786440 | tf_op jit(solution)/shard_map/ppermute | solution.py:22
  1.1 0.0 copy-start
  1.1 1.2 %copy-done = bf16[1,512,1024]{2,1,0:T(8,128)(2,1)S(1)} copy-done((bf16[1,512,1024]{2,1,0:T(8,128)(2,1)S(1)}, bf16[1,512,1024]{2,1,0:T(8,128)(2,1)}, u32[]{:S(2)}) %copy-start) | copy-done | bytes 1048600
  2.4 0.5 %across.1 = (bf16[272,256]{1,0:T(8,128)(2,1)S(1)}, bf16[272,256]{1,0:T(8,128)(2,1)S(1)}) custom-call(bf16[512,1024]{1,0:T(8,128)(2,1)S(1)} %bitcast.7), custom_call_target="tpu_custom_call" | custom-call | tf_op jit(solution)/shard_map/across/pallas_call | solution.py:355
  2.8 2.6 %collective-permute-start.2 = (bf16[272,256]{1,0:T(8,128)(2,1)S(1)}, bf16[272,256]{1,0:T(8,128)(2,1)S(1)}, u32[]{:S(2)}, u32[]{:S(2)}) collective-permute-start(bf16[272,256]{1,0:T(8,128)(2,1)S(1)} %get-tuple-element.21.refs_1_), channel_id=1, source_target_pairs={{0,4},{4,0},{8,12},{12,8},{1,5},{5,1},{9,13},{13,9},{2,6},{6,2},{1... | collective-permute-start | bytes 417800 | tf_op jit(solution)/shard_map/ppermute | solution.py:26
  5.4 0.0 copy-start.1
  5.4 1.5 %collective-permute-start.3 = (bf16[272,256]{1,0:T(8,128)(2,1)S(1)}, bf16[272,256]{1,0:T(8,128)(2,1)S(1)}, u32[]{:S(2)}, u32[]{:S(2)}) collective-permute-start(bf16[272,256]{1,0:T(8,128)(2,1)S(1)} %get-tuple-element.25), channel_id=1, source_target_pairs={{0,8},{4,12},{8,0},{12,4},{1,9},{5,13},{9,1},{13,5},{2,10},{6,14},... | collective-permute-start | bytes 417800 | tf_op jit(solution)/shard_map/ppermute | solution.py:26
  6.9 1.1 %batch.1 = (bf16[272,256]{1,0:T(8,128)(2,1)S(1)}, bf16[272,256]{1,0:T(8,128)(2,1)S(1)}, f32[1088,256]{1,0:T(8,128)S(1)}) custom-call(bf16[512,1024]{1,0:T(8,128)(2,1)S(1)} %bitcast.8, bf16[272,256]{1,0:T(8,128)(2,1)S(1)} %get-tuple-element.21.refs_1_), custom_call_target="tpu_custom_call" | custom-call | tf_op jit(solution)/shard_map/batch/pallas_call | solution.py:355
  8.0 0.6 %collective-permute-start = (bf16[272,256]{1,0:T(8,128)(2,1)S(1)}, bf16[272,256]{1,0:T(8,128)(2,1)S(1)}, u32[]{:S(2)}, u32[]{:S(2)}) collective-permute-start(bf16[272,256]{1,0:T(8,128)(2,1)S(1)} %get-tuple-element.23), channel_id=1, source_target_pairs={{0,4},{4,0},{8,12},{12,8},{1,5},{5,1},{9,13},{13,9},{2,6},{6,2},{1... | collective-permute-start | bytes 417800 | tf_op jit(solution)/shard_map/ppermute | solution.py:26
  8.6 0.1 collective-permute-start.1
  8.7 1.1 %collective-permute-done.2.refs_1_ = bf16[272,256]{1,0:T(8,128)(2,1)S(1)} collective-permute-done((bf16[272,256]{1,0:T(8,128)(2,1)S(1)}, bf16[272,256]{1,0:T(8,128)(2,1)S(1)}, u32[]{:S(2)}, u32[]{:S(2)}) %collective-permute-start.2) | collective-permute-done | bytes 139296 | tf_op jit(solution)/shard_map/ppermute | solution.py:26
  9.7 1.7 %collective-permute-done.3.refs_2_ = bf16[272,256]{1,0:T(8,128)(2,1)S(1)} collective-permute-done((bf16[272,256]{1,0:T(8,128)(2,1)S(1)}, bf16[272,256]{1,0:T(8,128)(2,1)S(1)}, u32[]{:S(2)}, u32[]{:S(2)}) %collective-permute-start.3) | collective-permute-done | bytes 139296 | tf_op jit(solution)/shard_map/ppermute | solution.py:26
  11.5 0.1 relay.1
  11.5 0.0 copy-start.2
  11.6 0.3 collective-permute-start.4
  11.9 1.8 %collective-permute-start.5 = (bf16[272,256]{1,0:T(8,128)(2,1)S(1)}, bf16[272,256]{1,0:T(8,128)(2,1)S(1)}, u32[]{:S(2)}, u32[]{:S(2)}) collective-permute-start(bf16[272,256]{1,0:T(8,128)(2,1)S(1)} %get-tuple-element.27.refs_3_), channel_id=1, source_target_pairs={{0,8},{4,12},{8,0},{12,4},{1,9},{5,13},{9,1},{13,5},{2,10},{6,14},... | collective-permute-start | bytes 417800 | tf_op jit(solution)/shard_map/ppermute | solution.py:26
  13.7 0.0 collective-permute-done.12
  13.7 0.0 copy-done.1
  13.7 0.5 %grad.1 = (bf16[256,256]{1,0:T(8,128)(2,1)S(1)}, bf16[256,256]{1,0:T(8,128)(2,1)S(1)}, f32[512,256]{1,0:T(8,128)S(1)}) custom-call(bf16[512,1024]{1,0:T(8,128)(2,1)S(1)} %bitcast.9, bf16[512,256]{1,0:T(8,128)(2,1)S(1)} %bitcast.12, bf16[272,256]{1,0:T(8,128)(2,1)S(1)} %get-tuple-element.26.refs_2_, bf16[272,256]{1,0:T(8,128)(2,1)S(1)} %get-tuple-element.27.refs_3_), custom_call_target="tpu_custom_call" | custom-call | tf_op jit(solution)/shard_map/grad/pallas_call | solution.py:355
  14.3 1.9 %collective-permute-start.13 = (bf16[256,256]{1,0:T(8,128)(2,1)S(1)}, bf16[256,256]{1,0:T(8,128)(2,1)S(1)}, u32[]{:S(2)}, u32[]{:S(2)}) collective-permute-start(bf16[256,256]{1,0:T(8,128)(2,1)S(1)} %get-tuple-element.34), channel_id=1, source_target_pairs={{0,4},{4,0},{8,12},{12,8},{1,5},{5,1},{9,13},{13,9},{2,6},{6,2},{1... | collective-permute-start | bytes 393224 | tf_op jit(solution)/shard_map/ppermute | solution.py:26
  16.2 0.0 collective-permute-done.refs_1_
  16.2 0.1 collective-permute-start.14
  16.3 0.0 collective-permute-done.1.refs_2_
  16.3 1.6 %collective-permute-done.4.refs_3_ = bf16[272,256]{1,0:T(8,128)(2,1)S(1)} collective-permute-done((bf16[272,256]{1,0:T(8,128)(2,1)S(1)}, bf16[272,256]{1,0:T(8,128)(2,1)S(1)}, u32[]{:S(2)}, u32[]{:S(2)}) %collective-permute-start.4) | collective-permute-done | bytes 139296 | tf_op jit(solution)/shard_map/ppermute | solution.py:26
  17.9 0.0 collective-permute-done.5.refs_4_
  17.9 0.0 copy-done.2
  17.9 0.4 %factor.1 = (bf16[272,256]{1,0:T(8,128)(2,1)S(1)}, bf16[288,256]{1,0:T(8,128)(2,1)S(1)}, f32[640,256]{1,0:T(8,128)S(1)}) custom-call(f32[1088,256]{1,0:T(8,128)S(1)} %get-tuple-element.22.refs_0_, bf16[272,256]{1,0:T(8,128)(2,1)S(1)} %collective-permute-done.refs_1_, bf16[272,256]{1,0:T(8,128)(2,1)S(1)} %collective-permute-done.1.refs_2_, ...), custom_call_target="tpu_custom_call" | custom-call | tf_op jit(solution)/shard_map/factor/pallas_call | solution.py:355
  18.3 2.3 %collective-permute-start.6 = (bf16[272,256]{1,0:T(8,128)(2,1)S(1)}, bf16[272,256]{1,0:T(8,128)(2,1)S(1)}, u32[]{:S(2)}, u32[]{:S(2)}) collective-permute-start(bf16[272,256]{1,0:T(8,128)(2,1)S(1)} %get-tuple-element.29.refs_2_.refs_3_), channel_id=1, source_target_pairs={{0,4},{4,0},{8,12},{12,8},{1,5},{5,1},{9,13},{13,9},{2,6},{6,2},{1... | collective-permute-start | bytes 417800 | tf_op jit(solution)/shard_map/ppermute | solution.py:26
  20.6 1.1 %collective-permute-start.9 = (bf16[288,256]{1,0:T(8,128)(2,1)S(1)}, bf16[288,256]{1,0:T(8,128)(2,1)S(1)}, u32[]{:S(2)}, u32[]{:S(2)}) collective-permute-start(bf16[288,256]{1,0:T(8,128)(2,1)S(1)} %get-tuple-element.30.refs_3_.refs_4_), channel_id=1, source_target_pairs={{0,8},{4,12},{8,0},{12,4},{1,9},{5,13},{9,1},{13,5},{2,10},{6,14},... | collective-permute-start | bytes 442376 | tf_op jit(solution)/shard_map/ppermute | solution.py:26
  21.7 0.9 %collective-permute-start.7 = (bf16[288,256]{1,0:T(8,128)(2,1)S(1)}, bf16[288,256]{1,0:T(8,128)(2,1)S(1)}, u32[]{:S(2)}, u32[]{:S(2)}) collective-permute-start(bf16[288,256]{1,0:T(8,128)(2,1)S(1)} %get-tuple-element.30.refs_3_.refs_4_), channel_id=1, source_target_pairs={{0,4},{4,0},{8,12},{12,8},{1,5},{5,1},{9,13},{13,9},{2,6},{6,2},{1... | collective-permute-start | bytes 442376 | tf_op jit(solution)/shard_map/ppermute | solution.py:26
  22.6 0.0 collective-permute-done.13.refs_1_
  22.6 0.1 collective-permute-start.8
  22.7 0.0 collective-permute-done.14.refs_2_
  22.7 2.0 %collective-permute-start.15 = (bf16[128,256]{1,0:T(8,128)(2,1)S(1)}, bf16[128,256]{1,0:T(8,128)(2,1)S(1)}, u32[]{:S(2)}, u32[]{:S(2)}) collective-permute-start(bf16[128,256]{1,0:T(8,128)(2,1)S(1)} %get-tuple-element.36), channel_id=1, source_target_pairs={{0,4},{4,0},{8,12},{12,8},{1,5},{5,1},{9,13},{13,9},{2,6},{6,2},{1... | collective-permute-start | bytes 196616 | tf_op jit(solution)/shard_map/ppermute | solution.py:26
  24.8 0.0 collective-permute-done.6.refs_4_.refs_5_
  24.8 1.5 %collective-permute-start.16 = (bf16[128,256]{1,0:T(8,128)(2,1)S(1)}, bf16[128,256]{1,0:T(8,128)(2,1)S(1)}, u32[]{:S(2)}, u32[]{:S(2)}) collective-permute-start(bf16[128,256]{1,0:T(8,128)(2,1)S(1)} %get-tuple-element.37), channel_id=1, source_target_pairs={{0,8},{4,12},{8,0},{12,4},{1,9},{5,13},{9,1},{13,5},{2,10},{6,14},... | collective-permute-start | bytes 196616 | tf_op jit(solution)/shard_map/ppermute | solution.py:26
  26.3 0.2 collective-permute-done.9.refs_7_.refs_6_
  26.5 0.7 %collective-permute-start.11 = (bf16[288,256]{1,0:T(8,128)(2,1)S(1)}, bf16[288,256]{1,0:T(8,128)(2,1)S(1)}, u32[]{:S(2)}, u32[]{:S(2)}) collective-permute-start(bf16[288,256]{1,0:T(8,128)(2,1)S(1)} %collective-permute-done.9.refs_7_.refs_6_), channel_id=1, source_target_pairs={{0,4},{4,0},{8,12},{12,8},{1,5},{5,1},{9,13},{13,9},{2,6},{6,2},{1... | collective-permute-start | bytes 442376 | tf_op jit(solution)/shard_map/ppermute | solution.py:26
  27.2 2.4 %collective-permute-done.15.refs_3_ = bf16[128,256]{1,0:T(8,128)(2,1)S(1)} collective-permute-done((bf16[128,256]{1,0:T(8,128)(2,1)S(1)}, bf16[128,256]{1,0:T(8,128)(2,1)S(1)}, u32[]{:S(2)}, u32[]{:S(2)}) %collective-permute-start.15) | collective-permute-done | bytes 65568 | tf_op jit(solution)/shard_map/ppermute | solution.py:26
  29.6 0.9 %collective-permute-start.10 = (bf16[272,256]{1,0:T(8,128)(2,1)S(1)}, bf16[272,256]{1,0:T(8,128)(2,1)S(1)}, u32[]{:S(2)}, u32[]{:S(2)}) collective-permute-start(bf16[272,256]{1,0:T(8,128)(2,1)S(1)} %collective-permute-done.6.refs_4_.refs_5_), channel_id=1, source_target_pairs={{0,8},{4,12},{8,0},{12,4},{1,9},{5,13},{9,1},{13,5},{2,10},{6,14},... | collective-permute-start | bytes 417800 | tf_op jit(solution)/shard_map/ppermute | solution.py:26
  30.6 0.0 collective-permute-done.16.refs_4_
  30.6 0.1 grad_total.1.refs_0_
  30.6 0.0 copy-start.3
  30.6 2.5 %collective-permute-start.17 = (bf16[256,256]{1,0:T(8,128)(2,1)S(1)}, bf16[256,256]{1,0:T(8,128)(2,1)S(1)}, u32[]{:S(2)}, u32[]{:S(2)}) collective-permute-start(bf16[256,256]{1,0:T(8,128)(2,1)S(1)} %grad_total.1.refs_0_), channel_id=1, source_target_pairs={{0,4},{4,0},{8,12},{12,8},{1,5},{5,1},{9,13},{13,9},{2,6},{6,2},{1... | collective-permute-start | bytes 393224 | tf_op jit(solution)/shard_map/ppermute | solution.py:26
  33.2 0.0 collective-permute-done.8.refs_6_
  33.2 0.2 collective-permute-start.18
  33.4 0.0 collective-permute-done.7.refs_5_
  33.4 1.3 %collective-permute-start.19 = (bf16[256,256]{1,0:T(8,128)(2,1)S(1)}, bf16[256,256]{1,0:T(8,128)(2,1)S(1)}, u32[]{:S(2)}, u32[]{:S(2)}) collective-permute-start(bf16[256,256]{1,0:T(8,128)(2,1)S(1)} %grad_total.1.refs_0_), channel_id=1, source_target_pairs={{0,12},{4,8},{8,4},{12,0},{1,13},{5,9},{9,5},{13,1},{2,14},{6,10},... | collective-permute-start | bytes 393224 | tf_op jit(solution)/shard_map/ppermute | solution.py:26
  35.4 0.0 collective-permute-done.10.refs_8_
  35.4 0.0 collective-permute-done.11.refs_9_
  35.4 3.8 %root.1 = (f32[256,1024]{1,0:T(8,128)}, bf16[256,1024]{1,0:T(8,128)(2,1)}, f32[8,128]{1,0:T(8,128)S(1)}) custom-call(s32[1,1]{1,0:T(1,128)S(6)} %copy.8.refs_0_, f32[640,256]{1,0:T(8,128)S(1)} %get-tuple-element.28.refs_1_, bf16[272,256]{1,0:T(8,128)(2,1)S(1)} %get-tuple-element.29.refs_2_.refs_3_, bf16[288,256]{1,0:T(8,128)(2,1)S(1)} %get-tuple-element.30.refs_3_.refs_4_, ...), custom_call_target="tpu_custom_call" | custom-call | tf_op jit(solution)/shard_map/root/pallas_call | solution.py:355
  39.2 0.0 collective-permute-done.17.refs_1_
  39.2 0.4 collective-permute-done.18.refs_2_
  39.5 0.0 collective-permute-done.19.refs_3_
  39.5 0.0 copy-done.3
  39.5 1.0 %step.1 = bf16[256,256]{1,0:T(8,128)(2,1)} custom-call(bf16[256,256]{1,0:T(8,128)(2,1)S(1)} %grad_total.1.refs_0_, bf16[256,256]{1,0:T(8,128)(2,1)S(1)} %collective-permute-done.17.refs_1_, bf16[256,256]{1,0:T(8,128)(2,1)S(1)} %collective-permute-done.18.refs_2_, bf16[256,256]{1,0:T(8,128)(2,1)S(1)} %collective-permute-done.19.refs_3_, ...), custom_call_target="tpu_custom_call" | custom-call | tf_op jit(solution)/shard_map/step/pallas_call | solution.py:355
  (1 shorter events, 0.0 us)
Async XLA Ops:
  0.6 13.1 %collective-permute-start.12 = (bf16[1,512,256]{2,1,0:T(8,128)(2,1)}, bf16[1,512,256]{2,1,0:T(8,128)(2,1)S(1)}, u32[]{:S(2)}, u32[]{:S(2)}) collective-permute-start(bf16[1,512,256]{2,1,0:T(8,128)(2,1)} %param.6), channel_id=1, source_target_pairs={{16,0},{0,16},{17,1},{1,17},{18,2},{2,18},{19,3},{3,19},{20,4},{4,... | collective-permute-start | bytes 786440 | tf_op jit(solution)/shard_map/ppermute | solution.py:22
  1.1 1.2 %copy-start = (bf16[1,512,1024]{2,1,0:T(8,128)(2,1)S(1)}, bf16[1,512,1024]{2,1,0:T(8,128)(2,1)}, u32[]{:S(2)}) copy-start(bf16[1,512,1024]{2,1,0:T(8,128)(2,1)} %param.5) | copy-start | bytes 3145732
  2.8 6.9 %collective-permute-start.2 = (bf16[272,256]{1,0:T(8,128)(2,1)S(1)}, bf16[272,256]{1,0:T(8,128)(2,1)S(1)}, u32[]{:S(2)}, u32[]{:S(2)}) collective-permute-start(bf16[272,256]{1,0:T(8,128)(2,1)S(1)} %get-tuple-element.21.refs_1_), channel_id=1, source_target_pairs={{0,4},{4,0},{8,12},{12,8},{1,5},{5,1},{9,13},{13,9},{2,6},{6,2},{1... | collective-permute-start | bytes 417800 | tf_op jit(solution)/shard_map/ppermute | solution.py:26
  5.4 8.3 %copy-start.1 = (bf16[1,512,1024]{2,1,0:T(8,128)(2,1)S(1)}, bf16[1,512,1024]{2,1,0:T(8,128)(2,1)}, u32[]{:S(2)}) copy-start(bf16[1,512,1024]{2,1,0:T(8,128)(2,1)} %param.5) | copy-start | bytes 3145732
  5.4 6.1 %collective-permute-start.3 = (bf16[272,256]{1,0:T(8,128)(2,1)S(1)}, bf16[272,256]{1,0:T(8,128)(2,1)S(1)}, u32[]{:S(2)}, u32[]{:S(2)}) collective-permute-start(bf16[272,256]{1,0:T(8,128)(2,1)S(1)} %get-tuple-element.25), channel_id=1, source_target_pairs={{0,8},{4,12},{8,0},{12,4},{1,9},{5,13},{9,1},{13,5},{2,10},{6,14},... | collective-permute-start | bytes 417800 | tf_op jit(solution)/shard_map/ppermute | solution.py:26
  8.0 8.2 %collective-permute-start = (bf16[272,256]{1,0:T(8,128)(2,1)S(1)}, bf16[272,256]{1,0:T(8,128)(2,1)S(1)}, u32[]{:S(2)}, u32[]{:S(2)}) collective-permute-start(bf16[272,256]{1,0:T(8,128)(2,1)S(1)} %get-tuple-element.23), channel_id=1, source_target_pairs={{0,4},{4,0},{8,12},{12,8},{1,5},{5,1},{9,13},{13,9},{2,6},{6,2},{1... | collective-permute-start | bytes 417800 | tf_op jit(solution)/shard_map/ppermute | solution.py:26
  8.6 7.7 %collective-permute-start.1 = (bf16[272,256]{1,0:T(8,128)(2,1)S(1)}, bf16[272,256]{1,0:T(8,128)(2,1)S(1)}, u32[]{:S(2)}, u32[]{:S(2)}) collective-permute-start(bf16[272,256]{1,0:T(8,128)(2,1)S(1)} %get-tuple-element.24), channel_id=1, source_target_pairs={{0,8},{4,12},{8,0},{12,4},{1,9},{5,13},{9,1},{13,5},{2,10},{6,14},... | collective-permute-start | bytes 417800 | tf_op jit(solution)/shard_map/ppermute | solution.py:26
  11.5 6.3 %copy-start.2 = (f32[1,1,256,1024]{3,2,1,0:T(8,128)S(1)}, f32[1,1,256,1024]{3,2,1,0:T(8,128)}, u32[]{:S(2)}) copy-start(f32[1,1,256,1024]{3,2,1,0:T(8,128)} %param.7) | copy-start | bytes 3145732
  11.6 6.3 %collective-permute-start.4 = (bf16[272,256]{1,0:T(8,128)(2,1)S(1)}, bf16[272,256]{1,0:T(8,128)(2,1)S(1)}, u32[]{:S(2)}, u32[]{:S(2)}) collective-permute-start(bf16[272,256]{1,0:T(8,128)(2,1)S(1)} %get-tuple-element.26.refs_2_), channel_id=1, source_target_pairs={{0,4},{4,0},{8,12},{12,8},{1,5},{5,1},{9,13},{13,9},{2,6},{6,2},{1... | collective-permute-start | bytes 417800 | tf_op jit(solution)/shard_map/ppermute | solution.py:26
  11.9 6.0 %collective-permute-start.5 = (bf16[272,256]{1,0:T(8,128)(2,1)S(1)}, bf16[272,256]{1,0:T(8,128)(2,1)S(1)}, u32[]{:S(2)}, u32[]{:S(2)}) collective-permute-start(bf16[272,256]{1,0:T(8,128)(2,1)S(1)} %get-tuple-element.27.refs_3_), channel_id=1, source_target_pairs={{0,8},{4,12},{8,0},{12,4},{1,9},{5,13},{9,1},{13,5},{2,10},{6,14},... | collective-permute-start | bytes 417800 | tf_op jit(solution)/shard_map/ppermute | solution.py:26
  14.3 8.3 %collective-permute-start.13 = (bf16[256,256]{1,0:T(8,128)(2,1)S(1)}, bf16[256,256]{1,0:T(8,128)(2,1)S(1)}, u32[]{:S(2)}, u32[]{:S(2)}) collective-permute-start(bf16[256,256]{1,0:T(8,128)(2,1)S(1)} %get-tuple-element.34), channel_id=1, source_target_pairs={{0,4},{4,0},{8,12},{12,8},{1,5},{5,1},{9,13},{13,9},{2,6},{6,2},{1... | collective-permute-start | bytes 393224 | tf_op jit(solution)/shard_map/ppermute | solution.py:26
  16.2 6.5 %collective-permute-start.14 = (bf16[256,256]{1,0:T(8,128)(2,1)S(1)}, bf16[256,256]{1,0:T(8,128)(2,1)S(1)}, u32[]{:S(2)}, u32[]{:S(2)}) collective-permute-start(bf16[256,256]{1,0:T(8,128)(2,1)S(1)} %get-tuple-element.35), channel_id=1, source_target_pairs={{0,8},{4,12},{8,0},{12,4},{1,9},{5,13},{9,1},{13,5},{2,10},{6,14},... | collective-permute-start | bytes 393224 | tf_op jit(solution)/shard_map/ppermute | solution.py:26
  18.3 6.5 %collective-permute-start.6 = (bf16[272,256]{1,0:T(8,128)(2,1)S(1)}, bf16[272,256]{1,0:T(8,128)(2,1)S(1)}, u32[]{:S(2)}, u32[]{:S(2)}) collective-permute-start(bf16[272,256]{1,0:T(8,128)(2,1)S(1)} %get-tuple-element.29.refs_2_.refs_3_), channel_id=1, source_target_pairs={{0,4},{4,0},{8,12},{12,8},{1,5},{5,1},{9,13},{13,9},{2,6},{6,2},{1... | collective-permute-start | bytes 417800 | tf_op jit(solution)/shard_map/ppermute | solution.py:26
  20.6 5.9 %collective-permute-start.9 = (bf16[288,256]{1,0:T(8,128)(2,1)S(1)}, bf16[288,256]{1,0:T(8,128)(2,1)S(1)}, u32[]{:S(2)}, u32[]{:S(2)}) collective-permute-start(bf16[288,256]{1,0:T(8,128)(2,1)S(1)} %get-tuple-element.30.refs_3_.refs_4_), channel_id=1, source_target_pairs={{0,8},{4,12},{8,0},{12,4},{1,9},{5,13},{9,1},{13,5},{2,10},{6,14},... | collective-permute-start | bytes 442376 | tf_op jit(solution)/shard_map/ppermute | solution.py:26
  21.7 11.7 %collective-permute-start.7 = (bf16[288,256]{1,0:T(8,128)(2,1)S(1)}, bf16[288,256]{1,0:T(8,128)(2,1)S(1)}, u32[]{:S(2)}, u32[]{:S(2)}) collective-permute-start(bf16[288,256]{1,0:T(8,128)(2,1)S(1)} %get-tuple-element.30.refs_3_.refs_4_), channel_id=1, source_target_pairs={{0,4},{4,0},{8,12},{12,8},{1,5},{5,1},{9,13},{13,9},{2,6},{6,2},{1... | collective-permute-start | bytes 442376 | tf_op jit(solution)/shard_map/ppermute | solution.py:26
  22.6 10.6 %collective-permute-start.8 = (bf16[272,256]{1,0:T(8,128)(2,1)S(1)}, bf16[272,256]{1,0:T(8,128)(2,1)S(1)}, u32[]{:S(2)}, u32[]{:S(2)}) collective-permute-start(bf16[272,256]{1,0:T(8,128)(2,1)S(1)} %get-tuple-element.29.refs_2_.refs_3_), channel_id=1, source_target_pairs={{0,8},{4,12},{8,0},{12,4},{1,9},{5,13},{9,1},{13,5},{2,10},{6,14},... | collective-permute-start | bytes 417800 | tf_op jit(solution)/shard_map/ppermute | solution.py:26
  22.7 6.9 %collective-permute-start.15 = (bf16[128,256]{1,0:T(8,128)(2,1)S(1)}, bf16[128,256]{1,0:T(8,128)(2,1)S(1)}, u32[]{:S(2)}, u32[]{:S(2)}) collective-permute-start(bf16[128,256]{1,0:T(8,128)(2,1)S(1)} %get-tuple-element.36), channel_id=1, source_target_pairs={{0,4},{4,0},{8,12},{12,8},{1,5},{5,1},{9,13},{13,9},{2,6},{6,2},{1... | collective-permute-start | bytes 196616 | tf_op jit(solution)/shard_map/ppermute | solution.py:26
  24.8 5.8 %collective-permute-start.16 = (bf16[128,256]{1,0:T(8,128)(2,1)S(1)}, bf16[128,256]{1,0:T(8,128)(2,1)S(1)}, u32[]{:S(2)}, u32[]{:S(2)}) collective-permute-start(bf16[128,256]{1,0:T(8,128)(2,1)S(1)} %get-tuple-element.37), channel_id=1, source_target_pairs={{0,8},{4,12},{8,0},{12,4},{1,9},{5,13},{9,1},{13,5},{2,10},{6,14},... | collective-permute-start | bytes 196616 | tf_op jit(solution)/shard_map/ppermute | solution.py:26
  26.5 8.9 %collective-permute-start.11 = (bf16[288,256]{1,0:T(8,128)(2,1)S(1)}, bf16[288,256]{1,0:T(8,128)(2,1)S(1)}, u32[]{:S(2)}, u32[]{:S(2)}) collective-permute-start(bf16[288,256]{1,0:T(8,128)(2,1)S(1)} %collective-permute-done.9.refs_7_.refs_6_), channel_id=1, source_target_pairs={{0,4},{4,0},{8,12},{12,8},{1,5},{5,1},{9,13},{13,9},{2,6},{6,2},{1... | collective-permute-start | bytes 442376 | tf_op jit(solution)/shard_map/ppermute | solution.py:26
  29.6 5.7 %collective-permute-start.10 = (bf16[272,256]{1,0:T(8,128)(2,1)S(1)}, bf16[272,256]{1,0:T(8,128)(2,1)S(1)}, u32[]{:S(2)}, u32[]{:S(2)}) collective-permute-start(bf16[272,256]{1,0:T(8,128)(2,1)S(1)} %collective-permute-done.6.refs_4_.refs_5_), channel_id=1, source_target_pairs={{0,8},{4,12},{8,0},{12,4},{1,9},{5,13},{9,1},{13,5},{2,10},{6,14},... | collective-permute-start | bytes 417800 | tf_op jit(solution)/shard_map/ppermute | solution.py:26
  30.6 8.9 %copy-start.3 = (bf16[1,1,256,1024]{3,2,1,0:T(8,128)(2,1)S(1)}, bf16[1,1,256,1024]{3,2,1,0:T(8,128)(2,1)}, u32[]{:S(2)}) copy-start(bf16[1,1,256,1024]{3,2,1,0:T(8,128)(2,1)} %param.8) | copy-start | bytes 1572868
  30.6 8.5 %collective-permute-start.17 = (bf16[256,256]{1,0:T(8,128)(2,1)S(1)}, bf16[256,256]{1,0:T(8,128)(2,1)S(1)}, u32[]{:S(2)}, u32[]{:S(2)}) collective-permute-start(bf16[256,256]{1,0:T(8,128)(2,1)S(1)} %grad_total.1.refs_0_), channel_id=1, source_target_pairs={{0,4},{4,0},{8,12},{12,8},{1,5},{5,1},{9,13},{13,9},{2,6},{6,2},{1... | collective-permute-start | bytes 393224 | tf_op jit(solution)/shard_map/ppermute | solution.py:26
  33.2 6.4 %collective-permute-start.18 = (bf16[256,256]{1,0:T(8,128)(2,1)S(1)}, bf16[256,256]{1,0:T(8,128)(2,1)S(1)}, u32[]{:S(2)}, u32[]{:S(2)}) collective-permute-start(bf16[256,256]{1,0:T(8,128)(2,1)S(1)} %grad_total.1.refs_0_), channel_id=1, source_target_pairs={{0,8},{4,12},{8,0},{12,4},{1,9},{5,13},{9,1},{13,5},{2,10},{6,14},... | collective-permute-start | bytes 393224 | tf_op jit(solution)/shard_map/ppermute | solution.py:26
  33.4 6.1 %collective-permute-start.19 = (bf16[256,256]{1,0:T(8,128)(2,1)S(1)}, bf16[256,256]{1,0:T(8,128)(2,1)S(1)}, u32[]{:S(2)}, u32[]{:S(2)}) collective-permute-start(bf16[256,256]{1,0:T(8,128)(2,1)S(1)} %grad_total.1.refs_0_), channel_id=1, source_target_pairs={{0,12},{4,8},{8,4},{12,0},{1,13},{5,9},{9,5},{13,1},{2,14},{6,10},... | collective-permute-start | bytes 393224 | tf_op jit(solution)/shard_map/ppermute | solution.py:26

commit v20 on v17

--- a/solution.py
+++ b/solution.py
@@ -413,7 +413,8 @@
         strip_y,
         after=[upper_x, lower_y],
     )
-    strips = [strip, swapped(strip, 1), swapped(strip, 2), swapped(strip, 3)]
+    from_across = swapped(strip, 3)
+    strips = [strip, swapped(strip, 1), swapped(strip, 2), from_across]
     factor, root, finished = call(
         root_kernel,
         [shape(share, F32, order), shape(share, BF16, order), shape(8, F32, 128)],

time: 40.7 us -> 40.7 us (level)
  no operation moved by 1% of the time
where the time goes in v20:
time: 40.7 us; the launch traced here: 40.5 us
  starting transfers between devices  23.1 us (57%)
  Pallas kernels  7.42 us (18%)
  waiting for transfers between devices  7.4 us (18%)
  between operations  1.38 us (3%)
  local copies, waits for them, and re-layouts  1.24 us (3%)
    ppermute x19, starting transfers between devices, swapped(): lax.ppermute(block, 'dp', [(i, i ^ offset) for i in range(lax.axis_size('...  22.6 us
    pallas_call x9, Pallas kernels, call(): pl.pallas_call(body, out_shape=outs, in_specs=in_specs, out_specs=out_spe...  7.42 us
    ppermute x19, waiting for transfers between devices, swapped(): lax.ppermute(block, 'dp', [(i, i ^ offset) for i in range(lax.axis_size('...  7.4 us
    unnamed x8, local copies, waits for them, and re-layouts  1.24 us
  transfers between devices with their start and end apart: 20, of which 6 were waited for; matrix products, arithmetic and copies ran while one was open for 0% of the time, Pallas kernels for 16%

profile of v20, /device:TPU:0, one launch (start us, length us, event | category | flops | bytes accessed | tf_op | source)
XLA Modules:
  0.0 40.5 jit_solution(10140463130107092738)
XLA Ops:
  0.6 0.5 %collective-permute-start.12 = (bf16[1,512,256]{2,1,0:T(8,128)(2,1)}, bf16[1,512,256]{2,1,0:T(8,128)(2,1)S(1)}, u32[]{:S(2)}, u32[]{:S(2)}) collective-permute-start(bf16[1,512,256]{2,1,0:T(8,128)(2,1)} %param.6), channel_id=1, source_target_pairs={{16,0},{0,16},{17,1},{1,17},{18,2},{2,18},{19,3},{3,19},{20,4},{4,... | collective-permute-start | bytes 786440 | tf_op jit(solution)/shard_map/ppermute | solution.py:22
  1.1 0.0 copy-start
  1.1 1.2 %copy-done = bf16[1,512,1024]{2,1,0:T(8,128)(2,1)S(1)} copy-done((bf16[1,512,1024]{2,1,0:T(8,128)(2,1)S(1)}, bf16[1,512,1024]{2,1,0:T(8,128)(2,1)}, u32[]{:S(2)}) %copy-start) | copy-done | bytes 1048600
  2.4 0.5 %across.1 = (bf16[272,256]{1,0:T(8,128)(2,1)S(1)}, bf16[272,256]{1,0:T(8,128)(2,1)S(1)}) custom-call(bf16[512,1024]{1,0:T(8,128)(2,1)S(1)} %bitcast.7), custom_call_target="tpu_custom_call" | custom-call | tf_op jit(solution)/shard_map/across/pallas_call | solution.py:351
  2.8 2.6 %collective-permute-start.2 = (bf16[272,256]{1,0:T(8,128)(2,1)S(1)}, bf16[272,256]{1,0:T(8,128)(2,1)S(1)}, u32[]{:S(2)}, u32[]{:S(2)}) collective-permute-start(bf16[272,256]{1,0:T(8,128)(2,1)S(1)} %get-tuple-element.21.refs_1_), channel_id=1, source_target_pairs={{0,4},{4,0},{8,12},{12,8},{1,5},{5,1},{9,13},{13,9},{2,6},{6,2},{1... | collective-permute-start | bytes 417800 | tf_op jit(solution)/shard_map/ppermute | solution.py:26
  5.4 0.0 copy-start.1
  5.4 1.5 %collective-permute-start.3 = (bf16[272,256]{1,0:T(8,128)(2,1)S(1)}, bf16[272,256]{1,0:T(8,128)(2,1)S(1)}, u32[]{:S(2)}, u32[]{:S(2)}) collective-permute-start(bf16[272,256]{1,0:T(8,128)(2,1)S(1)} %get-tuple-element.25), channel_id=1, source_target_pairs={{0,8},{4,12},{8,0},{12,4},{1,9},{5,13},{9,1},{13,5},{2,10},{6,14},... | collective-permute-start | bytes 417800 | tf_op jit(solution)/shard_map/ppermute | solution.py:26
  6.9 1.1 %batch.1 = (bf16[272,256]{1,0:T(8,128)(2,1)S(1)}, bf16[272,256]{1,0:T(8,128)(2,1)S(1)}, f32[1088,256]{1,0:T(8,128)S(1)}) custom-call(bf16[512,1024]{1,0:T(8,128)(2,1)S(1)} %bitcast.8, bf16[272,256]{1,0:T(8,128)(2,1)S(1)} %get-tuple-element.21.refs_1_), custom_call_target="tpu_custom_call" | custom-call | tf_op jit(solution)/shard_map/batch/pallas_call | solution.py:351
  8.0 0.6 %collective-permute-start = (bf16[272,256]{1,0:T(8,128)(2,1)S(1)}, bf16[272,256]{1,0:T(8,128)(2,1)S(1)}, u32[]{:S(2)}, u32[]{:S(2)}) collective-permute-start(bf16[272,256]{1,0:T(8,128)(2,1)S(1)} %get-tuple-element.23), channel_id=1, source_target_pairs={{0,4},{4,0},{8,12},{12,8},{1,5},{5,1},{9,13},{13,9},{2,6},{6,2},{1... | collective-permute-start | bytes 417800 | tf_op jit(solution)/shard_map/ppermute | solution.py:26
  8.6 0.1 collective-permute-start.1
  8.7 1.1 %collective-permute-done.2.refs_1_ = bf16[272,256]{1,0:T(8,128)(2,1)S(1)} collective-permute-done((bf16[272,256]{1,0:T(8,128)(2,1)S(1)}, bf16[272,256]{1,0:T(8,128)(2,1)S(1)}, u32[]{:S(2)}, u32[]{:S(2)}) %collective-permute-start.2) | collective-permute-done | bytes 139296 | tf_op jit(solution)/shard_map/ppermute | solution.py:26
  9.7 1.7 %collective-permute-done.3.refs_2_ = bf16[272,256]{1,0:T(8,128)(2,1)S(1)} collective-permute-done((bf16[272,256]{1,0:T(8,128)(2,1)S(1)}, bf16[272,256]{1,0:T(8,128)(2,1)S(1)}, u32[]{:S(2)}, u32[]{:S(2)}) %collective-permute-start.3) | collective-permute-done | bytes 139296 | tf_op jit(solution)/shard_map/ppermute | solution.py:26
  11.5 0.1 relay.1
  11.5 0.0 copy-start.2
  11.6 0.3 collective-permute-start.4
  11.9 1.8 %collective-permute-start.5 = (bf16[272,256]{1,0:T(8,128)(2,1)S(1)}, bf16[272,256]{1,0:T(8,128)(2,1)S(1)}, u32[]{:S(2)}, u32[]{:S(2)}) collective-permute-start(bf16[272,256]{1,0:T(8,128)(2,1)S(1)} %get-tuple-element.27.refs_3_), channel_id=1, source_target_pairs={{0,8},{4,12},{8,0},{12,4},{1,9},{5,13},{9,1},{13,5},{2,10},{6,14},... | collective-permute-start | bytes 417800 | tf_op jit(solution)/shard_map/ppermute | solution.py:26
  13.7 0.0 collective-permute-done.12
  13.7 0.0 copy-done.1
  13.7 0.5 %grad.1 = (bf16[256,256]{1,0:T(8,128)(2,1)S(1)}, bf16[256,256]{1,0:T(8,128)(2,1)S(1)}, f32[512,256]{1,0:T(8,128)S(1)}) custom-call(bf16[512,1024]{1,0:T(8,128)(2,1)S(1)} %bitcast.9, bf16[512,256]{1,0:T(8,128)(2,1)S(1)} %bitcast.12, bf16[272,256]{1,0:T(8,128)(2,1)S(1)} %get-tuple-element.26.refs_2_, bf16[272,256]{1,0:T(8,128)(2,1)S(1)} %get-tuple-element.27.refs_3_), custom_call_target="tpu_custom_call" | custom-call | tf_op jit(solution)/shard_map/grad/pallas_call | solution.py:351
  14.3 1.9 %collective-permute-start.13 = (bf16[256,256]{1,0:T(8,128)(2,1)S(1)}, bf16[256,256]{1,0:T(8,128)(2,1)S(1)}, u32[]{:S(2)}, u32[]{:S(2)}) collective-permute-start(bf16[256,256]{1,0:T(8,128)(2,1)S(1)} %get-tuple-element.34), channel_id=1, source_target_pairs={{0,4},{4,0},{8,12},{12,8},{1,5},{5,1},{9,13},{13,9},{2,6},{6,2},{1... | collective-permute-start | bytes 393224 | tf_op jit(solution)/shard_map/ppermute | solution.py:26
  16.2 0.0 collective-permute-done.refs_1_
  16.2 0.1 collective-permute-start.14
  16.3 0.0 collective-permute-done.1.refs_2_
  16.3 1.6 %collective-permute-done.4.refs_3_ = bf16[272,256]{1,0:T(8,128)(2,1)S(1)} collective-permute-done((bf16[272,256]{1,0:T(8,128)(2,1)S(1)}, bf16[272,256]{1,0:T(8,128)(2,1)S(1)}, u32[]{:S(2)}, u32[]{:S(2)}) %collective-permute-start.4) | collective-permute-done | bytes 139296 | tf_op jit(solution)/shard_map/ppermute | solution.py:26
  17.9 0.0 collective-permute-done.5.refs_4_
  17.9 0.0 copy-done.2
  17.9 0.4 %factor.1 = (bf16[272,256]{1,0:T(8,128)(2,1)S(1)}, bf16[288,256]{1,0:T(8,128)(2,1)S(1)}, f32[640,256]{1,0:T(8,128)S(1)}) custom-call(f32[1088,256]{1,0:T(8,128)S(1)} %get-tuple-element.22.refs_0_, bf16[272,256]{1,0:T(8,128)(2,1)S(1)} %collective-permute-done.refs_1_, bf16[272,256]{1,0:T(8,128)(2,1)S(1)} %collective-permute-done.1.refs_2_, ...), custom_call_target="tpu_custom_call" | custom-call | tf_op jit(solution)/shard_map/factor/pallas_call | solution.py:351
  18.3 2.3 %collective-permute-start.6 = (bf16[272,256]{1,0:T(8,128)(2,1)S(1)}, bf16[272,256]{1,0:T(8,128)(2,1)S(1)}, u32[]{:S(2)}, u32[]{:S(2)}) collective-permute-start(bf16[272,256]{1,0:T(8,128)(2,1)S(1)} %get-tuple-element.29.refs_2_.refs_3_), channel_id=1, source_target_pairs={{0,4},{4,0},{8,12},{12,8},{1,5},{5,1},{9,13},{13,9},{2,6},{6,2},{1... | collective-permute-start | bytes 417800 | tf_op jit(solution)/shard_map/ppermute | solution.py:26
  20.6 1.1 %collective-permute-start.9 = (bf16[288,256]{1,0:T(8,128)(2,1)S(1)}, bf16[288,256]{1,0:T(8,128)(2,1)S(1)}, u32[]{:S(2)}, u32[]{:S(2)}) collective-permute-start(bf16[288,256]{1,0:T(8,128)(2,1)S(1)} %get-tuple-element.30.refs_3_.refs_4_), channel_id=1, source_target_pairs={{0,8},{4,12},{8,0},{12,4},{1,9},{5,13},{9,1},{13,5},{2,10},{6,14},... | collective-permute-start | bytes 442376 | tf_op jit(solution)/shard_map/ppermute | solution.py:26
  21.7 0.9 %collective-permute-start.7 = (bf16[288,256]{1,0:T(8,128)(2,1)S(1)}, bf16[288,256]{1,0:T(8,128)(2,1)S(1)}, u32[]{:S(2)}, u32[]{:S(2)}) collective-permute-start(bf16[288,256]{1,0:T(8,128)(2,1)S(1)} %get-tuple-element.30.refs_3_.refs_4_), channel_id=1, source_target_pairs={{0,4},{4,0},{8,12},{12,8},{1,5},{5,1},{9,13},{13,9},{2,6},{6,2},{1... | collective-permute-start | bytes 442376 | tf_op jit(solution)/shard_map/ppermute | solution.py:26
  22.6 0.0 collective-permute-done.13.refs_1_
  22.6 0.1 collective-permute-start.8
  22.7 0.0 collective-permute-done.14.refs_2_
  22.7 2.0 %collective-permute-start.15 = (bf16[128,256]{1,0:T(8,128)(2,1)S(1)}, bf16[128,256]{1,0:T(8,128)(2,1)S(1)}, u32[]{:S(2)}, u32[]{:S(2)}) collective-permute-start(bf16[128,256]{1,0:T(8,128)(2,1)S(1)} %get-tuple-element.36), channel_id=1, source_target_pairs={{0,4},{4,0},{8,12},{12,8},{1,5},{5,1},{9,13},{13,9},{2,6},{6,2},{1... | collective-permute-start | bytes 196616 | tf_op jit(solution)/shard_map/ppermute | solution.py:26
  24.8 0.0 collective-permute-done.6.refs_4_.refs_5_
  24.8 1.5 %collective-permute-start.16 = (bf16[128,256]{1,0:T(8,128)(2,1)S(1)}, bf16[128,256]{1,0:T(8,128)(2,1)S(1)}, u32[]{:S(2)}, u32[]{:S(2)}) collective-permute-start(bf16[128,256]{1,0:T(8,128)(2,1)S(1)} %get-tuple-element.37), channel_id=1, source_target_pairs={{0,8},{4,12},{8,0},{12,4},{1,9},{5,13},{9,1},{13,5},{2,10},{6,14},... | collective-permute-start | bytes 196616 | tf_op jit(solution)/shard_map/ppermute | solution.py:26
  26.3 0.2 collective-permute-done.9.refs_7_.refs_6_
  26.5 0.7 %collective-permute-start.11 = (bf16[288,256]{1,0:T(8,128)(2,1)S(1)}, bf16[288,256]{1,0:T(8,128)(2,1)S(1)}, u32[]{:S(2)}, u32[]{:S(2)}) collective-permute-start(bf16[288,256]{1,0:T(8,128)(2,1)S(1)} %collective-permute-done.9.refs_7_.refs_6_), channel_id=1, source_target_pairs={{0,4},{4,0},{8,12},{12,8},{1,5},{5,1},{9,13},{13,9},{2,6},{6,2},{1... | collective-permute-start | bytes 442376 | tf_op jit(solution)/shard_map/ppermute | solution.py:26
  27.2 2.4 %collective-permute-done.15.refs_3_ = bf16[128,256]{1,0:T(8,128)(2,1)S(1)} collective-permute-done((bf16[128,256]{1,0:T(8,128)(2,1)S(1)}, bf16[128,256]{1,0:T(8,128)(2,1)S(1)}, u32[]{:S(2)}, u32[]{:S(2)}) %collective-permute-start.15) | collective-permute-done | bytes 65568 | tf_op jit(solution)/shard_map/ppermute | solution.py:26
  29.6 0.9 %collective-permute-start.10 = (bf16[272,256]{1,0:T(8,128)(2,1)S(1)}, bf16[272,256]{1,0:T(8,128)(2,1)S(1)}, u32[]{:S(2)}, u32[]{:S(2)}) collective-permute-start(bf16[272,256]{1,0:T(8,128)(2,1)S(1)} %collective-permute-done.6.refs_4_.refs_5_), channel_id=1, source_target_pairs={{0,8},{4,12},{8,0},{12,4},{1,9},{5,13},{9,1},{13,5},{2,10},{6,14},... | collective-permute-start | bytes 417800 | tf_op jit(solution)/shard_map/ppermute | solution.py:26
  30.6 0.0 collective-permute-done.16.refs_4_
  30.6 0.1 grad_total.1.refs_0_
  30.6 0.0 copy-start.3
  30.6 2.5 %collective-permute-start.17 = (bf16[256,256]{1,0:T(8,128)(2,1)S(1)}, bf16[256,256]{1,0:T(8,128)(2,1)S(1)}, u32[]{:S(2)}, u32[]{:S(2)}) collective-permute-start(bf16[256,256]{1,0:T(8,128)(2,1)S(1)} %grad_total.1.refs_0_), channel_id=1, source_target_pairs={{0,4},{4,0},{8,12},{12,8},{1,5},{5,1},{9,13},{13,9},{2,6},{6,2},{1... | collective-permute-start | bytes 393224 | tf_op jit(solution)/shard_map/ppermute | solution.py:26
  33.2 0.0 collective-permute-done.8.refs_6_
  33.2 0.2 collective-permute-start.18
  33.4 0.0 collective-permute-done.7.refs_5_
  33.4 1.3 %collective-permute-start.19 = (bf16[256,256]{1,0:T(8,128)(2,1)S(1)}, bf16[256,256]{1,0:T(8,128)(2,1)S(1)}, u32[]{:S(2)}, u32[]{:S(2)}) collective-permute-start(bf16[256,256]{1,0:T(8,128)(2,1)S(1)} %grad_total.1.refs_0_), channel_id=1, source_target_pairs={{0,12},{4,8},{8,4},{12,0},{1,13},{5,9},{9,5},{13,1},{2,14},{6,10},... | collective-permute-start | bytes 393224 | tf_op jit(solution)/shard_map/ppermute | solution.py:26
  35.4 0.0 collective-permute-done.10.refs_8_
  35.4 0.0 collective-permute-done.11.refs_9_
  35.4 3.8 %root.1 = (f32[256,1024]{1,0:T(8,128)}, bf16[256,1024]{1,0:T(8,128)(2,1)}, f32[8,128]{1,0:T(8,128)S(1)}) custom-call(s32[1,1]{1,0:T(1,128)S(6)} %copy.8.refs_0_, f32[640,256]{1,0:T(8,128)S(1)} %get-tuple-element.28.refs_1_, bf16[272,256]{1,0:T(8,128)(2,1)S(1)} %get-tuple-element.29.refs_2_.refs_3_, bf16[288,256]{1,0:T(8,128)(2,1)S(1)} %get-tuple-element.30.refs_3_.refs_4_, ...), custom_call_target="tpu_custom_call" | custom-call | tf_op jit(solution)/shard_map/root/pallas_call | solution.py:351
  39.2 0.0 collective-permute-done.17.refs_1_
  39.2 0.3 collective-permute-done.18.refs_2_
  39.5 0.0 collective-permute-done.19.refs_3_
  39.5 0.0 copy-done.3
  39.5 1.0 %step.1 = bf16[256,256]{1,0:T(8,128)(2,1)} custom-call(bf16[256,256]{1,0:T(8,128)(2,1)S(1)} %grad_total.1.refs_0_, bf16[256,256]{1,0:T(8,128)(2,1)S(1)} %collective-permute-done.17.refs_1_, bf16[256,256]{1,0:T(8,128)(2,1)S(1)} %collective-permute-done.18.refs_2_, bf16[256,256]{1,0:T(8,128)(2,1)S(1)} %collective-permute-done.19.refs_3_, ...), custom_call_target="tpu_custom_call" | custom-call | tf_op jit(solution)/shard_map/step/pallas_call | solution.py:351
  (1 shorter events, 0.0 us)
Async XLA Ops:
  0.6 13.1 %collective-permute-start.12 = (bf16[1,512,256]{2,1,0:T(8,128)(2,1)}, bf16[1,512,256]{2,1,0:T(8,128)(2,1)S(1)}, u32[]{:S(2)}, u32[]{:S(2)}) collective-permute-start(bf16[1,512,256]{2,1,0:T(8,128)(2,1)} %param.6), channel_id=1, source_target_pairs={{16,0},{0,16},{17,1},{1,17},{18,2},{2,18},{19,3},{3,19},{20,4},{4,... | collective-permute-start | bytes 786440 | tf_op jit(solution)/shard_map/ppermute | solution.py:22
  1.1 1.2 %copy-start = (bf16[1,512,1024]{2,1,0:T(8,128)(2,1)S(1)}, bf16[1,512,1024]{2,1,0:T(8,128)(2,1)}, u32[]{:S(2)}) copy-start(bf16[1,512,1024]{2,1,0:T(8,128)(2,1)} %param.5) | copy-start | bytes 3145732
  2.8 6.9 %collective-permute-start.2 = (bf16[272,256]{1,0:T(8,128)(2,1)S(1)}, bf16[272,256]{1,0:T(8,128)(2,1)S(1)}, u32[]{:S(2)}, u32[]{:S(2)}) collective-permute-start(bf16[272,256]{1,0:T(8,128)(2,1)S(1)} %get-tuple-element.21.refs_1_), channel_id=1, source_target_pairs={{0,4},{4,0},{8,12},{12,8},{1,5},{5,1},{9,13},{13,9},{2,6},{6,2},{1... | collective-permute-start | bytes 417800 | tf_op jit(solution)/shard_map/ppermute | solution.py:26
  5.4 8.3 %copy-start.1 = (bf16[1,512,1024]{2,1,0:T(8,128)(2,1)S(1)}, bf16[1,512,1024]{2,1,0:T(8,128)(2,1)}, u32[]{:S(2)}) copy-start(bf16[1,512,1024]{2,1,0:T(8,128)(2,1)} %param.5) | copy-start | bytes 3145732
  5.4 6.1 %collective-permute-start.3 = (bf16[272,256]{1,0:T(8,128)(2,1)S(1)}, bf16[272,256]{1,0:T(8,128)(2,1)S(1)}, u32[]{:S(2)}, u32[]{:S(2)}) collective-permute-start(bf16[272,256]{1,0:T(8,128)(2,1)S(1)} %get-tuple-element.25), channel_id=1, source_target_pairs={{0,8},{4,12},{8,0},{12,4},{1,9},{5,13},{9,1},{13,5},{2,10},{6,14},... | collective-permute-start | bytes 417800 | tf_op jit(solution)/shard_map/ppermute | solution.py:26
  8.0 8.2 %collective-permute-start = (bf16[272,256]{1,0:T(8,128)(2,1)S(1)}, bf16[272,256]{1,0:T(8,128)(2,1)S(1)}, u32[]{:S(2)}, u32[]{:S(2)}) collective-permute-start(bf16[272,256]{1,0:T(8,128)(2,1)S(1)} %get-tuple-element.23), channel_id=1, source_target_pairs={{0,4},{4,0},{8,12},{12,8},{1,5},{5,1},{9,13},{13,9},{2,6},{6,2},{1... | collective-permute-start | bytes 417800 | tf_op jit(solution)/shard_map/ppermute | solution.py:26
  8.6 7.7 %collective-permute-start.1 = (bf16[272,256]{1,0:T(8,128)(2,1)S(1)}, bf16[272,256]{1,0:T(8,128)(2,1)S(1)}, u32[]{:S(2)}, u32[]{:S(2)}) collective-permute-start(bf16[272,256]{1,0:T(8,128)(2,1)S(1)} %get-tuple-element.24), channel_id=1, source_target_pairs={{0,8},{4,12},{8,0},{12,4},{1,9},{5,13},{9,1},{13,5},{2,10},{6,14},... | collective-permute-start | bytes 417800 | tf_op jit(solution)/shard_map/ppermute | solution.py:26
  11.5 6.3 %copy-start.2 = (f32[1,1,256,1024]{3,2,1,0:T(8,128)S(1)}, f32[1,1,256,1024]{3,2,1,0:T(8,128)}, u32[]{:S(2)}) copy-start(f32[1,1,256,1024]{3,2,1,0:T(8,128)} %param.7) | copy-start | bytes 3145732
  11.6 6.3 %collective-permute-start.4 = (bf16[272,256]{1,0:T(8,128)(2,1)S(1)}, bf16[272,256]{1,0:T(8,128)(2,1)S(1)}, u32[]{:S(2)}, u32[]{:S(2)}) collective-permute-start(bf16[272,256]{1,0:T(8,128)(2,1)S(1)} %get-tuple-element.26.refs_2_), channel_id=1, source_target_pairs={{0,4},{4,0},{8,12},{12,8},{1,5},{5,1},{9,13},{13,9},{2,6},{6,2},{1... | collective-permute-start | bytes 417800 | tf_op jit(solution)/shard_map/ppermute | solution.py:26
  11.9 6.0 %collective-permute-start.5 = (bf16[272,256]{1,0:T(8,128)(2,1)S(1)}, bf16[272,256]{1,0:T(8,128)(2,1)S(1)}, u32[]{:S(2)}, u32[]{:S(2)}) collective-permute-start(bf16[272,256]{1,0:T(8,128)(2,1)S(1)} %get-tuple-element.27.refs_3_), channel_id=1, source_target_pairs={{0,8},{4,12},{8,0},{12,4},{1,9},{5,13},{9,1},{13,5},{2,10},{6,14},... | collective-permute-start | bytes 417800 | tf_op jit(solution)/shard_map/ppermute | solution.py:26
  14.3 8.3 %collective-permute-start.13 = (bf16[256,256]{1,0:T(8,128)(2,1)S(1)}, bf16[256,256]{1,0:T(8,128)(2,1)S(1)}, u32[]{:S(2)}, u32[]{:S(2)}) collective-permute-start(bf16[256,256]{1,0:T(8,128)(2,1)S(1)} %get-tuple-element.34), channel_id=1, source_target_pairs={{0,4},{4,0},{8,12},{12,8},{1,5},{5,1},{9,13},{13,9},{2,6},{6,2},{1... | collective-permute-start | bytes 393224 | tf_op jit(solution)/shard_map/ppermute | solution.py:26
  16.2 6.5 %collective-permute-start.14 = (bf16[256,256]{1,0:T(8,128)(2,1)S(1)}, bf16[256,256]{1,0:T(8,128)(2,1)S(1)}, u32[]{:S(2)}, u32[]{:S(2)}) collective-permute-start(bf16[256,256]{1,0:T(8,128)(2,1)S(1)} %get-tuple-element.35), channel_id=1, source_target_pairs={{0,8},{4,12},{8,0},{12,4},{1,9},{5,13},{9,1},{13,5},{2,10},{6,14},... | collective-permute-start | bytes 393224 | tf_op jit(solution)/shard_map/ppermute | solution.py:26
  18.3 6.5 %collective-permute-start.6 = (bf16[272,256]{1,0:T(8,128)(2,1)S(1)}, bf16[272,256]{1,0:T(8,128)(2,1)S(1)}, u32[]{:S(2)}, u32[]{:S(2)}) collective-permute-start(bf16[272,256]{1,0:T(8,128)(2,1)S(1)} %get-tuple-element.29.refs_2_.refs_3_), channel_id=1, source_target_pairs={{0,4},{4,0},{8,12},{12,8},{1,5},{5,1},{9,13},{13,9},{2,6},{6,2},{1... | collective-permute-start | bytes 417800 | tf_op jit(solution)/shard_map/ppermute | solution.py:26
  20.6 5.9 %collective-permute-start.9 = (bf16[288,256]{1,0:T(8,128)(2,1)S(1)}, bf16[288,256]{1,0:T(8,128)(2,1)S(1)}, u32[]{:S(2)}, u32[]{:S(2)}) collective-permute-start(bf16[288,256]{1,0:T(8,128)(2,1)S(1)} %get-tuple-element.30.refs_3_.refs_4_), channel_id=1, source_target_pairs={{0,8},{4,12},{8,0},{12,4},{1,9},{5,13},{9,1},{13,5},{2,10},{6,14},... | collective-permute-start | bytes 442376 | tf_op jit(solution)/shard_map/ppermute | solution.py:26
  21.7 11.7 %collective-permute-start.7 = (bf16[288,256]{1,0:T(8,128)(2,1)S(1)}, bf16[288,256]{1,0:T(8,128)(2,1)S(1)}, u32[]{:S(2)}, u32[]{:S(2)}) collective-permute-start(bf16[288,256]{1,0:T(8,128)(2,1)S(1)} %get-tuple-element.30.refs_3_.refs_4_), channel_id=1, source_target_pairs={{0,4},{4,0},{8,12},{12,8},{1,5},{5,1},{9,13},{13,9},{2,6},{6,2},{1... | collective-permute-start | bytes 442376 | tf_op jit(solution)/shard_map/ppermute | solution.py:26
  22.6 10.6 %collective-permute-start.8 = (bf16[272,256]{1,0:T(8,128)(2,1)S(1)}, bf16[272,256]{1,0:T(8,128)(2,1)S(1)}, u32[]{:S(2)}, u32[]{:S(2)}) collective-permute-start(bf16[272,256]{1,0:T(8,128)(2,1)S(1)} %get-tuple-element.29.refs_2_.refs_3_), channel_id=1, source_target_pairs={{0,8},{4,12},{8,0},{12,4},{1,9},{5,13},{9,1},{13,5},{2,10},{6,14},... | collective-permute-start | bytes 417800 | tf_op jit(solution)/shard_map/ppermute | solution.py:26
  22.7 6.9 %collective-permute-start.15 = (bf16[128,256]{1,0:T(8,128)(2,1)S(1)}, bf16[128,256]{1,0:T(8,128)(2,1)S(1)}, u32[]{:S(2)}, u32[]{:S(2)}) collective-permute-start(bf16[128,256]{1,0:T(8,128)(2,1)S(1)} %get-tuple-element.36), channel_id=1, source_target_pairs={{0,4},{4,0},{8,12},{12,8},{1,5},{5,1},{9,13},{13,9},{2,6},{6,2},{1... | collective-permute-start | bytes 196616 | tf_op jit(solution)/shard_map/ppermute | solution.py:26
  24.8 5.8 %collective-permute-start.16 = (bf16[128,256]{1,0:T(8,128)(2,1)S(1)}, bf16[128,256]{1,0:T(8,128)(2,1)S(1)}, u32[]{:S(2)}, u32[]{:S(2)}) collective-permute-start(bf16[128,256]{1,0:T(8,128)(2,1)S(1)} %get-tuple-element.37), channel_id=1, source_target_pairs={{0,8},{4,12},{8,0},{12,4},{1,9},{5,13},{9,1},{13,5},{2,10},{6,14},... | collective-permute-start | bytes 196616 | tf_op jit(solution)/shard_map/ppermute | solution.py:26
  26.5 8.9 %collective-permute-start.11 = (bf16[288,256]{1,0:T(8,128)(2,1)S(1)}, bf16[288,256]{1,0:T(8,128)(2,1)S(1)}, u32[]{:S(2)}, u32[]{:S(2)}) collective-permute-start(bf16[288,256]{1,0:T(8,128)(2,1)S(1)} %collective-permute-done.9.refs_7_.refs_6_), channel_id=1, source_target_pairs={{0,4},{4,0},{8,12},{12,8},{1,5},{5,1},{9,13},{13,9},{2,6},{6,2},{1... | collective-permute-start | bytes 442376 | tf_op jit(solution)/shard_map/ppermute | solution.py:26
  29.6 5.7 %collective-permute-start.10 = (bf16[272,256]{1,0:T(8,128)(2,1)S(1)}, bf16[272,256]{1,0:T(8,128)(2,1)S(1)}, u32[]{:S(2)}, u32[]{:S(2)}) collective-permute-start(bf16[272,256]{1,0:T(8,128)(2,1)S(1)} %collective-permute-done.6.refs_4_.refs_5_), channel_id=1, source_target_pairs={{0,8},{4,12},{8,0},{12,4},{1,9},{5,13},{9,1},{13,5},{2,10},{6,14},... | collective-permute-start | bytes 417800 | tf_op jit(solution)/shard_map/ppermute | solution.py:26
  30.6 8.9 %copy-start.3 = (bf16[1,1,256,1024]{3,2,1,0:T(8,128)(2,1)S(1)}, bf16[1,1,256,1024]{3,2,1,0:T(8,128)(2,1)}, u32[]{:S(2)}) copy-start(bf16[1,1,256,1024]{3,2,1,0:T(8,128)(2,1)} %param.8) | copy-start | bytes 1572868
  30.6 8.6 %collective-permute-start.17 = (bf16[256,256]{1,0:T(8,128)(2,1)S(1)}, bf16[256,256]{1,0:T(8,128)(2,1)S(1)}, u32[]{:S(2)}, u32[]{:S(2)}) collective-permute-start(bf16[256,256]{1,0:T(8,128)(2,1)S(1)} %grad_total.1.refs_0_), channel_id=1, source_target_pairs={{0,4},{4,0},{8,12},{12,8},{1,5},{5,1},{9,13},{13,9},{2,6},{6,2},{1... | collective-permute-start | bytes 393224 | tf_op jit(solution)/shard_map/ppermute | solution.py:26
  33.2 6.4 %collective-permute-start.18 = (bf16[256,256]{1,0:T(8,128)(2,1)S(1)}, bf16[256,256]{1,0:T(8,128)(2,1)S(1)}, u32[]{:S(2)}, u32[]{:S(2)}) collective-permute-start(bf16[256,256]{1,0:T(8,128)(2,1)S(1)} %grad_total.1.refs_0_), channel_id=1, source_target_pairs={{0,8},{4,12},{8,0},{12,4},{1,9},{5,13},{9,1},{13,5},{2,10},{6,14},... | collective-permute-start | bytes 393224 | tf_op jit(solution)/shard_map/ppermute | solution.py:26
  33.4 6.1 %collective-permute-start.19 = (bf16[256,256]{1,0:T(8,128)(2,1)S(1)}, bf16[256,256]{1,0:T(8,128)(2,1)S(1)}, u32[]{:S(2)}, u32[]{:S(2)}) collective-permute-start(bf16[256,256]{1,0:T(8,128)(2,1)S(1)} %grad_total.1.refs_0_), channel_id=1, source_target_pairs={{0,12},{4,8},{8,4},{12,0},{1,13},{5,9},{9,5},{13,1},{2,14},{6,10},... | collective-permute-start | bytes 393224 | tf_op jit(solution)/shard_map/ppermute | solution.py:26
